TPU v7x, 32 devices: a whole 2x2x4 slice. The times are simulated.
32 devices in a mesh: scene: 4 (over y, x), view: 4 (over z), row: 2 (over core).
Axes of the slice: x: 2, y: 2, z: 4, core: 2. Of those that a mesh axis runs over, the one named last changes fastest.
Arguments:
- latents: bfloat16 [4, 16, 2, 32, 1536], P('scene', 'view', 'row'), may hold values from -6 to 6
- norm_gain: float32 [1536], replicated, may hold values from 0.5 to 4
- w_query: bfloat16 [1536, 768], replicated, may hold values from -0.15625 to 0.15625
- w_key: bfloat16 [1536, 768], replicated, may hold values from -0.15625 to 0.15625
- w_value: bfloat16 [1536, 768], replicated, may hold values from -0.15625 to 0.15625
- w_out: bfloat16 [768, 1536], replicated, may hold values from -0.21875 to 0.21875
- kernel: bfloat16 [9, 1536], replicated, may hold values from -4 to 4
- partners: int32 [4, 16, 3], P('scene', 'view'), may hold values from -1 to 15, as said below
- counts: int32 [4, 16], P('scene', 'view'), may hold values from 2 to 3, as said below
- cotangent: bfloat16 [4, 16, 2, 32, 1536], P('scene', 'view', 'row'), may hold values from -1.5 to 1.5
Outputs:
- grad_query: float32 [1536, 768], P(('scene', 'view', 'row'))
- grad_key: float32 [1536, 768], P(('scene', 'view', 'row'))
- grad_value: float32 [1536, 768], P(('scene', 'view', 'row'))
- grad_out: float32 [768, 1536], P(('scene', 'view', 'row'))
Inputs may be any that keep to these rules, and one draw needn't show every extreme that they name: Entries j < counts of a view are distinct views held by other groups of 4 views (views 4 * i to 4 * i + 3 form group i); all partners that the views of one group take from another group are one and the same view; entries from counts on are -1. `counts`: the first view of every group has 3 partners.
All inputs are finite; a program needn't handle non-finite values.
Results may differ from a plain program's by a relative error of at most 0.0049.
The roundings to bfloat16 on the way count: a program that leaves them out, or rounds other values in their place, can miss the bound.
Values may be sent and summed in bfloat16 or wider, within the bound.
No kernel may reach another device: no remote copies, remote signals or barrier semaphores. Data moves between devices by JAX's collectives and lax.ppermute only.
A program may use at most 192 MiB of HBM per device.

v0:
```python
import jax
import jax.numpy as jnp
from jax import lax
from jax.sharding import PartitionSpec as P

HEAD_DIM = 64


epsilon = 1e-06


def padded_2(x, sides, width):
    for axis, dim in sides:
        count, length = (lax.axis_size(axis), x.shape[dim])
        up = [(i, (i + 1) % count) for i in range(count - 1)]
        down = [(j, i) for i, j in up]
        last = lax.slice_in_dim(x, length - width, length, axis=dim)
        leading = lax.slice_in_dim(x, 0, width, axis=dim)
        before = lax.ppermute(last, axis, up)
        after = lax.ppermute(leading, axis, down)
        x = jnp.concatenate([before, x, after], axis=dim)
    return x


def rim_conv(padded, kernel, rows, columns):
    result = padded[:, 1 : 1 + rows, 1 : 1 + columns].astype(jnp.float32)
    for row_step in range(3):
        for col_step in range(3):
            result = result + kernel[3 * row_step + col_step].astype(jnp.float32) * padded[
                :, 2 - row_step : 2 - row_step + rows, 2 - col_step : 2 - col_step + columns
            ].astype(jnp.float32)
    return result.astype(jnp.bfloat16)


def shards(latents, norm_gain, w_query, w_key, w_value, w_out, kernel, partners, counts, cotangent):
    views_here, strip_rows, columns, width = latents.shape[1:]
    inner_width = w_query.shape[1]
    head_count = inner_width // HEAD_DIM
    view_count = lax.axis_size("view")
    tokens_here = views_here * strip_rows * columns
    scale = HEAD_DIM ** (-0.5)
    lat_f = latents[0].astype(jnp.float32)
    normed = (
        lat_f * lax.rsqrt(jnp.mean(lat_f * lat_f, -1, keepdims=True) + epsilon) * norm_gain
    ).astype(jnp.bfloat16)
    flat_rows = normed.reshape(tokens_here, width)
    queries = jnp.dot(flat_rows, w_query, preferred_element_type=jnp.float32).astype(jnp.bfloat16)
    queries = queries.reshape(views_here, strip_rows * columns, head_count, HEAD_DIM)
    pair_weight = jnp.concatenate((w_key, w_value), axis=1)
    key_value = jnp.dot(flat_rows, pair_weight, preferred_element_type=jnp.float32).astype(
        jnp.bfloat16
    )
    key_value = key_value.reshape(views_here, strip_rows, columns, 2 * inner_width)
    partner_ids = partners[0]
    max_partners = partner_ids.shape[1]
    alive_slots = jnp.arange(max_partners, dtype=jnp.int32)[None, :] < counts[0][:, None]
    source_group = jnp.where(alive_slots, partner_ids // views_here, -1)
    source_view = partner_ids % views_here
    matches = source_group[:, :, None] == jnp.arange(view_count, dtype=jnp.int32)[None, None, :]
    wanted_ok = jnp.any(matches, axis=(0, 1)).astype(jnp.int32)
    wanted_view = jnp.max(jnp.where(matches, source_view[:, :, None], 0), axis=(0, 1))
    request = jnp.stack((wanted_view, wanted_ok), axis=1)
    granted = lax.all_to_all(request, "view", split_axis=0, concat_axis=0, tiled=True)
    grant_view = granted[:, 0]
    grant_ok = granted[:, 1] > 0
    safe_source = jnp.maximum(source_group, 0)
    full_own = lax.all_gather(key_value, "row", axis=1, tiled=True)
    outgoing = jnp.where(
        grant_ok[:, None, None, None],
        jnp.take(full_own, grant_view, axis=0),
        jnp.zeros((), jnp.bfloat16),
    )
    full_arrived = lax.all_to_all(outgoing, "view", split_axis=0, concat_axis=0, tiled=True)
    all_rows = full_own.shape[1]
    view_tokens = all_rows * columns
    block_count = 1 + max_partners
    fetched = jnp.take(full_arrived, safe_source, axis=0)
    blocks = jnp.concatenate((full_own[:, None], fetched), axis=1)
    blocks = blocks.reshape(views_here, block_count * view_tokens, 2, head_count, HEAD_DIM)
    key_rows = blocks[:, :, 0]
    value_rows = blocks[:, :, 1]
    block_alive = jnp.concatenate((jnp.ones((views_here, 1), bool), alive_slots), axis=1)
    key_alive = jnp.repeat(block_alive, view_tokens, axis=1)
    scores = (
        jnp.einsum("uqhd,ukhd->uhqk", queries, key_rows, preferred_element_type=jnp.float32) * scale
    )
    scores = jnp.where(key_alive[:, None, None, :], scores, -1e30)
    highest = jnp.max(scores, -1, keepdims=True)
    expo = jnp.exp(scores - highest)
    attention = expo / jnp.sum(expo, -1, keepdims=True)
    attention_b = attention.astype(jnp.bfloat16)
    mixed = jnp.einsum(
        "uhqk,ukhd->uqhd", attention_b, value_rows, preferred_element_type=jnp.float32
    )
    mixed = mixed.astype(jnp.bfloat16).reshape(tokens_here, inner_width)
    grad_in = cotangent[0]
    padded = padded_2(grad_in, (("row", 1),), 1)
    padded = jnp.pad(padded, ((0, 0), (0, 0), (1, 1), (0, 0)))
    upstream = rim_conv(padded, kernel, strip_rows, columns)
    up_flat = upstream.reshape(tokens_here, width)
    grad_out = jnp.einsum("ti,td->id", mixed, up_flat, preferred_element_type=jnp.float32)
    out_grad = jnp.einsum("td,id->ti", up_flat, w_out, preferred_element_type=jnp.float32).astype(
        jnp.bfloat16
    )
    out_grad = out_grad.reshape(views_here, strip_rows * columns, head_count, HEAD_DIM)
    dprob = jnp.einsum("uqhd,ukhd->uhqk", out_grad, value_rows, preferred_element_type=jnp.float32)
    row_delta = jnp.sum(attention * dprob, -1, keepdims=True)
    dscore = (attention * (dprob - row_delta) * scale).astype(jnp.bfloat16)
    dquery = jnp.einsum("uhqk,ukhd->uqhd", dscore, key_rows, preferred_element_type=jnp.float32)
    dquery = dquery.astype(jnp.bfloat16).reshape(tokens_here, inner_width)
    grad_query = jnp.einsum("tc,ti->ci", flat_rows, dquery, preferred_element_type=jnp.float32)
    dkey = jnp.einsum("uhqk,uqhd->ukhd", dscore, queries, preferred_element_type=jnp.float32)
    dvalue = jnp.einsum(
        "uhqk,uqhd->ukhd", attention_b, out_grad, preferred_element_type=jnp.float32
    )
    block_shape = (views_here, block_count, all_rows, columns, inner_width)
    dpair = jnp.concatenate((dkey.reshape(block_shape), dvalue.reshape(block_shape)), axis=-1)
    own_part = lax.optimization_barrier(dpair[:, 0].astype(jnp.bfloat16))
    match_table = matches.astype(jnp.float32)
    returned_part = jnp.einsum(
        "ujs,ujhwc->shwc", match_table, dpair[:, 1:], precision=lax.Precision.HIGHEST
    ).astype(jnp.bfloat16)
    came_back = lax.all_to_all(returned_part, "view", split_axis=0, concat_axis=0, tiled=True)
    grant_table = (
        (grant_view[:, None] == jnp.arange(views_here, dtype=jnp.int32)[None, :])
        & grant_ok[:, None]
    ).astype(jnp.float32)
    totals = own_part.astype(jnp.float32) + jnp.einsum(
        "ev,ehwc->vhwc", grant_table, came_back.astype(jnp.float32), precision=lax.Precision.HIGHEST
    )
    own_strip = lax.psum_scatter(totals, "row", scatter_dimension=1, tiled=True)
    own_strip = own_strip.reshape(tokens_here, 2 * inner_width)
    rows_f = flat_rows.astype(jnp.float32)
    grad_key = jnp.dot(rows_f.T, own_strip[:, :inner_width], precision=lax.Precision.HIGHEST)
    grad_value = jnp.dot(rows_f.T, own_strip[:, inner_width:], precision=lax.Precision.HIGHEST)
    summed = (
        lax.psum_scatter(grad_query, ("scene", "view", "row"), scatter_dimension=0, tiled=True),
        lax.psum_scatter(grad_key, ("scene", "view", "row"), scatter_dimension=0, tiled=True),
        lax.psum_scatter(grad_value, ("scene", "view", "row"), scatter_dimension=0, tiled=True),
        lax.psum_scatter(grad_out, ("scene", "view", "row"), scatter_dimension=0, tiled=True),
    )
    return (summed[0], summed[1], summed[2], summed[3])


def solution(mesh):
    placed = (
        P("scene", "view", "row", None, None),
        P(),
        P(),
        P(),
        P(),
        P(),
        P(),
        P("scene", "view", None),
        P("scene", "view"),
        P("scene", "view", "row", None, None),
    )
    return jax.shard_map(
        shards,
        mesh=mesh,
        in_specs=placed,
        out_specs=(
            P(("scene", "view", "row"), None),
            P(("scene", "view", "row"), None),
            P(("scene", "view", "row"), None),
            P(("scene", "view", "row"), None),
        ),
        check_vma=False,
    )
```

profile of v0, /device:TPU:0, one launch (start us, length us, event | category | flops | bytes accessed | tf_op | source)
XLA Modules:
  0.0 689.1 jit_solution(2820182510312205604)
XLA Ops:
  7.2 1.4 collective-permute-start.1
  8.6 4.5 collective-permute-start
  13.2 0.8 copy.82
  13.9 1.3 maximum_compare_fusion
  16.0 0.7 copy.83
  16.7 6.3 all-to-all-start
  23.0 0.7 fusion.91
  23.8 0.6 reshape.438
  24.4 1.1 multiply_reduce_fusion.1
  25.7 1.8 convert_reduce_fusion.8
  27.5 1.2 fusion.66
  28.7 1.2 convolution_convert_fusion.1
  29.8 0.6 copy-done.35
  30.4 2.5 fusion.11
  32.9 2.4 all_gather.3
  35.3 0.8 copy.84
  36.0 0.6 slice_bitcast_fusion
  36.6 0.6 gather_fusion
  37.3 1.0 select_select_fusion
  38.3 5.3 all-to-all-start.1
  43.8 0.7 broadcast_in_dim.97
  44.5 1.1 reshape.409
  45.6 1.7 fusion.35
  47.5 2.1 fusion.64
  49.5 0.8 copy-done.5
  50.3 0.9 convolution_convert_fusion
  51.2 1.1 reshape.411
  52.3 11.6 %all-to-all-done.1 = bf16[4,2,32,1536]{3,2,1,0:T(8,128)(2,1)S(1)} async-done(((bf16[4,2,32,1536]{3,2,1,0:T(8,128)(2,1)}), bf16[4,2,32,1536]{3,2,1,0:T(8,128)(2,1)S(1)}, u32[]{:S(2)}, u32[]{:S(2)}) %all-to-all-start.1) | async-done | bytes 786464 | tf_op jit(solution)/shard_map/all_to_all | solution.py:73
  64.0 2.2 gather_fusion.1
  66.2 2.0 broadcast_select_fusion
  68.1 2.0 pad_maximum_fusion.2
  70.2 11.3 %reshape.408 = bf16[4,256,2,12,64]{4,3,2,1,0:T(8,128)(2,1)} reshape(bf16[4,4,2,32,1536]{4,3,2,1,0:T(8,128)(2,1)} %pad_maximum_fusion.2) | data formatting | bytes 6291456 | tf_op jit(solution)/shard_map/reshape | solution.py:79
  81.5 6.2 fusion.102
  87.6 5.3 copy.110
  92.9 4.4 copy.111
  97.3 1.8 multiply_select_fusion
  99.2 1.5 fusion.103
  100.8 1.6 fusion.21
  102.4 6.6 convolution_bitcast_fusion
  109.0 13.9 %reshape.449 = f32[4,4,2,32,768]{3,2,1,4,0:T(2,128)} reshape(f32[4,256,12,64]{1,3,2,0:T(8,128)} %convolution_bitcast_fusion) | data formatting | bytes 6291456 | tf_op jit(solution)/shard_map/reshape | solution.py:117
  122.8 17.4 %copy.96 = f32[4,4,2,32,768]{4,1,0,3,2:T(4,128)} copy(f32[4,4,2,32,768]{3,2,1,4,0:T(2,128)} %reshape.449) | data formatting | bytes 6291456 | tf_op jit(solution)/shard_map/reshape | solution.py:117
  140.3 13.1 %convolution_bitcast_fusion.1 = f32[4,256,12,64]{1,3,2,0:T(8,128)} fusion(f32[4,12,32,256]{3,2,1,0:T(8,128)} %fusion.21, bf16[4,32,12,64]{3,2,1,0:T(8,128)(2,1)S(1)} %copy-done.9, f32[4,12,32,256]{3,2,1,0:T(8,128)} %get-tuple-element.23, f32[4,12,32]{2,1,0:T(8,128)S(1)} %get-tuple-element.22), kind=kOutput, calls=%fused_computation.22 | convolution fusion | flops 53085952 | bytes 6494208 | tf_op jit(solution)/shard_map/uhqk,uqhd->ukhd/dot_general | solution.py:112
  153.4 13.9 %reshape.448 = f32[4,4,2,32,768]{3,2,1,4,0:T(2,128)} reshape(f32[4,256,12,64]{1,3,2,0:T(8,128)} %convolution_bitcast_fusion.1) | data formatting | bytes 6291456 | tf_op jit(solution)/shard_map/reshape | solution.py:117
  167.2 17.0 %copy.95 = f32[4,4,2,32,768]{4,1,0,3,2:T(4,128)} copy(f32[4,4,2,32,768]{3,2,1,4,0:T(2,128)} %reshape.448) | data formatting | bytes 6291456 | tf_op jit(solution)/shard_map/reshape | solution.py:117
  184.2 10.6 %fusion.10 = bf16[4,2,32,1536]{3,0,2,1:T(4,128)(2,1)S(1)} fusion(f32[4,4,2,32,768]{4,1,0,3,2:T(4,128)} %copy.96, f32[4,4,2,32,768]{4,1,0,3,2:T(4,128)} %copy.95, s32[4,3]{1,0:T(4,128)S(1)} %copy-done.27), kind=kOutput, calls=%fused_computation.18 | convolution fusion | flops 58196016 | bytes 7077936 | tf_op jit(solution)/shard_map/ujs,ujhwc->shwc/dot_general | solution.py:120
  194.8 1.0 copy.98
  195.9 3.7 all-to-all-start.2
  199.6 4.2 fusion.30
  204.2 14.9 %all-to-all-done.2 = bf16[4,2,32,1536]{3,2,1,0:T(8,128)(2,1)S(1)} async-done(((bf16[4,2,32,1536]{3,2,1,0:T(8,128)(2,1)}), bf16[4,2,32,1536]{3,2,1,0:T(8,128)(2,1)S(1)}, u32[]{:S(2)}, u32[]{:S(2)}) %all-to-all-start.2) | async-done | bytes 786464 | tf_op jit(solution)/shard_map/all_to_all | solution.py:123
  219.2 0.7 fusion.67
  220.4 1.3 copy.101
  221.8 0.7 copy-done.14
  222.5 4.6 fusion.53
  228.1 2.9 fusion.105
  231.1 0.9 copy-done.4
  232.6 11.2 %fusion.48 = bf16[4,32,12,64]{3,1,2,0:T(8,128)(2,1)S(1)} fusion(f32[4,12,32,256]{3,2,1,0:T(8,128)} %fusion.21, bf16[4,256,1,12,64]{1,4,3,0,2:T(8,128)(2,1)S(1)} %copy-done.3, f32[4,12,32,256]{3,2,1,0:T(8,128)} %get-tuple-element.23, f32[4,12,32]{2,1,0:T(8,128)S(1)} %copy-done.15), kind=kOutput, calls=%fused_computation.47 | convolution fusion | flops 53184256 | bytes 4921344 | tf_op jit(solution)/shard_map/uhqk,ukhd->uqhd/dot_general | solution.py:109
  244.3 3.0 fusion.104
  247.4 5.3 fusion.71
  252.7 1.1 copy-done.12
  253.8 4.2 fusion.73
  258.0 87.3 %reduce-scatter.14.cloned.1.call-done = f32[24,1536]{1,0:T(8,128)} async-done(((f32[768,1536]{1,0:T(8,128)}), f32[24,1536]{1,0:T(8,128)}) %reduce-scatter.14.cloned.1.call-update) | async-done | bytes 147472 | tf_op jit(solution)/shard_map/reduce_scatter | solution.py:140
  345.3 112.2 %reduce-scatter.6.cloned.1.call-done = f32[48,768]{1,0:T(8,128)} async-done(((f32[1536,768]{1,0:T(8,128)}), f32[48,768]{1,0:T(8,128)}) %reduce-scatter.6.cloned.1.call-update) | async-done | bytes 147472 | tf_op jit(solution)/shard_map/reduce_scatter | solution.py:137
  457.5 113.0 %reduce-scatter.12.cloned.1.call-done = f32[48,768]{1,0:T(8,128)} async-done(((f32[1536,768]{1,0:T(8,128)}), f32[48,768]{1,0:T(8,128)}) %reduce-scatter.12.cloned.1.call-update) | async-done | bytes 147472 | tf_op jit(solution)/shard_map/reduce_scatter | solution.py:139
  570.4 112.0 %reduce-scatter.10.cloned.1.call-done = f32[48,768]{1,0:T(8,128)} async-done(((f32[1536,768]{1,0:T(8,128)}), f32[48,768]{1,0:T(8,128)}) %reduce-scatter.10.cloned.1.call-update) | async-done | bytes 147472 | tf_op jit(solution)/shard_map/reduce_scatter | solution.py:138
  (101 shorter events, 4.7 us)
Async XLA Ops:
  7.2 21.5 %copy-start = (bf16[1536,768]{1,0:T(8,128)(2,1)S(1)}, bf16[1536,768]{1,0:T(8,128)(2,1)}, u32[]{:S(2)}) copy-start(bf16[1536,768]{1,0:T(8,128)(2,1)} %param.12) | copy-start | bytes 7077892
  7.2 38.5 %collective-permute-start.1 = (bf16[4,1,32,1536]{3,2,0,1:T(8,128)(2,1)}, bf16[4,1,32,1536]{3,2,0,1:T(8,128)(2,1)}, u32[]{:S(2)}, u32[]{:S(2)}) collective-permute-start(bf16[4,1,32,1536]{3,2,0,1:T(8,128)(2,1)} %bitcast.142), channel_id=1, source_target_pairs={{1,0},{3,2},{5,4},{7,6},{9,8},{11,10},{13,12},{15,14},{17,16},{19,... | collective-permute-start | bytes 1179656 | tf_op jit(solution)/shard_map/ppermute | solution.py:20
  8.6 37.0 %collective-permute-start = (bf16[4,1,32,1536]{3,2,0,1:T(8,128)(2,1)}, bf16[4,1,32,1536]{3,2,0,1:T(8,128)(2,1)}, u32[]{:S(2)}, u32[]{:S(2)}) collective-permute-start(bf16[4,1,32,1536]{3,2,0,1:T(8,128)(2,1)} %bitcast.143), channel_id=1, source_target_pairs={{0,1},{2,3},{4,5},{6,7},{8,9},{10,11},{12,13},{14,15},{16,17},{18,... | collective-permute-start | bytes 1179656 | tf_op jit(solution)/shard_map/ppermute | solution.py:19
  15.3 0.6 copy-start.26
  16.7 18.6 %all-to-all-start = ((s32[4,1,2]{2,1,0:T(1,128)}), s32[4,1,2]{2,1,0:T(1,128)}, u32[]{:S(2)}, u32[]{:S(2)}) async-start(s32[4,1,2]{2,1,0:T(1,128)} %copy.83), calls=%async_computation | async-start | bytes 4096 | tf_op jit(solution)/shard_map/all_to_all | solution.py:63
  25.6 4.3 copy-start.24
  28.7 1.7 copy-start.35
  36.6 1.7 copy-start.28
  37.3 6.3 copy-start.32
  37.3 6.4 copy-start.33
  37.3 7.2 %copy-start.11 = (bf16[128,768]{1,0:T(8,128)(2,1)S(1)}, bf16[128,768]{1,0:T(8,128)(2,1)}, u32[]{:S(2)}) copy-start(bf16[128,768]{1,0:T(8,128)(2,1)} %convolution_convert_fusion.1) | copy-start | bytes 589828
  38.3 25.7 %all-to-all-start.1 = ((bf16[4,2,32,1536]{3,2,1,0:T(8,128)(2,1)}), bf16[4,2,32,1536]{3,2,1,0:T(8,128)(2,1)S(1)}, u32[]{:S(2)}, u32[]{:S(2)}) async-start(bf16[4,2,32,1536]{3,2,1,0:T(8,128)(2,1)} %select_select_fusion), calls=%async_computation.1 | async-start | bytes 1572864 | tf_op jit(solution)/shard_map/all_to_all | solution.py:73
  44.5 2.9 copy-start.17
  44.5 2.9 copy-start.18
  44.5 2.9 copy-start.19
  44.5 2.9 copy-start.20
  44.5 2.9 copy-start.21
  44.5 2.9 copy-start.22
  44.5 2.9 copy-start.23
  45.6 1.8 copy-start.10
  47.4 2.9 copy-start.7
  49.5 0.8 copy-start.5
  52.3 13.8 %copy-start.31 = (pred[4,3]{1,0:T(4,128)(4,1)S(1)}, pred[4,3]{1,0:T(4,128)(4,1)}, u32[]{:S(2)}) copy-start(pred[4,3]{1,0:T(4,128)(4,1)} %get-tuple-element.13) | copy-start | bytes 40
  92.9 4.4 copy-start.9
  92.9 4.5 copy-start.30
  99.2 1.7 copy-start.2
  99.2 1.7 copy-start.8
  100.8 39.4 %copy-start.13 = (f32[4,12,32]{2,1,0:T(8,128)}, f32[4,12,32]{2,1,0:T(8,128)S(1)}, u32[]{:S(2)}) copy-start(f32[4,12,32]{2,1,0:T(8,128)S(1)} %get-tuple-element.22) | copy-start | bytes 18436
  167.2 17.0 %copy-start.27 = (s32[4,3]{1,0:T(4,128)S(1)}, s32[4,3]{1,0:T(4,128)}, u32[]{:S(2)}) copy-start(s32[4,3]{1,0:T(4,128)} %copy-done.26) | copy-start | bytes 148
  195.9 23.3 %all-to-all-start.2 = ((bf16[4,2,32,1536]{3,2,1,0:T(8,128)(2,1)}), bf16[4,2,32,1536]{3,2,1,0:T(8,128)(2,1)S(1)}, u32[]{:S(2)}, u32[]{:S(2)}) async-start(bf16[4,2,32,1536]{3,2,1,0:T(8,128)(2,1)} %copy.98), calls=%async_computation.3 | async-start | bytes 1572864 | tf_op jit(solution)/shard_map/all_to_all | solution.py:123
  199.5 47.8 %reduce-scatter.8.cloned.1.call-start = ((), (), s32[]{:S(2)}) async-start(), calls=%async_computation.9 | async-start | bytes 2359296 | tf_op jit(solution)/shard_map/reduce_scatter | solution.py:131
  203.8 15.4 %copy-start.29 = (pred[4]{0:T(512)(128)(4,1)S(1)}, pred[4]{0:T(512)(128)(4,1)}, u32[]{:S(2)}) copy-start(pred[4]{0:T(512)(128)(4,1)} %copy-done.28) | copy-start | bytes 16
  203.8 15.4 %copy-start.34 = (s32[4]{0:T(128)S(1)}, s32[4]{0:T(128)}, u32[]{:S(2)}) copy-start(s32[4]{0:T(128)} %get-tuple-element.17) | copy-start | bytes 52
  221.7 0.8 copy-start.14
  221.7 123.6 %reduce-scatter.14.cloned.1.call-start = ((), (), s32[]{:S(2)}) async-start(), calls=%async_computation.12 | async-start | bytes 4866048 | tf_op jit(solution)/shard_map/reduce_scatter | solution.py:140
  227.1 1.0 copy-start.6
  231.0 1.0 copy-start.4
  231.0 1.0 copy-start.16
  231.0 1.0 copy-start.25
  231.0 1.6 copy-start.3
  231.0 1.6 copy-start.15
  231.1 226.4 %reduce-scatter.6.cloned.1.call-start = ((), (), s32[]{:S(2)}) async-start(), calls=%async_computation.8 | async-start | bytes 4866048 | tf_op jit(solution)/shard_map/reduce_scatter | solution.py:137
  247.3 323.2 %reduce-scatter.12.cloned.1.call-start = ((), (), s32[]{:S(2)}) async-start(), calls=%async_computation.11 | async-start | bytes 4866048 | tf_op jit(solution)/shard_map/reduce_scatter | solution.py:139
  252.6 1.1 copy-start.12
  252.7 429.8 %reduce-scatter.10.cloned.1.call-start = ((), (), s32[]{:S(2)}) async-start(), calls=%async_computation.10 | async-start | bytes 4866048 | tf_op jit(solution)/shard_map/reduce_scatter | solution.py:138
  258.0 424.5 %copy-start.1 = (bf16[1536,768]{1,0:T(8,128)(2,1)S(1)}, bf16[1536,768]{1,0:T(8,128)(2,1)}, u32[]{:S(2)}) copy-start(bf16[1536,768]{1,0:T(8,128)(2,1)} %param.12) | copy-start | bytes 7077892
Sparse Core Ops, SparseCore 0:
  221.8 8.1 reduce-scatter.7
  237.0 108.2 reduce-scatter.13
  351.4 106.0 reduce-scatter.5
  464.3 106.1 reduce-scatter.11
  576.3 106.0 reduce-scatter.9
where the time goes:
time: 694 us; the launch traced here: 689 us
  waiting for transfers between devices  451 us (65%)
  local copies, waits for them, and re-layouts  107 us (15%)
  matrix products  70.1 us (10%)
  other arithmetic  22.2 us (3%)
  starting transfers between devices  21.4 us (3%)
  between operations  14.5 us (2%)
    reduce_scatter x1, waiting for transfers between devices, shards(): lax.psum_scatter(grad_value, ('scene', 'view', 'row'), scatter_dimension=...  113 us
    reduce_scatter x1, waiting for transfers between devices, shards(): lax.psum_scatter(grad_query, ('scene', 'view', 'row'), scatter_dimension=...  112 us
    reduce_scatter x1, waiting for transfers between devices, shards(): lax.psum_scatter(grad_key, ('scene', 'view', 'row'), scatter_dimension=0,...  112 us
    reduce_scatter x1, waiting for transfers between devices, shards(): lax.psum_scatter(grad_out, ('scene', 'view', 'row'), scatter_dimension=0,...  87.3 us
    reshape x2, local copies, waits for them, and re-layouts, shards(): dvalue.reshape(block_shape)  31.2 us
    reshape x2, local copies, waits for them, and re-layouts, shards(): dkey.reshape(block_shape)  30.8 us
    unnamed x75, local copies, waits for them, and re-layouts  16.2 us
    all_to_all x1, waiting for transfers between devices, shards(): lax.all_to_all(returned_part, 'view', split_axis=0, concat_axis=0, tiled=...  14.9 us
  transfers between devices with their start and end apart: 10, of which 6 were waited for; matrix products, arithmetic and copies ran while one was open for 9% of the time, Pallas kernels for 0%

commit v1 on v0

v1 whole, which is shorter than its diff:
```python
import functools

import jax
import jax.numpy as jnp
from jax import lax
from jax.experimental import pallas as pl
from jax.experimental.pallas import tpu as pltpu
from jax.sharding import PartitionSpec as P

HEAD_DIM = 64
EPSILON = 1e-06
MASKED = -1e30
MIB = 1024 * 1024

VMEM = pl.BlockSpec(memory_space=pltpu.VMEM)
SMEM = pl.BlockSpec(memory_space=pltpu.SMEM)


def dot_nn(a, b):
    return lax.dot_general(a, b, (((1,), (0,)), ((), ())), preferred_element_type=jnp.float32)


def dot_nt(a, b):
    return lax.dot_general(a, b, (((1,), (1,)), ((), ())), preferred_element_type=jnp.float32)


def dot_tn(a, b):
    return lax.dot_general(a, b, (((0,), (0,)), ((), ())), preferred_element_type=jnp.float32)


def normalized(tokens, gain):
    x = tokens.astype(jnp.float32)
    mean = jnp.mean(x * x, -1, keepdims=True)
    return (x * lax.rsqrt(mean + EPSILON) * gain).astype(jnp.bfloat16)


def request_kernel(views, slots, groups, partners, counts, request, alive):
    for g in range(groups):
        request[g] = 0
        for u in range(views):
            alive[g * views + u] = 0
    for u in range(views):
        for j in range(slots):

            @pl.when(j < counts[u])
            def _():
                partner = partners[u, j]
                group = lax.div(partner, jnp.int32(views))
                request[group] = lax.rem(partner, jnp.int32(views))
                alive[group * views + u] = 1


def project_kernel(
    scalars, lat_own, lat_other, cot_own, cot_other, gain, taps, w_q, w_k, w_v, w_o,
    normed, queries, keys, values, upstream, out_grad,
):
    views, strip, width = lat_own.shape
    for u in range(views):
        for half, source in enumerate((lat_own, lat_other)):
            start = (2 * u + half) * strip
            normed[start : start + strip, :] = normalized(source[u], gain[...])
    rows = normed[...]
    queries[...] = dot_nn(rows, w_q[...]).astype(jnp.bfloat16)
    keys[...] = dot_nn(rows, w_k[...]).astype(jnp.bfloat16)
    values[...] = dot_nn(rows, w_v[...]).astype(jnp.bfloat16)

    first = scalars[0] == 0
    chunk = 512
    column = lax.broadcasted_iota(jnp.int32, (strip, 1), 0)
    not_first = (column > 0).astype(jnp.float32)
    not_last = (column < strip - 1).astype(jnp.float32)
    for c in range(0, width, chunk):
        lanes = slice(c, c + chunk)
        tap = taps[:, lanes].astype(jnp.float32)
        top, middle, bottom = tap[0:3], tap[3:6], tap[6:9]
        cross = (jnp.where(first, top, bottom), jnp.where(first, bottom, top))
        for u in range(views):
            strips = [ref[u, :, lanes].astype(jnp.float32) for ref in (cot_own, cot_other)]
            shifted = []
            for x in strips:
                after = pltpu.roll(x, strip - 1, 0) * not_last
                before = pltpu.roll(x, 1, 0) * not_first
                shifted.append((after, x, before))
            for half in range(2):
                total = strips[half]
                for b in range(3):
                    total = total + middle[b : b + 1] * shifted[half][b]
                    total = total + cross[half][b : b + 1] * shifted[1 - half][b]
                start = (2 * u + half) * strip
                upstream[start : start + strip, lanes] = total.astype(jnp.bfloat16)
    out_grad[...] = dot_nt(upstream[...], w_o[...]).astype(jnp.bfloat16)


def attention_kernel(
    views, scalars, alive, got_own, got_other, normed, queries, keys, values, out_grad, gain, w_k, w_v,
    normed_all, mixed, dquery, dkey, dvalue,
):
    groups, strip, _ = got_own.shape
    tokens = queries.shape[0]
    view_tokens = tokens // views
    scale = HEAD_DIM ** (-0.5)
    here = scalars[1]
    normed_all[:tokens, :] = normed[...]
    pair = 2 * HEAD_DIM
    span = 2 * view_tokens
    column_view = lax.broadcasted_iota(jnp.int32, (1, views * span), 1) // span
    slot_alive = []
    for j in range(groups - 1):
        group = j + (j >= here).astype(jnp.int32)
        start = tokens + 2 * j * strip
        normed_all[start : start + strip, :] = normalized(got_own[group], gain[...])
        normed_all[start + strip : start + 2 * strip, :] = normalized(got_other[group], gain[...])
        taken = jnp.zeros((1, views * span), jnp.int32)
        for u in range(views):
            taken = jnp.where(column_view == u, alive[group * views + u], taken)
        slot_alive.append(taken > 0)
    fetched = normed_all[tokens:, :]
    fetched_keys = dot_nn(fetched, w_k[...]).astype(jnp.bfloat16)
    fetched_values = dot_nn(fetched, w_v[...]).astype(jnp.bfloat16)
    low = lax.broadcasted_iota(jnp.int32, (1, 1, pair), 2) < HEAD_DIM
    low_b = low.astype(jnp.bfloat16)
    high_b = 1 - low_b

    def stacked(x):
        x = x.reshape(views, view_tokens, pair)
        return jnp.concatenate((x * low_b, x * high_b), axis=1).reshape(views * span, pair)

    def unstacked(x):
        x = x.reshape(views, 2, view_tokens, pair)
        return jnp.where(low, x[:, 0], x[:, 1]).reshape(tokens, pair).astype(jnp.bfloat16)

    def own_nt(a, b):
        return jnp.concatenate(
            [
                dot_nt(a[u * view_tokens : (u + 1) * view_tokens], b[u * span : (u + 1) * span])
                for u in range(views)
            ],
            axis=1,
        )

    def own_tn(a, b):
        return jnp.concatenate(
            [
                dot_tn(a[:, u * span : (u + 1) * span], b[u * view_tokens : (u + 1) * view_tokens])
                for u in range(views)
            ],
            axis=0,
        )

    def own_nn(a, b):
        return jnp.concatenate(
            [
                dot_nn(a[:, u * span : (u + 1) * span], b[u * span : (u + 1) * span])
                for u in range(views)
            ],
            axis=0,
        )

    for p in range(queries.shape[1] // pair):
        lanes = slice(p * pair, (p + 1) * pair)
        q = stacked(queries[:, lanes])
        g = stacked(out_grad[:, lanes])
        k_own, v_own = keys[:, lanes], values[:, lanes]
        k_far, v_far = fetched_keys[:, lanes], fetched_values[:, lanes]
        s_own = own_nt(k_own, q) * scale
        s_far = dot_nt(k_far, q) * scale
        s_far = jnp.concatenate(
            [
                jnp.where(slot_alive[j], s_far[j * view_tokens : (j + 1) * view_tokens], MASKED)
                for j in range(groups - 1)
            ],
            axis=0,
        )
        highest = jnp.maximum(
            jnp.max(s_own, 0, keepdims=True), jnp.max(s_far, 0, keepdims=True)
        )
        e_own = jnp.exp(s_own - highest)
        e_far = jnp.exp(s_far - highest)
        inverse = 1.0 / (jnp.sum(e_own, 0, keepdims=True) + jnp.sum(e_far, 0, keepdims=True))
        a_own = e_own * inverse
        a_far = e_far * inverse
        ab_own = a_own.astype(jnp.bfloat16)
        ab_far = a_far.astype(jnp.bfloat16)
        mixed[:, lanes] = unstacked(own_tn(ab_own, v_own) + dot_tn(ab_far, v_far))
        dvalue[:tokens, lanes] = own_nn(ab_own, g).astype(jnp.bfloat16)
        dvalue[tokens:, lanes] = dot_nn(ab_far, g).astype(jnp.bfloat16)
        dp_own = own_nt(v_own, g)
        dp_far = dot_nt(v_far, g)
        delta = jnp.sum(a_own * dp_own, 0, keepdims=True) + jnp.sum(a_far * dp_far, 0, keepdims=True)
        ds_own = (a_own * (dp_own - delta) * scale).astype(jnp.bfloat16)
        ds_far = (a_far * (dp_far - delta) * scale).astype(jnp.bfloat16)
        dquery[:, lanes] = unstacked(own_tn(ds_own, k_own) + dot_tn(ds_far, k_far))
        dkey[:tokens, lanes] = own_nn(ds_own, q).astype(jnp.bfloat16)
        dkey[tokens:, lanes] = dot_nn(ds_far, q).astype(jnp.bfloat16)


def outer_kernel(first, scalars, left, right, send, keep):
    size = send.shape[1]
    other = right[...]
    for i in range(2):
        start = pl.multiple_of(scalars[first + i] * size, size)
        send[i] = dot_tn(left[:, pl.ds(start, size)], other).astype(jnp.bfloat16)
    for i in range(2):
        start = pl.multiple_of(scalars[first + 2 + i] * size, size)
        keep[i] = dot_tn(left[:, pl.ds(start, size)], other)


def out_kernel(strip, scalars, mine, theirs, upstream, send, keep):
    tokens, inner = mine.shape
    width = upstream.shape[1] // 2
    start = pl.multiple_of(scalars[0] * width, width)
    right = upstream[:, pl.ds(start, width)]
    swapped = theirs[...].reshape(tokens // (2 * strip), 2, strip, inner)
    swapped = jnp.concatenate((swapped[:, 1:], swapped[:, :1]), axis=1).reshape(tokens, inner)
    from_mine = dot_tn(mine[...], right)
    from_theirs = dot_tn(swapped, right)
    keep_mine = scalars[0] == scalars[2]
    send[...] = jnp.where(keep_mine, from_theirs, from_mine).astype(jnp.bfloat16)
    keep[...] = jnp.where(keep_mine, from_mine, from_theirs)


def params(mebibytes):
    return pltpu.CompilerParams(vmem_limit_bytes=mebibytes * MIB)


def shape(dims, kind):
    return jax.ShapeDtypeStruct(dims, kind)


def shards(latents, norm_gain, w_query, w_key, w_value, w_out, kernel, partners, counts, cotangent):
    views, strip_rows, columns, width = latents.shape[1:]
    inner = w_query.shape[1]
    groups, rows = lax.axis_size("view"), lax.axis_size("row")
    scenes = lax.axis_size("scene")
    assert (strip_rows, rows, scenes) == (1, 2, 4)
    strip = strip_rows * columns
    slots = partners.shape[2]
    part = inner // rows
    tokens = views * 2 * strip
    key_tokens = tokens + (groups - 1) * 2 * strip
    bf16, f32, i32 = jnp.bfloat16, jnp.float32, jnp.int32

    row, view, scene = lax.axis_index("row"), lax.axis_index("view"), lax.axis_index("scene")
    x, y = scene % 2, scene // 2
    scalars = jnp.stack(
        (
            row, view, y, x,
            1 - x, 3 - x, x, 2 + x,
            2 - 2 * y, 3 - 2 * y, 2 * y, 2 * y + 1,
        )
    ).astype(i32)
    swap = [(0, 1), (1, 0)]
    along_x = [(i, i ^ 1) for i in range(scenes)]
    along_y = [(i, i ^ 2) for i in range(scenes)]

    request, alive = pl.pallas_call(
        functools.partial(request_kernel, views, slots, groups),
        in_specs=[SMEM, SMEM],
        out_specs=(SMEM, SMEM),
        out_shape=(shape((groups,), i32), shape((groups * views,), i32)),
        name="requests",
    )(partners[0], counts[0])
    granted = lax.all_to_all(request, "view", split_axis=0, concat_axis=0, tiled=True)

    lat = latents[0].reshape(views, strip, width)
    cot = cotangent[0].reshape(views, strip, width)
    lat_other = lax.ppermute(lat, "row", swap)
    cot_other = lax.ppermute(cot, "row", swap)

    outgoing = jnp.take(lat, granted, axis=0, mode="clip")
    got_own = lax.all_to_all(outgoing, "view", split_axis=0, concat_axis=0, tiled=True)
    got_other = lax.ppermute(got_own, "row", swap)

    gain = norm_gain.reshape(1, width)
    half_columns = pl.BlockSpec((width, part), lambda i, s: (0, s[0]))
    half_rows = pl.BlockSpec((part, width), lambda i, s: (s[0], 0))

    def whole(dims):
        return pl.BlockSpec(dims, lambda i, s: (0,) * len(dims))

    strip_spec = whole((views, strip, width))
    token_spec, part_spec = whole((tokens, width)), whole((tokens, part))
    normed, queries, keys, values, upstream, out_grad = pl.pallas_call(
        project_kernel,
        grid_spec=pltpu.PrefetchScalarGridSpec(
            num_scalar_prefetch=1,
            grid=(1,),
            in_specs=[
                strip_spec, strip_spec, strip_spec, strip_spec, whole((1, width)), whole((9, width)),
                half_columns, half_columns, half_columns, half_rows,
            ],
            out_specs=[token_spec, part_spec, part_spec, part_spec, token_spec, part_spec],
        ),
        out_shape=[
            shape((tokens, width), bf16),
            shape((tokens, part), bf16),
            shape((tokens, part), bf16),
            shape((tokens, part), bf16),
            shape((tokens, width), bf16),
            shape((tokens, part), bf16),
        ],
        compiler_params=params(40),
        cost_estimate=pl.CostEstimate(
            flops=8 * tokens * width * part + 40 * tokens * width,
            bytes_accessed=8 * width * part + 16 * tokens * width,
            transcendentals=tokens,
        ),
        name="project",
    )(scalars, lat, lat_other, cot, cot_other, gain, kernel, w_query, w_key, w_value, w_out)

    normed_all, mixed, dquery, dkey, dvalue = pl.pallas_call(
        functools.partial(attention_kernel, views),
        grid_spec=pltpu.PrefetchScalarGridSpec(
            num_scalar_prefetch=2,
            grid=(1,),
            in_specs=[
                pl.BlockSpec((groups, strip, width), lambda i, s, a: (0, 0, 0)),
                pl.BlockSpec((groups, strip, width), lambda i, s, a: (0, 0, 0)),
                pl.BlockSpec((tokens, width), lambda i, s, a: (0, 0)),
                pl.BlockSpec((tokens, part), lambda i, s, a: (0, 0)),
                pl.BlockSpec((tokens, part), lambda i, s, a: (0, 0)),
                pl.BlockSpec((tokens, part), lambda i, s, a: (0, 0)),
                pl.BlockSpec((tokens, part), lambda i, s, a: (0, 0)),
                pl.BlockSpec((1, width), lambda i, s, a: (0, 0)),
                pl.BlockSpec((width, part), lambda i, s, a: (0, s[0])),
                pl.BlockSpec((width, part), lambda i, s, a: (0, s[0])),
            ],
            out_specs=[
                pl.BlockSpec((key_tokens, width), lambda i, s, a: (0, 0)),
                pl.BlockSpec((tokens, part), lambda i, s, a: (0, 0)),
                pl.BlockSpec((tokens, part), lambda i, s, a: (0, 0)),
                pl.BlockSpec((key_tokens, part), lambda i, s, a: (0, 0)),
                pl.BlockSpec((key_tokens, part), lambda i, s, a: (0, 0)),
            ],
        ),
        out_shape=[
            shape((key_tokens, width), bf16),
            shape((tokens, part), bf16),
            shape((tokens, part), bf16),
            shape((key_tokens, part), bf16),
            shape((key_tokens, part), bf16),
        ],
        compiler_params=params(44),
        cost_estimate=pl.CostEstimate(
            flops=4 * (key_tokens - tokens) * width * part + 24 * groups * 2 * strip * tokens * part,
            bytes_accessed=4 * width * part + 8 * key_tokens * width,
            transcendentals=groups * 2 * strip * tokens * part // HEAD_DIM,
        ),
        name="attention",
    )(
        scalars, alive, got_own, got_other, normed, queries, keys, values, out_grad, gain, w_key, w_value
    )
    mixed_other = lax.ppermute(mixed, "row", swap)

    def outer(left, right, first, name):
        blocks = (2, width // 4, part)
        return pl.pallas_call(
            functools.partial(outer_kernel, first),
            in_specs=[SMEM, VMEM, VMEM],
            out_specs=(VMEM, VMEM),
            out_shape=(shape(blocks, bf16), shape(blocks, f32)),
            compiler_params=params(24),
            cost_estimate=pl.CostEstimate(
                flops=2 * left.shape[0] * width * part,
                bytes_accessed=6 * width * part // 2 + 2 * left.shape[0] * (width + part),
                transcendentals=0,
            ),
            name=name,
        )(scalars, left, right)

    q_send, q_keep = outer(normed_all[:tokens], dquery, 4, "grad_query")
    k_send, k_keep = outer(normed_all, dkey, 4, "grad_key")
    v_send, v_keep = outer(normed_all, dvalue, 8, "grad_value")
    o_send, o_keep = pl.pallas_call(
        functools.partial(out_kernel, strip),
        in_specs=[SMEM, VMEM, VMEM, VMEM],
        out_specs=(VMEM, VMEM),
        out_shape=(shape((inner // 2, width // 2), bf16), shape((inner // 2, width // 2), f32)),
        compiler_params=params(24),
        cost_estimate=pl.CostEstimate(
            flops=2 * tokens * width * part,
            bytes_accessed=6 * width * part // 2 + 2 * tokens * (width + inner),
            transcendentals=0,
        ),
        name="grad_out",
    )(scalars, mixed, mixed_other, upstream)
    o_send = o_send.reshape(2, inner // 4, width // 2)
    o_keep = o_keep.reshape(2, inner // 4, width // 2)

    def summed(send, keep, order, index):
        got = lax.ppermute(send, "scene", order[0])
        later = lax.dynamic_index_in_dim(keep, 1 - index, 0, False) + lax.dynamic_index_in_dim(
            got, 1 - index, 0, False
        ).astype(f32)
        got_later = lax.ppermute(later.astype(bf16), "scene", order[1])
        mine = lax.dynamic_index_in_dim(keep, index, 0, False) + lax.dynamic_index_in_dim(
            got, index, 0, False
        ).astype(f32)
        mine = (mine + got_later.astype(f32)).astype(bf16)
        spread = mine.reshape(groups * rows, mine.shape[0] // (groups * rows), mine.shape[1])
        got = lax.all_to_all(spread, ("view", "row"), split_axis=0, concat_axis=0, tiled=True)
        got = got.reshape(groups, rows, spread.shape[1], spread.shape[2]).astype(f32)
        total = jnp.sum(got, axis=0)
        return jnp.moveaxis(total, 0, 1).reshape(spread.shape[1], rows * spread.shape[2])

    return (
        summed(q_send, q_keep, (along_x, along_y), y),
        summed(k_send, k_keep, (along_x, along_y), y),
        summed(v_send, v_keep, (along_y, along_x), x),
        summed(o_send, o_keep, (along_y, along_x), x),
    )


def solution(mesh):
    tokens = P("scene", "view", "row", None, None)
    everywhere = P()
    grads = P(("scene", "view", "row"), None)
    return jax.shard_map(
        shards,
        mesh=mesh,
        in_specs=(
            tokens, everywhere, everywhere, everywhere, everywhere, everywhere, everywhere,
            P("scene", "view", None), P("scene", "view"), tokens,
        ),
        out_specs=(grads, grads, grads, grads),
        check_vma=False,
    )
```

time: 694 us -> 141 us (0.20)
  waiting for transfers between devices: 451 us -> 47.9 us
  local copies, waits for them, and re-layouts: 107 us -> 19.3 us
  matrix products: 70.1 us -> 0 us
  Pallas kernels: 0 us -> 16.9 us
  between operations: 14.5 us -> 0.92 us
  blocking collectives: 2.37 us -> 11.7 us
  other arithmetic: 22.2 us -> 14 us
  starting transfers between devices: 21.4 us -> 29.3 us
    reduce_scatter x5 -> x0, waiting for transfers between devices: 424 us -> none  [the longest x1 113 us: shards(): lax.psum_scatter(grad_value, ('scene', 'view', 'row'), scatter_dimension=...]
    reshape x9 -> x5, local copies, waits for them, and re-layouts: 76.2 us -> 2.69 us  [the longest x4 2.69 us: summed(): jnp.moveaxis(total, 0, 1).reshape(spread.shape[1], rows * spread.shape[2])]
    dot_general x15 -> x0, matrix products: 70.1 us -> none  [the longest x1 13.1 us: shards(): jnp.einsum('uhqk,uqhd->ukhd', dscore, queries, preferred_element_type=jnp...]
    ppermute x2 -> x12, waiting for transfers between devices: 0.01 us -> 22.1 us  [the longest x4 16.2 us: summed(): got = lax.ppermute(send, 'scene', order[0])]
    pallas_call x0 -> x7, Pallas kernels: none -> 16.9 us  [the longest x3 5.15 us: outer(): pl.pallas_call(functools.partial(outer_kernel, first), in_specs=[SMEM, VM...]
    all_to_all x0 -> x1, blocking collectives: none -> 11.7 us  [shards(): lax.all_to_all(request, 'view', split_axis=0, concat_axis=0, tiled=True)]
    convert_element_type x5 -> x8, other arithmetic: 5.22 us -> 12.7 us  [the longest x4 7.28 us: summed(): mine = (mine + got_later.astype(f32)).astype(bf16)]
    all_to_all x2 -> x4, starting transfers between devices: 9.98 us -> 15.7 us  [summed(): lax.all_to_all(spread, ('view', 'row'), split_axis=0, concat_axis=0, tile...]
  transfers between devices with their start and end apart: 10 -> 17, of which waited for: 6 -> 8; matrix products, arithmetic and copies ran while one was open for 9% -> 11% of each run, Pallas kernels for 0% -> 7%
where the time goes in v1:
time: 141 us; the launch traced here: 140 us
  waiting for transfers between devices  47.9 us (34%)
  starting transfers between devices  29.3 us (21%)
  local copies, waits for them, and re-layouts  19.3 us (14%)
  Pallas kernels  16.9 us (12%)
  other arithmetic  14 us (10%)
  blocking collectives  11.7 us (8%)
    ppermute x4, waiting for transfers between devices, summed(): got = lax.ppermute(send, 'scene', order[0])  16.2 us
    all_to_all x4, waiting for transfers between devices, summed(): lax.all_to_all(spread, ('view', 'row'), split_axis=0, concat_axis=0, tile...  15.9 us
    all_to_all x4, starting transfers between devices, summed(): lax.all_to_all(spread, ('view', 'row'), split_axis=0, concat_axis=0, tile...  15.7 us
    unnamed x41, local copies, waits for them, and re-layouts  13.4 us
    all_to_all x1, blocking collectives, shards(): lax.all_to_all(request, 'view', split_axis=0, concat_axis=0, tiled=True)  11.7 us
    all_to_all x1, waiting for transfers between devices, shards(): lax.all_to_all(outgoing, 'view', split_axis=0, concat_axis=0, tiled=True)  9.91 us
    convert_element_type x4, other arithmetic, summed(): mine = (mine + got_later.astype(f32)).astype(bf16)  7.28 us
    ppermute x4, waiting for transfers between devices, summed(): got_later = lax.ppermute(later.astype(bf16), 'scene', order[1])  5.89 us
  transfers between devices with their start and end apart: 17, of which 8 were waited for; matrix products, arithmetic and copies ran while one was open for 11% of the time, Pallas kernels for 7%

profile of v1, /device:TPU:0, one launch (start us, length us, event | category | flops | bytes accessed | tf_op | source)
XLA Modules:
  0.0 140.0 jit_solution(7570057710194124338)
XLA Ops:
  0.6 0.0 copy-start.5
  0.7 1.4 %copy.17 = s32[1,4,3]{2,1,0:T(4,128)} copy(s32[1,4,3]{1,0,2:T(1,128)} %param.17) | data formatting | bytes 96 | tf_op args[7]
  2.1 1.3 requests.1
  3.4 0.7 copy.18
  4.1 11.7 %all_to_all.34 = s32[4,1,1]{2,1,0:T(1,128)S(1)} all-to-all(s32[4,1,1]{2,1,0:T(1,128)S(1)} %copy.18), channel_id=1, replica_groups=mesh['scene'=4,'view'=4,'row'=2] {'view'}, dimensions={0} | all-to-all | bytes 32 | tf_op jit(solution)/shard_map/all_to_all | solution.py:263
  15.8 0.2 reduce
  15.9 2.3 %gather_fusion = bf16[4,32,1536]{2,1,0:T(8,128)(2,1)} fusion(bf16[4,32,1536]{2,1,0:T(8,128)(2,1)} %bitcast.66, s32[1024]{0:T(1024)S(1)} %pad_clamp_fusion), kind=kCustom, calls=%fused_computation | custom fusion | bytes 786448 | tf_op jit(solution)/shard_map/jit(_take)/gather | solution.py:270
  18.2 3.5 %all-to-all-start.1 = ((bf16[4,32,1536]{2,1,0:T(8,128)(2,1)}), bf16[4,32,1536]{2,1,0:T(8,128)(2,1)S(1)}, u32[]{:S(2)}, u32[]{:S(2)}) async-start(bf16[4,32,1536]{2,1,0:T(8,128)(2,1)} %gather_fusion), calls=%async_computation.1 | async-start | bytes 786432 | tf_op jit(solution)/shard_map/all_to_all | solution.py:271
  21.7 0.1 collective-permute-start.1
  21.8 0.5 collective-permute-start.2
  22.3 9.9 %all-to-all-done.1.got_own = bf16[4,32,1536]{2,1,0:T(8,128)(2,1)S(1)} async-done(((bf16[4,32,1536]{2,1,0:T(8,128)(2,1)}), bf16[4,32,1536]{2,1,0:T(8,128)(2,1)S(1)}, u32[]{:S(2)}, u32[]{:S(2)}) %all-to-all-start.1) | async-done | bytes 393248 | tf_op jit(solution)/shard_map/all_to_all | solution.py:271
  32.2 0.0 collective-permute-start
  32.2 0.1 stack.48.scalars
  32.3 0.0 collective-permute-done.1.lat_other
  32.4 0.0 copy-start
  32.4 1.7 %copy-done = bf16[1536,768]{1,0:T(8,128)(2,1)S(1)} copy-done((bf16[1536,768]{1,0:T(8,128)(2,1)S(1)}, bf16[1536,768]{1,0:T(8,128)(2,1)}, u32[]{:S(2)}) %copy-start) | copy-done | bytes 2359320
  34.0 1.7 %copy-done.2 = bf16[1536,768]{1,0:T(8,128)(2,1)S(1)} copy-done((bf16[1536,768]{1,0:T(8,128)(2,1)S(1)}, bf16[1536,768]{1,0:T(8,128)(2,1)}, u32[]{:S(2)}) %copy-start.2) | copy-done | bytes 2359320
  35.7 1.7 %copy-done.3 = bf16[1536,768]{1,0:T(8,128)(2,1)S(1)} copy-done((bf16[1536,768]{1,0:T(8,128)(2,1)S(1)}, bf16[1536,768]{1,0:T(8,128)(2,1)}, u32[]{:S(2)}) %copy-start.3) | copy-done | bytes 2359320
  37.4 1.7 %copy-done.4 = bf16[768,1536]{1,0:T(8,128)(2,1)S(1)} copy-done((bf16[768,1536]{1,0:T(8,128)(2,1)S(1)}, bf16[768,1536]{1,0:T(8,128)(2,1)}, u32[]{:S(2)}) %copy-start.4) | copy-done | bytes 2359320
  39.0 3.2 %project.1 = (bf16[256,1536]{1,0:T(8,128)(2,1)S(1)}, bf16[256,384]{1,0:T(8,128)(2,1)S(1)}, bf16[256,384]{1,0:T(8,128)(2,1)S(1)}, bf16[256,384]{1,0:T(8,128)(2,1)...) custom-call(s32[12]{0:T(128)S(1)} %stack.48.scalars, bf16[4,32,1536]{2,1,0:T(8,128)(2,1)S(1)} %bitcast.68, ...), custom_call_target="tpu_custom_call" | custom-call | flops 1223688192 | bytes 11010048 | tf_op jit(solution)/shard_map/project/pallas_call | solution.py:283
  42.2 0.9 copy-done.6
  43.1 0.0 collective-permute-done.got_other
  43.1 5.0 %attention.1 = (bf16[448,1536]{1,0:T(8,128)(2,1)S(1)}, bf16[256,384]{1,0:T(8,128)(2,1)S(1)}, bf16[256,384]{1,0:T(8,128)(2,1)S(1)}, bf16[448,384]{1,0:T(8,128)(2,1)S(1)}, bf16[448,384]{1,0:T(8,128)(2,1)S(1)}) custom-call(s32[12]{0:T(128)S(1)} %stack.48.scalars, s32[16]{0:T(128)S(1)} %copy-done.14, bf16[4,32,1536]{2,1,0:T(8,128)(2,1)S(1)} %all-to-all-done.1.got_own, ...), custom_call_target="tpu_custom_call" | custom-call | flops 1056964608 | bytes 7864320 | tf_op jit(solution)/shard_map/attention/pallas_call | solution.py:311
  48.2 0.1 slice.3.left
  48.2 1.1 grad_query.1
  49.4 1.6 %collective-permute-start.3 = (bf16[2,384,384]{2,1,0:T(8,128)(2,1)S(1)}, bf16[2,384,384]{2,1,0:T(8,128)(2,1)S(1)}, u32[]{:S(2)}, u32[]{:S(2)}) collective-permute-start(bf16[2,384,384]{2,1,0:T(8,128)(2,1)S(1)} %get-tuple-element.35), channel_id=1, source_target_pairs={{0,8},{8,0},{16,24},{24,16},{1,9},{9,1},{17,25},{25,17},{2,10},{10... | collective-permute-start | bytes 1769480 | tf_op jit(solution)/shard_map/ppermute | solution.py:391
  51.0 2.0 %grad_value.1 = (bf16[2,384,384]{2,1,0:T(8,128)(2,1)}, f32[2,384,384]{2,1,0:T(8,128)S(1)}) custom-call(s32[12]{0:T(128)S(1)} %stack.48.scalars, bf16[448,1536]{1,0:T(8,128)(2,1)S(1)} %get-tuple-element.32.left, bf16[448,384]{1,0:T(8,128)(2,1)S(1)} %get-tuple-element.39.right), custom_call_target="tpu_custom_call" | custom-call | flops 528482304 | bytes 3489792 | tf_op jit(solution)/shard_map/grad_value/pallas_call | solution.py:357
  52.9 1.5 %collective-permute-start.7 = (bf16[2,384,384]{2,1,0:T(8,128)(2,1)}, bf16[2,384,384]{2,1,0:T(8,128)(2,1)}, u32[]{:S(2)}, u32[]{:S(2)}) collective-permute-start(bf16[2,384,384]{2,1,0:T(8,128)(2,1)} %get-tuple-element.41), channel_id=1, source_target_pairs={{0,16},{8,24},{16,0},{24,8},{1,17},{9,25},{17,1},{25,9},{2,18},{10... | collective-permute-start | bytes 1769480 | tf_op jit(solution)/shard_map/ppermute | solution.py:391
  54.5 10.9 %collective-permute-done.3 = bf16[2,384,384]{2,1,0:T(8,128)(2,1)S(1)} collective-permute-done((bf16[2,384,384]{2,1,0:T(8,128)(2,1)S(1)}, bf16[2,384,384]{2,1,0:T(8,128)(2,1)S(1)}, u32[]{:S(2)}, u32[]{:S(2)}) %collective-permute-start.3) | collective-permute-done | bytes 589856 | tf_op jit(solution)/shard_map/ppermute | solution.py:391
  65.4 0.9 fusion.4
  66.2 1.5 %collective-permute-start.4 = (bf16[384,384]{1,0:T(8,128)(2,1)}, bf16[384,384]{1,0:T(8,128)(2,1)}, u32[]{:S(2)}, u32[]{:S(2)}) collective-permute-start(bf16[384,384]{1,0:T(8,128)(2,1)} %fusion.4), channel_id=1, source_target_pairs={{0,16},{8,24},{16,0},{24,8},{1,17},{9,25},{17,1},{25,9},{2,18},{10... | collective-permute-start | bytes 884744 | tf_op jit(solution)/shard_map/ppermute | solution.py:395
  67.8 1.3 copy-done.9
  69.1 1.0 copy-done.16
  70.1 2.0 %grad_key.1 = (bf16[2,384,384]{2,1,0:T(8,128)(2,1)}, f32[2,384,384]{2,1,0:T(8,128)S(1)}) custom-call(s32[12]{0:T(128)S(1)} %stack.48.scalars, bf16[448,1536]{1,0:T(8,128)(2,1)S(1)} %copy-done.9, bf16[448,384]{1,0:T(8,128)(2,1)S(1)} %copy-done.16), custom_call_target="tpu_custom_call" | custom-call | flops 528482304 | bytes 3489792 | tf_op jit(solution)/shard_map/grad_key/pallas_call | solution.py:357
  72.1 1.5 %collective-permute-start.5 = (bf16[2,384,384]{2,1,0:T(8,128)(2,1)}, bf16[2,384,384]{2,1,0:T(8,128)(2,1)}, u32[]{:S(2)}, u32[]{:S(2)}) collective-permute-start(bf16[2,384,384]{2,1,0:T(8,128)(2,1)} %get-tuple-element.38), channel_id=1, source_target_pairs={{0,8},{8,0},{16,24},{24,16},{1,9},{9,1},{17,25},{25,17},{2,10},{10... | collective-permute-start | bytes 1769480 | tf_op jit(solution)/shard_map/ppermute | solution.py:391
  73.6 1.8 %fusion.6 = bf16[384,384]{1,0:T(8,128)(2,1)} fusion(f32[2,384,384]{2,1,0:T(8,128)S(1)} %get-tuple-element.40, s32[]{:T(128)S(6)} %select_n.44, bf16[2,384,384]{2,1,0:T(8,128)(2,1)} %collective-permute-done.7), kind=kLoop, calls=%fused_computation.19 | loop fusion | flops 442368 | bytes 1179652 | tf_op jit(solution)/shard_map/convert_element_type | solution.py:395
  75.4 0.5 collective-permute-start.8
  76.0 1.8 %fusion.3 = bf16[384,384]{1,0:T(8,128)(2,1)} fusion(bf16[384,384]{1,0:T(8,128)(2,1)} %collective-permute-done.4, f32[2,384,384]{2,1,0:T(8,128)S(1)} %get-tuple-element.34, s32[]{:T(128)S(6)} %select_n.41, bf16[2,384,384]{2,1,0:T(8,128)(2,1)S(1)} %copy-done.18), kind=kLoop, calls=%fused_computation.12 | loop fusion | flops 737280 | bytes 1474564 | tf_op jit(solution)/shard_map/convert_element_type | solution.py:399
  77.8 4.1 %all-to-all-start.2 = ((bf16[8,48,384]{2,1,0:T(8,128)(2,1)}), bf16[8,48,384]{2,1,0:T(8,128)(2,1)}, u32[]{:S(2)}, u32[]{:S(2)}) async-start(bf16[8,48,384]{2,1,0:T(8,128)(2,1)} %bitcast.76), calls=%async_computation.2 | async-start | bytes 589824 | tf_op jit(solution)/shard_map/all_to_all | solution.py:401
  81.8 1.1 copy-done.7
  83.0 0.9 copy-done.12
  83.9 2.3 %grad_out.1 = (bf16[384,768]{1,0:T(8,128)(2,1)}, f32[384,768]{1,0:T(8,128)S(1)}) custom-call(s32[12]{0:T(128)S(1)} %stack.48.scalars, bf16[256,384]{1,0:T(8,128)(2,1)S(1)} %copy-done.12, bf16[256,384]{1,0:T(8,128)(2,1)} %collective-permute-done.9.theirs, bf16[256,1536]{1,0:T(8,128)(2,1)S(1)} %copy-done.7), custom_call_target="tpu_custom_call" | custom-call | flops 301989888 | bytes 2949120 | tf_op jit(solution)/shard_map/grad_out/pallas_call | solution.py:374
  86.2 0.9 collective-permute-start.10
  87.1 1.6 %collective-permute-done.5 = bf16[2,384,384]{2,1,0:T(8,128)(2,1)} collective-permute-done((bf16[2,384,384]{2,1,0:T(8,128)(2,1)}, bf16[2,384,384]{2,1,0:T(8,128)(2,1)}, u32[]{:S(2)}, u32[]{:S(2)}) %collective-permute-start.5) | collective-permute-done | bytes 589856 | tf_op jit(solution)/shard_map/ppermute | solution.py:391
  88.7 1.7 %fusion.5 = bf16[384,384]{1,0:T(8,128)(2,1)} fusion(f32[2,384,384]{2,1,0:T(8,128)S(1)} %get-tuple-element.37, s32[]{:T(128)S(6)} %select_n.42, bf16[2,384,384]{2,1,0:T(8,128)(2,1)} %collective-permute-done.5), kind=kLoop, calls=%fused_computation.18 | loop fusion | flops 442368 | bytes 1179652 | tf_op jit(solution)/shard_map/convert_element_type | solution.py:395
  90.4 0.5 collective-permute-start.6
  90.9 2.7 %collective-permute-done.8 = bf16[384,384]{1,0:T(8,128)(2,1)} collective-permute-done((bf16[384,384]{1,0:T(8,128)(2,1)}, bf16[384,384]{1,0:T(8,128)(2,1)}, u32[]{:S(2)}, u32[]{:S(2)}) %collective-permute-start.8) | collective-permute-done | bytes 294944 | tf_op jit(solution)/shard_map/ppermute | solution.py:395
  93.6 1.9 %fusion.1 = bf16[384,384]{1,0:T(8,128)(2,1)} fusion(bf16[384,384]{1,0:T(8,128)(2,1)} %collective-permute-done.8, f32[2,384,384]{2,1,0:T(8,128)S(1)} %get-tuple-element.40, s32[]{:T(128)S(6)} %select_n.43, bf16[2,384,384]{2,1,0:T(8,128)(2,1)} %collective-permute-done.7), kind=kLoop, calls=%fused_computation.8 | loop fusion | flops 737280 | bytes 1474564 | tf_op jit(solution)/shard_map/convert_element_type | solution.py:399
  95.5 3.4 %all-to-all-start.4 = ((bf16[8,48,384]{2,1,0:T(8,128)(2,1)}), bf16[8,48,384]{2,1,0:T(8,128)(2,1)S(1)}, u32[]{:S(2)}, u32[]{:S(2)}) async-start(bf16[8,48,384]{2,1,0:T(8,128)(2,1)} %bitcast.77), calls=%async_computation.4 | async-start | bytes 589824 | tf_op jit(solution)/shard_map/all_to_all | solution.py:401
  98.9 3.7 %collective-permute-done.10 = bf16[2,192,768]{2,1,0:T(8,128)(2,1)} collective-permute-done((bf16[2,192,768]{2,1,0:T(8,128)(2,1)}, bf16[2,192,768]{2,1,0:T(8,128)(2,1)}, u32[]{:S(2)}, u32[]{:S(2)}) %collective-permute-start.10) | collective-permute-done | bytes 589856 | tf_op jit(solution)/shard_map/ppermute | solution.py:391
  102.6 1.0 fusion.7
  103.6 1.6 %collective-permute-start.11 = (bf16[192,768]{1,0:T(8,128)(2,1)S(1)}, bf16[192,768]{1,0:T(8,128)(2,1)S(1)}, u32[]{:S(2)}, u32[]{:S(2)}) collective-permute-start(bf16[192,768]{1,0:T(8,128)(2,1)S(1)} %fusion.7), channel_id=1, source_target_pairs={{0,8},{8,0},{16,24},{24,16},{1,9},{9,1},{17,25},{25,17},{2,10},{10... | collective-permute-start | bytes 884744 | tf_op jit(solution)/shard_map/ppermute | solution.py:395
  105.2 3.2 %collective-permute-done.6 = bf16[384,384]{1,0:T(8,128)(2,1)} collective-permute-done((bf16[384,384]{1,0:T(8,128)(2,1)}, bf16[384,384]{1,0:T(8,128)(2,1)}, u32[]{:S(2)}, u32[]{:S(2)}) %collective-permute-start.6) | collective-permute-done | bytes 294944 | tf_op jit(solution)/shard_map/ppermute | solution.py:395
  108.4 1.9 %fusion.2 = bf16[384,384]{1,0:T(8,128)(2,1)} fusion(bf16[384,384]{1,0:T(8,128)(2,1)} %collective-permute-done.6, f32[2,384,384]{2,1,0:T(8,128)S(1)} %get-tuple-element.37, s32[]{:T(128)S(6)} %select_n.41, bf16[2,384,384]{2,1,0:T(8,128)(2,1)} %collective-permute-done.5), kind=kLoop, calls=%fused_computation.10 | loop fusion | flops 737280 | bytes 1474564 | tf_op jit(solution)/shard_map/convert_element_type | solution.py:399
  110.3 4.8 %all-to-all-start.3 = ((bf16[8,48,384]{2,1,0:T(8,128)(2,1)}), bf16[8,48,384]{2,1,0:T(8,128)(2,1)S(1)}, u32[]{:S(2)}, u32[]{:S(2)}) async-start(bf16[8,48,384]{2,1,0:T(8,128)(2,1)} %bitcast.23), calls=%async_computation.3 | async-start | bytes 589824 | tf_op jit(solution)/shard_map/all_to_all | solution.py:401
  115.0 1.8 %fusion = bf16[192,768]{1,0:T(8,128)(2,1)} fusion(bf16[192,768]{1,0:T(8,128)(2,1)S(1)} %collective-permute-done.11, f32[2,192,768]{2,1,0:T(8,128)S(1)} %bitcast.70, s32[]{:T(128)S(6)} %select_n.43, bf16[2,192,768]{2,1,0:T(8,128)(2,1)} %collective-permute-done.10), kind=kLoop, calls=%fused_computation.6 | loop fusion | flops 737280 | bytes 1474564 | tf_op jit(solution)/shard_map/convert_element_type | solution.py:399
  116.8 8.7 %all-to-all-done.3 = bf16[8,48,384]{2,1,0:T(8,128)(2,1)S(1)} async-done(((bf16[8,48,384]{2,1,0:T(8,128)(2,1)}), bf16[8,48,384]{2,1,0:T(8,128)(2,1)S(1)}, u32[]{:S(2)}, u32[]{:S(2)}) %all-to-all-start.3) | async-done | bytes 294944 | tf_op jit(solution)/shard_map/all_to_all | solution.py:401
  125.5 3.4 %all-to-all-start.5 = ((bf16[8,24,768]{2,1,0:T(8,128)(2,1)}), bf16[8,24,768]{2,1,0:T(8,128)(2,1)S(1)}, u32[]{:S(2)}, u32[]{:S(2)}) async-start(bf16[8,24,768]{2,1,0:T(8,128)(2,1)} %bitcast.35), calls=%async_computation.5 | async-start | bytes 589824 | tf_op jit(solution)/shard_map/all_to_all | solution.py:401
  128.9 1.0 convert_reduce_fusion.3
  129.9 0.7 copy.23
  130.6 0.7 copy.25
  131.4 0.7 copy.24
  132.0 7.2 %all-to-all-done.5 = bf16[8,24,768]{2,1,0:T(8,128)(2,1)S(1)} async-done(((bf16[8,24,768]{2,1,0:T(8,128)(2,1)}), bf16[8,24,768]{2,1,0:T(8,128)(2,1)S(1)}, u32[]{:S(2)}, u32[]{:S(2)}) %all-to-all-start.5) | async-done | bytes 294944 | tf_op jit(solution)/shard_map/all_to_all | solution.py:401
  139.3 0.7 copy.26
  (42 shorter events, 0.2 us)
Async XLA Ops:
  0.6 21.1 %copy-start.5 = (bf16[1,4,1,32,1536]{4,3,2,1,0:T(8,128)(2,1)S(1)}, bf16[1,4,1,32,1536]{4,3,2,1,0:T(8,128)(2,1)}, u32[]{:S(2)}) copy-start(bf16[1,4,1,32,1536]{4,3,2,1,0:T(8,128)(2,1)} %param.10) | copy-start | bytes 1179652
  0.6 21.2 %copy-start.10 = (bf16[1,4,1,32,1536]{4,3,2,1,0:T(8,128)(2,1)S(1)}, bf16[1,4,1,32,1536]{4,3,2,1,0:T(8,128)(2,1)}, u32[]{:S(2)}) copy-start(bf16[1,4,1,32,1536]{4,3,2,1,0:T(8,128)(2,1)} %param.19) | copy-start | bytes 1179652
  0.7 31.6 %copy-start.19 = (f32[1536]{0:T(1024)S(1)}, f32[1536]{0:T(1024)}, u32[]{:S(2)}) copy-start(f32[1536]{0:T(1024)} %param.11) | copy-start | bytes 18436
  0.7 31.7 %copy-start.13 = (bf16[9,1536]{1,0:T(8,128)(2,1)S(1)}, bf16[9,1536]{1,0:T(8,128)(2,1)}, u32[]{:S(2)}) copy-start(bf16[9,1536]{1,0:T(8,128)(2,1)} %taps.1) | copy-start | bytes 82948
  18.2 14.0 %all-to-all-start.1 = ((bf16[4,32,1536]{2,1,0:T(8,128)(2,1)}), bf16[4,32,1536]{2,1,0:T(8,128)(2,1)S(1)}, u32[]{:S(2)}, u32[]{:S(2)}) async-start(bf16[4,32,1536]{2,1,0:T(8,128)(2,1)} %gather_fusion), calls=%async_computation.1 | async-start | bytes 786432 | tf_op jit(solution)/shard_map/all_to_all | solution.py:271
  21.7 10.6 %collective-permute-start.1 = (bf16[4,32,1536]{2,1,0:T(8,128)(2,1)S(1)}, bf16[4,32,1536]{2,1,0:T(8,128)(2,1)S(1)}, u32[]{:S(2)}, u32[]{:S(2)}) collective-permute-start(bf16[4,32,1536]{2,1,0:T(8,128)(2,1)S(1)} %bitcast.67), channel_id=1, source_target_pairs={{0,1},{1,0},{2,3},{3,2},{4,5},{5,4},{6,7},{7,6},{8,9},{9,8},{10,11... | collective-permute-start | bytes 1179656 | tf_op jit(solution)/shard_map/ppermute | solution.py:267
  21.8 10.5 %collective-permute-start.2 = (bf16[4,32,1536]{2,1,0:T(8,128)(2,1)S(1)}, bf16[4,32,1536]{2,1,0:T(8,128)(2,1)S(1)}, u32[]{:S(2)}, u32[]{:S(2)}) collective-permute-start(bf16[4,32,1536]{2,1,0:T(8,128)(2,1)S(1)} %bitcast.71), channel_id=1, source_target_pairs={{0,1},{1,0},{2,3},{3,2},{4,5},{5,4},{6,7},{7,6},{8,9},{9,8},{10,11... | collective-permute-start | bytes 1179656 | tf_op jit(solution)/shard_map/ppermute | solution.py:268
  32.2 10.9 %collective-permute-start = (bf16[4,32,1536]{2,1,0:T(8,128)(2,1)S(1)}, bf16[4,32,1536]{2,1,0:T(8,128)(2,1)S(1)}, u32[]{:S(2)}, u32[]{:S(2)}) collective-permute-start(bf16[4,32,1536]{2,1,0:T(8,128)(2,1)S(1)} %all-to-all-done.1.got_own), channel_id=1, source_target_pairs={{0,1},{1,0},{2,3},{3,2},{4,5},{5,4},{6,7},{7,6},{8,9},{9,8},{10,11... | collective-permute-start | bytes 1179656 | tf_op jit(solution)/shard_map/ppermute | solution.py:272
  32.2 10.9 %copy-start.14 = (s32[16]{0:T(128)S(1)}, s32[16]{0:T(128)}, u32[]{:S(2)}) copy-start(s32[16]{0:T(128)} %get-tuple-element.25.alive) | copy-start | bytes 196
  32.4 1.7 %copy-start = (bf16[1536,768]{1,0:T(8,128)(2,1)S(1)}, bf16[1536,768]{1,0:T(8,128)(2,1)}, u32[]{:S(2)}) copy-start(bf16[1536,768]{1,0:T(8,128)(2,1)} %w_k.3) | copy-start | bytes 7077892
  34.0 1.7 %copy-start.2 = (bf16[1536,768]{1,0:T(8,128)(2,1)S(1)}, bf16[1536,768]{1,0:T(8,128)(2,1)}, u32[]{:S(2)}) copy-start(bf16[1536,768]{1,0:T(8,128)(2,1)} %w_v.3) | copy-start | bytes 7077892
  35.7 1.7 %copy-start.3 = (bf16[1536,768]{1,0:T(8,128)(2,1)S(1)}, bf16[1536,768]{1,0:T(8,128)(2,1)}, u32[]{:S(2)}) copy-start(bf16[1536,768]{1,0:T(8,128)(2,1)} %w_q.1) | copy-start | bytes 7077892
  37.4 1.7 %copy-start.4 = (bf16[768,1536]{1,0:T(8,128)(2,1)S(1)}, bf16[768,1536]{1,0:T(8,128)(2,1)}, u32[]{:S(2)}) copy-start(bf16[768,1536]{1,0:T(8,128)(2,1)} %w_o.1) | copy-start | bytes 7077892
  39.0 4.1 %copy-start.1 = (bf16[1536,768]{1,0:T(8,128)(2,1)S(1)}, bf16[1536,768]{1,0:T(8,128)(2,1)}, u32[]{:S(2)}) copy-start(bf16[1536,768]{1,0:T(8,128)(2,1)} %w_k.3) | copy-start | bytes 7077892
  42.2 0.9 copy-start.6
  48.1 1.2 copy-start.11
  48.1 1.2 copy-start.15
  48.2 2.8 %copy-start.8 = (bf16[448,1536]{1,0:T(8,128)(2,1)}, bf16[448,1536]{1,0:T(8,128)(2,1)S(1)}, u32[]{:S(2)}) copy-start(bf16[448,1536]{1,0:T(8,128)(2,1)S(1)} %get-tuple-element.32.left) | copy-start | bytes 4128772
  49.4 16.0 %collective-permute-start.3 = (bf16[2,384,384]{2,1,0:T(8,128)(2,1)S(1)}, bf16[2,384,384]{2,1,0:T(8,128)(2,1)S(1)}, u32[]{:S(2)}, u32[]{:S(2)}) collective-permute-start(bf16[2,384,384]{2,1,0:T(8,128)(2,1)S(1)} %get-tuple-element.35), channel_id=1, source_target_pairs={{0,8},{8,0},{16,24},{24,16},{1,9},{9,1},{17,25},{25,17},{2,10},{10... | collective-permute-start | bytes 1769480 | tf_op jit(solution)/shard_map/ppermute | solution.py:391
  52.9 20.7 %collective-permute-start.7 = (bf16[2,384,384]{2,1,0:T(8,128)(2,1)}, bf16[2,384,384]{2,1,0:T(8,128)(2,1)}, u32[]{:S(2)}, u32[]{:S(2)}) collective-permute-start(bf16[2,384,384]{2,1,0:T(8,128)(2,1)} %get-tuple-element.41), channel_id=1, source_target_pairs={{0,16},{8,24},{16,0},{24,8},{1,17},{9,25},{17,1},{25,9},{2,18},{10... | collective-permute-start | bytes 1769480 | tf_op jit(solution)/shard_map/ppermute | solution.py:391
  65.4 2.4 %copy-start.17 = (bf16[2,384,384]{2,1,0:T(8,128)(2,1)}, bf16[2,384,384]{2,1,0:T(8,128)(2,1)S(1)}, u32[]{:S(2)}) copy-start(bf16[2,384,384]{2,1,0:T(8,128)(2,1)S(1)} %collective-permute-done.3) | copy-start | bytes 1769476
  66.2 9.7 %collective-permute-start.4 = (bf16[384,384]{1,0:T(8,128)(2,1)}, bf16[384,384]{1,0:T(8,128)(2,1)}, u32[]{:S(2)}, u32[]{:S(2)}) collective-permute-start(bf16[384,384]{1,0:T(8,128)(2,1)} %fusion.4), channel_id=1, source_target_pairs={{0,16},{8,24},{16,0},{24,8},{1,17},{9,25},{17,1},{25,9},{2,18},{10... | collective-permute-start | bytes 884744 | tf_op jit(solution)/shard_map/ppermute | solution.py:395
  67.8 1.3 copy-start.9
  69.1 1.0 copy-start.16
  72.1 16.6 %collective-permute-start.5 = (bf16[2,384,384]{2,1,0:T(8,128)(2,1)}, bf16[2,384,384]{2,1,0:T(8,128)(2,1)}, u32[]{:S(2)}, u32[]{:S(2)}) collective-permute-start(bf16[2,384,384]{2,1,0:T(8,128)(2,1)} %get-tuple-element.38), channel_id=1, source_target_pairs={{0,8},{8,0},{16,24},{24,16},{1,9},{9,1},{17,25},{25,17},{2,10},{10... | collective-permute-start | bytes 1769480 | tf_op jit(solution)/shard_map/ppermute | solution.py:391
  73.6 2.4 %copy-start.18 = (bf16[2,384,384]{2,1,0:T(8,128)(2,1)S(1)}, bf16[2,384,384]{2,1,0:T(8,128)(2,1)}, u32[]{:S(2)}) copy-start(bf16[2,384,384]{2,1,0:T(8,128)(2,1)} %copy-done.17) | copy-start | bytes 1769476
  73.6 8.2 %collective-permute-start.9 = (bf16[256,384]{1,0:T(8,128)(2,1)}, bf16[256,384]{1,0:T(8,128)(2,1)}, u32[]{:S(2)}, u32[]{:S(2)}) collective-permute-start(bf16[256,384]{1,0:T(8,128)(2,1)} %copy-done.11), channel_id=1, source_target_pairs={{0,1},{1,0},{2,3},{3,2},{4,5},{5,4},{6,7},{7,6},{8,9},{9,8},{10,11... | collective-permute-start | bytes 589832 | tf_op jit(solution)/shard_map/ppermute | solution.py:353
  75.4 18.2 %collective-permute-start.8 = (bf16[384,384]{1,0:T(8,128)(2,1)}, bf16[384,384]{1,0:T(8,128)(2,1)}, u32[]{:S(2)}, u32[]{:S(2)}) collective-permute-start(bf16[384,384]{1,0:T(8,128)(2,1)} %fusion.6), channel_id=1, source_target_pairs={{0,8},{8,0},{16,24},{24,16},{1,9},{9,1},{17,25},{25,17},{2,10},{10... | collective-permute-start | bytes 884744 | tf_op jit(solution)/shard_map/ppermute | solution.py:395
  77.8 17.7 %all-to-all-start.2 = ((bf16[8,48,384]{2,1,0:T(8,128)(2,1)}), bf16[8,48,384]{2,1,0:T(8,128)(2,1)}, u32[]{:S(2)}, u32[]{:S(2)}) async-start(bf16[8,48,384]{2,1,0:T(8,128)(2,1)} %bitcast.76), calls=%async_computation.2 | async-start | bytes 589824 | tf_op jit(solution)/shard_map/all_to_all | solution.py:401
  81.8 1.1 copy-start.7
  83.0 0.9 copy-start.12
  86.2 16.5 %collective-permute-start.10 = (bf16[2,192,768]{2,1,0:T(8,128)(2,1)}, bf16[2,192,768]{2,1,0:T(8,128)(2,1)}, u32[]{:S(2)}, u32[]{:S(2)}) collective-permute-start(bf16[2,192,768]{2,1,0:T(8,128)(2,1)} %bitcast.32), channel_id=1, source_target_pairs={{0,16},{8,24},{16,0},{24,8},{1,17},{9,25},{17,1},{25,9},{2,18},{10... | collective-permute-start | bytes 1769480 | tf_op jit(solution)/shard_map/ppermute | solution.py:391
  90.4 18.0 %collective-permute-start.6 = (bf16[384,384]{1,0:T(8,128)(2,1)}, bf16[384,384]{1,0:T(8,128)(2,1)}, u32[]{:S(2)}, u32[]{:S(2)}) collective-permute-start(bf16[384,384]{1,0:T(8,128)(2,1)} %fusion.5), channel_id=1, source_target_pairs={{0,16},{8,24},{16,0},{24,8},{1,17},{9,25},{17,1},{25,9},{2,18},{10... | collective-permute-start | bytes 884744 | tf_op jit(solution)/shard_map/ppermute | solution.py:395
  95.5 14.8 %all-to-all-start.4 = ((bf16[8,48,384]{2,1,0:T(8,128)(2,1)}), bf16[8,48,384]{2,1,0:T(8,128)(2,1)S(1)}, u32[]{:S(2)}, u32[]{:S(2)}) async-start(bf16[8,48,384]{2,1,0:T(8,128)(2,1)} %bitcast.77), calls=%async_computation.4 | async-start | bytes 589824 | tf_op jit(solution)/shard_map/all_to_all | solution.py:401
  103.6 11.4 %collective-permute-start.11 = (bf16[192,768]{1,0:T(8,128)(2,1)S(1)}, bf16[192,768]{1,0:T(8,128)(2,1)S(1)}, u32[]{:S(2)}, u32[]{:S(2)}) collective-permute-start(bf16[192,768]{1,0:T(8,128)(2,1)S(1)} %fusion.7), channel_id=1, source_target_pairs={{0,8},{8,0},{16,24},{24,16},{1,9},{9,1},{17,25},{25,17},{2,10},{10... | collective-permute-start | bytes 884744 | tf_op jit(solution)/shard_map/ppermute | solution.py:395
  110.3 15.2 %all-to-all-start.3 = ((bf16[8,48,384]{2,1,0:T(8,128)(2,1)}), bf16[8,48,384]{2,1,0:T(8,128)(2,1)S(1)}, u32[]{:S(2)}, u32[]{:S(2)}) async-start(bf16[8,48,384]{2,1,0:T(8,128)(2,1)} %bitcast.23), calls=%async_computation.3 | async-start | bytes 589824 | tf_op jit(solution)/shard_map/all_to_all | solution.py:401
  125.5 13.8 %all-to-all-start.5 = ((bf16[8,24,768]{2,1,0:T(8,128)(2,1)}), bf16[8,24,768]{2,1,0:T(8,128)(2,1)S(1)}, u32[]{:S(2)}, u32[]{:S(2)}) async-start(bf16[8,24,768]{2,1,0:T(8,128)(2,1)} %bitcast.35), calls=%async_computation.5 | async-start | bytes 589824 | tf_op jit(solution)/shard_map/all_to_all | solution.py:401

commit v2 on v1

v2 whole, which is shorter than its diff:
```python
import functools

import jax
import jax.numpy as jnp
from jax import lax
from jax.experimental import pallas as pl
from jax.experimental.pallas import tpu as pltpu
from jax.sharding import PartitionSpec as P

HEAD_DIM = 64
EPSILON = 1e-06
MASKED = -1e30
MIB = 1024 * 1024

VMEM = pl.BlockSpec(memory_space=pltpu.VMEM)
HBM = pl.BlockSpec(memory_space=pltpu.HBM)
SMEM = pl.BlockSpec(memory_space=pltpu.SMEM)


def dot_nn(a, b):
    return lax.dot_general(a, b, (((1,), (0,)), ((), ())), preferred_element_type=jnp.float32)


def dot_nt(a, b):
    return lax.dot_general(a, b, (((1,), (1,)), ((), ())), preferred_element_type=jnp.float32)


def dot_tn(a, b):
    return lax.dot_general(a, b, (((0,), (0,)), ((), ())), preferred_element_type=jnp.float32)


def normalized(tokens, gain):
    x = tokens.astype(jnp.float32)
    mean = jnp.mean(x * x, -1, keepdims=True)
    return (x * lax.rsqrt(mean + EPSILON) * gain).astype(jnp.bfloat16)


def request_kernel(views, slots, groups, partners, counts, request, alive):
    for g in range(groups):
        request[g] = 0
        for u in range(views):
            alive[g * views + u] = 0
    for u in range(views):
        for j in range(slots):

            @pl.when(j < counts[0, u])
            def _():
                partner = partners[0, u, j]
                group = lax.div(partner, jnp.int32(views))
                request[group] = lax.rem(partner, jnp.int32(views))
                alive[group * views + u] = 1


def pick_kernel(groups, scalars, *refs):
    requests, lat, outgoing = refs[: groups - 1], refs[groups - 1], refs[groups:]
    for request, out in zip(requests, outgoing):
        out[...] = lat[request[scalars[1]]]


def weight_copy(scalars, source, target, arrived, index, axis):
    size = target.shape[axis]
    half = pl.ds(pl.multiple_of(scalars[0] * size, size), size)
    part = source.at[:, half] if axis == 1 else source.at[half, :]
    return pltpu.make_async_copy(part, target, arrived.at[index])


def project_kernel(
    scalars, lat_own, lat_other, cot_own, cot_other, gain, taps, w_query, w_key, w_value, w_out,
    normed, queries, keys, values, upstream, out_grad, up_half, *refs,
):
    quarters, (w_q, w_k, w_v, w_o, arrived) = refs[:4], refs[4:]
    views, strip, width = lat_own.shape
    copies = [
        weight_copy(scalars, w_query, w_q, arrived, 0, 1),
        weight_copy(scalars, w_key, w_k, arrived, 1, 1),
        weight_copy(scalars, w_value, w_v, arrived, 2, 1),
        weight_copy(scalars, w_out, w_o, arrived, 3, 0),
    ]
    for copy in copies:
        copy.start()
    row = scalars[0]

    def strip_of(u, half):
        index = 2 * u + (row if half == 0 else 1 - row)
        return pl.ds(pl.multiple_of(index * strip, strip), strip)

    for u in range(views):
        for half, source in enumerate((lat_own, lat_other)):
            normed[strip_of(u, half), :] = normalized(source[u], gain[...])
    first = row == 0
    chunk = 512
    column = lax.broadcasted_iota(jnp.int32, (strip, 1), 0)
    not_first = (column > 0).astype(jnp.float32)
    not_last = (column < strip - 1).astype(jnp.float32)
    for c in range(0, width, chunk):
        lanes = slice(c, c + chunk)
        tap = taps[:, lanes].astype(jnp.float32)
        top, middle, bottom = tap[0:3], tap[3:6], tap[6:9]
        cross = (jnp.where(first, top, bottom), jnp.where(first, bottom, top))
        for u in range(views):
            strips = [ref[u, :, lanes].astype(jnp.float32) for ref in (cot_own, cot_other)]
            shifted = []
            for x in strips:
                after = pltpu.roll(x, strip - 1, 0) * not_last
                before = pltpu.roll(x, 1, 0) * not_first
                shifted.append((after, x, before))
            for half in range(2):
                total = strips[half]
                for b in range(3):
                    total = total + middle[b : b + 1] * shifted[half][b]
                    total = total + cross[half][b : b + 1] * shifted[1 - half][b]
                upstream[strip_of(u, half), lanes] = total.astype(jnp.bfloat16)
    size = width // 4
    for m, quarter in enumerate(quarters):
        start = pl.multiple_of(lax.bitwise_xor(scalars[2], jnp.int32(m)) * size, size)
        quarter[...] = normed[:, pl.ds(start, size)]
    up_half[...] = upstream[:, pl.ds(pl.multiple_of(row * (width // 2), width // 2), width // 2)]
    rows = normed[...]
    for copy, weight, result in zip(copies, (w_q, w_k, w_v), (queries, keys, values)):
        copy.wait()
        result[...] = dot_nn(rows, weight[...]).astype(jnp.bfloat16)
    copies[3].wait()
    out_grad[...] = dot_nt(upstream[...], w_o[...]).astype(jnp.bfloat16)


def attention_kernel(views, groups, scalars, alive, *refs):
    got_own, got_other, refs = refs[: groups - 1], refs[groups - 1 : 2 * groups - 2], refs[2 * groups - 2 :]
    normed, queries, keys, values, out_grad, gain, w_key, w_value, *refs = refs
    normed_all, mixed_t, dquery, dkey, dvalue, w_k, w_v, arrived = refs
    copies = [
        weight_copy(scalars, w_key, w_k, arrived, 0, 1),
        weight_copy(scalars, w_value, w_v, arrived, 1, 1),
    ]
    for copy in copies:
        copy.start()
    strip = got_own[0].shape[0]
    tokens = queries.shape[0]
    view_tokens = tokens // views
    scale = HEAD_DIM ** (-0.5)
    here = scalars[1]
    normed_all[:tokens, :] = normed[...]
    pair = 2 * HEAD_DIM
    span = 2 * view_tokens
    column_view = lax.broadcasted_iota(jnp.int32, (1, views * span), 1) // span
    slot_alive = []
    for j in range(groups - 1):
        group = lax.bitwise_xor(here, jnp.int32(j + 1))
        start = tokens + 2 * j * strip
        normed_all[start : start + strip, :] = normalized(got_own[j][...], gain[...])
        normed_all[start + strip : start + 2 * strip, :] = normalized(got_other[j][...], gain[...])
        taken = jnp.zeros((1, views * span), jnp.int32)
        for u in range(views):
            taken = jnp.where(column_view == u, alive[group * views + u], taken)
        slot_alive.append(taken > 0)
    fetched = normed_all[tokens:, :]
    for copy in copies:
        copy.wait()
    fetched_keys = dot_nn(fetched, w_k[...]).astype(jnp.bfloat16)
    fetched_values = dot_nn(fetched, w_v[...]).astype(jnp.bfloat16)
    low = lax.broadcasted_iota(jnp.int32, (1, 1, pair), 2) < HEAD_DIM
    low_b = low.astype(jnp.bfloat16)
    high_b = 1 - low_b

    def stacked(x):
        x = x.reshape(views, view_tokens, pair)
        return jnp.concatenate((x * low_b, x * high_b), axis=1).reshape(views * span, pair)

    def unstacked(x):
        x = x.reshape(views, 2, view_tokens, pair)
        return jnp.where(low, x[:, 0], x[:, 1]).reshape(tokens, pair)

    def own_nt(a, b):
        return jnp.concatenate(
            [
                dot_nt(a[u * view_tokens : (u + 1) * view_tokens], b[u * span : (u + 1) * span])
                for u in range(views)
            ],
            axis=1,
        )

    def own_tn(a, b):
        return jnp.concatenate(
            [
                dot_tn(a[:, u * span : (u + 1) * span], b[u * view_tokens : (u + 1) * view_tokens])
                for u in range(views)
            ],
            axis=0,
        )

    def own_nn(a, b):
        return jnp.concatenate(
            [
                dot_nn(a[:, u * span : (u + 1) * span], b[u * span : (u + 1) * span])
                for u in range(views)
            ],
            axis=0,
        )

    for p in range(queries.shape[1] // pair):
        lanes = slice(p * pair, (p + 1) * pair)
        q = stacked(queries[:, lanes])
        g = stacked(out_grad[:, lanes])
        k_own, v_own = keys[:, lanes], values[:, lanes]
        k_far, v_far = fetched_keys[:, lanes], fetched_values[:, lanes]
        s_own = own_nt(k_own, q) * scale
        s_far = dot_nt(k_far, q) * scale
        s_far = jnp.concatenate(
            [
                jnp.where(slot_alive[j], s_far[j * view_tokens : (j + 1) * view_tokens], MASKED)
                for j in range(groups - 1)
            ],
            axis=0,
        )
        highest = jnp.maximum(
            jnp.max(s_own, 0, keepdims=True), jnp.max(s_far, 0, keepdims=True)
        )
        e_own = jnp.exp(s_own - highest)
        e_far = jnp.exp(s_far - highest)
        inverse = 1.0 / (jnp.sum(e_own, 0, keepdims=True) + jnp.sum(e_far, 0, keepdims=True))
        a_own = e_own * inverse
        a_far = e_far * inverse
        ab_own = a_own.astype(jnp.bfloat16)
        ab_far = a_far.astype(jnp.bfloat16)
        mix = unstacked(own_tn(ab_own, v_own) + dot_tn(ab_far, v_far))
        mixed_t[lanes, :] = mix.T.astype(jnp.bfloat16)
        dvalue[:tokens, lanes] = own_nn(ab_own, g).astype(jnp.bfloat16)
        dvalue[tokens:, lanes] = dot_nn(ab_far, g).astype(jnp.bfloat16)
        dp_own = own_nt(v_own, g)
        dp_far = dot_nt(v_far, g)
        delta = jnp.sum(a_own * dp_own, 0, keepdims=True) + jnp.sum(a_far * dp_far, 0, keepdims=True)
        ds_own = (a_own * (dp_own - delta) * scale).astype(jnp.bfloat16)
        ds_far = (a_far * (dp_far - delta) * scale).astype(jnp.bfloat16)
        dq = unstacked(own_tn(ds_own, k_own) + dot_tn(ds_far, k_far))
        dquery[:, lanes] = dq.astype(jnp.bfloat16)
        dkey[:tokens, lanes] = own_nn(ds_own, q).astype(jnp.bfloat16)
        dkey[tokens:, lanes] = dot_nn(ds_far, q).astype(jnp.bfloat16)


def key_value_kernel(scalars, left, dkey, dvalue, k_send, v_send, k_keep, v_keep):
    size = k_send.shape[1]
    x, y = scalars[3], scalars[4]
    for side, (k_out, v_out) in enumerate(((k_send, v_send), (k_keep, v_keep))):
        x_out = x if side else 1 - x
        y_out = y if side else 1 - y
        for right, result, blocks in (
            (dkey, k_out, (x_out, 2 + x_out)),
            (dvalue, v_out, (2 * y_out, 2 * y_out + 1)),
        ):
            for i, block in enumerate(blocks):
                columns = pl.ds(pl.multiple_of(block * size, size), size)
                result[i] = dot_tn(left[:, columns], right[...]).astype(result.dtype)


def half_sum_kernel(scalars, k_keep, k_got, v_keep, v_got, k_later, v_later, k_now, v_now):
    x, y = scalars[3], scalars[4]
    for index, keep, got, later, now in ((y, k_keep, k_got, k_later, k_now), (x, v_keep, v_got, v_later, v_now)):
        later[...] = (keep[1 - index] + got[1 - index].astype(jnp.float32)).astype(jnp.bfloat16)
        now[...] = keep[index] + got[index].astype(jnp.float32)


def pack_kernel(k_now, k_got, v_now, v_got, packed):
    size = k_now.shape[1]
    packed[:, :size] = (k_now[...] + k_got[...].astype(jnp.float32)).astype(jnp.bfloat16)
    packed[:, size:] = (v_now[...] + v_got[...].astype(jnp.float32)).astype(jnp.bfloat16)


def unpack_kernel(rows, packed, key, value):
    sources, _, both = packed.shape
    size = both // 2
    for r in range(rows):
        total = packed[r].astype(jnp.float32)
        for i in range(r + rows, sources, rows):
            total = total + packed[i].astype(jnp.float32)
        key[:, r * size : (r + 1) * size] = total[:, :size]
        value[:, r * size : (r + 1) * size] = total[:, size:]


def share_kernel(scalars, mine, theirs, *quarters):
    size = quarters[0].shape[0]
    for m, quarter in enumerate(quarters):
        scene = lax.bitwise_xor(scalars[2], jnp.int32(m))
        owner, place = lax.div(scene, jnp.int32(2)), lax.rem(scene, jnp.int32(2))
        rows = pl.ds(pl.multiple_of(place * size, size), size)
        is_mine = owner == scalars[0]

        @pl.when(is_mine)
        def _():
            quarter[...] = mine[rows, :]

        @pl.when(jnp.logical_not(is_mine))
        def _():
            quarter[...] = theirs[rows, :]


def query_out_kernel(*refs):
    normed, dquery, mixed_t, up_half, packed = refs[0:4], refs[4:8], refs[8:12], refs[12:16], refs[16]
    grad_q = dot_tn(normed[0][...], dquery[0][...])
    grad_o = dot_nn(mixed_t[0][...], up_half[0][...])
    for m in range(1, 4):
        grad_q = grad_q + dot_tn(normed[m][...], dquery[m][...])
        grad_o = grad_o + dot_nn(mixed_t[m][...], up_half[m][...])
    targets, size, _ = packed.shape
    for i in range(targets):
        packed[i] = jnp.concatenate(
            (
                grad_o[i * size : (i + 1) * size],
                grad_q[2 * i * size : (2 * i + 1) * size],
                grad_q[(2 * i + 1) * size : (2 * i + 2) * size],
            ),
            axis=1,
        ).astype(jnp.bfloat16)


def unpack_query_out_kernel(rows, packed, query, out):
    sources, size, width = packed.shape
    half, quarter = width // 2, width // 4
    for r in range(rows):
        total = packed[r].astype(jnp.float32)
        for i in range(r + rows, sources, rows):
            total = total + packed[i].astype(jnp.float32)
        out[:, r * half : (r + 1) * half] = total[:, :half]
        columns = slice(r * quarter, (r + 1) * quarter)
        query[:size, columns] = total[:, half : half + quarter]
        query[size:, columns] = total[:, half + quarter :]


def params(mebibytes):
    return pltpu.CompilerParams(vmem_limit_bytes=mebibytes * MIB)


def shape(dims, kind):
    return jax.ShapeDtypeStruct(dims, kind)


def shards(latents, norm_gain, w_query, w_key, w_value, w_out, kernel, partners, counts, cotangent):
    views, strip_rows, columns, width = latents.shape[1:]
    inner = w_query.shape[1]
    groups, rows = lax.axis_size("view"), lax.axis_size("row")
    scenes = lax.axis_size("scene")
    assert (strip_rows, rows, scenes) == (1, 2, 4)
    strip = strip_rows * columns
    slots = partners.shape[2]
    part = inner // rows
    tokens = views * 2 * strip
    key_tokens = tokens + (groups - 1) * 2 * strip
    bf16, f32, i32 = jnp.bfloat16, jnp.float32, jnp.int32

    row, view, scene = lax.axis_index("row"), lax.axis_index("view"), lax.axis_index("scene")
    scalars = jnp.stack((row, view, scene, scene % 2, scene // 2)).astype(i32)
    swap = [(0, 1), (1, 0)]
    across = [[(i, i ^ m) for i in range(scenes)] for m in range(scenes)]
    along_x, along_y = across[1], across[2]

    request, alive = pl.pallas_call(
        functools.partial(request_kernel, views, slots, groups),
        in_specs=[SMEM, SMEM],
        out_specs=(SMEM, SMEM),
        out_shape=(shape((groups,), i32), shape((groups * views,), i32)),
        name="requests",
    )(partners, counts)
    between = [[(i, i ^ d) for i in range(groups)] for d in range(1, groups)]
    granted = [lax.ppermute(request, "view", pairs) for pairs in between]

    lat = latents[0].reshape(views, strip, width)
    cot = cotangent[0].reshape(views, strip, width)
    lat_other = lax.ppermute(lat, "row", swap)
    cot_other = lax.ppermute(cot, "row", swap)

    outgoing = pl.pallas_call(
        functools.partial(pick_kernel, groups),
        in_specs=[SMEM] * groups + [VMEM],
        out_specs=[VMEM] * (groups - 1),
        out_shape=[shape((strip, width), bf16)] * (groups - 1),
        compiler_params=params(8),
        name="pick",
    )(scalars, *granted, lat)
    got_own = [lax.ppermute(part_out, "view", pairs) for part_out, pairs in zip(outgoing, between)]
    got_other = [lax.ppermute(got, "row", swap) for got in got_own]

    gain = norm_gain.reshape(1, width)
    normed, queries, keys, values, upstream, out_grad, up_half, *quarters = pl.pallas_call(
        project_kernel,
        in_specs=[SMEM] + [VMEM] * 6 + [HBM] * 4,
        out_specs=[VMEM] * 11,
        out_shape=[
            shape((tokens, width), bf16),
            shape((tokens, part), bf16),
            shape((tokens, part), bf16),
            shape((tokens, part), bf16),
            shape((tokens, width), bf16),
            shape((tokens, part), bf16),
            shape((tokens, width // 2), bf16),
        ]
        + [shape((tokens, width // 4), bf16)] * 4,
        scratch_shapes=[
            pltpu.VMEM((width, part), bf16),
            pltpu.VMEM((width, part), bf16),
            pltpu.VMEM((width, part), bf16),
            pltpu.VMEM((part, width), bf16),
            pltpu.SemaphoreType.DMA((4,)),
        ],
        compiler_params=params(28),
        cost_estimate=pl.CostEstimate(
            flops=8 * tokens * width * part + 40 * tokens * width,
            bytes_accessed=8 * width * part + 16 * tokens * width,
            transcendentals=tokens,
        ),
        name="project",
    )(scalars, lat, lat_other, cot, cot_other, gain, kernel, w_query, w_key, w_value, w_out)

    normed_far = [quarters[0]] + [lax.ppermute(quarters[m], "scene", across[m]) for m in range(1, 4)]
    up_far = [up_half] + [lax.ppermute(up_half, "scene", across[m]) for m in range(1, 4)]

    normed_all, mixed_t, dquery, dkey, dvalue = pl.pallas_call(
        functools.partial(attention_kernel, views, groups),
        in_specs=[SMEM] * 2 + [VMEM] * (2 * groups - 2 + 6) + [HBM] * 2,
        out_specs=[VMEM] * 5,
        out_shape=[
            shape((key_tokens, width), bf16),
            shape((part, tokens), bf16),
            shape((tokens, part), bf16),
            shape((key_tokens, part), bf16),
            shape((key_tokens, part), bf16),
        ],
        scratch_shapes=[
            pltpu.VMEM((width, part), bf16),
            pltpu.VMEM((width, part), bf16),
            pltpu.SemaphoreType.DMA((2,)),
        ],
        compiler_params=params(24 + groups),
        cost_estimate=pl.CostEstimate(
            flops=4 * (key_tokens - tokens) * width * part + 24 * groups * 2 * strip * tokens * part,
            bytes_accessed=4 * width * part + 8 * key_tokens * width,
            transcendentals=groups * 2 * strip * tokens * part // HEAD_DIM,
        ),
        name="attention",
    )(
        scalars, alive, *got_own, *got_other, normed, queries, keys, values, out_grad, gain, w_key, w_value
    )
    quarter = width // 4
    two, one = (2, quarter, part), (quarter, part)
    k_send, v_send, k_keep, v_keep = pl.pallas_call(
        key_value_kernel,
        in_specs=[SMEM] + [VMEM] * 3,
        out_specs=[VMEM] * 4,
        out_shape=[shape(two, bf16)] * 2 + [shape(two, f32)] * 2,
        compiler_params=params(24),
        cost_estimate=pl.CostEstimate(
            flops=4 * key_tokens * width * part, bytes_accessed=12 * width * part, transcendentals=0
        ),
        name="grad_key_value",
    )(scalars, normed_all, dkey, dvalue)
    k_got = lax.ppermute(k_send, "scene", along_x)
    v_got = lax.ppermute(v_send, "scene", along_y)

    mixed_other = lax.ppermute(mixed_t, "row", swap)
    dquery_far = [dquery] + [lax.ppermute(dquery, "scene", across[m]) for m in range(1, 4)]
    shares = pl.pallas_call(
        share_kernel,
        in_specs=[SMEM] + [VMEM] * 2,
        out_specs=[VMEM] * 4,
        out_shape=[shape((inner // 4, tokens), bf16)] * 4,
        compiler_params=params(8),
        name="share_mixed",
    )(scalars, mixed_t, mixed_other)
    mixed_far = [shares[0]] + [lax.ppermute(shares[m], "scene", across[m]) for m in range(1, 4)]
    targets = groups * rows
    q_rows, o_rows = width // (4 * targets), inner // (4 * targets)
    packed = pl.pallas_call(
        query_out_kernel,
        in_specs=[VMEM] * 16,
        out_specs=VMEM,
        out_shape=shape((targets, o_rows, width), bf16),
        compiler_params=params(16),
        cost_estimate=pl.CostEstimate(
            flops=4 * tokens * width * part, bytes_accessed=8 * tokens * width, transcendentals=0
        ),
        name="grad_query_out",
    )(*normed_far, *dquery_far, *mixed_far, *up_far)
    packed = lax.all_to_all(packed, ("view", "row"), split_axis=0, concat_axis=0, tiled=True)
    grad_query, grad_out = pl.pallas_call(
        functools.partial(unpack_query_out_kernel, rows),
        in_specs=[VMEM],
        out_specs=[VMEM] * 2,
        out_shape=[shape((q_rows, inner), f32), shape((o_rows, width), f32)],
        compiler_params=params(8),
        name="sum_query_out",
    )(packed)

    k_later, v_later, k_now, v_now = pl.pallas_call(
        half_sum_kernel,
        in_specs=[SMEM] + [VMEM] * 4,
        out_specs=[VMEM] * 4,
        out_shape=[shape(one, bf16)] * 2 + [shape(one, f32)] * 2,
        compiler_params=params(16),
        name="sum_first",
    )(scalars, k_keep, k_got, v_keep, v_got)
    k_got = lax.ppermute(k_later, "scene", along_y)
    v_got = lax.ppermute(v_later, "scene", along_x)
    packed = pl.pallas_call(
        pack_kernel,
        in_specs=[VMEM] * 4,
        out_specs=VMEM,
        out_shape=shape((quarter, 2 * part), bf16),
        compiler_params=params(16),
        name="sum_second",
    )(k_now, k_got, v_now, v_got)
    packed = packed.reshape(targets, q_rows, 2 * part)
    packed = lax.all_to_all(packed, ("view", "row"), split_axis=0, concat_axis=0, tiled=True)
    grad_key, grad_value = pl.pallas_call(
        functools.partial(unpack_kernel, rows),
        in_specs=[VMEM],
        out_specs=[VMEM] * 2,
        out_shape=[shape((q_rows, inner), f32)] * 2,
        compiler_params=params(8),
        name="sum_key_value",
    )(packed)
    return grad_query, grad_key, grad_value, grad_out


def solution(mesh):
    tokens = P("scene", "view", "row", None, None)
    everywhere = P()
    grads = P(("scene", "view", "row"), None)
    return jax.shard_map(
        shards,
        mesh=mesh,
        in_specs=(
            tokens, everywhere, everywhere, everywhere, everywhere, everywhere, everywhere,
            P("scene", "view", None), P("scene", "view"), tokens,
        ),
        out_specs=(grads, grads, grads, grads),
        check_vma=False,
    )
```

time: 141 us -> 144 us (1.021)
  waiting for transfers between devices: 47.9 us -> 68.2 us
  other arithmetic: 14 us -> 0 us
  starting transfers between devices: 29.3 us -> 41.4 us
  blocking collectives: 11.7 us -> 0 us
  local copies, waits for them, and re-layouts: 19.3 us -> 12.6 us
  Pallas kernels: 16.9 us -> 20.5 us
    ppermute x10 -> x26, waiting for transfers between devices: 22.1 us -> 52.2 us  [the longest x3 18.1 us: shards(): lax.ppermute(dquery, 'scene', across[m])]
    ppermute x10 -> x26, starting transfers between devices: 9.66 us -> 32.4 us  [the longest x3 5.66 us: shards(): lax.ppermute(up_half, 'scene', across[m])]
    convert_element_type x8 -> x0, other arithmetic: 12.7 us -> none  [the longest x4 7.28 us: summed(): mine = (mine + got_later.astype(f32)).astype(bf16)]
    all_to_all x1 -> x0, blocking collectives: 11.7 us -> none  [shards(): lax.all_to_all(request, 'view', split_axis=0, concat_axis=0, tiled=True)]
    all_to_all x5 -> x2, starting transfers between devices: 19.1 us -> 8.41 us  [shards(): lax.all_to_all(packed, ('view', 'row'), split_axis=0, concat_axis=0, tile...]
    all_to_all x5 -> x2, waiting for transfers between devices: 25.8 us -> 16 us  [shards(): lax.all_to_all(packed, ('view', 'row'), split_axis=0, concat_axis=0, tile...]
    pallas_call x6 -> x10, Pallas kernels: 15.6 us -> 19.2 us  [the longest x1 5.38 us: shards(): pl.pallas_call(functools.partial(attention_kernel, views, groups), in_spe...]
    reshape x4 -> x0, local copies, waits for them, and re-layouts: 2.69 us -> none  [summed(): jnp.moveaxis(total, 0, 1).reshape(spread.shape[1], rows * spread.shape[2])]
  transfers between devices with their start and end apart: 17 -> 30, of which waited for: 8 -> 13; matrix products, arithmetic and copies ran while one was open for 11% -> 1% of each run, Pallas kernels for 7% -> 13%
where the time goes in v2:
time: 144 us; the launch traced here: 143 us
  waiting for transfers between devices  68.2 us (47%)
  starting transfers between devices  41.4 us (29%)
  Pallas kernels  20.5 us (14%)
  local copies, waits for them, and re-layouts  12.6 us (9%)
    ppermute x3, waiting for transfers between devices, shards(): lax.ppermute(dquery, 'scene', across[m])  18.1 us
    all_to_all x2, waiting for transfers between devices, shards(): lax.all_to_all(packed, ('view', 'row'), split_axis=0, concat_axis=0, tile...  16 us
    ppermute x1, waiting for transfers between devices, shards(): k_got = lax.ppermute(k_send, 'scene', along_x)  12.9 us
    unnamed x23, local copies, waits for them, and re-layouts  11.8 us
    all_to_all x2, starting transfers between devices, shards(): lax.all_to_all(packed, ('view', 'row'), split_axis=0, concat_axis=0, tile...  8.41 us
    ppermute x1, waiting for transfers between devices, shards(): k_got = lax.ppermute(k_later, 'scene', along_y)  5.93 us
    ppermute x3, starting transfers between devices, shards(): lax.ppermute(up_half, 'scene', across[m])  5.66 us
    ppermute x3, starting transfers between devices, shards(): granted = [lax.ppermute(request, 'view', pairs) for pairs in between]  5.66 us
  transfers between devices with their start and end apart: 30, of which 13 were waited for; matrix products, arithmetic and copies ran while one was open for 1% of the time, Pallas kernels for 13%

profile of v2, /device:TPU:0, one launch (start us, length us, event | category | flops | bytes accessed | tf_op | source)
XLA Modules:
  0.0 143.5 jit_solution(8028607235896837835)
XLA Ops:
  0.6 0.5 collective-permute-start
  1.1 0.1 collective-permute-start.1
  1.2 1.3 copy.14.partners
  2.6 1.3 requests.1
  3.9 3.1 %collective-permute-start.5 = (s32[4]{0:T(128)}, s32[4]{0:T(128)S(1)}, u32[]{:S(2)}, u32[]{:S(2)}) collective-permute-start(s32[4]{0:T(128)} %get-tuple-element.45), channel_id=1, source_target_pairs={{0,2},{2,0},{4,6},{6,4},{1,3},{3,1},{5,7},{7,5},{8,10},{10,8},{12,... | collective-permute-start | bytes 56 | tf_op jit(solution)/shard_map/ppermute | solution.py:362
  6.9 2.6 %collective-permute-start.6 = (s32[4]{0:T(128)}, s32[4]{0:T(128)S(1)}, u32[]{:S(2)}, u32[]{:S(2)}) collective-permute-start(s32[4]{0:T(128)} %get-tuple-element.45), channel_id=1, source_target_pairs={{0,4},{2,6},{4,0},{6,2},{1,5},{3,7},{5,1},{7,3},{8,12},{10,14},{12... | collective-permute-start | bytes 56 | tf_op jit(solution)/shard_map/ppermute | solution.py:362
  9.5 0.0 collective-permute-start.7
  9.5 0.1 stack.23.scalars
  9.6 2.0 %collective-permute-done.6.refs_1_ = s32[4]{0:T(128)S(1)} collective-permute-done((s32[4]{0:T(128)}, s32[4]{0:T(128)S(1)}, u32[]{:S(2)}, u32[]{:S(2)}) %collective-permute-start.6) | collective-permute-done | bytes 48 | tf_op jit(solution)/shard_map/ppermute | solution.py:362
  11.6 3.5 %collective-permute-done.7.refs_2_ = s32[4]{0:T(128)S(1)} collective-permute-done((s32[4]{0:T(128)}, s32[4]{0:T(128)S(1)}, u32[]{:S(2)}, u32[]{:S(2)}) %collective-permute-start.7) | collective-permute-done | bytes 48 | tf_op jit(solution)/shard_map/ppermute | solution.py:362
  15.1 1.0 copy-done.6
  16.1 0.6 pick.1
  16.7 0.1 collective-permute-start.8
  16.7 0.6 collective-permute-start.9
  17.3 3.8 %collective-permute-start.10 = (bf16[32,1536]{1,0:T(8,128)(2,1)S(1)}, bf16[32,1536]{1,0:T(8,128)(2,1)S(1)}, u32[]{:S(2)}, u32[]{:S(2)}) collective-permute-start(bf16[32,1536]{1,0:T(8,128)(2,1)S(1)} %get-tuple-element.48), channel_id=1, source_target_pairs={{0,6},{2,4},{4,2},{6,0},{1,7},{3,5},{5,3},{7,1},{8,14},{10,12},{12... | collective-permute-start | bytes 294920 | tf_op jit(solution)/shard_map/ppermute | solution.py:377
  21.1 0.7 reshape.14.gain.refs_11_
  21.8 0.9 collective-permute-done.8.refs_0_
  22.7 0.0 collective-permute-start.11
  22.7 3.2 %collective-permute-done.9.refs_1_ = bf16[32,1536]{1,0:T(8,128)(2,1)S(1)} collective-permute-done((bf16[32,1536]{1,0:T(8,128)(2,1)S(1)}, bf16[32,1536]{1,0:T(8,128)(2,1)S(1)}, u32[]{:S(2)}, u32[]{:S(2)}) %collective-permute-start.9) | collective-permute-done | bytes 98336 | tf_op jit(solution)/shard_map/ppermute | solution.py:377
  25.9 0.0 collective-permute-start.12
  25.9 0.5 collective-permute-start.13
  26.4 1.7 %copy-done = bf16[1536,768]{1,0:T(8,128)(2,1)S(1)} copy-done((bf16[1536,768]{1,0:T(8,128)(2,1)S(1)}, bf16[1536,768]{1,0:T(8,128)(2,1)}, u32[]{:S(2)}) %copy-start) | copy-done | bytes 2359320
  28.1 1.7 %copy-done.2 = bf16[1536,768]{1,0:T(8,128)(2,1)S(1)} copy-done((bf16[1536,768]{1,0:T(8,128)(2,1)S(1)}, bf16[1536,768]{1,0:T(8,128)(2,1)}, u32[]{:S(2)}) %copy-start.2) | copy-done | bytes 2359320
  29.8 1.7 %copy-done.4 = bf16[1536,768]{1,0:T(8,128)(2,1)S(1)} copy-done((bf16[1536,768]{1,0:T(8,128)(2,1)S(1)}, bf16[1536,768]{1,0:T(8,128)(2,1)}, u32[]{:S(2)}) %copy-start.4) | copy-done | bytes 2359320
  31.4 1.7 %copy-done.5 = bf16[768,1536]{1,0:T(8,128)(2,1)S(1)} copy-done((bf16[768,1536]{1,0:T(8,128)(2,1)S(1)}, bf16[768,1536]{1,0:T(8,128)(2,1)}, u32[]{:S(2)}) %copy-start.5) | copy-done | bytes 2359320
  33.1 1.0 copy-done.7
  34.1 1.0 copy-done.8
  35.1 0.8 copy-done.9
  35.9 5.3 %project.1 = (bf16[256,1536]{1,0:T(8,128)(2,1)S(1)}, bf16[256,384]{1,0:T(8,128)(2,1)S(1)}, bf16[256,384]{1,0:T(8,128)(2,1)S(1)}, bf16[256,384]{1,0:T(8,128)(2,1)...) custom-call(s32[5]{0:T(128)S(1)} %stack.23.scalars, ...), custom_call_target="tpu_custom_call" | custom-call | flops 1223688192 | bytes 11010048 | tf_op jit(solution)/shard_map/project/pallas_call | solution.py:381
  41.2 1.6 %collective-permute-start.2 = (bf16[256,384]{1,0:T(8,128)(2,1)S(1)}, bf16[256,384]{1,0:T(8,128)(2,1)S(1)}, u32[]{:S(2)}, u32[]{:S(2)}) collective-permute-start(bf16[256,384]{1,0:T(8,128)(2,1)S(1)} %get-tuple-element.41), channel_id=1, source_target_pairs={{0,8},{8,0},{16,24},{24,16},{1,9},{9,1},{17,25},{25,17},{2,10},{10... | collective-permute-start | bytes 589832 | tf_op jit(solution)/shard_map/ppermute | solution.py:411
  42.7 1.5 %collective-permute-start.3 = (bf16[256,384]{1,0:T(8,128)(2,1)S(1)}, bf16[256,384]{1,0:T(8,128)(2,1)S(1)}, u32[]{:S(2)}, u32[]{:S(2)}) collective-permute-start(bf16[256,384]{1,0:T(8,128)(2,1)S(1)} %get-tuple-element.42), channel_id=1, source_target_pairs={{0,16},{8,24},{16,0},{24,8},{1,17},{9,25},{17,1},{25,9},{2,18},{10... | collective-permute-start | bytes 589832 | tf_op jit(solution)/shard_map/ppermute | solution.py:411
  44.3 0.5 collective-permute-start.4
  44.8 5.4 %attention.1 = (bf16[448,1536]{1,0:T(8,128)(2,1)S(1)}, bf16[384,256]{1,0:T(8,128)(2,1)S(1)}, bf16[256,384]{1,0:T(8,128)(2,1)S(1)}, bf16[448,384]{1,0:T(8,128)(2,1)S(1)}, bf16[448,384]{1,0:T(8,128)(2,1)S(1)}) custom-call(s32[5]{0:T(128)S(1)} %stack.23.scalars, s32[16]{0:T(128)S(1)} %copy-done.10, bf16[32,1536]{1,0:T(8,128)(2,1)S(1)} %collective-permute-done.8.refs_0_, ...), custom_call_target="tpu_custom_call" | custom-call | flops 1056964608 | bytes 7864320 | tf_op jit(solution)/shard_map/attention/pallas_call | solution.py:414
  50.1 1.6 %collective-permute-start.14 = (bf16[256,384]{1,0:T(8,128)(2,1)S(1)}, bf16[256,384]{1,0:T(8,128)(2,1)S(1)}, u32[]{:S(2)}, u32[]{:S(2)}) collective-permute-start(bf16[256,384]{1,0:T(8,128)(2,1)S(1)} %get-tuple-element.54.refs_4_), channel_id=1, source_target_pairs={{0,8},{8,0},{16,24},{24,16},{1,9},{9,1},{17,25},{25,17},{2,10},{10... | collective-permute-start | bytes 589832 | tf_op jit(solution)/shard_map/ppermute | solution.py:457
  51.7 1.5 %collective-permute-start.15 = (bf16[256,384]{1,0:T(8,128)(2,1)S(1)}, bf16[256,384]{1,0:T(8,128)(2,1)S(1)}, u32[]{:S(2)}, u32[]{:S(2)}) collective-permute-start(bf16[256,384]{1,0:T(8,128)(2,1)S(1)} %get-tuple-element.54.refs_4_), channel_id=1, source_target_pairs={{0,16},{8,24},{16,0},{24,8},{1,17},{9,25},{17,1},{25,9},{2,18},{10... | collective-permute-start | bytes 589832 | tf_op jit(solution)/shard_map/ppermute | solution.py:457
  53.2 0.2 collective-permute-done.3.refs_2_
  53.4 0.3 collective-permute-start.21
  53.8 1.8 %collective-permute-start.22 = (bf16[256,768]{1,0:T(8,128)(2,1)S(1)}, bf16[256,768]{1,0:T(8,128)(2,1)S(1)}, u32[]{:S(2)}, u32[]{:S(2)}) collective-permute-start(bf16[256,768]{1,0:T(8,128)(2,1)S(1)} %get-tuple-element.60.refs_12_), channel_id=1, source_target_pairs={{0,16},{8,24},{16,0},{24,8},{1,17},{9,25},{17,1},{25,9},{2,18},{10... | collective-permute-start | bytes 1179656 | tf_op jit(solution)/shard_map/ppermute | solution.py:412
  55.5 1.4 collective-permute-done.14.refs_5_
  56.9 3.6 %collective-permute-start.23 = (bf16[256,768]{1,0:T(8,128)(2,1)S(1)}, bf16[256,768]{1,0:T(8,128)(2,1)S(1)}, u32[]{:S(2)}, u32[]{:S(2)}) collective-permute-start(bf16[256,768]{1,0:T(8,128)(2,1)S(1)} %get-tuple-element.60.refs_12_), channel_id=1, source_target_pairs={{0,24},{8,16},{16,8},{24,0},{1,25},{9,17},{17,9},{25,1},{2,26},{10... | collective-permute-start | bytes 1179656 | tf_op jit(solution)/shard_map/ppermute | solution.py:412
  60.5 0.0 collective-permute-start.16
  60.5 0.6 share_mixed.1
  61.2 1.9 %collective-permute-start.18 = (bf16[192,256]{1,0:T(8,128)(2,1)S(1)}, bf16[192,256]{1,0:T(8,128)(2,1)S(1)}, u32[]{:S(2)}, u32[]{:S(2)}) collective-permute-start(bf16[192,256]{1,0:T(8,128)(2,1)S(1)} %get-tuple-element.57), channel_id=1, source_target_pairs={{0,8},{8,0},{16,24},{24,16},{1,9},{9,1},{17,25},{25,17},{2,10},{10... | collective-permute-start | bytes 294920 | tf_op jit(solution)/shard_map/ppermute | solution.py:466
  63.1 16.6 %collective-permute-done.16.refs_7_ = bf16[256,384]{1,0:T(8,128)(2,1)S(1)} collective-permute-done((bf16[256,384]{1,0:T(8,128)(2,1)S(1)}, bf16[256,384]{1,0:T(8,128)(2,1)S(1)}, u32[]{:S(2)}, u32[]{:S(2)}) %collective-permute-start.16) | collective-permute-done | bytes 196640 | tf_op jit(solution)/shard_map/ppermute | solution.py:457
  79.7 0.0 collective-permute-done.18.refs_9_
  79.8 2.8 %collective-permute-start.20 = (bf16[192,256]{1,0:T(8,128)(2,1)S(1)}, bf16[192,256]{1,0:T(8,128)(2,1)S(1)}, u32[]{:S(2)}, u32[]{:S(2)}) collective-permute-start(bf16[192,256]{1,0:T(8,128)(2,1)S(1)} %get-tuple-element.59), channel_id=1, source_target_pairs={{0,24},{8,16},{16,8},{24,0},{1,25},{9,17},{17,9},{25,1},{2,26},{10... | collective-permute-start | bytes 294920 | tf_op jit(solution)/shard_map/ppermute | solution.py:466
  82.6 3.5 %collective-permute-done.19.refs_10_ = bf16[192,256]{1,0:T(8,128)(2,1)S(1)} collective-permute-done((bf16[192,256]{1,0:T(8,128)(2,1)S(1)}, bf16[192,256]{1,0:T(8,128)(2,1)S(1)}, u32[]{:S(2)}, u32[]{:S(2)}) %collective-permute-start.19) | collective-permute-done | bytes 98336 | tf_op jit(solution)/shard_map/ppermute | solution.py:466
  86.1 1.8 %grad_query_out.1 = bf16[8,24,1536]{2,1,0:T(8,128)(2,1)} custom-call(bf16[256,384]{1,0:T(8,128)(2,1)S(1)} %get-tuple-element.40.refs_0_, bf16[256,384]{1,0:T(8,128)(2,1)S(1)} %collective-permute-done.2.refs_1_, bf16[256,384]{1,0:T(8,128)(2,1)S(1)} %collective-permute-done.3.refs_2_, bf16[256,384]{1,0:T(8,128)(2,1)S(1)} %collective-permute-done.4.refs_3_, ...), custom_call_target="tpu_custom_call" | custom-call | flops 603979776 | bytes 3145728 | tf_op jit(solution)/shard_map/grad_query_out/pallas_call | solution.py:469
  87.9 3.7 %all-to-all-start = ((bf16[8,24,1536]{2,1,0:T(8,128)(2,1)}), bf16[8,24,1536]{2,1,0:T(8,128)(2,1)S(1)}, u32[]{:S(2)}, u32[]{:S(2)}) async-start(bf16[8,24,1536]{2,1,0:T(8,128)(2,1)} %grad_query_out.1), calls=%async_computation | async-start | bytes 1179648 | tf_op jit(solution)/shard_map/all_to_all | solution.py:480
  91.6 2.4 %grad_key_value.1 = (bf16[2,384,384]{2,1,0:T(8,128)(2,1)S(1)}, bf16[2,384,384]{2,1,0:T(8,128)(2,1)S(1)}, f32[2,384,384]{2,1,0:T(8,128)S(1)}, f32[2,384,384]{2,1,0:T(8,128)S(1)}) custom-call(s32[5]{0:T(128)S(1)} %stack.23.scalars, bf16[448,1536]{1,0:T(8,128)(2,1)S(1)} %get-tuple-element.62.left, bf16[448,384]{1,0:T(8,128)(2,1)S(1)} %get-tuple-element.63.dkey, ...), custom_call_target="tpu_custom_call" | custom-call | flops 1056964608 | bytes 7077888 | tf_op jit(solution)/shard_map/grad_key_value/pallas_call | solution.py:442
  94.0 1.2 collective-permute-start.24
  95.2 1.4 collective-permute-start.25
  96.6 12.9 %collective-permute-done.24.k_got = bf16[2,384,384]{2,1,0:T(8,128)(2,1)S(1)} collective-permute-done((bf16[2,384,384]{2,1,0:T(8,128)(2,1)S(1)}, bf16[2,384,384]{2,1,0:T(8,128)(2,1)S(1)}, u32[]{:S(2)}, u32[]{:S(2)}) %collective-permute-start.24) | collective-permute-done | bytes 589856 | tf_op jit(solution)/shard_map/ppermute | solution.py:453
  109.5 0.8 collective-permute-done.25.v_got
  110.3 0.7 sum_first.1
  111.1 1.5 %collective-permute-start.26 = (bf16[384,384]{1,0:T(8,128)(2,1)S(1)}, bf16[384,384]{1,0:T(8,128)(2,1)S(1)}, u32[]{:S(2)}, u32[]{:S(2)}) collective-permute-start(bf16[384,384]{1,0:T(8,128)(2,1)S(1)} %get-tuple-element.70), channel_id=1, source_target_pairs={{0,16},{8,24},{16,0},{24,8},{1,17},{9,25},{17,1},{25,9},{2,18},{10... | collective-permute-start | bytes 884744 | tf_op jit(solution)/shard_map/ppermute | solution.py:498
  112.6 0.6 collective-permute-start.27
  113.2 5.9 %collective-permute-done.26.k_got = bf16[384,384]{1,0:T(8,128)(2,1)S(1)} collective-permute-done((bf16[384,384]{1,0:T(8,128)(2,1)S(1)}, bf16[384,384]{1,0:T(8,128)(2,1)S(1)}, u32[]{:S(2)}, u32[]{:S(2)}) %collective-permute-start.26) | collective-permute-done | bytes 294944 | tf_op jit(solution)/shard_map/ppermute | solution.py:498
  119.2 1.2 collective-permute-done.27.v_got
  120.3 0.9 sum_second.1
  121.3 4.7 %all-to-all-start.1 = ((bf16[8,48,768]{2,1,0:T(8,128)(2,1)}), bf16[8,48,768]{2,1,0:T(8,128)(2,1)S(1)}, u32[]{:S(2)}, u32[]{:S(2)}) async-start(bf16[8,48,768]{2,1,0:T(8,128)(2,1)} %bitcast.7), calls=%async_computation.1 | async-start | bytes 1179648 | tf_op jit(solution)/shard_map/all_to_all | solution.py:509
  126.0 0.8 sum_query_out.1
  126.7 16.0 %all-to-all-done.1.packed = bf16[8,48,768]{2,1,0:T(8,128)(2,1)S(1)} async-done(((bf16[8,48,768]{2,1,0:T(8,128)(2,1)}), bf16[8,48,768]{2,1,0:T(8,128)(2,1)S(1)}, u32[]{:S(2)}, u32[]{:S(2)}) %all-to-all-start.1) | async-done | bytes 589856 | tf_op jit(solution)/shard_map/all_to_all | solution.py:509
  142.7 0.8 sum_key_value.1
  (32 shorter events, 0.1 us)
Async XLA Ops:
  0.6 25.8 %collective-permute-start = (bf16[4,32,1536]{2,1,0:T(8,128)(2,1)}, bf16[4,32,1536]{2,1,0:T(8,128)(2,1)S(1)}, u32[]{:S(2)}, u32[]{:S(2)}) collective-permute-start(bf16[4,32,1536]{2,1,0:T(8,128)(2,1)} %bitcast.8), channel_id=1, source_target_pairs={{0,1},{1,0},{2,3},{3,2},{4,5},{5,4},{6,7},{7,6},{8,9},{9,8},{10,11... | collective-permute-start | bytes 1179656 | tf_op jit(solution)/shard_map/ppermute | solution.py:366
  1.1 25.3 %collective-permute-start.1 = (bf16[4,32,1536]{2,1,0:T(8,128)(2,1)}, bf16[4,32,1536]{2,1,0:T(8,128)(2,1)S(1)}, u32[]{:S(2)}, u32[]{:S(2)}) collective-permute-start(bf16[4,32,1536]{2,1,0:T(8,128)(2,1)} %bitcast.11), channel_id=1, source_target_pairs={{0,1},{1,0},{2,3},{3,2},{4,5},{5,4},{6,7},{7,6},{8,9},{9,8},{10,11... | collective-permute-start | bytes 1179656 | tf_op jit(solution)/shard_map/ppermute | solution.py:367
  3.9 5.7 %collective-permute-start.5 = (s32[4]{0:T(128)}, s32[4]{0:T(128)S(1)}, u32[]{:S(2)}, u32[]{:S(2)}) collective-permute-start(s32[4]{0:T(128)} %get-tuple-element.45), channel_id=1, source_target_pairs={{0,2},{2,0},{4,6},{6,4},{1,3},{3,1},{5,7},{7,5},{8,10},{10,8},{12,... | collective-permute-start | bytes 56 | tf_op jit(solution)/shard_map/ppermute | solution.py:362
  6.9 4.7 %collective-permute-start.6 = (s32[4]{0:T(128)}, s32[4]{0:T(128)S(1)}, u32[]{:S(2)}, u32[]{:S(2)}) collective-permute-start(s32[4]{0:T(128)} %get-tuple-element.45), channel_id=1, source_target_pairs={{0,4},{2,6},{4,0},{6,2},{1,5},{3,7},{5,1},{7,3},{8,12},{10,14},{12... | collective-permute-start | bytes 56 | tf_op jit(solution)/shard_map/ppermute | solution.py:362
  9.5 5.5 %collective-permute-start.7 = (s32[4]{0:T(128)}, s32[4]{0:T(128)S(1)}, u32[]{:S(2)}, u32[]{:S(2)}) collective-permute-start(s32[4]{0:T(128)} %get-tuple-element.45), channel_id=1, source_target_pairs={{0,6},{2,4},{4,2},{6,0},{1,7},{3,5},{5,3},{7,1},{8,14},{10,12},{12... | collective-permute-start | bytes 56 | tf_op jit(solution)/shard_map/ppermute | solution.py:362
  15.1 1.0 copy-start.6
  16.7 6.0 %collective-permute-start.8 = (bf16[32,1536]{1,0:T(8,128)(2,1)S(1)}, bf16[32,1536]{1,0:T(8,128)(2,1)S(1)}, u32[]{:S(2)}, u32[]{:S(2)}) collective-permute-start(bf16[32,1536]{1,0:T(8,128)(2,1)S(1)} %get-tuple-element.46), channel_id=1, source_target_pairs={{0,2},{2,0},{4,6},{6,4},{1,3},{3,1},{5,7},{7,5},{8,10},{10,8},{12,... | collective-permute-start | bytes 294920 | tf_op jit(solution)/shard_map/ppermute | solution.py:377
  16.7 9.2 %collective-permute-start.9 = (bf16[32,1536]{1,0:T(8,128)(2,1)S(1)}, bf16[32,1536]{1,0:T(8,128)(2,1)S(1)}, u32[]{:S(2)}, u32[]{:S(2)}) collective-permute-start(bf16[32,1536]{1,0:T(8,128)(2,1)S(1)} %get-tuple-element.47), channel_id=1, source_target_pairs={{0,4},{2,6},{4,0},{6,2},{1,5},{3,7},{5,1},{7,3},{8,12},{10,14},{12... | collective-permute-start | bytes 294920 | tf_op jit(solution)/shard_map/ppermute | solution.py:377
  17.3 8.6 %collective-permute-start.10 = (bf16[32,1536]{1,0:T(8,128)(2,1)S(1)}, bf16[32,1536]{1,0:T(8,128)(2,1)S(1)}, u32[]{:S(2)}, u32[]{:S(2)}) collective-permute-start(bf16[32,1536]{1,0:T(8,128)(2,1)S(1)} %get-tuple-element.48), channel_id=1, source_target_pairs={{0,6},{2,4},{4,2},{6,0},{1,7},{3,5},{5,3},{7,1},{8,14},{10,12},{12... | collective-permute-start | bytes 294920 | tf_op jit(solution)/shard_map/ppermute | solution.py:377
  21.1 23.6 %copy-start.10 = (s32[16]{0:T(128)S(1)}, s32[16]{0:T(128)}, u32[]{:S(2)}) copy-start(s32[16]{0:T(128)} %get-tuple-element.44.alive) | copy-start | bytes 196
  22.7 21.6 %collective-permute-start.11 = (bf16[32,1536]{1,0:T(8,128)(2,1)S(1)}, bf16[32,1536]{1,0:T(8,128)(2,1)S(1)}, u32[]{:S(2)}, u32[]{:S(2)}) collective-permute-start(bf16[32,1536]{1,0:T(8,128)(2,1)S(1)} %collective-permute-done.8.refs_0_), channel_id=1, source_target_pairs={{0,1},{1,0},{2,3},{3,2},{4,5},{5,4},{6,7},{7,6},{8,9},{9,8},{10,11... | collective-permute-start | bytes 294920 | tf_op jit(solution)/shard_map/ppermute | solution.py:378
  25.9 18.8 %collective-permute-start.12 = (bf16[32,1536]{1,0:T(8,128)(2,1)S(1)}, bf16[32,1536]{1,0:T(8,128)(2,1)S(1)}, u32[]{:S(2)}, u32[]{:S(2)}) collective-permute-start(bf16[32,1536]{1,0:T(8,128)(2,1)S(1)} %collective-permute-done.9.refs_1_), channel_id=1, source_target_pairs={{0,1},{1,0},{2,3},{3,2},{4,5},{5,4},{6,7},{7,6},{8,9},{9,8},{10,11... | collective-permute-start | bytes 294920 | tf_op jit(solution)/shard_map/ppermute | solution.py:378
  25.9 18.8 %collective-permute-start.13 = (bf16[32,1536]{1,0:T(8,128)(2,1)S(1)}, bf16[32,1536]{1,0:T(8,128)(2,1)S(1)}, u32[]{:S(2)}, u32[]{:S(2)}) collective-permute-start(bf16[32,1536]{1,0:T(8,128)(2,1)S(1)} %collective-permute-done.10.refs_2_), channel_id=1, source_target_pairs={{0,1},{1,0},{2,3},{3,2},{4,5},{5,4},{6,7},{7,6},{8,9},{9,8},{10,11... | collective-permute-start | bytes 294920 | tf_op jit(solution)/shard_map/ppermute | solution.py:378
  26.4 1.7 %copy-start = (bf16[1536,768]{1,0:T(8,128)(2,1)S(1)}, bf16[1536,768]{1,0:T(8,128)(2,1)}, u32[]{:S(2)}) copy-start(bf16[1536,768]{1,0:T(8,128)(2,1)} %refs_12_.1) | copy-start | bytes 7077892
  28.1 1.7 %copy-start.2 = (bf16[1536,768]{1,0:T(8,128)(2,1)S(1)}, bf16[1536,768]{1,0:T(8,128)(2,1)}, u32[]{:S(2)}) copy-start(bf16[1536,768]{1,0:T(8,128)(2,1)} %refs_13_.1) | copy-start | bytes 7077892
  29.8 1.7 %copy-start.4 = (bf16[1536,768]{1,0:T(8,128)(2,1)S(1)}, bf16[1536,768]{1,0:T(8,128)(2,1)}, u32[]{:S(2)}) copy-start(bf16[1536,768]{1,0:T(8,128)(2,1)} %w_query.1) | copy-start | bytes 7077892
  31.4 1.7 %copy-start.5 = (bf16[768,1536]{1,0:T(8,128)(2,1)S(1)}, bf16[768,1536]{1,0:T(8,128)(2,1)}, u32[]{:S(2)}) copy-start(bf16[768,1536]{1,0:T(8,128)(2,1)} %w_out.1) | copy-start | bytes 7077892
  33.1 1.0 copy-start.7
  34.1 1.0 copy-start.8
  35.1 0.8 copy-start.9
  35.9 8.9 %copy-start.1 = (bf16[1536,768]{1,0:T(8,128)(2,1)S(1)}, bf16[1536,768]{1,0:T(8,128)(2,1)}, u32[]{:S(2)}) copy-start(bf16[1536,768]{1,0:T(8,128)(2,1)} %refs_12_.1) | copy-start | bytes 7077892
  35.9 8.9 %copy-start.3 = (bf16[1536,768]{1,0:T(8,128)(2,1)S(1)}, bf16[1536,768]{1,0:T(8,128)(2,1)}, u32[]{:S(2)}) copy-start(bf16[1536,768]{1,0:T(8,128)(2,1)} %refs_13_.1) | copy-start | bytes 7077892
  41.2 10.5 %collective-permute-start.2 = (bf16[256,384]{1,0:T(8,128)(2,1)S(1)}, bf16[256,384]{1,0:T(8,128)(2,1)S(1)}, u32[]{:S(2)}, u32[]{:S(2)}) collective-permute-start(bf16[256,384]{1,0:T(8,128)(2,1)S(1)} %get-tuple-element.41), channel_id=1, source_target_pairs={{0,8},{8,0},{16,24},{24,16},{1,9},{9,1},{17,25},{25,17},{2,10},{10... | collective-permute-start | bytes 589832 | tf_op jit(solution)/shard_map/ppermute | solution.py:411
  42.7 10.7 %collective-permute-start.3 = (bf16[256,384]{1,0:T(8,128)(2,1)S(1)}, bf16[256,384]{1,0:T(8,128)(2,1)S(1)}, u32[]{:S(2)}, u32[]{:S(2)}) collective-permute-start(bf16[256,384]{1,0:T(8,128)(2,1)S(1)} %get-tuple-element.42), channel_id=1, source_target_pairs={{0,16},{8,24},{16,0},{24,8},{1,17},{9,25},{17,1},{25,9},{2,18},{10... | collective-permute-start | bytes 589832 | tf_op jit(solution)/shard_map/ppermute | solution.py:411
  44.3 9.5 %collective-permute-start.4 = (bf16[256,384]{1,0:T(8,128)(2,1)S(1)}, bf16[256,384]{1,0:T(8,128)(2,1)S(1)}, u32[]{:S(2)}, u32[]{:S(2)}) collective-permute-start(bf16[256,384]{1,0:T(8,128)(2,1)S(1)} %get-tuple-element.43), channel_id=1, source_target_pairs={{0,24},{8,16},{16,8},{24,0},{1,25},{9,17},{17,9},{25,1},{2,26},{10... | collective-permute-start | bytes 589832 | tf_op jit(solution)/shard_map/ppermute | solution.py:411
  50.1 6.8 %collective-permute-start.14 = (bf16[256,384]{1,0:T(8,128)(2,1)S(1)}, bf16[256,384]{1,0:T(8,128)(2,1)S(1)}, u32[]{:S(2)}, u32[]{:S(2)}) collective-permute-start(bf16[256,384]{1,0:T(8,128)(2,1)S(1)} %get-tuple-element.54.refs_4_), channel_id=1, source_target_pairs={{0,8},{8,0},{16,24},{24,16},{1,9},{9,1},{17,25},{25,17},{2,10},{10... | collective-permute-start | bytes 589832 | tf_op jit(solution)/shard_map/ppermute | solution.py:457
  51.7 8.8 %collective-permute-start.17 = (bf16[384,256]{1,0:T(8,128)(2,1)S(1)}, bf16[384,256]{1,0:T(8,128)(2,1)S(1)}, u32[]{:S(2)}, u32[]{:S(2)}) collective-permute-start(bf16[384,256]{1,0:T(8,128)(2,1)S(1)} %get-tuple-element.55.mine), channel_id=1, source_target_pairs={{0,1},{1,0},{2,3},{3,2},{4,5},{5,4},{6,7},{7,6},{8,9},{9,8},{10,11... | collective-permute-start | bytes 589832 | tf_op jit(solution)/shard_map/ppermute | solution.py:456
  51.7 9.4 %collective-permute-start.15 = (bf16[256,384]{1,0:T(8,128)(2,1)S(1)}, bf16[256,384]{1,0:T(8,128)(2,1)S(1)}, u32[]{:S(2)}, u32[]{:S(2)}) collective-permute-start(bf16[256,384]{1,0:T(8,128)(2,1)S(1)} %get-tuple-element.54.refs_4_), channel_id=1, source_target_pairs={{0,16},{8,24},{16,0},{24,8},{1,17},{9,25},{17,1},{25,9},{2,18},{10... | collective-permute-start | bytes 589832 | tf_op jit(solution)/shard_map/ppermute | solution.py:457
  53.4 32.7 %collective-permute-start.21 = (bf16[256,768]{1,0:T(8,128)(2,1)S(1)}, bf16[256,768]{1,0:T(8,128)(2,1)S(1)}, u32[]{:S(2)}, u32[]{:S(2)}) collective-permute-start(bf16[256,768]{1,0:T(8,128)(2,1)S(1)} %get-tuple-element.60.refs_12_), channel_id=1, source_target_pairs={{0,8},{8,0},{16,24},{24,16},{1,9},{9,1},{17,25},{25,17},{2,10},{10... | collective-permute-start | bytes 1179656 | tf_op jit(solution)/shard_map/ppermute | solution.py:412
  53.8 32.3 %collective-permute-start.22 = (bf16[256,768]{1,0:T(8,128)(2,1)S(1)}, bf16[256,768]{1,0:T(8,128)(2,1)S(1)}, u32[]{:S(2)}, u32[]{:S(2)}) collective-permute-start(bf16[256,768]{1,0:T(8,128)(2,1)S(1)} %get-tuple-element.60.refs_12_), channel_id=1, source_target_pairs={{0,16},{8,24},{16,0},{24,8},{1,17},{9,25},{17,1},{25,9},{2,18},{10... | collective-permute-start | bytes 1179656 | tf_op jit(solution)/shard_map/ppermute | solution.py:412
  56.9 29.1 %collective-permute-start.23 = (bf16[256,768]{1,0:T(8,128)(2,1)S(1)}, bf16[256,768]{1,0:T(8,128)(2,1)S(1)}, u32[]{:S(2)}, u32[]{:S(2)}) collective-permute-start(bf16[256,768]{1,0:T(8,128)(2,1)S(1)} %get-tuple-element.60.refs_12_), channel_id=1, source_target_pairs={{0,24},{8,16},{16,8},{24,0},{1,25},{9,17},{17,9},{25,1},{2,26},{10... | collective-permute-start | bytes 1179656 | tf_op jit(solution)/shard_map/ppermute | solution.py:412
  60.5 19.2 %collective-permute-start.16 = (bf16[256,384]{1,0:T(8,128)(2,1)S(1)}, bf16[256,384]{1,0:T(8,128)(2,1)S(1)}, u32[]{:S(2)}, u32[]{:S(2)}) collective-permute-start(bf16[256,384]{1,0:T(8,128)(2,1)S(1)} %get-tuple-element.54.refs_4_), channel_id=1, source_target_pairs={{0,24},{8,16},{16,8},{24,0},{1,25},{9,17},{17,9},{25,1},{2,26},{10... | collective-permute-start | bytes 589832 | tf_op jit(solution)/shard_map/ppermute | solution.py:457
  61.2 18.6 %collective-permute-start.18 = (bf16[192,256]{1,0:T(8,128)(2,1)S(1)}, bf16[192,256]{1,0:T(8,128)(2,1)S(1)}, u32[]{:S(2)}, u32[]{:S(2)}) collective-permute-start(bf16[192,256]{1,0:T(8,128)(2,1)S(1)} %get-tuple-element.57), channel_id=1, source_target_pairs={{0,8},{8,0},{16,24},{24,16},{1,9},{9,1},{17,25},{25,17},{2,10},{10... | collective-permute-start | bytes 294920 | tf_op jit(solution)/shard_map/ppermute | solution.py:466
  79.7 6.4 %collective-permute-start.19 = (bf16[192,256]{1,0:T(8,128)(2,1)S(1)}, bf16[192,256]{1,0:T(8,128)(2,1)S(1)}, u32[]{:S(2)}, u32[]{:S(2)}) collective-permute-start(bf16[192,256]{1,0:T(8,128)(2,1)S(1)} %get-tuple-element.58), channel_id=1, source_target_pairs={{0,16},{8,24},{16,0},{24,8},{1,17},{9,25},{17,1},{25,9},{2,18},{10... | collective-permute-start | bytes 294920 | tf_op jit(solution)/shard_map/ppermute | solution.py:466
  79.8 6.3 %collective-permute-start.20 = (bf16[192,256]{1,0:T(8,128)(2,1)S(1)}, bf16[192,256]{1,0:T(8,128)(2,1)S(1)}, u32[]{:S(2)}, u32[]{:S(2)}) collective-permute-start(bf16[192,256]{1,0:T(8,128)(2,1)S(1)} %get-tuple-element.59), channel_id=1, source_target_pairs={{0,24},{8,16},{16,8},{24,0},{1,25},{9,17},{17,9},{25,1},{2,26},{10... | collective-permute-start | bytes 294920 | tf_op jit(solution)/shard_map/ppermute | solution.py:466
  87.9 33.4 %all-to-all-start = ((bf16[8,24,1536]{2,1,0:T(8,128)(2,1)}), bf16[8,24,1536]{2,1,0:T(8,128)(2,1)S(1)}, u32[]{:S(2)}, u32[]{:S(2)}) async-start(bf16[8,24,1536]{2,1,0:T(8,128)(2,1)} %grad_query_out.1), calls=%async_computation | async-start | bytes 1179648 | tf_op jit(solution)/shard_map/all_to_all | solution.py:480
  94.0 15.5 %collective-permute-start.24 = (bf16[2,384,384]{2,1,0:T(8,128)(2,1)S(1)}, bf16[2,384,384]{2,1,0:T(8,128)(2,1)S(1)}, u32[]{:S(2)}, u32[]{:S(2)}) collective-permute-start(bf16[2,384,384]{2,1,0:T(8,128)(2,1)S(1)} %get-tuple-element.66), channel_id=1, source_target_pairs={{0,8},{8,0},{16,24},{24,16},{1,9},{9,1},{17,25},{25,17},{2,10},{10... | collective-permute-start | bytes 1769480 | tf_op jit(solution)/shard_map/ppermute | solution.py:453
  95.2 15.2 %collective-permute-start.25 = (bf16[2,384,384]{2,1,0:T(8,128)(2,1)S(1)}, bf16[2,384,384]{2,1,0:T(8,128)(2,1)S(1)}, u32[]{:S(2)}, u32[]{:S(2)}) collective-permute-start(bf16[2,384,384]{2,1,0:T(8,128)(2,1)S(1)} %get-tuple-element.68), channel_id=1, source_target_pairs={{0,16},{8,24},{16,0},{24,8},{1,17},{9,25},{17,1},{25,9},{2,18},{10... | collective-permute-start | bytes 1769480 | tf_op jit(solution)/shard_map/ppermute | solution.py:454
  111.1 8.1 %collective-permute-start.26 = (bf16[384,384]{1,0:T(8,128)(2,1)S(1)}, bf16[384,384]{1,0:T(8,128)(2,1)S(1)}, u32[]{:S(2)}, u32[]{:S(2)}) collective-permute-start(bf16[384,384]{1,0:T(8,128)(2,1)S(1)} %get-tuple-element.70), channel_id=1, source_target_pairs={{0,16},{8,24},{16,0},{24,8},{1,17},{9,25},{17,1},{25,9},{2,18},{10... | collective-permute-start | bytes 884744 | tf_op jit(solution)/shard_map/ppermute | solution.py:498
  112.6 7.7 %collective-permute-start.27 = (bf16[384,384]{1,0:T(8,128)(2,1)S(1)}, bf16[384,384]{1,0:T(8,128)(2,1)S(1)}, u32[]{:S(2)}, u32[]{:S(2)}) collective-permute-start(bf16[384,384]{1,0:T(8,128)(2,1)S(1)} %get-tuple-element.72), channel_id=1, source_target_pairs={{0,8},{8,0},{16,24},{24,16},{1,9},{9,1},{17,25},{25,17},{2,10},{10... | collective-permute-start | bytes 884744 | tf_op jit(solution)/shard_map/ppermute | solution.py:499
  121.3 21.5 %all-to-all-start.1 = ((bf16[8,48,768]{2,1,0:T(8,128)(2,1)}), bf16[8,48,768]{2,1,0:T(8,128)(2,1)S(1)}, u32[]{:S(2)}, u32[]{:S(2)}) async-start(bf16[8,48,768]{2,1,0:T(8,128)(2,1)} %bitcast.7), calls=%async_computation.1 | async-start | bytes 1179648 | tf_op jit(solution)/shard_map/all_to_all | solution.py:509

commit v3 on v2

--- a/solution.py
+++ b/solution.py
@@ -23,6 +23,10 @@
 
 def dot_nt(a, b):
     return lax.dot_general(a, b, (((1,), (1,)), ((), ())), preferred_element_type=jnp.float32)
+
+
+def dot_tt(a, b):
+    return lax.dot_general(a, b, (((0,), (1,)), ((), ())), preferred_element_type=jnp.float32)
 
 
 def dot_tn(a, b):
@@ -66,9 +70,9 @@
 
 def project_kernel(
     scalars, lat_own, lat_other, cot_own, cot_other, gain, taps, w_query, w_key, w_value, w_out,
-    normed, queries, keys, values, upstream, out_grad, up_half, *refs,
+    normed, queries, keys, values, out_grad, *refs,
 ):
-    quarters, (w_q, w_k, w_v, w_o, arrived) = refs[:4], refs[4:]
+    bundles, (upstream, w_q, w_k, w_v, w_o, arrived) = refs[:4], refs[4:]
     views, strip, width = lat_own.shape
     copies = [
         weight_copy(scalars, w_query, w_q, arrived, 0, 1),
@@ -110,11 +114,12 @@
                     total = total + middle[b : b + 1] * shifted[half][b]
                     total = total + cross[half][b : b + 1] * shifted[1 - half][b]
                 upstream[strip_of(u, half), lanes] = total.astype(jnp.bfloat16)
-    size = width // 4
-    for m, quarter in enumerate(quarters):
+    size, half_size = width // 4, width // 2
+    up_half = upstream[:, pl.ds(pl.multiple_of(row * half_size, half_size), half_size)]
+    for m, bundle in enumerate(bundles):
         start = pl.multiple_of(lax.bitwise_xor(scalars[2], jnp.int32(m)) * size, size)
-        quarter[...] = normed[:, pl.ds(start, size)]
-    up_half[...] = upstream[:, pl.ds(pl.multiple_of(row * (width // 2), width // 2), width // 2)]
+        bundle[:, :size] = normed[:, pl.ds(start, size)]
+        bundle[:, size:] = up_half
     rows = normed[...]
     for copy, weight, result in zip(copies, (w_q, w_k, w_v), (queries, keys, values)):
         copy.wait()
@@ -126,7 +131,7 @@
 def attention_kernel(views, groups, scalars, alive, *refs):
     got_own, got_other, refs = refs[: groups - 1], refs[groups - 1 : 2 * groups - 2], refs[2 * groups - 2 :]
     normed, queries, keys, values, out_grad, gain, w_key, w_value, *refs = refs
-    normed_all, mixed_t, dquery, dkey, dvalue, w_k, w_v, arrived = refs
+    normed_all, mixed_t, dquery_t, dkey, dvalue, w_k, w_v, arrived = refs
     copies = [
         weight_copy(scalars, w_key, w_k, arrived, 0, 1),
         weight_copy(scalars, w_value, w_v, arrived, 1, 1),
@@ -231,7 +236,7 @@
         ds_own = (a_own * (dp_own - delta) * scale).astype(jnp.bfloat16)
         ds_far = (a_far * (dp_far - delta) * scale).astype(jnp.bfloat16)
         dq = unstacked(own_tn(ds_own, k_own) + dot_tn(ds_far, k_far))
-        dquery[:, lanes] = dq.astype(jnp.bfloat16)
+        dquery_t[lanes, :] = dq.T.astype(jnp.bfloat16)
         dkey[:tokens, lanes] = own_nn(ds_own, q).astype(jnp.bfloat16)
         dkey[tokens:, lanes] = dot_nn(ds_far, q).astype(jnp.bfloat16)
 
@@ -275,30 +280,32 @@
         value[:, r * size : (r + 1) * size] = total[:, size:]
 
 
-def share_kernel(scalars, mine, theirs, *quarters):
-    size = quarters[0].shape[0]
-    for m, quarter in enumerate(quarters):
+def share_kernel(scalars, dquery_t, mine, theirs, *bundles):
+    inner = dquery_t.shape[0]
+    size = bundles[0].shape[0] - inner
+    for m, bundle in enumerate(bundles):
         scene = lax.bitwise_xor(scalars[2], jnp.int32(m))
         owner, place = lax.div(scene, jnp.int32(2)), lax.rem(scene, jnp.int32(2))
         rows = pl.ds(pl.multiple_of(place * size, size), size)
         is_mine = owner == scalars[0]
+        bundle[:inner, :] = dquery_t[...]
 
         @pl.when(is_mine)
         def _():
-            quarter[...] = mine[rows, :]
+            bundle[inner:, :] = mine[rows, :]
 
         @pl.when(jnp.logical_not(is_mine))
         def _():
-            quarter[...] = theirs[rows, :]
-
-
-def query_out_kernel(*refs):
-    normed, dquery, mixed_t, up_half, packed = refs[0:4], refs[4:8], refs[8:12], refs[12:16], refs[16]
-    grad_q = dot_tn(normed[0][...], dquery[0][...])
-    grad_o = dot_nn(mixed_t[0][...], up_half[0][...])
-    for m in range(1, 4):
-        grad_q = grad_q + dot_tn(normed[m][...], dquery[m][...])
-        grad_o = grad_o + dot_nn(mixed_t[m][...], up_half[m][...])
+            bundle[inner:, :] = theirs[rows, :]
+
+
+def query_out_kernel(inner, *refs):
+    early, late, packed = refs[0:4], refs[4:8], refs[8]
+    quarter = packed.shape[2] // 4
+    grad_q = grad_o = 0.0
+    for left, right in zip(early, late):
+        grad_q = grad_q + dot_tt(left[:, :quarter], right[:inner, :])
+        grad_o = grad_o + dot_nn(right[inner:, :], left[:, quarter:])
     targets, size, _ = packed.shape
     for i in range(targets):
         packed[i] = jnp.concatenate(
@@ -366,6 +373,37 @@
     lat_other = lax.ppermute(lat, "row", swap)
     cot_other = lax.ppermute(cot, "row", swap)
 
+    gain = norm_gain.reshape(1, width)
+    normed, queries, keys, values, out_grad, *early = pl.pallas_call(
+        project_kernel,
+        in_specs=[SMEM] + [VMEM] * 6 + [HBM] * 4,
+        out_specs=[VMEM] * 9,
+        out_shape=[
+            shape((tokens, width), bf16),
+            shape((tokens, part), bf16),
+            shape((tokens, part), bf16),
+            shape((tokens, part), bf16),
+            shape((tokens, part), bf16),
+        ]
+        + [shape((tokens, 3 * width // 4), bf16)] * 4,
+        scratch_shapes=[
+            pltpu.VMEM((tokens, width), bf16),
+            pltpu.VMEM((width, part), bf16),
+            pltpu.VMEM((width, part), bf16),
+            pltpu.VMEM((width, part), bf16),
+            pltpu.VMEM((part, width), bf16),
+            pltpu.SemaphoreType.DMA((4,)),
+        ],
+        compiler_params=params(52),
+        cost_estimate=pl.CostEstimate(
+            flops=8 * tokens * width * part + 40 * tokens * width,
+            bytes_accessed=8 * width * part + 16 * tokens * width,
+            transcendentals=tokens,
+        ),
+        name="project",
+    )(scalars, lat, lat_other, cot, cot_other, gain, kernel, w_query, w_key, w_value, w_out)
+
+    normed, granted = lax.optimization_barrier((normed, granted))
     outgoing = pl.pallas_call(
         functools.partial(pick_kernel, groups),
         in_specs=[SMEM] * groups + [VMEM],
@@ -377,48 +415,17 @@
     got_own = [lax.ppermute(part_out, "view", pairs) for part_out, pairs in zip(outgoing, between)]
     got_other = [lax.ppermute(got, "row", swap) for got in got_own]
 
-    gain = norm_gain.reshape(1, width)
-    normed, queries, keys, values, upstream, out_grad, up_half, *quarters = pl.pallas_call(
-        project_kernel,
-        in_specs=[SMEM] + [VMEM] * 6 + [HBM] * 4,
-        out_specs=[VMEM] * 11,
-        out_shape=[
-            shape((tokens, width), bf16),
-            shape((tokens, part), bf16),
-            shape((tokens, part), bf16),
-            shape((tokens, part), bf16),
-            shape((tokens, width), bf16),
-            shape((tokens, part), bf16),
-            shape((tokens, width // 2), bf16),
-        ]
-        + [shape((tokens, width // 4), bf16)] * 4,
-        scratch_shapes=[
-            pltpu.VMEM((width, part), bf16),
-            pltpu.VMEM((width, part), bf16),
-            pltpu.VMEM((width, part), bf16),
-            pltpu.VMEM((part, width), bf16),
-            pltpu.SemaphoreType.DMA((4,)),
-        ],
-        compiler_params=params(28),
-        cost_estimate=pl.CostEstimate(
-            flops=8 * tokens * width * part + 40 * tokens * width,
-            bytes_accessed=8 * width * part + 16 * tokens * width,
-            transcendentals=tokens,
-        ),
-        name="project",
-    )(scalars, lat, lat_other, cot, cot_other, gain, kernel, w_query, w_key, w_value, w_out)
-
-    normed_far = [quarters[0]] + [lax.ppermute(quarters[m], "scene", across[m]) for m in range(1, 4)]
-    up_far = [up_half] + [lax.ppermute(up_half, "scene", across[m]) for m in range(1, 4)]
-
-    normed_all, mixed_t, dquery, dkey, dvalue = pl.pallas_call(
+    early, outgoing = lax.optimization_barrier((early, outgoing))
+    early = [early[0]] + [lax.ppermute(early[m], "scene", across[m]) for m in range(1, 4)]
+
+    normed_all, mixed_t, dquery_t, dkey, dvalue = pl.pallas_call(
         functools.partial(attention_kernel, views, groups),
         in_specs=[SMEM] * 2 + [VMEM] * (2 * groups - 2 + 6) + [HBM] * 2,
         out_specs=[VMEM] * 5,
         out_shape=[
             shape((key_tokens, width), bf16),
             shape((part, tokens), bf16),
-            shape((tokens, part), bf16),
+            shape((part, tokens), bf16),
             shape((key_tokens, part), bf16),
             shape((key_tokens, part), bf16),
         ],
@@ -427,7 +434,7 @@
             pltpu.VMEM((width, part), bf16),
             pltpu.SemaphoreType.DMA((2,)),
         ],
-        compiler_params=params(24 + groups),
+        compiler_params=params(50),
         cost_estimate=pl.CostEstimate(
             flops=4 * (key_tokens - tokens) * width * part + 24 * groups * 2 * strip * tokens * part,
             bytes_accessed=4 * width * part + 8 * key_tokens * width,
@@ -453,22 +460,22 @@
     k_got = lax.ppermute(k_send, "scene", along_x)
     v_got = lax.ppermute(v_send, "scene", along_y)
 
+    mixed_t, dquery_t, k_send, v_send = lax.optimization_barrier((mixed_t, dquery_t, k_send, v_send))
     mixed_other = lax.ppermute(mixed_t, "row", swap)
-    dquery_far = [dquery] + [lax.ppermute(dquery, "scene", across[m]) for m in range(1, 4)]
-    shares = pl.pallas_call(
+    late = pl.pallas_call(
         share_kernel,
-        in_specs=[SMEM] + [VMEM] * 2,
+        in_specs=[SMEM] + [VMEM] * 3,
         out_specs=[VMEM] * 4,
-        out_shape=[shape((inner // 4, tokens), bf16)] * 4,
+        out_shape=[shape((part + inner // 4, tokens), bf16)] * 4,
         compiler_params=params(8),
-        name="share_mixed",
-    )(scalars, mixed_t, mixed_other)
-    mixed_far = [shares[0]] + [lax.ppermute(shares[m], "scene", across[m]) for m in range(1, 4)]
+        name="share",
+    )(scalars, dquery_t, mixed_t, mixed_other)
+    late = [late[0]] + [lax.ppermute(late[m], "scene", across[m]) for m in range(1, 4)]
     targets = groups * rows
     q_rows, o_rows = width // (4 * targets), inner // (4 * targets)
     packed = pl.pallas_call(
-        query_out_kernel,
-        in_specs=[VMEM] * 16,
+        functools.partial(query_out_kernel, part),
+        in_specs=[VMEM] * 8,
         out_specs=VMEM,
         out_shape=shape((targets, o_rows, width), bf16),
         compiler_params=params(16),
@@ -476,7 +483,7 @@
             flops=4 * tokens * width * part, bytes_accessed=8 * tokens * width, transcendentals=0
         ),
         name="grad_query_out",
-    )(*normed_far, *dquery_far, *mixed_far, *up_far)
+    )(*early, *late)
     packed = lax.all_to_all(packed, ("view", "row"), split_axis=0, concat_axis=0, tiled=True)
     grad_query, grad_out = pl.pallas_call(
         functools.partial(unpack_query_out_kernel, rows),

time: 144 us -> 130 us (0.903)
  starting transfers between devices: 41.4 us -> 32.8 us
  local copies, waits for them, and re-layouts: 12.6 us -> 8.18 us
  waiting for transfers between devices: 68.2 us -> 64.9 us
  Pallas kernels: 20.5 us -> 22.4 us
    ppermute x12 -> x6, starting transfers between devices: 17 us -> 8.14 us  [the longest x3 4.58 us: shards(): lax.ppermute(early[m], 'scene', across[m])]
    ppermute x3, waiting for transfers between devices: 5.46 us -> 0.01 us  [shards(): granted = [lax.ppermute(request, 'view', pairs) for pairs in between]]
    unnamed x23 -> x19, local copies, waits for them, and re-layouts: 11.8 us -> 7.4 us
    ppermute x12 -> x6, waiting for transfers between devices: 21.8 us -> 20.5 us  [the longest x3 15.2 us: shards(): lax.ppermute(early[m], 'scene', across[m])]
  transfers between devices with their start and end apart: 30 -> 24, of which waited for: 13 -> 9; matrix products, arithmetic and copies ran while one was open for 1% -> 2% of each run, Pallas kernels for 13% -> 15%
where the time goes in v3:
time: 130 us; the launch traced here: 129 us
  waiting for transfers between devices  64.9 us (50%)
  starting transfers between devices  32.8 us (25%)
  Pallas kernels  22.4 us (17%)
  local copies, waits for them, and re-layouts  8.18 us (6%)
    all_to_all x2, waiting for transfers between devices, shards(): lax.all_to_all(packed, ('view', 'row'), split_axis=0, concat_axis=0, tile...  16 us
    ppermute x3, waiting for transfers between devices, shards(): lax.ppermute(early[m], 'scene', across[m])  15.2 us
    ppermute x1, waiting for transfers between devices, shards(): k_got = lax.ppermute(k_send, 'scene', along_x)  12.9 us
    all_to_all x2, starting transfers between devices, shards(): lax.all_to_all(packed, ('view', 'row'), split_axis=0, concat_axis=0, tile...  8.21 us
    unnamed x19, local copies, waits for them, and re-layouts  7.4 us
    pallas_call x1, Pallas kernels, shards(): pl.pallas_call(functools.partial(attention_kernel, views, groups), in_spe...  6.55 us
    ppermute x1, waiting for transfers between devices, shards(): k_got = lax.ppermute(k_later, 'scene', along_y)  6.26 us
    pallas_call x1, Pallas kernels, shards(): pl.pallas_call(project_kernel, in_specs=[SMEM] + [VMEM] * 6 + [HBM] * 4,...  5.93 us
  transfers between devices with their start and end apart: 24, of which 9 were waited for; matrix products, arithmetic and copies ran while one was open for 2% of the time, Pallas kernels for 15%

profile of v3, /device:TPU:0, one launch (start us, length us, event | category | flops | bytes accessed | tf_op | source)
XLA Modules:
  0.0 129.1 jit_solution(6986849094715262153)
XLA Ops:
  0.6 0.5 collective-permute-start
  1.1 0.1 collective-permute-start.1
  1.2 1.3 %copy.14.partners = s32[1,4,3]{2,1,0:T(4,128)} copy(s32[1,4,3]{1,0,2:T(1,128)} %param.17) | data formatting | bytes 96 | tf_op args[7]
  2.6 1.3 requests.1
  3.9 5.1 %collective-permute-start.4 = (s32[4]{0:T(128)}, s32[4]{0:T(128)S(1)}, u32[]{:S(2)}, u32[]{:S(2)}) collective-permute-start(s32[4]{0:T(128)} %get-tuple-element.54), channel_id=1, source_target_pairs={{0,6},{2,4},{4,2},{6,0},{1,7},{3,5},{5,3},{7,1},{8,14},{10,12},{12... | collective-permute-start | bytes 56 | tf_op jit(solution)/shard_map/ppermute | solution.py:369
  8.9 0.0 collective-permute-start.3
  9.0 0.6 collective-permute-start.2
  9.6 0.7 reshape.14.gain.refs_11_
  10.3 0.1 stack.23.scalars
  10.4 0.0 collective-permute-done.lat_other
  10.4 0.0 collective-permute-done.1.cot_other
  10.4 0.7 copy-done.8
  11.1 1.0 copy-done
  12.1 1.0 copy-done.3
  13.1 0.8 copy-done.4
  13.9 5.9 %project.1 = (bf16[256,1536]{1,0:T(8,128)(2,1)}, bf16[256,384]{1,0:T(8,128)(2,1)S(1)}, bf16[256,384]{1,0:T(8,128)(2,1)S(1)}, bf16[256,384]{1,0:T(8,128)(2,1)S(1)...) custom-call(s32[5]{0:T(128)S(1)} %stack.23.scalars, ...), custom_call_target="tpu_custom_call" | custom-call | flops 1223688192 | bytes 11010048 | tf_op jit(solution)/shard_map/project/pallas_call | solution.py:377
  19.9 0.0 collective-permute-done.4.refs_2_
  19.9 0.0 collective-permute-done.3.refs_1_
  19.9 0.0 collective-permute-done.2.refs_0_
  19.9 0.6 pick.1
  20.5 1.5 %collective-permute-start.8 = (bf16[32,1536]{1,0:T(8,128)(2,1)S(1)}, bf16[32,1536]{1,0:T(8,128)(2,1)S(1)}, u32[]{:S(2)}, u32[]{:S(2)}) collective-permute-start(bf16[32,1536]{1,0:T(8,128)(2,1)S(1)} %get-tuple-element.58), channel_id=1, source_target_pairs={{0,2},{2,0},{4,6},{6,4},{1,3},{3,1},{5,7},{7,5},{8,10},{10,8},{12,... | collective-permute-start | bytes 294920 | tf_op jit(solution)/shard_map/ppermute | solution.py:415
  21.9 2.9 %collective-permute-start.9 = (bf16[32,1536]{1,0:T(8,128)(2,1)S(1)}, bf16[32,1536]{1,0:T(8,128)(2,1)S(1)}, u32[]{:S(2)}, u32[]{:S(2)}) collective-permute-start(bf16[32,1536]{1,0:T(8,128)(2,1)S(1)} %get-tuple-element.59), channel_id=1, source_target_pairs={{0,4},{2,6},{4,0},{6,2},{1,5},{3,7},{5,1},{7,3},{8,12},{10,14},{12... | collective-permute-start | bytes 294920 | tf_op jit(solution)/shard_map/ppermute | solution.py:415
  24.9 0.1 collective-permute-start.10
  24.9 1.6 %collective-permute-start.5 = (bf16[256,1152]{1,0:T(8,128)(2,1)}, bf16[256,1152]{1,0:T(8,128)(2,1)S(1)}, u32[]{:S(2)}, u32[]{:S(2)}) collective-permute-start(bf16[256,1152]{1,0:T(8,128)(2,1)} %get-tuple-element.62), channel_id=1, source_target_pairs={{0,8},{8,0},{16,24},{24,16},{1,9},{9,1},{17,25},{25,17},{2,10},{10... | collective-permute-start | bytes 1769480 | tf_op jit(solution)/shard_map/ppermute | solution.py:419
  26.6 0.0 collective-permute-done.8.refs_0_
  26.6 0.0 collective-permute-start.11
  26.6 5.5 %collective-permute-done.9.refs_1_ = bf16[32,1536]{1,0:T(8,128)(2,1)S(1)} collective-permute-done((bf16[32,1536]{1,0:T(8,128)(2,1)S(1)}, bf16[32,1536]{1,0:T(8,128)(2,1)S(1)}, u32[]{:S(2)}, u32[]{:S(2)}) %collective-permute-start.9) | collective-permute-done | bytes 98336 | tf_op jit(solution)/shard_map/ppermute | solution.py:415
  32.1 0.0 collective-permute-start.12
  32.1 0.0 collective-permute-done.10.refs_2_
  32.1 0.5 collective-permute-start.13
  32.6 1.5 %collective-permute-start.6 = (bf16[256,1152]{1,0:T(8,128)(2,1)}, bf16[256,1152]{1,0:T(8,128)(2,1)S(1)}, u32[]{:S(2)}, u32[]{:S(2)}) collective-permute-start(bf16[256,1152]{1,0:T(8,128)(2,1)} %get-tuple-element.63), channel_id=1, source_target_pairs={{0,16},{8,24},{16,0},{24,8},{1,17},{9,25},{17,1},{25,9},{2,18},{10... | collective-permute-start | bytes 1769480 | tf_op jit(solution)/shard_map/ppermute | solution.py:419
  34.1 0.0 collective-permute-done.11.refs_3_
  34.1 1.4 %collective-permute-start.7 = (bf16[256,1152]{1,0:T(8,128)(2,1)}, bf16[256,1152]{1,0:T(8,128)(2,1)S(1)}, u32[]{:S(2)}, u32[]{:S(2)}) collective-permute-start(bf16[256,1152]{1,0:T(8,128)(2,1)} %get-tuple-element.64), channel_id=1, source_target_pairs={{0,24},{8,16},{16,8},{24,0},{1,25},{9,17},{17,9},{25,1},{2,26},{10... | collective-permute-start | bytes 1769480 | tf_op jit(solution)/shard_map/ppermute | solution.py:419
  35.5 0.0 collective-permute-done.12.refs_4_
  35.5 1.1 copy-done.1
  36.7 6.6 %attention.1 = (bf16[448,1536]{1,0:T(8,128)(2,1)}, bf16[384,256]{1,0:T(8,128)(2,1)S(1)}, bf16[384,256]{1,0:T(8,128)(2,1)S(1)}, bf16[448,384]{1,0:T(8,128)(2,1)S(1)}, bf16[448,384]{1,0:T(8,128)(2,1)S(1)}) custom-call(s32[5]{0:T(128)S(1)} %stack.23.scalars, s32[16]{0:T(128)S(1)} %copy-done.5, bf16[32,1536]{1,0:T(8,128)(2,1)S(1)} %collective-permute-done.8.refs_0_, ...), custom_call_target="tpu_custom_call" | custom-call | flops 1056964608 | bytes 7864320 | tf_op jit(solution)/shard_map/attention/pallas_call | solution.py:421
  43.3 1.4 %copy-done.6 = bf16[448,1536]{1,0:T(8,128)(2,1)S(1)} copy-done((bf16[448,1536]{1,0:T(8,128)(2,1)S(1)}, bf16[448,1536]{1,0:T(8,128)(2,1)}, u32[]{:S(2)}) %copy-start.6) | copy-done | bytes 1376280
  44.6 2.4 %grad_key_value.1 = (bf16[2,384,384]{2,1,0:T(8,128)(2,1)S(1)}, bf16[2,384,384]{2,1,0:T(8,128)(2,1)S(1)}, f32[2,384,384]{2,1,0:T(8,128)S(1)}, f32[2,384,384]{2,1,0:T(8,128)S(1)}) custom-call(s32[5]{0:T(128)S(1)} %stack.23.scalars, bf16[448,1536]{1,0:T(8,128)(2,1)S(1)} %copy-done.6, bf16[448,384]{1,0:T(8,128)(2,1)S(1)} %get-tuple-element.74.dkey, ...), custom_call_target="tpu_custom_call" | custom-call | flops 1056964608 | bytes 7077888 | tf_op jit(solution)/shard_map/grad_key_value/pallas_call | solution.py:449
  47.1 0.1 collective-permute-start.14
  47.1 1.4 %collective-permute-done.14.theirs = bf16[384,256]{1,0:T(8,128)(2,1)S(1)} collective-permute-done((bf16[384,256]{1,0:T(8,128)(2,1)S(1)}, bf16[384,256]{1,0:T(8,128)(2,1)S(1)}, u32[]{:S(2)}, u32[]{:S(2)}) %collective-permute-start.14) | collective-permute-done | bytes 196640 | tf_op jit(solution)/shard_map/ppermute | solution.py:464
  48.6 0.6 share.1
  49.2 0.6 collective-permute-start.15
  49.8 1.5 %collective-permute-start.16 = (bf16[576,256]{1,0:T(8,128)(2,1)S(1)}, bf16[576,256]{1,0:T(8,128)(2,1)S(1)}, u32[]{:S(2)}, u32[]{:S(2)}) collective-permute-start(bf16[576,256]{1,0:T(8,128)(2,1)S(1)} %get-tuple-element.82), channel_id=1, source_target_pairs={{0,16},{8,24},{16,0},{24,8},{1,17},{9,25},{17,1},{25,9},{2,18},{10... | collective-permute-start | bytes 884744 | tf_op jit(solution)/shard_map/ppermute | solution.py:473
  51.3 1.4 %collective-permute-start.17 = (bf16[576,256]{1,0:T(8,128)(2,1)S(1)}, bf16[576,256]{1,0:T(8,128)(2,1)S(1)}, u32[]{:S(2)}, u32[]{:S(2)}) collective-permute-start(bf16[576,256]{1,0:T(8,128)(2,1)S(1)} %get-tuple-element.83), channel_id=1, source_target_pairs={{0,24},{8,16},{16,8},{24,0},{1,25},{9,17},{17,9},{25,1},{2,26},{10... | collective-permute-start | bytes 884744 | tf_op jit(solution)/shard_map/ppermute | solution.py:473
  52.8 15.2 %collective-permute-done.6.refs_2_ = bf16[256,1152]{1,0:T(8,128)(2,1)S(1)} collective-permute-done((bf16[256,1152]{1,0:T(8,128)(2,1)}, bf16[256,1152]{1,0:T(8,128)(2,1)S(1)}, u32[]{:S(2)}, u32[]{:S(2)}) %collective-permute-start.6) | collective-permute-done | bytes 589856 | tf_op jit(solution)/shard_map/ppermute | solution.py:419
  67.9 0.0 collective-permute-done.7.refs_3_
  67.9 5.4 %collective-permute-done.16.refs_6_ = bf16[576,256]{1,0:T(8,128)(2,1)S(1)} collective-permute-done((bf16[576,256]{1,0:T(8,128)(2,1)S(1)}, bf16[576,256]{1,0:T(8,128)(2,1)S(1)}, u32[]{:S(2)}, u32[]{:S(2)}) %collective-permute-start.16) | collective-permute-done | bytes 294944 | tf_op jit(solution)/shard_map/ppermute | solution.py:473
  73.3 1.8 %grad_query_out.1 = bf16[8,24,1536]{2,1,0:T(8,128)(2,1)} custom-call(bf16[256,1152]{1,0:T(8,128)(2,1)S(1)} %copy-done.2, bf16[256,1152]{1,0:T(8,128)(2,1)S(1)} %collective-permute-done.5.refs_1_, bf16[256,1152]{1,0:T(8,128)(2,1)S(1)} %collective-permute-done.6.refs_2_, bf16[256,1152]{1,0:T(8,128)(2,1)S(1)} %collective-permute-done.7.refs_3_, ...), custom_call_target="tpu_custom_call" | custom-call | flops 603979776 | bytes 3145728 | tf_op jit(solution)/shard_map/grad_query_out/pallas_call | solution.py:476
  75.1 3.9 %all-to-all-start = ((bf16[8,24,1536]{2,1,0:T(8,128)(2,1)}), bf16[8,24,1536]{2,1,0:T(8,128)(2,1)S(1)}, u32[]{:S(2)}, u32[]{:S(2)}) async-start(bf16[8,24,1536]{2,1,0:T(8,128)(2,1)} %grad_query_out.1), calls=%async_computation | async-start | bytes 1179648 | tf_op jit(solution)/shard_map/all_to_all | solution.py:487
  79.0 1.5 %collective-permute-start.18 = (bf16[2,384,384]{2,1,0:T(8,128)(2,1)}, bf16[2,384,384]{2,1,0:T(8,128)(2,1)S(1)}, u32[]{:S(2)}, u32[]{:S(2)}) collective-permute-start(bf16[2,384,384]{2,1,0:T(8,128)(2,1)} %copy-done.7), channel_id=1, source_target_pairs={{0,8},{8,0},{16,24},{24,16},{1,9},{9,1},{17,25},{25,17},{2,10},{10... | collective-permute-start | bytes 1769480 | tf_op jit(solution)/shard_map/ppermute | solution.py:460
  80.5 1.5 %collective-permute-start.19 = (bf16[2,384,384]{2,1,0:T(8,128)(2,1)S(1)}, bf16[2,384,384]{2,1,0:T(8,128)(2,1)S(1)}, u32[]{:S(2)}, u32[]{:S(2)}) collective-permute-start(bf16[2,384,384]{2,1,0:T(8,128)(2,1)S(1)} %get-tuple-element.77), channel_id=1, source_target_pairs={{0,16},{8,24},{16,0},{24,8},{1,17},{9,25},{17,1},{25,9},{2,18},{10... | collective-permute-start | bytes 1769480 | tf_op jit(solution)/shard_map/ppermute | solution.py:461
  82.0 12.9 %collective-permute-done.18.k_got = bf16[2,384,384]{2,1,0:T(8,128)(2,1)S(1)} collective-permute-done((bf16[2,384,384]{2,1,0:T(8,128)(2,1)}, bf16[2,384,384]{2,1,0:T(8,128)(2,1)S(1)}, u32[]{:S(2)}, u32[]{:S(2)}) %collective-permute-start.18) | collective-permute-done | bytes 589856 | tf_op jit(solution)/shard_map/ppermute | solution.py:460
  94.9 1.0 collective-permute-done.19.v_got
  95.9 0.8 sum_first.1
  96.7 1.6 %collective-permute-start.20 = (bf16[384,384]{1,0:T(8,128)(2,1)S(1)}, bf16[384,384]{1,0:T(8,128)(2,1)S(1)}, u32[]{:S(2)}, u32[]{:S(2)}) collective-permute-start(bf16[384,384]{1,0:T(8,128)(2,1)S(1)} %get-tuple-element.88), channel_id=1, source_target_pairs={{0,16},{8,24},{16,0},{24,8},{1,17},{9,25},{17,1},{25,9},{2,18},{10... | collective-permute-start | bytes 884744 | tf_op jit(solution)/shard_map/ppermute | solution.py:505
  98.3 0.5 collective-permute-start.21
  98.8 6.3 %collective-permute-done.20.k_got = bf16[384,384]{1,0:T(8,128)(2,1)S(1)} collective-permute-done((bf16[384,384]{1,0:T(8,128)(2,1)S(1)}, bf16[384,384]{1,0:T(8,128)(2,1)S(1)}, u32[]{:S(2)}, u32[]{:S(2)}) %collective-permute-start.20) | collective-permute-done | bytes 294944 | tf_op jit(solution)/shard_map/ppermute | solution.py:505
  105.1 1.2 collective-permute-done.21.v_got
  106.3 0.9 sum_second.1
  107.3 0.0 all-to-all-done.packed
  107.3 4.3 %all-to-all-start.1 = ((bf16[8,48,768]{2,1,0:T(8,128)(2,1)}), bf16[8,48,768]{2,1,0:T(8,128)(2,1)S(1)}, u32[]{:S(2)}, u32[]{:S(2)}) async-start(bf16[8,48,768]{2,1,0:T(8,128)(2,1)} %bitcast.7), calls=%async_computation.1 | async-start | bytes 1179648 | tf_op jit(solution)/shard_map/all_to_all | solution.py:516
  111.6 0.8 sum_query_out.1
  112.4 16.0 %all-to-all-done.1.packed = bf16[8,48,768]{2,1,0:T(8,128)(2,1)S(1)} async-done(((bf16[8,48,768]{2,1,0:T(8,128)(2,1)}), bf16[8,48,768]{2,1,0:T(8,128)(2,1)S(1)}, u32[]{:S(2)}, u32[]{:S(2)}) %all-to-all-start.1) | async-done | bytes 589856 | tf_op jit(solution)/shard_map/all_to_all | solution.py:516
  128.4 0.8 sum_key_value.1
  (16 shorter events, 0.0 us)
Async XLA Ops:
  0.6 9.8 %collective-permute-start = (bf16[4,32,1536]{2,1,0:T(8,128)(2,1)}, bf16[4,32,1536]{2,1,0:T(8,128)(2,1)S(1)}, u32[]{:S(2)}, u32[]{:S(2)}) collective-permute-start(bf16[4,32,1536]{2,1,0:T(8,128)(2,1)} %bitcast.8), channel_id=1, source_target_pairs={{0,1},{1,0},{2,3},{3,2},{4,5},{5,4},{6,7},{7,6},{8,9},{9,8},{10,11... | collective-permute-start | bytes 1179656 | tf_op jit(solution)/shard_map/ppermute | solution.py:373
  1.1 9.2 %collective-permute-start.1 = (bf16[4,32,1536]{2,1,0:T(8,128)(2,1)}, bf16[4,32,1536]{2,1,0:T(8,128)(2,1)S(1)}, u32[]{:S(2)}, u32[]{:S(2)}) collective-permute-start(bf16[4,32,1536]{2,1,0:T(8,128)(2,1)} %bitcast.11), channel_id=1, source_target_pairs={{0,1},{1,0},{2,3},{3,2},{4,5},{5,4},{6,7},{7,6},{8,9},{9,8},{10,11... | collective-permute-start | bytes 1179656 | tf_op jit(solution)/shard_map/ppermute | solution.py:374
  3.9 16.0 %collective-permute-start.4 = (s32[4]{0:T(128)}, s32[4]{0:T(128)S(1)}, u32[]{:S(2)}, u32[]{:S(2)}) collective-permute-start(s32[4]{0:T(128)} %get-tuple-element.54), channel_id=1, source_target_pairs={{0,6},{2,4},{4,2},{6,0},{1,7},{3,5},{5,3},{7,1},{8,14},{10,12},{12... | collective-permute-start | bytes 56 | tf_op jit(solution)/shard_map/ppermute | solution.py:369
  8.9 10.9 %collective-permute-start.3 = (s32[4]{0:T(128)}, s32[4]{0:T(128)S(1)}, u32[]{:S(2)}, u32[]{:S(2)}) collective-permute-start(s32[4]{0:T(128)} %get-tuple-element.54), channel_id=1, source_target_pairs={{0,4},{2,6},{4,0},{6,2},{1,5},{3,7},{5,1},{7,3},{8,12},{10,14},{12... | collective-permute-start | bytes 56 | tf_op jit(solution)/shard_map/ppermute | solution.py:369
  9.0 10.9 %collective-permute-start.2 = (s32[4]{0:T(128)}, s32[4]{0:T(128)S(1)}, u32[]{:S(2)}, u32[]{:S(2)}) collective-permute-start(s32[4]{0:T(128)} %get-tuple-element.54), channel_id=1, source_target_pairs={{0,2},{2,0},{4,6},{6,4},{1,3},{3,1},{5,7},{7,5},{8,10},{10,8},{12,... | collective-permute-start | bytes 56 | tf_op jit(solution)/shard_map/ppermute | solution.py:369
  10.3 25.2 %copy-start.5 = (s32[16]{0:T(128)S(1)}, s32[16]{0:T(128)}, u32[]{:S(2)}) copy-start(s32[16]{0:T(128)} %get-tuple-element.65.alive) | copy-start | bytes 196
  10.4 0.7 copy-start.8
  11.1 1.0 copy-start
  12.1 1.0 copy-start.3
  13.1 0.8 copy-start.4
  20.5 6.1 %collective-permute-start.8 = (bf16[32,1536]{1,0:T(8,128)(2,1)S(1)}, bf16[32,1536]{1,0:T(8,128)(2,1)S(1)}, u32[]{:S(2)}, u32[]{:S(2)}) collective-permute-start(bf16[32,1536]{1,0:T(8,128)(2,1)S(1)} %get-tuple-element.58), channel_id=1, source_target_pairs={{0,2},{2,0},{4,6},{6,4},{1,3},{3,1},{5,7},{7,5},{8,10},{10,8},{12,... | collective-permute-start | bytes 294920 | tf_op jit(solution)/shard_map/ppermute | solution.py:415
  21.9 10.1 %collective-permute-start.9 = (bf16[32,1536]{1,0:T(8,128)(2,1)S(1)}, bf16[32,1536]{1,0:T(8,128)(2,1)S(1)}, u32[]{:S(2)}, u32[]{:S(2)}) collective-permute-start(bf16[32,1536]{1,0:T(8,128)(2,1)S(1)} %get-tuple-element.59), channel_id=1, source_target_pairs={{0,4},{2,6},{4,0},{6,2},{1,5},{3,7},{5,1},{7,3},{8,12},{10,14},{12... | collective-permute-start | bytes 294920 | tf_op jit(solution)/shard_map/ppermute | solution.py:415
  24.9 7.2 %collective-permute-start.10 = (bf16[32,1536]{1,0:T(8,128)(2,1)S(1)}, bf16[32,1536]{1,0:T(8,128)(2,1)S(1)}, u32[]{:S(2)}, u32[]{:S(2)}) collective-permute-start(bf16[32,1536]{1,0:T(8,128)(2,1)S(1)} %get-tuple-element.60), channel_id=1, source_target_pairs={{0,6},{2,4},{4,2},{6,0},{1,7},{3,5},{5,3},{7,1},{8,14},{10,12},{12... | collective-permute-start | bytes 294920 | tf_op jit(solution)/shard_map/ppermute | solution.py:415
  24.9 26.4 %collective-permute-start.5 = (bf16[256,1152]{1,0:T(8,128)(2,1)}, bf16[256,1152]{1,0:T(8,128)(2,1)S(1)}, u32[]{:S(2)}, u32[]{:S(2)}) collective-permute-start(bf16[256,1152]{1,0:T(8,128)(2,1)} %get-tuple-element.62), channel_id=1, source_target_pairs={{0,8},{8,0},{16,24},{24,16},{1,9},{9,1},{17,25},{25,17},{2,10},{10... | collective-permute-start | bytes 1769480 | tf_op jit(solution)/shard_map/ppermute | solution.py:419
  26.6 7.5 %collective-permute-start.11 = (bf16[32,1536]{1,0:T(8,128)(2,1)S(1)}, bf16[32,1536]{1,0:T(8,128)(2,1)S(1)}, u32[]{:S(2)}, u32[]{:S(2)}) collective-permute-start(bf16[32,1536]{1,0:T(8,128)(2,1)S(1)} %collective-permute-done.8.refs_0_), channel_id=1, source_target_pairs={{0,1},{1,0},{2,3},{3,2},{4,5},{5,4},{6,7},{7,6},{8,9},{9,8},{10,11... | collective-permute-start | bytes 294920 | tf_op jit(solution)/shard_map/ppermute | solution.py:416
  32.1 3.5 %collective-permute-start.12 = (bf16[32,1536]{1,0:T(8,128)(2,1)S(1)}, bf16[32,1536]{1,0:T(8,128)(2,1)S(1)}, u32[]{:S(2)}, u32[]{:S(2)}) collective-permute-start(bf16[32,1536]{1,0:T(8,128)(2,1)S(1)} %collective-permute-done.9.refs_1_), channel_id=1, source_target_pairs={{0,1},{1,0},{2,3},{3,2},{4,5},{5,4},{6,7},{7,6},{8,9},{9,8},{10,11... | collective-permute-start | bytes 294920 | tf_op jit(solution)/shard_map/ppermute | solution.py:416
  32.1 3.5 %collective-permute-start.13 = (bf16[32,1536]{1,0:T(8,128)(2,1)S(1)}, bf16[32,1536]{1,0:T(8,128)(2,1)S(1)}, u32[]{:S(2)}, u32[]{:S(2)}) collective-permute-start(bf16[32,1536]{1,0:T(8,128)(2,1)S(1)} %collective-permute-done.10.refs_2_), channel_id=1, source_target_pairs={{0,1},{1,0},{2,3},{3,2},{4,5},{5,4},{6,7},{7,6},{8,9},{9,8},{10,11... | collective-permute-start | bytes 294920 | tf_op jit(solution)/shard_map/ppermute | solution.py:416
  32.6 35.4 %collective-permute-start.6 = (bf16[256,1152]{1,0:T(8,128)(2,1)}, bf16[256,1152]{1,0:T(8,128)(2,1)S(1)}, u32[]{:S(2)}, u32[]{:S(2)}) collective-permute-start(bf16[256,1152]{1,0:T(8,128)(2,1)} %get-tuple-element.63), channel_id=1, source_target_pairs={{0,16},{8,24},{16,0},{24,8},{1,17},{9,25},{17,1},{25,9},{2,18},{10... | collective-permute-start | bytes 1769480 | tf_op jit(solution)/shard_map/ppermute | solution.py:419
  34.1 33.8 %collective-permute-start.7 = (bf16[256,1152]{1,0:T(8,128)(2,1)}, bf16[256,1152]{1,0:T(8,128)(2,1)S(1)}, u32[]{:S(2)}, u32[]{:S(2)}) collective-permute-start(bf16[256,1152]{1,0:T(8,128)(2,1)} %get-tuple-element.64), channel_id=1, source_target_pairs={{0,24},{8,16},{16,8},{24,0},{1,25},{9,17},{17,9},{25,1},{2,26},{10... | collective-permute-start | bytes 1769480 | tf_op jit(solution)/shard_map/ppermute | solution.py:419
  35.5 1.1 copy-start.1
  43.2 30.1 %copy-start.2 = (bf16[256,1152]{1,0:T(8,128)(2,1)S(1)}, bf16[256,1152]{1,0:T(8,128)(2,1)}, u32[]{:S(2)}) copy-start(bf16[256,1152]{1,0:T(8,128)(2,1)} %get-tuple-element.61.refs_0_) | copy-start | bytes 1769476
  43.2 1.4 %copy-start.6 = (bf16[448,1536]{1,0:T(8,128)(2,1)S(1)}, bf16[448,1536]{1,0:T(8,128)(2,1)}, u32[]{:S(2)}) copy-start(bf16[448,1536]{1,0:T(8,128)(2,1)} %get-tuple-element.73.left) | copy-start | bytes 4128772
  47.0 26.3 %copy-start.7 = (bf16[2,384,384]{2,1,0:T(8,128)(2,1)}, bf16[2,384,384]{2,1,0:T(8,128)(2,1)S(1)}, u32[]{:S(2)}) copy-start(bf16[2,384,384]{2,1,0:T(8,128)(2,1)S(1)} %get-tuple-element.76) | copy-start | bytes 1769476
  47.1 1.5 %collective-permute-start.14 = (bf16[384,256]{1,0:T(8,128)(2,1)S(1)}, bf16[384,256]{1,0:T(8,128)(2,1)S(1)}, u32[]{:S(2)}, u32[]{:S(2)}) collective-permute-start(bf16[384,256]{1,0:T(8,128)(2,1)S(1)} %get-tuple-element.79.mine), channel_id=1, source_target_pairs={{0,1},{1,0},{2,3},{3,2},{4,5},{5,4},{6,7},{7,6},{8,9},{9,8},{10,11... | collective-permute-start | bytes 589832 | tf_op jit(solution)/shard_map/ppermute | solution.py:464
  49.2 18.7 %collective-permute-start.15 = (bf16[576,256]{1,0:T(8,128)(2,1)S(1)}, bf16[576,256]{1,0:T(8,128)(2,1)S(1)}, u32[]{:S(2)}, u32[]{:S(2)}) collective-permute-start(bf16[576,256]{1,0:T(8,128)(2,1)S(1)} %get-tuple-element.81), channel_id=1, source_target_pairs={{0,8},{8,0},{16,24},{24,16},{1,9},{9,1},{17,25},{25,17},{2,10},{10... | collective-permute-start | bytes 884744 | tf_op jit(solution)/shard_map/ppermute | solution.py:473
  49.8 23.5 %collective-permute-start.16 = (bf16[576,256]{1,0:T(8,128)(2,1)S(1)}, bf16[576,256]{1,0:T(8,128)(2,1)S(1)}, u32[]{:S(2)}, u32[]{:S(2)}) collective-permute-start(bf16[576,256]{1,0:T(8,128)(2,1)S(1)} %get-tuple-element.82), channel_id=1, source_target_pairs={{0,16},{8,24},{16,0},{24,8},{1,17},{9,25},{17,1},{25,9},{2,18},{10... | collective-permute-start | bytes 884744 | tf_op jit(solution)/shard_map/ppermute | solution.py:473
  51.3 22.0 %collective-permute-start.17 = (bf16[576,256]{1,0:T(8,128)(2,1)S(1)}, bf16[576,256]{1,0:T(8,128)(2,1)S(1)}, u32[]{:S(2)}, u32[]{:S(2)}) collective-permute-start(bf16[576,256]{1,0:T(8,128)(2,1)S(1)} %get-tuple-element.83), channel_id=1, source_target_pairs={{0,24},{8,16},{16,8},{24,0},{1,25},{9,17},{17,9},{25,1},{2,26},{10... | collective-permute-start | bytes 884744 | tf_op jit(solution)/shard_map/ppermute | solution.py:473
  75.1 32.2 %all-to-all-start = ((bf16[8,24,1536]{2,1,0:T(8,128)(2,1)}), bf16[8,24,1536]{2,1,0:T(8,128)(2,1)S(1)}, u32[]{:S(2)}, u32[]{:S(2)}) async-start(bf16[8,24,1536]{2,1,0:T(8,128)(2,1)} %grad_query_out.1), calls=%async_computation | async-start | bytes 1179648 | tf_op jit(solution)/shard_map/all_to_all | solution.py:487
  79.0 15.9 %collective-permute-start.18 = (bf16[2,384,384]{2,1,0:T(8,128)(2,1)}, bf16[2,384,384]{2,1,0:T(8,128)(2,1)S(1)}, u32[]{:S(2)}, u32[]{:S(2)}) collective-permute-start(bf16[2,384,384]{2,1,0:T(8,128)(2,1)} %copy-done.7), channel_id=1, source_target_pairs={{0,8},{8,0},{16,24},{24,16},{1,9},{9,1},{17,25},{25,17},{2,10},{10... | collective-permute-start | bytes 1769480 | tf_op jit(solution)/shard_map/ppermute | solution.py:460
  80.5 15.5 %collective-permute-start.19 = (bf16[2,384,384]{2,1,0:T(8,128)(2,1)S(1)}, bf16[2,384,384]{2,1,0:T(8,128)(2,1)S(1)}, u32[]{:S(2)}, u32[]{:S(2)}) collective-permute-start(bf16[2,384,384]{2,1,0:T(8,128)(2,1)S(1)} %get-tuple-element.77), channel_id=1, source_target_pairs={{0,16},{8,24},{16,0},{24,8},{1,17},{9,25},{17,1},{25,9},{2,18},{10... | collective-permute-start | bytes 1769480 | tf_op jit(solution)/shard_map/ppermute | solution.py:461
  96.7 8.4 %collective-permute-start.20 = (bf16[384,384]{1,0:T(8,128)(2,1)S(1)}, bf16[384,384]{1,0:T(8,128)(2,1)S(1)}, u32[]{:S(2)}, u32[]{:S(2)}) collective-permute-start(bf16[384,384]{1,0:T(8,128)(2,1)S(1)} %get-tuple-element.88), channel_id=1, source_target_pairs={{0,16},{8,24},{16,0},{24,8},{1,17},{9,25},{17,1},{25,9},{2,18},{10... | collective-permute-start | bytes 884744 | tf_op jit(solution)/shard_map/ppermute | solution.py:505
  98.3 8.0 %collective-permute-start.21 = (bf16[384,384]{1,0:T(8,128)(2,1)S(1)}, bf16[384,384]{1,0:T(8,128)(2,1)S(1)}, u32[]{:S(2)}, u32[]{:S(2)}) collective-permute-start(bf16[384,384]{1,0:T(8,128)(2,1)S(1)} %get-tuple-element.90), channel_id=1, source_target_pairs={{0,8},{8,0},{16,24},{24,16},{1,9},{9,1},{17,25},{25,17},{2,10},{10... | collective-permute-start | bytes 884744 | tf_op jit(solution)/shard_map/ppermute | solution.py:506
  107.3 21.1 %all-to-all-start.1 = ((bf16[8,48,768]{2,1,0:T(8,128)(2,1)}), bf16[8,48,768]{2,1,0:T(8,128)(2,1)S(1)}, u32[]{:S(2)}, u32[]{:S(2)}) async-start(bf16[8,48,768]{2,1,0:T(8,128)(2,1)} %bitcast.7), calls=%async_computation.1 | async-start | bytes 1179648 | tf_op jit(solution)/shard_map/all_to_all | solution.py:516

commit v4 on v3

v4 whole, which is shorter than its diff:
```python
import functools

import jax
import jax.numpy as jnp
from jax import lax
from jax.experimental import pallas as pl
from jax.experimental.pallas import tpu as pltpu
from jax.sharding import PartitionSpec as P

HEAD_DIM = 64
EPSILON = 1e-06
MASKED = -1e30
MIB = 1024 * 1024
LITTLE = pl.CostEstimate(flops=1, bytes_accessed=1, transcendentals=0)

VMEM = pl.BlockSpec(memory_space=pltpu.VMEM)
HBM = pl.BlockSpec(memory_space=pltpu.HBM)
SMEM = pl.BlockSpec(memory_space=pltpu.SMEM)


def dot_nn(a, b):
    return lax.dot_general(a, b, (((1,), (0,)), ((), ())), preferred_element_type=jnp.float32)


def dot_nt(a, b):
    return lax.dot_general(a, b, (((1,), (1,)), ((), ())), preferred_element_type=jnp.float32)


def dot_tn(a, b):
    return lax.dot_general(a, b, (((0,), (0,)), ((), ())), preferred_element_type=jnp.float32)


def normalized(tokens, gain):
    x = tokens.astype(jnp.float32)
    mean = jnp.mean(x * x, -1, keepdims=True)
    return (x * lax.rsqrt(mean + EPSILON) * gain).astype(jnp.bfloat16)


def request_kernel(views, slots, groups, partners, counts, request, alive):
    for g in range(groups):
        request[g] = 0
        for u in range(views):
            alive[g * views + u] = 0
    for u in range(views):
        for j in range(slots):

            @pl.when(j < counts[0, u])
            def _():
                partner = partners[0, u, j]
                group = lax.div(partner, jnp.int32(views))
                request[group] = lax.rem(partner, jnp.int32(views))
                alive[group * views + u] = 1


def pick_kernel(groups, scalars, *refs):
    requests, lat, outgoing = refs[: groups - 1], refs[groups - 1], refs[groups:]
    for request, out in zip(requests, outgoing):
        out[...] = lat[request[scalars[1]]]


def weight_copy(scalars, source, target, arrived, index, axis):
    size = target.shape[axis]
    half = pl.ds(pl.multiple_of(scalars[0] * size, size), size)
    part = source.at[:, half] if axis == 1 else source.at[half, :]
    return pltpu.make_async_copy(part, target, arrived.at[index])


def project_kernel(
    scalars, lat_own_far, lat_other_far, cot_own_far, cot_other_far, gain, taps, w_query, w_key, w_value, w_out,
    normed, queries, keys, values, out_grad, up_half,
    lat_own, lat_other, cot_own, cot_other, upstream, w_q, w_k, w_v, w_o, arrived,
):
    views, strip, width = lat_own.shape
    inputs = [
        pltpu.make_async_copy(source, target, arrived.at[4 + i])
        for i, (source, target) in enumerate(
            (
                (lat_own_far, lat_own),
                (lat_other_far, lat_other),
                (cot_own_far, cot_own),
                (cot_other_far, cot_other),
            )
        )
    ]
    copies = [
        weight_copy(scalars, w_query, w_q, arrived, 0, 1),
        weight_copy(scalars, w_key, w_k, arrived, 1, 1),
        weight_copy(scalars, w_value, w_v, arrived, 2, 1),
        weight_copy(scalars, w_out, w_o, arrived, 3, 0),
    ]
    for copy in inputs + copies:
        copy.start()
    scale = gain[...].reshape(1, width)
    row = scalars[0]

    def strip_of(u, half):
        index = 2 * u + (row if half == 0 else 1 - row)
        return pl.ds(pl.multiple_of(index * strip, strip), strip)

    for half, source in enumerate((lat_own, lat_other)):
        inputs[half].wait()
        for u in range(views):
            normed[strip_of(u, half), :] = normalized(source[u], scale)
    first = row == 0
    for copy in inputs[2:]:
        copy.wait()
    chunk = 512
    column = lax.broadcasted_iota(jnp.int32, (strip, 1), 0)
    not_first = (column > 0).astype(jnp.float32)
    not_last = (column < strip - 1).astype(jnp.float32)
    for c in range(0, width, chunk):
        lanes = slice(c, c + chunk)
        tap = taps[:, lanes].astype(jnp.float32)
        top, middle, bottom = tap[0:3], tap[3:6], tap[6:9]
        cross = (jnp.where(first, top, bottom), jnp.where(first, bottom, top))
        for u in range(views):
            strips = [ref[u, :, lanes].astype(jnp.float32) for ref in (cot_own, cot_other)]
            shifted = []
            for x in strips:
                after = pltpu.roll(x, strip - 1, 0) * not_last
                before = pltpu.roll(x, 1, 0) * not_first
                shifted.append((after, x, before))
            for half in range(2):
                total = strips[half]
                for b in range(3):
                    total = total + middle[b : b + 1] * shifted[half][b]
                    total = total + cross[half][b : b + 1] * shifted[1 - half][b]
                upstream[strip_of(u, half), lanes] = total.astype(jnp.bfloat16)
    half_size = width // 2
    for scene in range(up_half.shape[0]):
        up_half[scene] = upstream[:, pl.ds(pl.multiple_of(row * half_size, half_size), half_size)]
    rows = normed[...]
    for copy, weight, result in zip(copies, (w_q, w_k, w_v), (queries, keys, values)):
        copy.wait()
        result[...] = dot_nn(rows, weight[...]).astype(jnp.bfloat16)
    copies[3].wait()
    out_grad[...] = dot_nt(upstream[...], w_o[...]).astype(jnp.bfloat16)


def attention_kernel(views, groups, scalars, alive, *refs):
    got_own, got_other, refs = refs[: groups - 1], refs[groups - 1 : 2 * groups - 2], refs[2 * groups - 2 :]
    normed, queries, keys, values, out_grad, gain, w_key, w_value, *refs = refs
    normed_all, mixed_t, dquery, dkey, dvalue, w_k, w_v, arrived = refs
    copies = [
        weight_copy(scalars, w_key, w_k, arrived, 0, 1),
        weight_copy(scalars, w_value, w_v, arrived, 1, 1),
    ]
    for copy in copies:
        copy.start()
    strip = got_own[0].shape[0]
    tokens = queries.shape[0]
    view_tokens = tokens // views
    scale = HEAD_DIM ** (-0.5)
    here = scalars[1]
    scale_row = gain[...].reshape(1, normed.shape[1])
    normed_all[:tokens, :] = normed[...]
    pair = 2 * HEAD_DIM
    span = 2 * view_tokens
    column_view = lax.broadcasted_iota(jnp.int32, (1, views * span), 1) // span
    slot_alive = []
    for j in range(groups - 1):
        group = lax.bitwise_xor(here, jnp.int32(j + 1))
        start = tokens + 2 * j * strip
        normed_all[start : start + strip, :] = normalized(got_own[j][...], scale_row)
        normed_all[start + strip : start + 2 * strip, :] = normalized(got_other[j][...], scale_row)
        taken = jnp.zeros((1, views * span), jnp.int32)
        for u in range(views):
            taken = jnp.where(column_view == u, alive[group * views + u], taken)
        slot_alive.append(taken > 0)
    low = lax.broadcasted_iota(jnp.int32, (1, 1, pair), 2) < HEAD_DIM
    low_b = low.astype(jnp.bfloat16)
    high_b = 1 - low_b

    def stacked(x):
        x = x.reshape(views, view_tokens, pair)
        return jnp.concatenate((x * low_b, x * high_b), axis=1).reshape(views * span, pair)

    def unstacked(x):
        x = x.reshape(views, 2, view_tokens, pair)
        return jnp.where(low, x[:, 0], x[:, 1]).reshape(tokens, pair)

    def own_nt(a, b):
        return jnp.concatenate(
            [
                dot_nt(a[u * view_tokens : (u + 1) * view_tokens], b[u * span : (u + 1) * span])
                for u in range(views)
            ],
            axis=1,
        )

    def own_tn(a, b):
        return jnp.concatenate(
            [
                dot_tn(a[:, u * span : (u + 1) * span], b[u * view_tokens : (u + 1) * view_tokens])
                for u in range(views)
            ],
            axis=0,
        )

    def own_nn(a, b):
        return jnp.concatenate(
            [
                dot_nn(a[:, u * span : (u + 1) * span], b[u * span : (u + 1) * span])
                for u in range(views)
            ],
            axis=0,
        )

    own = []
    for p in range(queries.shape[1] // pair):
        lanes = slice(p * pair, (p + 1) * pair)
        q, g = stacked(queries[:, lanes]), stacked(out_grad[:, lanes])
        k_own, v_own = keys[:, lanes], values[:, lanes]
        own.append((q, g, k_own, v_own, own_nt(k_own, q) * scale, own_nt(v_own, g)))
    fetched = normed_all[tokens:, :]
    for copy in copies:
        copy.wait()
    fetched_keys = dot_nn(fetched, w_k[...]).astype(jnp.bfloat16)
    fetched_values = dot_nn(fetched, w_v[...]).astype(jnp.bfloat16)
    for p, (q, g, k_own, v_own, s_own, dp_own) in enumerate(own):
        lanes = slice(p * pair, (p + 1) * pair)
        k_far, v_far = fetched_keys[:, lanes], fetched_values[:, lanes]
        s_far = dot_nt(k_far, q) * scale
        s_far = jnp.concatenate(
            [
                jnp.where(slot_alive[j], s_far[j * view_tokens : (j + 1) * view_tokens], MASKED)
                for j in range(groups - 1)
            ],
            axis=0,
        )
        highest = jnp.maximum(
            jnp.max(s_own, 0, keepdims=True), jnp.max(s_far, 0, keepdims=True)
        )
        e_own = jnp.exp(s_own - highest)
        e_far = jnp.exp(s_far - highest)
        inverse = 1.0 / (jnp.sum(e_own, 0, keepdims=True) + jnp.sum(e_far, 0, keepdims=True))
        a_own = e_own * inverse
        a_far = e_far * inverse
        ab_own = a_own.astype(jnp.bfloat16)
        ab_far = a_far.astype(jnp.bfloat16)
        mix = unstacked(own_tn(ab_own, v_own) + dot_tn(ab_far, v_far))
        mixed_t[lanes, :] = mix.T.astype(jnp.bfloat16)
        dvalue[:tokens, lanes] = own_nn(ab_own, g).astype(jnp.bfloat16)
        dvalue[tokens:, lanes] = dot_nn(ab_far, g).astype(jnp.bfloat16)
        dp_far = dot_nt(v_far, g)
        delta = jnp.sum(a_own * dp_own, 0, keepdims=True) + jnp.sum(a_far * dp_far, 0, keepdims=True)
        ds_own = (a_own * (dp_own - delta) * scale).astype(jnp.bfloat16)
        ds_far = (a_far * (dp_far - delta) * scale).astype(jnp.bfloat16)
        dq = unstacked(own_tn(ds_own, k_own) + dot_tn(ds_far, k_far))
        dquery[:, lanes] = dq.astype(jnp.bfloat16)
        dkey[:tokens, lanes] = own_nn(ds_own, q).astype(jnp.bfloat16)
        dkey[tokens:, lanes] = dot_nn(ds_far, q).astype(jnp.bfloat16)


def halves_kernel(scalars, left, right, x_send, y_send, x_keep, y_keep):
    size = x_send.shape[2]
    rows = x_send.shape[1]
    x, y = scalars[3], scalars[4]
    other = right[...]
    for dy, dx in ((1, 1), (0, 1), (1, 0), (0, 0)):
        block = 2 * lax.bitwise_xor(y, jnp.int32(dy)) + lax.bitwise_xor(x, jnp.int32(dx))
        columns = pl.ds(pl.multiple_of(block * 2 * rows, 2 * rows), 2 * rows)
        part = dot_tn(left[:, columns], other)
        x_out, y_out = (x_send if dx else x_keep), (y_send if dy else y_keep)
        x_out[dy] = part[:rows].astype(x_out.dtype)
        y_out[dx] = part[rows:].astype(y_out.dtype)


def first_sum_kernel(x_keep, x_got, y_keep, y_got, x_later, y_later, x_now, y_now):
    for keep, got, later, now in ((x_keep, x_got, x_later, x_now), (y_keep, y_got, y_later, y_now)):
        later[...] = (keep[1] + got[1].astype(jnp.float32)).astype(jnp.bfloat16)
        now[...] = keep[0] + got[0].astype(jnp.float32)


def second_sum_kernel(x_now, x_got, y_now, y_got, packed):
    rows = x_now.shape[0]
    packed[:rows, :] = (x_now[...] + x_got[...].astype(jnp.float32)).astype(jnp.bfloat16)
    packed[rows:, :] = (y_now[...] + y_got[...].astype(jnp.float32)).astype(jnp.bfloat16)


def last_sum_kernel(rows, packed, result):
    sources, _, size = packed.shape
    for r in range(rows):
        total = packed[r].astype(jnp.float32)
        for i in range(r + rows, sources, rows):
            total = total + packed[i].astype(jnp.float32)
        result[:, r * size : (r + 1) * size] = total


def share_kernel(scalars, mine, theirs, shares):
    size = shares.shape[1]
    for core, (here, there) in enumerate(((mine, theirs), (theirs, mine))):

        @pl.when(scalars[0] == core)
        def _():
            for i in range(2):
                shares[i] = here[i * size : (i + 1) * size, :]
                shares[2 + i] = there[i * size : (i + 1) * size, :]


def out_kernel(mixed_t, up_half, packed):
    total = dot_nn(mixed_t[0], up_half[0])
    for scene in range(1, mixed_t.shape[0]):
        total = total + dot_nn(mixed_t[scene], up_half[scene])
    packed[...] = total.astype(jnp.bfloat16)


def params(mebibytes):
    return pltpu.CompilerParams(vmem_limit_bytes=mebibytes * MIB)


def shape(dims, kind):
    return jax.ShapeDtypeStruct(dims, kind)


def shards(latents, norm_gain, w_query, w_key, w_value, w_out, kernel, partners, counts, cotangent):
    views, strip_rows, columns, width = latents.shape[1:]
    inner = w_query.shape[1]
    groups, rows = lax.axis_size("view"), lax.axis_size("row")
    scenes = lax.axis_size("scene")
    assert (strip_rows, rows, scenes) == (1, 2, 4)
    strip = strip_rows * columns
    slots = partners.shape[2]
    part = inner // rows
    tokens = views * 2 * strip
    key_tokens = tokens + (groups - 1) * 2 * strip
    bf16, f32, i32 = jnp.bfloat16, jnp.float32, jnp.int32

    row, view, scene = lax.axis_index("row"), lax.axis_index("view"), lax.axis_index("scene")
    scalars = jnp.stack((row, view, scene, scene % 2, scene // 2)).astype(i32)
    swap = [(0, 1), (1, 0)]
    along_x, along_y = [(i, i ^ 1) for i in range(scenes)], [(i, i ^ 2) for i in range(scenes)]

    request, alive = pl.pallas_call(
        functools.partial(request_kernel, views, slots, groups),
        in_specs=[SMEM, SMEM],
        out_specs=(SMEM, SMEM),
        out_shape=(shape((groups,), i32), shape((groups * views,), i32)),
        cost_estimate=LITTLE,
        name="requests",
    )(partners, counts)
    between = [[(i, i ^ d) for i in range(groups)] for d in range(1, groups)]
    granted = [lax.ppermute(request, "view", pairs) for pairs in between]

    lat = latents[0].reshape(views, strip, width)
    cot = cotangent[0].reshape(views, strip, width)
    lat_other = lax.ppermute(lat, "row", swap)
    cot_other = lax.ppermute(cot, "row", swap)

    normed, queries, keys, values, out_grad, up_half = pl.pallas_call(
        project_kernel,
        in_specs=[SMEM] + [HBM] * 4 + [VMEM] * 2 + [HBM] * 4,
        out_specs=[VMEM] * 6,
        out_shape=[
            shape((tokens, width), bf16),
            shape((tokens, part), bf16),
            shape((tokens, part), bf16),
            shape((tokens, part), bf16),
            shape((tokens, part), bf16),
            shape((scenes, tokens, width // 2), bf16),
        ],
        scratch_shapes=[pltpu.VMEM((views, strip, width), bf16)] * 4
        + [
            pltpu.VMEM((tokens, width), bf16),
            pltpu.VMEM((width, part), bf16),
            pltpu.VMEM((width, part), bf16),
            pltpu.VMEM((width, part), bf16),
            pltpu.VMEM((part, width), bf16),
            pltpu.SemaphoreType.DMA((8,)),
        ],
        compiler_params=params(51),
        cost_estimate=LITTLE,
        name="project",
    )(scalars, lat, lat_other, cot, cot_other, norm_gain, kernel, w_query, w_key, w_value, w_out)

    normed, granted = lax.optimization_barrier((normed, granted))
    outgoing = pl.pallas_call(
        functools.partial(pick_kernel, groups),
        in_specs=[SMEM] * groups + [VMEM],
        out_specs=[VMEM] * (groups - 1),
        out_shape=[shape((strip, width), bf16)] * (groups - 1),
        compiler_params=params(8),
        cost_estimate=LITTLE,
        name="pick",
    )(scalars, *granted, lat)
    got_own = [lax.ppermute(part_out, "view", pairs) for part_out, pairs in zip(outgoing, between)]
    got_other = [lax.ppermute(got, "row", swap) for got in got_own]

    up_far = lax.all_to_all(up_half, "scene", split_axis=0, concat_axis=0, tiled=True)

    normed_all, mixed_t, dquery, dkey, dvalue = pl.pallas_call(
        functools.partial(attention_kernel, views, groups),
        in_specs=[SMEM] * 2 + [VMEM] * (2 * groups - 2 + 6) + [HBM] * 2,
        out_specs=[VMEM] * 5,
        out_shape=[
            shape((key_tokens, width), bf16),
            shape((part, tokens), bf16),
            shape((tokens, part), bf16),
            shape((key_tokens, part), bf16),
            shape((key_tokens, part), bf16),
        ],
        scratch_shapes=[
            pltpu.VMEM((width, part), bf16),
            pltpu.VMEM((width, part), bf16),
            pltpu.SemaphoreType.DMA((2,)),
        ],
        compiler_params=params(48),
        cost_estimate=LITTLE,
        name="attention",
    )(
        scalars, alive, *got_own, *got_other, normed, queries, keys, values, out_grad, norm_gain, w_key, w_value
    )
    def call(kernel_body, results, operands, name, first=VMEM, mebibytes=16):
        outputs = pl.pallas_call(
            kernel_body,
            in_specs=[first] + [VMEM] * (len(operands) - 1),
            out_specs=[VMEM] * len(results),
            out_shape=results,
            compiler_params=params(mebibytes),
            cost_estimate=LITTLE,
            name=name,
        )(*operands)
        return list(outputs)

    def after(value, *earlier):
        return lax.optimization_barrier((value, *earlier))[0]

    half = width // 8
    blocks, block = (2, half, part), (half, part)

    def partial(left, right, name):
        results = [shape(blocks, bf16)] * 2 + [shape(blocks, f32)] * 2
        return call(halves_kernel, results, (scalars, left, right), name, SMEM, 24)

    def first_exchange(sends):
        return lax.ppermute(sends[0], "scene", along_x), lax.ppermute(sends[1], "scene", along_y)

    def first_sum(parts, got, name):
        results = [shape(block, bf16)] * 2 + [shape(block, f32)] * 2
        return call(first_sum_kernel, results, (parts[2], got[0], parts[3], got[1]), name)

    def second_exchange(sums):
        return lax.ppermute(sums[0], "scene", along_y), lax.ppermute(sums[1], "scene", along_x)

    def second_sum(sums, got, name):
        results = [shape((2 * half, part), bf16)]
        return call(second_sum_kernel, results, (sums[2], got[0], sums[3], got[1]), name)[0]

    targets = groups * rows

    def last_sum(packed, name):
        size = packed.shape[0] // targets
        packed = packed.reshape(targets, size, packed.shape[1])
        packed = lax.all_to_all(packed, ("view", "row"), split_axis=0, concat_axis=0, tiled=True)
        results = [shape((size, rows * packed.shape[2]), f32)]
        return call(functools.partial(last_sum_kernel, rows), results, (packed,), name)[0]

    q_parts = partial(normed, dquery, "grad_query")
    q_got = first_exchange(q_parts)
    k_parts = partial(normed_all, after(dkey, q_parts[0]), "grad_key")
    k_got = first_exchange(k_parts)
    v_parts = partial(normed_all, after(dvalue, k_parts[0]), "grad_value")
    v_got = first_exchange(v_parts)

    mixed_other = lax.ppermute(mixed_t, "row", swap)
    shares = call(
        share_kernel,
        [shape((scenes, inner // 4, tokens), bf16)],
        (scalars, mixed_t, mixed_other),
        "share",
        SMEM,
    )[0]
    mixed_far = lax.all_to_all(shares, "scene", split_axis=0, concat_axis=0, tiled=True)

    q_sums = first_sum(q_parts, q_got, "first_sum_query")
    q_got = second_exchange(q_sums)
    k_parts[2] = after(k_parts[2], q_sums[0])
    k_sums = first_sum(k_parts, k_got, "first_sum_key")
    k_got = second_exchange(k_sums)
    mixed_far = after(mixed_far, k_sums[0])
    o_packed = call(out_kernel, [shape((inner // 4, width // 2), bf16)], (mixed_far, up_far), "grad_out")[0]
    q_sums[2] = after(q_sums[2], o_packed)
    q_packed = second_sum(q_sums, q_got, "second_sum_query")
    v_parts[2] = after(v_parts[2], q_packed)
    v_sums = first_sum(v_parts, v_got, "first_sum_value")
    v_got = second_exchange(v_sums)
    k_sums[2] = after(k_sums[2], v_sums[0])
    k_packed = second_sum(k_sums, k_got, "second_sum_key")
    v_sums[2] = after(v_sums[2], k_packed)
    v_packed = second_sum(v_sums, v_got, "second_sum_value")
    return (
        last_sum(q_packed, "last_sum_query"),
        last_sum(k_packed, "last_sum_key"),
        last_sum(v_packed, "last_sum_value"),
        last_sum(o_packed, "last_sum_out"),
    )


def solution(mesh):
    tokens = P("scene", "view", "row", None, None)
    everywhere = P()
    grads = P(("scene", "view", "row"), None)
    return jax.shard_map(
        shards,
        mesh=mesh,
        in_specs=(
            tokens, everywhere, everywhere, everywhere, everywhere, everywhere, everywhere,
            P("scene", "view", None), P("scene", "view"), tokens,
        ),
        out_specs=(grads, grads, grads, grads),
        check_vma=False,
    )
```

time: 130 us -> 160 us (1.23)
  blocking collectives: 0 us -> 26.1 us
  waiting for transfers between devices: 64.9 us -> 54.6 us
  starting transfers between devices: 32.8 us -> 38.3 us
  Pallas kernels: 22.4 us -> 26.9 us
  local copies, waits for them, and re-layouts: 8.18 us -> 12.6 us
    all_to_all x0 -> x2, blocking collectives: none -> 26.1 us  [the longest x1 15 us: last_sum(): lax.all_to_all(packed, ('view', 'row'), split_axis=0, concat_axis=0, tile...]
    ppermute x10 -> x12, waiting for transfers between devices: 42 us -> 34.1 us  [the longest x3 25.9 us: first_exchange(): lax.ppermute(sends[0], 'scene', along_x)]
    all_to_all x2 -> x4, starting transfers between devices: 8.21 us -> 14.1 us  [the longest x3 10.6 us: last_sum(): lax.all_to_all(packed, ('view', 'row'), split_axis=0, concat_axis=0, tile...]
    unnamed x19 -> x49, local copies, waits for them, and re-layouts: 7.4 us -> 12.5 us
    all_to_all x2 -> x4, waiting for transfers between devices: 16 us -> 11.4 us  [the longest x3 11.4 us: last_sum(): lax.all_to_all(packed, ('view', 'row'), split_axis=0, concat_axis=0, tile...]
    pallas_call x8 -> x16, Pallas kernels: 14 us -> 18.4 us  [the longest x15 12.4 us: call(): pl.pallas_call(kernel_body, in_specs=[first] + [VMEM] * (len(operands) -...]
    ppermute x3, waiting for transfers between devices: 5.47 us -> 7.18 us  [shards(): lax.ppermute(part_out, 'view', pairs)]
    ppermute x10 -> x12, starting transfers between devices: 13.3 us -> 12.6 us  [the longest x3 4.15 us: first_exchange(): lax.ppermute(sends[0], 'scene', along_x)]
  transfers between devices with their start and end apart: 24 -> 28, of which waited for: 9 -> 14; matrix products, arithmetic and copies ran while one was open for 2% -> 1% of each run, Pallas kernels for 15% -> 10%
where the time goes in v4:
time: 160 us; the launch traced here: 159 us
  waiting for transfers between devices  54.6 us (34%)
  starting transfers between devices  38.3 us (24%)
  Pallas kernels  26.9 us (17%)
  blocking collectives  26.1 us (16%)
  local copies, waits for them, and re-layouts  12.6 us (8%)
    ppermute x3, waiting for transfers between devices, first_exchange(): lax.ppermute(sends[0], 'scene', along_x)  25.9 us
    all_to_all x1, blocking collectives, last_sum(): lax.all_to_all(packed, ('view', 'row'), split_axis=0, concat_axis=0, tile...  15 us
    unnamed x49, local copies, waits for them, and re-layouts  12.5 us
    pallas_call x15, Pallas kernels, call(): pl.pallas_call(kernel_body, in_specs=[first] + [VMEM] * (len(operands) -...  12.4 us
    all_to_all x3, waiting for transfers between devices, last_sum(): lax.all_to_all(packed, ('view', 'row'), split_axis=0, concat_axis=0, tile...  11.4 us
    all_to_all x1, blocking collectives, shards(): lax.all_to_all(shares, 'scene', split_axis=0, concat_axis=0, tiled=True)  11.2 us
    all_to_all x3, starting transfers between devices, last_sum(): lax.all_to_all(packed, ('view', 'row'), split_axis=0, concat_axis=0, tile...  10.6 us
    ppermute x3, waiting for transfers between devices, shards(): lax.ppermute(part_out, 'view', pairs)  7.18 us
  transfers between devices with their start and end apart: 28, of which 14 were waited for; matrix products, arithmetic and copies ran while one was open for 1% of the time, Pallas kernels for 10%

profile of v4, /device:TPU:0, one launch (start us, length us, event | category | flops | bytes accessed | tf_op | source)
XLA Modules:
  0.0 159.5 jit_solution(17106483957190842968)
XLA Ops:
  0.6 0.5 collective-permute-start
  1.2 1.3 copy.14.partners
  2.6 1.3 requests.1
  3.9 3.1 %collective-permute-start.2 = (s32[4]{0:T(128)}, s32[4]{0:T(128)S(1)}, u32[]{:S(2)}, u32[]{:S(2)}) collective-permute-start(s32[4]{0:T(128)} %get-tuple-element.57), channel_id=1, source_target_pairs={{0,2},{2,0},{4,6},{6,4},{1,3},{3,1},{5,7},{7,5},{8,10},{10,8},{12,... | collective-permute-start | bytes 56 | tf_op jit(solution)/shard_map/ppermute | solution.py:343
  6.9 2.6 %collective-permute-start.3 = (s32[4]{0:T(128)}, s32[4]{0:T(128)S(1)}, u32[]{:S(2)}, u32[]{:S(2)}) collective-permute-start(s32[4]{0:T(128)} %get-tuple-element.57), channel_id=1, source_target_pairs={{0,4},{2,6},{4,0},{6,2},{1,5},{3,7},{5,1},{7,3},{8,12},{10,14},{12... | collective-permute-start | bytes 56 | tf_op jit(solution)/shard_map/ppermute | solution.py:343
  9.6 1.0 copy-done.2
  10.6 1.0 copy-done.3
  11.6 0.8 copy-done.16
  12.4 0.7 copy-done.17
  13.1 6.0 %project.1 = (bf16[256,1536]{1,0:T(8,128)(2,1)}, bf16[256,384]{1,0:T(8,128)(2,1)S(1)}, bf16[256,384]{1,0:T(8,128)(2,1)S(1)}, bf16[256,384]{1,0:T(8,128)(2,1)S(1)...) custom-call(s32[5]{0:T(128)S(1)} %stack.23.scalars, bf16[4,32,1536]{2,1,0:T(8,128)(2,1)S(1)} %bitcast.12, ...), custom_call_target="tpu_custom_call" | custom-call | flops 1 | bytes 1 | tf_op jit(solution)/shard_map/project/pallas_call | solution.py:350
  19.1 0.6 pick.1
  19.7 1.0 collective-permute-start.5
  20.7 3.5 %collective-permute-start.6 = (bf16[32,1536]{1,0:T(8,128)(2,1)S(1)}, bf16[32,1536]{1,0:T(8,128)(2,1)S(1)}, u32[]{:S(2)}, u32[]{:S(2)}) collective-permute-start(bf16[32,1536]{1,0:T(8,128)(2,1)S(1)} %get-tuple-element.64), channel_id=1, source_target_pairs={{0,4},{2,6},{4,0},{6,2},{1,5},{3,7},{5,1},{7,3},{8,12},{10,14},{12... | collective-permute-start | bytes 294920 | tf_op jit(solution)/shard_map/ppermute | solution.py:386
  24.2 1.1 collective-permute-done.5.refs_0_
  25.3 6.1 %collective-permute-done.6.refs_1_ = bf16[32,1536]{1,0:T(8,128)(2,1)S(1)} collective-permute-done((bf16[32,1536]{1,0:T(8,128)(2,1)S(1)}, bf16[32,1536]{1,0:T(8,128)(2,1)S(1)}, u32[]{:S(2)}, u32[]{:S(2)}) %collective-permute-start.6) | collective-permute-done | bytes 98336 | tf_op jit(solution)/shard_map/ppermute | solution.py:386
  31.9 0.8 collective-permute-done.9.refs_4_
  32.8 1.1 copy-done
  34.0 6.6 %attention.1 = (bf16[448,1536]{1,0:T(8,128)(2,1)S(1)}, bf16[384,256]{1,0:T(8,128)(2,1)S(1)}, bf16[256,384]{1,0:T(8,128)(2,1)S(1)}, bf16[448,384]{1,0:T(8,128)(2,1)S(1)}, bf16[448,384]{1,0:T(8,128)(2,1)S(1)}) custom-call(s32[5]{0:T(128)S(1)} %stack.23.scalars, s32[16]{0:T(128)S(1)} %copy-done.19, bf16[32,1536]{1,0:T(8,128)(2,1)S(1)} %collective-permute-done.5.refs_0_, ...), custom_call_target="tpu_custom_call" | custom-call | flops 1 | bytes 1 | tf_op jit(solution)/shard_map/attention/pallas_call | solution.py:391
  41.0 1.1 collective-permute-done.13.theirs
  42.1 0.6 share.1
  42.7 11.2 %all_to_all.30.mixed_t = bf16[4,192,256]{2,1,0:T(8,128)(2,1)S(1)} all-to-all(bf16[4,192,256]{2,1,0:T(8,128)(2,1)S(1)} %share.1), channel_id=1, replica_groups=mesh['scene'=4,'view'=4,'row'=2] {'scene'}, dimensions={0} | all-to-all | bytes 786432 | tf_op jit(solution)/shard_map/all_to_all | solution.py:473
  53.8 3.6 %all-to-all-start.1 = ((bf16[4,256,768]{2,1,0:T(8,128)(2,1)}), bf16[4,256,768]{2,1,0:T(8,128)(2,1)S(1)}, u32[]{:S(2)}, u32[]{:S(2)}) async-start(bf16[4,256,768]{2,1,0:T(8,128)(2,1)} %get-tuple-element.88), calls=%async_computation.1 | async-start | bytes 3145728 | tf_op jit(solution)/shard_map/all_to_all | solution.py:389
  57.4 1.1 copy-done.1
  58.5 1.1 grad_query.1
  59.7 2.0 %collective-permute-start.11 = (bf16[2,192,384]{2,1,0:T(8,128)(2,1)S(1)}, bf16[2,192,384]{2,1,0:T(8,128)(2,1)S(1)}, u32[]{:S(2)}, u32[]{:S(2)}) collective-permute-start(bf16[2,192,384]{2,1,0:T(8,128)(2,1)S(1)} %get-tuple-element.72), channel_id=1, source_target_pairs={{0,8},{8,0},{16,24},{24,16},{1,9},{9,1},{17,25},{25,17},{2,10},{10... | collective-permute-start | bytes 884744 | tf_op jit(solution)/shard_map/ppermute | solution.py:436
  61.7 1.5 collective-permute-start.12
  63.2 1.0 copy-done.7
  64.2 1.6 grad_key.1
  65.7 0.6 collective-permute-start.14
  66.5 17.9 %collective-permute-done.11.x_got = bf16[2,192,384]{2,1,0:T(8,128)(2,1)S(1)} collective-permute-done((bf16[2,192,384]{2,1,0:T(8,128)(2,1)S(1)}, bf16[2,192,384]{2,1,0:T(8,128)(2,1)S(1)}, u32[]{:S(2)}, u32[]{:S(2)}) %collective-permute-start.11) | collective-permute-done | bytes 294944 | tf_op jit(solution)/shard_map/ppermute | solution.py:436
  84.4 0.8 first_sum_query.1
  85.2 0.7 copy-done.12
  85.9 1.5 collective-permute-start.16
  87.3 0.6 collective-permute-start.17
  87.9 2.2 %collective-permute-done.14.x_got = bf16[2,192,384]{2,1,0:T(8,128)(2,1)S(1)} collective-permute-done((bf16[2,192,384]{2,1,0:T(8,128)(2,1)S(1)}, bf16[2,192,384]{2,1,0:T(8,128)(2,1)S(1)}, u32[]{:S(2)}, u32[]{:S(2)}) %collective-permute-start.14) | collective-permute-done | bytes 294944 | tf_op jit(solution)/shard_map/ppermute | solution.py:436
  90.3 0.7 copy-done.8
  91.0 0.7 copy-done.10
  91.7 0.7 copy-done.20
  92.4 0.7 copy-done.22
  93.0 1.2 grad_out.1
  94.3 1.8 %second_sum_query.1 = bf16[384,384]{1,0:T(8,128)(2,1)} custom-call(f32[192,384]{1,0:T(8,128)S(1)} %copy-done.13, bf16[192,384]{1,0:T(8,128)(2,1)S(1)} %collective-permute-done.16.x_got, f32[192,384]{1,0:T(8,128)S(1)} %copy-done.15, bf16[192,384]{1,0:T(8,128)(2,1)} %collective-permute-done.17.y_got), custom_call_target="tpu_custom_call" | custom-call | flops 1 | bytes 1 | tf_op jit(solution)/shard_map/second_sum_query/pallas_call | solution.py:414
  96.1 3.7 %all-to-all-start.2 = ((bf16[8,48,384]{2,1,0:T(8,128)(2,1)}), bf16[8,48,384]{2,1,0:T(8,128)(2,1)S(1)}, u32[]{:S(2)}, u32[]{:S(2)}) async-start(bf16[8,48,384]{2,1,0:T(8,128)(2,1)} %bitcast.7), calls=%async_computation.2 | async-start | bytes 589824 | tf_op jit(solution)/shard_map/all_to_all | solution.py:454
  99.8 1.0 copy-done.5
  100.8 1.6 grad_value.1
  102.3 1.5 collective-permute-start.18
  103.8 0.6 collective-permute-start.19
  104.4 1.4 collective-permute-start.20
  105.8 0.6 collective-permute-start.21
  106.5 5.7 %collective-permute-done.18.x_got = bf16[2,192,384]{2,1,0:T(8,128)(2,1)S(1)} collective-permute-done((bf16[2,192,384]{2,1,0:T(8,128)(2,1)S(1)}, bf16[2,192,384]{2,1,0:T(8,128)(2,1)S(1)}, u32[]{:S(2)}, u32[]{:S(2)}) %collective-permute-start.18) | collective-permute-done | bytes 294944 | tf_op jit(solution)/shard_map/ppermute | solution.py:436
  112.2 1.4 collective-permute-done.19.y_got
  113.7 2.4 %collective-permute-done.20.x_got = bf16[192,384]{1,0:T(8,128)(2,1)S(1)} collective-permute-done((bf16[192,384]{1,0:T(8,128)(2,1)S(1)}, bf16[192,384]{1,0:T(8,128)(2,1)S(1)}, u32[]{:S(2)}, u32[]{:S(2)}) %collective-permute-start.20) | collective-permute-done | bytes 147488 | tf_op jit(solution)/shard_map/ppermute | solution.py:443
  116.2 15.0 %all_to_all.31.packed = bf16[8,48,384]{2,1,0:T(8,128)(2,1)S(1)} all-to-all(bf16[8,48,384]{2,1,0:T(8,128)(2,1)S(1)} %bitcast.14), channel_id=1, replica_groups=mesh['scene'=4,'view'=4,'row'=2] {'view','row'}, dimensions={0} | all-to-all | bytes 589824 | tf_op jit(solution)/shard_map/all_to_all | solution.py:454
  131.2 3.4 %all-to-all-start.5 = ((bf16[8,24,768]{2,1,0:T(8,128)(2,1)}), bf16[8,24,768]{2,1,0:T(8,128)(2,1)S(1)}, u32[]{:S(2)}, u32[]{:S(2)}) async-start(bf16[8,24,768]{2,1,0:T(8,128)(2,1)} %bitcast.10), calls=%async_computation.5 | async-start | bytes 589824 | tf_op jit(solution)/shard_map/all_to_all | solution.py:454
  134.6 0.7 collective-permute-start.22
  135.3 1.5 collective-permute-start.23
  136.8 4.0 %collective-permute-done.22.x_got = bf16[192,384]{1,0:T(8,128)(2,1)S(1)} collective-permute-done((bf16[192,384]{1,0:T(8,128)(2,1)S(1)}, bf16[192,384]{1,0:T(8,128)(2,1)S(1)}, u32[]{:S(2)}, u32[]{:S(2)}) %collective-permute-start.22) | collective-permute-done | bytes 147488 | tf_op jit(solution)/shard_map/ppermute | solution.py:443
  141.1 0.8 second_sum_value.1
  141.9 3.1 %all-to-all-done.5.packed = bf16[8,24,768]{2,1,0:T(8,128)(2,1)S(1)} async-done(((bf16[8,24,768]{2,1,0:T(8,128)(2,1)}), bf16[8,24,768]{2,1,0:T(8,128)(2,1)S(1)}, u32[]{:S(2)}, u32[]{:S(2)}) %all-to-all-start.5) | async-done | bytes 294944 | tf_op jit(solution)/shard_map/all_to_all | solution.py:454
  145.0 3.4 %all-to-all-start.4 = ((bf16[8,48,384]{2,1,0:T(8,128)(2,1)}), bf16[8,48,384]{2,1,0:T(8,128)(2,1)S(1)}, u32[]{:S(2)}, u32[]{:S(2)}) async-start(bf16[8,48,384]{2,1,0:T(8,128)(2,1)} %bitcast.9), calls=%async_computation.4 | async-start | bytes 589824 | tf_op jit(solution)/shard_map/all_to_all | solution.py:454
  148.4 0.7 last_sum_query.1
  149.1 0.7 last_sum_key.1
  149.8 0.7 last_sum_out.1
  150.5 8.3 %all-to-all-done.4.packed = bf16[8,48,384]{2,1,0:T(8,128)(2,1)S(1)} async-done(((bf16[8,48,384]{2,1,0:T(8,128)(2,1)}), bf16[8,48,384]{2,1,0:T(8,128)(2,1)S(1)}, u32[]{:S(2)}, u32[]{:S(2)}) %all-to-all-start.4) | async-done | bytes 294944 | tf_op jit(solution)/shard_map/all_to_all | solution.py:454
  158.8 0.7 last_sum_value.1
  (63 shorter events, 2.0 us)
Async XLA Ops:
  0.6 9.0 %collective-permute-start = (bf16[4,32,1536]{2,1,0:T(8,128)(2,1)}, bf16[4,32,1536]{2,1,0:T(8,128)(2,1)S(1)}, u32[]{:S(2)}, u32[]{:S(2)}) collective-permute-start(bf16[4,32,1536]{2,1,0:T(8,128)(2,1)} %bitcast.11), channel_id=1, source_target_pairs={{0,1},{1,0},{2,3},{3,2},{4,5},{5,4},{6,7},{7,6},{8,9},{9,8},{10,11... | collective-permute-start | bytes 1179656 | tf_op jit(solution)/shard_map/ppermute | solution.py:347
  1.1 8.5 %collective-permute-start.1 = (bf16[4,32,1536]{2,1,0:T(8,128)(2,1)}, bf16[4,32,1536]{2,1,0:T(8,128)(2,1)S(1)}, u32[]{:S(2)}, u32[]{:S(2)}) collective-permute-start(bf16[4,32,1536]{2,1,0:T(8,128)(2,1)} %bitcast.15), channel_id=1, source_target_pairs={{0,1},{1,0},{2,3},{3,2},{4,5},{5,4},{6,7},{7,6},{8,9},{9,8},{10,11... | collective-permute-start | bytes 1179656 | tf_op jit(solution)/shard_map/ppermute | solution.py:348
  3.9 15.3 %collective-permute-start.2 = (s32[4]{0:T(128)}, s32[4]{0:T(128)S(1)}, u32[]{:S(2)}, u32[]{:S(2)}) collective-permute-start(s32[4]{0:T(128)} %get-tuple-element.57), channel_id=1, source_target_pairs={{0,2},{2,0},{4,6},{6,4},{1,3},{3,1},{5,7},{7,5},{8,10},{10,8},{12,... | collective-permute-start | bytes 56 | tf_op jit(solution)/shard_map/ppermute | solution.py:343
  6.9 12.2 %collective-permute-start.3 = (s32[4]{0:T(128)}, s32[4]{0:T(128)S(1)}, u32[]{:S(2)}, u32[]{:S(2)}) collective-permute-start(s32[4]{0:T(128)} %get-tuple-element.57), channel_id=1, source_target_pairs={{0,4},{2,6},{4,0},{6,2},{1,5},{3,7},{5,1},{7,3},{8,12},{10,14},{12... | collective-permute-start | bytes 56 | tf_op jit(solution)/shard_map/ppermute | solution.py:343
  9.5 9.6 %collective-permute-start.4 = (s32[4]{0:T(128)}, s32[4]{0:T(128)S(1)}, u32[]{:S(2)}, u32[]{:S(2)}) collective-permute-start(s32[4]{0:T(128)} %get-tuple-element.57), channel_id=1, source_target_pairs={{0,6},{2,4},{4,2},{6,0},{1,7},{3,5},{5,3},{7,1},{8,14},{10,12},{12... | collective-permute-start | bytes 56 | tf_op jit(solution)/shard_map/ppermute | solution.py:343
  9.5 23.3 %copy-start.19 = (s32[16]{0:T(128)S(1)}, s32[16]{0:T(128)}, u32[]{:S(2)}) copy-start(s32[16]{0:T(128)} %get-tuple-element.59.alive) | copy-start | bytes 196
  9.6 1.0 copy-start.2
  10.6 1.0 copy-start.3
  11.6 0.8 copy-start.16
  12.4 0.7 copy-start.17
  13.1 19.7 %copy-start.18 = (f32[1536]{0:T(1024)S(1)}, f32[1536]{0:T(1024)}, u32[]{:S(2)}) copy-start(f32[1536]{0:T(1024)} %refs_11_.1) | copy-start | bytes 18436
  19.7 5.6 %collective-permute-start.5 = (bf16[32,1536]{1,0:T(8,128)(2,1)S(1)}, bf16[32,1536]{1,0:T(8,128)(2,1)S(1)}, u32[]{:S(2)}, u32[]{:S(2)}) collective-permute-start(bf16[32,1536]{1,0:T(8,128)(2,1)S(1)} %get-tuple-element.63), channel_id=1, source_target_pairs={{0,2},{2,0},{4,6},{6,4},{1,3},{3,1},{5,7},{7,5},{8,10},{10,8},{12,... | collective-permute-start | bytes 294920 | tf_op jit(solution)/shard_map/ppermute | solution.py:386
  20.7 10.7 %collective-permute-start.6 = (bf16[32,1536]{1,0:T(8,128)(2,1)S(1)}, bf16[32,1536]{1,0:T(8,128)(2,1)S(1)}, u32[]{:S(2)}, u32[]{:S(2)}) collective-permute-start(bf16[32,1536]{1,0:T(8,128)(2,1)S(1)} %get-tuple-element.64), channel_id=1, source_target_pairs={{0,4},{2,6},{4,0},{6,2},{1,5},{3,7},{5,1},{7,3},{8,12},{10,14},{12... | collective-permute-start | bytes 294920 | tf_op jit(solution)/shard_map/ppermute | solution.py:386
  24.2 7.2 %collective-permute-start.7 = (bf16[32,1536]{1,0:T(8,128)(2,1)S(1)}, bf16[32,1536]{1,0:T(8,128)(2,1)S(1)}, u32[]{:S(2)}, u32[]{:S(2)}) collective-permute-start(bf16[32,1536]{1,0:T(8,128)(2,1)S(1)} %get-tuple-element.65), channel_id=1, source_target_pairs={{0,6},{2,4},{4,2},{6,0},{1,7},{3,5},{5,3},{7,1},{8,14},{10,12},{12... | collective-permute-start | bytes 294920 | tf_op jit(solution)/shard_map/ppermute | solution.py:386
  25.3 6.6 %collective-permute-start.8 = (bf16[32,1536]{1,0:T(8,128)(2,1)S(1)}, bf16[32,1536]{1,0:T(8,128)(2,1)S(1)}, u32[]{:S(2)}, u32[]{:S(2)}) collective-permute-start(bf16[32,1536]{1,0:T(8,128)(2,1)S(1)} %collective-permute-done.5.refs_0_), channel_id=1, source_target_pairs={{0,1},{1,0},{2,3},{3,2},{4,5},{5,4},{6,7},{7,6},{8,9},{9,8},{10,11... | collective-permute-start | bytes 294920 | tf_op jit(solution)/shard_map/ppermute | solution.py:387
  31.4 1.3 collective-permute-start.9
  31.4 1.5 collective-permute-start.10
  32.8 1.1 copy-start
  40.6 13.3 %copy-start.4 = (bf16[448,384]{1,0:T(8,128)(2,1)}, bf16[448,384]{1,0:T(8,128)(2,1)S(1)}, u32[]{:S(2)}) copy-start(bf16[448,384]{1,0:T(8,128)(2,1)S(1)} %get-tuple-element.94.right) | copy-start | bytes 1032196
  40.6 13.3 %copy-start.6 = (bf16[448,384]{1,0:T(8,128)(2,1)}, bf16[448,384]{1,0:T(8,128)(2,1)S(1)}, u32[]{:S(2)}) copy-start(bf16[448,384]{1,0:T(8,128)(2,1)S(1)} %get-tuple-element.79.right) | copy-start | bytes 1032196
  40.6 1.5 collective-permute-start.13
  53.8 39.2 %all-to-all-start.1 = ((bf16[4,256,768]{2,1,0:T(8,128)(2,1)}), bf16[4,256,768]{2,1,0:T(8,128)(2,1)S(1)}, u32[]{:S(2)}, u32[]{:S(2)}) async-start(bf16[4,256,768]{2,1,0:T(8,128)(2,1)} %get-tuple-element.88), calls=%async_computation.1 | async-start | bytes 3145728 | tf_op jit(solution)/shard_map/all_to_all | solution.py:389
  57.4 1.1 copy-start.1
  59.7 24.7 %collective-permute-start.11 = (bf16[2,192,384]{2,1,0:T(8,128)(2,1)S(1)}, bf16[2,192,384]{2,1,0:T(8,128)(2,1)S(1)}, u32[]{:S(2)}, u32[]{:S(2)}) collective-permute-start(bf16[2,192,384]{2,1,0:T(8,128)(2,1)S(1)} %get-tuple-element.72), channel_id=1, source_target_pairs={{0,8},{8,0},{16,24},{24,16},{1,9},{9,1},{17,25},{25,17},{2,10},{10... | collective-permute-start | bytes 884744 | tf_op jit(solution)/shard_map/ppermute | solution.py:436
  61.7 22.6 %collective-permute-start.12 = (bf16[2,192,384]{2,1,0:T(8,128)(2,1)S(1)}, bf16[2,192,384]{2,1,0:T(8,128)(2,1)S(1)}, u32[]{:S(2)}, u32[]{:S(2)}) collective-permute-start(bf16[2,192,384]{2,1,0:T(8,128)(2,1)S(1)} %get-tuple-element.74), channel_id=1, source_target_pairs={{0,16},{8,24},{16,0},{24,8},{1,17},{9,25},{17,1},{25,9},{2,18},{10... | collective-permute-start | bytes 884744 | tf_op jit(solution)/shard_map/ppermute | solution.py:436
  63.2 1.0 copy-start.7
  65.7 24.4 %collective-permute-start.14 = (bf16[2,192,384]{2,1,0:T(8,128)(2,1)S(1)}, bf16[2,192,384]{2,1,0:T(8,128)(2,1)S(1)}, u32[]{:S(2)}, u32[]{:S(2)}) collective-permute-start(bf16[2,192,384]{2,1,0:T(8,128)(2,1)S(1)} %get-tuple-element.83), channel_id=1, source_target_pairs={{0,8},{8,0},{16,24},{24,16},{1,9},{9,1},{17,25},{25,17},{2,10},{10... | collective-permute-start | bytes 884744 | tf_op jit(solution)/shard_map/ppermute | solution.py:436
  66.4 23.8 %collective-permute-start.15 = (bf16[2,192,384]{2,1,0:T(8,128)(2,1)S(1)}, bf16[2,192,384]{2,1,0:T(8,128)(2,1)S(1)}, u32[]{:S(2)}, u32[]{:S(2)}) collective-permute-start(bf16[2,192,384]{2,1,0:T(8,128)(2,1)S(1)} %get-tuple-element.85), channel_id=1, source_target_pairs={{0,16},{8,24},{16,0},{24,8},{1,17},{9,25},{17,1},{25,9},{2,18},{10... | collective-permute-start | bytes 884744 | tf_op jit(solution)/shard_map/ppermute | solution.py:436
  85.2 0.7 copy-start.12
  85.9 4.4 %copy-start.14 = (f32[192,384]{1,0:T(8,128)}, f32[192,384]{1,0:T(8,128)S(1)}, u32[]{:S(2)}) copy-start(f32[192,384]{1,0:T(8,128)S(1)} %get-tuple-element.90.y_now) | copy-start | bytes 884740
  85.9 8.4 %collective-permute-start.16 = (bf16[192,384]{1,0:T(8,128)(2,1)}, bf16[192,384]{1,0:T(8,128)(2,1)S(1)}, u32[]{:S(2)}, u32[]{:S(2)}) collective-permute-start(bf16[192,384]{1,0:T(8,128)(2,1)} %get-tuple-element.81), channel_id=1, source_target_pairs={{0,16},{8,24},{16,0},{24,8},{1,17},{9,25},{17,1},{25,9},{2,18},{10... | collective-permute-start | bytes 442376 | tf_op jit(solution)/shard_map/ppermute | solution.py:443
  87.3 6.9 %collective-permute-start.17 = (bf16[192,384]{1,0:T(8,128)(2,1)}, bf16[192,384]{1,0:T(8,128)(2,1)}, u32[]{:S(2)}, u32[]{:S(2)}) collective-permute-start(bf16[192,384]{1,0:T(8,128)(2,1)} %get-tuple-element.91), channel_id=1, source_target_pairs={{0,8},{8,0},{16,24},{24,16},{1,9},{9,1},{17,25},{25,17},{2,10},{10... | collective-permute-start | bytes 442376 | tf_op jit(solution)/shard_map/ppermute | solution.py:443
  90.3 0.7 copy-start.8
  91.0 0.7 copy-start.10
  91.7 0.7 copy-start.20
  92.4 0.7 copy-start.22
  93.0 1.2 copy-start.13
  93.0 1.2 copy-start.15
  94.2 10.2 %copy-start.23 = (bf16[192,384]{1,0:T(8,128)(2,1)S(1)}, bf16[192,384]{1,0:T(8,128)(2,1)}, u32[]{:S(2)}) copy-start(bf16[192,384]{1,0:T(8,128)(2,1)} %copy-done.22) | copy-start | bytes 442372
  94.2 11.6 %copy-start.21 = (bf16[192,384]{1,0:T(8,128)(2,1)S(1)}, bf16[192,384]{1,0:T(8,128)(2,1)}, u32[]{:S(2)}) copy-start(bf16[192,384]{1,0:T(8,128)(2,1)} %copy-done.20) | copy-start | bytes 442372
  94.3 21.8 %copy-start.9 = (f32[192,384]{1,0:T(8,128)S(1)}, f32[192,384]{1,0:T(8,128)}, u32[]{:S(2)}) copy-start(f32[192,384]{1,0:T(8,128)} %copy-done.8) | copy-start | bytes 884740
  94.3 21.8 %copy-start.11 = (f32[192,384]{1,0:T(8,128)S(1)}, f32[192,384]{1,0:T(8,128)}, u32[]{:S(2)}) copy-start(f32[192,384]{1,0:T(8,128)} %copy-done.10) | copy-start | bytes 884740
  96.1 20.1 %all-to-all-start.2 = ((bf16[8,48,384]{2,1,0:T(8,128)(2,1)}), bf16[8,48,384]{2,1,0:T(8,128)(2,1)S(1)}, u32[]{:S(2)}, u32[]{:S(2)}) async-start(bf16[8,48,384]{2,1,0:T(8,128)(2,1)} %bitcast.7), calls=%async_computation.2 | async-start | bytes 589824 | tf_op jit(solution)/shard_map/all_to_all | solution.py:454
  99.8 1.0 copy-start.5
  102.3 9.9 %collective-permute-start.18 = (bf16[2,192,384]{2,1,0:T(8,128)(2,1)S(1)}, bf16[2,192,384]{2,1,0:T(8,128)(2,1)S(1)}, u32[]{:S(2)}, u32[]{:S(2)}) collective-permute-start(bf16[2,192,384]{2,1,0:T(8,128)(2,1)S(1)} %get-tuple-element.97), channel_id=1, source_target_pairs={{0,8},{8,0},{16,24},{24,16},{1,9},{9,1},{17,25},{25,17},{2,10},{10... | collective-permute-start | bytes 884744 | tf_op jit(solution)/shard_map/ppermute | solution.py:436
  103.8 9.8 %collective-permute-start.19 = (bf16[2,192,384]{2,1,0:T(8,128)(2,1)S(1)}, bf16[2,192,384]{2,1,0:T(8,128)(2,1)S(1)}, u32[]{:S(2)}, u32[]{:S(2)}) collective-permute-start(bf16[2,192,384]{2,1,0:T(8,128)(2,1)S(1)} %get-tuple-element.99), channel_id=1, source_target_pairs={{0,16},{8,24},{16,0},{24,8},{1,17},{9,25},{17,1},{25,9},{2,18},{10... | collective-permute-start | bytes 884744 | tf_op jit(solution)/shard_map/ppermute | solution.py:436
  104.4 11.7 %collective-permute-start.20 = (bf16[192,384]{1,0:T(8,128)(2,1)S(1)}, bf16[192,384]{1,0:T(8,128)(2,1)S(1)}, u32[]{:S(2)}, u32[]{:S(2)}) collective-permute-start(bf16[192,384]{1,0:T(8,128)(2,1)S(1)} %copy-done.23), channel_id=1, source_target_pairs={{0,16},{8,24},{16,0},{24,8},{1,17},{9,25},{17,1},{25,9},{2,18},{10... | collective-permute-start | bytes 442376 | tf_op jit(solution)/shard_map/ppermute | solution.py:443
  105.8 10.3 %collective-permute-start.21 = (bf16[192,384]{1,0:T(8,128)(2,1)S(1)}, bf16[192,384]{1,0:T(8,128)(2,1)S(1)}, u32[]{:S(2)}, u32[]{:S(2)}) collective-permute-start(bf16[192,384]{1,0:T(8,128)(2,1)S(1)} %copy-done.21), channel_id=1, source_target_pairs={{0,8},{8,0},{16,24},{24,16},{1,9},{9,1},{17,25},{25,17},{2,10},{10... | collective-permute-start | bytes 442376 | tf_op jit(solution)/shard_map/ppermute | solution.py:443
  131.2 13.8 %all-to-all-start.5 = ((bf16[8,24,768]{2,1,0:T(8,128)(2,1)}), bf16[8,24,768]{2,1,0:T(8,128)(2,1)S(1)}, u32[]{:S(2)}, u32[]{:S(2)}) async-start(bf16[8,24,768]{2,1,0:T(8,128)(2,1)} %bitcast.10), calls=%async_computation.5 | async-start | bytes 589824 | tf_op jit(solution)/shard_map/all_to_all | solution.py:454
  134.6 6.2 %collective-permute-start.22 = (bf16[192,384]{1,0:T(8,128)(2,1)S(1)}, bf16[192,384]{1,0:T(8,128)(2,1)S(1)}, u32[]{:S(2)}, u32[]{:S(2)}) collective-permute-start(bf16[192,384]{1,0:T(8,128)(2,1)S(1)} %get-tuple-element.100), channel_id=1, source_target_pairs={{0,16},{8,24},{16,0},{24,8},{1,17},{9,25},{17,1},{25,9},{2,18},{10... | collective-permute-start | bytes 442376 | tf_op jit(solution)/shard_map/ppermute | solution.py:443
  135.3 5.8 %collective-permute-start.23 = (bf16[192,384]{1,0:T(8,128)(2,1)S(1)}, bf16[192,384]{1,0:T(8,128)(2,1)S(1)}, u32[]{:S(2)}, u32[]{:S(2)}) collective-permute-start(bf16[192,384]{1,0:T(8,128)(2,1)S(1)} %get-tuple-element.107), channel_id=1, source_target_pairs={{0,8},{8,0},{16,24},{24,16},{1,9},{9,1},{17,25},{25,17},{2,10},{10... | collective-permute-start | bytes 442376 | tf_op jit(solution)/shard_map/ppermute | solution.py:443
  145.0 13.8 %all-to-all-start.4 = ((bf16[8,48,384]{2,1,0:T(8,128)(2,1)}), bf16[8,48,384]{2,1,0:T(8,128)(2,1)S(1)}, u32[]{:S(2)}, u32[]{:S(2)}) async-start(bf16[8,48,384]{2,1,0:T(8,128)(2,1)} %bitcast.9), calls=%async_computation.4 | async-start | bytes 589824 | tf_op jit(solution)/shard_map/all_to_all | solution.py:454

commit v5 on v4

--- a/solution.py
+++ b/solution.py
@@ -67,8 +67,8 @@
 
 def project_kernel(
     scalars, lat_own_far, lat_other_far, cot_own_far, cot_other_far, gain, taps, w_query, w_key, w_value, w_out,
-    normed, queries, keys, values, out_grad, up_half,
-    lat_own, lat_other, cot_own, cot_other, upstream, w_q, w_k, w_v, w_o, arrived,
+    normed, queries, keys, values, out_grad, upstream,
+    lat_own, lat_other, cot_own, cot_other, w_q, w_k, w_v, w_o, arrived,
 ):
     views, strip, width = lat_own.shape
     inputs = [
@@ -126,9 +126,6 @@
                     total = total + middle[b : b + 1] * shifted[half][b]
                     total = total + cross[half][b : b + 1] * shifted[1 - half][b]
                 upstream[strip_of(u, half), lanes] = total.astype(jnp.bfloat16)
-    half_size = width // 2
-    for scene in range(up_half.shape[0]):
-        up_half[scene] = upstream[:, pl.ds(pl.multiple_of(row * half_size, half_size), half_size)]
     rows = normed[...]
     for copy, weight, result in zip(copies, (w_q, w_k, w_v), (queries, keys, values)):
         copy.wait()
@@ -140,7 +137,7 @@
 def attention_kernel(views, groups, scalars, alive, *refs):
     got_own, got_other, refs = refs[: groups - 1], refs[groups - 1 : 2 * groups - 2], refs[2 * groups - 2 :]
     normed, queries, keys, values, out_grad, gain, w_key, w_value, *refs = refs
-    normed_all, mixed_t, dquery, dkey, dvalue, w_k, w_v, arrived = refs
+    normed_all, mixed, dquery, dkey, dvalue, w_k, w_v, arrived = refs
     copies = [
         weight_copy(scalars, w_key, w_k, arrived, 0, 1),
         weight_copy(scalars, w_value, w_v, arrived, 1, 1),
@@ -239,7 +236,7 @@
         ab_own = a_own.astype(jnp.bfloat16)
         ab_far = a_far.astype(jnp.bfloat16)
         mix = unstacked(own_tn(ab_own, v_own) + dot_tn(ab_far, v_far))
-        mixed_t[lanes, :] = mix.T.astype(jnp.bfloat16)
+        mixed[:, lanes] = mix.astype(jnp.bfloat16)
         dvalue[:tokens, lanes] = own_nn(ab_own, g).astype(jnp.bfloat16)
         dvalue[tokens:, lanes] = dot_nn(ab_far, g).astype(jnp.bfloat16)
         dp_far = dot_nt(v_far, g)
@@ -252,18 +249,36 @@
         dkey[tokens:, lanes] = dot_nn(ds_far, q).astype(jnp.bfloat16)
 
 
-def halves_kernel(scalars, left, right, x_send, y_send, x_keep, y_keep):
-    size = x_send.shape[2]
-    rows = x_send.shape[1]
+def by_quarters(scalars, left, right, send, keep, x_first):
+    size = send.shape[1]
     x, y = scalars[3], scalars[4]
-    other = right[...]
-    for dy, dx in ((1, 1), (0, 1), (1, 0), (0, 0)):
-        block = 2 * lax.bitwise_xor(y, jnp.int32(dy)) + lax.bitwise_xor(x, jnp.int32(dx))
-        columns = pl.ds(pl.multiple_of(block * 2 * rows, 2 * rows), 2 * rows)
-        part = dot_tn(left[:, columns], other)
-        x_out, y_out = (x_send if dx else x_keep), (y_send if dy else y_keep)
-        x_out[dy] = part[:rows].astype(x_out.dtype)
-        y_out[dx] = part[rows:].astype(y_out.dtype)
+    for target, first in ((send, 1), (keep, 0)):
+        for second in (1, 0):
+            dx, dy = (first, second) if x_first else (second, first)
+            block = 2 * lax.bitwise_xor(y, jnp.int32(dy)) + lax.bitwise_xor(x, jnp.int32(dx))
+            columns = pl.ds(pl.multiple_of(block * size, size), size)
+            target[second] = dot_tn(left[:, columns], right[...]).astype(target.dtype)
+
+
+def query_key_kernel(scalars, normed, dquery, normed_all, dkey, q_send, k_send, q_keep, k_keep):
+    by_quarters(scalars, normed, dquery, q_send, q_keep, True)
+    by_quarters(scalars, normed_all, dkey, k_send, k_keep, False)
+
+
+def value_out_kernel(
+    scalars, normed_all, dvalue, mine, theirs, upstream, v_send, o_send, v_keep, o_keep
+):
+    by_quarters(scalars, normed_all, dvalue, v_send, v_keep, True)
+    row, x, y = scalars[0], scalars[3], scalars[4]
+    size, width = o_send.shape[1:]
+    right = upstream[:, pl.ds(pl.multiple_of(row * width, width), width)]
+    from_mine, from_theirs = dot_tn(mine[...], right), dot_tn(theirs[...], right)
+    keep_mine = row == y
+    for block in range(2):
+        place = pl.ds(lax.bitwise_xor(x, jnp.int32(block)), 1)
+        rows = slice(block * size, (block + 1) * size)
+        o_send[place] = jnp.where(keep_mine, from_theirs[rows], from_mine[rows])[None].astype(o_send.dtype)
+        o_keep[place] = jnp.where(keep_mine, from_mine[rows], from_theirs[rows])[None]
 
 
 def first_sum_kernel(x_keep, x_got, y_keep, y_got, x_later, y_later, x_now, y_now):
@@ -272,37 +287,51 @@
         now[...] = keep[0] + got[0].astype(jnp.float32)
 
 
-def second_sum_kernel(x_now, x_got, y_now, y_got, packed):
-    rows = x_now.shape[0]
-    packed[:rows, :] = (x_now[...] + x_got[...].astype(jnp.float32)).astype(jnp.bfloat16)
-    packed[rows:, :] = (y_now[...] + y_got[...].astype(jnp.float32)).astype(jnp.bfloat16)
-
-
-def last_sum_kernel(rows, packed, result):
-    sources, _, size = packed.shape
+def pack_query_key_kernel(q_now, q_got, k_now, k_got, packed):
+    size = q_now.shape[1]
+    packed[:, :size] = (q_now[...] + q_got[...].astype(jnp.float32)).astype(jnp.bfloat16)
+    packed[:, size:] = (k_now[...] + k_got[...].astype(jnp.float32)).astype(jnp.bfloat16)
+
+
+def pack_value_out_kernel(v_now, v_got, o_now, o_got, packed):
+    grad_v = v_now[...] + v_got[...].astype(jnp.float32)
+    grad_o = o_now[...] + o_got[...].astype(jnp.float32)
+    targets, size, _ = packed.shape
+    for i in range(targets):
+        packed[i] = jnp.concatenate(
+            (
+                grad_o[i * size : (i + 1) * size],
+                grad_v[2 * i * size : (2 * i + 1) * size],
+                grad_v[(2 * i + 1) * size : (2 * i + 2) * size],
+            ),
+            axis=1,
+        ).astype(jnp.bfloat16)
+
+
+def summed_views(rows, packed):
     for r in range(rows):
         total = packed[r].astype(jnp.float32)
-        for i in range(r + rows, sources, rows):
+        for i in range(r + rows, packed.shape[0], rows):
             total = total + packed[i].astype(jnp.float32)
-        result[:, r * size : (r + 1) * size] = total
-
-
-def share_kernel(scalars, mine, theirs, shares):
-    size = shares.shape[1]
-    for core, (here, there) in enumerate(((mine, theirs), (theirs, mine))):
-
-        @pl.when(scalars[0] == core)
-        def _():
-            for i in range(2):
-                shares[i] = here[i * size : (i + 1) * size, :]
-                shares[2 + i] = there[i * size : (i + 1) * size, :]
-
-
-def out_kernel(mixed_t, up_half, packed):
-    total = dot_nn(mixed_t[0], up_half[0])
-    for scene in range(1, mixed_t.shape[0]):
-        total = total + dot_nn(mixed_t[scene], up_half[scene])
-    packed[...] = total.astype(jnp.bfloat16)
+        yield r, total
+
+
+def last_query_key_kernel(rows, packed, query, key):
+    size = packed.shape[2] // 2
+    for r, total in summed_views(rows, packed):
+        columns = slice(r * size, (r + 1) * size)
+        query[:, columns] = total[:, :size]
+        key[:, columns] = total[:, size:]
+
+
+def last_value_out_kernel(rows, packed, value, out):
+    _, size, width = packed.shape
+    half, quarter = width // 2, width // 4
+    for r, total in summed_views(rows, packed):
+        columns = slice(r * quarter, (r + 1) * quarter)
+        out[:, r * half : (r + 1) * half] = total[:, :half]
+        value[:size, columns] = total[:, half : half + quarter]
+        value[size:, columns] = total[:, half + quarter :]
 
 
 def params(mebibytes):
@@ -347,7 +376,7 @@
     lat_other = lax.ppermute(lat, "row", swap)
     cot_other = lax.ppermute(cot, "row", swap)
 
-    normed, queries, keys, values, out_grad, up_half = pl.pallas_call(
+    normed, queries, keys, values, out_grad, upstream = pl.pallas_call(
         project_kernel,
         in_specs=[SMEM] + [HBM] * 4 + [VMEM] * 2 + [HBM] * 4,
         out_specs=[VMEM] * 6,
@@ -357,11 +386,10 @@
             shape((tokens, part), bf16),
             shape((tokens, part), bf16),
             shape((tokens, part), bf16),
-            shape((scenes, tokens, width // 2), bf16),
+            shape((tokens, width), bf16),
         ],
         scratch_shapes=[pltpu.VMEM((views, strip, width), bf16)] * 4
         + [
-            pltpu.VMEM((tokens, width), bf16),
             pltpu.VMEM((width, part), bf16),
             pltpu.VMEM((width, part), bf16),
             pltpu.VMEM((width, part), bf16),
@@ -386,15 +414,13 @@
     got_own = [lax.ppermute(part_out, "view", pairs) for part_out, pairs in zip(outgoing, between)]
     got_other = [lax.ppermute(got, "row", swap) for got in got_own]
 
-    up_far = lax.all_to_all(up_half, "scene", split_axis=0, concat_axis=0, tiled=True)
-
-    normed_all, mixed_t, dquery, dkey, dvalue = pl.pallas_call(
+    normed_all, mixed, dquery, dkey, dvalue = pl.pallas_call(
         functools.partial(attention_kernel, views, groups),
         in_specs=[SMEM] * 2 + [VMEM] * (2 * groups - 2 + 6) + [HBM] * 2,
         out_specs=[VMEM] * 5,
         out_shape=[
             shape((key_tokens, width), bf16),
-            shape((part, tokens), bf16),
+            shape((tokens, part), bf16),
             shape((tokens, part), bf16),
             shape((key_tokens, part), bf16),
             shape((key_tokens, part), bf16),
@@ -425,75 +451,76 @@
     def after(value, *earlier):
         return lax.optimization_barrier((value, *earlier))[0]
 
-    half = width // 8
-    blocks, block = (2, half, part), (half, part)
-
-    def partial(left, right, name):
-        results = [shape(blocks, bf16)] * 2 + [shape(blocks, f32)] * 2
-        return call(halves_kernel, results, (scalars, left, right), name, SMEM, 24)
+    targets = groups * rows
+    q_size, o_size = width // 4, inner // 4
+    q_rows, o_rows = q_size // targets, o_size // targets
+    q_block, o_block = (q_size, part), (o_size, width // 2)
 
     def first_exchange(sends):
         return lax.ppermute(sends[0], "scene", along_x), lax.ppermute(sends[1], "scene", along_y)
 
     def first_sum(parts, got, name):
-        results = [shape(block, bf16)] * 2 + [shape(block, f32)] * 2
+        blocks = [part_now.shape[1:] for part_now in parts[:2]]
+        results = [shape(block, bf16) for block in blocks] + [shape(block, f32) for block in blocks]
         return call(first_sum_kernel, results, (parts[2], got[0], parts[3], got[1]), name)
 
     def second_exchange(sums):
         return lax.ppermute(sums[0], "scene", along_y), lax.ppermute(sums[1], "scene", along_x)
 
-    def second_sum(sums, got, name):
-        results = [shape((2 * half, part), bf16)]
-        return call(second_sum_kernel, results, (sums[2], got[0], sums[3], got[1]), name)[0]
-
-    targets = groups * rows
-
-    def last_sum(packed, name):
-        size = packed.shape[0] // targets
-        packed = packed.reshape(targets, size, packed.shape[1])
-        packed = lax.all_to_all(packed, ("view", "row"), split_axis=0, concat_axis=0, tiled=True)
-        results = [shape((size, rows * packed.shape[2]), f32)]
-        return call(functools.partial(last_sum_kernel, rows), results, (packed,), name)[0]
-
-    q_parts = partial(normed, dquery, "grad_query")
-    q_got = first_exchange(q_parts)
-    k_parts = partial(normed_all, after(dkey, q_parts[0]), "grad_key")
-    k_got = first_exchange(k_parts)
-    v_parts = partial(normed_all, after(dvalue, k_parts[0]), "grad_value")
-    v_got = first_exchange(v_parts)
-
-    mixed_other = lax.ppermute(mixed_t, "row", swap)
-    shares = call(
-        share_kernel,
-        [shape((scenes, inner // 4, tokens), bf16)],
-        (scalars, mixed_t, mixed_other),
-        "share",
+    def across_views(packed):
+        return lax.all_to_all(packed, ("view", "row"), split_axis=0, concat_axis=0, tiled=True)
+
+    mixed_other = lax.ppermute(mixed, "row", swap)
+
+    results = [shape((2, *q_block), bf16)] * 2 + [shape((2, *q_block), f32)] * 2
+    qk_parts = call(
+        query_key_kernel, results, (scalars, normed, dquery, normed_all, dkey), "grad_query_key", SMEM, 24
+    )
+    qk_got = first_exchange(qk_parts)
+    results = [shape((2, *block), kind) for kind in (bf16, f32) for block in (q_block, o_block)]
+    vo_parts = call(
+        value_out_kernel,
+        results,
+        (scalars, normed_all, after(dvalue, qk_parts[0]), mixed, mixed_other, upstream),
+        "grad_value_out",
         SMEM,
+        24,
+    )
+    vo_got = first_exchange(vo_parts)
+
+    qk_sums = first_sum(qk_parts, qk_got, "first_sum_query_key")
+    qk_got = second_exchange(qk_sums)
+    packed = call(
+        pack_query_key_kernel,
+        [shape((q_size, 2 * part), bf16)],
+        (qk_sums[2], qk_got[0], qk_sums[3], qk_got[1]),
+        "second_sum_query_key",
     )[0]
-    mixed_far = lax.all_to_all(shares, "scene", split_axis=0, concat_axis=0, tiled=True)
-
-    q_sums = first_sum(q_parts, q_got, "first_sum_query")
-    q_got = second_exchange(q_sums)
-    k_parts[2] = after(k_parts[2], q_sums[0])
-    k_sums = first_sum(k_parts, k_got, "first_sum_key")
-    k_got = second_exchange(k_sums)
-    mixed_far = after(mixed_far, k_sums[0])
-    o_packed = call(out_kernel, [shape((inner // 4, width // 2), bf16)], (mixed_far, up_far), "grad_out")[0]
-    q_sums[2] = after(q_sums[2], o_packed)
-    q_packed = second_sum(q_sums, q_got, "second_sum_query")
-    v_parts[2] = after(v_parts[2], q_packed)
-    v_sums = first_sum(v_parts, v_got, "first_sum_value")
-    v_got = second_exchange(v_sums)
-    k_sums[2] = after(k_sums[2], v_sums[0])
-    k_packed = second_sum(k_sums, k_got, "second_sum_key")
-    v_sums[2] = after(v_sums[2], k_packed)
-    v_packed = second_sum(v_sums, v_got, "second_sum_value")
-    return (
-        last_sum(q_packed, "last_sum_query"),
-        last_sum(k_packed, "last_sum_key"),
-        last_sum(v_packed, "last_sum_value"),
-        last_sum(o_packed, "last_sum_out"),
+    vo_parts[2] = after(vo_parts[2], packed)
+    packed = across_views(packed.reshape(targets, q_rows, 2 * part))
+    grad_query, grad_key = call(
+        functools.partial(last_query_key_kernel, rows),
+        [shape((q_rows, inner), f32)] * 2,
+        (packed,),
+        "last_sum_query_key",
     )
+
+    vo_sums = first_sum(vo_parts, vo_got, "first_sum_value_out")
+    vo_got = second_exchange(vo_sums)
+    packed = call(
+        pack_value_out_kernel,
+        [shape((targets, o_rows, width), bf16)],
+        (vo_sums[2], vo_got[0], vo_sums[3], vo_got[1]),
+        "second_sum_value_out",
+    )[0]
+    packed = across_views(packed)
+    grad_value, grad_out = call(
+        functools.partial(last_value_out_kernel, rows),
+        [shape((q_rows, inner), f32), shape((o_rows, width), f32)],
+        (packed,),
+        "last_sum_value_out",
+    )
+    return grad_query, grad_key, grad_value, grad_out
 
 
 def solution(mesh):

time: 160 us -> 125 us (0.78)
  blocking collectives: 26.1 us -> 0 us
  waiting for transfers between devices: 54.6 us -> 65.9 us
  starting transfers between devices: 38.3 us -> 29.5 us
  local copies, waits for them, and re-layouts: 12.6 us -> 6.05 us
  Pallas kernels: 26.9 us -> 21.8 us
    all_to_all x2 -> x0, blocking collectives: 26.1 us -> none  [the longest x1 15 us: last_sum(): lax.all_to_all(packed, ('view', 'row'), split_axis=0, concat_axis=0, tile...]
    ppermute x3 -> x2, waiting for transfers between devices: 1.46 us -> 13.8 us  [first_exchange(): lax.ppermute(sends[1], 'scene', along_y)]
    ppermute x3 -> x2, waiting for transfers between devices: 25.9 us -> 14.1 us  [first_exchange(): lax.ppermute(sends[0], 'scene', along_x)]
    unnamed x49 -> x17, local copies, waits for them, and re-layouts: 12.5 us -> 5.96 us
    ppermute x3 -> x2, waiting for transfers between devices: 6.37 us -> 12.5 us  [second_exchange(): lax.ppermute(sums[0], 'scene', along_y)]
    all_to_all x4 -> x2, starting transfers between devices: 14.1 us -> 8.08 us  [across_views(): lax.all_to_all(packed, ('view', 'row'), split_axis=0, concat_axis=0, tile...]
    pallas_call x15 -> x8, Pallas kernels: 12.4 us -> 7.68 us  [call(): pl.pallas_call(kernel_body, in_specs=[first] + [VMEM] * (len(operands) -...]
    all_to_all x4 -> x2, waiting for transfers between devices: 11.4 us -> 16 us  [across_views(): lax.all_to_all(packed, ('view', 'row'), split_axis=0, concat_axis=0, tile...]
  transfers between devices with their start and end apart: 28 -> 22, of which waited for: 14 -> 13; matrix products, arithmetic and copies ran while one was open for 1% -> 1% of each run, Pallas kernels for 10% -> 9%
where the time goes in v5:
time: 125 us; the launch traced here: 124 us
  waiting for transfers between devices  65.9 us (53%)
  starting transfers between devices  29.5 us (24%)
  Pallas kernels  21.8 us (17%)
  local copies, waits for them, and re-layouts  6.05 us (5%)
    all_to_all x2, waiting for transfers between devices, across_views(): lax.all_to_all(packed, ('view', 'row'), split_axis=0, concat_axis=0, tile...  16 us
    ppermute x2, waiting for transfers between devices, first_exchange(): lax.ppermute(sends[0], 'scene', along_x)  14.1 us
    ppermute x2, waiting for transfers between devices, first_exchange(): lax.ppermute(sends[1], 'scene', along_y)  13.8 us
    ppermute x2, waiting for transfers between devices, second_exchange(): lax.ppermute(sums[0], 'scene', along_y)  12.5 us
    all_to_all x2, starting transfers between devices, across_views(): lax.all_to_all(packed, ('view', 'row'), split_axis=0, concat_axis=0, tile...  8.08 us
    pallas_call x8, Pallas kernels, call(): pl.pallas_call(kernel_body, in_specs=[first] + [VMEM] * (len(operands) -...  7.68 us
    ppermute x3, waiting for transfers between devices, shards(): lax.ppermute(part_out, 'view', pairs)  7.11 us
    pallas_call x1, Pallas kernels, shards(): pl.pallas_call(functools.partial(attention_kernel, views, groups), in_spe...  6.56 us
  transfers between devices with their start and end apart: 22, of which 13 were waited for; matrix products, arithmetic and copies ran while one was open for 1% of the time, Pallas kernels for 9%

profile of v5, /device:TPU:0, one launch (start us, length us, event | category | flops | bytes accessed | tf_op | source)
XLA Modules:
  0.0 124.0 jit_solution(6364350413281594185)
XLA Ops:
  0.6 0.5 collective-permute-start
  1.1 0.1 collective-permute-start.1
  1.2 1.3 %copy.14.partners = s32[1,4,3]{2,1,0:T(4,128)} copy(s32[1,4,3]{1,0,2:T(1,128)} %param.17) | data formatting | bytes 96 | tf_op args[7]
  2.6 1.3 %requests.1 = (s32[4]{0:T(128)}, s32[16]{0:T(128)}) custom-call(s32[1,4,3]{2,1,0:T(4,128)} %copy.14.partners, s32[1,4]{1,0:T(1,128)} %counts.1), custom_call_target="tpu_custom_call" | custom-call | flops 1 | bytes 1 | tf_op jit(solution)/shard_map/requests/pallas_call | solution.py:363
  3.9 5.1 %collective-permute-start.4 = (s32[4]{0:T(128)}, s32[4]{0:T(128)S(1)}, u32[]{:S(2)}, u32[]{:S(2)}) collective-permute-start(s32[4]{0:T(128)} %get-tuple-element.47), channel_id=1, source_target_pairs={{0,6},{2,4},{4,2},{6,0},{1,7},{3,5},{5,3},{7,1},{8,14},{10,12},{12... | collective-permute-start | bytes 56 | tf_op jit(solution)/shard_map/ppermute | solution.py:372
  8.9 0.0 collective-permute-start.3
  9.0 0.6 collective-permute-start.2
  9.6 0.1 stack.23.scalars
  9.7 0.0 collective-permute-done.lat_other_far
  9.7 0.0 collective-permute-done.1.cot_other_far
  9.7 1.0 copy-done.1
  10.7 1.0 copy-done.3
  11.7 0.8 copy-done.4
  12.5 0.7 copy-done.5
  13.2 5.7 %project.1 = (bf16[256,1536]{1,0:T(8,128)(2,1)}, bf16[256,384]{1,0:T(8,128)(2,1)S(1)}, bf16[256,384]{1,0:T(8,128)(2,1)S(1)}, bf16[256,384]{1,0:T(8,128)(2,1)S(1)...) custom-call(s32[5]{0:T(128)S(1)} %stack.23.scalars, bf16[4,32,1536]{2,1,0:T(8,128)(2,1)S(1)} %bitcast.9, ...), custom_call_target="tpu_custom_call" | custom-call | flops 1 | bytes 1 | tf_op jit(solution)/shard_map/project/pallas_call | solution.py:379
  18.9 0.0 collective-permute-done.4.refs_2_
  18.9 0.0 collective-permute-done.3.refs_1_
  18.9 0.0 collective-permute-done.2.refs_0_
  19.0 0.6 pick.1
  19.6 1.5 %collective-permute-start.5 = (bf16[32,1536]{1,0:T(8,128)(2,1)S(1)}, bf16[32,1536]{1,0:T(8,128)(2,1)S(1)}, u32[]{:S(2)}, u32[]{:S(2)}) collective-permute-start(bf16[32,1536]{1,0:T(8,128)(2,1)S(1)} %get-tuple-element.53), channel_id=1, source_target_pairs={{0,2},{2,0},{4,6},{6,4},{1,3},{3,1},{5,7},{7,5},{8,10},{10,8},{12,... | collective-permute-start | bytes 294920 | tf_op jit(solution)/shard_map/ppermute | solution.py:414
  21.0 2.9 %collective-permute-start.6 = (bf16[32,1536]{1,0:T(8,128)(2,1)S(1)}, bf16[32,1536]{1,0:T(8,128)(2,1)S(1)}, u32[]{:S(2)}, u32[]{:S(2)}) collective-permute-start(bf16[32,1536]{1,0:T(8,128)(2,1)S(1)} %get-tuple-element.54), channel_id=1, source_target_pairs={{0,4},{2,6},{4,0},{6,2},{1,5},{3,7},{5,1},{7,3},{8,12},{10,14},{12... | collective-permute-start | bytes 294920 | tf_op jit(solution)/shard_map/ppermute | solution.py:414
  23.9 0.1 collective-permute-start.7
  24.0 1.1 collective-permute-done.5.refs_0_
  25.1 0.0 collective-permute-start.8
  25.1 6.0 %collective-permute-done.6.refs_1_ = bf16[32,1536]{1,0:T(8,128)(2,1)S(1)} collective-permute-done((bf16[32,1536]{1,0:T(8,128)(2,1)S(1)}, bf16[32,1536]{1,0:T(8,128)(2,1)S(1)}, u32[]{:S(2)}, u32[]{:S(2)}) %collective-permute-start.6) | collective-permute-done | bytes 98336 | tf_op jit(solution)/shard_map/ppermute | solution.py:414
  31.1 0.0 collective-permute-start.9
  31.1 0.0 collective-permute-done.7.refs_2_
  31.1 0.5 collective-permute-start.10
  31.6 0.0 collective-permute-done.8.refs_3_
  31.6 0.8 collective-permute-done.9.refs_4_
  32.4 0.2 collective-permute-done.10.refs_5_
  32.6 1.1 copy-done
  33.7 6.6 %attention.1 = (bf16[448,1536]{1,0:T(8,128)(2,1)S(1)}, bf16[256,384]{1,0:T(8,128)(2,1)S(1)}, bf16[256,384]{1,0:T(8,128)(2,1)S(1)}, bf16[448,384]{1,0:T(8,128)(2,1)S(1)}, bf16[448,384]{1,0:T(8,128)(2,1)S(1)}) custom-call(s32[5]{0:T(128)S(1)} %stack.23.scalars, s32[16]{0:T(128)S(1)} %copy-done.7, bf16[32,1536]{1,0:T(8,128)(2,1)S(1)} %collective-permute-done.5.refs_0_, ...), custom_call_target="tpu_custom_call" | custom-call | flops 1 | bytes 1 | tf_op jit(solution)/shard_map/attention/pallas_call | solution.py:417
  40.3 2.0 %grad_query_key.1 = (bf16[2,384,384]{2,1,0:T(8,128)(2,1)S(1)}, bf16[2,384,384]{2,1,0:T(8,128)(2,1)S(1)}, f32[2,384,384]{2,1,0:T(8,128)S(1)}, f32[2,384,384]{2,1,0:T(8,128)S(1)}) custom-call(s32[5]{0:T(128)S(1)} %stack.23.scalars, bf16[256,1536]{1,0:T(8,128)(2,1)S(1)} %copy-done, bf16[256,384]{1,0:T(8,128)(2,1)S(1)} %get-tuple-element.60.dquery, ...), custom_call_target="tpu_custom_call" | custom-call | flops 1 | bytes 1 | tf_op jit(solution)/shard_map/grad_query_key/pallas_call | solution.py:440
  42.3 1.6 %collective-permute-start.12 = (bf16[2,384,384]{2,1,0:T(8,128)(2,1)S(1)}, bf16[2,384,384]{2,1,0:T(8,128)(2,1)S(1)}, u32[]{:S(2)}, u32[]{:S(2)}) collective-permute-start(bf16[2,384,384]{2,1,0:T(8,128)(2,1)S(1)} %get-tuple-element.66), channel_id=1, source_target_pairs={{0,16},{8,24},{16,0},{24,8},{1,17},{9,25},{17,1},{25,9},{2,18},{10... | collective-permute-start | bytes 1769480 | tf_op jit(solution)/shard_map/ppermute | solution.py:460
  43.9 1.5 %collective-permute-start.11 = (bf16[2,384,384]{2,1,0:T(8,128)(2,1)S(1)}, bf16[2,384,384]{2,1,0:T(8,128)(2,1)S(1)}, u32[]{:S(2)}, u32[]{:S(2)}) collective-permute-start(bf16[2,384,384]{2,1,0:T(8,128)(2,1)S(1)} %get-tuple-element.64), channel_id=1, source_target_pairs={{0,8},{8,0},{16,24},{24,16},{1,9},{9,1},{17,25},{25,17},{2,10},{10... | collective-permute-start | bytes 1769480 | tf_op jit(solution)/shard_map/ppermute | solution.py:460
  45.3 12.6 %collective-permute-done.12.y_got = bf16[2,384,384]{2,1,0:T(8,128)(2,1)S(1)} collective-permute-done((bf16[2,384,384]{2,1,0:T(8,128)(2,1)S(1)}, bf16[2,384,384]{2,1,0:T(8,128)(2,1)S(1)}, u32[]{:S(2)}, u32[]{:S(2)}) %collective-permute-start.12) | collective-permute-done | bytes 589856 | tf_op jit(solution)/shard_map/ppermute | solution.py:460
  57.9 1.2 collective-permute-done.11.x_got
  59.2 0.2 first_sum_query_key.1
  59.4 0.6 collective-permute-start.13
  60.0 1.5 %collective-permute-start.14 = (bf16[384,384]{1,0:T(8,128)(2,1)S(1)}, bf16[384,384]{1,0:T(8,128)(2,1)S(1)}, u32[]{:S(2)}, u32[]{:S(2)}) collective-permute-start(bf16[384,384]{1,0:T(8,128)(2,1)S(1)} %get-tuple-element.70), channel_id=1, source_target_pairs={{0,8},{8,0},{16,24},{24,16},{1,9},{9,1},{17,25},{25,17},{2,10},{10... | collective-permute-start | bytes 884744 | tf_op jit(solution)/shard_map/ppermute | solution.py:468
  61.5 0.0 collective-permute-start.15
  61.5 6.1 %collective-permute-done.13.q_got = bf16[384,384]{1,0:T(8,128)(2,1)S(1)} collective-permute-done((bf16[384,384]{1,0:T(8,128)(2,1)S(1)}, bf16[384,384]{1,0:T(8,128)(2,1)S(1)}, u32[]{:S(2)}, u32[]{:S(2)}) %collective-permute-start.13) | collective-permute-done | bytes 294944 | tf_op jit(solution)/shard_map/ppermute | solution.py:468
  67.6 0.3 collective-permute-done.14.k_got
  67.9 0.9 second_sum_query_key.1
  68.9 3.7 %all-to-all-start = ((bf16[8,48,768]{2,1,0:T(8,128)(2,1)}), bf16[8,48,768]{2,1,0:T(8,128)(2,1)S(1)}, u32[]{:S(2)}, u32[]{:S(2)}) async-start(bf16[8,48,768]{2,1,0:T(8,128)(2,1)} %bitcast.7), calls=%async_computation | async-start | bytes 1179648 | tf_op jit(solution)/shard_map/all_to_all | solution.py:471
  72.6 0.0 collective-permute-done.15.theirs
  72.6 0.0 copy-done.2
  72.6 1.9 %grad_value_out.1 = (bf16[2,384,384]{2,1,0:T(8,128)(2,1)S(1)}, bf16[2,192,768]{2,1,0:T(8,128)(2,1)S(1)}, f32[2,384,384]{2,1,0:T(8,128)S(1)}, f32[2,192,768]{2,1,0:T(8,128)S(1)}) custom-call(s32[5]{0:T(128)S(1)} %stack.23.scalars, bf16[448,1536]{1,0:T(8,128)(2,1)S(1)} %get-tuple-element.61.normed_all, bf16[448,384]{1,0:T(8,128)(2,1)S(1)} %get-tuple-element.74.dvalue, ...), custom_call_target="tpu_custom_call" | custom-call | flops 1 | bytes 1 | tf_op jit(solution)/shard_map/grad_value_out/pallas_call | solution.py:440
  74.5 1.6 %collective-permute-start.16 = (bf16[2,384,384]{2,1,0:T(8,128)(2,1)S(1)}, bf16[2,384,384]{2,1,0:T(8,128)(2,1)S(1)}, u32[]{:S(2)}, u32[]{:S(2)}) collective-permute-start(bf16[2,384,384]{2,1,0:T(8,128)(2,1)S(1)} %get-tuple-element.79), channel_id=1, source_target_pairs={{0,8},{8,0},{16,24},{24,16},{1,9},{9,1},{17,25},{25,17},{2,10},{10... | collective-permute-start | bytes 1769480 | tf_op jit(solution)/shard_map/ppermute | solution.py:460
  76.1 1.4 %collective-permute-start.17 = (bf16[2,192,768]{2,1,0:T(8,128)(2,1)S(1)}, bf16[2,192,768]{2,1,0:T(8,128)(2,1)S(1)}, u32[]{:S(2)}, u32[]{:S(2)}) collective-permute-start(bf16[2,192,768]{2,1,0:T(8,128)(2,1)S(1)} %get-tuple-element.81), channel_id=1, source_target_pairs={{0,16},{8,24},{16,0},{24,8},{1,17},{9,25},{17,1},{25,9},{2,18},{10... | collective-permute-start | bytes 1769480 | tf_op jit(solution)/shard_map/ppermute | solution.py:460
  77.5 12.8 %collective-permute-done.16.x_got = bf16[2,384,384]{2,1,0:T(8,128)(2,1)S(1)} collective-permute-done((bf16[2,384,384]{2,1,0:T(8,128)(2,1)S(1)}, bf16[2,384,384]{2,1,0:T(8,128)(2,1)S(1)}, u32[]{:S(2)}, u32[]{:S(2)}) %collective-permute-start.16) | collective-permute-done | bytes 589856 | tf_op jit(solution)/shard_map/ppermute | solution.py:460
  90.3 1.2 collective-permute-done.17.y_got
  91.5 0.2 first_sum_value_out.1
  91.7 1.5 %collective-permute-start.18 = (bf16[384,384]{1,0:T(8,128)(2,1)S(1)}, bf16[384,384]{1,0:T(8,128)(2,1)S(1)}, u32[]{:S(2)}, u32[]{:S(2)}) collective-permute-start(bf16[384,384]{1,0:T(8,128)(2,1)S(1)} %get-tuple-element.83), channel_id=1, source_target_pairs={{0,16},{8,24},{16,0},{24,8},{1,17},{9,25},{17,1},{25,9},{2,18},{10... | collective-permute-start | bytes 884744 | tf_op jit(solution)/shard_map/ppermute | solution.py:468
  93.2 0.5 collective-permute-start.19
  93.7 6.4 %collective-permute-done.18.v_got = bf16[384,384]{1,0:T(8,128)(2,1)S(1)} collective-permute-done((bf16[384,384]{1,0:T(8,128)(2,1)S(1)}, bf16[384,384]{1,0:T(8,128)(2,1)S(1)}, u32[]{:S(2)}, u32[]{:S(2)}) %collective-permute-start.18) | collective-permute-done | bytes 294944 | tf_op jit(solution)/shard_map/ppermute | solution.py:468
  100.1 1.1 collective-permute-done.19.o_got
  101.2 0.9 second_sum_value_out.1
  102.1 0.0 all-to-all-done.packed
  102.1 4.4 %all-to-all-start.1 = ((bf16[8,24,1536]{2,1,0:T(8,128)(2,1)}), bf16[8,24,1536]{2,1,0:T(8,128)(2,1)S(1)}, u32[]{:S(2)}, u32[]{:S(2)}) async-start(bf16[8,24,1536]{2,1,0:T(8,128)(2,1)} %second_sum_value_out.1), calls=%async_computation.1 | async-start | bytes 1179648 | tf_op jit(solution)/shard_map/all_to_all | solution.py:471
  106.5 0.8 last_sum_query_key.1
  107.3 16.0 %all-to-all-done.1.packed = bf16[8,24,1536]{2,1,0:T(8,128)(2,1)S(1)} async-done(((bf16[8,24,1536]{2,1,0:T(8,128)(2,1)}), bf16[8,24,1536]{2,1,0:T(8,128)(2,1)S(1)}, u32[]{:S(2)}, u32[]{:S(2)}) %all-to-all-start.1) | async-done | bytes 589856 | tf_op jit(solution)/shard_map/all_to_all | solution.py:471
  123.3 0.8 last_sum_value_out.1
  (10 shorter events, 0.0 us)
Async XLA Ops:
  0.6 9.0 %collective-permute-start = (bf16[4,32,1536]{2,1,0:T(8,128)(2,1)}, bf16[4,32,1536]{2,1,0:T(8,128)(2,1)S(1)}, u32[]{:S(2)}, u32[]{:S(2)}) collective-permute-start(bf16[4,32,1536]{2,1,0:T(8,128)(2,1)} %bitcast.8), channel_id=1, source_target_pairs={{0,1},{1,0},{2,3},{3,2},{4,5},{5,4},{6,7},{7,6},{8,9},{9,8},{10,11... | collective-permute-start | bytes 1179656 | tf_op jit(solution)/shard_map/ppermute | solution.py:376
  1.1 8.5 %collective-permute-start.1 = (bf16[4,32,1536]{2,1,0:T(8,128)(2,1)}, bf16[4,32,1536]{2,1,0:T(8,128)(2,1)S(1)}, u32[]{:S(2)}, u32[]{:S(2)}) collective-permute-start(bf16[4,32,1536]{2,1,0:T(8,128)(2,1)} %bitcast.11), channel_id=1, source_target_pairs={{0,1},{1,0},{2,3},{3,2},{4,5},{5,4},{6,7},{7,6},{8,9},{9,8},{10,11... | collective-permute-start | bytes 1179656 | tf_op jit(solution)/shard_map/ppermute | solution.py:377
  3.9 15.1 %collective-permute-start.4 = (s32[4]{0:T(128)}, s32[4]{0:T(128)S(1)}, u32[]{:S(2)}, u32[]{:S(2)}) collective-permute-start(s32[4]{0:T(128)} %get-tuple-element.47), channel_id=1, source_target_pairs={{0,6},{2,4},{4,2},{6,0},{1,7},{3,5},{5,3},{7,1},{8,14},{10,12},{12... | collective-permute-start | bytes 56 | tf_op jit(solution)/shard_map/ppermute | solution.py:372
  8.9 10.0 %collective-permute-start.3 = (s32[4]{0:T(128)}, s32[4]{0:T(128)S(1)}, u32[]{:S(2)}, u32[]{:S(2)}) collective-permute-start(s32[4]{0:T(128)} %get-tuple-element.47), channel_id=1, source_target_pairs={{0,4},{2,6},{4,0},{6,2},{1,5},{3,7},{5,1},{7,3},{8,12},{10,14},{12... | collective-permute-start | bytes 56 | tf_op jit(solution)/shard_map/ppermute | solution.py:372
  9.0 10.0 %collective-permute-start.2 = (s32[4]{0:T(128)}, s32[4]{0:T(128)S(1)}, u32[]{:S(2)}, u32[]{:S(2)}) collective-permute-start(s32[4]{0:T(128)} %get-tuple-element.47), channel_id=1, source_target_pairs={{0,2},{2,0},{4,6},{6,4},{1,3},{3,1},{5,7},{7,5},{8,10},{10,8},{12,... | collective-permute-start | bytes 56 | tf_op jit(solution)/shard_map/ppermute | solution.py:372
  9.6 23.0 %copy-start.7 = (s32[16]{0:T(128)S(1)}, s32[16]{0:T(128)}, u32[]{:S(2)}) copy-start(s32[16]{0:T(128)} %get-tuple-element.49.alive) | copy-start | bytes 196
  9.7 1.0 copy-start.1
  10.7 1.0 copy-start.3
  11.7 0.8 copy-start.4
  12.5 0.7 copy-start.5
  13.2 19.4 %copy-start.6 = (f32[1536]{0:T(1024)S(1)}, f32[1536]{0:T(1024)}, u32[]{:S(2)}) copy-start(f32[1536]{0:T(1024)} %refs_11_.1) | copy-start | bytes 18436
  19.6 5.6 %collective-permute-start.5 = (bf16[32,1536]{1,0:T(8,128)(2,1)S(1)}, bf16[32,1536]{1,0:T(8,128)(2,1)S(1)}, u32[]{:S(2)}, u32[]{:S(2)}) collective-permute-start(bf16[32,1536]{1,0:T(8,128)(2,1)S(1)} %get-tuple-element.53), channel_id=1, source_target_pairs={{0,2},{2,0},{4,6},{6,4},{1,3},{3,1},{5,7},{7,5},{8,10},{10,8},{12,... | collective-permute-start | bytes 294920 | tf_op jit(solution)/shard_map/ppermute | solution.py:414
  21.0 10.1 %collective-permute-start.6 = (bf16[32,1536]{1,0:T(8,128)(2,1)S(1)}, bf16[32,1536]{1,0:T(8,128)(2,1)S(1)}, u32[]{:S(2)}, u32[]{:S(2)}) collective-permute-start(bf16[32,1536]{1,0:T(8,128)(2,1)S(1)} %get-tuple-element.54), channel_id=1, source_target_pairs={{0,4},{2,6},{4,0},{6,2},{1,5},{3,7},{5,1},{7,3},{8,12},{10,14},{12... | collective-permute-start | bytes 294920 | tf_op jit(solution)/shard_map/ppermute | solution.py:414
  23.9 7.2 %collective-permute-start.7 = (bf16[32,1536]{1,0:T(8,128)(2,1)S(1)}, bf16[32,1536]{1,0:T(8,128)(2,1)S(1)}, u32[]{:S(2)}, u32[]{:S(2)}) collective-permute-start(bf16[32,1536]{1,0:T(8,128)(2,1)S(1)} %get-tuple-element.55), channel_id=1, source_target_pairs={{0,6},{2,4},{4,2},{6,0},{1,7},{3,5},{5,3},{7,1},{8,14},{10,12},{12... | collective-permute-start | bytes 294920 | tf_op jit(solution)/shard_map/ppermute | solution.py:414
  25.1 6.5 %collective-permute-start.8 = (bf16[32,1536]{1,0:T(8,128)(2,1)S(1)}, bf16[32,1536]{1,0:T(8,128)(2,1)S(1)}, u32[]{:S(2)}, u32[]{:S(2)}) collective-permute-start(bf16[32,1536]{1,0:T(8,128)(2,1)S(1)} %collective-permute-done.5.refs_0_), channel_id=1, source_target_pairs={{0,1},{1,0},{2,3},{3,2},{4,5},{5,4},{6,7},{7,6},{8,9},{9,8},{10,11... | collective-permute-start | bytes 294920 | tf_op jit(solution)/shard_map/ppermute | solution.py:415
  31.1 1.3 %collective-permute-start.9 = (bf16[32,1536]{1,0:T(8,128)(2,1)S(1)}, bf16[32,1536]{1,0:T(8,128)(2,1)S(1)}, u32[]{:S(2)}, u32[]{:S(2)}) collective-permute-start(bf16[32,1536]{1,0:T(8,128)(2,1)S(1)} %collective-permute-done.6.refs_1_), channel_id=1, source_target_pairs={{0,1},{1,0},{2,3},{3,2},{4,5},{5,4},{6,7},{7,6},{8,9},{9,8},{10,11... | collective-permute-start | bytes 294920 | tf_op jit(solution)/shard_map/ppermute | solution.py:415
  31.1 1.5 %collective-permute-start.10 = (bf16[32,1536]{1,0:T(8,128)(2,1)S(1)}, bf16[32,1536]{1,0:T(8,128)(2,1)S(1)}, u32[]{:S(2)}, u32[]{:S(2)}) collective-permute-start(bf16[32,1536]{1,0:T(8,128)(2,1)S(1)} %collective-permute-done.7.refs_2_), channel_id=1, source_target_pairs={{0,1},{1,0},{2,3},{3,2},{4,5},{5,4},{6,7},{7,6},{8,9},{9,8},{10,11... | collective-permute-start | bytes 294920 | tf_op jit(solution)/shard_map/ppermute | solution.py:415
  32.6 1.1 copy-start
  42.3 15.7 %collective-permute-start.12 = (bf16[2,384,384]{2,1,0:T(8,128)(2,1)S(1)}, bf16[2,384,384]{2,1,0:T(8,128)(2,1)S(1)}, u32[]{:S(2)}, u32[]{:S(2)}) collective-permute-start(bf16[2,384,384]{2,1,0:T(8,128)(2,1)S(1)} %get-tuple-element.66), channel_id=1, source_target_pairs={{0,16},{8,24},{16,0},{24,8},{1,17},{9,25},{17,1},{25,9},{2,18},{10... | collective-permute-start | bytes 1769480 | tf_op jit(solution)/shard_map/ppermute | solution.py:460
  43.9 15.3 %collective-permute-start.11 = (bf16[2,384,384]{2,1,0:T(8,128)(2,1)S(1)}, bf16[2,384,384]{2,1,0:T(8,128)(2,1)S(1)}, u32[]{:S(2)}, u32[]{:S(2)}) collective-permute-start(bf16[2,384,384]{2,1,0:T(8,128)(2,1)S(1)} %get-tuple-element.64), channel_id=1, source_target_pairs={{0,8},{8,0},{16,24},{24,16},{1,9},{9,1},{17,25},{25,17},{2,10},{10... | collective-permute-start | bytes 1769480 | tf_op jit(solution)/shard_map/ppermute | solution.py:460
  59.4 8.2 %collective-permute-start.13 = (bf16[384,384]{1,0:T(8,128)(2,1)S(1)}, bf16[384,384]{1,0:T(8,128)(2,1)S(1)}, u32[]{:S(2)}, u32[]{:S(2)}) collective-permute-start(bf16[384,384]{1,0:T(8,128)(2,1)S(1)} %get-tuple-element.68), channel_id=1, source_target_pairs={{0,16},{8,24},{16,0},{24,8},{1,17},{9,25},{17,1},{25,9},{2,18},{10... | collective-permute-start | bytes 884744 | tf_op jit(solution)/shard_map/ppermute | solution.py:468
  60.0 8.0 %collective-permute-start.14 = (bf16[384,384]{1,0:T(8,128)(2,1)S(1)}, bf16[384,384]{1,0:T(8,128)(2,1)S(1)}, u32[]{:S(2)}, u32[]{:S(2)}) collective-permute-start(bf16[384,384]{1,0:T(8,128)(2,1)S(1)} %get-tuple-element.70), channel_id=1, source_target_pairs={{0,8},{8,0},{16,24},{24,16},{1,9},{9,1},{17,25},{25,17},{2,10},{10... | collective-permute-start | bytes 884744 | tf_op jit(solution)/shard_map/ppermute | solution.py:468
  61.5 11.1 %collective-permute-start.15 = (bf16[256,384]{1,0:T(8,128)(2,1)S(1)}, bf16[256,384]{1,0:T(8,128)(2,1)S(1)}, u32[]{:S(2)}, u32[]{:S(2)}) collective-permute-start(bf16[256,384]{1,0:T(8,128)(2,1)S(1)} %get-tuple-element.75.mine), channel_id=1, source_target_pairs={{0,1},{1,0},{2,3},{3,2},{4,5},{5,4},{6,7},{7,6},{8,9},{9,8},{10,11... | collective-permute-start | bytes 589832 | tf_op jit(solution)/shard_map/ppermute | solution.py:473
  67.9 4.7 %copy-start.2 = (bf16[256,1536]{1,0:T(8,128)(2,1)S(1)}, bf16[256,1536]{1,0:T(8,128)(2,1)}, u32[]{:S(2)}) copy-start(bf16[256,1536]{1,0:T(8,128)(2,1)} %get-tuple-element.76.upstream) | copy-start | bytes 2359300
  68.9 33.3 %all-to-all-start = ((bf16[8,48,768]{2,1,0:T(8,128)(2,1)}), bf16[8,48,768]{2,1,0:T(8,128)(2,1)S(1)}, u32[]{:S(2)}, u32[]{:S(2)}) async-start(bf16[8,48,768]{2,1,0:T(8,128)(2,1)} %bitcast.7), calls=%async_computation | async-start | bytes 1179648 | tf_op jit(solution)/shard_map/all_to_all | solution.py:471
  74.5 15.8 %collective-permute-start.16 = (bf16[2,384,384]{2,1,0:T(8,128)(2,1)S(1)}, bf16[2,384,384]{2,1,0:T(8,128)(2,1)S(1)}, u32[]{:S(2)}, u32[]{:S(2)}) collective-permute-start(bf16[2,384,384]{2,1,0:T(8,128)(2,1)S(1)} %get-tuple-element.79), channel_id=1, source_target_pairs={{0,8},{8,0},{16,24},{24,16},{1,9},{9,1},{17,25},{25,17},{2,10},{10... | collective-permute-start | bytes 1769480 | tf_op jit(solution)/shard_map/ppermute | solution.py:460
  76.1 15.4 %collective-permute-start.17 = (bf16[2,192,768]{2,1,0:T(8,128)(2,1)S(1)}, bf16[2,192,768]{2,1,0:T(8,128)(2,1)S(1)}, u32[]{:S(2)}, u32[]{:S(2)}) collective-permute-start(bf16[2,192,768]{2,1,0:T(8,128)(2,1)S(1)} %get-tuple-element.81), channel_id=1, source_target_pairs={{0,16},{8,24},{16,0},{24,8},{1,17},{9,25},{17,1},{25,9},{2,18},{10... | collective-permute-start | bytes 1769480 | tf_op jit(solution)/shard_map/ppermute | solution.py:460
  91.7 8.4 %collective-permute-start.18 = (bf16[384,384]{1,0:T(8,128)(2,1)S(1)}, bf16[384,384]{1,0:T(8,128)(2,1)S(1)}, u32[]{:S(2)}, u32[]{:S(2)}) collective-permute-start(bf16[384,384]{1,0:T(8,128)(2,1)S(1)} %get-tuple-element.83), channel_id=1, source_target_pairs={{0,16},{8,24},{16,0},{24,8},{1,17},{9,25},{17,1},{25,9},{2,18},{10... | collective-permute-start | bytes 884744 | tf_op jit(solution)/shard_map/ppermute | solution.py:468
  93.2 8.0 %collective-permute-start.19 = (bf16[192,768]{1,0:T(8,128)(2,1)S(1)}, bf16[192,768]{1,0:T(8,128)(2,1)S(1)}, u32[]{:S(2)}, u32[]{:S(2)}) collective-permute-start(bf16[192,768]{1,0:T(8,128)(2,1)S(1)} %get-tuple-element.85), channel_id=1, source_target_pairs={{0,8},{8,0},{16,24},{24,16},{1,9},{9,1},{17,25},{25,17},{2,10},{10... | collective-permute-start | bytes 884744 | tf_op jit(solution)/shard_map/ppermute | solution.py:468
  102.1 21.1 %all-to-all-start.1 = ((bf16[8,24,1536]{2,1,0:T(8,128)(2,1)}), bf16[8,24,1536]{2,1,0:T(8,128)(2,1)S(1)}, u32[]{:S(2)}, u32[]{:S(2)}) async-start(bf16[8,24,1536]{2,1,0:T(8,128)(2,1)} %second_sum_value_out.1), calls=%async_computation.1 | async-start | bytes 1179648 | tf_op jit(solution)/shard_map/all_to_all | solution.py:471

commit v6 on v5

--- a/solution.py
+++ b/solution.py
@@ -12,6 +12,7 @@
 MASKED = -1e30
 MIB = 1024 * 1024
 LITTLE = pl.CostEstimate(flops=1, bytes_accessed=1, transcendentals=0)
+MUCH = pl.CostEstimate(flops=40_000_000_000, bytes_accessed=1, transcendentals=0)
 
 VMEM = pl.BlockSpec(memory_space=pltpu.VMEM)
 HBM = pl.BlockSpec(memory_space=pltpu.HBM)
@@ -136,8 +137,8 @@
 
 def attention_kernel(views, groups, scalars, alive, *refs):
     got_own, got_other, refs = refs[: groups - 1], refs[groups - 1 : 2 * groups - 2], refs[2 * groups - 2 :]
-    normed, queries, keys, values, out_grad, gain, w_key, w_value, *refs = refs
-    normed_all, mixed, dquery, dkey, dvalue, w_k, w_v, arrived = refs
+    queries, keys, values, out_grad, gain, w_key, w_value, *refs = refs
+    normed_far, mixed, dquery, dkey, dvalue, w_k, w_v, arrived = refs
     copies = [
         weight_copy(scalars, w_key, w_k, arrived, 0, 1),
         weight_copy(scalars, w_value, w_v, arrived, 1, 1),
@@ -149,17 +150,16 @@
     view_tokens = tokens // views
     scale = HEAD_DIM ** (-0.5)
     here = scalars[1]
-    scale_row = gain[...].reshape(1, normed.shape[1])
-    normed_all[:tokens, :] = normed[...]
+    scale_row = gain[...].reshape(1, normed_far.shape[1])
     pair = 2 * HEAD_DIM
     span = 2 * view_tokens
     column_view = lax.broadcasted_iota(jnp.int32, (1, views * span), 1) // span
     slot_alive = []
     for j in range(groups - 1):
         group = lax.bitwise_xor(here, jnp.int32(j + 1))
-        start = tokens + 2 * j * strip
-        normed_all[start : start + strip, :] = normalized(got_own[j][...], scale_row)
-        normed_all[start + strip : start + 2 * strip, :] = normalized(got_other[j][...], scale_row)
+        start = 2 * j * strip
+        normed_far[start : start + strip, :] = normalized(got_own[j][...], scale_row)
+        normed_far[start + strip : start + 2 * strip, :] = normalized(got_other[j][...], scale_row)
         taken = jnp.zeros((1, views * span), jnp.int32)
         for u in range(views):
             taken = jnp.where(column_view == u, alive[group * views + u], taken)
@@ -209,7 +209,7 @@
         q, g = stacked(queries[:, lanes]), stacked(out_grad[:, lanes])
         k_own, v_own = keys[:, lanes], values[:, lanes]
         own.append((q, g, k_own, v_own, own_nt(k_own, q) * scale, own_nt(v_own, g)))
-    fetched = normed_all[tokens:, :]
+    fetched = normed_far[...]
     for copy in copies:
         copy.wait()
     fetched_keys = dot_nn(fetched, w_k[...]).astype(jnp.bfloat16)
@@ -249,7 +249,7 @@
         dkey[tokens:, lanes] = dot_nn(ds_far, q).astype(jnp.bfloat16)
 
 
-def by_quarters(scalars, left, right, send, keep, x_first):
+def by_quarters(scalars, lefts, right, send, keep, x_first):
     size = send.shape[1]
     x, y = scalars[3], scalars[4]
     for target, first in ((send, 1), (keep, 0)):
@@ -257,18 +257,22 @@
             dx, dy = (first, second) if x_first else (second, first)
             block = 2 * lax.bitwise_xor(y, jnp.int32(dy)) + lax.bitwise_xor(x, jnp.int32(dx))
             columns = pl.ds(pl.multiple_of(block * size, size), size)
-            target[second] = dot_tn(left[:, columns], right[...]).astype(target.dtype)
-
-
-def query_key_kernel(scalars, normed, dquery, normed_all, dkey, q_send, k_send, q_keep, k_keep):
-    by_quarters(scalars, normed, dquery, q_send, q_keep, True)
-    by_quarters(scalars, normed_all, dkey, k_send, k_keep, False)
+            total, start = 0.0, 0
+            for left in lefts:
+                total = total + dot_tn(left[:, columns], right[start : start + left.shape[0], :])
+                start += left.shape[0]
+            target[second] = total.astype(target.dtype)
+
+
+def query_key_kernel(scalars, normed, normed_far, dquery, dkey, q_send, k_send, q_keep, k_keep):
+    by_quarters(scalars, (normed,), dquery, q_send, q_keep, True)
+    by_quarters(scalars, (normed, normed_far), dkey, k_send, k_keep, False)
 
 
 def value_out_kernel(
-    scalars, normed_all, dvalue, mine, theirs, upstream, v_send, o_send, v_keep, o_keep
+    scalars, normed, normed_far, dvalue, mine, theirs, upstream, v_send, o_send, v_keep, o_keep
 ):
-    by_quarters(scalars, normed_all, dvalue, v_send, v_keep, True)
+    by_quarters(scalars, (normed, normed_far), dvalue, v_send, v_keep, True)
     row, x, y = scalars[0], scalars[3], scalars[4]
     size, width = o_send.shape[1:]
     right = upstream[:, pl.ds(pl.multiple_of(row * width, width), width)]
@@ -376,6 +380,16 @@
     lat_other = lax.ppermute(lat, "row", swap)
     cot_other = lax.ppermute(cot, "row", swap)
 
+    outgoing = pl.pallas_call(
+        functools.partial(pick_kernel, groups),
+        in_specs=[SMEM] * groups + [VMEM],
+        out_specs=[VMEM] * (groups - 1),
+        out_shape=[shape((strip, width), bf16)] * (groups - 1),
+        compiler_params=params(8),
+        cost_estimate=LITTLE,
+        name="pick",
+    )(scalars, *granted, lat)
+    got_own = [lax.ppermute(part_out, "view", pairs) for part_out, pairs in zip(outgoing, between)]
     normed, queries, keys, values, out_grad, upstream = pl.pallas_call(
         project_kernel,
         in_specs=[SMEM] + [HBM] * 4 + [VMEM] * 2 + [HBM] * 4,
@@ -401,25 +415,15 @@
         name="project",
     )(scalars, lat, lat_other, cot, cot_other, norm_gain, kernel, w_query, w_key, w_value, w_out)
 
-    normed, granted = lax.optimization_barrier((normed, granted))
-    outgoing = pl.pallas_call(
-        functools.partial(pick_kernel, groups),
-        in_specs=[SMEM] * groups + [VMEM],
-        out_specs=[VMEM] * (groups - 1),
-        out_shape=[shape((strip, width), bf16)] * (groups - 1),
-        compiler_params=params(8),
-        cost_estimate=LITTLE,
-        name="pick",
-    )(scalars, *granted, lat)
-    got_own = [lax.ppermute(part_out, "view", pairs) for part_out, pairs in zip(outgoing, between)]
+    got_own, normed = lax.optimization_barrier((got_own, normed))
     got_other = [lax.ppermute(got, "row", swap) for got in got_own]
 
-    normed_all, mixed, dquery, dkey, dvalue = pl.pallas_call(
+    normed_far, mixed, dquery, dkey, dvalue = pl.pallas_call(
         functools.partial(attention_kernel, views, groups),
-        in_specs=[SMEM] * 2 + [VMEM] * (2 * groups - 2 + 6) + [HBM] * 2,
+        in_specs=[SMEM] * 2 + [VMEM] * (2 * groups - 2 + 5) + [HBM] * 2,
         out_specs=[VMEM] * 5,
         out_shape=[
-            shape((key_tokens, width), bf16),
+            shape((key_tokens - tokens, width), bf16),
             shape((tokens, part), bf16),
             shape((tokens, part), bf16),
             shape((key_tokens, part), bf16),
@@ -434,16 +438,16 @@
         cost_estimate=LITTLE,
         name="attention",
     )(
-        scalars, alive, *got_own, *got_other, normed, queries, keys, values, out_grad, norm_gain, w_key, w_value
+        scalars, alive, *got_own, *got_other, queries, keys, values, out_grad, norm_gain, w_key, w_value
     )
-    def call(kernel_body, results, operands, name, first=VMEM, mebibytes=16):
+    def call(kernel_body, results, operands, name, first=VMEM, mebibytes=16, cost=LITTLE):
         outputs = pl.pallas_call(
             kernel_body,
             in_specs=[first] + [VMEM] * (len(operands) - 1),
             out_specs=[VMEM] * len(results),
             out_shape=results,
             compiler_params=params(mebibytes),
-            cost_estimate=LITTLE,
+            cost_estimate=cost,
             name=name,
         )(*operands)
         return list(outputs)
@@ -459,10 +463,10 @@
     def first_exchange(sends):
         return lax.ppermute(sends[0], "scene", along_x), lax.ppermute(sends[1], "scene", along_y)
 
-    def first_sum(parts, got, name):
+    def first_sum(parts, got, name, cost=LITTLE):
         blocks = [part_now.shape[1:] for part_now in parts[:2]]
         results = [shape(block, bf16) for block in blocks] + [shape(block, f32) for block in blocks]
-        return call(first_sum_kernel, results, (parts[2], got[0], parts[3], got[1]), name)
+        return call(first_sum_kernel, results, (parts[2], got[0], parts[3], got[1]), name, cost=cost)
 
     def second_exchange(sums):
         return lax.ppermute(sums[0], "scene", along_y), lax.ppermute(sums[1], "scene", along_x)
@@ -474,21 +478,21 @@
 
     results = [shape((2, *q_block), bf16)] * 2 + [shape((2, *q_block), f32)] * 2
     qk_parts = call(
-        query_key_kernel, results, (scalars, normed, dquery, normed_all, dkey), "grad_query_key", SMEM, 24
+        query_key_kernel, results, (scalars, normed, normed_far, dquery, dkey), "grad_query_key", SMEM, 24
     )
     qk_got = first_exchange(qk_parts)
     results = [shape((2, *block), kind) for kind in (bf16, f32) for block in (q_block, o_block)]
     vo_parts = call(
         value_out_kernel,
         results,
-        (scalars, normed_all, after(dvalue, qk_parts[0]), mixed, mixed_other, upstream),
+        (scalars, normed, normed_far, after(dvalue, qk_parts[0]), mixed, mixed_other, upstream),
         "grad_value_out",
         SMEM,
         24,
     )
-    vo_got = first_exchange(vo_parts)
-
+    qk_parts[2] = after(qk_parts[2], vo_parts[0])
     qk_sums = first_sum(qk_parts, qk_got, "first_sum_query_key")
+    vo_got = first_exchange([after(send, qk_sums[0]) for send in vo_parts[:2]])
     qk_got = second_exchange(qk_sums)
     packed = call(
         pack_query_key_kernel,
@@ -505,13 +509,14 @@
         "last_sum_query_key",
     )
 
-    vo_sums = first_sum(vo_parts, vo_got, "first_sum_value_out")
+    vo_sums = first_sum(vo_parts, vo_got, "first_sum_value_out", MUCH)
     vo_got = second_exchange(vo_sums)
     packed = call(
         pack_value_out_kernel,
         [shape((targets, o_rows, width), bf16)],
         (vo_sums[2], vo_got[0], vo_sums[3], vo_got[1]),
         "second_sum_value_out",
+        cost=MUCH,
     )[0]
     packed = across_views(packed)
     grad_value, grad_out = call(

time: 125 us -> 122 us (0.976)
  starting transfers between devices: 29.5 us -> 26.9 us
    ppermute x2, waiting for transfers between devices: 1.46 us -> 17.1 us  [second_exchange(): lax.ppermute(sums[1], 'scene', along_x)]
    all_to_all x2, waiting for transfers between devices: 16 us -> 29 us  [across_views(): lax.all_to_all(packed, ('view', 'row'), split_axis=0, concat_axis=0, tile...]
    ppermute x2, waiting for transfers between devices: 14.1 us -> 1.24 us  [first_exchange(): lax.ppermute(sends[0], 'scene', along_x)]
    ppermute x2, waiting for transfers between devices: 12.5 us -> 3.2 us  [second_exchange(): lax.ppermute(sums[0], 'scene', along_y)]
    ppermute x3, waiting for transfers between devices: 7.11 us -> 0.01 us  [shards(): lax.ppermute(part_out, 'view', pairs)]
    ppermute x2, waiting for transfers between devices: 13.8 us -> 9.01 us  [first_exchange(): lax.ppermute(sends[1], 'scene', along_y)]
    ppermute x3, waiting for transfers between devices: 0.01 us -> 3.93 us  [shards(): granted = [lax.ppermute(request, 'view', pairs) for pairs in between]]
    ppermute x1, waiting for transfers between devices: 0.01 us -> 1.44 us  [shards(): mixed_other = lax.ppermute(mixed, 'row', swap)]
  transfers between devices with their start and end apart: 22 -> 22, of which waited for: 13 -> 14; matrix products, arithmetic and copies ran while one was open for 1% -> 1% of each run, Pallas kernels for 9% -> 10%
where the time goes in v6:
time: 122 us; the launch traced here: 121 us
  waiting for transfers between devices  66.2 us (54%)
  starting transfers between devices  26.9 us (22%)
  Pallas kernels  21.6 us (18%)
  local copies, waits for them, and re-layouts  5.92 us (5%)
    all_to_all x2, waiting for transfers between devices, across_views(): lax.all_to_all(packed, ('view', 'row'), split_axis=0, concat_axis=0, tile...  29 us
    ppermute x2, waiting for transfers between devices, second_exchange(): lax.ppermute(sums[1], 'scene', along_x)  17.1 us
    ppermute x2, waiting for transfers between devices, first_exchange(): lax.ppermute(sends[1], 'scene', along_y)  9.01 us
    pallas_call x8, Pallas kernels, call(): pl.pallas_call(kernel_body, in_specs=[first] + [VMEM] * (len(operands) -...  7.8 us
    all_to_all x2, starting transfers between devices, across_views(): lax.all_to_all(packed, ('view', 'row'), split_axis=0, concat_axis=0, tile...  7.08 us
    pallas_call x1, Pallas kernels, shards(): pl.pallas_call(functools.partial(attention_kernel, views, groups), in_spe...  6.22 us
    unnamed x19, local copies, waits for them, and re-layouts  5.83 us
    pallas_call x1, Pallas kernels, shards(): pl.pallas_call(project_kernel, in_specs=[SMEM] + [HBM] * 4 + [VMEM] * 2 +...  5.76 us
  transfers between devices with their start and end apart: 22, of which 14 were waited for; matrix products, arithmetic and copies ran while one was open for 1% of the time, Pallas kernels for 10%

profile of v6, /device:TPU:0, one launch (start us, length us, event | category | flops | bytes accessed | tf_op | source)
XLA Modules:
  0.0 121.5 jit_solution(9723627812462140211)
XLA Ops:
  0.6 0.5 collective-permute-start.6
  1.1 0.1 collective-permute-start.7
  1.2 1.3 %copy.14.partners = s32[1,4,3]{2,1,0:T(4,128)} copy(s32[1,4,3]{1,0,2:T(1,128)} %param.17) | data formatting | bytes 96 | tf_op args[7]
  2.6 1.3 %requests.1 = (s32[4]{0:T(128)}, s32[16]{0:T(128)}) custom-call(s32[1,4,3]{2,1,0:T(4,128)} %copy.14.partners, s32[1,4]{1,0:T(1,128)} %counts.1), custom_call_target="tpu_custom_call" | custom-call | flops 1 | bytes 1 | tf_op jit(solution)/shard_map/requests/pallas_call | solution.py:367
  3.9 5.1 %collective-permute-start.2 = (s32[4]{0:T(128)}, s32[4]{0:T(128)S(1)}, u32[]{:S(2)}, u32[]{:S(2)}) collective-permute-start(s32[4]{0:T(128)} %get-tuple-element.49), channel_id=1, source_target_pairs={{0,6},{2,4},{4,2},{6,0},{1,7},{3,5},{5,3},{7,1},{8,14},{10,12},{12... | collective-permute-start | bytes 56 | tf_op jit(solution)/shard_map/ppermute | solution.py:376
  8.9 0.0 collective-permute-start.1
  9.0 0.6 collective-permute-start
  9.6 0.1 stack.23.scalars
  9.7 1.0 collective-permute-done.2.refs_2_
  10.7 2.9 %collective-permute-done.1.refs_1_ = s32[4]{0:T(128)S(1)} collective-permute-done((s32[4]{0:T(128)}, s32[4]{0:T(128)S(1)}, u32[]{:S(2)}, u32[]{:S(2)}) %collective-permute-start.1) | collective-permute-done | bytes 48 | tf_op jit(solution)/shard_map/ppermute | solution.py:376
  13.6 0.0 collective-permute-done.refs_0_
  13.6 1.0 copy-done.2
  14.6 0.6 pick.1
  15.2 0.1 collective-permute-start.3
  15.3 2.1 %collective-permute-start.4 = (bf16[32,1536]{1,0:T(8,128)(2,1)S(1)}, bf16[32,1536]{1,0:T(8,128)(2,1)S(1)}, u32[]{:S(2)}, u32[]{:S(2)}) collective-permute-start(bf16[32,1536]{1,0:T(8,128)(2,1)S(1)} %get-tuple-element.51), channel_id=1, source_target_pairs={{0,4},{2,6},{4,0},{6,2},{1,5},{3,7},{5,1},{7,3},{8,12},{10,14},{12... | collective-permute-start | bytes 294920 | tf_op jit(solution)/shard_map/ppermute | solution.py:392
  17.4 2.3 %collective-permute-start.5 = (bf16[32,1536]{1,0:T(8,128)(2,1)S(1)}, bf16[32,1536]{1,0:T(8,128)(2,1)S(1)}, u32[]{:S(2)}, u32[]{:S(2)}) collective-permute-start(bf16[32,1536]{1,0:T(8,128)(2,1)S(1)} %get-tuple-element.52), channel_id=1, source_target_pairs={{0,6},{2,4},{4,2},{6,0},{1,7},{3,5},{5,3},{7,1},{8,14},{10,12},{12... | collective-permute-start | bytes 294920 | tf_op jit(solution)/shard_map/ppermute | solution.py:392
  19.7 0.0 collective-permute-done.6.lat_other_far
  19.7 0.0 collective-permute-done.7.cot_other_far
  19.7 1.0 copy-done.3
  20.7 1.0 copy-done.5
  21.7 0.8 copy-done.6
  22.5 0.7 copy-done.7
  23.1 5.8 %project.1 = (bf16[256,1536]{1,0:T(8,128)(2,1)}, bf16[256,384]{1,0:T(8,128)(2,1)S(1)}, bf16[256,384]{1,0:T(8,128)(2,1)S(1)}, bf16[256,384]{1,0:T(8,128)(2,1)S(1)...) custom-call(s32[5]{0:T(128)S(1)} %stack.23.scalars, bf16[4,32,1536]{2,1,0:T(8,128)(2,1)S(1)} %bitcast.10, ...), custom_call_target="tpu_custom_call" | custom-call | flops 1 | bytes 1 | tf_op jit(solution)/shard_map/project/pallas_call | solution.py:393
  28.9 0.0 collective-permute-done.3.refs_0_
  28.9 0.0 collective-permute-done.4.refs_1_
  28.9 0.0 collective-permute-done.5.refs_2_
  28.9 0.1 collective-permute-start.8
  29.0 0.5 collective-permute-start.9
  29.5 0.1 collective-permute-start.10
  29.6 0.7 collective-permute-done.8.refs_3_
  30.3 0.2 collective-permute-done.9.refs_4_
  30.5 0.4 collective-permute-done.10.refs_5_
  30.8 0.0 copy-done.8
  30.8 6.2 %attention.1 = (bf16[192,1536]{1,0:T(8,128)(2,1)S(1)}, bf16[256,384]{1,0:T(8,128)(2,1)S(1)}, bf16[256,384]{1,0:T(8,128)(2,1)S(1)}, bf16[448,384]{1,0:T(8,128)(2,1)S(1)}, bf16[448,384]{1,0:T(8,128)(2,1)S(1)}) custom-call(s32[5]{0:T(128)S(1)} %stack.23.scalars, s32[16]{0:T(128)S(1)} %copy-done.8, bf16[32,1536]{1,0:T(8,128)(2,1)S(1)} %collective-permute-done.3.refs_0_, ...), custom_call_target="tpu_custom_call" | custom-call | flops 1 | bytes 1 | tf_op jit(solution)/shard_map/attention/pallas_call | solution.py:421
  37.1 2.0 %grad_query_key.1 = (bf16[2,384,384]{2,1,0:T(8,128)(2,1)S(1)}, bf16[2,384,384]{2,1,0:T(8,128)(2,1)S(1)}, f32[2,384,384]{2,1,0:T(8,128)S(1)}, f32[2,384,384]{2,1,0:T(8,128)S(1)}) custom-call(s32[5]{0:T(128)S(1)} %stack.23.scalars, bf16[256,1536]{1,0:T(8,128)(2,1)S(1)} %copy-done.1, bf16[192,1536]{1,0:T(8,128)(2,1)S(1)} %get-tuple-element.63.normed_far, ...), custom_call_target="tpu_custom_call" | custom-call | flops 1 | bytes 1 | tf_op jit(solution)/shard_map/grad_query_key/pallas_call | solution.py:444
  39.1 1.6 %collective-permute-start.13 = (bf16[2,384,384]{2,1,0:T(8,128)(2,1)S(1)}, bf16[2,384,384]{2,1,0:T(8,128)(2,1)S(1)}, u32[]{:S(2)}, u32[]{:S(2)}) collective-permute-start(bf16[2,384,384]{2,1,0:T(8,128)(2,1)S(1)} %get-tuple-element.75), channel_id=1, source_target_pairs={{0,16},{8,24},{16,0},{24,8},{1,17},{9,25},{17,1},{25,9},{2,18},{10... | collective-permute-start | bytes 1769480 | tf_op jit(solution)/shard_map/ppermute | solution.py:464
  40.6 1.5 %collective-permute-start.12 = (bf16[2,384,384]{2,1,0:T(8,128)(2,1)S(1)}, bf16[2,384,384]{2,1,0:T(8,128)(2,1)S(1)}, u32[]{:S(2)}, u32[]{:S(2)}) collective-permute-start(bf16[2,384,384]{2,1,0:T(8,128)(2,1)S(1)} %get-tuple-element.68), channel_id=1, source_target_pairs={{0,8},{8,0},{16,24},{24,16},{1,9},{9,1},{17,25},{25,17},{2,10},{10... | collective-permute-start | bytes 1769480 | tf_op jit(solution)/shard_map/ppermute | solution.py:464
  42.1 0.0 collective-permute-start.11
  42.1 1.4 %collective-permute-done.11.theirs = bf16[256,384]{1,0:T(8,128)(2,1)S(1)} collective-permute-done((bf16[256,384]{1,0:T(8,128)(2,1)S(1)}, bf16[256,384]{1,0:T(8,128)(2,1)S(1)}, u32[]{:S(2)}, u32[]{:S(2)}) %collective-permute-start.11) | collective-permute-done | bytes 196640 | tf_op jit(solution)/shard_map/ppermute | solution.py:477
  43.6 1.9 %grad_value_out.1 = (bf16[2,384,384]{2,1,0:T(8,128)(2,1)S(1)}, bf16[2,192,768]{2,1,0:T(8,128)(2,1)S(1)}, f32[2,384,384]{2,1,0:T(8,128)S(1)}, f32[2,192,768]{2,1,0:T(8,128)S(1)}) custom-call(s32[5]{0:T(128)S(1)} %stack.23.scalars, bf16[256,1536]{1,0:T(8,128)(2,1)S(1)} %copy-done.1, bf16[192,1536]{1,0:T(8,128)(2,1)S(1)} %get-tuple-element.63.normed_far, ...), custom_call_target="tpu_custom_call" | custom-call | flops 1 | bytes 1 | tf_op jit(solution)/shard_map/grad_value_out/pallas_call | solution.py:444
  45.5 9.0 %collective-permute-done.13.y_got = bf16[2,384,384]{2,1,0:T(8,128)(2,1)S(1)} collective-permute-done((bf16[2,384,384]{2,1,0:T(8,128)(2,1)S(1)}, bf16[2,384,384]{2,1,0:T(8,128)(2,1)S(1)}, u32[]{:S(2)}, u32[]{:S(2)}) %collective-permute-start.13) | collective-permute-done | bytes 589856 | tf_op jit(solution)/shard_map/ppermute | solution.py:464
  54.5 1.2 %collective-permute-done.12.x_got = bf16[2,384,384]{2,1,0:T(8,128)(2,1)S(1)} collective-permute-done((bf16[2,384,384]{2,1,0:T(8,128)(2,1)S(1)}, bf16[2,384,384]{2,1,0:T(8,128)(2,1)S(1)}, u32[]{:S(2)}, u32[]{:S(2)}) %collective-permute-start.12) | collective-permute-done | bytes 589856 | tf_op jit(solution)/shard_map/ppermute | solution.py:464
  55.7 0.2 first_sum_query_key.1
  56.0 1.6 %collective-permute-start.16 = (bf16[2,384,384]{2,1,0:T(8,128)(2,1)S(1)}, bf16[2,384,384]{2,1,0:T(8,128)(2,1)S(1)}, u32[]{:S(2)}, u32[]{:S(2)}) collective-permute-start(bf16[2,384,384]{2,1,0:T(8,128)(2,1)S(1)} %get-tuple-element.84), channel_id=1, source_target_pairs={{0,8},{8,0},{16,24},{24,16},{1,9},{9,1},{17,25},{25,17},{2,10},{10... | collective-permute-start | bytes 1769480 | tf_op jit(solution)/shard_map/ppermute | solution.py:464
  57.5 0.5 collective-permute-start.17
  58.1 0.5 collective-permute-start.15
  58.6 1.5 %collective-permute-start.14 = (bf16[384,384]{1,0:T(8,128)(2,1)S(1)}, bf16[384,384]{1,0:T(8,128)(2,1)S(1)}, u32[]{:S(2)}, u32[]{:S(2)}) collective-permute-start(bf16[384,384]{1,0:T(8,128)(2,1)S(1)} %get-tuple-element.77), channel_id=1, source_target_pairs={{0,16},{8,24},{16,0},{24,8},{1,17},{9,25},{17,1},{25,9},{2,18},{10... | collective-permute-start | bytes 884744 | tf_op jit(solution)/shard_map/ppermute | solution.py:472
  60.1 16.5 %collective-permute-done.15.k_got = bf16[384,384]{1,0:T(8,128)(2,1)S(1)} collective-permute-done((bf16[384,384]{1,0:T(8,128)(2,1)S(1)}, bf16[384,384]{1,0:T(8,128)(2,1)S(1)}, u32[]{:S(2)}, u32[]{:S(2)}) %collective-permute-start.15) | collective-permute-done | bytes 294944 | tf_op jit(solution)/shard_map/ppermute | solution.py:472
  76.6 1.2 collective-permute-done.14.q_got
  77.8 0.9 second_sum_query_key.1
  78.7 0.0 collective-permute-done.16.x_got
  78.7 0.0 collective-permute-done.17.y_got
  78.7 0.3 first_sum_value_out.1
  79.0 0.7 collective-permute-start.18
  79.7 0.6 collective-permute-start.19
  80.2 3.5 %all-to-all-start = ((bf16[8,48,768]{2,1,0:T(8,128)(2,1)}), bf16[8,48,768]{2,1,0:T(8,128)(2,1)S(1)}, u32[]{:S(2)}, u32[]{:S(2)}) async-start(bf16[8,48,768]{2,1,0:T(8,128)(2,1)} %bitcast.7), calls=%async_computation | async-start | bytes 1179648 | tf_op jit(solution)/shard_map/all_to_all | solution.py:475
  83.8 2.0 %collective-permute-done.18.v_got = bf16[384,384]{1,0:T(8,128)(2,1)S(1)} collective-permute-done((bf16[384,384]{1,0:T(8,128)(2,1)S(1)}, bf16[384,384]{1,0:T(8,128)(2,1)S(1)}, u32[]{:S(2)}, u32[]{:S(2)}) %collective-permute-start.18) | collective-permute-done | bytes 294944 | tf_op jit(solution)/shard_map/ppermute | solution.py:472
  85.8 0.6 collective-permute-done.19.o_got
  86.4 1.0 second_sum_value_out.1
  87.3 13.1 %all-to-all-done.packed = bf16[8,48,768]{2,1,0:T(8,128)(2,1)S(1)} async-done(((bf16[8,48,768]{2,1,0:T(8,128)(2,1)}), bf16[8,48,768]{2,1,0:T(8,128)(2,1)S(1)}, u32[]{:S(2)}, u32[]{:S(2)}) %all-to-all-start) | async-done | bytes 589856 | tf_op jit(solution)/shard_map/all_to_all | solution.py:475
  100.5 3.5 %all-to-all-start.1 = ((bf16[8,24,1536]{2,1,0:T(8,128)(2,1)}), bf16[8,24,1536]{2,1,0:T(8,128)(2,1)S(1)}, u32[]{:S(2)}, u32[]{:S(2)}) async-start(bf16[8,24,1536]{2,1,0:T(8,128)(2,1)} %second_sum_value_out.1), calls=%async_computation.1 | async-start | bytes 1179648 | tf_op jit(solution)/shard_map/all_to_all | solution.py:475
  104.0 0.8 last_sum_query_key.1
  104.8 15.9 %all-to-all-done.1.packed = bf16[8,24,1536]{2,1,0:T(8,128)(2,1)S(1)} async-done(((bf16[8,24,1536]{2,1,0:T(8,128)(2,1)}), bf16[8,24,1536]{2,1,0:T(8,128)(2,1)S(1)}, u32[]{:S(2)}, u32[]{:S(2)}) %all-to-all-start.1) | async-done | bytes 589856 | tf_op jit(solution)/shard_map/all_to_all | solution.py:475
  120.7 0.8 last_sum_value_out.1
  (12 shorter events, 0.0 us)
Async XLA Ops:
  0.6 19.0 %collective-permute-start.6 = (bf16[4,32,1536]{2,1,0:T(8,128)(2,1)}, bf16[4,32,1536]{2,1,0:T(8,128)(2,1)S(1)}, u32[]{:S(2)}, u32[]{:S(2)}) collective-permute-start(bf16[4,32,1536]{2,1,0:T(8,128)(2,1)} %bitcast.8), channel_id=1, source_target_pairs={{0,1},{1,0},{2,3},{3,2},{4,5},{5,4},{6,7},{7,6},{8,9},{9,8},{10,11... | collective-permute-start | bytes 1179656 | tf_op jit(solution)/shard_map/ppermute | solution.py:380
  1.1 18.5 %collective-permute-start.7 = (bf16[4,32,1536]{2,1,0:T(8,128)(2,1)}, bf16[4,32,1536]{2,1,0:T(8,128)(2,1)S(1)}, u32[]{:S(2)}, u32[]{:S(2)}) collective-permute-start(bf16[4,32,1536]{2,1,0:T(8,128)(2,1)} %bitcast.11), channel_id=1, source_target_pairs={{0,1},{1,0},{2,3},{3,2},{4,5},{5,4},{6,7},{7,6},{8,9},{9,8},{10,11... | collective-permute-start | bytes 1179656 | tf_op jit(solution)/shard_map/ppermute | solution.py:381
  3.9 6.8 %collective-permute-start.2 = (s32[4]{0:T(128)}, s32[4]{0:T(128)S(1)}, u32[]{:S(2)}, u32[]{:S(2)}) collective-permute-start(s32[4]{0:T(128)} %get-tuple-element.49), channel_id=1, source_target_pairs={{0,6},{2,4},{4,2},{6,0},{1,7},{3,5},{5,3},{7,1},{8,14},{10,12},{12... | collective-permute-start | bytes 56 | tf_op jit(solution)/shard_map/ppermute | solution.py:376
  8.9 4.7 %collective-permute-start.1 = (s32[4]{0:T(128)}, s32[4]{0:T(128)S(1)}, u32[]{:S(2)}, u32[]{:S(2)}) collective-permute-start(s32[4]{0:T(128)} %get-tuple-element.49), channel_id=1, source_target_pairs={{0,4},{2,6},{4,0},{6,2},{1,5},{3,7},{5,1},{7,3},{8,12},{10,14},{12... | collective-permute-start | bytes 56 | tf_op jit(solution)/shard_map/ppermute | solution.py:376
  9.0 4.7 %collective-permute-start = (s32[4]{0:T(128)}, s32[4]{0:T(128)S(1)}, u32[]{:S(2)}, u32[]{:S(2)}) collective-permute-start(s32[4]{0:T(128)} %get-tuple-element.49), channel_id=1, source_target_pairs={{0,2},{2,0},{4,6},{6,4},{1,3},{3,1},{5,7},{7,5},{8,10},{10,8},{12,... | collective-permute-start | bytes 56 | tf_op jit(solution)/shard_map/ppermute | solution.py:376
  13.6 1.0 copy-start.2
  15.2 13.7 %collective-permute-start.3 = (bf16[32,1536]{1,0:T(8,128)(2,1)S(1)}, bf16[32,1536]{1,0:T(8,128)(2,1)S(1)}, u32[]{:S(2)}, u32[]{:S(2)}) collective-permute-start(bf16[32,1536]{1,0:T(8,128)(2,1)S(1)} %get-tuple-element.50), channel_id=1, source_target_pairs={{0,2},{2,0},{4,6},{6,4},{1,3},{3,1},{5,7},{7,5},{8,10},{10,8},{12,... | collective-permute-start | bytes 294920 | tf_op jit(solution)/shard_map/ppermute | solution.py:392
  15.3 13.7 %collective-permute-start.4 = (bf16[32,1536]{1,0:T(8,128)(2,1)S(1)}, bf16[32,1536]{1,0:T(8,128)(2,1)S(1)}, u32[]{:S(2)}, u32[]{:S(2)}) collective-permute-start(bf16[32,1536]{1,0:T(8,128)(2,1)S(1)} %get-tuple-element.51), channel_id=1, source_target_pairs={{0,4},{2,6},{4,0},{6,2},{1,5},{3,7},{5,1},{7,3},{8,12},{10,14},{12... | collective-permute-start | bytes 294920 | tf_op jit(solution)/shard_map/ppermute | solution.py:392
  17.4 13.5 %copy-start.8 = (s32[16]{0:T(128)S(1)}, s32[16]{0:T(128)}, u32[]{:S(2)}) copy-start(s32[16]{0:T(128)} %get-tuple-element.55.alive) | copy-start | bytes 196
  17.4 13.5 %copy-start = (bf16[1536,768]{1,0:T(8,128)(2,1)S(1)}, bf16[1536,768]{1,0:T(8,128)(2,1)}, u32[]{:S(2)}) copy-start(bf16[1536,768]{1,0:T(8,128)(2,1)} %refs_11_.1) | copy-start | bytes 7077892
  17.4 11.6 %collective-permute-start.5 = (bf16[32,1536]{1,0:T(8,128)(2,1)S(1)}, bf16[32,1536]{1,0:T(8,128)(2,1)S(1)}, u32[]{:S(2)}, u32[]{:S(2)}) collective-permute-start(bf16[32,1536]{1,0:T(8,128)(2,1)S(1)} %get-tuple-element.52), channel_id=1, source_target_pairs={{0,6},{2,4},{4,2},{6,0},{1,7},{3,5},{5,3},{7,1},{8,14},{10,12},{12... | collective-permute-start | bytes 294920 | tf_op jit(solution)/shard_map/ppermute | solution.py:392
  19.7 1.0 copy-start.3
  20.7 1.0 copy-start.5
  21.7 0.8 copy-start.6
  22.5 0.7 copy-start.7
  28.9 1.4 %collective-permute-start.8 = (bf16[32,1536]{1,0:T(8,128)(2,1)S(1)}, bf16[32,1536]{1,0:T(8,128)(2,1)S(1)}, u32[]{:S(2)}, u32[]{:S(2)}) collective-permute-start(bf16[32,1536]{1,0:T(8,128)(2,1)S(1)} %collective-permute-done.3.refs_0_), channel_id=1, source_target_pairs={{0,1},{1,0},{2,3},{3,2},{4,5},{5,4},{6,7},{7,6},{8,9},{9,8},{10,11... | collective-permute-start | bytes 294920 | tf_op jit(solution)/shard_map/ppermute | solution.py:419
  29.0 1.4 %collective-permute-start.9 = (bf16[32,1536]{1,0:T(8,128)(2,1)S(1)}, bf16[32,1536]{1,0:T(8,128)(2,1)S(1)}, u32[]{:S(2)}, u32[]{:S(2)}) collective-permute-start(bf16[32,1536]{1,0:T(8,128)(2,1)S(1)} %collective-permute-done.4.refs_1_), channel_id=1, source_target_pairs={{0,1},{1,0},{2,3},{3,2},{4,5},{5,4},{6,7},{7,6},{8,9},{9,8},{10,11... | collective-permute-start | bytes 294920 | tf_op jit(solution)/shard_map/ppermute | solution.py:419
  29.5 1.3 %collective-permute-start.10 = (bf16[32,1536]{1,0:T(8,128)(2,1)S(1)}, bf16[32,1536]{1,0:T(8,128)(2,1)S(1)}, u32[]{:S(2)}, u32[]{:S(2)}) collective-permute-start(bf16[32,1536]{1,0:T(8,128)(2,1)S(1)} %collective-permute-done.5.refs_2_), channel_id=1, source_target_pairs={{0,1},{1,0},{2,3},{3,2},{4,5},{5,4},{6,7},{7,6},{8,9},{9,8},{10,11... | collective-permute-start | bytes 294920 | tf_op jit(solution)/shard_map/ppermute | solution.py:419
  30.8 6.2 %copy-start.1 = (bf16[256,1536]{1,0:T(8,128)(2,1)S(1)}, bf16[256,1536]{1,0:T(8,128)(2,1)}, u32[]{:S(2)}) copy-start(bf16[256,1536]{1,0:T(8,128)(2,1)} %get-tuple-element.54.normed) | copy-start | bytes 2359300
  37.1 6.5 %copy-start.4 = (bf16[256,1536]{1,0:T(8,128)(2,1)S(1)}, bf16[256,1536]{1,0:T(8,128)(2,1)}, u32[]{:S(2)}) copy-start(bf16[256,1536]{1,0:T(8,128)(2,1)} %get-tuple-element.71.upstream) | copy-start | bytes 2359300
  39.1 15.4 %collective-permute-start.13 = (bf16[2,384,384]{2,1,0:T(8,128)(2,1)S(1)}, bf16[2,384,384]{2,1,0:T(8,128)(2,1)S(1)}, u32[]{:S(2)}, u32[]{:S(2)}) collective-permute-start(bf16[2,384,384]{2,1,0:T(8,128)(2,1)S(1)} %get-tuple-element.75), channel_id=1, source_target_pairs={{0,16},{8,24},{16,0},{24,8},{1,17},{9,25},{17,1},{25,9},{2,18},{10... | collective-permute-start | bytes 1769480 | tf_op jit(solution)/shard_map/ppermute | solution.py:464
  40.6 15.1 %collective-permute-start.12 = (bf16[2,384,384]{2,1,0:T(8,128)(2,1)S(1)}, bf16[2,384,384]{2,1,0:T(8,128)(2,1)S(1)}, u32[]{:S(2)}, u32[]{:S(2)}) collective-permute-start(bf16[2,384,384]{2,1,0:T(8,128)(2,1)S(1)} %get-tuple-element.68), channel_id=1, source_target_pairs={{0,8},{8,0},{16,24},{24,16},{1,9},{9,1},{17,25},{25,17},{2,10},{10... | collective-permute-start | bytes 1769480 | tf_op jit(solution)/shard_map/ppermute | solution.py:464
  42.1 1.4 %collective-permute-start.11 = (bf16[256,384]{1,0:T(8,128)(2,1)S(1)}, bf16[256,384]{1,0:T(8,128)(2,1)S(1)}, u32[]{:S(2)}, u32[]{:S(2)}) collective-permute-start(bf16[256,384]{1,0:T(8,128)(2,1)S(1)} %get-tuple-element.70.mine), channel_id=1, source_target_pairs={{0,1},{1,0},{2,3},{3,2},{4,5},{5,4},{6,7},{7,6},{8,9},{9,8},{10,11... | collective-permute-start | bytes 589832 | tf_op jit(solution)/shard_map/ppermute | solution.py:477
  56.0 22.8 %collective-permute-start.16 = (bf16[2,384,384]{2,1,0:T(8,128)(2,1)S(1)}, bf16[2,384,384]{2,1,0:T(8,128)(2,1)S(1)}, u32[]{:S(2)}, u32[]{:S(2)}) collective-permute-start(bf16[2,384,384]{2,1,0:T(8,128)(2,1)S(1)} %get-tuple-element.84), channel_id=1, source_target_pairs={{0,8},{8,0},{16,24},{24,16},{1,9},{9,1},{17,25},{25,17},{2,10},{10... | collective-permute-start | bytes 1769480 | tf_op jit(solution)/shard_map/ppermute | solution.py:464
  57.5 21.2 %collective-permute-start.17 = (bf16[2,192,768]{2,1,0:T(8,128)(2,1)S(1)}, bf16[2,192,768]{2,1,0:T(8,128)(2,1)S(1)}, u32[]{:S(2)}, u32[]{:S(2)}) collective-permute-start(bf16[2,192,768]{2,1,0:T(8,128)(2,1)S(1)} %get-tuple-element.87), channel_id=1, source_target_pairs={{0,16},{8,24},{16,0},{24,8},{1,17},{9,25},{17,1},{25,9},{2,18},{10... | collective-permute-start | bytes 1769480 | tf_op jit(solution)/shard_map/ppermute | solution.py:464
  58.1 18.6 %collective-permute-start.15 = (bf16[384,384]{1,0:T(8,128)(2,1)S(1)}, bf16[384,384]{1,0:T(8,128)(2,1)S(1)}, u32[]{:S(2)}, u32[]{:S(2)}) collective-permute-start(bf16[384,384]{1,0:T(8,128)(2,1)S(1)} %get-tuple-element.79), channel_id=1, source_target_pairs={{0,8},{8,0},{16,24},{24,16},{1,9},{9,1},{17,25},{25,17},{2,10},{10... | collective-permute-start | bytes 884744 | tf_op jit(solution)/shard_map/ppermute | solution.py:472
  58.6 19.2 %collective-permute-start.14 = (bf16[384,384]{1,0:T(8,128)(2,1)S(1)}, bf16[384,384]{1,0:T(8,128)(2,1)S(1)}, u32[]{:S(2)}, u32[]{:S(2)}) collective-permute-start(bf16[384,384]{1,0:T(8,128)(2,1)S(1)} %get-tuple-element.77), channel_id=1, source_target_pairs={{0,16},{8,24},{16,0},{24,8},{1,17},{9,25},{17,1},{25,9},{2,18},{10... | collective-permute-start | bytes 884744 | tf_op jit(solution)/shard_map/ppermute | solution.py:472
  79.0 6.8 %collective-permute-start.18 = (bf16[384,384]{1,0:T(8,128)(2,1)S(1)}, bf16[384,384]{1,0:T(8,128)(2,1)S(1)}, u32[]{:S(2)}, u32[]{:S(2)}) collective-permute-start(bf16[384,384]{1,0:T(8,128)(2,1)S(1)} %get-tuple-element.89), channel_id=1, source_target_pairs={{0,16},{8,24},{16,0},{24,8},{1,17},{9,25},{17,1},{25,9},{2,18},{10... | collective-permute-start | bytes 884744 | tf_op jit(solution)/shard_map/ppermute | solution.py:472
  79.7 6.7 %collective-permute-start.19 = (bf16[192,768]{1,0:T(8,128)(2,1)S(1)}, bf16[192,768]{1,0:T(8,128)(2,1)S(1)}, u32[]{:S(2)}, u32[]{:S(2)}) collective-permute-start(bf16[192,768]{1,0:T(8,128)(2,1)S(1)} %get-tuple-element.91), channel_id=1, source_target_pairs={{0,8},{8,0},{16,24},{24,16},{1,9},{9,1},{17,25},{25,17},{2,10},{10... | collective-permute-start | bytes 884744 | tf_op jit(solution)/shard_map/ppermute | solution.py:472
  80.2 20.2 %all-to-all-start = ((bf16[8,48,768]{2,1,0:T(8,128)(2,1)}), bf16[8,48,768]{2,1,0:T(8,128)(2,1)S(1)}, u32[]{:S(2)}, u32[]{:S(2)}) async-start(bf16[8,48,768]{2,1,0:T(8,128)(2,1)} %bitcast.7), calls=%async_computation | async-start | bytes 1179648 | tf_op jit(solution)/shard_map/all_to_all | solution.py:475
  100.5 20.2 %all-to-all-start.1 = ((bf16[8,24,1536]{2,1,0:T(8,128)(2,1)}), bf16[8,24,1536]{2,1,0:T(8,128)(2,1)S(1)}, u32[]{:S(2)}, u32[]{:S(2)}) async-start(bf16[8,24,1536]{2,1,0:T(8,128)(2,1)} %second_sum_value_out.1), calls=%async_computation.1 | async-start | bytes 1179648 | tf_op jit(solution)/shard_map/all_to_all | solution.py:475

commit v7 on v6

--- a/solution.py
+++ b/solution.py
@@ -15,7 +15,6 @@
 MUCH = pl.CostEstimate(flops=40_000_000_000, bytes_accessed=1, transcendentals=0)
 
 VMEM = pl.BlockSpec(memory_space=pltpu.VMEM)
-HBM = pl.BlockSpec(memory_space=pltpu.HBM)
 SMEM = pl.BlockSpec(memory_space=pltpu.SMEM)
 
 
@@ -59,38 +58,15 @@
         out[...] = lat[request[scalars[1]]]
 
 
-def weight_copy(scalars, source, target, arrived, index, axis):
-    size = target.shape[axis]
-    half = pl.ds(pl.multiple_of(scalars[0] * size, size), size)
-    part = source.at[:, half] if axis == 1 else source.at[half, :]
-    return pltpu.make_async_copy(part, target, arrived.at[index])
+def core_half(scalars, size):
+    return pl.ds(pl.multiple_of(scalars[0] * size, size), size)
 
 
 def project_kernel(
-    scalars, lat_own_far, lat_other_far, cot_own_far, cot_other_far, gain, taps, w_query, w_key, w_value, w_out,
+    scalars, lat_own, lat_other, cot_own, cot_other, gain, taps, w_query, w_key, w_value, w_out,
     normed, queries, keys, values, out_grad, upstream,
-    lat_own, lat_other, cot_own, cot_other, w_q, w_k, w_v, w_o, arrived,
 ):
     views, strip, width = lat_own.shape
-    inputs = [
-        pltpu.make_async_copy(source, target, arrived.at[4 + i])
-        for i, (source, target) in enumerate(
-            (
-                (lat_own_far, lat_own),
-                (lat_other_far, lat_other),
-                (cot_own_far, cot_own),
-                (cot_other_far, cot_other),
-            )
-        )
-    ]
-    copies = [
-        weight_copy(scalars, w_query, w_q, arrived, 0, 1),
-        weight_copy(scalars, w_key, w_k, arrived, 1, 1),
-        weight_copy(scalars, w_value, w_v, arrived, 2, 1),
-        weight_copy(scalars, w_out, w_o, arrived, 3, 0),
-    ]
-    for copy in inputs + copies:
-        copy.start()
     scale = gain[...].reshape(1, width)
     row = scalars[0]
 
@@ -99,12 +75,9 @@
         return pl.ds(pl.multiple_of(index * strip, strip), strip)
 
     for half, source in enumerate((lat_own, lat_other)):
-        inputs[half].wait()
         for u in range(views):
             normed[strip_of(u, half), :] = normalized(source[u], scale)
     first = row == 0
-    for copy in inputs[2:]:
-        copy.wait()
     chunk = 512
     column = lax.broadcasted_iota(jnp.int32, (strip, 1), 0)
     not_first = (column > 0).astype(jnp.float32)
@@ -128,23 +101,16 @@
                     total = total + cross[half][b : b + 1] * shifted[1 - half][b]
                 upstream[strip_of(u, half), lanes] = total.astype(jnp.bfloat16)
     rows = normed[...]
-    for copy, weight, result in zip(copies, (w_q, w_k, w_v), (queries, keys, values)):
-        copy.wait()
-        result[...] = dot_nn(rows, weight[...]).astype(jnp.bfloat16)
-    copies[3].wait()
-    out_grad[...] = dot_nt(upstream[...], w_o[...]).astype(jnp.bfloat16)
+    half = core_half(scalars, queries.shape[1])
+    for weight, result in ((w_query, queries), (w_key, keys), (w_value, values)):
+        result[...] = dot_nn(rows, weight[:, half]).astype(jnp.bfloat16)
+    out_grad[...] = dot_nt(upstream[...], w_out[half, :]).astype(jnp.bfloat16)
 
 
 def attention_kernel(views, groups, scalars, alive, *refs):
     got_own, got_other, refs = refs[: groups - 1], refs[groups - 1 : 2 * groups - 2], refs[2 * groups - 2 :]
     queries, keys, values, out_grad, gain, w_key, w_value, *refs = refs
-    normed_far, mixed, dquery, dkey, dvalue, w_k, w_v, arrived = refs
-    copies = [
-        weight_copy(scalars, w_key, w_k, arrived, 0, 1),
-        weight_copy(scalars, w_value, w_v, arrived, 1, 1),
-    ]
-    for copy in copies:
-        copy.start()
+    normed_far, mixed, dquery, dkey, dvalue = refs
     strip = got_own[0].shape[0]
     tokens = queries.shape[0]
     view_tokens = tokens // views
@@ -210,10 +176,9 @@
         k_own, v_own = keys[:, lanes], values[:, lanes]
         own.append((q, g, k_own, v_own, own_nt(k_own, q) * scale, own_nt(v_own, g)))
     fetched = normed_far[...]
-    for copy in copies:
-        copy.wait()
-    fetched_keys = dot_nn(fetched, w_k[...]).astype(jnp.bfloat16)
-    fetched_values = dot_nn(fetched, w_v[...]).astype(jnp.bfloat16)
+    half = core_half(scalars, queries.shape[1])
+    fetched_keys = dot_nn(fetched, w_key[:, half]).astype(jnp.bfloat16)
+    fetched_values = dot_nn(fetched, w_value[:, half]).astype(jnp.bfloat16)
     for p, (q, g, k_own, v_own, s_own, dp_own) in enumerate(own):
         lanes = slice(p * pair, (p + 1) * pair)
         k_far, v_far = fetched_keys[:, lanes], fetched_values[:, lanes]
@@ -269,20 +234,43 @@
     by_quarters(scalars, (normed, normed_far), dkey, k_send, k_keep, False)
 
 
-def value_out_kernel(
-    scalars, normed, normed_far, dvalue, mine, theirs, upstream, v_send, o_send, v_keep, o_keep
-):
-    by_quarters(scalars, (normed, normed_far), dvalue, v_send, v_keep, True)
+def value_out_kernel(scalars, normed, normed_far, dvalue, mine, theirs, upstream, send, keep):
     row, x, y = scalars[0], scalars[3], scalars[4]
-    size, width = o_send.shape[1:]
-    right = upstream[:, pl.ds(pl.multiple_of(row * width, width), width)]
+    odd = lax.rem(scalars[1], jnp.int32(2)) == 1
+    _, _, pairs, size, width = send.shape
+    half, quarter = width // 2, width // 4
+    right = upstream[:, core_half(scalars, half)]
     from_mine, from_theirs = dot_tn(mine[...], right), dot_tn(theirs[...], right)
-    keep_mine = row == y
-    for block in range(2):
-        place = pl.ds(lax.bitwise_xor(x, jnp.int32(block)), 1)
-        rows = slice(block * size, (block + 1) * size)
-        o_send[place] = jnp.where(keep_mine, from_theirs[rows], from_mine[rows])[None].astype(o_send.dtype)
-        o_keep[place] = jnp.where(keep_mine, from_mine[rows], from_theirs[rows])[None]
+    for dy in range(2):
+        grad_o = jnp.where(row == lax.bitwise_xor(y, jnp.int32(dy)), from_mine, from_theirs)
+        low, high = grad_o[: 2 * pairs * size], grad_o[2 * pairs * size :]
+        for dx in range(2):
+            to_x = lax.bitwise_xor(x, jnp.int32(dx))
+            o_part = jnp.where(to_x == 0, low, high)
+            block = 2 * lax.bitwise_xor(y, jnp.int32(dy)) + to_x
+            columns = pl.ds(pl.multiple_of(block * quarter, quarter), quarter)
+            tokens = normed.shape[0]
+            v_part = dot_tn(normed[:, columns], dvalue[:tokens, :])
+            v_part = v_part + dot_tn(normed_far[:, columns], dvalue[tokens:, :])
+            for pair in range(pairs):
+                tiles = []
+                for view in (2 * pair, 2 * pair + 1):
+                    v_view = v_part[2 * view * size : 2 * (view + 1) * size]
+                    tiles.append((o_part[view * size : (view + 1) * size], v_view[:size], v_view[size:]))
+                for target, take_odd in ((send, jnp.logical_not(odd)), (keep, odd)):
+                    tile = [jnp.where(take_odd, second, first) for first, second in zip(*tiles)]
+                    target[dy, dx, pair] = jnp.concatenate(tile, axis=1).astype(target.dtype)
+
+
+def view_sum_kernel(keep, got, x_send, y_send, x_keep, y_keep):
+    half = keep.shape[4] // 2
+    for second in range(2):
+        for target, first in ((x_send, 1), (x_keep, 0)):
+            total = keep[second, first, :, :, half:] + got[second, first, :, :, half:].astype(jnp.float32)
+            target[second] = total.astype(target.dtype)
+        for target, first in ((y_send, 1), (y_keep, 0)):
+            total = keep[first, second, :, :, :half] + got[first, second, :, :, :half].astype(jnp.float32)
+            target[second] = total.astype(target.dtype)
 
 
 def first_sum_kernel(x_keep, x_got, y_keep, y_got, x_later, y_later, x_now, y_now):
@@ -297,19 +285,39 @@
     packed[:, size:] = (k_now[...] + k_got[...].astype(jnp.float32)).astype(jnp.bfloat16)
 
 
-def pack_value_out_kernel(v_now, v_got, o_now, o_got, packed):
-    grad_v = v_now[...] + v_got[...].astype(jnp.float32)
-    grad_o = o_now[...] + o_got[...].astype(jnp.float32)
-    targets, size, _ = packed.shape
-    for i in range(targets):
-        packed[i] = jnp.concatenate(
-            (
-                grad_o[i * size : (i + 1) * size],
-                grad_v[2 * i * size : (2 * i + 1) * size],
-                grad_v[(2 * i + 1) * size : (2 * i + 2) * size],
-            ),
-            axis=1,
-        ).astype(jnp.bfloat16)
+def tile_halves_kernel(bit, out_and_value, scalars, *refs):
+    addends, (send, keep) = refs[:-2], refs[-2:]
+    count = keep.shape[0]
+    mine = lax.rem(lax.div(scalars[1], jnp.int32(2 << bit)), jnp.int32(2))
+    for target, part in ((send, 1 - mine), (keep, mine)):
+        for i in range(count):
+            place = pl.ds(part * count + i, 1)
+            total = [now[place] + got[place].astype(jnp.float32) for now, got in zip(addends[::2], addends[1::2])]
+            total = jnp.concatenate(total, axis=2) if out_and_value else total[0]
+            target[i] = total[0].astype(target.dtype)
+
+
+def tile_cores_kernel(scalars, keep, got, send, mine):
+    total = keep[0] + got[0].astype(jnp.float32)
+    size, width = mine.shape
+    half, quarter = width // 2, width // 4
+    parts = []
+    for core in range(2):
+        value = total[:, half + core * quarter : half + (core + 1) * quarter]
+        out = total[core * size : (core + 1) * size, :half]
+        parts.append(jnp.concatenate((out, value[:size], value[size:]), axis=1))
+    send[...] = jnp.where(scalars[0] == 0, parts[1], parts[0])
+    mine[...] = jnp.where(scalars[0] == 0, parts[0], parts[1])
+
+
+def place_kernel(scalars, mine, theirs, value, out):
+    size, width = mine.shape
+    half, quarter = width // 2, width // 4
+    for source, core in ((mine, scalars[0]), (theirs, 1 - scalars[0])):
+        out[:, pl.ds(pl.multiple_of(core * half, half), half)] = source[:, :half]
+        columns = pl.ds(pl.multiple_of(core * quarter, quarter), quarter)
+        value[:size, columns] = source[:, half : half + quarter]
+        value[size:, columns] = source[:, half + quarter :]
 
 
 def summed_views(rows, packed):
@@ -326,16 +334,6 @@
         columns = slice(r * size, (r + 1) * size)
         query[:, columns] = total[:, :size]
         key[:, columns] = total[:, size:]
-
-
-def last_value_out_kernel(rows, packed, value, out):
-    _, size, width = packed.shape
-    half, quarter = width // 2, width // 4
-    for r, total in summed_views(rows, packed):
-        columns = slice(r * quarter, (r + 1) * quarter)
-        out[:, r * half : (r + 1) * half] = total[:, :half]
-        value[:size, columns] = total[:, half : half + quarter]
-        value[size:, columns] = total[:, half + quarter :]
 
 
 def params(mebibytes):
@@ -369,7 +367,8 @@
         in_specs=[SMEM, SMEM],
         out_specs=(SMEM, SMEM),
         out_shape=(shape((groups,), i32), shape((groups * views,), i32)),
-        cost_estimate=LITTLE,
+        cost_estimate=MUCH,
+        compiler_params=params(4),
         name="requests",
     )(partners, counts)
     between = [[(i, i ^ d) for i in range(groups)] for d in range(1, groups)]
@@ -386,13 +385,13 @@
         out_specs=[VMEM] * (groups - 1),
         out_shape=[shape((strip, width), bf16)] * (groups - 1),
         compiler_params=params(8),
-        cost_estimate=LITTLE,
+        cost_estimate=MUCH,
         name="pick",
     )(scalars, *granted, lat)
     got_own = [lax.ppermute(part_out, "view", pairs) for part_out, pairs in zip(outgoing, between)]
     normed, queries, keys, values, out_grad, upstream = pl.pallas_call(
         project_kernel,
-        in_specs=[SMEM] + [HBM] * 4 + [VMEM] * 2 + [HBM] * 4,
+        in_specs=[SMEM] + [VMEM] * 10,
         out_specs=[VMEM] * 6,
         out_shape=[
             shape((tokens, width), bf16),
@@ -402,15 +401,7 @@
             shape((tokens, part), bf16),
             shape((tokens, width), bf16),
         ],
-        scratch_shapes=[pltpu.VMEM((views, strip, width), bf16)] * 4
-        + [
-            pltpu.VMEM((width, part), bf16),
-            pltpu.VMEM((width, part), bf16),
-            pltpu.VMEM((width, part), bf16),
-            pltpu.VMEM((part, width), bf16),
-            pltpu.SemaphoreType.DMA((8,)),
-        ],
-        compiler_params=params(51),
+        compiler_params=params(28),
         cost_estimate=LITTLE,
         name="project",
     )(scalars, lat, lat_other, cot, cot_other, norm_gain, kernel, w_query, w_key, w_value, w_out)
@@ -420,7 +411,7 @@
 
     normed_far, mixed, dquery, dkey, dvalue = pl.pallas_call(
         functools.partial(attention_kernel, views, groups),
-        in_specs=[SMEM] * 2 + [VMEM] * (2 * groups - 2 + 5) + [HBM] * 2,
+        in_specs=[SMEM] * 2 + [VMEM] * (2 * groups - 2 + 7),
         out_specs=[VMEM] * 5,
         out_shape=[
             shape((key_tokens - tokens, width), bf16),
@@ -429,12 +420,7 @@
             shape((key_tokens, part), bf16),
             shape((key_tokens, part), bf16),
         ],
-        scratch_shapes=[
-            pltpu.VMEM((width, part), bf16),
-            pltpu.VMEM((width, part), bf16),
-            pltpu.SemaphoreType.DMA((2,)),
-        ],
-        compiler_params=params(48),
+        compiler_params=params(28 + groups),
         cost_estimate=LITTLE,
         name="attention",
     )(
@@ -456,9 +442,9 @@
         return lax.optimization_barrier((value, *earlier))[0]
 
     targets = groups * rows
-    q_size, o_size = width // 4, inner // 4
-    q_rows, o_rows = q_size // targets, o_size // targets
-    q_block, o_block = (q_size, part), (o_size, width // 2)
+    q_size = width // 4
+    q_rows, o_rows = q_size // targets, inner // (4 * targets)
+    q_block = (q_size, part)
 
     def first_exchange(sends):
         return lax.ppermute(sends[0], "scene", along_x), lax.ppermute(sends[1], "scene", along_y)
@@ -481,18 +467,19 @@
         query_key_kernel, results, (scalars, normed, normed_far, dquery, dkey), "grad_query_key", SMEM, 24
     )
     qk_got = first_exchange(qk_parts)
-    results = [shape((2, *block), kind) for kind in (bf16, f32) for block in (q_block, o_block)]
-    vo_parts = call(
+    pairs = groups // 2
+    tile = (2 * o_rows, width)
+    send, keep = call(
         value_out_kernel,
-        results,
+        [shape((2, 2, pairs, *tile), kind) for kind in (bf16, f32)],
         (scalars, normed, normed_far, after(dvalue, qk_parts[0]), mixed, mixed_other, upstream),
         "grad_value_out",
         SMEM,
         24,
     )
-    qk_parts[2] = after(qk_parts[2], vo_parts[0])
+    got = lax.ppermute(send, "view", [(i, i ^ 1) for i in range(groups)])
+    qk_parts[2] = after(qk_parts[2], send)
     qk_sums = first_sum(qk_parts, qk_got, "first_sum_query_key")
-    vo_got = first_exchange([after(send, qk_sums[0]) for send in vo_parts[:2]])
     qk_got = second_exchange(qk_sums)
     packed = call(
         pack_query_key_kernel,
@@ -500,7 +487,7 @@
         (qk_sums[2], qk_got[0], qk_sums[3], qk_got[1]),
         "second_sum_query_key",
     )[0]
-    vo_parts[2] = after(vo_parts[2], packed)
+    keep = after(keep, packed)
     packed = across_views(packed.reshape(targets, q_rows, 2 * part))
     grad_query, grad_key = call(
         functools.partial(last_query_key_kernel, rows),
@@ -509,21 +496,46 @@
         "last_sum_query_key",
     )
 
+    part_shape = (2, pairs, 2 * o_rows, width // 2)
+    vo_parts = call(
+        view_sum_kernel,
+        [shape(part_shape, bf16)] * 2 + [shape(part_shape, f32)] * 2,
+        (keep, got),
+        "view_sum_value_out",
+        cost=MUCH,
+    )
+    vo_got = first_exchange(vo_parts)
     vo_sums = first_sum(vo_parts, vo_got, "first_sum_value_out", MUCH)
-    vo_got = second_exchange(vo_sums)
-    packed = call(
-        pack_value_out_kernel,
-        [shape((targets, o_rows, width), bf16)],
-        (vo_sums[2], vo_got[0], vo_sums[3], vo_got[1]),
-        "second_sum_value_out",
+    v_got, o_got = second_exchange(vo_sums)
+    addends = (vo_sums[3], o_got, vo_sums[2], v_got)
+    bit = pairs.bit_length() - 1
+    while bit > 0:
+        bit -= 1
+        send, keep = call(
+            functools.partial(tile_halves_kernel, bit, len(addends) == 4),
+            [shape((1 << bit, *tile), kind) for kind in (bf16, f32)],
+            (scalars, *addends),
+            "view_bit_value_out",
+            SMEM,
+            cost=MUCH,
+        )
+        got = lax.ppermute(send, "view", [(i, i ^ (2 << bit)) for i in range(groups)])
+        addends = (keep, got)
+    send, mine = call(
+        tile_cores_kernel,
+        [shape((o_rows, width), f32)] * 2,
+        (scalars, *addends),
+        "last_sum_value_out",
+        SMEM,
         cost=MUCH,
-    )[0]
-    packed = across_views(packed)
+    )
+    theirs = lax.ppermute(send, "row", swap)
     grad_value, grad_out = call(
-        functools.partial(last_value_out_kernel, rows),
+        place_kernel,
         [shape((q_rows, inner), f32), shape((o_rows, width), f32)],
-        (packed,),
-        "last_sum_value_out",
+        (scalars, mine, theirs),
+        "place_value_out",
+        SMEM,
     )
     return grad_query, grad_key, grad_value, grad_out
 

time: 122 us -> 104 us (0.85)
  waiting for transfers between devices: 66.2 us -> 52.6 us
  local copies, waits for them, and re-layouts: 5.92 us -> 1.54 us
  starting transfers between devices: 26.9 us -> 29.9 us
  Pallas kernels: 21.6 us -> 19 us
    all_to_all x2 -> x1, waiting for transfers between devices: 29 us -> 14.7 us  [across_views(): lax.all_to_all(packed, ('view', 'row'), split_axis=0, concat_axis=0, tile...]
    ppermute x2, waiting for transfers between devices: 17.1 us -> 3.41 us  [second_exchange(): lax.ppermute(sums[1], 'scene', along_x)]
    ppermute x2, waiting for transfers between devices: 1.24 us -> 6.68 us  [first_exchange(): lax.ppermute(sends[0], 'scene', along_x)]
    ppermute x0 -> x3, starting transfers between devices: none -> 4.62 us  [the longest x1 2.86 us: shards(): got = lax.ppermute(send, 'view', [(i, i ^ 2 << bit) for i in range(groups)])]
    ppermute x2, waiting for transfers between devices: 9.01 us -> 13.5 us  [first_exchange(): lax.ppermute(sends[1], 'scene', along_y)]
    unnamed x19, local copies, waits for them, and re-layouts: 5.83 us -> 1.46 us
    all_to_all x2 -> x1, starting transfers between devices: 7.08 us -> 3.54 us  [across_views(): lax.all_to_all(packed, ('view', 'row'), split_axis=0, concat_axis=0, tile...]
    ppermute x2, waiting for transfers between devices: 3.2 us -> 6.38 us  [second_exchange(): lax.ppermute(sums[0], 'scene', along_y)]
  transfers between devices with their start and end apart: 22 -> 24, of which waited for: 14 -> 17; matrix products, arithmetic and copies ran while one was open for 1% -> 0% of each run, Pallas kernels for 10% -> 8%
where the time goes in v7:
time: 104 us
  waiting for transfers between devices  52.6 us (51%)
  starting transfers between devices  29.9 us (29%)
  Pallas kernels  19 us (18%)
  local copies, waits for them, and re-layouts  1.54 us (1%)
    all_to_all x1, waiting for transfers between devices, across_views(): lax.all_to_all(packed, ('view', 'row'), split_axis=0, concat_axis=0, tile...  14.7 us
    ppermute x2, waiting for transfers between devices, first_exchange(): lax.ppermute(sends[1], 'scene', along_y)  13.5 us
    pallas_call x10, Pallas kernels, call(): pl.pallas_call(kernel_body, in_specs=[first] + [VMEM] * (len(operands) -...  8.64 us
    ppermute x2, waiting for transfers between devices, first_exchange(): lax.ppermute(sends[0], 'scene', along_x)  6.68 us
    ppermute x2, waiting for transfers between devices, second_exchange(): lax.ppermute(sums[0], 'scene', along_y)  6.38 us
    ppermute x3, starting transfers between devices, shards(): granted = [lax.ppermute(request, 'view', pairs) for pairs in between]  5.76 us
    pallas_call x1, Pallas kernels, shards(): pl.pallas_call(functools.partial(attention_kernel, views, groups), in_spe...  4.87 us
    ppermute x3, starting transfers between devices, shards(): lax.ppermute(part_out, 'view', pairs)  4.44 us
  transfers between devices with their start and end apart: 24, of which 17 were waited for; matrix products, arithmetic and copies ran while one was open for 0% of the time, Pallas kernels for 8%

profile of v7, /device:TPU:0, one launch (start us, length us, event | category | flops | bytes accessed | tf_op | source)
XLA Modules:
  0.0 103.8 jit_solution(7545129616834986004)
XLA Ops:
  0.6 0.8 copy.14.partners
  1.4 0.7 copy-done.8
  2.1 1.2 %requests.1 = (s32[4]{0:T(128)S(1)}, s32[16]{0:T(128)S(1)}) custom-call(s32[1,4,3]{2,1,0:T(4,128)S(1)} %copy.14.partners, s32[1,4]{1,0:T(1,128)S(1)} %copy-done.8), custom_call_target="tpu_custom_call" | custom-call | flops 40000000000 | bytes 1 | tf_op jit(solution)/shard_map/requests/pallas_call | solution.py:365
  3.3 5.1 %collective-permute-start.2 = (s32[4]{0:T(128)S(1)}, s32[4]{0:T(128)S(1)}, u32[]{:S(2)}, u32[]{:S(2)}) collective-permute-start(s32[4]{0:T(128)S(1)} %get-tuple-element.53), channel_id=1, source_target_pairs={{0,6},{2,4},{4,2},{6,0},{1,7},{3,5},{5,3},{7,1},{8,14},{10,12},{12... | collective-permute-start | bytes 56 | tf_op jit(solution)/shard_map/ppermute | solution.py:375
  8.4 0.0 collective-permute-start.1
  8.4 0.6 collective-permute-start
  9.1 0.0 collective-permute-start.6
  9.1 0.5 collective-permute-start.7
  9.6 0.1 stack.23.scalars
  9.7 0.0 copy-start.6
  9.7 0.0 copy-start.7
  9.7 0.2 collective-permute-done.2.refs_2_
  9.9 2.9 %collective-permute-done.1.refs_1_ = s32[4]{0:T(128)S(1)} collective-permute-done((s32[4]{0:T(128)S(1)}, s32[4]{0:T(128)S(1)}, u32[]{:S(2)}, u32[]{:S(2)}) %collective-permute-start.1) | collective-permute-done | bytes 48 | tf_op jit(solution)/shard_map/ppermute | solution.py:375
  12.8 0.0 collective-permute-done.refs_0_
  12.9 0.6 pick.1
  13.4 0.1 collective-permute-start.3
  13.5 2.1 %collective-permute-start.4 = (bf16[32,1536]{1,0:T(8,128)(2,1)S(1)}, bf16[32,1536]{1,0:T(8,128)(2,1)S(1)}, u32[]{:S(2)}, u32[]{:S(2)}) collective-permute-start(bf16[32,1536]{1,0:T(8,128)(2,1)S(1)} %get-tuple-element.55), channel_id=1, source_target_pairs={{0,4},{2,6},{4,0},{6,2},{1,5},{3,7},{5,1},{7,3},{8,12},{10,14},{12... | collective-permute-start | bytes 294920 | tf_op jit(solution)/shard_map/ppermute | solution.py:391
  15.6 2.3 %collective-permute-start.5 = (bf16[32,1536]{1,0:T(8,128)(2,1)S(1)}, bf16[32,1536]{1,0:T(8,128)(2,1)S(1)}, u32[]{:S(2)}, u32[]{:S(2)}) collective-permute-start(bf16[32,1536]{1,0:T(8,128)(2,1)S(1)} %get-tuple-element.56), channel_id=1, source_target_pairs={{0,6},{2,4},{4,2},{6,0},{1,7},{3,5},{5,3},{7,1},{8,14},{10,12},{12... | collective-permute-start | bytes 294920 | tf_op jit(solution)/shard_map/ppermute | solution.py:391
  18.0 3.7 %project.1 = (bf16[256,1536]{1,0:T(8,128)(2,1)S(1)}, bf16[256,384]{1,0:T(8,128)(2,1)S(1)}, bf16[256,384]{1,0:T(8,128)(2,1)S(1)}, bf16[256,384]{1,0:T(8,128)(2,1)...) custom-call(s32[5]{0:T(128)S(1)} %stack.23.scalars, bf16[4,32,1536]{2,1,0:T(8,128)(2,1)S(1)} %bitcast.10, ...), custom_call_target="tpu_custom_call" | custom-call | flops 1 | bytes 1 | tf_op jit(solution)/shard_map/project/pallas_call | solution.py:392
  21.7 1.4 %collective-permute-done.4.refs_1_ = bf16[32,1536]{1,0:T(8,128)(2,1)S(1)} collective-permute-done((bf16[32,1536]{1,0:T(8,128)(2,1)S(1)}, bf16[32,1536]{1,0:T(8,128)(2,1)S(1)}, u32[]{:S(2)}, u32[]{:S(2)}) %collective-permute-start.4) | collective-permute-done | bytes 98336 | tf_op jit(solution)/shard_map/ppermute | solution.py:391
  23.1 0.0 collective-permute-done.5.refs_2_
  23.1 0.0 collective-permute-start.8
  23.1 0.5 collective-permute-start.9
  23.6 0.0 collective-permute-start.10
  23.6 0.8 collective-permute-done.8.refs_3_
  24.4 0.2 collective-permute-done.9.refs_4_
  24.5 0.4 collective-permute-done.10.refs_5_
  24.9 4.9 %attention.1 = (bf16[192,1536]{1,0:T(8,128)(2,1)S(1)}, bf16[256,384]{1,0:T(8,128)(2,1)S(1)}, bf16[256,384]{1,0:T(8,128)(2,1)S(1)}, bf16[448,384]{1,0:T(8,128)(2,1)S(1)}, bf16[448,384]{1,0:T(8,128)(2,1)S(1)}) custom-call(s32[5]{0:T(128)S(1)} %stack.23.scalars, s32[16]{0:T(128)S(1)} %get-tuple-element.59.alive, ...), custom_call_target="tpu_custom_call" | custom-call | flops 1 | bytes 1 | tf_op jit(solution)/shard_map/attention/pallas_call | solution.py:412
  29.8 0.2 collective-permute-start.11
  30.0 2.0 %grad_query_key.1 = (bf16[2,384,384]{2,1,0:T(8,128)(2,1)S(1)}, bf16[2,384,384]{2,1,0:T(8,128)(2,1)S(1)}, f32[2,384,384]{2,1,0:T(8,128)S(1)}, f32[2,384,384]{2,1,0:T(8,128)S(1)}) custom-call(s32[5]{0:T(128)S(1)} %stack.23.scalars, bf16[256,1536]{1,0:T(8,128)(2,1)S(1)} %get-tuple-element.58.normed, bf16[192,1536]{1,0:T(8,128)(2,1)S(1)} %get-tuple-element.67.normed_far, ...), custom_call_target="tpu_custom_call" | custom-call | flops 1 | bytes 1 | tf_op jit(solution)/shard_map/grad_query_key/pallas_call | solution.py:430
  31.9 0.0 collective-permute-done.11.theirs
  32.0 2.0 %grad_value_out.1 = (bf16[2,2,2,48,1536]{4,3,2,1,0:T(8,128)(2,1)S(1)}, f32[2,2,2,48,1536]{4,3,2,1,0:T(8,128)S(1)}) custom-call(s32[5]{0:T(128)S(1)} %stack.23.scalars, bf16[256,1536]{1,0:T(8,128)(2,1)S(1)} %get-tuple-element.58.normed, bf16[192,1536]{1,0:T(8,128)(2,1)S(1)} %get-tuple-element.67.normed_far, bf16[448,384]{1,0:T(8,128)(2,1)S(1)} %get-tuple-element.73.dvalue, ...), custom_call_target="tpu_custom_call" | custom-call | flops 1 | bytes 1 | tf_op jit(solution)/shard_map/grad_value_out/pallas_call | solution.py:430
  34.0 1.7 %collective-permute-start.16 = (bf16[2,2,2,48,1536]{4,3,2,1,0:T(8,128)(2,1)S(1)}, bf16[2,2,2,48,1536]{4,3,2,1,0:T(8,128)(2,1)S(1)}, u32[]{:S(2)}, u32[]{:S(2)}) collective-permute-start(bf16[2,2,2,48,1536]{4,3,2,1,0:T(8,128)(2,1)S(1)} %get-tuple-element.76), channel_id=1, source_target_pairs={{0,2},{2,0},{4,6},{6,4},{1,3},{3,1},{5,7},{7,5},{8,10},{10,8},{12,... | collective-permute-start | bytes 3538952 | tf_op jit(solution)/shard_map/ppermute | solution.py:480
  35.7 1.5 %collective-permute-start.13 = (bf16[2,384,384]{2,1,0:T(8,128)(2,1)S(1)}, bf16[2,384,384]{2,1,0:T(8,128)(2,1)S(1)}, u32[]{:S(2)}, u32[]{:S(2)}) collective-permute-start(bf16[2,384,384]{2,1,0:T(8,128)(2,1)S(1)} %get-tuple-element.79), channel_id=1, source_target_pairs={{0,16},{8,24},{16,0},{24,8},{1,17},{9,25},{17,1},{25,9},{2,18},{10... | collective-permute-start | bytes 1769480 | tf_op jit(solution)/shard_map/ppermute | solution.py:450
  37.2 1.5 %collective-permute-start.12 = (bf16[2,384,384]{2,1,0:T(8,128)(2,1)S(1)}, bf16[2,384,384]{2,1,0:T(8,128)(2,1)S(1)}, u32[]{:S(2)}, u32[]{:S(2)}) collective-permute-start(bf16[2,384,384]{2,1,0:T(8,128)(2,1)S(1)} %get-tuple-element.72), channel_id=1, source_target_pairs={{0,8},{8,0},{16,24},{24,16},{1,9},{9,1},{17,25},{25,17},{2,10},{10... | collective-permute-start | bytes 1769480 | tf_op jit(solution)/shard_map/ppermute | solution.py:450
  38.7 12.3 %collective-permute-done.13.y_got = bf16[2,384,384]{2,1,0:T(8,128)(2,1)S(1)} collective-permute-done((bf16[2,384,384]{2,1,0:T(8,128)(2,1)S(1)}, bf16[2,384,384]{2,1,0:T(8,128)(2,1)S(1)}, u32[]{:S(2)}, u32[]{:S(2)}) %collective-permute-start.13) | collective-permute-done | bytes 589856 | tf_op jit(solution)/shard_map/ppermute | solution.py:450
  51.0 1.2 %collective-permute-done.12.x_got = bf16[2,384,384]{2,1,0:T(8,128)(2,1)S(1)} collective-permute-done((bf16[2,384,384]{2,1,0:T(8,128)(2,1)S(1)}, bf16[2,384,384]{2,1,0:T(8,128)(2,1)S(1)}, u32[]{:S(2)}, u32[]{:S(2)}) %collective-permute-start.12) | collective-permute-done | bytes 589856 | tf_op jit(solution)/shard_map/ppermute | solution.py:450
  52.2 0.2 first_sum_query_key.1
  52.4 0.6 collective-permute-start.14
  53.0 1.5 %collective-permute-start.15 = (bf16[384,384]{1,0:T(8,128)(2,1)S(1)}, bf16[384,384]{1,0:T(8,128)(2,1)S(1)}, u32[]{:S(2)}, u32[]{:S(2)}) collective-permute-start(bf16[384,384]{1,0:T(8,128)(2,1)S(1)} %get-tuple-element.83), channel_id=1, source_target_pairs={{0,8},{8,0},{16,24},{24,16},{1,9},{9,1},{17,25},{25,17},{2,10},{10... | collective-permute-start | bytes 884744 | tf_op jit(solution)/shard_map/ppermute | solution.py:458
  54.5 5.8 %collective-permute-done.14.q_got = bf16[384,384]{1,0:T(8,128)(2,1)S(1)} collective-permute-done((bf16[384,384]{1,0:T(8,128)(2,1)S(1)}, bf16[384,384]{1,0:T(8,128)(2,1)S(1)}, u32[]{:S(2)}, u32[]{:S(2)}) %collective-permute-start.14) | collective-permute-done | bytes 294944 | tf_op jit(solution)/shard_map/ppermute | solution.py:458
  60.3 0.3 collective-permute-done.15.k_got
  60.7 0.9 second_sum_query_key.1
  61.6 0.7 collective-permute-done.16.got
  62.3 0.2 view_sum_value_out.1
  62.5 1.5 %collective-permute-start.17 = (bf16[2,2,48,768]{3,2,1,0:T(8,128)(2,1)S(1)}, bf16[2,2,48,768]{3,2,1,0:T(8,128)(2,1)S(1)}, u32[]{:S(2)}, u32[]{:S(2)}) collective-permute-start(bf16[2,2,48,768]{3,2,1,0:T(8,128)(2,1)S(1)} %get-tuple-element.89), channel_id=1, source_target_pairs={{0,8},{8,0},{16,24},{24,16},{1,9},{9,1},{17,25},{25,17},{2,10},{10... | collective-permute-start | bytes 884744 | tf_op jit(solution)/shard_map/ppermute | solution.py:450
  64.0 1.5 %collective-permute-start.18 = (bf16[2,2,48,768]{3,2,1,0:T(8,128)(2,1)S(1)}, bf16[2,2,48,768]{3,2,1,0:T(8,128)(2,1)S(1)}, u32[]{:S(2)}, u32[]{:S(2)}) collective-permute-start(bf16[2,2,48,768]{3,2,1,0:T(8,128)(2,1)S(1)} %get-tuple-element.91), channel_id=1, source_target_pairs={{0,16},{8,24},{16,0},{24,8},{1,17},{9,25},{17,1},{25,9},{2,18},{10... | collective-permute-start | bytes 884744 | tf_op jit(solution)/shard_map/ppermute | solution.py:450
  65.5 5.5 %collective-permute-done.17.x_got = bf16[2,2,48,768]{3,2,1,0:T(8,128)(2,1)S(1)} collective-permute-done((bf16[2,2,48,768]{3,2,1,0:T(8,128)(2,1)S(1)}, bf16[2,2,48,768]{3,2,1,0:T(8,128)(2,1)S(1)}, u32[]{:S(2)}, u32[]{:S(2)}) %collective-permute-start.17) | collective-permute-done | bytes 294944 | tf_op jit(solution)/shard_map/ppermute | solution.py:450
  71.0 1.2 %collective-permute-done.18.y_got = bf16[2,2,48,768]{3,2,1,0:T(8,128)(2,1)S(1)} collective-permute-done((bf16[2,2,48,768]{3,2,1,0:T(8,128)(2,1)S(1)}, bf16[2,2,48,768]{3,2,1,0:T(8,128)(2,1)S(1)}, u32[]{:S(2)}, u32[]{:S(2)}) %collective-permute-start.18) | collective-permute-done | bytes 294944 | tf_op jit(solution)/shard_map/ppermute | solution.py:450
  72.2 0.1 first_sum_value_out.1
  72.3 0.6 collective-permute-start.19
  72.9 1.5 %collective-permute-start.20 = (bf16[2,48,768]{2,1,0:T(8,128)(2,1)S(1)}, bf16[2,48,768]{2,1,0:T(8,128)(2,1)S(1)}, u32[]{:S(2)}, u32[]{:S(2)}) collective-permute-start(bf16[2,48,768]{2,1,0:T(8,128)(2,1)S(1)} %get-tuple-element.95), channel_id=1, source_target_pairs={{0,16},{8,24},{16,0},{24,8},{1,17},{9,25},{17,1},{25,9},{2,18},{10... | collective-permute-start | bytes 442376 | tf_op jit(solution)/shard_map/ppermute | solution.py:458
  74.4 3.1 %collective-permute-done.19.refs_1_ = bf16[2,48,768]{2,1,0:T(8,128)(2,1)S(1)} collective-permute-done((bf16[2,48,768]{2,1,0:T(8,128)(2,1)S(1)}, bf16[2,48,768]{2,1,0:T(8,128)(2,1)S(1)}, u32[]{:S(2)}, u32[]{:S(2)}) %collective-permute-start.19) | collective-permute-done | bytes 147488 | tf_op jit(solution)/shard_map/ppermute | solution.py:458
  77.5 0.5 collective-permute-done.20.refs_3_
  78.1 0.6 view_bit_value_out.1
  78.7 2.9 %collective-permute-start.21 = (bf16[1,48,1536]{2,1,0:T(8,128)(2,1)S(1)}, bf16[1,48,1536]{2,1,0:T(8,128)(2,1)S(1)}, u32[]{:S(2)}, u32[]{:S(2)}) collective-permute-start(bf16[1,48,1536]{2,1,0:T(8,128)(2,1)S(1)} %get-tuple-element.97), channel_id=1, source_target_pairs={{0,4},{2,6},{4,0},{6,2},{1,5},{3,7},{5,1},{7,3},{8,12},{10,14},{12... | collective-permute-start | bytes 442376 | tf_op jit(solution)/shard_map/ppermute | solution.py:522
  81.5 3.5 %all-to-all-start = ((bf16[8,48,768]{2,1,0:T(8,128)(2,1)}), bf16[8,48,768]{2,1,0:T(8,128)(2,1)S(1)}, u32[]{:S(2)}, u32[]{:S(2)}) async-start(bf16[8,48,768]{2,1,0:T(8,128)(2,1)} %bitcast.7), calls=%async_computation | async-start | bytes 1179648 | tf_op jit(solution)/shard_map/all_to_all | solution.py:461
  85.1 1.3 %collective-permute-done.21.got = bf16[1,48,1536]{2,1,0:T(8,128)(2,1)S(1)} collective-permute-done((bf16[1,48,1536]{2,1,0:T(8,128)(2,1)S(1)}, bf16[1,48,1536]{2,1,0:T(8,128)(2,1)S(1)}, u32[]{:S(2)}, u32[]{:S(2)}) %collective-permute-start.21) | collective-permute-done | bytes 147488 | tf_op jit(solution)/shard_map/ppermute | solution.py:522
  86.4 0.6 last_sum_value_out.1
  86.9 0.1 collective-permute-start.22
  87.0 14.7 %all-to-all-done.packed = bf16[8,48,768]{2,1,0:T(8,128)(2,1)S(1)} async-done(((bf16[8,48,768]{2,1,0:T(8,128)(2,1)}), bf16[8,48,768]{2,1,0:T(8,128)(2,1)S(1)}, u32[]{:S(2)}, u32[]{:S(2)}) %all-to-all-start) | async-done | bytes 589856 | tf_op jit(solution)/shard_map/all_to_all | solution.py:461
  101.8 0.8 last_sum_query_key.1
  102.5 0.0 collective-permute-done.22.theirs
  102.5 1.3 %place_value_out.1 = (f32[48,768]{1,0:T(8,128)}, f32[24,1536]{1,0:T(8,128)}) custom-call(s32[5]{0:T(128)S(1)} %stack.23.scalars, f32[24,1536]{1,0:T(8,128)S(1)} %get-tuple-element.98.mine, f32[24,1536]{1,0:T(8,128)S(1)} %collective-permute-done.22.theirs), custom_call_target="tpu_custom_call" | custom-call | flops 1 | bytes 1 | tf_op jit(solution)/shard_map/place_value_out/pallas_call | solution.py:430
  (18 shorter events, 0.0 us)
Async XLA Ops:
  1.4 0.7 copy-start.8
  2.1 7.0 %copy-start.4 = (bf16[1,4,1,32,1536]{4,3,2,1,0:T(8,128)(2,1)S(1)}, bf16[1,4,1,32,1536]{4,3,2,1,0:T(8,128)(2,1)}, u32[]{:S(2)}) copy-start(bf16[1,4,1,32,1536]{4,3,2,1,0:T(8,128)(2,1)} %param.10) | copy-start | bytes 1179652
  2.1 7.0 %copy-start.5 = (bf16[1,4,1,32,1536]{4,3,2,1,0:T(8,128)(2,1)S(1)}, bf16[1,4,1,32,1536]{4,3,2,1,0:T(8,128)(2,1)}, u32[]{:S(2)}) copy-start(bf16[1,4,1,32,1536]{4,3,2,1,0:T(8,128)(2,1)} %param.19) | copy-start | bytes 1179652
  3.3 6.6 %collective-permute-start.2 = (s32[4]{0:T(128)S(1)}, s32[4]{0:T(128)S(1)}, u32[]{:S(2)}, u32[]{:S(2)}) collective-permute-start(s32[4]{0:T(128)S(1)} %get-tuple-element.53), channel_id=1, source_target_pairs={{0,6},{2,4},{4,2},{6,0},{1,7},{3,5},{5,3},{7,1},{8,14},{10,12},{12... | collective-permute-start | bytes 56 | tf_op jit(solution)/shard_map/ppermute | solution.py:375
  8.4 4.4 %collective-permute-start.1 = (s32[4]{0:T(128)S(1)}, s32[4]{0:T(128)S(1)}, u32[]{:S(2)}, u32[]{:S(2)}) collective-permute-start(s32[4]{0:T(128)S(1)} %get-tuple-element.53), channel_id=1, source_target_pairs={{0,4},{2,6},{4,0},{6,2},{1,5},{3,7},{5,1},{7,3},{8,12},{10,14},{12... | collective-permute-start | bytes 56 | tf_op jit(solution)/shard_map/ppermute | solution.py:375
  8.4 4.4 %collective-permute-start = (s32[4]{0:T(128)S(1)}, s32[4]{0:T(128)S(1)}, u32[]{:S(2)}, u32[]{:S(2)}) collective-permute-start(s32[4]{0:T(128)S(1)} %get-tuple-element.53), channel_id=1, source_target_pairs={{0,2},{2,0},{4,6},{6,4},{1,3},{3,1},{5,7},{7,5},{8,10},{10,8},{12,... | collective-permute-start | bytes 56 | tf_op jit(solution)/shard_map/ppermute | solution.py:375
  9.1 8.8 %collective-permute-start.6 = (bf16[4,32,1536]{2,1,0:T(8,128)(2,1)S(1)}, bf16[4,32,1536]{2,1,0:T(8,128)(2,1)S(1)}, u32[]{:S(2)}, u32[]{:S(2)}) collective-permute-start(bf16[4,32,1536]{2,1,0:T(8,128)(2,1)S(1)} %bitcast.8), channel_id=1, source_target_pairs={{0,1},{1,0},{2,3},{3,2},{4,5},{5,4},{6,7},{7,6},{8,9},{9,8},{10,11... | collective-permute-start | bytes 1179656 | tf_op jit(solution)/shard_map/ppermute | solution.py:379
  9.1 8.8 %collective-permute-start.7 = (bf16[4,32,1536]{2,1,0:T(8,128)(2,1)S(1)}, bf16[4,32,1536]{2,1,0:T(8,128)(2,1)S(1)}, u32[]{:S(2)}, u32[]{:S(2)}) collective-permute-start(bf16[4,32,1536]{2,1,0:T(8,128)(2,1)S(1)} %bitcast.11), channel_id=1, source_target_pairs={{0,1},{1,0},{2,3},{3,2},{4,5},{5,4},{6,7},{7,6},{8,9},{9,8},{10,11... | collective-permute-start | bytes 1179656 | tf_op jit(solution)/shard_map/ppermute | solution.py:380
  9.7 8.3 %copy-start = (bf16[1536,768]{1,0:T(8,128)(2,1)S(1)}, bf16[1536,768]{1,0:T(8,128)(2,1)}, u32[]{:S(2)}) copy-start(bf16[1536,768]{1,0:T(8,128)(2,1)} %refs_11_.1) | copy-start | bytes 7077892
  9.7 8.3 %copy-start.1 = (bf16[1536,768]{1,0:T(8,128)(2,1)S(1)}, bf16[1536,768]{1,0:T(8,128)(2,1)}, u32[]{:S(2)}) copy-start(bf16[1536,768]{1,0:T(8,128)(2,1)} %refs_12_.1) | copy-start | bytes 7077892
  9.7 8.3 %copy-start.2 = (bf16[1536,768]{1,0:T(8,128)(2,1)S(1)}, bf16[1536,768]{1,0:T(8,128)(2,1)}, u32[]{:S(2)}) copy-start(bf16[1536,768]{1,0:T(8,128)(2,1)} %w_query.1) | copy-start | bytes 7077892
  9.7 8.3 %copy-start.3 = (bf16[768,1536]{1,0:T(8,128)(2,1)S(1)}, bf16[768,1536]{1,0:T(8,128)(2,1)}, u32[]{:S(2)}) copy-start(bf16[768,1536]{1,0:T(8,128)(2,1)} %w_out.1) | copy-start | bytes 7077892
  9.7 8.3 %copy-start.6 = (bf16[9,1536]{1,0:T(8,128)(2,1)S(1)}, bf16[9,1536]{1,0:T(8,128)(2,1)}, u32[]{:S(2)}) copy-start(bf16[9,1536]{1,0:T(8,128)(2,1)} %taps.1) | copy-start | bytes 82948
  9.7 8.3 %copy-start.7 = (f32[1536]{0:T(1024)S(1)}, f32[1536]{0:T(1024)}, u32[]{:S(2)}) copy-start(f32[1536]{0:T(1024)} %refs_10_.1) | copy-start | bytes 18436
  13.4 8.2 %collective-permute-start.3 = (bf16[32,1536]{1,0:T(8,128)(2,1)S(1)}, bf16[32,1536]{1,0:T(8,128)(2,1)S(1)}, u32[]{:S(2)}, u32[]{:S(2)}) collective-permute-start(bf16[32,1536]{1,0:T(8,128)(2,1)S(1)} %get-tuple-element.54), channel_id=1, source_target_pairs={{0,2},{2,0},{4,6},{6,4},{1,3},{3,1},{5,7},{7,5},{8,10},{10,8},{12,... | collective-permute-start | bytes 294920 | tf_op jit(solution)/shard_map/ppermute | solution.py:391
  13.5 9.5 %collective-permute-start.4 = (bf16[32,1536]{1,0:T(8,128)(2,1)S(1)}, bf16[32,1536]{1,0:T(8,128)(2,1)S(1)}, u32[]{:S(2)}, u32[]{:S(2)}) collective-permute-start(bf16[32,1536]{1,0:T(8,128)(2,1)S(1)} %get-tuple-element.55), channel_id=1, source_target_pairs={{0,4},{2,6},{4,0},{6,2},{1,5},{3,7},{5,1},{7,3},{8,12},{10,14},{12... | collective-permute-start | bytes 294920 | tf_op jit(solution)/shard_map/ppermute | solution.py:391
  15.6 7.5 %collective-permute-start.5 = (bf16[32,1536]{1,0:T(8,128)(2,1)S(1)}, bf16[32,1536]{1,0:T(8,128)(2,1)S(1)}, u32[]{:S(2)}, u32[]{:S(2)}) collective-permute-start(bf16[32,1536]{1,0:T(8,128)(2,1)S(1)} %get-tuple-element.56), channel_id=1, source_target_pairs={{0,6},{2,4},{4,2},{6,0},{1,7},{3,5},{5,3},{7,1},{8,14},{10,12},{12... | collective-permute-start | bytes 294920 | tf_op jit(solution)/shard_map/ppermute | solution.py:391
  23.1 1.3 %collective-permute-start.8 = (bf16[32,1536]{1,0:T(8,128)(2,1)S(1)}, bf16[32,1536]{1,0:T(8,128)(2,1)S(1)}, u32[]{:S(2)}, u32[]{:S(2)}) collective-permute-start(bf16[32,1536]{1,0:T(8,128)(2,1)S(1)} %collective-permute-done.3.refs_0_), channel_id=1, source_target_pairs={{0,1},{1,0},{2,3},{3,2},{4,5},{5,4},{6,7},{7,6},{8,9},{9,8},{10,11... | collective-permute-start | bytes 294920 | tf_op jit(solution)/shard_map/ppermute | solution.py:410
  23.1 1.5 %collective-permute-start.9 = (bf16[32,1536]{1,0:T(8,128)(2,1)S(1)}, bf16[32,1536]{1,0:T(8,128)(2,1)S(1)}, u32[]{:S(2)}, u32[]{:S(2)}) collective-permute-start(bf16[32,1536]{1,0:T(8,128)(2,1)S(1)} %collective-permute-done.4.refs_1_), channel_id=1, source_target_pairs={{0,1},{1,0},{2,3},{3,2},{4,5},{5,4},{6,7},{7,6},{8,9},{9,8},{10,11... | collective-permute-start | bytes 294920 | tf_op jit(solution)/shard_map/ppermute | solution.py:410
  23.6 1.3 %collective-permute-start.10 = (bf16[32,1536]{1,0:T(8,128)(2,1)S(1)}, bf16[32,1536]{1,0:T(8,128)(2,1)S(1)}, u32[]{:S(2)}, u32[]{:S(2)}) collective-permute-start(bf16[32,1536]{1,0:T(8,128)(2,1)S(1)} %collective-permute-done.5.refs_2_), channel_id=1, source_target_pairs={{0,1},{1,0},{2,3},{3,2},{4,5},{5,4},{6,7},{7,6},{8,9},{9,8},{10,11... | collective-permute-start | bytes 294920 | tf_op jit(solution)/shard_map/ppermute | solution.py:410
  29.8 2.2 %collective-permute-start.11 = (bf16[256,384]{1,0:T(8,128)(2,1)S(1)}, bf16[256,384]{1,0:T(8,128)(2,1)S(1)}, u32[]{:S(2)}, u32[]{:S(2)}) collective-permute-start(bf16[256,384]{1,0:T(8,128)(2,1)S(1)} %get-tuple-element.74.mine), channel_id=1, source_target_pairs={{0,1},{1,0},{2,3},{3,2},{4,5},{5,4},{6,7},{7,6},{8,9},{9,8},{10,11... | collective-permute-start | bytes 589832 | tf_op jit(solution)/shard_map/ppermute | solution.py:463
  34.0 28.3 %collective-permute-start.16 = (bf16[2,2,2,48,1536]{4,3,2,1,0:T(8,128)(2,1)S(1)}, bf16[2,2,2,48,1536]{4,3,2,1,0:T(8,128)(2,1)S(1)}, u32[]{:S(2)}, u32[]{:S(2)}) collective-permute-start(bf16[2,2,2,48,1536]{4,3,2,1,0:T(8,128)(2,1)S(1)} %get-tuple-element.76), channel_id=1, source_target_pairs={{0,2},{2,0},{4,6},{6,4},{1,3},{3,1},{5,7},{7,5},{8,10},{10,8},{12,... | collective-permute-start | bytes 3538952 | tf_op jit(solution)/shard_map/ppermute | solution.py:480
  35.7 15.3 %collective-permute-start.13 = (bf16[2,384,384]{2,1,0:T(8,128)(2,1)S(1)}, bf16[2,384,384]{2,1,0:T(8,128)(2,1)S(1)}, u32[]{:S(2)}, u32[]{:S(2)}) collective-permute-start(bf16[2,384,384]{2,1,0:T(8,128)(2,1)S(1)} %get-tuple-element.79), channel_id=1, source_target_pairs={{0,16},{8,24},{16,0},{24,8},{1,17},{9,25},{17,1},{25,9},{2,18},{10... | collective-permute-start | bytes 1769480 | tf_op jit(solution)/shard_map/ppermute | solution.py:450
  37.2 15.0 %collective-permute-start.12 = (bf16[2,384,384]{2,1,0:T(8,128)(2,1)S(1)}, bf16[2,384,384]{2,1,0:T(8,128)(2,1)S(1)}, u32[]{:S(2)}, u32[]{:S(2)}) collective-permute-start(bf16[2,384,384]{2,1,0:T(8,128)(2,1)S(1)} %get-tuple-element.72), channel_id=1, source_target_pairs={{0,8},{8,0},{16,24},{24,16},{1,9},{9,1},{17,25},{25,17},{2,10},{10... | collective-permute-start | bytes 1769480 | tf_op jit(solution)/shard_map/ppermute | solution.py:450
  52.4 7.9 %collective-permute-start.14 = (bf16[384,384]{1,0:T(8,128)(2,1)S(1)}, bf16[384,384]{1,0:T(8,128)(2,1)S(1)}, u32[]{:S(2)}, u32[]{:S(2)}) collective-permute-start(bf16[384,384]{1,0:T(8,128)(2,1)S(1)} %get-tuple-element.81), channel_id=1, source_target_pairs={{0,16},{8,24},{16,0},{24,8},{1,17},{9,25},{17,1},{25,9},{2,18},{10... | collective-permute-start | bytes 884744 | tf_op jit(solution)/shard_map/ppermute | solution.py:458
  53.0 7.6 %collective-permute-start.15 = (bf16[384,384]{1,0:T(8,128)(2,1)S(1)}, bf16[384,384]{1,0:T(8,128)(2,1)S(1)}, u32[]{:S(2)}, u32[]{:S(2)}) collective-permute-start(bf16[384,384]{1,0:T(8,128)(2,1)S(1)} %get-tuple-element.83), channel_id=1, source_target_pairs={{0,8},{8,0},{16,24},{24,16},{1,9},{9,1},{17,25},{25,17},{2,10},{10... | collective-permute-start | bytes 884744 | tf_op jit(solution)/shard_map/ppermute | solution.py:458
  62.5 8.5 %collective-permute-start.17 = (bf16[2,2,48,768]{3,2,1,0:T(8,128)(2,1)S(1)}, bf16[2,2,48,768]{3,2,1,0:T(8,128)(2,1)S(1)}, u32[]{:S(2)}, u32[]{:S(2)}) collective-permute-start(bf16[2,2,48,768]{3,2,1,0:T(8,128)(2,1)S(1)} %get-tuple-element.89), channel_id=1, source_target_pairs={{0,8},{8,0},{16,24},{24,16},{1,9},{9,1},{17,25},{25,17},{2,10},{10... | collective-permute-start | bytes 884744 | tf_op jit(solution)/shard_map/ppermute | solution.py:450
  64.0 8.2 %collective-permute-start.18 = (bf16[2,2,48,768]{3,2,1,0:T(8,128)(2,1)S(1)}, bf16[2,2,48,768]{3,2,1,0:T(8,128)(2,1)S(1)}, u32[]{:S(2)}, u32[]{:S(2)}) collective-permute-start(bf16[2,2,48,768]{3,2,1,0:T(8,128)(2,1)S(1)} %get-tuple-element.91), channel_id=1, source_target_pairs={{0,16},{8,24},{16,0},{24,8},{1,17},{9,25},{17,1},{25,9},{2,18},{10... | collective-permute-start | bytes 884744 | tf_op jit(solution)/shard_map/ppermute | solution.py:450
  72.3 5.2 %collective-permute-start.19 = (bf16[2,48,768]{2,1,0:T(8,128)(2,1)S(1)}, bf16[2,48,768]{2,1,0:T(8,128)(2,1)S(1)}, u32[]{:S(2)}, u32[]{:S(2)}) collective-permute-start(bf16[2,48,768]{2,1,0:T(8,128)(2,1)S(1)} %get-tuple-element.93), channel_id=1, source_target_pairs={{0,8},{8,0},{16,24},{24,16},{1,9},{9,1},{17,25},{25,17},{2,10},{10... | collective-permute-start | bytes 442376 | tf_op jit(solution)/shard_map/ppermute | solution.py:458
  72.9 5.1 %collective-permute-start.20 = (bf16[2,48,768]{2,1,0:T(8,128)(2,1)S(1)}, bf16[2,48,768]{2,1,0:T(8,128)(2,1)S(1)}, u32[]{:S(2)}, u32[]{:S(2)}) collective-permute-start(bf16[2,48,768]{2,1,0:T(8,128)(2,1)S(1)} %get-tuple-element.95), channel_id=1, source_target_pairs={{0,16},{8,24},{16,0},{24,8},{1,17},{9,25},{17,1},{25,9},{2,18},{10... | collective-permute-start | bytes 442376 | tf_op jit(solution)/shard_map/ppermute | solution.py:458
  78.7 7.7 %collective-permute-start.21 = (bf16[1,48,1536]{2,1,0:T(8,128)(2,1)S(1)}, bf16[1,48,1536]{2,1,0:T(8,128)(2,1)S(1)}, u32[]{:S(2)}, u32[]{:S(2)}) collective-permute-start(bf16[1,48,1536]{2,1,0:T(8,128)(2,1)S(1)} %get-tuple-element.97), channel_id=1, source_target_pairs={{0,4},{2,6},{4,0},{6,2},{1,5},{3,7},{5,1},{7,3},{8,12},{10,14},{12... | collective-permute-start | bytes 442376 | tf_op jit(solution)/shard_map/ppermute | solution.py:522
  81.5 20.2 %all-to-all-start = ((bf16[8,48,768]{2,1,0:T(8,128)(2,1)}), bf16[8,48,768]{2,1,0:T(8,128)(2,1)S(1)}, u32[]{:S(2)}, u32[]{:S(2)}) async-start(bf16[8,48,768]{2,1,0:T(8,128)(2,1)} %bitcast.7), calls=%async_computation | async-start | bytes 1179648 | tf_op jit(solution)/shard_map/all_to_all | solution.py:461
  86.9 15.6 %collective-permute-start.22 = (f32[24,1536]{1,0:T(8,128)S(1)}, f32[24,1536]{1,0:T(8,128)S(1)}, u32[]{:S(2)}, u32[]{:S(2)}) collective-permute-start(f32[24,1536]{1,0:T(8,128)S(1)} %get-tuple-element.99), channel_id=1, source_target_pairs={{0,1},{1,0},{2,3},{3,2},{4,5},{5,4},{6,7},{7,6},{8,9},{9,8},{10,11... | collective-permute-start | bytes 442376 | tf_op jit(solution)/shard_map/ppermute | solution.py:532

commit v8 on v7

--- a/solution.py
+++ b/solution.py
@@ -285,39 +285,50 @@
     packed[:, size:] = (k_now[...] + k_got[...].astype(jnp.float32)).astype(jnp.bfloat16)
 
 
-def tile_halves_kernel(bit, out_and_value, scalars, *refs):
+def summed_tile(addends, place):
+    place = pl.ds(place, 1)
+    total = [now[place] + got[place].astype(jnp.float32) for now, got in zip(addends[::2], addends[1::2])]
+    return (jnp.concatenate(total, axis=2) if len(total) == 2 else total[0])[0]
+
+
+def view_bit(scalars, bit):
+    return lax.rem(lax.div(scalars[1], jnp.int32(2 << bit)), jnp.int32(2))
+
+
+def tile_halves_kernel(bit, scalars, *refs):
     addends, (send, keep) = refs[:-2], refs[-2:]
     count = keep.shape[0]
-    mine = lax.rem(lax.div(scalars[1], jnp.int32(2 << bit)), jnp.int32(2))
+    mine = view_bit(scalars, bit)
     for target, part in ((send, 1 - mine), (keep, mine)):
         for i in range(count):
-            place = pl.ds(part * count + i, 1)
-            total = [now[place] + got[place].astype(jnp.float32) for now, got in zip(addends[::2], addends[1::2])]
-            total = jnp.concatenate(total, axis=2) if out_and_value else total[0]
-            target[i] = total[0].astype(target.dtype)
-
-
-def tile_cores_kernel(scalars, keep, got, send, mine):
-    total = keep[0] + got[0].astype(jnp.float32)
+            target[i] = summed_tile(addends, part * count + i).astype(target.dtype)
+
+
+def tile_cores_kernel(scalars, *refs):
+    addends, (far_same, far_cross, near_cross, mine) = refs[:-4], refs[-4:]
     size, width = mine.shape
     half, quarter = width // 2, width // 4
-    parts = []
-    for core in range(2):
-        value = total[:, half + core * quarter : half + (core + 1) * quarter]
-        out = total[core * size : (core + 1) * size, :half]
-        parts.append(jnp.concatenate((out, value[:size], value[size:]), axis=1))
-    send[...] = jnp.where(scalars[0] == 0, parts[1], parts[0])
-    mine[...] = jnp.where(scalars[0] == 0, parts[0], parts[1])
-
-
-def place_kernel(scalars, mine, theirs, value, out):
+    bit = view_bit(scalars, 0)
+    for place, same, cross in ((1 - bit, far_same, far_cross), (bit, mine, near_cross)):
+        total = summed_tile(addends, place)
+        parts = []
+        for core in range(2):
+            value = total[:, half + core * quarter : half + (core + 1) * quarter]
+            out = total[core * size : (core + 1) * size, :half]
+            parts.append(jnp.concatenate((out, value[:size], value[size:]), axis=1))
+        same[...] = jnp.where(scalars[0] == 0, parts[0], parts[1]).astype(same.dtype)
+        cross[...] = jnp.where(scalars[0] == 0, parts[1], parts[0]).astype(cross.dtype)
+
+
+def place_kernel(scalars, mine, far_same, near_cross, far_cross, value, out):
     size, width = mine.shape
     half, quarter = width // 2, width // 4
-    for source, core in ((mine, scalars[0]), (theirs, 1 - scalars[0])):
-        out[:, pl.ds(pl.multiple_of(core * half, half), half)] = source[:, :half]
+    for near, far, core in ((mine, far_same, scalars[0]), (near_cross, far_cross, 1 - scalars[0])):
+        total = near[...] + far[...].astype(jnp.float32)
+        out[:, pl.ds(pl.multiple_of(core * half, half), half)] = total[:, :half]
         columns = pl.ds(pl.multiple_of(core * quarter, quarter), quarter)
-        value[:size, columns] = source[:, half : half + quarter]
-        value[size:, columns] = source[:, half + quarter :]
+        value[:size, columns] = total[:, half : half + quarter]
+        value[size:, columns] = total[:, half + quarter :]
 
 
 def summed_views(rows, packed):
@@ -505,36 +516,33 @@
         cost=MUCH,
     )
     vo_got = first_exchange(vo_parts)
-    vo_sums = first_sum(vo_parts, vo_got, "first_sum_value_out", MUCH)
+    vo_sums = first_sum(vo_parts, vo_got, "first_sum_value_out")
     v_got, o_got = second_exchange(vo_sums)
     addends = (vo_sums[3], o_got, vo_sums[2], v_got)
-    bit = pairs.bit_length() - 1
-    while bit > 0:
-        bit -= 1
+    for bit in reversed(range(1, pairs.bit_length() - 1)):
         send, keep = call(
-            functools.partial(tile_halves_kernel, bit, len(addends) == 4),
+            functools.partial(tile_halves_kernel, bit),
             [shape((1 << bit, *tile), kind) for kind in (bf16, f32)],
             (scalars, *addends),
             "view_bit_value_out",
             SMEM,
-            cost=MUCH,
         )
-        got = lax.ppermute(send, "view", [(i, i ^ (2 << bit)) for i in range(groups)])
-        addends = (keep, got)
-    send, mine = call(
+        addends = (keep, lax.ppermute(send, "view", [(i, i ^ (2 << bit)) for i in range(groups)]))
+    far_same, far_cross, near_cross, mine = call(
         tile_cores_kernel,
-        [shape((o_rows, width), f32)] * 2,
+        [shape((o_rows, width), kind) for kind in (bf16, bf16, f32, f32)],
         (scalars, *addends),
-        "last_sum_value_out",
+        "last_parts_value_out",
         SMEM,
-        cost=MUCH,
-    )
-    theirs = lax.ppermute(send, "row", swap)
+    )
+    far_same = lax.ppermute(far_same, "view", [(i, i ^ 2) for i in range(groups)])
+    far_cross = lax.ppermute(far_cross, ("view", "row"), [(i, i ^ 5) for i in range(targets)])
+    near_cross = lax.ppermute(near_cross, "row", swap)
     grad_value, grad_out = call(
         place_kernel,
         [shape((q_rows, inner), f32), shape((o_rows, width), f32)],
-        (scalars, mine, theirs),
-        "place_value_out",
+        (scalars, after(mine, grad_key), far_same, near_cross, far_cross),
+        "last_sum_value_out",
         SMEM,
     )
     return grad_query, grad_key, grad_value, grad_out

time: 104 us -> 97.6 us (0.938)
  waiting for transfers between devices: 52.6 us -> 43.6 us
  local copies, waits for them, and re-layouts: 1.54 us -> 3.2 us
    all_to_all x1, waiting for transfers between devices: 14.7 us -> 0.01 us  [across_views(): lax.all_to_all(packed, ('view', 'row'), split_axis=0, concat_axis=0, tile...]
    ppermute x2 -> x3, waiting for transfers between devices: 1.29 us -> 6.48 us  [the longest x1 3.96 us: shards(): lax.ppermute(far_same, 'view', [(i, i ^ 2) for i in range(groups)])]
    unnamed x19 -> x23, local copies, waits for them, and re-layouts: 1.46 us -> 3.12 us
    pallas_call x10 -> x9, Pallas kernels: 8.64 us -> 9.38 us  [call(): pl.pallas_call(kernel_body, in_specs=[first] + [VMEM] * (len(operands) -...]
    ppermute x2 -> x3, starting transfers between devices: 2.93 us -> 2.83 us  [the longest x1 2.63 us: shards(): lax.ppermute(far_same, 'view', [(i, i ^ 2) for i in range(groups)])]
  transfers between devices with their start and end apart: 24 -> 25, of which waited for: 17 -> 16; matrix products, arithmetic and copies ran while one was open for 0% -> 0% of each run, Pallas kernels for 8% -> 11%
where the time goes in v8:
time: 97.6 us; the launch traced here: 97.3 us
  waiting for transfers between devices  43.6 us (45%)
  starting transfers between devices  30 us (31%)
  Pallas kernels  19.8 us (20%)
  local copies, waits for them, and re-layouts  3.2 us (3%)
    ppermute x2, waiting for transfers between devices, first_exchange(): lax.ppermute(sends[1], 'scene', along_y)  13.5 us
    pallas_call x9, Pallas kernels, call(): pl.pallas_call(kernel_body, in_specs=[first] + [VMEM] * (len(operands) -...  9.38 us
    ppermute x2, waiting for transfers between devices, first_exchange(): lax.ppermute(sends[0], 'scene', along_x)  7.71 us
    ppermute x2, waiting for transfers between devices, second_exchange(): lax.ppermute(sums[0], 'scene', along_y)  6.44 us
    ppermute x3, starting transfers between devices, shards(): granted = [lax.ppermute(request, 'view', pairs) for pairs in between]  5.76 us
    pallas_call x1, Pallas kernels, shards(): pl.pallas_call(functools.partial(attention_kernel, views, groups), in_spe...  4.87 us
    ppermute x3, starting transfers between devices, shards(): lax.ppermute(part_out, 'view', pairs)  4.44 us
    ppermute x1, waiting for transfers between devices, shards(): lax.ppermute(far_same, 'view', [(i, i ^ 2) for i in range(groups)])  3.96 us
  transfers between devices with their start and end apart: 25, of which 16 were waited for; matrix products, arithmetic and copies ran while one was open for 0% of the time, Pallas kernels for 11%

profile of v8, /device:TPU:0, one launch (start us, length us, event | category | flops | bytes accessed | tf_op | source)
XLA Modules:
  0.0 97.3 jit_solution(16264112045216178270)
XLA Ops:
  0.6 0.8 copy.14.partners
  1.4 0.7 copy-done.10
  2.1 1.2 %requests.1 = (s32[4]{0:T(128)S(1)}, s32[16]{0:T(128)S(1)}) custom-call(s32[1,4,3]{2,1,0:T(4,128)S(1)} %copy.14.partners, s32[1,4]{1,0:T(1,128)S(1)} %copy-done.10), custom_call_target="tpu_custom_call" | custom-call | flops 40000000000 | bytes 1 | tf_op jit(solution)/shard_map/requests/pallas_call | solution.py:376
  3.3 5.1 %collective-permute-start.2 = (s32[4]{0:T(128)S(1)}, s32[4]{0:T(128)S(1)}, u32[]{:S(2)}, u32[]{:S(2)}) collective-permute-start(s32[4]{0:T(128)S(1)} %get-tuple-element.54), channel_id=1, source_target_pairs={{0,6},{2,4},{4,2},{6,0},{1,7},{3,5},{5,3},{7,1},{8,14},{10,12},{12... | collective-permute-start | bytes 56 | tf_op jit(solution)/shard_map/ppermute | solution.py:386
  8.4 0.0 collective-permute-start.1
  8.4 0.6 collective-permute-start
  9.1 0.5 collective-permute-start.7
  9.6 0.1 stack.23.scalars
  9.7 0.0 copy-start.6
  9.7 0.0 copy-start.7
  9.7 0.2 collective-permute-done.2.refs_2_
  9.9 2.9 %collective-permute-done.1.refs_1_ = s32[4]{0:T(128)S(1)} collective-permute-done((s32[4]{0:T(128)S(1)}, s32[4]{0:T(128)S(1)}, u32[]{:S(2)}, u32[]{:S(2)}) %collective-permute-start.1) | collective-permute-done | bytes 48 | tf_op jit(solution)/shard_map/ppermute | solution.py:386
  12.8 0.0 collective-permute-done.refs_0_
  12.9 0.6 pick.1
  13.4 0.1 collective-permute-start.3
  13.5 2.1 %collective-permute-start.4 = (bf16[32,1536]{1,0:T(8,128)(2,1)S(1)}, bf16[32,1536]{1,0:T(8,128)(2,1)S(1)}, u32[]{:S(2)}, u32[]{:S(2)}) collective-permute-start(bf16[32,1536]{1,0:T(8,128)(2,1)S(1)} %get-tuple-element.56), channel_id=1, source_target_pairs={{0,4},{2,6},{4,0},{6,2},{1,5},{3,7},{5,1},{7,3},{8,12},{10,14},{12... | collective-permute-start | bytes 294920 | tf_op jit(solution)/shard_map/ppermute | solution.py:402
  15.6 2.3 %collective-permute-start.5 = (bf16[32,1536]{1,0:T(8,128)(2,1)S(1)}, bf16[32,1536]{1,0:T(8,128)(2,1)S(1)}, u32[]{:S(2)}, u32[]{:S(2)}) collective-permute-start(bf16[32,1536]{1,0:T(8,128)(2,1)S(1)} %get-tuple-element.57), channel_id=1, source_target_pairs={{0,6},{2,4},{4,2},{6,0},{1,7},{3,5},{5,3},{7,1},{8,14},{10,12},{12... | collective-permute-start | bytes 294920 | tf_op jit(solution)/shard_map/ppermute | solution.py:402
  17.9 0.0 collective-permute-done.6.lat_other
  18.0 3.7 %project.1 = (bf16[256,1536]{1,0:T(8,128)(2,1)S(1)}, bf16[256,384]{1,0:T(8,128)(2,1)S(1)}, bf16[256,384]{1,0:T(8,128)(2,1)S(1)}, bf16[256,384]{1,0:T(8,128)(2,1)...) custom-call(s32[5]{0:T(128)S(1)} %stack.23.scalars, bf16[4,32,1536]{2,1,0:T(8,128)(2,1)S(1)} %bitcast.10, ...), custom_call_target="tpu_custom_call" | custom-call | flops 1 | bytes 1 | tf_op jit(solution)/shard_map/project/pallas_call | solution.py:403
  21.7 0.0 collective-permute-done.3.refs_0_
  21.7 1.4 %collective-permute-done.4.refs_1_ = bf16[32,1536]{1,0:T(8,128)(2,1)S(1)} collective-permute-done((bf16[32,1536]{1,0:T(8,128)(2,1)S(1)}, bf16[32,1536]{1,0:T(8,128)(2,1)S(1)}, u32[]{:S(2)}, u32[]{:S(2)}) %collective-permute-start.4) | collective-permute-done | bytes 98336 | tf_op jit(solution)/shard_map/ppermute | solution.py:402
  23.1 0.0 collective-permute-start.8
  23.1 0.5 collective-permute-start.9
  23.6 0.0 collective-permute-start.10
  23.6 0.8 collective-permute-done.8.refs_3_
  24.4 0.2 collective-permute-done.9.refs_4_
  24.5 0.4 collective-permute-done.10.refs_5_
  24.9 4.9 %attention.1 = (bf16[192,1536]{1,0:T(8,128)(2,1)S(1)}, bf16[256,384]{1,0:T(8,128)(2,1)S(1)}, bf16[256,384]{1,0:T(8,128)(2,1)S(1)}, bf16[448,384]{1,0:T(8,128)(2,1)S(1)}, bf16[448,384]{1,0:T(8,128)(2,1)S(1)}) custom-call(s32[5]{0:T(128)S(1)} %stack.23.scalars, s32[16]{0:T(128)S(1)} %get-tuple-element.60.alive, ...), custom_call_target="tpu_custom_call" | custom-call | flops 1 | bytes 1 | tf_op jit(solution)/shard_map/attention/pallas_call | solution.py:423
  29.8 0.2 collective-permute-start.11
  30.0 2.0 %grad_query_key.1 = (bf16[2,384,384]{2,1,0:T(8,128)(2,1)S(1)}, bf16[2,384,384]{2,1,0:T(8,128)(2,1)S(1)}, f32[2,384,384]{2,1,0:T(8,128)S(1)}, f32[2,384,384]{2,1,0:T(8,128)S(1)}) custom-call(s32[5]{0:T(128)S(1)} %stack.23.scalars, bf16[256,1536]{1,0:T(8,128)(2,1)S(1)} %get-tuple-element.59.normed, bf16[192,1536]{1,0:T(8,128)(2,1)S(1)} %get-tuple-element.68.normed_far, ...), custom_call_target="tpu_custom_call" | custom-call | flops 1 | bytes 1 | tf_op jit(solution)/shard_map/grad_query_key/pallas_call | solution.py:441
  31.9 0.0 collective-permute-done.11.theirs
  32.0 2.0 %grad_value_out.1 = (bf16[2,2,2,48,1536]{4,3,2,1,0:T(8,128)(2,1)S(1)}, f32[2,2,2,48,1536]{4,3,2,1,0:T(8,128)S(1)}) custom-call(s32[5]{0:T(128)S(1)} %stack.23.scalars, bf16[256,1536]{1,0:T(8,128)(2,1)S(1)} %get-tuple-element.59.normed, bf16[192,1536]{1,0:T(8,128)(2,1)S(1)} %get-tuple-element.68.normed_far, bf16[448,384]{1,0:T(8,128)(2,1)S(1)} %get-tuple-element.74.dvalue, ...), custom_call_target="tpu_custom_call" | custom-call | flops 1 | bytes 1 | tf_op jit(solution)/shard_map/grad_value_out/pallas_call | solution.py:441
  34.0 1.7 %collective-permute-start.16 = (bf16[2,2,2,48,1536]{4,3,2,1,0:T(8,128)(2,1)S(1)}, bf16[2,2,2,48,1536]{4,3,2,1,0:T(8,128)(2,1)}, u32[]{:S(2)}, u32[]{:S(2)}) collective-permute-start(bf16[2,2,2,48,1536]{4,3,2,1,0:T(8,128)(2,1)S(1)} %get-tuple-element.77), channel_id=1, source_target_pairs={{0,2},{2,0},{4,6},{6,4},{1,3},{3,1},{5,7},{7,5},{8,10},{10,8},{12,... | collective-permute-start | bytes 3538952 | tf_op jit(solution)/shard_map/ppermute | solution.py:491
  35.7 1.5 %collective-permute-start.13 = (bf16[2,384,384]{2,1,0:T(8,128)(2,1)S(1)}, bf16[2,384,384]{2,1,0:T(8,128)(2,1)S(1)}, u32[]{:S(2)}, u32[]{:S(2)}) collective-permute-start(bf16[2,384,384]{2,1,0:T(8,128)(2,1)S(1)} %get-tuple-element.80), channel_id=1, source_target_pairs={{0,16},{8,24},{16,0},{24,8},{1,17},{9,25},{17,1},{25,9},{2,18},{10... | collective-permute-start | bytes 1769480 | tf_op jit(solution)/shard_map/ppermute | solution.py:461
  37.2 1.5 %collective-permute-start.12 = (bf16[2,384,384]{2,1,0:T(8,128)(2,1)S(1)}, bf16[2,384,384]{2,1,0:T(8,128)(2,1)S(1)}, u32[]{:S(2)}, u32[]{:S(2)}) collective-permute-start(bf16[2,384,384]{2,1,0:T(8,128)(2,1)S(1)} %get-tuple-element.73), channel_id=1, source_target_pairs={{0,8},{8,0},{16,24},{24,16},{1,9},{9,1},{17,25},{25,17},{2,10},{10... | collective-permute-start | bytes 1769480 | tf_op jit(solution)/shard_map/ppermute | solution.py:461
  38.7 12.3 %collective-permute-done.13.y_got = bf16[2,384,384]{2,1,0:T(8,128)(2,1)S(1)} collective-permute-done((bf16[2,384,384]{2,1,0:T(8,128)(2,1)S(1)}, bf16[2,384,384]{2,1,0:T(8,128)(2,1)S(1)}, u32[]{:S(2)}, u32[]{:S(2)}) %collective-permute-start.13) | collective-permute-done | bytes 589856 | tf_op jit(solution)/shard_map/ppermute | solution.py:461
  51.0 1.2 %collective-permute-done.12.x_got = bf16[2,384,384]{2,1,0:T(8,128)(2,1)S(1)} collective-permute-done((bf16[2,384,384]{2,1,0:T(8,128)(2,1)S(1)}, bf16[2,384,384]{2,1,0:T(8,128)(2,1)S(1)}, u32[]{:S(2)}, u32[]{:S(2)}) %collective-permute-start.12) | collective-permute-done | bytes 589856 | tf_op jit(solution)/shard_map/ppermute | solution.py:461
  52.2 0.2 first_sum_query_key.1
  52.4 0.6 collective-permute-start.14
  53.0 1.5 %collective-permute-start.15 = (bf16[384,384]{1,0:T(8,128)(2,1)S(1)}, bf16[384,384]{1,0:T(8,128)(2,1)S(1)}, u32[]{:S(2)}, u32[]{:S(2)}) collective-permute-start(bf16[384,384]{1,0:T(8,128)(2,1)S(1)} %get-tuple-element.84), channel_id=1, source_target_pairs={{0,8},{8,0},{16,24},{24,16},{1,9},{9,1},{17,25},{25,17},{2,10},{10... | collective-permute-start | bytes 884744 | tf_op jit(solution)/shard_map/ppermute | solution.py:469
  54.5 5.9 %collective-permute-done.14.q_got = bf16[384,384]{1,0:T(8,128)(2,1)S(1)} collective-permute-done((bf16[384,384]{1,0:T(8,128)(2,1)S(1)}, bf16[384,384]{1,0:T(8,128)(2,1)S(1)}, u32[]{:S(2)}, u32[]{:S(2)}) %collective-permute-start.14) | collective-permute-done | bytes 294944 | tf_op jit(solution)/shard_map/ppermute | solution.py:469
  60.5 0.3 collective-permute-done.15.k_got
  60.8 0.9 second_sum_query_key.1
  61.7 3.9 %all-to-all-start = ((bf16[8,48,768]{2,1,0:T(8,128)(2,1)}), bf16[8,48,768]{2,1,0:T(8,128)(2,1)S(1)}, u32[]{:S(2)}, u32[]{:S(2)}) async-start(bf16[8,48,768]{2,1,0:T(8,128)(2,1)} %bitcast.7), calls=%async_computation | async-start | bytes 1179648 | tf_op jit(solution)/shard_map/all_to_all | solution.py:472
  65.6 0.0 collective-permute-done.16.got
  65.6 1.7 %copy-done.9 = f32[2,2,2,48,1536]{4,3,2,1,0:T(8,128)S(1)} copy-done((f32[2,2,2,48,1536]{4,3,2,1,0:T(8,128)S(1)}, f32[2,2,2,48,1536]{4,3,2,1,0:T(8,128)}, u32[]{:S(2)}) %copy-start.9) | copy-done | bytes 2359320
  67.3 1.4 %view_sum_value_out.1 = (bf16[2,2,48,768]{3,2,1,0:T(8,128)(2,1)S(1)}, bf16[2,2,48,768]{3,2,1,0:T(8,128)(2,1)S(1)}, f32[2,2,48,768]{3,2,1,0:T(8,128)S(1)}, f32[2,2,48,768]{3,2,1,0:T(8,128)S(1)}) custom-call(f32[2,2,2,48,1536]{4,3,2,1,0:T(8,128)S(1)} %copy-done.9, bf16[2,2,2,48,1536]{4,3,2,1,0:T(8,128)(2,1)} %collective-permute-done.16.got), custom_call_target="tpu_custom_call" | custom-call | flops 40000000000 | bytes 1 | tf_op jit(solution)/shard_map/view_sum_value_out/pallas_call | solution.py:441
  68.7 1.6 %collective-permute-start.17 = (bf16[2,2,48,768]{3,2,1,0:T(8,128)(2,1)S(1)}, bf16[2,2,48,768]{3,2,1,0:T(8,128)(2,1)S(1)}, u32[]{:S(2)}, u32[]{:S(2)}) collective-permute-start(bf16[2,2,48,768]{3,2,1,0:T(8,128)(2,1)S(1)} %get-tuple-element.90), channel_id=1, source_target_pairs={{0,8},{8,0},{16,24},{24,16},{1,9},{9,1},{17,25},{25,17},{2,10},{10... | collective-permute-start | bytes 884744 | tf_op jit(solution)/shard_map/ppermute | solution.py:461
  70.3 1.4 %collective-permute-start.18 = (bf16[2,2,48,768]{3,2,1,0:T(8,128)(2,1)S(1)}, bf16[2,2,48,768]{3,2,1,0:T(8,128)(2,1)S(1)}, u32[]{:S(2)}, u32[]{:S(2)}) collective-permute-start(bf16[2,2,48,768]{3,2,1,0:T(8,128)(2,1)S(1)} %get-tuple-element.92), channel_id=1, source_target_pairs={{0,16},{8,24},{16,0},{24,8},{1,17},{9,25},{17,1},{25,9},{2,18},{10... | collective-permute-start | bytes 884744 | tf_op jit(solution)/shard_map/ppermute | solution.py:461
  71.7 6.5 %collective-permute-done.17.x_got = bf16[2,2,48,768]{3,2,1,0:T(8,128)(2,1)S(1)} collective-permute-done((bf16[2,2,48,768]{3,2,1,0:T(8,128)(2,1)S(1)}, bf16[2,2,48,768]{3,2,1,0:T(8,128)(2,1)S(1)}, u32[]{:S(2)}, u32[]{:S(2)}) %collective-permute-start.17) | collective-permute-done | bytes 294944 | tf_op jit(solution)/shard_map/ppermute | solution.py:461
  78.2 1.2 %collective-permute-done.18.y_got = bf16[2,2,48,768]{3,2,1,0:T(8,128)(2,1)S(1)} collective-permute-done((bf16[2,2,48,768]{3,2,1,0:T(8,128)(2,1)S(1)}, bf16[2,2,48,768]{3,2,1,0:T(8,128)(2,1)S(1)}, u32[]{:S(2)}, u32[]{:S(2)}) %collective-permute-start.18) | collective-permute-done | bytes 294944 | tf_op jit(solution)/shard_map/ppermute | solution.py:461
  79.5 0.1 first_sum_value_out.1
  79.6 0.6 collective-permute-start.19
  80.2 1.4 %collective-permute-start.20 = (bf16[2,48,768]{2,1,0:T(8,128)(2,1)S(1)}, bf16[2,48,768]{2,1,0:T(8,128)(2,1)S(1)}, u32[]{:S(2)}, u32[]{:S(2)}) collective-permute-start(bf16[2,48,768]{2,1,0:T(8,128)(2,1)S(1)} %get-tuple-element.96), channel_id=1, source_target_pairs={{0,16},{8,24},{16,0},{24,8},{1,17},{9,25},{17,1},{25,9},{2,18},{10... | collective-permute-start | bytes 442376 | tf_op jit(solution)/shard_map/ppermute | solution.py:469
  81.6 3.2 %collective-permute-done.19.refs_1_ = bf16[2,48,768]{2,1,0:T(8,128)(2,1)S(1)} collective-permute-done((bf16[2,48,768]{2,1,0:T(8,128)(2,1)S(1)}, bf16[2,48,768]{2,1,0:T(8,128)(2,1)S(1)}, u32[]{:S(2)}, u32[]{:S(2)}) %collective-permute-start.19) | collective-permute-done | bytes 147488 | tf_op jit(solution)/shard_map/ppermute | solution.py:469
  84.8 0.5 collective-permute-done.20.refs_3_
  85.3 0.6 last_parts_value_out.1
  85.9 0.1 collective-permute-start.22
  86.0 2.6 %collective-permute-start.21 = (bf16[24,1536]{1,0:T(8,128)(2,1)S(1)}, bf16[24,1536]{1,0:T(8,128)(2,1)S(1)}, u32[]{:S(2)}, u32[]{:S(2)}) collective-permute-start(bf16[24,1536]{1,0:T(8,128)(2,1)S(1)} %get-tuple-element.99), channel_id=1, source_target_pairs={{0,4},{2,6},{4,0},{6,2},{1,5},{3,7},{5,1},{7,3},{8,12},{10,14},{12... | collective-permute-start | bytes 221192 | tf_op jit(solution)/shard_map/ppermute | solution.py:538
  88.6 0.1 collective-permute-start.23
  88.8 0.8 last_sum_query_key.1
  89.5 4.0 %collective-permute-done.21.far_same = bf16[24,1536]{1,0:T(8,128)(2,1)S(1)} collective-permute-done((bf16[24,1536]{1,0:T(8,128)(2,1)S(1)}, bf16[24,1536]{1,0:T(8,128)(2,1)S(1)}, u32[]{:S(2)}, u32[]{:S(2)}) %collective-permute-start.21) | collective-permute-done | bytes 73760 | tf_op jit(solution)/shard_map/ppermute | solution.py:538
  93.5 2.5 %collective-permute-done.23.far_cross = bf16[24,1536]{1,0:T(8,128)(2,1)S(1)} collective-permute-done((bf16[24,1536]{1,0:T(8,128)(2,1)S(1)}, bf16[24,1536]{1,0:T(8,128)(2,1)S(1)}, u32[]{:S(2)}, u32[]{:S(2)}) %collective-permute-start.23) | collective-permute-done | bytes 73760 | tf_op jit(solution)/shard_map/ppermute | solution.py:539
  96.0 1.3 %last_sum_value_out.1 = (f32[48,768]{1,0:T(8,128)}, f32[24,1536]{1,0:T(8,128)}) custom-call(s32[5]{0:T(128)S(1)} %stack.23.scalars, f32[24,1536]{1,0:T(8,128)S(1)} %get-tuple-element.98.mine, bf16[24,1536]{1,0:T(8,128)(2,1)S(1)} %collective-permute-done.21.far_same, f32[24,1536]{1,0:T(8,128)S(1)} %collective-permute-done.22.near_cross, ...), custom_call_target="tpu_custom_call" | custom-call | flops 1 | bytes 1 | tf_op jit(solution)/shard_map/last_sum_value_out/pallas_call | solution.py:441
  (23 shorter events, 0.0 us)
Async XLA Ops:
  1.4 0.7 copy-start.10
  2.1 7.0 %copy-start.4 = (bf16[1,4,1,32,1536]{4,3,2,1,0:T(8,128)(2,1)S(1)}, bf16[1,4,1,32,1536]{4,3,2,1,0:T(8,128)(2,1)}, u32[]{:S(2)}) copy-start(bf16[1,4,1,32,1536]{4,3,2,1,0:T(8,128)(2,1)} %param.10) | copy-start | bytes 1179652
  2.1 7.0 %copy-start.5 = (bf16[1,4,1,32,1536]{4,3,2,1,0:T(8,128)(2,1)S(1)}, bf16[1,4,1,32,1536]{4,3,2,1,0:T(8,128)(2,1)}, u32[]{:S(2)}) copy-start(bf16[1,4,1,32,1536]{4,3,2,1,0:T(8,128)(2,1)} %param.19) | copy-start | bytes 1179652
  3.3 6.6 %collective-permute-start.2 = (s32[4]{0:T(128)S(1)}, s32[4]{0:T(128)S(1)}, u32[]{:S(2)}, u32[]{:S(2)}) collective-permute-start(s32[4]{0:T(128)S(1)} %get-tuple-element.54), channel_id=1, source_target_pairs={{0,6},{2,4},{4,2},{6,0},{1,7},{3,5},{5,3},{7,1},{8,14},{10,12},{12... | collective-permute-start | bytes 56 | tf_op jit(solution)/shard_map/ppermute | solution.py:386
  8.4 4.4 %collective-permute-start.1 = (s32[4]{0:T(128)S(1)}, s32[4]{0:T(128)S(1)}, u32[]{:S(2)}, u32[]{:S(2)}) collective-permute-start(s32[4]{0:T(128)S(1)} %get-tuple-element.54), channel_id=1, source_target_pairs={{0,4},{2,6},{4,0},{6,2},{1,5},{3,7},{5,1},{7,3},{8,12},{10,14},{12... | collective-permute-start | bytes 56 | tf_op jit(solution)/shard_map/ppermute | solution.py:386
  8.4 4.4 %collective-permute-start = (s32[4]{0:T(128)S(1)}, s32[4]{0:T(128)S(1)}, u32[]{:S(2)}, u32[]{:S(2)}) collective-permute-start(s32[4]{0:T(128)S(1)} %get-tuple-element.54), channel_id=1, source_target_pairs={{0,2},{2,0},{4,6},{6,4},{1,3},{3,1},{5,7},{7,5},{8,10},{10,8},{12,... | collective-permute-start | bytes 56 | tf_op jit(solution)/shard_map/ppermute | solution.py:386
  9.1 8.8 %collective-permute-start.6 = (bf16[4,32,1536]{2,1,0:T(8,128)(2,1)S(1)}, bf16[4,32,1536]{2,1,0:T(8,128)(2,1)S(1)}, u32[]{:S(2)}, u32[]{:S(2)}) collective-permute-start(bf16[4,32,1536]{2,1,0:T(8,128)(2,1)S(1)} %bitcast.8), channel_id=1, source_target_pairs={{0,1},{1,0},{2,3},{3,2},{4,5},{5,4},{6,7},{7,6},{8,9},{9,8},{10,11... | collective-permute-start | bytes 1179656 | tf_op jit(solution)/shard_map/ppermute | solution.py:390
  9.1 8.8 %collective-permute-start.7 = (bf16[4,32,1536]{2,1,0:T(8,128)(2,1)S(1)}, bf16[4,32,1536]{2,1,0:T(8,128)(2,1)S(1)}, u32[]{:S(2)}, u32[]{:S(2)}) collective-permute-start(bf16[4,32,1536]{2,1,0:T(8,128)(2,1)S(1)} %bitcast.11), channel_id=1, source_target_pairs={{0,1},{1,0},{2,3},{3,2},{4,5},{5,4},{6,7},{7,6},{8,9},{9,8},{10,11... | collective-permute-start | bytes 1179656 | tf_op jit(solution)/shard_map/ppermute | solution.py:391
  9.7 8.3 %copy-start = (bf16[1536,768]{1,0:T(8,128)(2,1)S(1)}, bf16[1536,768]{1,0:T(8,128)(2,1)}, u32[]{:S(2)}) copy-start(bf16[1536,768]{1,0:T(8,128)(2,1)} %refs_11_.1) | copy-start | bytes 7077892
  9.7 8.3 %copy-start.1 = (bf16[1536,768]{1,0:T(8,128)(2,1)S(1)}, bf16[1536,768]{1,0:T(8,128)(2,1)}, u32[]{:S(2)}) copy-start(bf16[1536,768]{1,0:T(8,128)(2,1)} %refs_12_.1) | copy-start | bytes 7077892
  9.7 8.3 %copy-start.2 = (bf16[1536,768]{1,0:T(8,128)(2,1)S(1)}, bf16[1536,768]{1,0:T(8,128)(2,1)}, u32[]{:S(2)}) copy-start(bf16[1536,768]{1,0:T(8,128)(2,1)} %w_query.1) | copy-start | bytes 7077892
  9.7 8.3 %copy-start.3 = (bf16[768,1536]{1,0:T(8,128)(2,1)S(1)}, bf16[768,1536]{1,0:T(8,128)(2,1)}, u32[]{:S(2)}) copy-start(bf16[768,1536]{1,0:T(8,128)(2,1)} %w_out.1) | copy-start | bytes 7077892
  9.7 8.3 %copy-start.6 = (bf16[9,1536]{1,0:T(8,128)(2,1)S(1)}, bf16[9,1536]{1,0:T(8,128)(2,1)}, u32[]{:S(2)}) copy-start(bf16[9,1536]{1,0:T(8,128)(2,1)} %taps.1) | copy-start | bytes 82948
  9.7 8.3 %copy-start.7 = (f32[1536]{0:T(1024)S(1)}, f32[1536]{0:T(1024)}, u32[]{:S(2)}) copy-start(f32[1536]{0:T(1024)} %refs_10_.1) | copy-start | bytes 18436
  13.4 8.2 %collective-permute-start.3 = (bf16[32,1536]{1,0:T(8,128)(2,1)S(1)}, bf16[32,1536]{1,0:T(8,128)(2,1)S(1)}, u32[]{:S(2)}, u32[]{:S(2)}) collective-permute-start(bf16[32,1536]{1,0:T(8,128)(2,1)S(1)} %get-tuple-element.55), channel_id=1, source_target_pairs={{0,2},{2,0},{4,6},{6,4},{1,3},{3,1},{5,7},{7,5},{8,10},{10,8},{12,... | collective-permute-start | bytes 294920 | tf_op jit(solution)/shard_map/ppermute | solution.py:402
  13.5 9.5 %collective-permute-start.4 = (bf16[32,1536]{1,0:T(8,128)(2,1)S(1)}, bf16[32,1536]{1,0:T(8,128)(2,1)S(1)}, u32[]{:S(2)}, u32[]{:S(2)}) collective-permute-start(bf16[32,1536]{1,0:T(8,128)(2,1)S(1)} %get-tuple-element.56), channel_id=1, source_target_pairs={{0,4},{2,6},{4,0},{6,2},{1,5},{3,7},{5,1},{7,3},{8,12},{10,14},{12... | collective-permute-start | bytes 294920 | tf_op jit(solution)/shard_map/ppermute | solution.py:402
  15.6 7.5 %collective-permute-start.5 = (bf16[32,1536]{1,0:T(8,128)(2,1)S(1)}, bf16[32,1536]{1,0:T(8,128)(2,1)S(1)}, u32[]{:S(2)}, u32[]{:S(2)}) collective-permute-start(bf16[32,1536]{1,0:T(8,128)(2,1)S(1)} %get-tuple-element.57), channel_id=1, source_target_pairs={{0,6},{2,4},{4,2},{6,0},{1,7},{3,5},{5,3},{7,1},{8,14},{10,12},{12... | collective-permute-start | bytes 294920 | tf_op jit(solution)/shard_map/ppermute | solution.py:402
  23.1 1.3 %collective-permute-start.8 = (bf16[32,1536]{1,0:T(8,128)(2,1)S(1)}, bf16[32,1536]{1,0:T(8,128)(2,1)S(1)}, u32[]{:S(2)}, u32[]{:S(2)}) collective-permute-start(bf16[32,1536]{1,0:T(8,128)(2,1)S(1)} %collective-permute-done.3.refs_0_), channel_id=1, source_target_pairs={{0,1},{1,0},{2,3},{3,2},{4,5},{5,4},{6,7},{7,6},{8,9},{9,8},{10,11... | collective-permute-start | bytes 294920 | tf_op jit(solution)/shard_map/ppermute | solution.py:421
  23.1 1.5 %collective-permute-start.9 = (bf16[32,1536]{1,0:T(8,128)(2,1)S(1)}, bf16[32,1536]{1,0:T(8,128)(2,1)S(1)}, u32[]{:S(2)}, u32[]{:S(2)}) collective-permute-start(bf16[32,1536]{1,0:T(8,128)(2,1)S(1)} %collective-permute-done.4.refs_1_), channel_id=1, source_target_pairs={{0,1},{1,0},{2,3},{3,2},{4,5},{5,4},{6,7},{7,6},{8,9},{9,8},{10,11... | collective-permute-start | bytes 294920 | tf_op jit(solution)/shard_map/ppermute | solution.py:421
  23.6 1.3 %collective-permute-start.10 = (bf16[32,1536]{1,0:T(8,128)(2,1)S(1)}, bf16[32,1536]{1,0:T(8,128)(2,1)S(1)}, u32[]{:S(2)}, u32[]{:S(2)}) collective-permute-start(bf16[32,1536]{1,0:T(8,128)(2,1)S(1)} %collective-permute-done.5.refs_2_), channel_id=1, source_target_pairs={{0,1},{1,0},{2,3},{3,2},{4,5},{5,4},{6,7},{7,6},{8,9},{9,8},{10,11... | collective-permute-start | bytes 294920 | tf_op jit(solution)/shard_map/ppermute | solution.py:421
  29.8 2.2 %collective-permute-start.11 = (bf16[256,384]{1,0:T(8,128)(2,1)S(1)}, bf16[256,384]{1,0:T(8,128)(2,1)S(1)}, u32[]{:S(2)}, u32[]{:S(2)}) collective-permute-start(bf16[256,384]{1,0:T(8,128)(2,1)S(1)} %get-tuple-element.75.mine), channel_id=1, source_target_pairs={{0,1},{1,0},{2,3},{3,2},{4,5},{5,4},{6,7},{7,6},{8,9},{9,8},{10,11... | collective-permute-start | bytes 589832 | tf_op jit(solution)/shard_map/ppermute | solution.py:474
  34.0 27.7 %copy-start.8 = (f32[2,2,2,48,1536]{4,3,2,1,0:T(8,128)}, f32[2,2,2,48,1536]{4,3,2,1,0:T(8,128)S(1)}, u32[]{:S(2)}) copy-start(f32[2,2,2,48,1536]{4,3,2,1,0:T(8,128)S(1)} %get-tuple-element.88.keep) | copy-start | bytes 7077892
  34.0 31.6 %collective-permute-start.16 = (bf16[2,2,2,48,1536]{4,3,2,1,0:T(8,128)(2,1)S(1)}, bf16[2,2,2,48,1536]{4,3,2,1,0:T(8,128)(2,1)}, u32[]{:S(2)}, u32[]{:S(2)}) collective-permute-start(bf16[2,2,2,48,1536]{4,3,2,1,0:T(8,128)(2,1)S(1)} %get-tuple-element.77), channel_id=1, source_target_pairs={{0,2},{2,0},{4,6},{6,4},{1,3},{3,1},{5,7},{7,5},{8,10},{10,8},{12,... | collective-permute-start | bytes 3538952 | tf_op jit(solution)/shard_map/ppermute | solution.py:491
  35.7 15.3 %collective-permute-start.13 = (bf16[2,384,384]{2,1,0:T(8,128)(2,1)S(1)}, bf16[2,384,384]{2,1,0:T(8,128)(2,1)S(1)}, u32[]{:S(2)}, u32[]{:S(2)}) collective-permute-start(bf16[2,384,384]{2,1,0:T(8,128)(2,1)S(1)} %get-tuple-element.80), channel_id=1, source_target_pairs={{0,16},{8,24},{16,0},{24,8},{1,17},{9,25},{17,1},{25,9},{2,18},{10... | collective-permute-start | bytes 1769480 | tf_op jit(solution)/shard_map/ppermute | solution.py:461
  37.2 15.0 %collective-permute-start.12 = (bf16[2,384,384]{2,1,0:T(8,128)(2,1)S(1)}, bf16[2,384,384]{2,1,0:T(8,128)(2,1)S(1)}, u32[]{:S(2)}, u32[]{:S(2)}) collective-permute-start(bf16[2,384,384]{2,1,0:T(8,128)(2,1)S(1)} %get-tuple-element.73), channel_id=1, source_target_pairs={{0,8},{8,0},{16,24},{24,16},{1,9},{9,1},{17,25},{25,17},{2,10},{10... | collective-permute-start | bytes 1769480 | tf_op jit(solution)/shard_map/ppermute | solution.py:461
  52.4 8.0 %collective-permute-start.14 = (bf16[384,384]{1,0:T(8,128)(2,1)S(1)}, bf16[384,384]{1,0:T(8,128)(2,1)S(1)}, u32[]{:S(2)}, u32[]{:S(2)}) collective-permute-start(bf16[384,384]{1,0:T(8,128)(2,1)S(1)} %get-tuple-element.82), channel_id=1, source_target_pairs={{0,16},{8,24},{16,0},{24,8},{1,17},{9,25},{17,1},{25,9},{2,18},{10... | collective-permute-start | bytes 884744 | tf_op jit(solution)/shard_map/ppermute | solution.py:469
  53.0 7.7 %collective-permute-start.15 = (bf16[384,384]{1,0:T(8,128)(2,1)S(1)}, bf16[384,384]{1,0:T(8,128)(2,1)S(1)}, u32[]{:S(2)}, u32[]{:S(2)}) collective-permute-start(bf16[384,384]{1,0:T(8,128)(2,1)S(1)} %get-tuple-element.84), channel_id=1, source_target_pairs={{0,8},{8,0},{16,24},{24,16},{1,9},{9,1},{17,25},{25,17},{2,10},{10... | collective-permute-start | bytes 884744 | tf_op jit(solution)/shard_map/ppermute | solution.py:469
  61.7 27.1 %all-to-all-start = ((bf16[8,48,768]{2,1,0:T(8,128)(2,1)}), bf16[8,48,768]{2,1,0:T(8,128)(2,1)S(1)}, u32[]{:S(2)}, u32[]{:S(2)}) async-start(bf16[8,48,768]{2,1,0:T(8,128)(2,1)} %bitcast.7), calls=%async_computation | async-start | bytes 1179648 | tf_op jit(solution)/shard_map/all_to_all | solution.py:472
  65.6 1.7 %copy-start.9 = (f32[2,2,2,48,1536]{4,3,2,1,0:T(8,128)S(1)}, f32[2,2,2,48,1536]{4,3,2,1,0:T(8,128)}, u32[]{:S(2)}) copy-start(f32[2,2,2,48,1536]{4,3,2,1,0:T(8,128)} %copy-done.8) | copy-start | bytes 7077892
  68.7 9.5 %collective-permute-start.17 = (bf16[2,2,48,768]{3,2,1,0:T(8,128)(2,1)S(1)}, bf16[2,2,48,768]{3,2,1,0:T(8,128)(2,1)S(1)}, u32[]{:S(2)}, u32[]{:S(2)}) collective-permute-start(bf16[2,2,48,768]{3,2,1,0:T(8,128)(2,1)S(1)} %get-tuple-element.90), channel_id=1, source_target_pairs={{0,8},{8,0},{16,24},{24,16},{1,9},{9,1},{17,25},{25,17},{2,10},{10... | collective-permute-start | bytes 884744 | tf_op jit(solution)/shard_map/ppermute | solution.py:461
  70.3 9.1 %collective-permute-start.18 = (bf16[2,2,48,768]{3,2,1,0:T(8,128)(2,1)S(1)}, bf16[2,2,48,768]{3,2,1,0:T(8,128)(2,1)S(1)}, u32[]{:S(2)}, u32[]{:S(2)}) collective-permute-start(bf16[2,2,48,768]{3,2,1,0:T(8,128)(2,1)S(1)} %get-tuple-element.92), channel_id=1, source_target_pairs={{0,16},{8,24},{16,0},{24,8},{1,17},{9,25},{17,1},{25,9},{2,18},{10... | collective-permute-start | bytes 884744 | tf_op jit(solution)/shard_map/ppermute | solution.py:461
  79.6 5.2 %collective-permute-start.19 = (bf16[2,48,768]{2,1,0:T(8,128)(2,1)S(1)}, bf16[2,48,768]{2,1,0:T(8,128)(2,1)S(1)}, u32[]{:S(2)}, u32[]{:S(2)}) collective-permute-start(bf16[2,48,768]{2,1,0:T(8,128)(2,1)S(1)} %get-tuple-element.94), channel_id=1, source_target_pairs={{0,8},{8,0},{16,24},{24,16},{1,9},{9,1},{17,25},{25,17},{2,10},{10... | collective-permute-start | bytes 442376 | tf_op jit(solution)/shard_map/ppermute | solution.py:469
  80.2 5.1 %collective-permute-start.20 = (bf16[2,48,768]{2,1,0:T(8,128)(2,1)S(1)}, bf16[2,48,768]{2,1,0:T(8,128)(2,1)S(1)}, u32[]{:S(2)}, u32[]{:S(2)}) collective-permute-start(bf16[2,48,768]{2,1,0:T(8,128)(2,1)S(1)} %get-tuple-element.96), channel_id=1, source_target_pairs={{0,16},{8,24},{16,0},{24,8},{1,17},{9,25},{17,1},{25,9},{2,18},{10... | collective-permute-start | bytes 442376 | tf_op jit(solution)/shard_map/ppermute | solution.py:469
  85.9 10.1 %collective-permute-start.22 = (f32[24,1536]{1,0:T(8,128)S(1)}, f32[24,1536]{1,0:T(8,128)S(1)}, u32[]{:S(2)}, u32[]{:S(2)}) collective-permute-start(f32[24,1536]{1,0:T(8,128)S(1)} %get-tuple-element.100), channel_id=1, source_target_pairs={{0,1},{1,0},{2,3},{3,2},{4,5},{5,4},{6,7},{7,6},{8,9},{9,8},{10,11... | collective-permute-start | bytes 442376 | tf_op jit(solution)/shard_map/ppermute | solution.py:540
  86.0 7.5 %collective-permute-start.21 = (bf16[24,1536]{1,0:T(8,128)(2,1)S(1)}, bf16[24,1536]{1,0:T(8,128)(2,1)S(1)}, u32[]{:S(2)}, u32[]{:S(2)}) collective-permute-start(bf16[24,1536]{1,0:T(8,128)(2,1)S(1)} %get-tuple-element.99), channel_id=1, source_target_pairs={{0,4},{2,6},{4,0},{6,2},{1,5},{3,7},{5,1},{7,3},{8,12},{10,14},{12... | collective-permute-start | bytes 221192 | tf_op jit(solution)/shard_map/ppermute | solution.py:538
  88.6 7.4 %collective-permute-start.23 = (bf16[24,1536]{1,0:T(8,128)(2,1)S(1)}, bf16[24,1536]{1,0:T(8,128)(2,1)S(1)}, u32[]{:S(2)}, u32[]{:S(2)}) collective-permute-start(bf16[24,1536]{1,0:T(8,128)(2,1)S(1)} %get-tuple-element.101), channel_id=1, source_target_pairs={{0,5},{1,4},{2,7},{3,6},{4,1},{5,0},{6,3},{7,2},{8,13},{9,12},{10,... | collective-permute-start | bytes 221192 | tf_op jit(solution)/shard_map/ppermute | solution.py:539

commit v9 on v8

--- a/solution.py
+++ b/solution.py
@@ -9,6 +9,7 @@
 
 HEAD_DIM = 64
 EPSILON = 1e-06
+SCALE = HEAD_DIM ** (-0.5)
 MASKED = -1e30
 MIB = 1024 * 1024
 LITTLE = pl.CostEstimate(flops=1, bytes_accessed=1, transcendentals=0)
@@ -36,17 +37,17 @@
     return (x * lax.rsqrt(mean + EPSILON) * gain).astype(jnp.bfloat16)
 
 
-def request_kernel(views, slots, groups, partners, counts, request, alive):
+def request_kernel(views, slots, groups, partners, request, alive):
     for g in range(groups):
         request[g] = 0
         for u in range(views):
             alive[g * views + u] = 0
     for u in range(views):
         for j in range(slots):
-
-            @pl.when(j < counts[0, u])
+            partner = partners[0, u, j]
+
+            @pl.when(partner >= 0)
             def _():
-                partner = partners[0, u, j]
                 group = lax.div(partner, jnp.int32(views))
                 request[group] = lax.rem(partner, jnp.int32(views))
                 alive[group * views + u] = 1
@@ -107,14 +108,47 @@
     out_grad[...] = dot_nt(upstream[...], w_out[half, :]).astype(jnp.bfloat16)
 
 
-def attention_kernel(views, groups, scalars, alive, *refs):
+def stacked(x, views):
+    tokens, pair = x.shape
+    low = (lax.broadcasted_iota(jnp.int32, (1, 1, pair), 2) < pair // 2).astype(x.dtype)
+    x = x.reshape(views, tokens // views, pair)
+    return jnp.concatenate((x * low, x * (1 - low)), axis=1).reshape(2 * tokens, pair)
+
+
+def unstacked(x, views):
+    rows, pair = x.shape
+    low = lax.broadcasted_iota(jnp.int32, (1, 1, pair), 2) < pair // 2
+    x = x.reshape(views, 2, rows // (2 * views), pair)
+    return jnp.where(low, x[:, 0], x[:, 1]).reshape(rows // 2, pair)
+
+
+def view_parts(x, views, axis):
+    size = x.shape[axis] // views
+    return [lax.slice_in_dim(x, u * size, (u + 1) * size, axis=axis) for u in range(views)]
+
+
+def own_nt(a, b, views):
+    pairs = zip(view_parts(a, views, 0), view_parts(b, views, 0))
+    return jnp.concatenate([dot_nt(x, y) for x, y in pairs], axis=1)
+
+
+def own_tn(a, b, views):
+    pairs = zip(view_parts(a, views, 1), view_parts(b, views, 0))
+    return jnp.concatenate([dot_tn(x, y) for x, y in pairs], axis=0)
+
+
+def own_nn(a, b, views):
+    pairs = zip(view_parts(a, views, 1), view_parts(b, views, 0))
+    return jnp.concatenate([dot_nn(x, y) for x, y in pairs], axis=0)
+
+
+def forward_kernel(views, groups, scalars, alive, *refs):
     got_own, got_other, refs = refs[: groups - 1], refs[groups - 1 : 2 * groups - 2], refs[2 * groups - 2 :]
     queries, keys, values, out_grad, gain, w_key, w_value, *refs = refs
-    normed_far, mixed, dquery, dkey, dvalue = refs
+    normed_far, keys_far, values_far, attention_own, attention_far, mixed, dvalue = refs
     strip = got_own[0].shape[0]
-    tokens = queries.shape[0]
+    tokens, part = queries.shape
     view_tokens = tokens // views
-    scale = HEAD_DIM ** (-0.5)
     here = scalars[1]
     scale_row = gain[...].reshape(1, normed_far.shape[1])
     pair = 2 * HEAD_DIM
@@ -130,59 +164,15 @@
         for u in range(views):
             taken = jnp.where(column_view == u, alive[group * views + u], taken)
         slot_alive.append(taken > 0)
-    low = lax.broadcasted_iota(jnp.int32, (1, 1, pair), 2) < HEAD_DIM
-    low_b = low.astype(jnp.bfloat16)
-    high_b = 1 - low_b
-
-    def stacked(x):
-        x = x.reshape(views, view_tokens, pair)
-        return jnp.concatenate((x * low_b, x * high_b), axis=1).reshape(views * span, pair)
-
-    def unstacked(x):
-        x = x.reshape(views, 2, view_tokens, pair)
-        return jnp.where(low, x[:, 0], x[:, 1]).reshape(tokens, pair)
-
-    def own_nt(a, b):
-        return jnp.concatenate(
-            [
-                dot_nt(a[u * view_tokens : (u + 1) * view_tokens], b[u * span : (u + 1) * span])
-                for u in range(views)
-            ],
-            axis=1,
-        )
-
-    def own_tn(a, b):
-        return jnp.concatenate(
-            [
-                dot_tn(a[:, u * span : (u + 1) * span], b[u * view_tokens : (u + 1) * view_tokens])
-                for u in range(views)
-            ],
-            axis=0,
-        )
-
-    def own_nn(a, b):
-        return jnp.concatenate(
-            [
-                dot_nn(a[:, u * span : (u + 1) * span], b[u * span : (u + 1) * span])
-                for u in range(views)
-            ],
-            axis=0,
-        )
-
-    own = []
-    for p in range(queries.shape[1] // pair):
+    fetched = normed_far[...]
+    half = core_half(scalars, part)
+    keys_far[...] = dot_nn(fetched, w_key[:, half]).astype(jnp.bfloat16)
+    values_far[...] = dot_nn(fetched, w_value[:, half]).astype(jnp.bfloat16)
+    for p in range(part // pair):
         lanes = slice(p * pair, (p + 1) * pair)
-        q, g = stacked(queries[:, lanes]), stacked(out_grad[:, lanes])
-        k_own, v_own = keys[:, lanes], values[:, lanes]
-        own.append((q, g, k_own, v_own, own_nt(k_own, q) * scale, own_nt(v_own, g)))
-    fetched = normed_far[...]
-    half = core_half(scalars, queries.shape[1])
-    fetched_keys = dot_nn(fetched, w_key[:, half]).astype(jnp.bfloat16)
-    fetched_values = dot_nn(fetched, w_value[:, half]).astype(jnp.bfloat16)
-    for p, (q, g, k_own, v_own, s_own, dp_own) in enumerate(own):
-        lanes = slice(p * pair, (p + 1) * pair)
-        k_far, v_far = fetched_keys[:, lanes], fetched_values[:, lanes]
-        s_far = dot_nt(k_far, q) * scale
+        q, g = stacked(queries[:, lanes], views), stacked(out_grad[:, lanes], views)
+        s_own = own_nt(keys[:, lanes], q, views) * SCALE
+        s_far = dot_nt(keys_far[:, lanes], q) * SCALE
         s_far = jnp.concatenate(
             [
                 jnp.where(slot_alive[j], s_far[j * view_tokens : (j + 1) * view_tokens], MASKED)
@@ -190,27 +180,36 @@
             ],
             axis=0,
         )
-        highest = jnp.maximum(
-            jnp.max(s_own, 0, keepdims=True), jnp.max(s_far, 0, keepdims=True)
-        )
+        highest = jnp.maximum(jnp.max(s_own, 0, keepdims=True), jnp.max(s_far, 0, keepdims=True))
         e_own = jnp.exp(s_own - highest)
         e_far = jnp.exp(s_far - highest)
         inverse = 1.0 / (jnp.sum(e_own, 0, keepdims=True) + jnp.sum(e_far, 0, keepdims=True))
-        a_own = e_own * inverse
-        a_far = e_far * inverse
-        ab_own = a_own.astype(jnp.bfloat16)
-        ab_far = a_far.astype(jnp.bfloat16)
-        mix = unstacked(own_tn(ab_own, v_own) + dot_tn(ab_far, v_far))
-        mixed[:, lanes] = mix.astype(jnp.bfloat16)
-        dvalue[:tokens, lanes] = own_nn(ab_own, g).astype(jnp.bfloat16)
-        dvalue[tokens:, lanes] = dot_nn(ab_far, g).astype(jnp.bfloat16)
-        dp_far = dot_nt(v_far, g)
+        a_own, a_far = e_own * inverse, e_far * inverse
+        attention_own[p], attention_far[p] = a_own, a_far
+        a_own, a_far = a_own.astype(jnp.bfloat16), a_far.astype(jnp.bfloat16)
+        mix = own_tn(a_own, values[:, lanes], views) + dot_tn(a_far, values_far[:, lanes])
+        mixed[:, lanes] = unstacked(mix, views).astype(jnp.bfloat16)
+        dvalue[:tokens, lanes] = own_nn(a_own, g, views).astype(jnp.bfloat16)
+        dvalue[tokens:, lanes] = dot_nn(a_far, g).astype(jnp.bfloat16)
+
+
+def backward_kernel(
+    views, queries, keys, values, out_grad, keys_far, values_far, attention_own, attention_far, dquery, dkey
+):
+    tokens, part = queries.shape
+    pair = 2 * HEAD_DIM
+    for p in range(part // pair):
+        lanes = slice(p * pair, (p + 1) * pair)
+        q, g = stacked(queries[:, lanes], views), stacked(out_grad[:, lanes], views)
+        a_own, a_far = attention_own[p], attention_far[p]
+        dp_own = own_nt(values[:, lanes], g, views)
+        dp_far = dot_nt(values_far[:, lanes], g)
         delta = jnp.sum(a_own * dp_own, 0, keepdims=True) + jnp.sum(a_far * dp_far, 0, keepdims=True)
-        ds_own = (a_own * (dp_own - delta) * scale).astype(jnp.bfloat16)
-        ds_far = (a_far * (dp_far - delta) * scale).astype(jnp.bfloat16)
-        dq = unstacked(own_tn(ds_own, k_own) + dot_tn(ds_far, k_far))
-        dquery[:, lanes] = dq.astype(jnp.bfloat16)
-        dkey[:tokens, lanes] = own_nn(ds_own, q).astype(jnp.bfloat16)
+        ds_own = (a_own * (dp_own - delta) * SCALE).astype(jnp.bfloat16)
+        ds_far = (a_far * (dp_far - delta) * SCALE).astype(jnp.bfloat16)
+        dq = own_tn(ds_own, keys[:, lanes], views) + dot_tn(ds_far, keys_far[:, lanes])
+        dquery[:, lanes] = unstacked(dq, views).astype(jnp.bfloat16)
+        dkey[:tokens, lanes] = own_nn(ds_own, q, views).astype(jnp.bfloat16)
         dkey[tokens:, lanes] = dot_nn(ds_far, q).astype(jnp.bfloat16)
 
 
@@ -375,13 +374,13 @@
 
     request, alive = pl.pallas_call(
         functools.partial(request_kernel, views, slots, groups),
-        in_specs=[SMEM, SMEM],
+        in_specs=[SMEM],
         out_specs=(SMEM, SMEM),
         out_shape=(shape((groups,), i32), shape((groups * views,), i32)),
         cost_estimate=MUCH,
         compiler_params=params(4),
         name="requests",
-    )(partners, counts)
+    )(partners)
     between = [[(i, i ^ d) for i in range(groups)] for d in range(1, groups)]
     granted = [lax.ppermute(request, "view", pairs) for pairs in between]
 
@@ -420,23 +419,6 @@
     got_own, normed = lax.optimization_barrier((got_own, normed))
     got_other = [lax.ppermute(got, "row", swap) for got in got_own]
 
-    normed_far, mixed, dquery, dkey, dvalue = pl.pallas_call(
-        functools.partial(attention_kernel, views, groups),
-        in_specs=[SMEM] * 2 + [VMEM] * (2 * groups - 2 + 7),
-        out_specs=[VMEM] * 5,
-        out_shape=[
-            shape((key_tokens - tokens, width), bf16),
-            shape((tokens, part), bf16),
-            shape((tokens, part), bf16),
-            shape((key_tokens, part), bf16),
-            shape((key_tokens, part), bf16),
-        ],
-        compiler_params=params(28 + groups),
-        cost_estimate=LITTLE,
-        name="attention",
-    )(
-        scalars, alive, *got_own, *got_other, queries, keys, values, out_grad, norm_gain, w_key, w_value
-    )
     def call(kernel_body, results, operands, name, first=VMEM, mebibytes=16, cost=LITTLE):
         outputs = pl.pallas_call(
             kernel_body,
@@ -449,6 +431,35 @@
         )(*operands)
         return list(outputs)
 
+    far_tokens, head_pairs = key_tokens - tokens, part // (2 * HEAD_DIM)
+    normed_far, keys_far, values_far, attention_own, attention_far, mixed, dvalue = pl.pallas_call(
+        functools.partial(forward_kernel, views, groups),
+        in_specs=[SMEM] * 2 + [VMEM] * (2 * groups - 2 + 7),
+        out_specs=[VMEM] * 7,
+        out_shape=[
+            shape((far_tokens, width), bf16),
+            shape((far_tokens, part), bf16),
+            shape((far_tokens, part), bf16),
+            shape((head_pairs, 2 * strip, 2 * tokens), f32),
+            shape((head_pairs, far_tokens, 2 * tokens), f32),
+            shape((tokens, part), bf16),
+            shape((key_tokens, part), bf16),
+        ],
+        compiler_params=params(28 + groups // 2),
+        cost_estimate=LITTLE,
+        name="attention_forward",
+    )(
+        scalars, alive, *got_own, *got_other, queries, keys, values, out_grad, norm_gain, w_key, w_value
+    )
+    mixed_other = lax.ppermute(mixed, "row", swap)
+    dquery, dkey = call(
+        functools.partial(backward_kernel, views),
+        [shape((tokens, part), bf16), shape((key_tokens, part), bf16)],
+        (queries, keys, values, out_grad, keys_far, values_far, attention_own, attention_far),
+        "attention_backward",
+        mebibytes=28 + groups // 2,
+    )
+
     def after(value, *earlier):
         return lax.optimization_barrier((value, *earlier))[0]
 
@@ -471,25 +482,22 @@
     def across_views(packed):
         return lax.all_to_all(packed, ("view", "row"), split_axis=0, concat_axis=0, tiled=True)
 
-    mixed_other = lax.ppermute(mixed, "row", swap)
-
-    results = [shape((2, *q_block), bf16)] * 2 + [shape((2, *q_block), f32)] * 2
-    qk_parts = call(
-        query_key_kernel, results, (scalars, normed, normed_far, dquery, dkey), "grad_query_key", SMEM, 24
-    )
-    qk_got = first_exchange(qk_parts)
     pairs = groups // 2
     tile = (2 * o_rows, width)
     send, keep = call(
         value_out_kernel,
         [shape((2, 2, pairs, *tile), kind) for kind in (bf16, f32)],
-        (scalars, normed, normed_far, after(dvalue, qk_parts[0]), mixed, mixed_other, upstream),
+        (scalars, normed, normed_far, after(dvalue, dkey), mixed, mixed_other, upstream),
         "grad_value_out",
         SMEM,
         24,
     )
     got = lax.ppermute(send, "view", [(i, i ^ 1) for i in range(groups)])
-    qk_parts[2] = after(qk_parts[2], send)
+    results = [shape((2, *q_block), bf16)] * 2 + [shape((2, *q_block), f32)] * 2
+    qk_parts = call(
+        query_key_kernel, results, (scalars, normed, normed_far, after(dquery, send), dkey), "grad_query_key", SMEM, 24
+    )
+    qk_got = first_exchange(qk_parts)
     qk_sums = first_sum(qk_parts, qk_got, "first_sum_query_key")
     qk_got = second_exchange(qk_sums)
     packed = call(
@@ -498,8 +506,15 @@
         (qk_sums[2], qk_got[0], qk_sums[3], qk_got[1]),
         "second_sum_query_key",
     )[0]
-    keep = after(keep, packed)
-    packed = across_views(packed.reshape(targets, q_rows, 2 * part))
+    part_shape = (2, pairs, 2 * o_rows, width // 2)
+    vo_parts = call(
+        view_sum_kernel,
+        [shape(part_shape, bf16)] * 2 + [shape(part_shape, f32)] * 2,
+        (keep, after(got, packed)),
+        "view_sum_value_out",
+    )
+    vo_got = first_exchange(vo_parts)
+    packed = across_views(after(packed, vo_parts[0]).reshape(targets, q_rows, 2 * part))
     grad_query, grad_key = call(
         functools.partial(last_query_key_kernel, rows),
         [shape((q_rows, inner), f32)] * 2,
@@ -507,16 +522,7 @@
         "last_sum_query_key",
     )
 
-    part_shape = (2, pairs, 2 * o_rows, width // 2)
-    vo_parts = call(
-        view_sum_kernel,
-        [shape(part_shape, bf16)] * 2 + [shape(part_shape, f32)] * 2,
-        (keep, got),
-        "view_sum_value_out",
-        cost=MUCH,
-    )
-    vo_got = first_exchange(vo_parts)
-    vo_sums = first_sum(vo_parts, vo_got, "first_sum_value_out")
+    vo_sums = first_sum(vo_parts, vo_got, "first_sum_value_out", MUCH)
     v_got, o_got = second_exchange(vo_sums)
     addends = (vo_sums[3], o_got, vo_sums[2], v_got)
     for bit in reversed(range(1, pairs.bit_length() - 1)):

time: 97.6 us -> 91.6 us (0.939)
  local copies, waits for them, and re-layouts: 3.2 us -> 0.89 us
  starting transfers between devices: 30 us -> 28.5 us
  waiting for transfers between devices: 43.6 us -> 42.4 us
  Pallas kernels: 19.8 us -> 18.8 us
    ppermute x2, waiting for transfers between devices: 13.5 us -> 2.92 us  [first_exchange(): lax.ppermute(sends[1], 'scene', along_y)]
    all_to_all x1, waiting for transfers between devices: 0.01 us -> 7.48 us  [across_views(): lax.all_to_all(packed, ('view', 'row'), split_axis=0, concat_axis=0, tile...]
    ppermute x2, waiting for transfers between devices: 7.71 us -> 13 us  [first_exchange(): lax.ppermute(sends[0], 'scene', along_x)]
    ppermute x1, waiting for transfers between devices: 3.96 us -> 0.82 us  [shards(): lax.ppermute(far_same, 'view', [(i, i ^ 2) for i in range(groups)])]
    unnamed x23 -> x17, local copies, waits for them, and re-layouts: 3.12 us -> 0.8 us
    ppermute x1, waiting for transfers between devices: 2.52 us -> 0.63 us  [shards(): lax.ppermute(far_cross, ('view', 'row'), [(i, i ^ 5) for i in range(targe...]
    pallas_call x1, Pallas kernels: 4.87 us -> 3.42 us  [shards(): pl.pallas_call(functools.partial(forward_kernel, views, groups), in_specs...]
    pallas_call x9 -> x10, Pallas kernels: 9.38 us -> 9.91 us  [call(): pl.pallas_call(kernel_body, in_specs=[first] + [VMEM] * (len(operands) -...]
  transfers between devices with their start and end apart: 25 -> 25, of which waited for: 16 -> 17; matrix products, arithmetic and copies ran while one was open for 0% -> 0% of each run, Pallas kernels for 11% -> 12%
where the time goes in v9:
time: 91.6 us; the launch traced here: 91.4 us
  waiting for transfers between devices  42.4 us (46%)
  starting transfers between devices  28.5 us (31%)
  Pallas kernels  18.8 us (21%)
    ppermute x2, waiting for transfers between devices, first_exchange(): lax.ppermute(sends[0], 'scene', along_x)  13 us
    pallas_call x10, Pallas kernels, call(): pl.pallas_call(kernel_body, in_specs=[first] + [VMEM] * (len(operands) -...  9.91 us
    all_to_all x1, waiting for transfers between devices, across_views(): lax.all_to_all(packed, ('view', 'row'), split_axis=0, concat_axis=0, tile...  7.48 us
    ppermute x2, waiting for transfers between devices, second_exchange(): lax.ppermute(sums[0], 'scene', along_y)  7.28 us
    ppermute x3, starting transfers between devices, shards(): granted = [lax.ppermute(request, 'view', pairs) for pairs in between]  5.76 us
    ppermute x3, starting transfers between devices, shards(): lax.ppermute(part_out, 'view', pairs)  4.44 us
    ppermute x2, waiting for transfers between devices, second_exchange(): lax.ppermute(sums[1], 'scene', along_x)  4.39 us
    all_to_all x1, starting transfers between devices, across_views(): lax.all_to_all(packed, ('view', 'row'), split_axis=0, concat_axis=0, tile...  3.92 us
  transfers between devices with their start and end apart: 25, of which 17 were waited for; matrix products, arithmetic and copies ran while one was open for 0% of the time, Pallas kernels for 12%

profile of v9, /device:TPU:0, one launch (start us, length us, event | category | flops | bytes accessed | tf_op | source)
XLA Modules:
  0.0 91.4 jit_solution(3480234974066324335)
XLA Ops:
  0.6 0.8 copy.13.partners
  1.4 1.2 %requests.1 = (s32[4]{0:T(128)S(1)}, s32[16]{0:T(128)S(1)}) custom-call(s32[1,4,3]{2,1,0:T(4,128)S(1)} %copy.13.partners), custom_call_target="tpu_custom_call" | custom-call | flops 40000000000 | bytes 1 | tf_op jit(solution)/shard_map/requests/pallas_call | solution.py:375
  2.6 5.1 %collective-permute-start.2 = (s32[4]{0:T(128)S(1)}, s32[4]{0:T(128)S(1)}, u32[]{:S(2)}, u32[]{:S(2)}) collective-permute-start(s32[4]{0:T(128)S(1)} %get-tuple-element.59), channel_id=1, source_target_pairs={{0,6},{2,4},{4,2},{6,0},{1,7},{3,5},{5,3},{7,1},{8,14},{10,12},{12... | collective-permute-start | bytes 56 | tf_op jit(solution)/shard_map/ppermute | solution.py:385
  7.7 0.0 collective-permute-start.1
  7.7 0.6 collective-permute-start
  8.4 0.0 collective-permute-start.6
  8.4 0.5 collective-permute-start.7
  8.9 0.1 stack.23.scalars
  9.0 0.0 copy-start.6
  9.0 0.0 copy-start.7
  9.0 0.2 collective-permute-done.2.refs_2_
  9.3 2.9 %collective-permute-done.1.refs_1_ = s32[4]{0:T(128)S(1)} collective-permute-done((s32[4]{0:T(128)S(1)}, s32[4]{0:T(128)S(1)}, u32[]{:S(2)}, u32[]{:S(2)}) %collective-permute-start.1) | collective-permute-done | bytes 48 | tf_op jit(solution)/shard_map/ppermute | solution.py:385
  12.2 0.0 collective-permute-done.refs_0_
  12.2 0.6 pick.1
  12.8 0.1 collective-permute-start.3
  12.9 2.1 %collective-permute-start.4 = (bf16[32,1536]{1,0:T(8,128)(2,1)S(1)}, bf16[32,1536]{1,0:T(8,128)(2,1)S(1)}, u32[]{:S(2)}, u32[]{:S(2)}) collective-permute-start(bf16[32,1536]{1,0:T(8,128)(2,1)S(1)} %get-tuple-element.61), channel_id=1, source_target_pairs={{0,4},{2,6},{4,0},{6,2},{1,5},{3,7},{5,1},{7,3},{8,12},{10,14},{12... | collective-permute-start | bytes 294920 | tf_op jit(solution)/shard_map/ppermute | solution.py:401
  15.0 2.3 %collective-permute-start.5 = (bf16[32,1536]{1,0:T(8,128)(2,1)S(1)}, bf16[32,1536]{1,0:T(8,128)(2,1)S(1)}, u32[]{:S(2)}, u32[]{:S(2)}) collective-permute-start(bf16[32,1536]{1,0:T(8,128)(2,1)S(1)} %get-tuple-element.62), channel_id=1, source_target_pairs={{0,6},{2,4},{4,2},{6,0},{1,7},{3,5},{5,3},{7,1},{8,14},{10,12},{12... | collective-permute-start | bytes 294920 | tf_op jit(solution)/shard_map/ppermute | solution.py:401
  17.2 0.0 collective-permute-done.6.lat_other
  17.3 3.7 %project.1 = (bf16[256,1536]{1,0:T(8,128)(2,1)S(1)}, bf16[256,384]{1,0:T(8,128)(2,1)S(1)}, bf16[256,384]{1,0:T(8,128)(2,1)S(1)}, bf16[256,384]{1,0:T(8,128)(2,1)...) custom-call(s32[5]{0:T(128)S(1)} %stack.23.scalars, bf16[4,32,1536]{2,1,0:T(8,128)(2,1)S(1)} %bitcast.10, ...), custom_call_target="tpu_custom_call" | custom-call | flops 1 | bytes 1 | tf_op jit(solution)/shard_map/project/pallas_call | solution.py:402
  21.0 1.4 %collective-permute-done.4.refs_1_ = bf16[32,1536]{1,0:T(8,128)(2,1)S(1)} collective-permute-done((bf16[32,1536]{1,0:T(8,128)(2,1)S(1)}, bf16[32,1536]{1,0:T(8,128)(2,1)S(1)}, u32[]{:S(2)}, u32[]{:S(2)}) %collective-permute-start.4) | collective-permute-done | bytes 98336 | tf_op jit(solution)/shard_map/ppermute | solution.py:401
  22.4 0.0 collective-permute-done.5.refs_2_
  22.4 0.0 collective-permute-start.8
  22.4 0.5 collective-permute-start.9
  22.9 0.0 collective-permute-start.10
  22.9 0.8 collective-permute-done.8.refs_3_
  23.7 0.2 collective-permute-done.9.refs_4_
  23.9 0.4 collective-permute-done.10.refs_5_
  24.2 3.4 %attention_forward.1 = (bf16[192,1536]{1,0:T(8,128)(2,1)S(1)}, bf16[192,384]{1,0:T(8,128)(2,1)S(1)}, bf16[192,384]{1,0:T(8,128)(2,1)S(1)}, f32[3,64,512]{2,1,0:T...) custom-call(s32[5]{0:T(128)S(1)} %stack.23.scalars, ...), custom_call_target="tpu_custom_call" | custom-call | flops 1 | bytes 1 | tf_op jit(solution)/shard_map/attention_forward/pallas_call | solution.py:435
  27.6 0.2 collective-permute-start.11
  27.9 1.8 %attention_backward.1 = (bf16[256,384]{1,0:T(8,128)(2,1)S(1)}, bf16[448,384]{1,0:T(8,128)(2,1)S(1)}) custom-call(bf16[256,384]{1,0:T(8,128)(2,1)S(1)} %get-tuple-element.69.refs_6_.queries, bf16[256,384]{1,0:T(8,128)(2,1)S(1)} %get-tuple-element.70.refs_7_.keys, bf16[256,384]{1,0:T(8,128)(2,1)S(1)} %get-tuple-element.71.refs_8_.values, ...), custom_call_target="tpu_custom_call" | custom-call | flops 1 | bytes 1 | tf_op jit(solution)/shard_map/attention_backward/pallas_call | solution.py:423
  29.7 0.0 collective-permute-done.11.theirs
  29.7 2.0 %grad_value_out.1 = (bf16[2,2,2,48,1536]{4,3,2,1,0:T(8,128)(2,1)S(1)}, f32[2,2,2,48,1536]{4,3,2,1,0:T(8,128)S(1)}) custom-call(s32[5]{0:T(128)S(1)} %stack.23.scalars, bf16[256,1536]{1,0:T(8,128)(2,1)S(1)} %get-tuple-element.64.normed, bf16[192,1536]{1,0:T(8,128)(2,1)S(1)} %get-tuple-element.73.normed_far, bf16[448,384]{1,0:T(8,128)(2,1)S(1)} %get-tuple-element.81.dvalue, ...), custom_call_target="tpu_custom_call" | custom-call | flops 1 | bytes 1 | tf_op jit(solution)/shard_map/grad_value_out/pallas_call | solution.py:423
  31.7 1.7 %collective-permute-start.16 = (bf16[2,2,2,48,1536]{4,3,2,1,0:T(8,128)(2,1)S(1)}, bf16[2,2,2,48,1536]{4,3,2,1,0:T(8,128)(2,1)S(1)}, u32[]{:S(2)}, u32[]{:S(2)}) collective-permute-start(bf16[2,2,2,48,1536]{4,3,2,1,0:T(8,128)(2,1)S(1)} %get-tuple-element.84), channel_id=1, source_target_pairs={{0,2},{2,0},{4,6},{6,4},{1,3},{3,1},{5,7},{7,5},{8,10},{10,8},{12,... | collective-permute-start | bytes 3538952 | tf_op jit(solution)/shard_map/ppermute | solution.py:495
  33.4 2.0 %grad_query_key.1 = (bf16[2,384,384]{2,1,0:T(8,128)(2,1)S(1)}, bf16[2,384,384]{2,1,0:T(8,128)(2,1)S(1)}, f32[2,384,384]{2,1,0:T(8,128)S(1)}, f32[2,384,384]{2,1,0:T(8,128)S(1)}) custom-call(s32[5]{0:T(128)S(1)} %stack.23.scalars, bf16[256,1536]{1,0:T(8,128)(2,1)S(1)} %get-tuple-element.64.normed, bf16[192,1536]{1,0:T(8,128)(2,1)S(1)} %get-tuple-element.73.normed_far, ...), custom_call_target="tpu_custom_call" | custom-call | flops 1 | bytes 1 | tf_op jit(solution)/shard_map/grad_query_key/pallas_call | solution.py:423
  35.4 1.6 %collective-permute-start.12 = (bf16[2,384,384]{2,1,0:T(8,128)(2,1)S(1)}, bf16[2,384,384]{2,1,0:T(8,128)(2,1)S(1)}, u32[]{:S(2)}, u32[]{:S(2)}) collective-permute-start(bf16[2,384,384]{2,1,0:T(8,128)(2,1)S(1)} %get-tuple-element.87), channel_id=1, source_target_pairs={{0,8},{8,0},{16,24},{24,16},{1,9},{9,1},{17,25},{25,17},{2,10},{10... | collective-permute-start | bytes 1769480 | tf_op jit(solution)/shard_map/ppermute | solution.py:472
  36.9 1.5 %collective-permute-start.13 = (bf16[2,384,384]{2,1,0:T(8,128)(2,1)S(1)}, bf16[2,384,384]{2,1,0:T(8,128)(2,1)S(1)}, u32[]{:S(2)}, u32[]{:S(2)}) collective-permute-start(bf16[2,384,384]{2,1,0:T(8,128)(2,1)S(1)} %get-tuple-element.89), channel_id=1, source_target_pairs={{0,16},{8,24},{16,0},{24,8},{1,17},{9,25},{17,1},{25,9},{2,18},{10... | collective-permute-start | bytes 1769480 | tf_op jit(solution)/shard_map/ppermute | solution.py:472
  38.5 12.3 %collective-permute-done.12.x_got = bf16[2,384,384]{2,1,0:T(8,128)(2,1)S(1)} collective-permute-done((bf16[2,384,384]{2,1,0:T(8,128)(2,1)S(1)}, bf16[2,384,384]{2,1,0:T(8,128)(2,1)S(1)}, u32[]{:S(2)}, u32[]{:S(2)}) %collective-permute-start.12) | collective-permute-done | bytes 589856 | tf_op jit(solution)/shard_map/ppermute | solution.py:472
  50.7 1.2 %collective-permute-done.13.y_got = bf16[2,384,384]{2,1,0:T(8,128)(2,1)S(1)} collective-permute-done((bf16[2,384,384]{2,1,0:T(8,128)(2,1)S(1)}, bf16[2,384,384]{2,1,0:T(8,128)(2,1)S(1)}, u32[]{:S(2)}, u32[]{:S(2)}) %collective-permute-start.13) | collective-permute-done | bytes 589856 | tf_op jit(solution)/shard_map/ppermute | solution.py:472
  52.0 0.2 first_sum_query_key.1
  52.2 1.6 %collective-permute-start.14 = (bf16[384,384]{1,0:T(8,128)(2,1)S(1)}, bf16[384,384]{1,0:T(8,128)(2,1)S(1)}, u32[]{:S(2)}, u32[]{:S(2)}) collective-permute-start(bf16[384,384]{1,0:T(8,128)(2,1)S(1)} %get-tuple-element.91), channel_id=1, source_target_pairs={{0,16},{8,24},{16,0},{24,8},{1,17},{9,25},{17,1},{25,9},{2,18},{10... | collective-permute-start | bytes 884744 | tf_op jit(solution)/shard_map/ppermute | solution.py:480
  53.8 0.5 collective-permute-start.15
  54.3 5.8 %collective-permute-done.14.q_got = bf16[384,384]{1,0:T(8,128)(2,1)S(1)} collective-permute-done((bf16[384,384]{1,0:T(8,128)(2,1)S(1)}, bf16[384,384]{1,0:T(8,128)(2,1)S(1)}, u32[]{:S(2)}, u32[]{:S(2)}) %collective-permute-start.14) | collective-permute-done | bytes 294944 | tf_op jit(solution)/shard_map/ppermute | solution.py:480
  60.1 1.2 %collective-permute-done.15.k_got = bf16[384,384]{1,0:T(8,128)(2,1)S(1)} collective-permute-done((bf16[384,384]{1,0:T(8,128)(2,1)S(1)}, bf16[384,384]{1,0:T(8,128)(2,1)S(1)}, u32[]{:S(2)}, u32[]{:S(2)}) %collective-permute-start.15) | collective-permute-done | bytes 294944 | tf_op jit(solution)/shard_map/ppermute | solution.py:480
  61.3 0.9 %second_sum_query_key.1 = bf16[384,768]{1,0:T(8,128)(2,1)} custom-call(f32[384,384]{1,0:T(8,128)S(1)} %get-tuple-element.90.q_now, bf16[384,384]{1,0:T(8,128)(2,1)S(1)} %collective-permute-done.14.q_got, f32[384,384]{1,0:T(8,128)S(1)} %get-tuple-element.92.k_now, bf16[384,384]{1,0:T(8,128)(2,1)S(1)} %collective-permute-done.15.k_got), custom_call_target="tpu_custom_call" | custom-call | flops 1 | bytes 1 | tf_op jit(solution)/shard_map/second_sum_query_key/pallas_call | solution.py:423
  62.3 0.2 view_sum_value_out.1
  62.4 0.6 collective-permute-start.18
  63.0 0.6 collective-permute-start.17
  63.6 3.9 %all-to-all-start = ((bf16[8,48,768]{2,1,0:T(8,128)(2,1)}), bf16[8,48,768]{2,1,0:T(8,128)(2,1)S(1)}, u32[]{:S(2)}, u32[]{:S(2)}) async-start(bf16[8,48,768]{2,1,0:T(8,128)(2,1)} %bitcast.7), calls=%async_computation | async-start | bytes 1179648 | tf_op jit(solution)/shard_map/all_to_all | solution.py:483
  67.5 1.7 %collective-permute-done.18.y_got = bf16[2,2,48,768]{3,2,1,0:T(8,128)(2,1)S(1)} collective-permute-done((bf16[2,2,48,768]{3,2,1,0:T(8,128)(2,1)S(1)}, bf16[2,2,48,768]{3,2,1,0:T(8,128)(2,1)S(1)}, u32[]{:S(2)}, u32[]{:S(2)}) %collective-permute-start.18) | collective-permute-done | bytes 294944 | tf_op jit(solution)/shard_map/ppermute | solution.py:472
  69.2 0.7 collective-permute-done.17.x_got
  69.9 0.1 first_sum_value_out.1
  70.1 1.6 %collective-permute-start.19 = (bf16[2,48,768]{2,1,0:T(8,128)(2,1)S(1)}, bf16[2,48,768]{2,1,0:T(8,128)(2,1)S(1)}, u32[]{:S(2)}, u32[]{:S(2)}) collective-permute-start(bf16[2,48,768]{2,1,0:T(8,128)(2,1)S(1)} %get-tuple-element.104), channel_id=1, source_target_pairs={{0,8},{8,0},{16,24},{24,16},{1,9},{9,1},{17,25},{25,17},{2,10},{10... | collective-permute-start | bytes 442376 | tf_op jit(solution)/shard_map/ppermute | solution.py:480
  71.6 0.5 collective-permute-start.20
  72.1 3.1 %collective-permute-done.19.refs_1_ = bf16[2,48,768]{2,1,0:T(8,128)(2,1)S(1)} collective-permute-done((bf16[2,48,768]{2,1,0:T(8,128)(2,1)S(1)}, bf16[2,48,768]{2,1,0:T(8,128)(2,1)S(1)}, u32[]{:S(2)}, u32[]{:S(2)}) %collective-permute-start.19) | collective-permute-done | bytes 147488 | tf_op jit(solution)/shard_map/ppermute | solution.py:480
  75.3 1.5 %collective-permute-done.20.refs_3_ = bf16[2,48,768]{2,1,0:T(8,128)(2,1)S(1)} collective-permute-done((bf16[2,48,768]{2,1,0:T(8,128)(2,1)S(1)}, bf16[2,48,768]{2,1,0:T(8,128)(2,1)S(1)}, u32[]{:S(2)}, u32[]{:S(2)}) %collective-permute-start.20) | collective-permute-done | bytes 147488 | tf_op jit(solution)/shard_map/ppermute | solution.py:480
  76.8 0.6 last_parts_value_out.1
  77.4 0.1 collective-permute-start.22
  77.5 2.9 %collective-permute-start.21 = (bf16[24,1536]{1,0:T(8,128)(2,1)S(1)}, bf16[24,1536]{1,0:T(8,128)(2,1)S(1)}, u32[]{:S(2)}, u32[]{:S(2)}) collective-permute-start(bf16[24,1536]{1,0:T(8,128)(2,1)S(1)} %get-tuple-element.109), channel_id=1, source_target_pairs={{0,4},{2,6},{4,0},{6,2},{1,5},{3,7},{5,1},{7,3},{8,12},{10,14},{12... | collective-permute-start | bytes 221192 | tf_op jit(solution)/shard_map/ppermute | solution.py:544
  80.4 0.1 collective-permute-start.23
  80.4 7.5 %all-to-all-done.packed = bf16[8,48,768]{2,1,0:T(8,128)(2,1)S(1)} async-done(((bf16[8,48,768]{2,1,0:T(8,128)(2,1)}), bf16[8,48,768]{2,1,0:T(8,128)(2,1)S(1)}, u32[]{:S(2)}, u32[]{:S(2)}) %all-to-all-start) | async-done | bytes 589856 | tf_op jit(solution)/shard_map/all_to_all | solution.py:483
  87.9 0.8 last_sum_query_key.1
  88.7 0.8 collective-permute-done.21.far_same
  89.5 0.6 collective-permute-done.23.far_cross
  90.1 1.3 %last_sum_value_out.1 = (f32[48,768]{1,0:T(8,128)}, f32[24,1536]{1,0:T(8,128)}) custom-call(s32[5]{0:T(128)S(1)} %stack.23.scalars, f32[24,1536]{1,0:T(8,128)S(1)} %get-tuple-element.108.mine, bf16[24,1536]{1,0:T(8,128)(2,1)S(1)} %collective-permute-done.21.far_same, f32[24,1536]{1,0:T(8,128)S(1)} %collective-permute-done.22.near_cross, ...), custom_call_target="tpu_custom_call" | custom-call | flops 1 | bytes 1 | tf_op jit(solution)/shard_map/last_sum_value_out/pallas_call | solution.py:423
  (18 shorter events, 0.0 us)
Async XLA Ops:
  1.4 7.0 %copy-start.4 = (bf16[1,4,1,32,1536]{4,3,2,1,0:T(8,128)(2,1)S(1)}, bf16[1,4,1,32,1536]{4,3,2,1,0:T(8,128)(2,1)}, u32[]{:S(2)}) copy-start(bf16[1,4,1,32,1536]{4,3,2,1,0:T(8,128)(2,1)} %param.10) | copy-start | bytes 1179652
  1.4 7.0 %copy-start.5 = (bf16[1,4,1,32,1536]{4,3,2,1,0:T(8,128)(2,1)S(1)}, bf16[1,4,1,32,1536]{4,3,2,1,0:T(8,128)(2,1)}, u32[]{:S(2)}) copy-start(bf16[1,4,1,32,1536]{4,3,2,1,0:T(8,128)(2,1)} %param.18) | copy-start | bytes 1179652
  2.6 6.6 %collective-permute-start.2 = (s32[4]{0:T(128)S(1)}, s32[4]{0:T(128)S(1)}, u32[]{:S(2)}, u32[]{:S(2)}) collective-permute-start(s32[4]{0:T(128)S(1)} %get-tuple-element.59), channel_id=1, source_target_pairs={{0,6},{2,4},{4,2},{6,0},{1,7},{3,5},{5,3},{7,1},{8,14},{10,12},{12... | collective-permute-start | bytes 56 | tf_op jit(solution)/shard_map/ppermute | solution.py:385
  7.7 4.4 %collective-permute-start.1 = (s32[4]{0:T(128)S(1)}, s32[4]{0:T(128)S(1)}, u32[]{:S(2)}, u32[]{:S(2)}) collective-permute-start(s32[4]{0:T(128)S(1)} %get-tuple-element.59), channel_id=1, source_target_pairs={{0,4},{2,6},{4,0},{6,2},{1,5},{3,7},{5,1},{7,3},{8,12},{10,14},{12... | collective-permute-start | bytes 56 | tf_op jit(solution)/shard_map/ppermute | solution.py:385
  7.7 4.4 %collective-permute-start = (s32[4]{0:T(128)S(1)}, s32[4]{0:T(128)S(1)}, u32[]{:S(2)}, u32[]{:S(2)}) collective-permute-start(s32[4]{0:T(128)S(1)} %get-tuple-element.59), channel_id=1, source_target_pairs={{0,2},{2,0},{4,6},{6,4},{1,3},{3,1},{5,7},{7,5},{8,10},{10,8},{12,... | collective-permute-start | bytes 56 | tf_op jit(solution)/shard_map/ppermute | solution.py:385
  8.4 8.8 %collective-permute-start.6 = (bf16[4,32,1536]{2,1,0:T(8,128)(2,1)S(1)}, bf16[4,32,1536]{2,1,0:T(8,128)(2,1)S(1)}, u32[]{:S(2)}, u32[]{:S(2)}) collective-permute-start(bf16[4,32,1536]{2,1,0:T(8,128)(2,1)S(1)} %bitcast.8), channel_id=1, source_target_pairs={{0,1},{1,0},{2,3},{3,2},{4,5},{5,4},{6,7},{7,6},{8,9},{9,8},{10,11... | collective-permute-start | bytes 1179656 | tf_op jit(solution)/shard_map/ppermute | solution.py:389
  8.4 8.8 %collective-permute-start.7 = (bf16[4,32,1536]{2,1,0:T(8,128)(2,1)S(1)}, bf16[4,32,1536]{2,1,0:T(8,128)(2,1)S(1)}, u32[]{:S(2)}, u32[]{:S(2)}) collective-permute-start(bf16[4,32,1536]{2,1,0:T(8,128)(2,1)S(1)} %bitcast.11), channel_id=1, source_target_pairs={{0,1},{1,0},{2,3},{3,2},{4,5},{5,4},{6,7},{7,6},{8,9},{9,8},{10,11... | collective-permute-start | bytes 1179656 | tf_op jit(solution)/shard_map/ppermute | solution.py:390
  9.0 8.3 %copy-start = (bf16[1536,768]{1,0:T(8,128)(2,1)S(1)}, bf16[1536,768]{1,0:T(8,128)(2,1)}, u32[]{:S(2)}) copy-start(bf16[1536,768]{1,0:T(8,128)(2,1)} %refs_11_.1) | copy-start | bytes 7077892
  9.0 8.3 %copy-start.1 = (bf16[1536,768]{1,0:T(8,128)(2,1)S(1)}, bf16[1536,768]{1,0:T(8,128)(2,1)}, u32[]{:S(2)}) copy-start(bf16[1536,768]{1,0:T(8,128)(2,1)} %refs_12_.1) | copy-start | bytes 7077892
  9.0 8.3 %copy-start.2 = (bf16[1536,768]{1,0:T(8,128)(2,1)S(1)}, bf16[1536,768]{1,0:T(8,128)(2,1)}, u32[]{:S(2)}) copy-start(bf16[1536,768]{1,0:T(8,128)(2,1)} %w_query.1) | copy-start | bytes 7077892
  9.0 8.3 %copy-start.3 = (bf16[768,1536]{1,0:T(8,128)(2,1)S(1)}, bf16[768,1536]{1,0:T(8,128)(2,1)}, u32[]{:S(2)}) copy-start(bf16[768,1536]{1,0:T(8,128)(2,1)} %w_out.1) | copy-start | bytes 7077892
  9.0 8.3 %copy-start.6 = (bf16[9,1536]{1,0:T(8,128)(2,1)S(1)}, bf16[9,1536]{1,0:T(8,128)(2,1)}, u32[]{:S(2)}) copy-start(bf16[9,1536]{1,0:T(8,128)(2,1)} %taps.1) | copy-start | bytes 82948
  9.0 8.3 %copy-start.7 = (f32[1536]{0:T(1024)S(1)}, f32[1536]{0:T(1024)}, u32[]{:S(2)}) copy-start(f32[1536]{0:T(1024)} %refs_10_.1) | copy-start | bytes 18436
  12.8 8.2 %collective-permute-start.3 = (bf16[32,1536]{1,0:T(8,128)(2,1)S(1)}, bf16[32,1536]{1,0:T(8,128)(2,1)S(1)}, u32[]{:S(2)}, u32[]{:S(2)}) collective-permute-start(bf16[32,1536]{1,0:T(8,128)(2,1)S(1)} %get-tuple-element.60), channel_id=1, source_target_pairs={{0,2},{2,0},{4,6},{6,4},{1,3},{3,1},{5,7},{7,5},{8,10},{10,8},{12,... | collective-permute-start | bytes 294920 | tf_op jit(solution)/shard_map/ppermute | solution.py:401
  12.9 9.5 %collective-permute-start.4 = (bf16[32,1536]{1,0:T(8,128)(2,1)S(1)}, bf16[32,1536]{1,0:T(8,128)(2,1)S(1)}, u32[]{:S(2)}, u32[]{:S(2)}) collective-permute-start(bf16[32,1536]{1,0:T(8,128)(2,1)S(1)} %get-tuple-element.61), channel_id=1, source_target_pairs={{0,4},{2,6},{4,0},{6,2},{1,5},{3,7},{5,1},{7,3},{8,12},{10,14},{12... | collective-permute-start | bytes 294920 | tf_op jit(solution)/shard_map/ppermute | solution.py:401
  15.0 7.5 %collective-permute-start.5 = (bf16[32,1536]{1,0:T(8,128)(2,1)S(1)}, bf16[32,1536]{1,0:T(8,128)(2,1)S(1)}, u32[]{:S(2)}, u32[]{:S(2)}) collective-permute-start(bf16[32,1536]{1,0:T(8,128)(2,1)S(1)} %get-tuple-element.62), channel_id=1, source_target_pairs={{0,6},{2,4},{4,2},{6,0},{1,7},{3,5},{5,3},{7,1},{8,14},{10,12},{12... | collective-permute-start | bytes 294920 | tf_op jit(solution)/shard_map/ppermute | solution.py:401
  22.4 1.3 %collective-permute-start.8 = (bf16[32,1536]{1,0:T(8,128)(2,1)S(1)}, bf16[32,1536]{1,0:T(8,128)(2,1)S(1)}, u32[]{:S(2)}, u32[]{:S(2)}) collective-permute-start(bf16[32,1536]{1,0:T(8,128)(2,1)S(1)} %collective-permute-done.3.refs_0_), channel_id=1, source_target_pairs={{0,1},{1,0},{2,3},{3,2},{4,5},{5,4},{6,7},{7,6},{8,9},{9,8},{10,11... | collective-permute-start | bytes 294920 | tf_op jit(solution)/shard_map/ppermute | solution.py:420
  22.4 1.5 %collective-permute-start.9 = (bf16[32,1536]{1,0:T(8,128)(2,1)S(1)}, bf16[32,1536]{1,0:T(8,128)(2,1)S(1)}, u32[]{:S(2)}, u32[]{:S(2)}) collective-permute-start(bf16[32,1536]{1,0:T(8,128)(2,1)S(1)} %collective-permute-done.4.refs_1_), channel_id=1, source_target_pairs={{0,1},{1,0},{2,3},{3,2},{4,5},{5,4},{6,7},{7,6},{8,9},{9,8},{10,11... | collective-permute-start | bytes 294920 | tf_op jit(solution)/shard_map/ppermute | solution.py:420
  22.9 1.3 %collective-permute-start.10 = (bf16[32,1536]{1,0:T(8,128)(2,1)S(1)}, bf16[32,1536]{1,0:T(8,128)(2,1)S(1)}, u32[]{:S(2)}, u32[]{:S(2)}) collective-permute-start(bf16[32,1536]{1,0:T(8,128)(2,1)S(1)} %collective-permute-done.5.refs_2_), channel_id=1, source_target_pairs={{0,1},{1,0},{2,3},{3,2},{4,5},{5,4},{6,7},{7,6},{8,9},{9,8},{10,11... | collective-permute-start | bytes 294920 | tf_op jit(solution)/shard_map/ppermute | solution.py:420
  27.6 2.0 %collective-permute-start.11 = (bf16[256,384]{1,0:T(8,128)(2,1)S(1)}, bf16[256,384]{1,0:T(8,128)(2,1)S(1)}, u32[]{:S(2)}, u32[]{:S(2)}) collective-permute-start(bf16[256,384]{1,0:T(8,128)(2,1)S(1)} %get-tuple-element.82.mine), channel_id=1, source_target_pairs={{0,1},{1,0},{2,3},{3,2},{4,5},{5,4},{6,7},{7,6},{8,9},{9,8},{10,11... | collective-permute-start | bytes 589832 | tf_op jit(solution)/shard_map/ppermute | solution.py:454
  31.7 30.5 %collective-permute-start.16 = (bf16[2,2,2,48,1536]{4,3,2,1,0:T(8,128)(2,1)S(1)}, bf16[2,2,2,48,1536]{4,3,2,1,0:T(8,128)(2,1)S(1)}, u32[]{:S(2)}, u32[]{:S(2)}) collective-permute-start(bf16[2,2,2,48,1536]{4,3,2,1,0:T(8,128)(2,1)S(1)} %get-tuple-element.84), channel_id=1, source_target_pairs={{0,2},{2,0},{4,6},{6,4},{1,3},{3,1},{5,7},{7,5},{8,10},{10,8},{12,... | collective-permute-start | bytes 3538952 | tf_op jit(solution)/shard_map/ppermute | solution.py:495
  35.4 15.4 %collective-permute-start.12 = (bf16[2,384,384]{2,1,0:T(8,128)(2,1)S(1)}, bf16[2,384,384]{2,1,0:T(8,128)(2,1)S(1)}, u32[]{:S(2)}, u32[]{:S(2)}) collective-permute-start(bf16[2,384,384]{2,1,0:T(8,128)(2,1)S(1)} %get-tuple-element.87), channel_id=1, source_target_pairs={{0,8},{8,0},{16,24},{24,16},{1,9},{9,1},{17,25},{25,17},{2,10},{10... | collective-permute-start | bytes 1769480 | tf_op jit(solution)/shard_map/ppermute | solution.py:472
  36.9 15.0 %collective-permute-start.13 = (bf16[2,384,384]{2,1,0:T(8,128)(2,1)S(1)}, bf16[2,384,384]{2,1,0:T(8,128)(2,1)S(1)}, u32[]{:S(2)}, u32[]{:S(2)}) collective-permute-start(bf16[2,384,384]{2,1,0:T(8,128)(2,1)S(1)} %get-tuple-element.89), channel_id=1, source_target_pairs={{0,16},{8,24},{16,0},{24,8},{1,17},{9,25},{17,1},{25,9},{2,18},{10... | collective-permute-start | bytes 1769480 | tf_op jit(solution)/shard_map/ppermute | solution.py:472
  52.2 7.9 %collective-permute-start.14 = (bf16[384,384]{1,0:T(8,128)(2,1)S(1)}, bf16[384,384]{1,0:T(8,128)(2,1)S(1)}, u32[]{:S(2)}, u32[]{:S(2)}) collective-permute-start(bf16[384,384]{1,0:T(8,128)(2,1)S(1)} %get-tuple-element.91), channel_id=1, source_target_pairs={{0,16},{8,24},{16,0},{24,8},{1,17},{9,25},{17,1},{25,9},{2,18},{10... | collective-permute-start | bytes 884744 | tf_op jit(solution)/shard_map/ppermute | solution.py:480
  53.8 7.6 %collective-permute-start.15 = (bf16[384,384]{1,0:T(8,128)(2,1)S(1)}, bf16[384,384]{1,0:T(8,128)(2,1)S(1)}, u32[]{:S(2)}, u32[]{:S(2)}) collective-permute-start(bf16[384,384]{1,0:T(8,128)(2,1)S(1)} %get-tuple-element.93), channel_id=1, source_target_pairs={{0,8},{8,0},{16,24},{24,16},{1,9},{9,1},{17,25},{25,17},{2,10},{10... | collective-permute-start | bytes 884744 | tf_op jit(solution)/shard_map/ppermute | solution.py:480
  62.4 6.8 %collective-permute-start.18 = (bf16[2,2,48,768]{3,2,1,0:T(8,128)(2,1)S(1)}, bf16[2,2,48,768]{3,2,1,0:T(8,128)(2,1)S(1)}, u32[]{:S(2)}, u32[]{:S(2)}) collective-permute-start(bf16[2,2,48,768]{3,2,1,0:T(8,128)(2,1)S(1)} %get-tuple-element.102), channel_id=1, source_target_pairs={{0,16},{8,24},{16,0},{24,8},{1,17},{9,25},{17,1},{25,9},{2,18},{10... | collective-permute-start | bytes 884744 | tf_op jit(solution)/shard_map/ppermute | solution.py:472
  63.0 6.9 %collective-permute-start.17 = (bf16[2,2,48,768]{3,2,1,0:T(8,128)(2,1)S(1)}, bf16[2,2,48,768]{3,2,1,0:T(8,128)(2,1)S(1)}, u32[]{:S(2)}, u32[]{:S(2)}) collective-permute-start(bf16[2,2,48,768]{3,2,1,0:T(8,128)(2,1)S(1)} %get-tuple-element.96), channel_id=1, source_target_pairs={{0,8},{8,0},{16,24},{24,16},{1,9},{9,1},{17,25},{25,17},{2,10},{10... | collective-permute-start | bytes 884744 | tf_op jit(solution)/shard_map/ppermute | solution.py:472
  63.6 24.3 %all-to-all-start = ((bf16[8,48,768]{2,1,0:T(8,128)(2,1)}), bf16[8,48,768]{2,1,0:T(8,128)(2,1)S(1)}, u32[]{:S(2)}, u32[]{:S(2)}) async-start(bf16[8,48,768]{2,1,0:T(8,128)(2,1)} %bitcast.7), calls=%async_computation | async-start | bytes 1179648 | tf_op jit(solution)/shard_map/all_to_all | solution.py:483
  70.1 5.2 %collective-permute-start.19 = (bf16[2,48,768]{2,1,0:T(8,128)(2,1)S(1)}, bf16[2,48,768]{2,1,0:T(8,128)(2,1)S(1)}, u32[]{:S(2)}, u32[]{:S(2)}) collective-permute-start(bf16[2,48,768]{2,1,0:T(8,128)(2,1)S(1)} %get-tuple-element.104), channel_id=1, source_target_pairs={{0,8},{8,0},{16,24},{24,16},{1,9},{9,1},{17,25},{25,17},{2,10},{10... | collective-permute-start | bytes 442376 | tf_op jit(solution)/shard_map/ppermute | solution.py:480
  71.6 5.1 %collective-permute-start.20 = (bf16[2,48,768]{2,1,0:T(8,128)(2,1)S(1)}, bf16[2,48,768]{2,1,0:T(8,128)(2,1)S(1)}, u32[]{:S(2)}, u32[]{:S(2)}) collective-permute-start(bf16[2,48,768]{2,1,0:T(8,128)(2,1)S(1)} %get-tuple-element.106), channel_id=1, source_target_pairs={{0,16},{8,24},{16,0},{24,8},{1,17},{9,25},{17,1},{25,9},{2,18},{10... | collective-permute-start | bytes 442376 | tf_op jit(solution)/shard_map/ppermute | solution.py:480
  77.4 12.7 %collective-permute-start.22 = (f32[24,1536]{1,0:T(8,128)S(1)}, f32[24,1536]{1,0:T(8,128)S(1)}, u32[]{:S(2)}, u32[]{:S(2)}) collective-permute-start(f32[24,1536]{1,0:T(8,128)S(1)} %get-tuple-element.110), channel_id=1, source_target_pairs={{0,1},{1,0},{2,3},{3,2},{4,5},{5,4},{6,7},{7,6},{8,9},{9,8},{10,11... | collective-permute-start | bytes 442376 | tf_op jit(solution)/shard_map/ppermute | solution.py:546
  77.5 12.0 %collective-permute-start.21 = (bf16[24,1536]{1,0:T(8,128)(2,1)S(1)}, bf16[24,1536]{1,0:T(8,128)(2,1)S(1)}, u32[]{:S(2)}, u32[]{:S(2)}) collective-permute-start(bf16[24,1536]{1,0:T(8,128)(2,1)S(1)} %get-tuple-element.109), channel_id=1, source_target_pairs={{0,4},{2,6},{4,0},{6,2},{1,5},{3,7},{5,1},{7,3},{8,12},{10,14},{12... | collective-permute-start | bytes 221192 | tf_op jit(solution)/shard_map/ppermute | solution.py:544
  80.4 9.8 %collective-permute-start.23 = (bf16[24,1536]{1,0:T(8,128)(2,1)S(1)}, bf16[24,1536]{1,0:T(8,128)(2,1)S(1)}, u32[]{:S(2)}, u32[]{:S(2)}) collective-permute-start(bf16[24,1536]{1,0:T(8,128)(2,1)S(1)} %get-tuple-element.111), channel_id=1, source_target_pairs={{0,5},{1,4},{2,7},{3,6},{4,1},{5,0},{6,3},{7,2},{8,13},{9,12},{10,... | collective-permute-start | bytes 221192 | tf_op jit(solution)/shard_map/ppermute | solution.py:545

commit v10 on v9

--- a/solution.py
+++ b/solution.py
@@ -37,26 +37,17 @@
     return (x * lax.rsqrt(mean + EPSILON) * gain).astype(jnp.bfloat16)
 
 
-def request_kernel(views, slots, groups, partners, request, alive):
-    for g in range(groups):
-        request[g] = 0
-        for u in range(views):
-            alive[g * views + u] = 0
-    for u in range(views):
-        for j in range(slots):
-            partner = partners[0, u, j]
-
-            @pl.when(partner >= 0)
-            def _():
-                group = lax.div(partner, jnp.int32(views))
-                request[group] = lax.rem(partner, jnp.int32(views))
-                alive[group * views + u] = 1
-
-
 def pick_kernel(groups, scalars, *refs):
-    requests, lat, outgoing = refs[: groups - 1], refs[groups - 1], refs[groups:]
-    for request, out in zip(requests, outgoing):
-        out[...] = lat[request[scalars[1]]]
+    tables, lat, outgoing = refs[: groups - 1], refs[groups - 1], refs[groups:]
+    views = lat.shape[0]
+    for table, out in zip(tables, outgoing):
+        wanted = jnp.int32(0)
+        for u in range(table.shape[1]):
+            for j in range(table.shape[2]):
+                partner = table[0, u, j]
+                here = (partner >= 0) & (lax.div(partner, jnp.int32(views)) == scalars[1])
+                wanted = jnp.where(here, lax.rem(partner, jnp.int32(views)), wanted)
+        out[...] = lat[wanted]
 
 
 def core_half(scalars, size):
@@ -142,7 +133,7 @@
     return jnp.concatenate([dot_nn(x, y) for x, y in pairs], axis=0)
 
 
-def forward_kernel(views, groups, scalars, alive, *refs):
+def forward_kernel(views, groups, scalars, partners, *refs):
     got_own, got_other, refs = refs[: groups - 1], refs[groups - 1 : 2 * groups - 2], refs[2 * groups - 2 :]
     queries, keys, values, out_grad, gain, w_key, w_value, *refs = refs
     normed_far, keys_far, values_far, attention_own, attention_far, mixed, dvalue = refs
@@ -162,7 +153,12 @@
         normed_far[start + strip : start + 2 * strip, :] = normalized(got_other[j][...], scale_row)
         taken = jnp.zeros((1, views * span), jnp.int32)
         for u in range(views):
-            taken = jnp.where(column_view == u, alive[group * views + u], taken)
+            found = jnp.int32(0)
+            for slot in range(partners.shape[2]):
+                partner = partners[0, u, slot]
+                same = (partner >= 0) & (lax.div(partner, jnp.int32(views)) == group)
+                found = jnp.where(same, 1, found)
+            taken = jnp.where(column_view == u, found, taken)
         slot_alive.append(taken > 0)
     fetched = normed_far[...]
     half = core_half(scalars, part)
@@ -278,10 +274,16 @@
         now[...] = keep[0] + got[0].astype(jnp.float32)
 
 
-def pack_query_key_kernel(q_now, q_got, k_now, k_got, packed):
-    size = q_now.shape[1]
-    packed[:, :size] = (q_now[...] + q_got[...].astype(jnp.float32)).astype(jnp.bfloat16)
-    packed[:, size:] = (k_now[...] + k_got[...].astype(jnp.float32)).astype(jnp.bfloat16)
+def query_key_tiles_kernel(scalars, q_now, q_got, k_now, k_got, send, keep):
+    odd = lax.rem(scalars[1], jnp.int32(2)) == 1
+    total = [now[...] + got[...].astype(jnp.float32) for now, got in ((q_now, q_got), (k_now, k_got))]
+    total = jnp.concatenate(total, axis=1)
+    pairs, size, _ = send.shape
+    for pair in range(pairs):
+        first = total[2 * pair * size : (2 * pair + 1) * size]
+        second = total[(2 * pair + 1) * size : (2 * pair + 2) * size]
+        send[pair] = jnp.where(odd, first, second).astype(send.dtype)
+        keep[pair] = jnp.where(odd, second, first)
 
 
 def summed_tile(addends, place):
@@ -303,47 +305,52 @@
             target[i] = summed_tile(addends, part * count + i).astype(target.dtype)
 
 
-def tile_cores_kernel(scalars, *refs):
+def query_key_cores(tile):
+    size = tile.shape[0] // 2
+    return tile[:size], tile[size:]
+
+
+def value_out_cores(tile):
+    size, width = tile.shape[0] // 2, tile.shape[1]
+    half, quarter = width // 2, width // 4
+    parts = []
+    for core in range(2):
+        value = tile[:, half + core * quarter : half + (core + 1) * quarter]
+        out = tile[core * size : (core + 1) * size, :half]
+        parts.append(jnp.concatenate((out, value[:size], value[size:]), axis=1))
+    return parts
+
+
+def tile_cores_kernel(split, scalars, *refs):
     addends, (far_same, far_cross, near_cross, mine) = refs[:-4], refs[-4:]
+    bit = view_bit(scalars, 0)
+    for place, same, cross in ((1 - bit, far_same, far_cross), (bit, mine, near_cross)):
+        parts = split(summed_tile(addends, place))
+        same[...] = jnp.where(scalars[0] == 0, parts[0], parts[1]).astype(same.dtype)
+        cross[...] = jnp.where(scalars[0] == 0, parts[1], parts[0]).astype(cross.dtype)
+
+
+def last_sums(scalars, mine, far_same, near_cross, far_cross):
+    for near, far, core in ((mine, far_same, scalars[0]), (near_cross, far_cross, 1 - scalars[0])):
+        yield near[...] + far[...].astype(jnp.float32), core
+
+
+def place_query_key_kernel(scalars, mine, far_same, near_cross, far_cross, query, key):
+    size = mine.shape[1] // 2
+    for total, core in last_sums(scalars, mine, far_same, near_cross, far_cross):
+        columns = pl.ds(pl.multiple_of(core * size, size), size)
+        query[:, columns] = total[:, :size]
+        key[:, columns] = total[:, size:]
+
+
+def place_value_out_kernel(scalars, mine, far_same, near_cross, far_cross, value, out):
     size, width = mine.shape
     half, quarter = width // 2, width // 4
-    bit = view_bit(scalars, 0)
-    for place, same, cross in ((1 - bit, far_same, far_cross), (bit, mine, near_cross)):
-        total = summed_tile(addends, place)
-        parts = []
-        for core in range(2):
-            value = total[:, half + core * quarter : half + (core + 1) * quarter]
-            out = total[core * size : (core + 1) * size, :half]
-            parts.append(jnp.concatenate((out, value[:size], value[size:]), axis=1))
-        same[...] = jnp.where(scalars[0] == 0, parts[0], parts[1]).astype(same.dtype)
-        cross[...] = jnp.where(scalars[0] == 0, parts[1], parts[0]).astype(cross.dtype)
-
-
-def place_kernel(scalars, mine, far_same, near_cross, far_cross, value, out):
-    size, width = mine.shape
-    half, quarter = width // 2, width // 4
-    for near, far, core in ((mine, far_same, scalars[0]), (near_cross, far_cross, 1 - scalars[0])):
-        total = near[...] + far[...].astype(jnp.float32)
+    for total, core in last_sums(scalars, mine, far_same, near_cross, far_cross):
         out[:, pl.ds(pl.multiple_of(core * half, half), half)] = total[:, :half]
         columns = pl.ds(pl.multiple_of(core * quarter, quarter), quarter)
         value[:size, columns] = total[:, half : half + quarter]
         value[size:, columns] = total[:, half + quarter :]
-
-
-def summed_views(rows, packed):
-    for r in range(rows):
-        total = packed[r].astype(jnp.float32)
-        for i in range(r + rows, packed.shape[0], rows):
-            total = total + packed[i].astype(jnp.float32)
-        yield r, total
-
-
-def last_query_key_kernel(rows, packed, query, key):
-    size = packed.shape[2] // 2
-    for r, total in summed_views(rows, packed):
-        columns = slice(r * size, (r + 1) * size)
-        query[:, columns] = total[:, :size]
-        key[:, columns] = total[:, size:]
 
 
 def params(mebibytes):
@@ -361,7 +368,6 @@
     scenes = lax.axis_size("scene")
     assert (strip_rows, rows, scenes) == (1, 2, 4)
     strip = strip_rows * columns
-    slots = partners.shape[2]
     part = inner // rows
     tokens = views * 2 * strip
     key_tokens = tokens + (groups - 1) * 2 * strip
@@ -372,17 +378,8 @@
     swap = [(0, 1), (1, 0)]
     along_x, along_y = [(i, i ^ 1) for i in range(scenes)], [(i, i ^ 2) for i in range(scenes)]
 
-    request, alive = pl.pallas_call(
-        functools.partial(request_kernel, views, slots, groups),
-        in_specs=[SMEM],
-        out_specs=(SMEM, SMEM),
-        out_shape=(shape((groups,), i32), shape((groups * views,), i32)),
-        cost_estimate=MUCH,
-        compiler_params=params(4),
-        name="requests",
-    )(partners)
     between = [[(i, i ^ d) for i in range(groups)] for d in range(1, groups)]
-    granted = [lax.ppermute(request, "view", pairs) for pairs in between]
+    granted = [lax.ppermute(partners, "view", pairs) for pairs in between]
 
     lat = latents[0].reshape(views, strip, width)
     cot = cotangent[0].reshape(views, strip, width)
@@ -449,7 +446,7 @@
         cost_estimate=LITTLE,
         name="attention_forward",
     )(
-        scalars, alive, *got_own, *got_other, queries, keys, values, out_grad, norm_gain, w_key, w_value
+        scalars, partners, *got_own, *got_other, queries, keys, values, out_grad, norm_gain, w_key, w_value
     )
     mixed_other = lax.ppermute(mixed, "row", swap)
     dquery, dkey = call(
@@ -479,10 +476,34 @@
     def second_exchange(sums):
         return lax.ppermute(sums[0], "scene", along_y), lax.ppermute(sums[1], "scene", along_x)
 
-    def across_views(packed):
-        return lax.all_to_all(packed, ("view", "row"), split_axis=0, concat_axis=0, tiled=True)
-
     pairs = groups // 2
+    neighbours = [(i, i ^ 1) for i in range(groups)]
+    split_rows = {"query_key": q_rows, "value_out": o_rows}
+
+    def last_parts(addends, split, name):
+        tile = (addends[0].shape[1], sum(now.shape[2] for now in addends[::2]))
+        for bit in reversed(range(1, pairs.bit_length() - 1)):
+            send, keep = call(
+                functools.partial(tile_halves_kernel, bit),
+                [shape((1 << bit, *tile), kind) for kind in (bf16, f32)],
+                (scalars, *addends),
+                "view_bit_" + name,
+                SMEM,
+            )
+            addends = (keep, lax.ppermute(send, "view", [(i, i ^ (2 << bit)) for i in range(groups)]))
+        lanes = tile[0] * tile[1] // (2 * split_rows[name])
+        far_same, far_cross, near_cross, mine = call(
+            functools.partial(tile_cores_kernel, split),
+            [shape((split_rows[name], lanes), kind) for kind in (bf16, bf16, f32, f32)],
+            (scalars, *addends),
+            "last_parts_" + name,
+            SMEM,
+        )
+        far_same = lax.ppermute(far_same, "view", [(i, i ^ 2) for i in range(groups)])
+        far_cross = lax.ppermute(far_cross, ("view", "row"), [(i, i ^ 5) for i in range(targets)])
+        near_cross = lax.ppermute(near_cross, "row", swap)
+        return mine, far_same, near_cross, far_cross
+
     tile = (2 * o_rows, width)
     send, keep = call(
         value_out_kernel,
@@ -492,7 +513,7 @@
         SMEM,
         24,
     )
-    got = lax.ppermute(send, "view", [(i, i ^ 1) for i in range(groups)])
+    got = lax.ppermute(send, "view", neighbours)
     results = [shape((2, *q_block), bf16)] * 2 + [shape((2, *q_block), f32)] * 2
     qk_parts = call(
         query_key_kernel, results, (scalars, normed, normed_far, after(dquery, send), dkey), "grad_query_key", SMEM, 24
@@ -500,54 +521,39 @@
     qk_got = first_exchange(qk_parts)
     qk_sums = first_sum(qk_parts, qk_got, "first_sum_query_key")
     qk_got = second_exchange(qk_sums)
-    packed = call(
-        pack_query_key_kernel,
-        [shape((q_size, 2 * part), bf16)],
-        (qk_sums[2], qk_got[0], qk_sums[3], qk_got[1]),
+    qk_tile = (2 * q_rows, 2 * part)
+    qk_send, qk_keep = call(
+        query_key_tiles_kernel,
+        [shape((pairs, *qk_tile), kind) for kind in (bf16, f32)],
+        (scalars, qk_sums[2], qk_got[0], qk_sums[3], qk_got[1]),
         "second_sum_query_key",
-    )[0]
+        SMEM,
+    )
+    qk_addends = (qk_keep, lax.ppermute(qk_send, "view", neighbours))
     part_shape = (2, pairs, 2 * o_rows, width // 2)
     vo_parts = call(
         view_sum_kernel,
         [shape(part_shape, bf16)] * 2 + [shape(part_shape, f32)] * 2,
-        (keep, after(got, packed)),
+        (keep, after(got, qk_send)),
         "view_sum_value_out",
     )
     vo_got = first_exchange(vo_parts)
-    packed = across_views(after(packed, vo_parts[0]).reshape(targets, q_rows, 2 * part))
-    grad_query, grad_key = call(
-        functools.partial(last_query_key_kernel, rows),
-        [shape((q_rows, inner), f32)] * 2,
-        (packed,),
-        "last_sum_query_key",
-    )
-
-    vo_sums = first_sum(vo_parts, vo_got, "first_sum_value_out", MUCH)
+    vo_sums = first_sum(vo_parts, vo_got, "first_sum_value_out")
     v_got, o_got = second_exchange(vo_sums)
     addends = (vo_sums[3], o_got, vo_sums[2], v_got)
-    for bit in reversed(range(1, pairs.bit_length() - 1)):
-        send, keep = call(
-            functools.partial(tile_halves_kernel, bit),
-            [shape((1 << bit, *tile), kind) for kind in (bf16, f32)],
-            (scalars, *addends),
-            "view_bit_value_out",
-            SMEM,
-        )
-        addends = (keep, lax.ppermute(send, "view", [(i, i ^ (2 << bit)) for i in range(groups)]))
-    far_same, far_cross, near_cross, mine = call(
-        tile_cores_kernel,
-        [shape((o_rows, width), kind) for kind in (bf16, bf16, f32, f32)],
-        (scalars, *addends),
-        "last_parts_value_out",
+    qk_parts = last_parts((after(qk_addends[0], vo_sums[0]), qk_addends[1]), query_key_cores, "query_key")
+    vo_parts = last_parts((after(addends[0], qk_parts[0]), *addends[1:]), value_out_cores, "value_out")
+    grad_query, grad_key = call(
+        place_query_key_kernel,
+        [shape((q_rows, inner), f32)] * 2,
+        (scalars, *qk_parts),
+        "last_sum_query_key",
         SMEM,
     )
-    far_same = lax.ppermute(far_same, "view", [(i, i ^ 2) for i in range(groups)])
-    far_cross = lax.ppermute(far_cross, ("view", "row"), [(i, i ^ 5) for i in range(targets)])
-    near_cross = lax.ppermute(near_cross, "row", swap)
     grad_value, grad_out = call(
-        place_kernel,
+        place_value_out_kernel,
         [shape((q_rows, inner), f32), shape((o_rows, width), f32)],
-        (scalars, after(mine, grad_key), far_same, near_cross, far_cross),
+        (scalars, after(vo_parts[0], grad_query), *vo_parts[1:]),
         "last_sum_value_out",
         SMEM,
     )

time: 91.6 us -> 91.9 us (level)
  waiting for transfers between devices: 42.4 us -> 39.8 us
  starting transfers between devices: 28.5 us -> 30.5 us
  local copies, waits for them, and re-layouts: 0.89 us -> 1.88 us
    all_to_all x1 -> x0, waiting for transfers between devices: 7.48 us -> none  [across_views(): lax.all_to_all(packed, ('view', 'row'), split_axis=0, concat_axis=0, tile...]
    ppermute x7 -> x11, starting transfers between devices: 10.4 us -> 16.4 us  [the longest x3 5.62 us: shards(): granted = [lax.ppermute(partners, 'view', pairs) for pairs in between]]
    ppermute x7 -> x11, waiting for transfers between devices: 4.61 us -> 10.3 us  [the longest x2 5.53 us: last_parts(): lax.ppermute(far_cross, ('view', 'row'), [(i, i ^ 5) for i in range(targe...]
    all_to_all x1 -> x0, starting transfers between devices: 3.92 us -> none  [across_views(): lax.all_to_all(packed, ('view', 'row'), split_axis=0, concat_axis=0, tile...]
    ppermute x2, waiting for transfers between devices: 13 us -> 16.5 us  [first_exchange(): lax.ppermute(sends[0], 'scene', along_x)]
    ppermute x2, waiting for transfers between devices: 4.39 us -> 1.25 us  [second_exchange(): lax.ppermute(sums[1], 'scene', along_x)]
    pallas_call x1 -> x0, Pallas kernels: 1.22 us -> none  [shards(): pl.pallas_call(functools.partial(request_kernel, views, slots, groups), i...]
    unnamed x17 -> x19, local copies, waits for them, and re-layouts: 0.8 us -> 1.79 us
  transfers between devices with their start and end apart: 25 -> 28, of which waited for: 17 -> 17; matrix products, arithmetic and copies ran while one was open for 0% -> 0% of each run, Pallas kernels for 12% -> 13%
where the time goes in v10:
time: 91.9 us; the launch traced here: 91.7 us
  waiting for transfers between devices  39.8 us (43%)
  starting transfers between devices  30.5 us (33%)
  Pallas kernels  18.7 us (20%)
  local copies, waits for them, and re-layouts  1.88 us (2%)
    ppermute x2, waiting for transfers between devices, first_exchange(): lax.ppermute(sends[0], 'scene', along_x)  16.5 us
    pallas_call x11, Pallas kernels, call(): pl.pallas_call(kernel_body, in_specs=[first] + [VMEM] * (len(operands) -...  10.8 us
    ppermute x2, waiting for transfers between devices, second_exchange(): lax.ppermute(sums[0], 'scene', along_y)  6.4 us
    ppermute x3, starting transfers between devices, shards(): granted = [lax.ppermute(partners, 'view', pairs) for pairs in between]  5.62 us
    ppermute x2, waiting for transfers between devices, last_parts(): lax.ppermute(far_cross, ('view', 'row'), [(i, i ^ 5) for i in range(targe...  5.53 us
    ppermute x3, starting transfers between devices, shards(): lax.ppermute(part_out, 'view', pairs)  4.45 us
    ppermute x2, starting transfers between devices, last_parts(): lax.ppermute(far_cross, ('view', 'row'), [(i, i ^ 5) for i in range(targe...  3.89 us
    pallas_call x1, Pallas kernels, shards(): pl.pallas_call(project_kernel, in_specs=[SMEM] + [VMEM] * 10, out_specs=[...  3.67 us
  transfers between devices with their start and end apart: 28, of which 17 were waited for; matrix products, arithmetic and copies ran while one was open for 0% of the time, Pallas kernels for 13%

profile of v10, /device:TPU:0, one launch (start us, length us, event | category | flops | bytes accessed | tf_op | source)
XLA Modules:
  0.0 91.7 jit_solution(12216125046754476730)
XLA Ops:
  0.6 0.8 copy.13.partners
  1.4 5.0 %collective-permute-start.2 = (s32[1,4,3]{2,1,0:T(4,128)S(1)}, s32[1,4,3]{2,1,0:T(4,128)S(1)}, u32[]{:S(2)}, u32[]{:S(2)}) collective-permute-start(s32[1,4,3]{2,1,0:T(4,128)S(1)} %copy.13.partners), channel_id=1, source_target_pairs={{0,6},{2,4},{4,2},{6,0},{1,7},{3,5},{5,3},{7,1},{8,14},{10,12},{12... | collective-permute-start | bytes 152 | tf_op jit(solution)/shard_map/ppermute | solution.py:382
  6.5 0.6 collective-permute-start
  7.0 0.0 collective-permute-start.6
  7.0 0.5 collective-permute-start.7
  7.5 0.1 stack.23.scalars
  7.6 0.4 collective-permute-done.2.refs_2_
  8.0 2.9 %collective-permute-done.1.refs_1_ = s32[1,4,3]{2,1,0:T(4,128)S(1)} collective-permute-done((s32[1,4,3]{2,1,0:T(4,128)S(1)}, s32[1,4,3]{2,1,0:T(4,128)S(1)}, u32[]{:S(2)}, u32[]{:S(2)}) %collective-permute-start.1) | collective-permute-done | bytes 80 | tf_op jit(solution)/shard_map/ppermute | solution.py:382
  10.9 1.0 %copy-done.4 = bf16[1,4,1,32,1536]{4,3,2,1,0:T(8,128)(2,1)S(1)} copy-done((bf16[1,4,1,32,1536]{4,3,2,1,0:T(8,128)(2,1)S(1)}, bf16[1,4,1,32,1536]{4,3,2,1,0:T(8,128)(2,1)}, u32[]{:S(2)}) %copy-start.4) | copy-done | bytes 393240
  11.9 0.8 pick.1
  12.7 0.4 collective-permute-start.3
  13.2 2.1 %collective-permute-start.4 = (bf16[32,1536]{1,0:T(8,128)(2,1)S(1)}, bf16[32,1536]{1,0:T(8,128)(2,1)S(1)}, u32[]{:S(2)}, u32[]{:S(2)}) collective-permute-start(bf16[32,1536]{1,0:T(8,128)(2,1)S(1)} %get-tuple-element.65), channel_id=1, source_target_pairs={{0,4},{2,6},{4,0},{6,2},{1,5},{3,7},{5,1},{7,3},{8,12},{10,14},{12... | collective-permute-start | bytes 294920 | tf_op jit(solution)/shard_map/ppermute | solution.py:398
  15.3 1.9 %collective-permute-start.5 = (bf16[32,1536]{1,0:T(8,128)(2,1)S(1)}, bf16[32,1536]{1,0:T(8,128)(2,1)S(1)}, u32[]{:S(2)}, u32[]{:S(2)}) collective-permute-start(bf16[32,1536]{1,0:T(8,128)(2,1)S(1)} %get-tuple-element.66), channel_id=1, source_target_pairs={{0,6},{2,4},{4,2},{6,0},{1,7},{3,5},{5,3},{7,1},{8,14},{10,12},{12... | collective-permute-start | bytes 294920 | tf_op jit(solution)/shard_map/ppermute | solution.py:398
  17.3 3.7 %project.1 = (bf16[256,1536]{1,0:T(8,128)(2,1)S(1)}, bf16[256,384]{1,0:T(8,128)(2,1)S(1)}, bf16[256,384]{1,0:T(8,128)(2,1)S(1)}, bf16[256,384]{1,0:T(8,128)(2,1)...) custom-call(s32[5]{0:T(128)S(1)} %stack.23.scalars, bf16[4,32,1536]{2,1,0:T(8,128)(2,1)S(1)} %bitcast.9, ...), custom_call_target="tpu_custom_call" | custom-call | flops 1 | bytes 1 | tf_op jit(solution)/shard_map/project/pallas_call | solution.py:399
  21.0 2.0 %collective-permute-done.4.refs_1_ = bf16[32,1536]{1,0:T(8,128)(2,1)S(1)} collective-permute-done((bf16[32,1536]{1,0:T(8,128)(2,1)S(1)}, bf16[32,1536]{1,0:T(8,128)(2,1)S(1)}, u32[]{:S(2)}, u32[]{:S(2)}) %collective-permute-start.4) | collective-permute-done | bytes 98336 | tf_op jit(solution)/shard_map/ppermute | solution.py:398
  23.0 0.0 collective-permute-start.8
  23.0 0.5 collective-permute-start.9
  23.5 0.0 collective-permute-start.10
  23.5 0.8 collective-permute-done.8.refs_3_
  24.3 0.2 collective-permute-done.9.refs_4_
  24.4 0.4 collective-permute-done.10.refs_5_
  24.8 3.4 %attention_forward.1 = (bf16[192,1536]{1,0:T(8,128)(2,1)S(1)}, bf16[192,384]{1,0:T(8,128)(2,1)S(1)}, bf16[192,384]{1,0:T(8,128)(2,1)S(1)}, f32[3,64,512]{2,1,0:T...) custom-call(s32[5]{0:T(128)S(1)} %stack.23.scalars, ...), custom_call_target="tpu_custom_call" | custom-call | flops 1 | bytes 1 | tf_op jit(solution)/shard_map/attention_forward/pallas_call | solution.py:432
  28.2 0.2 collective-permute-start.11
  28.4 1.8 %attention_backward.1 = (bf16[256,384]{1,0:T(8,128)(2,1)S(1)}, bf16[448,384]{1,0:T(8,128)(2,1)S(1)}) custom-call(bf16[256,384]{1,0:T(8,128)(2,1)S(1)} %get-tuple-element.72.refs_6_.queries, bf16[256,384]{1,0:T(8,128)(2,1)S(1)} %get-tuple-element.73.refs_7_.keys, bf16[256,384]{1,0:T(8,128)(2,1)S(1)} %get-tuple-element.74.refs_8_.values, ...), custom_call_target="tpu_custom_call" | custom-call | flops 1 | bytes 1 | tf_op jit(solution)/shard_map/attention_backward/pallas_call | solution.py:420
  30.3 0.0 collective-permute-done.11.theirs
  30.3 2.0 %grad_value_out.1 = (bf16[2,2,2,48,1536]{4,3,2,1,0:T(8,128)(2,1)S(1)}, f32[2,2,2,48,1536]{4,3,2,1,0:T(8,128)S(1)}) custom-call(s32[5]{0:T(128)S(1)} %stack.23.scalars, bf16[256,1536]{1,0:T(8,128)(2,1)S(1)} %get-tuple-element.68.normed, bf16[192,1536]{1,0:T(8,128)(2,1)S(1)} %get-tuple-element.76.normed_far, bf16[448,384]{1,0:T(8,128)(2,1)S(1)} %get-tuple-element.84.dvalue, ...), custom_call_target="tpu_custom_call" | custom-call | flops 1 | bytes 1 | tf_op jit(solution)/shard_map/grad_value_out/pallas_call | solution.py:420
  32.3 1.7 %collective-permute-start.16 = (bf16[2,2,2,48,1536]{4,3,2,1,0:T(8,128)(2,1)S(1)}, bf16[2,2,2,48,1536]{4,3,2,1,0:T(8,128)(2,1)S(1)}, u32[]{:S(2)}, u32[]{:S(2)}) collective-permute-start(bf16[2,2,2,48,1536]{4,3,2,1,0:T(8,128)(2,1)S(1)} %get-tuple-element.87), channel_id=1, source_target_pairs={{0,2},{2,0},{4,6},{6,4},{1,3},{3,1},{5,7},{7,5},{8,10},{10,8},{12,... | collective-permute-start | bytes 3538952 | tf_op jit(solution)/shard_map/ppermute | solution.py:516
  34.0 2.0 %grad_query_key.1 = (bf16[2,384,384]{2,1,0:T(8,128)(2,1)S(1)}, bf16[2,384,384]{2,1,0:T(8,128)(2,1)S(1)}, f32[2,384,384]{2,1,0:T(8,128)S(1)}, f32[2,384,384]{2,1,0:T(8,128)S(1)}) custom-call(s32[5]{0:T(128)S(1)} %stack.23.scalars, bf16[256,1536]{1,0:T(8,128)(2,1)S(1)} %get-tuple-element.68.normed, bf16[192,1536]{1,0:T(8,128)(2,1)S(1)} %get-tuple-element.76.normed_far, ...), custom_call_target="tpu_custom_call" | custom-call | flops 1 | bytes 1 | tf_op jit(solution)/shard_map/grad_query_key/pallas_call | solution.py:420
  36.0 1.5 %collective-permute-start.12 = (bf16[2,384,384]{2,1,0:T(8,128)(2,1)S(1)}, bf16[2,384,384]{2,1,0:T(8,128)(2,1)S(1)}, u32[]{:S(2)}, u32[]{:S(2)}) collective-permute-start(bf16[2,384,384]{2,1,0:T(8,128)(2,1)S(1)} %get-tuple-element.90), channel_id=1, source_target_pairs={{0,8},{8,0},{16,24},{24,16},{1,9},{9,1},{17,25},{25,17},{2,10},{10... | collective-permute-start | bytes 1769480 | tf_op jit(solution)/shard_map/ppermute | solution.py:469
  37.4 1.5 %collective-permute-start.13 = (bf16[2,384,384]{2,1,0:T(8,128)(2,1)S(1)}, bf16[2,384,384]{2,1,0:T(8,128)(2,1)S(1)}, u32[]{:S(2)}, u32[]{:S(2)}) collective-permute-start(bf16[2,384,384]{2,1,0:T(8,128)(2,1)S(1)} %get-tuple-element.92), channel_id=1, source_target_pairs={{0,16},{8,24},{16,0},{24,8},{1,17},{9,25},{17,1},{25,9},{2,18},{10... | collective-permute-start | bytes 1769480 | tf_op jit(solution)/shard_map/ppermute | solution.py:469
  39.0 12.4 %collective-permute-done.12.x_got = bf16[2,384,384]{2,1,0:T(8,128)(2,1)S(1)} collective-permute-done((bf16[2,384,384]{2,1,0:T(8,128)(2,1)S(1)}, bf16[2,384,384]{2,1,0:T(8,128)(2,1)S(1)}, u32[]{:S(2)}, u32[]{:S(2)}) %collective-permute-start.12) | collective-permute-done | bytes 589856 | tf_op jit(solution)/shard_map/ppermute | solution.py:469
  51.3 1.1 %collective-permute-done.13.y_got = bf16[2,384,384]{2,1,0:T(8,128)(2,1)S(1)} collective-permute-done((bf16[2,384,384]{2,1,0:T(8,128)(2,1)S(1)}, bf16[2,384,384]{2,1,0:T(8,128)(2,1)S(1)}, u32[]{:S(2)}, u32[]{:S(2)}) %collective-permute-start.13) | collective-permute-done | bytes 589856 | tf_op jit(solution)/shard_map/ppermute | solution.py:469
  52.5 0.2 first_sum_query_key.1
  52.7 1.6 %collective-permute-start.14 = (bf16[384,384]{1,0:T(8,128)(2,1)S(1)}, bf16[384,384]{1,0:T(8,128)(2,1)S(1)}, u32[]{:S(2)}, u32[]{:S(2)}) collective-permute-start(bf16[384,384]{1,0:T(8,128)(2,1)S(1)} %get-tuple-element.94), channel_id=1, source_target_pairs={{0,16},{8,24},{16,0},{24,8},{1,17},{9,25},{17,1},{25,9},{2,18},{10... | collective-permute-start | bytes 884744 | tf_op jit(solution)/shard_map/ppermute | solution.py:477
  54.3 0.5 collective-permute-start.15
  54.8 5.8 %collective-permute-done.14.q_got = bf16[384,384]{1,0:T(8,128)(2,1)S(1)} collective-permute-done((bf16[384,384]{1,0:T(8,128)(2,1)S(1)}, bf16[384,384]{1,0:T(8,128)(2,1)S(1)}, u32[]{:S(2)}, u32[]{:S(2)}) %collective-permute-start.14) | collective-permute-done | bytes 294944 | tf_op jit(solution)/shard_map/ppermute | solution.py:477
  60.6 1.2 %collective-permute-done.15.k_got = bf16[384,384]{1,0:T(8,128)(2,1)S(1)} collective-permute-done((bf16[384,384]{1,0:T(8,128)(2,1)S(1)}, bf16[384,384]{1,0:T(8,128)(2,1)S(1)}, u32[]{:S(2)}, u32[]{:S(2)}) %collective-permute-start.15) | collective-permute-done | bytes 294944 | tf_op jit(solution)/shard_map/ppermute | solution.py:477
  61.8 0.7 second_sum_query_key.1
  62.5 0.0 collective-permute-done.16.got
  62.5 0.2 view_sum_value_out.1
  62.7 0.7 collective-permute-start.17
  63.4 0.5 collective-permute-start.18
  63.9 1.5 %collective-permute-start.19 = (bf16[2,96,768]{2,1,0:T(8,128)(2,1)S(1)}, bf16[2,96,768]{2,1,0:T(8,128)(2,1)S(1)}, u32[]{:S(2)}, u32[]{:S(2)}) collective-permute-start(bf16[2,96,768]{2,1,0:T(8,128)(2,1)S(1)} %get-tuple-element.99), channel_id=1, source_target_pairs={{0,2},{2,0},{4,6},{6,4},{1,3},{3,1},{5,7},{7,5},{8,10},{10,8},{12,... | collective-permute-start | bytes 884744 | tf_op jit(solution)/shard_map/ppermute | solution.py:532
  65.4 4.1 %collective-permute-done.17.x_got = bf16[2,2,48,768]{3,2,1,0:T(8,128)(2,1)S(1)} collective-permute-done((bf16[2,2,48,768]{3,2,1,0:T(8,128)(2,1)S(1)}, bf16[2,2,48,768]{3,2,1,0:T(8,128)(2,1)S(1)}, u32[]{:S(2)}, u32[]{:S(2)}) %collective-permute-start.17) | collective-permute-done | bytes 294944 | tf_op jit(solution)/shard_map/ppermute | solution.py:469
  69.5 0.9 %collective-permute-done.18.y_got = bf16[2,2,48,768]{3,2,1,0:T(8,128)(2,1)S(1)} collective-permute-done((bf16[2,2,48,768]{3,2,1,0:T(8,128)(2,1)S(1)}, bf16[2,2,48,768]{3,2,1,0:T(8,128)(2,1)S(1)}, u32[]{:S(2)}, u32[]{:S(2)}) %collective-permute-start.18) | collective-permute-done | bytes 294944 | tf_op jit(solution)/shard_map/ppermute | solution.py:469
  70.4 0.1 first_sum_value_out.1
  70.5 1.2 %collective-permute-start.23 = (bf16[2,48,768]{2,1,0:T(8,128)(2,1)S(1)}, bf16[2,48,768]{2,1,0:T(8,128)(2,1)S(1)}, u32[]{:S(2)}, u32[]{:S(2)}) collective-permute-start(bf16[2,48,768]{2,1,0:T(8,128)(2,1)S(1)} %get-tuple-element.115), channel_id=1, source_target_pairs={{0,8},{8,0},{16,24},{24,16},{1,9},{9,1},{17,25},{25,17},{2,10},{10... | collective-permute-start | bytes 442376 | tf_op jit(solution)/shard_map/ppermute | solution.py:477
  71.7 1.0 %collective-permute-start.24 = (bf16[2,48,768]{2,1,0:T(8,128)(2,1)S(1)}, bf16[2,48,768]{2,1,0:T(8,128)(2,1)S(1)}, u32[]{:S(2)}, u32[]{:S(2)}) collective-permute-start(bf16[2,48,768]{2,1,0:T(8,128)(2,1)S(1)} %get-tuple-element.105), channel_id=1, source_target_pairs={{0,16},{8,24},{16,0},{24,8},{1,17},{9,25},{17,1},{25,9},{2,18},{10... | collective-permute-start | bytes 442376 | tf_op jit(solution)/shard_map/ppermute | solution.py:477
  72.7 0.6 last_parts_query_key.1
  73.3 0.1 collective-permute-start.21
  73.4 2.9 %collective-permute-start.20 = (bf16[48,768]{1,0:T(8,128)(2,1)S(1)}, bf16[48,768]{1,0:T(8,128)(2,1)S(1)}, u32[]{:S(2)}, u32[]{:S(2)}) collective-permute-start(bf16[48,768]{1,0:T(8,128)(2,1)S(1)} %get-tuple-element.108), channel_id=1, source_target_pairs={{0,4},{2,6},{4,0},{6,2},{1,5},{3,7},{5,1},{7,3},{8,12},{10,14},{12... | collective-permute-start | bytes 221192 | tf_op jit(solution)/shard_map/ppermute | solution.py:502
  76.2 0.0 collective-permute-done.23.refs_1_
  76.2 0.6 collective-permute-done.24.refs_3_
  76.8 0.6 last_parts_value_out.1
  77.5 0.1 collective-permute-start.26
  77.6 2.3 %collective-permute-start.22 = (bf16[48,768]{1,0:T(8,128)(2,1)S(1)}, bf16[48,768]{1,0:T(8,128)(2,1)S(1)}, u32[]{:S(2)}, u32[]{:S(2)}) collective-permute-start(bf16[48,768]{1,0:T(8,128)(2,1)S(1)} %get-tuple-element.110), channel_id=1, source_target_pairs={{0,5},{1,4},{2,7},{3,6},{4,1},{5,0},{6,3},{7,2},{8,13},{9,12},{10,... | collective-permute-start | bytes 221192 | tf_op jit(solution)/shard_map/ppermute | solution.py:503
  79.9 0.7 collective-permute-start.25
  80.6 0.1 collective-permute-done.20.far_same
  80.7 1.6 %collective-permute-start.27 = (bf16[24,1536]{1,0:T(8,128)(2,1)S(1)}, bf16[24,1536]{1,0:T(8,128)(2,1)S(1)}, u32[]{:S(2)}, u32[]{:S(2)}) collective-permute-start(bf16[24,1536]{1,0:T(8,128)(2,1)S(1)} %get-tuple-element.121), channel_id=1, source_target_pairs={{0,5},{1,4},{2,7},{3,6},{4,1},{5,0},{6,3},{7,2},{8,13},{9,12},{10,... | collective-permute-start | bytes 221192 | tf_op jit(solution)/shard_map/ppermute | solution.py:503
  82.2 5.1 %collective-permute-done.22.far_cross = bf16[48,768]{1,0:T(8,128)(2,1)S(1)} collective-permute-done((bf16[48,768]{1,0:T(8,128)(2,1)S(1)}, bf16[48,768]{1,0:T(8,128)(2,1)S(1)}, u32[]{:S(2)}, u32[]{:S(2)}) %collective-permute-start.22) | collective-permute-done | bytes 73760 | tf_op jit(solution)/shard_map/ppermute | solution.py:503
  87.3 1.3 %last_sum_query_key.1 = (f32[48,768]{1,0:T(8,128)}, f32[48,768]{1,0:T(8,128)}) custom-call(s32[5]{0:T(128)S(1)} %stack.23.scalars, f32[48,768]{1,0:T(8,128)S(1)} %get-tuple-element.107.mine, bf16[48,768]{1,0:T(8,128)(2,1)S(1)} %collective-permute-done.20.far_same, f32[48,768]{1,0:T(8,128)S(1)} %collective-permute-done.21.near_cross, ...), custom_call_target="tpu_custom_call" | custom-call | flops 1 | bytes 1 | tf_op jit(solution)/shard_map/last_sum_query_key/pallas_call | solution.py:420
  88.6 1.4 %collective-permute-done.25.far_same = bf16[24,1536]{1,0:T(8,128)(2,1)S(1)} collective-permute-done((bf16[24,1536]{1,0:T(8,128)(2,1)S(1)}, bf16[24,1536]{1,0:T(8,128)(2,1)S(1)}, u32[]{:S(2)}, u32[]{:S(2)}) %collective-permute-start.25) | collective-permute-done | bytes 73760 | tf_op jit(solution)/shard_map/ppermute | solution.py:502
  90.0 0.5 collective-permute-done.27.far_cross
  90.4 1.3 %last_sum_value_out.1 = (f32[48,768]{1,0:T(8,128)}, f32[24,1536]{1,0:T(8,128)}) custom-call(s32[5]{0:T(128)S(1)} %stack.23.scalars, f32[24,1536]{1,0:T(8,128)S(1)} %get-tuple-element.118.mine, bf16[24,1536]{1,0:T(8,128)(2,1)S(1)} %collective-permute-done.25.far_same, f32[24,1536]{1,0:T(8,128)S(1)} %collective-permute-done.26.near_cross, ...), custom_call_target="tpu_custom_call" | custom-call | flops 1 | bytes 1 | tf_op jit(solution)/shard_map/last_sum_value_out/pallas_call | solution.py:420
  (26 shorter events, 0.1 us)
Async XLA Ops:
  1.4 6.6 %collective-permute-start.2 = (s32[1,4,3]{2,1,0:T(4,128)S(1)}, s32[1,4,3]{2,1,0:T(4,128)S(1)}, u32[]{:S(2)}, u32[]{:S(2)}) collective-permute-start(s32[1,4,3]{2,1,0:T(4,128)S(1)} %copy.13.partners), channel_id=1, source_target_pairs={{0,6},{2,4},{4,2},{6,0},{1,7},{3,5},{5,3},{7,1},{8,14},{10,12},{12... | collective-permute-start | bytes 152 | tf_op jit(solution)/shard_map/ppermute | solution.py:382
  6.4 4.5 %collective-permute-start.1 = (s32[1,4,3]{2,1,0:T(4,128)S(1)}, s32[1,4,3]{2,1,0:T(4,128)S(1)}, u32[]{:S(2)}, u32[]{:S(2)}) collective-permute-start(s32[1,4,3]{2,1,0:T(4,128)S(1)} %copy.13.partners), channel_id=1, source_target_pairs={{0,4},{2,6},{4,0},{6,2},{1,5},{3,7},{5,1},{7,3},{8,12},{10,14},{12... | collective-permute-start | bytes 152 | tf_op jit(solution)/shard_map/ppermute | solution.py:382
  6.5 4.5 %collective-permute-start = (s32[1,4,3]{2,1,0:T(4,128)S(1)}, s32[1,4,3]{2,1,0:T(4,128)S(1)}, u32[]{:S(2)}, u32[]{:S(2)}) collective-permute-start(s32[1,4,3]{2,1,0:T(4,128)S(1)} %copy.13.partners), channel_id=1, source_target_pairs={{0,2},{2,0},{4,6},{6,4},{1,3},{3,1},{5,7},{7,5},{8,10},{10,8},{12,... | collective-permute-start | bytes 152 | tf_op jit(solution)/shard_map/ppermute | solution.py:382
  7.0 10.2 %collective-permute-start.6 = (bf16[4,32,1536]{2,1,0:T(8,128)(2,1)}, bf16[4,32,1536]{2,1,0:T(8,128)(2,1)S(1)}, u32[]{:S(2)}, u32[]{:S(2)}) collective-permute-start(bf16[4,32,1536]{2,1,0:T(8,128)(2,1)} %bitcast.7), channel_id=1, source_target_pairs={{0,1},{1,0},{2,3},{3,2},{4,5},{5,4},{6,7},{7,6},{8,9},{9,8},{10,11... | collective-permute-start | bytes 1179656 | tf_op jit(solution)/shard_map/ppermute | solution.py:386
  7.0 10.2 %collective-permute-start.7 = (bf16[4,32,1536]{2,1,0:T(8,128)(2,1)}, bf16[4,32,1536]{2,1,0:T(8,128)(2,1)S(1)}, u32[]{:S(2)}, u32[]{:S(2)}) collective-permute-start(bf16[4,32,1536]{2,1,0:T(8,128)(2,1)} %bitcast.10), channel_id=1, source_target_pairs={{0,1},{1,0},{2,3},{3,2},{4,5},{5,4},{6,7},{7,6},{8,9},{9,8},{10,11... | collective-permute-start | bytes 1179656 | tf_op jit(solution)/shard_map/ppermute | solution.py:387
  7.6 9.6 %copy-start = (bf16[1536,768]{1,0:T(8,128)(2,1)S(1)}, bf16[1536,768]{1,0:T(8,128)(2,1)}, u32[]{:S(2)}) copy-start(bf16[1536,768]{1,0:T(8,128)(2,1)} %refs_11_.1) | copy-start | bytes 7077892
  7.6 9.6 %copy-start.1 = (bf16[1536,768]{1,0:T(8,128)(2,1)S(1)}, bf16[1536,768]{1,0:T(8,128)(2,1)}, u32[]{:S(2)}) copy-start(bf16[1536,768]{1,0:T(8,128)(2,1)} %refs_12_.1) | copy-start | bytes 7077892
  7.6 9.6 %copy-start.2 = (bf16[1536,768]{1,0:T(8,128)(2,1)S(1)}, bf16[1536,768]{1,0:T(8,128)(2,1)}, u32[]{:S(2)}) copy-start(bf16[1536,768]{1,0:T(8,128)(2,1)} %w_query.1) | copy-start | bytes 7077892
  7.6 9.6 %copy-start.3 = (bf16[768,1536]{1,0:T(8,128)(2,1)S(1)}, bf16[768,1536]{1,0:T(8,128)(2,1)}, u32[]{:S(2)}) copy-start(bf16[768,1536]{1,0:T(8,128)(2,1)} %w_out.1) | copy-start | bytes 7077892
  10.9 1.0 %copy-start.4 = (bf16[1,4,1,32,1536]{4,3,2,1,0:T(8,128)(2,1)S(1)}, bf16[1,4,1,32,1536]{4,3,2,1,0:T(8,128)(2,1)}, u32[]{:S(2)}) copy-start(bf16[1,4,1,32,1536]{4,3,2,1,0:T(8,128)(2,1)} %param.10) | copy-start | bytes 1179652
  11.9 5.3 %copy-start.5 = (bf16[1,4,1,32,1536]{4,3,2,1,0:T(8,128)(2,1)S(1)}, bf16[1,4,1,32,1536]{4,3,2,1,0:T(8,128)(2,1)}, u32[]{:S(2)}) copy-start(bf16[1,4,1,32,1536]{4,3,2,1,0:T(8,128)(2,1)} %param.10) | copy-start | bytes 1179652
  11.9 5.3 %copy-start.6 = (bf16[1,4,1,32,1536]{4,3,2,1,0:T(8,128)(2,1)S(1)}, bf16[1,4,1,32,1536]{4,3,2,1,0:T(8,128)(2,1)}, u32[]{:S(2)}) copy-start(bf16[1,4,1,32,1536]{4,3,2,1,0:T(8,128)(2,1)} %param.18) | copy-start | bytes 1179652
  11.9 5.3 %copy-start.7 = (bf16[9,1536]{1,0:T(8,128)(2,1)S(1)}, bf16[9,1536]{1,0:T(8,128)(2,1)}, u32[]{:S(2)}) copy-start(bf16[9,1536]{1,0:T(8,128)(2,1)} %taps.1) | copy-start | bytes 82948
  11.9 5.3 %copy-start.8 = (f32[1536]{0:T(1024)S(1)}, f32[1536]{0:T(1024)}, u32[]{:S(2)}) copy-start(f32[1536]{0:T(1024)} %refs_10_.1) | copy-start | bytes 18436
  12.7 8.2 %collective-permute-start.3 = (bf16[32,1536]{1,0:T(8,128)(2,1)S(1)}, bf16[32,1536]{1,0:T(8,128)(2,1)S(1)}, u32[]{:S(2)}, u32[]{:S(2)}) collective-permute-start(bf16[32,1536]{1,0:T(8,128)(2,1)S(1)} %get-tuple-element.64), channel_id=1, source_target_pairs={{0,2},{2,0},{4,6},{6,4},{1,3},{3,1},{5,7},{7,5},{8,10},{10,8},{12,... | collective-permute-start | bytes 294920 | tf_op jit(solution)/shard_map/ppermute | solution.py:398
  13.2 9.8 %collective-permute-start.4 = (bf16[32,1536]{1,0:T(8,128)(2,1)S(1)}, bf16[32,1536]{1,0:T(8,128)(2,1)S(1)}, u32[]{:S(2)}, u32[]{:S(2)}) collective-permute-start(bf16[32,1536]{1,0:T(8,128)(2,1)S(1)} %get-tuple-element.65), channel_id=1, source_target_pairs={{0,4},{2,6},{4,0},{6,2},{1,5},{3,7},{5,1},{7,3},{8,12},{10,14},{12... | collective-permute-start | bytes 294920 | tf_op jit(solution)/shard_map/ppermute | solution.py:398
  15.3 7.7 %collective-permute-start.5 = (bf16[32,1536]{1,0:T(8,128)(2,1)S(1)}, bf16[32,1536]{1,0:T(8,128)(2,1)S(1)}, u32[]{:S(2)}, u32[]{:S(2)}) collective-permute-start(bf16[32,1536]{1,0:T(8,128)(2,1)S(1)} %get-tuple-element.66), channel_id=1, source_target_pairs={{0,6},{2,4},{4,2},{6,0},{1,7},{3,5},{5,3},{7,1},{8,14},{10,12},{12... | collective-permute-start | bytes 294920 | tf_op jit(solution)/shard_map/ppermute | solution.py:398
  23.0 1.3 %collective-permute-start.8 = (bf16[32,1536]{1,0:T(8,128)(2,1)S(1)}, bf16[32,1536]{1,0:T(8,128)(2,1)S(1)}, u32[]{:S(2)}, u32[]{:S(2)}) collective-permute-start(bf16[32,1536]{1,0:T(8,128)(2,1)S(1)} %collective-permute-done.3.refs_0_), channel_id=1, source_target_pairs={{0,1},{1,0},{2,3},{3,2},{4,5},{5,4},{6,7},{7,6},{8,9},{9,8},{10,11... | collective-permute-start | bytes 294920 | tf_op jit(solution)/shard_map/ppermute | solution.py:417
  23.0 1.5 %collective-permute-start.9 = (bf16[32,1536]{1,0:T(8,128)(2,1)S(1)}, bf16[32,1536]{1,0:T(8,128)(2,1)S(1)}, u32[]{:S(2)}, u32[]{:S(2)}) collective-permute-start(bf16[32,1536]{1,0:T(8,128)(2,1)S(1)} %collective-permute-done.4.refs_1_), channel_id=1, source_target_pairs={{0,1},{1,0},{2,3},{3,2},{4,5},{5,4},{6,7},{7,6},{8,9},{9,8},{10,11... | collective-permute-start | bytes 294920 | tf_op jit(solution)/shard_map/ppermute | solution.py:417
  23.5 1.3 %collective-permute-start.10 = (bf16[32,1536]{1,0:T(8,128)(2,1)S(1)}, bf16[32,1536]{1,0:T(8,128)(2,1)S(1)}, u32[]{:S(2)}, u32[]{:S(2)}) collective-permute-start(bf16[32,1536]{1,0:T(8,128)(2,1)S(1)} %collective-permute-done.5.refs_2_), channel_id=1, source_target_pairs={{0,1},{1,0},{2,3},{3,2},{4,5},{5,4},{6,7},{7,6},{8,9},{9,8},{10,11... | collective-permute-start | bytes 294920 | tf_op jit(solution)/shard_map/ppermute | solution.py:417
  28.2 2.0 %collective-permute-start.11 = (bf16[256,384]{1,0:T(8,128)(2,1)S(1)}, bf16[256,384]{1,0:T(8,128)(2,1)S(1)}, u32[]{:S(2)}, u32[]{:S(2)}) collective-permute-start(bf16[256,384]{1,0:T(8,128)(2,1)S(1)} %get-tuple-element.85.mine), channel_id=1, source_target_pairs={{0,1},{1,0},{2,3},{3,2},{4,5},{5,4},{6,7},{7,6},{8,9},{9,8},{10,11... | collective-permute-start | bytes 589832 | tf_op jit(solution)/shard_map/ppermute | solution.py:451
  32.3 30.2 %collective-permute-start.16 = (bf16[2,2,2,48,1536]{4,3,2,1,0:T(8,128)(2,1)S(1)}, bf16[2,2,2,48,1536]{4,3,2,1,0:T(8,128)(2,1)S(1)}, u32[]{:S(2)}, u32[]{:S(2)}) collective-permute-start(bf16[2,2,2,48,1536]{4,3,2,1,0:T(8,128)(2,1)S(1)} %get-tuple-element.87), channel_id=1, source_target_pairs={{0,2},{2,0},{4,6},{6,4},{1,3},{3,1},{5,7},{7,5},{8,10},{10,8},{12,... | collective-permute-start | bytes 3538952 | tf_op jit(solution)/shard_map/ppermute | solution.py:516
  36.0 15.4 %collective-permute-start.12 = (bf16[2,384,384]{2,1,0:T(8,128)(2,1)S(1)}, bf16[2,384,384]{2,1,0:T(8,128)(2,1)S(1)}, u32[]{:S(2)}, u32[]{:S(2)}) collective-permute-start(bf16[2,384,384]{2,1,0:T(8,128)(2,1)S(1)} %get-tuple-element.90), channel_id=1, source_target_pairs={{0,8},{8,0},{16,24},{24,16},{1,9},{9,1},{17,25},{25,17},{2,10},{10... | collective-permute-start | bytes 1769480 | tf_op jit(solution)/shard_map/ppermute | solution.py:469
  37.4 15.0 %collective-permute-start.13 = (bf16[2,384,384]{2,1,0:T(8,128)(2,1)S(1)}, bf16[2,384,384]{2,1,0:T(8,128)(2,1)S(1)}, u32[]{:S(2)}, u32[]{:S(2)}) collective-permute-start(bf16[2,384,384]{2,1,0:T(8,128)(2,1)S(1)} %get-tuple-element.92), channel_id=1, source_target_pairs={{0,16},{8,24},{16,0},{24,8},{1,17},{9,25},{17,1},{25,9},{2,18},{10... | collective-permute-start | bytes 1769480 | tf_op jit(solution)/shard_map/ppermute | solution.py:469
  52.7 7.9 %collective-permute-start.14 = (bf16[384,384]{1,0:T(8,128)(2,1)S(1)}, bf16[384,384]{1,0:T(8,128)(2,1)S(1)}, u32[]{:S(2)}, u32[]{:S(2)}) collective-permute-start(bf16[384,384]{1,0:T(8,128)(2,1)S(1)} %get-tuple-element.94), channel_id=1, source_target_pairs={{0,16},{8,24},{16,0},{24,8},{1,17},{9,25},{17,1},{25,9},{2,18},{10... | collective-permute-start | bytes 884744 | tf_op jit(solution)/shard_map/ppermute | solution.py:477
  54.3 7.6 %collective-permute-start.15 = (bf16[384,384]{1,0:T(8,128)(2,1)S(1)}, bf16[384,384]{1,0:T(8,128)(2,1)S(1)}, u32[]{:S(2)}, u32[]{:S(2)}) collective-permute-start(bf16[384,384]{1,0:T(8,128)(2,1)S(1)} %get-tuple-element.96), channel_id=1, source_target_pairs={{0,8},{8,0},{16,24},{24,16},{1,9},{9,1},{17,25},{25,17},{2,10},{10... | collective-permute-start | bytes 884744 | tf_op jit(solution)/shard_map/ppermute | solution.py:477
  62.7 6.8 %collective-permute-start.17 = (bf16[2,2,48,768]{3,2,1,0:T(8,128)(2,1)S(1)}, bf16[2,2,48,768]{3,2,1,0:T(8,128)(2,1)S(1)}, u32[]{:S(2)}, u32[]{:S(2)}) collective-permute-start(bf16[2,2,48,768]{3,2,1,0:T(8,128)(2,1)S(1)} %get-tuple-element.102), channel_id=1, source_target_pairs={{0,8},{8,0},{16,24},{24,16},{1,9},{9,1},{17,25},{25,17},{2,10},{10... | collective-permute-start | bytes 884744 | tf_op jit(solution)/shard_map/ppermute | solution.py:469
  63.4 7.0 %collective-permute-start.18 = (bf16[2,2,48,768]{3,2,1,0:T(8,128)(2,1)S(1)}, bf16[2,2,48,768]{3,2,1,0:T(8,128)(2,1)S(1)}, u32[]{:S(2)}, u32[]{:S(2)}) collective-permute-start(bf16[2,2,48,768]{3,2,1,0:T(8,128)(2,1)S(1)} %get-tuple-element.104), channel_id=1, source_target_pairs={{0,16},{8,24},{16,0},{24,8},{1,17},{9,25},{17,1},{25,9},{2,18},{10... | collective-permute-start | bytes 884744 | tf_op jit(solution)/shard_map/ppermute | solution.py:469
  63.9 8.8 %collective-permute-start.19 = (bf16[2,96,768]{2,1,0:T(8,128)(2,1)S(1)}, bf16[2,96,768]{2,1,0:T(8,128)(2,1)S(1)}, u32[]{:S(2)}, u32[]{:S(2)}) collective-permute-start(bf16[2,96,768]{2,1,0:T(8,128)(2,1)S(1)} %get-tuple-element.99), channel_id=1, source_target_pairs={{0,2},{2,0},{4,6},{6,4},{1,3},{3,1},{5,7},{7,5},{8,10},{10,8},{12,... | collective-permute-start | bytes 884744 | tf_op jit(solution)/shard_map/ppermute | solution.py:532
  70.5 5.7 %collective-permute-start.23 = (bf16[2,48,768]{2,1,0:T(8,128)(2,1)S(1)}, bf16[2,48,768]{2,1,0:T(8,128)(2,1)S(1)}, u32[]{:S(2)}, u32[]{:S(2)}) collective-permute-start(bf16[2,48,768]{2,1,0:T(8,128)(2,1)S(1)} %get-tuple-element.115), channel_id=1, source_target_pairs={{0,8},{8,0},{16,24},{24,16},{1,9},{9,1},{17,25},{25,17},{2,10},{10... | collective-permute-start | bytes 442376 | tf_op jit(solution)/shard_map/ppermute | solution.py:477
  71.7 5.1 %collective-permute-start.24 = (bf16[2,48,768]{2,1,0:T(8,128)(2,1)S(1)}, bf16[2,48,768]{2,1,0:T(8,128)(2,1)S(1)}, u32[]{:S(2)}, u32[]{:S(2)}) collective-permute-start(bf16[2,48,768]{2,1,0:T(8,128)(2,1)S(1)} %get-tuple-element.105), channel_id=1, source_target_pairs={{0,16},{8,24},{16,0},{24,8},{1,17},{9,25},{17,1},{25,9},{2,18},{10... | collective-permute-start | bytes 442376 | tf_op jit(solution)/shard_map/ppermute | solution.py:477
  73.3 14.0 %collective-permute-start.21 = (f32[48,768]{1,0:T(8,128)S(1)}, f32[48,768]{1,0:T(8,128)S(1)}, u32[]{:S(2)}, u32[]{:S(2)}) collective-permute-start(f32[48,768]{1,0:T(8,128)S(1)} %get-tuple-element.109), channel_id=1, source_target_pairs={{0,1},{1,0},{2,3},{3,2},{4,5},{5,4},{6,7},{7,6},{8,9},{9,8},{10,11... | collective-permute-start | bytes 442376 | tf_op jit(solution)/shard_map/ppermute | solution.py:504
  73.4 7.3 %collective-permute-start.20 = (bf16[48,768]{1,0:T(8,128)(2,1)S(1)}, bf16[48,768]{1,0:T(8,128)(2,1)S(1)}, u32[]{:S(2)}, u32[]{:S(2)}) collective-permute-start(bf16[48,768]{1,0:T(8,128)(2,1)S(1)} %get-tuple-element.108), channel_id=1, source_target_pairs={{0,4},{2,6},{4,0},{6,2},{1,5},{3,7},{5,1},{7,3},{8,12},{10,14},{12... | collective-permute-start | bytes 221192 | tf_op jit(solution)/shard_map/ppermute | solution.py:502
  77.5 13.0 %collective-permute-start.26 = (f32[24,1536]{1,0:T(8,128)S(1)}, f32[24,1536]{1,0:T(8,128)S(1)}, u32[]{:S(2)}, u32[]{:S(2)}) collective-permute-start(f32[24,1536]{1,0:T(8,128)S(1)} %get-tuple-element.120), channel_id=1, source_target_pairs={{0,1},{1,0},{2,3},{3,2},{4,5},{5,4},{6,7},{7,6},{8,9},{9,8},{10,11... | collective-permute-start | bytes 442376 | tf_op jit(solution)/shard_map/ppermute | solution.py:504
  77.6 9.7 %collective-permute-start.22 = (bf16[48,768]{1,0:T(8,128)(2,1)S(1)}, bf16[48,768]{1,0:T(8,128)(2,1)S(1)}, u32[]{:S(2)}, u32[]{:S(2)}) collective-permute-start(bf16[48,768]{1,0:T(8,128)(2,1)S(1)} %get-tuple-element.110), channel_id=1, source_target_pairs={{0,5},{1,4},{2,7},{3,6},{4,1},{5,0},{6,3},{7,2},{8,13},{9,12},{10,... | collective-permute-start | bytes 221192 | tf_op jit(solution)/shard_map/ppermute | solution.py:503
  79.9 10.1 %collective-permute-start.25 = (bf16[24,1536]{1,0:T(8,128)(2,1)S(1)}, bf16[24,1536]{1,0:T(8,128)(2,1)S(1)}, u32[]{:S(2)}, u32[]{:S(2)}) collective-permute-start(bf16[24,1536]{1,0:T(8,128)(2,1)S(1)} %get-tuple-element.119), channel_id=1, source_target_pairs={{0,4},{2,6},{4,0},{6,2},{1,5},{3,7},{5,1},{7,3},{8,12},{10,14},{12... | collective-permute-start | bytes 221192 | tf_op jit(solution)/shard_map/ppermute | solution.py:502
  80.7 9.8 %collective-permute-start.27 = (bf16[24,1536]{1,0:T(8,128)(2,1)S(1)}, bf16[24,1536]{1,0:T(8,128)(2,1)S(1)}, u32[]{:S(2)}, u32[]{:S(2)}) collective-permute-start(bf16[24,1536]{1,0:T(8,128)(2,1)S(1)} %get-tuple-element.121), channel_id=1, source_target_pairs={{0,5},{1,4},{2,7},{3,6},{4,1},{5,0},{6,3},{7,2},{8,13},{9,12},{10,... | collective-permute-start | bytes 221192 | tf_op jit(solution)/shard_map/ppermute | solution.py:503

commit v11 on v10

--- a/solution.py
+++ b/solution.py
@@ -37,17 +37,26 @@
     return (x * lax.rsqrt(mean + EPSILON) * gain).astype(jnp.bfloat16)
 
 
+def request_kernel(views, slots, groups, partners, request, alive):
+    for g in range(groups):
+        request[g] = 0
+        for u in range(views):
+            alive[g * views + u] = 0
+    for u in range(views):
+        for j in range(slots):
+            partner = partners[0, u, j]
+
+            @pl.when(partner >= 0)
+            def _():
+                group = lax.div(partner, jnp.int32(views))
+                request[group] = lax.rem(partner, jnp.int32(views))
+                alive[group * views + u] = 1
+
+
 def pick_kernel(groups, scalars, *refs):
-    tables, lat, outgoing = refs[: groups - 1], refs[groups - 1], refs[groups:]
-    views = lat.shape[0]
-    for table, out in zip(tables, outgoing):
-        wanted = jnp.int32(0)
-        for u in range(table.shape[1]):
-            for j in range(table.shape[2]):
-                partner = table[0, u, j]
-                here = (partner >= 0) & (lax.div(partner, jnp.int32(views)) == scalars[1])
-                wanted = jnp.where(here, lax.rem(partner, jnp.int32(views)), wanted)
-        out[...] = lat[wanted]
+    requests, lat, outgoing = refs[: groups - 1], refs[groups - 1], refs[groups:]
+    for request, out in zip(requests, outgoing):
+        out[...] = lat[request[scalars[1]]]
 
 
 def core_half(scalars, size):
@@ -133,7 +142,7 @@
     return jnp.concatenate([dot_nn(x, y) for x, y in pairs], axis=0)
 
 
-def forward_kernel(views, groups, scalars, partners, *refs):
+def forward_kernel(views, groups, scalars, alive, *refs):
     got_own, got_other, refs = refs[: groups - 1], refs[groups - 1 : 2 * groups - 2], refs[2 * groups - 2 :]
     queries, keys, values, out_grad, gain, w_key, w_value, *refs = refs
     normed_far, keys_far, values_far, attention_own, attention_far, mixed, dvalue = refs
@@ -153,12 +162,7 @@
         normed_far[start + strip : start + 2 * strip, :] = normalized(got_other[j][...], scale_row)
         taken = jnp.zeros((1, views * span), jnp.int32)
         for u in range(views):
-            found = jnp.int32(0)
-            for slot in range(partners.shape[2]):
-                partner = partners[0, u, slot]
-                same = (partner >= 0) & (lax.div(partner, jnp.int32(views)) == group)
-                found = jnp.where(same, 1, found)
-            taken = jnp.where(column_view == u, found, taken)
+            taken = jnp.where(column_view == u, alive[group * views + u], taken)
         slot_alive.append(taken > 0)
     fetched = normed_far[...]
     half = core_half(scalars, part)
@@ -209,24 +213,20 @@
         dkey[tokens:, lanes] = dot_nn(ds_far, q).astype(jnp.bfloat16)
 
 
-def by_quarters(scalars, lefts, right, send, keep, x_first):
-    size = send.shape[1]
+def halves_kernel(scalars, *refs):
+    lefts, (right, x_send, y_send, x_keep, y_keep) = refs[:-5], refs[-5:]
+    rows = x_send.shape[1]
     x, y = scalars[3], scalars[4]
-    for target, first in ((send, 1), (keep, 0)):
-        for second in (1, 0):
-            dx, dy = (first, second) if x_first else (second, first)
-            block = 2 * lax.bitwise_xor(y, jnp.int32(dy)) + lax.bitwise_xor(x, jnp.int32(dx))
-            columns = pl.ds(pl.multiple_of(block * size, size), size)
-            total, start = 0.0, 0
-            for left in lefts:
-                total = total + dot_tn(left[:, columns], right[start : start + left.shape[0], :])
-                start += left.shape[0]
-            target[second] = total.astype(target.dtype)
-
-
-def query_key_kernel(scalars, normed, normed_far, dquery, dkey, q_send, k_send, q_keep, k_keep):
-    by_quarters(scalars, (normed,), dquery, q_send, q_keep, True)
-    by_quarters(scalars, (normed, normed_far), dkey, k_send, k_keep, False)
+    for dy, dx in ((1, 1), (0, 1), (1, 0), (0, 0)):
+        block = 2 * lax.bitwise_xor(y, jnp.int32(dy)) + lax.bitwise_xor(x, jnp.int32(dx))
+        columns = pl.ds(pl.multiple_of(block * 2 * rows, 2 * rows), 2 * rows)
+        total, start = 0.0, 0
+        for left in lefts:
+            total = total + dot_tn(left[:, columns], right[start : start + left.shape[0], :])
+            start += left.shape[0]
+        x_out, y_out = (x_send if dx else x_keep), (y_send if dy else y_keep)
+        x_out[dy] = total[:rows].astype(x_out.dtype)
+        y_out[dx] = total[rows:].astype(y_out.dtype)
 
 
 def value_out_kernel(scalars, normed, normed_far, dvalue, mine, theirs, upstream, send, keep):
@@ -274,16 +274,16 @@
         now[...] = keep[0] + got[0].astype(jnp.float32)
 
 
-def query_key_tiles_kernel(scalars, q_now, q_got, k_now, k_got, send, keep):
+def view_tiles_kernel(scalars, x_now, x_got, y_now, y_got, send, keep):
     odd = lax.rem(scalars[1], jnp.int32(2)) == 1
-    total = [now[...] + got[...].astype(jnp.float32) for now, got in ((q_now, q_got), (k_now, k_got))]
-    total = jnp.concatenate(total, axis=1)
     pairs, size, _ = send.shape
-    for pair in range(pairs):
-        first = total[2 * pair * size : (2 * pair + 1) * size]
-        second = total[(2 * pair + 1) * size : (2 * pair + 2) * size]
-        send[pair] = jnp.where(odd, first, second).astype(send.dtype)
-        keep[pair] = jnp.where(odd, second, first)
+    for half, (now, got) in enumerate(((x_now, x_got), (y_now, y_got))):
+        total = now[...] + got[...].astype(jnp.float32)
+        for i in range(pairs // 2):
+            first, second = total[2 * i * size : (2 * i + 1) * size], total[(2 * i + 1) * size : (2 * i + 2) * size]
+            pair = half * (pairs // 2) + i
+            send[pair] = jnp.where(odd, first, second).astype(send.dtype)
+            keep[pair] = jnp.where(odd, second, first)
 
 
 def summed_tile(addends, place):
@@ -305,7 +305,7 @@
             target[i] = summed_tile(addends, part * count + i).astype(target.dtype)
 
 
-def query_key_cores(tile):
+def row_cores(tile):
     size = tile.shape[0] // 2
     return tile[:size], tile[size:]
 
@@ -335,12 +335,10 @@
         yield near[...] + far[...].astype(jnp.float32), core
 
 
-def place_query_key_kernel(scalars, mine, far_same, near_cross, far_cross, query, key):
-    size = mine.shape[1] // 2
+def place_kernel(scalars, mine, far_same, near_cross, far_cross, result):
+    size = mine.shape[1]
     for total, core in last_sums(scalars, mine, far_same, near_cross, far_cross):
-        columns = pl.ds(pl.multiple_of(core * size, size), size)
-        query[:, columns] = total[:, :size]
-        key[:, columns] = total[:, size:]
+        result[:, pl.ds(pl.multiple_of(core * size, size), size)] = total
 
 
 def place_value_out_kernel(scalars, mine, far_same, near_cross, far_cross, value, out):
@@ -364,6 +362,7 @@
 def shards(latents, norm_gain, w_query, w_key, w_value, w_out, kernel, partners, counts, cotangent):
     views, strip_rows, columns, width = latents.shape[1:]
     inner = w_query.shape[1]
+    slots = partners.shape[2]
     groups, rows = lax.axis_size("view"), lax.axis_size("row")
     scenes = lax.axis_size("scene")
     assert (strip_rows, rows, scenes) == (1, 2, 4)
@@ -378,8 +377,17 @@
     swap = [(0, 1), (1, 0)]
     along_x, along_y = [(i, i ^ 1) for i in range(scenes)], [(i, i ^ 2) for i in range(scenes)]
 
+    request, alive = pl.pallas_call(
+        functools.partial(request_kernel, views, slots, groups),
+        in_specs=[SMEM],
+        out_specs=(SMEM, SMEM),
+        out_shape=(shape((groups,), i32), shape((groups * views,), i32)),
+        cost_estimate=MUCH,
+        compiler_params=params(4),
+        name="requests",
+    )(partners)
     between = [[(i, i ^ d) for i in range(groups)] for d in range(1, groups)]
-    granted = [lax.ppermute(partners, "view", pairs) for pairs in between]
+    granted = [lax.ppermute(request, "view", pairs) for pairs in between]
 
     lat = latents[0].reshape(views, strip, width)
     cot = cotangent[0].reshape(views, strip, width)
@@ -446,7 +454,7 @@
         cost_estimate=LITTLE,
         name="attention_forward",
     )(
-        scalars, partners, *got_own, *got_other, queries, keys, values, out_grad, norm_gain, w_key, w_value
+        scalars, alive, *got_own, *got_other, queries, keys, values, out_grad, norm_gain, w_key, w_value
     )
     mixed_other = lax.ppermute(mixed, "row", swap)
     dquery, dkey = call(
@@ -463,7 +471,6 @@
     targets = groups * rows
     q_size = width // 4
     q_rows, o_rows = q_size // targets, inner // (4 * targets)
-    q_block = (q_size, part)
 
     def first_exchange(sends):
         return lax.ppermute(sends[0], "scene", along_x), lax.ppermute(sends[1], "scene", along_y)
@@ -478,7 +485,7 @@
 
     pairs = groups // 2
     neighbours = [(i, i ^ 1) for i in range(groups)]
-    split_rows = {"query_key": q_rows, "value_out": o_rows}
+    split_rows = {"query": q_rows, "key": q_rows, "value_out": o_rows}
 
     def last_parts(addends, split, name):
         tile = (addends[0].shape[1], sum(now.shape[2] for now in addends[::2]))
@@ -514,46 +521,54 @@
         24,
     )
     got = lax.ppermute(send, "view", neighbours)
-    results = [shape((2, *q_block), bf16)] * 2 + [shape((2, *q_block), f32)] * 2
-    qk_parts = call(
-        query_key_kernel, results, (scalars, normed, normed_far, after(dquery, send), dkey), "grad_query_key", SMEM, 24
-    )
-    qk_got = first_exchange(qk_parts)
-    qk_sums = first_sum(qk_parts, qk_got, "first_sum_query_key")
-    qk_got = second_exchange(qk_sums)
-    qk_tile = (2 * q_rows, 2 * part)
-    qk_send, qk_keep = call(
-        query_key_tiles_kernel,
-        [shape((pairs, *qk_tile), kind) for kind in (bf16, f32)],
-        (scalars, qk_sums[2], qk_got[0], qk_sums[3], qk_got[1]),
-        "second_sum_query_key",
-        SMEM,
-    )
-    qk_addends = (qk_keep, lax.ppermute(qk_send, "view", neighbours))
+    def partial(lefts, right, name):
+        block = (2, q_size // 2, part)
+        results = [shape(block, bf16)] * 2 + [shape(block, f32)] * 2
+        parts = call(halves_kernel, results, (scalars, *lefts, right), name, SMEM, 24)
+        return parts, first_exchange(parts)
+
+    def view_tiles(sums, got, name):
+        send, keep = call(
+            view_tiles_kernel,
+            [shape((pairs, 2 * q_rows, part), kind) for kind in (bf16, f32)],
+            (scalars, sums[2], got[0], sums[3], got[1]),
+            name,
+            SMEM,
+        )
+        return keep, lax.ppermute(send, "view", neighbours)
+
+    q_parts, q_got = partial((normed,), after(dquery, send), "grad_query")
+    k_parts, k_got = partial((normed, normed_far), after(dkey, q_parts[0]), "grad_key")
+    q_sums = first_sum(q_parts, q_got, "first_sum_query")
+    q_got = second_exchange(q_sums)
+    k_parts[2] = after(k_parts[2], q_sums[0])
+    k_sums = first_sum(k_parts, k_got, "first_sum_key")
+    k_got = second_exchange(k_sums)
+    q_sums[2] = after(q_sums[2], k_sums[0])
+    q_addends = view_tiles(q_sums, q_got, "view_tiles_query")
+    k_sums[2] = after(k_sums[2], q_addends[0])
+    k_addends = view_tiles(k_sums, k_got, "view_tiles_key")
+    q_last = last_parts((after(q_addends[0], k_addends[0]), q_addends[1]), row_cores, "query")
     part_shape = (2, pairs, 2 * o_rows, width // 2)
     vo_parts = call(
         view_sum_kernel,
         [shape(part_shape, bf16)] * 2 + [shape(part_shape, f32)] * 2,
-        (keep, after(got, qk_send)),
+        (keep, after(got, q_last[0])),
         "view_sum_value_out",
     )
     vo_got = first_exchange(vo_parts)
+    k_last = last_parts((after(k_addends[0], vo_parts[0]), k_addends[1]), row_cores, "key")
+    grad_query = call(place_kernel, [shape((q_rows, inner), f32)], (scalars, *q_last), "last_sum_query", SMEM)[0]
+    vo_parts[2] = after(vo_parts[2], k_last[0], grad_query)
     vo_sums = first_sum(vo_parts, vo_got, "first_sum_value_out")
     v_got, o_got = second_exchange(vo_sums)
-    addends = (vo_sums[3], o_got, vo_sums[2], v_got)
-    qk_parts = last_parts((after(qk_addends[0], vo_sums[0]), qk_addends[1]), query_key_cores, "query_key")
-    vo_parts = last_parts((after(addends[0], qk_parts[0]), *addends[1:]), value_out_cores, "value_out")
-    grad_query, grad_key = call(
-        place_query_key_kernel,
-        [shape((q_rows, inner), f32)] * 2,
-        (scalars, *qk_parts),
-        "last_sum_query_key",
-        SMEM,
-    )
+    vo_addends = (after(vo_sums[3], k_last[1], k_last[3]), o_got, vo_sums[2], v_got)
+    vo_last = last_parts(vo_addends, value_out_cores, "value_out")
+    grad_key = call(place_kernel, [shape((q_rows, inner), f32)], (scalars, *k_last), "last_sum_key", SMEM)[0]
     grad_value, grad_out = call(
         place_value_out_kernel,
         [shape((q_rows, inner), f32), shape((o_rows, width), f32)],
-        (scalars, after(vo_parts[0], grad_query), *vo_parts[1:]),
+        (scalars, after(vo_last[0], grad_key), *vo_last[1:]),
         "last_sum_value_out",
         SMEM,
     )

time: 91.9 us -> 100 us (1.088)
  Pallas kernels: 18.7 us -> 22.8 us
  waiting for transfers between devices: 39.8 us -> 42.9 us
  starting transfers between devices: 30.5 us -> 32.6 us
    ppermute x2 -> x3, waiting for transfers between devices: 1.47 us -> 13.5 us  [last_parts(): lax.ppermute(far_same, 'view', [(i, i ^ 2) for i in range(groups)])]
    ppermute x2 -> x3, waiting for transfers between devices: 16.5 us -> 6.72 us  [first_exchange(): lax.ppermute(sends[0], 'scene', along_x)]
    ppermute x4 -> x5, waiting for transfers between devices: 3.31 us -> 8.07 us  [the longest x3 4.69 us: shards(): granted = [lax.ppermute(request, 'view', pairs) for pairs in between]]
    ppermute x2 -> x3, waiting for transfers between devices: 6.4 us -> 1.98 us  [second_exchange(): lax.ppermute(sums[0], 'scene', along_y)]
    pallas_call x11 -> x16, Pallas kernels: 10.8 us -> 13.9 us  [call(): pl.pallas_call(kernel_body, in_specs=[first] + [VMEM] * (len(operands) -...]
    ppermute x2 -> x3, starting transfers between devices: 3.89 us -> 1.32 us  [last_parts(): lax.ppermute(far_cross, ('view', 'row'), [(i, i ^ 5) for i in range(targe...]
    ppermute x2 -> x3, starting transfers between devices: 2.15 us -> 3.72 us  [first_exchange(): lax.ppermute(sends[0], 'scene', along_x)]
    ppermute x2 -> x3, starting transfers between devices: 2.03 us -> 3.54 us  [first_exchange(): lax.ppermute(sends[1], 'scene', along_y)]
  transfers between devices with their start and end apart: 28 -> 36, of which waited for: 17 -> 20; matrix products, arithmetic and copies ran while one was open for 0% -> 0% of each run, Pallas kernels for 13% -> 14%
where the time goes in v11:
time: 100 us
  waiting for transfers between devices  42.9 us (43%)
  starting transfers between devices  32.6 us (33%)
  Pallas kernels  22.8 us (23%)
    pallas_call x16, Pallas kernels, call(): pl.pallas_call(kernel_body, in_specs=[first] + [VMEM] * (len(operands) -...  13.9 us
    ppermute x3, waiting for transfers between devices, last_parts(): lax.ppermute(far_same, 'view', [(i, i ^ 2) for i in range(groups)])  13.5 us
    ppermute x3, waiting for transfers between devices, first_exchange(): lax.ppermute(sends[0], 'scene', along_x)  6.72 us
    ppermute x3, waiting for transfers between devices, last_parts(): lax.ppermute(far_cross, ('view', 'row'), [(i, i ^ 5) for i in range(targe...  5.78 us
    ppermute x3, starting transfers between devices, shards(): granted = [lax.ppermute(request, 'view', pairs) for pairs in between]  5.68 us
    ppermute x3, waiting for transfers between devices, shards(): granted = [lax.ppermute(request, 'view', pairs) for pairs in between]  4.69 us
    ppermute x3, starting transfers between devices, shards(): lax.ppermute(part_out, 'view', pairs)  4.44 us
    ppermute x3, starting transfers between devices, first_exchange(): lax.ppermute(sends[0], 'scene', along_x)  3.72 us
  transfers between devices with their start and end apart: 36, of which 20 were waited for; matrix products, arithmetic and copies ran while one was open for 0% of the time, Pallas kernels for 14%

profile of v11, /device:TPU:0, one launch (start us, length us, event | category | flops | bytes accessed | tf_op | source)
XLA Modules:
  0.0 100.1 jit_solution(8092583468435401148)
XLA Ops:
  0.6 0.8 copy.13.partners
  1.4 1.2 %requests.1 = (s32[4]{0:T(128)S(1)}, s32[16]{0:T(128)S(1)}) custom-call(s32[1,4,3]{2,1,0:T(4,128)S(1)} %copy.13.partners), custom_call_target="tpu_custom_call" | custom-call | flops 40000000000 | bytes 1 | tf_op jit(solution)/shard_map/requests/pallas_call | solution.py:380
  2.6 3.1 %collective-permute-start = (s32[4]{0:T(128)S(1)}, s32[4]{0:T(128)S(1)}, u32[]{:S(2)}, u32[]{:S(2)}) collective-permute-start(s32[4]{0:T(128)S(1)} %get-tuple-element.84), channel_id=1, source_target_pairs={{0,2},{2,0},{4,6},{6,4},{1,3},{3,1},{5,7},{7,5},{8,10},{10,8},{12,... | collective-permute-start | bytes 56 | tf_op jit(solution)/shard_map/ppermute | solution.py:390
  5.7 2.6 %collective-permute-start.1 = (s32[4]{0:T(128)S(1)}, s32[4]{0:T(128)S(1)}, u32[]{:S(2)}, u32[]{:S(2)}) collective-permute-start(s32[4]{0:T(128)S(1)} %get-tuple-element.84), channel_id=1, source_target_pairs={{0,4},{2,6},{4,0},{6,2},{1,5},{3,7},{5,1},{7,3},{8,12},{10,14},{12... | collective-permute-start | bytes 56 | tf_op jit(solution)/shard_map/ppermute | solution.py:390
  8.3 0.5 collective-permute-start.7
  9.0 1.2 %collective-permute-done.1.refs_1_ = s32[4]{0:T(128)S(1)} collective-permute-done((s32[4]{0:T(128)S(1)}, s32[4]{0:T(128)S(1)}, u32[]{:S(2)}, u32[]{:S(2)}) %collective-permute-start.1) | collective-permute-done | bytes 48 | tf_op jit(solution)/shard_map/ppermute | solution.py:390
  10.2 3.5 %collective-permute-done.2.refs_2_ = s32[4]{0:T(128)S(1)} collective-permute-done((s32[4]{0:T(128)S(1)}, s32[4]{0:T(128)S(1)}, u32[]{:S(2)}, u32[]{:S(2)}) %collective-permute-start.2) | collective-permute-done | bytes 48 | tf_op jit(solution)/shard_map/ppermute | solution.py:390
  13.6 0.6 pick.1
  14.3 0.6 collective-permute-start.4
  14.9 3.8 %collective-permute-start.5 = (bf16[32,1536]{1,0:T(8,128)(2,1)S(1)}, bf16[32,1536]{1,0:T(8,128)(2,1)S(1)}, u32[]{:S(2)}, u32[]{:S(2)}) collective-permute-start(bf16[32,1536]{1,0:T(8,128)(2,1)S(1)} %get-tuple-element.87), channel_id=1, source_target_pairs={{0,6},{2,4},{4,2},{6,0},{1,7},{3,5},{5,3},{7,1},{8,14},{10,12},{12... | collective-permute-start | bytes 294920 | tf_op jit(solution)/shard_map/ppermute | solution.py:406
  18.8 3.7 %project.1 = (bf16[256,1536]{1,0:T(8,128)(2,1)S(1)}, bf16[256,384]{1,0:T(8,128)(2,1)S(1)}, bf16[256,384]{1,0:T(8,128)(2,1)S(1)}, bf16[256,384]{1,0:T(8,128)(2,1)...) custom-call(s32[5]{0:T(128)S(1)} %stack.23.scalars, bf16[4,32,1536]{2,1,0:T(8,128)(2,1)S(1)} %bitcast.9, ...), custom_call_target="tpu_custom_call" | custom-call | flops 1 | bytes 1 | tf_op jit(solution)/shard_map/project/pallas_call | solution.py:407
  22.4 1.0 collective-permute-done.4.refs_1_
  23.4 0.5 collective-permute-start.9
  23.9 0.8 collective-permute-done.8.refs_3_
  24.9 0.4 collective-permute-done.10.refs_5_
  25.2 3.4 %attention_forward.1 = (bf16[192,1536]{1,0:T(8,128)(2,1)S(1)}, bf16[192,384]{1,0:T(8,128)(2,1)S(1)}, bf16[192,384]{1,0:T(8,128)(2,1)S(1)}, f32[3,64,512]{2,1,0:T...) custom-call(s32[5]{0:T(128)S(1)} %stack.23.scalars, ...), custom_call_target="tpu_custom_call" | custom-call | flops 1 | bytes 1 | tf_op jit(solution)/shard_map/attention_forward/pallas_call | solution.py:440
  28.6 0.2 collective-permute-start.11
  28.9 1.8 %attention_backward.1 = (bf16[256,384]{1,0:T(8,128)(2,1)S(1)}, bf16[448,384]{1,0:T(8,128)(2,1)S(1)}) custom-call(bf16[256,384]{1,0:T(8,128)(2,1)S(1)} %get-tuple-element.90.refs_6_.queries, bf16[256,384]{1,0:T(8,128)(2,1)S(1)} %get-tuple-element.91.refs_7_.keys, bf16[256,384]{1,0:T(8,128)(2,1)S(1)} %get-tuple-element.92.refs_8_.values, ...), custom_call_target="tpu_custom_call" | custom-call | flops 1 | bytes 1 | tf_op jit(solution)/shard_map/attention_backward/pallas_call | solution.py:428
  30.7 2.0 %grad_value_out.1 = (bf16[2,2,2,48,1536]{4,3,2,1,0:T(8,128)(2,1)S(1)}, f32[2,2,2,48,1536]{4,3,2,1,0:T(8,128)S(1)}) custom-call(s32[5]{0:T(128)S(1)} %stack.23.scalars, bf16[256,1536]{1,0:T(8,128)(2,1)S(1)} %get-tuple-element.89.normed.refs_0_, bf16[192,1536]{1,0:T(8,128)(2,1)S(1)} %get-tuple-element.103.normed_far.refs_1_, ...), custom_call_target="tpu_custom_call" | custom-call | flops 1 | bytes 1 | tf_op jit(solution)/shard_map/grad_value_out/pallas_call | solution.py:428
  32.7 1.7 %collective-permute-start.24 = (bf16[2,2,2,48,1536]{4,3,2,1,0:T(8,128)(2,1)S(1)}, bf16[2,2,2,48,1536]{4,3,2,1,0:T(8,128)(2,1)S(1)}, u32[]{:S(2)}, u32[]{:S(2)}) collective-permute-start(bf16[2,2,2,48,1536]{4,3,2,1,0:T(8,128)(2,1)S(1)} %get-tuple-element.109), channel_id=1, source_target_pairs={{0,2},{2,0},{4,6},{6,4},{1,3},{3,1},{5,7},{7,5},{8,10},{10,8},{12,... | collective-permute-start | bytes 3538952 | tf_op jit(solution)/shard_map/ppermute | solution.py:523
  34.4 1.1 %grad_query.1 = (bf16[2,192,384]{2,1,0:T(8,128)(2,1)S(1)}, bf16[2,192,384]{2,1,0:T(8,128)(2,1)S(1)}, f32[2,192,384]{2,1,0:T(8,128)S(1)}, f32[2,192,384]{2,1,0:T(8,128)S(1)}) custom-call(s32[5]{0:T(128)S(1)} %stack.23.scalars, bf16[256,1536]{1,0:T(8,128)(2,1)S(1)} %get-tuple-element.89.normed.refs_0_, bf16[256,384]{1,0:T(8,128)(2,1)S(1)} %get-tuple-element.110.refs_1_), custom_call_target="tpu_custom_call" | custom-call | flops 1 | bytes 1 | tf_op jit(solution)/shard_map/grad_query/pallas_call | solution.py:428
  35.5 1.6 %collective-permute-start.12 = (bf16[2,192,384]{2,1,0:T(8,128)(2,1)S(1)}, bf16[2,192,384]{2,1,0:T(8,128)(2,1)S(1)}, u32[]{:S(2)}, u32[]{:S(2)}) collective-permute-start(bf16[2,192,384]{2,1,0:T(8,128)(2,1)S(1)} %get-tuple-element.112), channel_id=1, source_target_pairs={{0,8},{8,0},{16,24},{24,16},{1,9},{9,1},{17,25},{25,17},{2,10},{10... | collective-permute-start | bytes 884744 | tf_op jit(solution)/shard_map/ppermute | solution.py:476
  37.1 1.5 %collective-permute-start.13 = (bf16[2,192,384]{2,1,0:T(8,128)(2,1)S(1)}, bf16[2,192,384]{2,1,0:T(8,128)(2,1)S(1)}, u32[]{:S(2)}, u32[]{:S(2)}) collective-permute-start(bf16[2,192,384]{2,1,0:T(8,128)(2,1)S(1)} %get-tuple-element.114), channel_id=1, source_target_pairs={{0,16},{8,24},{16,0},{24,8},{1,17},{9,25},{17,1},{25,9},{2,18},{10... | collective-permute-start | bytes 884744 | tf_op jit(solution)/shard_map/ppermute | solution.py:476
  38.6 1.6 %grad_key.1 = (bf16[2,192,384]{2,1,0:T(8,128)(2,1)S(1)}, bf16[2,192,384]{2,1,0:T(8,128)(2,1)S(1)}, f32[2,192,384]{2,1,0:T(8,128)S(1)}, f32[2,192,384]{2,1,0:T(8,128)S(1)}) custom-call(s32[5]{0:T(128)S(1)} %stack.23.scalars, bf16[256,1536]{1,0:T(8,128)(2,1)S(1)} %get-tuple-element.89.normed.refs_0_, ...), custom_call_target="tpu_custom_call" | custom-call | flops 1 | bytes 1 | tf_op jit(solution)/shard_map/grad_key/pallas_call | solution.py:428
  40.2 0.6 collective-permute-start.14
  40.8 0.5 collective-permute-start.15
  41.3 4.2 %collective-permute-done.12.x_got = bf16[2,192,384]{2,1,0:T(8,128)(2,1)S(1)} collective-permute-done((bf16[2,192,384]{2,1,0:T(8,128)(2,1)S(1)}, bf16[2,192,384]{2,1,0:T(8,128)(2,1)S(1)}, u32[]{:S(2)}, u32[]{:S(2)}) %collective-permute-start.12) | collective-permute-done | bytes 294944 | tf_op jit(solution)/shard_map/ppermute | solution.py:476
  45.5 1.5 %collective-permute-done.13.y_got = bf16[2,192,384]{2,1,0:T(8,128)(2,1)S(1)} collective-permute-done((bf16[2,192,384]{2,1,0:T(8,128)(2,1)S(1)}, bf16[2,192,384]{2,1,0:T(8,128)(2,1)S(1)}, u32[]{:S(2)}, u32[]{:S(2)}) %collective-permute-start.13) | collective-permute-done | bytes 294944 | tf_op jit(solution)/shard_map/ppermute | solution.py:476
  47.1 1.6 %collective-permute-start.16 = (bf16[192,384]{1,0:T(8,128)(2,1)S(1)}, bf16[192,384]{1,0:T(8,128)(2,1)S(1)}, u32[]{:S(2)}, u32[]{:S(2)}) collective-permute-start(bf16[192,384]{1,0:T(8,128)(2,1)S(1)} %get-tuple-element.118), channel_id=1, source_target_pairs={{0,16},{8,24},{16,0},{24,8},{1,17},{9,25},{17,1},{25,9},{2,18},{10... | collective-permute-start | bytes 442376 | tf_op jit(solution)/shard_map/ppermute | solution.py:484
  48.7 0.5 collective-permute-start.17
  49.2 2.6 %collective-permute-done.14.x_got = bf16[2,192,384]{2,1,0:T(8,128)(2,1)S(1)} collective-permute-done((bf16[2,192,384]{2,1,0:T(8,128)(2,1)S(1)}, bf16[2,192,384]{2,1,0:T(8,128)(2,1)S(1)}, u32[]{:S(2)}, u32[]{:S(2)}) %collective-permute-start.14) | collective-permute-done | bytes 294944 | tf_op jit(solution)/shard_map/ppermute | solution.py:476
  51.8 1.5 %collective-permute-done.15.y_got = bf16[2,192,384]{2,1,0:T(8,128)(2,1)S(1)} collective-permute-done((bf16[2,192,384]{2,1,0:T(8,128)(2,1)S(1)}, bf16[2,192,384]{2,1,0:T(8,128)(2,1)S(1)}, u32[]{:S(2)}, u32[]{:S(2)}) %collective-permute-start.15) | collective-permute-done | bytes 294944 | tf_op jit(solution)/shard_map/ppermute | solution.py:476
  53.4 1.6 %collective-permute-start.18 = (bf16[192,384]{1,0:T(8,128)(2,1)S(1)}, bf16[192,384]{1,0:T(8,128)(2,1)S(1)}, u32[]{:S(2)}, u32[]{:S(2)}) collective-permute-start(bf16[192,384]{1,0:T(8,128)(2,1)S(1)} %get-tuple-element.123), channel_id=1, source_target_pairs={{0,16},{8,24},{16,0},{24,8},{1,17},{9,25},{17,1},{25,9},{2,18},{10... | collective-permute-start | bytes 442376 | tf_op jit(solution)/shard_map/ppermute | solution.py:484
  55.0 0.5 collective-permute-start.19
  55.6 0.9 collective-permute-done.16.x_got
  56.5 0.6 view_tiles_query.1
  57.1 0.5 collective-permute-start.20
  57.6 1.1 %collective-permute-done.18.x_got = bf16[192,384]{1,0:T(8,128)(2,1)S(1)} collective-permute-done((bf16[192,384]{1,0:T(8,128)(2,1)S(1)}, bf16[192,384]{1,0:T(8,128)(2,1)S(1)}, u32[]{:S(2)}, u32[]{:S(2)}) %collective-permute-start.18) | collective-permute-done | bytes 147488 | tf_op jit(solution)/shard_map/ppermute | solution.py:484
  58.6 1.5 %collective-permute-done.19.y_got = bf16[192,384]{1,0:T(8,128)(2,1)S(1)} collective-permute-done((bf16[192,384]{1,0:T(8,128)(2,1)S(1)}, bf16[192,384]{1,0:T(8,128)(2,1)S(1)}, u32[]{:S(2)}, u32[]{:S(2)}) %collective-permute-start.19) | collective-permute-done | bytes 147488 | tf_op jit(solution)/shard_map/ppermute | solution.py:484
  60.2 0.6 view_tiles_key.1
  60.8 3.4 %collective-permute-done.20.refs_1_ = bf16[2,96,384]{2,1,0:T(8,128)(2,1)S(1)} collective-permute-done((bf16[2,96,384]{2,1,0:T(8,128)(2,1)S(1)}, bf16[2,96,384]{2,1,0:T(8,128)(2,1)S(1)}, u32[]{:S(2)}, u32[]{:S(2)}) %collective-permute-start.20) | collective-permute-done | bytes 147488 | tf_op jit(solution)/shard_map/ppermute | solution.py:538
  64.2 0.6 last_parts_query.1
  64.8 0.3 view_sum_value_out.1
  65.0 1.6 %collective-permute-start.29 = (bf16[2,2,48,768]{3,2,1,0:T(8,128)(2,1)S(1)}, bf16[2,2,48,768]{3,2,1,0:T(8,128)(2,1)S(1)}, u32[]{:S(2)}, u32[]{:S(2)}) collective-permute-start(bf16[2,2,48,768]{3,2,1,0:T(8,128)(2,1)S(1)} %get-tuple-element.141), channel_id=1, source_target_pairs={{0,8},{8,0},{16,24},{24,16},{1,9},{9,1},{17,25},{25,17},{2,10},{10... | collective-permute-start | bytes 884744 | tf_op jit(solution)/shard_map/ppermute | solution.py:476
  66.6 1.5 %collective-permute-start.30 = (bf16[2,2,48,768]{3,2,1,0:T(8,128)(2,1)S(1)}, bf16[2,2,48,768]{3,2,1,0:T(8,128)(2,1)S(1)}, u32[]{:S(2)}, u32[]{:S(2)}) collective-permute-start(bf16[2,2,48,768]{3,2,1,0:T(8,128)(2,1)S(1)} %get-tuple-element.151), channel_id=1, source_target_pairs={{0,16},{8,24},{16,0},{24,8},{1,17},{9,25},{17,1},{25,9},{2,18},{10... | collective-permute-start | bytes 884744 | tf_op jit(solution)/shard_map/ppermute | solution.py:476
  68.1 1.6 %collective-permute-start.25 = (bf16[2,96,384]{2,1,0:T(8,128)(2,1)S(1)}, bf16[2,96,384]{2,1,0:T(8,128)(2,1)S(1)}, u32[]{:S(2)}, u32[]{:S(2)}) collective-permute-start(bf16[2,96,384]{2,1,0:T(8,128)(2,1)S(1)} %get-tuple-element.143), channel_id=1, source_target_pairs={{0,2},{2,0},{4,6},{6,4},{1,3},{3,1},{5,7},{7,5},{8,10},{10,8},{12,... | collective-permute-start | bytes 442376 | tf_op jit(solution)/shard_map/ppermute | solution.py:538
  69.7 0.8 collective-permute-start.21
  70.5 4.5 %collective-permute-done.21.far_same = bf16[48,384]{1,0:T(8,128)(2,1)S(1)} collective-permute-done((bf16[48,384]{1,0:T(8,128)(2,1)S(1)}, bf16[48,384]{1,0:T(8,128)(2,1)S(1)}, u32[]{:S(2)}, u32[]{:S(2)}) %collective-permute-start.21) | collective-permute-done | bytes 36896 | tf_op jit(solution)/shard_map/ppermute | solution.py:509
  75.0 4.4 %collective-permute-done.23.far_cross = bf16[48,384]{1,0:T(8,128)(2,1)S(1)} collective-permute-done((bf16[48,384]{1,0:T(8,128)(2,1)S(1)}, bf16[48,384]{1,0:T(8,128)(2,1)S(1)}, u32[]{:S(2)}, u32[]{:S(2)}) %collective-permute-start.23) | collective-permute-done | bytes 36896 | tf_op jit(solution)/shard_map/ppermute | solution.py:510
  79.4 1.2 %last_sum_query.1 = f32[48,768]{1,0:T(8,128)} custom-call(s32[5]{0:T(128)S(1)} %stack.23.scalars, f32[48,384]{1,0:T(8,128)S(1)} %get-tuple-element.135.mine, bf16[48,384]{1,0:T(8,128)(2,1)S(1)} %collective-permute-done.21.far_same, f32[48,384]{1,0:T(8,128)S(1)} %collective-permute-done.22.near_cross, bf16[48,384]{1,0:T(8,128)(2,1)S(1)} %collective-permute-done.23.far_cross), custom_call_target="tpu_custom_call" | custom-call | flops 1 | bytes 1 | tf_op jit(solution)/shard_map/last_sum_query/pallas_call | solution.py:428
  80.6 0.6 last_parts_key.1
  81.4 0.6 collective-permute-start.31
  82.0 0.5 collective-permute-start.32
  82.5 1.1 %collective-permute-start.26 = (bf16[48,384]{1,0:T(8,128)(2,1)S(1)}, bf16[48,384]{1,0:T(8,128)(2,1)S(1)}, u32[]{:S(2)}, u32[]{:S(2)}) collective-permute-start(bf16[48,384]{1,0:T(8,128)(2,1)S(1)} %get-tuple-element.145), channel_id=1, source_target_pairs={{0,4},{2,6},{4,0},{6,2},{1,5},{3,7},{5,1},{7,3},{8,12},{10,14},{12... | collective-permute-start | bytes 110600 | tf_op jit(solution)/shard_map/ppermute | solution.py:509
  83.5 4.9 %collective-permute-done.26.far_same = bf16[48,384]{1,0:T(8,128)(2,1)S(1)} collective-permute-done((bf16[48,384]{1,0:T(8,128)(2,1)S(1)}, bf16[48,384]{1,0:T(8,128)(2,1)S(1)}, u32[]{:S(2)}, u32[]{:S(2)}) %collective-permute-start.26) | collective-permute-done | bytes 36896 | tf_op jit(solution)/shard_map/ppermute | solution.py:509
  88.6 0.6 last_parts_value_out.1
  89.2 0.2 collective-permute-start.34
  89.4 0.3 collective-permute-start.27
  89.8 1.1 %collective-permute-start.33 = (bf16[24,1536]{1,0:T(8,128)(2,1)S(1)}, bf16[24,1536]{1,0:T(8,128)(2,1)S(1)}, u32[]{:S(2)}, u32[]{:S(2)}) collective-permute-start(bf16[24,1536]{1,0:T(8,128)(2,1)S(1)} %get-tuple-element.159), channel_id=1, source_target_pairs={{0,4},{2,6},{4,0},{6,2},{1,5},{3,7},{5,1},{7,3},{8,12},{10,14},{12... | collective-permute-start | bytes 221192 | tf_op jit(solution)/shard_map/ppermute | solution.py:509
  90.9 1.3 %collective-permute-start.35 = (bf16[24,1536]{1,0:T(8,128)(2,1)S(1)}, bf16[24,1536]{1,0:T(8,128)(2,1)S(1)}, u32[]{:S(2)}, u32[]{:S(2)}) collective-permute-start(bf16[24,1536]{1,0:T(8,128)(2,1)S(1)} %get-tuple-element.161), channel_id=1, source_target_pairs={{0,5},{1,4},{2,7},{3,6},{4,1},{5,0},{6,3},{7,2},{8,13},{9,12},{10,... | collective-permute-start | bytes 221192 | tf_op jit(solution)/shard_map/ppermute | solution.py:510
  92.2 1.2 %last_sum_key.1 = f32[48,768]{1,0:T(8,128)} custom-call(s32[5]{0:T(128)S(1)} %stack.23.scalars, f32[48,384]{1,0:T(8,128)S(1)} %get-tuple-element.144.mine, bf16[48,384]{1,0:T(8,128)(2,1)S(1)} %collective-permute-done.26.far_same, f32[48,384]{1,0:T(8,128)S(1)} %collective-permute-done.27.near_cross, bf16[48,384]{1,0:T(8,128)(2,1)S(1)} %collective-permute-done.28.far_cross), custom_call_target="tpu_custom_call" | custom-call | flops 1 | bytes 1 | tf_op jit(solution)/shard_map/last_sum_key/pallas_call | solution.py:428
  93.4 4.1 %collective-permute-done.33.far_same = bf16[24,1536]{1,0:T(8,128)(2,1)S(1)} collective-permute-done((bf16[24,1536]{1,0:T(8,128)(2,1)S(1)}, bf16[24,1536]{1,0:T(8,128)(2,1)S(1)}, u32[]{:S(2)}, u32[]{:S(2)}) %collective-permute-start.33) | collective-permute-done | bytes 73760 | tf_op jit(solution)/shard_map/ppermute | solution.py:509
  97.5 1.3 %collective-permute-done.35.far_cross = bf16[24,1536]{1,0:T(8,128)(2,1)S(1)} collective-permute-done((bf16[24,1536]{1,0:T(8,128)(2,1)S(1)}, bf16[24,1536]{1,0:T(8,128)(2,1)S(1)}, u32[]{:S(2)}, u32[]{:S(2)}) %collective-permute-start.35) | collective-permute-done | bytes 73760 | tf_op jit(solution)/shard_map/ppermute | solution.py:510
  98.8 1.3 %last_sum_value_out.1 = (f32[48,768]{1,0:T(8,128)}, f32[24,1536]{1,0:T(8,128)}) custom-call(s32[5]{0:T(128)S(1)} %stack.23.scalars, f32[24,1536]{1,0:T(8,128)S(1)} %get-tuple-element.158.mine, bf16[24,1536]{1,0:T(8,128)(2,1)S(1)} %collective-permute-done.33.far_same, f32[24,1536]{1,0:T(8,128)S(1)} %collective-permute-done.34.near_cross, ...), custom_call_target="tpu_custom_call" | custom-call | flops 1 | bytes 1 | tf_op jit(solution)/shard_map/last_sum_value_out/pallas_call | solution.py:428
  (46 shorter events, 0.8 us)
Async XLA Ops:
  1.4 6.9 %copy-start.4 = (bf16[1,4,1,32,1536]{4,3,2,1,0:T(8,128)(2,1)S(1)}, bf16[1,4,1,32,1536]{4,3,2,1,0:T(8,128)(2,1)}, u32[]{:S(2)}) copy-start(bf16[1,4,1,32,1536]{4,3,2,1,0:T(8,128)(2,1)} %param.10) | copy-start | bytes 1179652
  1.4 6.9 %copy-start.5 = (bf16[1,4,1,32,1536]{4,3,2,1,0:T(8,128)(2,1)S(1)}, bf16[1,4,1,32,1536]{4,3,2,1,0:T(8,128)(2,1)}, u32[]{:S(2)}) copy-start(bf16[1,4,1,32,1536]{4,3,2,1,0:T(8,128)(2,1)} %param.18) | copy-start | bytes 1179652
  2.6 6.3 %collective-permute-start = (s32[4]{0:T(128)S(1)}, s32[4]{0:T(128)S(1)}, u32[]{:S(2)}, u32[]{:S(2)}) collective-permute-start(s32[4]{0:T(128)S(1)} %get-tuple-element.84), channel_id=1, source_target_pairs={{0,2},{2,0},{4,6},{6,4},{1,3},{3,1},{5,7},{7,5},{8,10},{10,8},{12,... | collective-permute-start | bytes 56 | tf_op jit(solution)/shard_map/ppermute | solution.py:390
  5.7 4.4 %collective-permute-start.1 = (s32[4]{0:T(128)S(1)}, s32[4]{0:T(128)S(1)}, u32[]{:S(2)}, u32[]{:S(2)}) collective-permute-start(s32[4]{0:T(128)S(1)} %get-tuple-element.84), channel_id=1, source_target_pairs={{0,4},{2,6},{4,0},{6,2},{1,5},{3,7},{5,1},{7,3},{8,12},{10,14},{12... | collective-permute-start | bytes 56 | tf_op jit(solution)/shard_map/ppermute | solution.py:390
  8.3 5.3 %collective-permute-start.2 = (s32[4]{0:T(128)S(1)}, s32[4]{0:T(128)S(1)}, u32[]{:S(2)}, u32[]{:S(2)}) collective-permute-start(s32[4]{0:T(128)S(1)} %get-tuple-element.84), channel_id=1, source_target_pairs={{0,6},{2,4},{4,2},{6,0},{1,7},{3,5},{5,3},{7,1},{8,14},{10,12},{12... | collective-permute-start | bytes 56 | tf_op jit(solution)/shard_map/ppermute | solution.py:390
  8.3 10.4 %collective-permute-start.6 = (bf16[4,32,1536]{2,1,0:T(8,128)(2,1)S(1)}, bf16[4,32,1536]{2,1,0:T(8,128)(2,1)S(1)}, u32[]{:S(2)}, u32[]{:S(2)}) collective-permute-start(bf16[4,32,1536]{2,1,0:T(8,128)(2,1)S(1)} %bitcast.7), channel_id=1, source_target_pairs={{0,1},{1,0},{2,3},{3,2},{4,5},{5,4},{6,7},{7,6},{8,9},{9,8},{10,11... | collective-permute-start | bytes 1179656 | tf_op jit(solution)/shard_map/ppermute | solution.py:394
  8.3 10.4 %collective-permute-start.7 = (bf16[4,32,1536]{2,1,0:T(8,128)(2,1)S(1)}, bf16[4,32,1536]{2,1,0:T(8,128)(2,1)S(1)}, u32[]{:S(2)}, u32[]{:S(2)}) collective-permute-start(bf16[4,32,1536]{2,1,0:T(8,128)(2,1)S(1)} %bitcast.10), channel_id=1, source_target_pairs={{0,1},{1,0},{2,3},{3,2},{4,5},{5,4},{6,7},{7,6},{8,9},{9,8},{10,11... | collective-permute-start | bytes 1179656 | tf_op jit(solution)/shard_map/ppermute | solution.py:395
  8.9 9.8 %copy-start = (bf16[1536,768]{1,0:T(8,128)(2,1)S(1)}, bf16[1536,768]{1,0:T(8,128)(2,1)}, u32[]{:S(2)}) copy-start(bf16[1536,768]{1,0:T(8,128)(2,1)} %refs_11_.1) | copy-start | bytes 7077892
  8.9 9.8 %copy-start.1 = (bf16[1536,768]{1,0:T(8,128)(2,1)S(1)}, bf16[1536,768]{1,0:T(8,128)(2,1)}, u32[]{:S(2)}) copy-start(bf16[1536,768]{1,0:T(8,128)(2,1)} %refs_12_.1) | copy-start | bytes 7077892
  8.9 9.8 %copy-start.2 = (bf16[1536,768]{1,0:T(8,128)(2,1)S(1)}, bf16[1536,768]{1,0:T(8,128)(2,1)}, u32[]{:S(2)}) copy-start(bf16[1536,768]{1,0:T(8,128)(2,1)} %w_query.1) | copy-start | bytes 7077892
  8.9 9.8 %copy-start.3 = (bf16[768,1536]{1,0:T(8,128)(2,1)S(1)}, bf16[768,1536]{1,0:T(8,128)(2,1)}, u32[]{:S(2)}) copy-start(bf16[768,1536]{1,0:T(8,128)(2,1)} %w_out.1) | copy-start | bytes 7077892
  8.9 9.8 %copy-start.6 = (bf16[9,1536]{1,0:T(8,128)(2,1)S(1)}, bf16[9,1536]{1,0:T(8,128)(2,1)}, u32[]{:S(2)}) copy-start(bf16[9,1536]{1,0:T(8,128)(2,1)} %taps.1) | copy-start | bytes 82948
  8.9 9.8 %copy-start.7 = (f32[1536]{0:T(1024)S(1)}, f32[1536]{0:T(1024)}, u32[]{:S(2)}) copy-start(f32[1536]{0:T(1024)} %refs_10_.1) | copy-start | bytes 18436
  14.2 8.2 %collective-permute-start.3 = (bf16[32,1536]{1,0:T(8,128)(2,1)S(1)}, bf16[32,1536]{1,0:T(8,128)(2,1)S(1)}, u32[]{:S(2)}, u32[]{:S(2)}) collective-permute-start(bf16[32,1536]{1,0:T(8,128)(2,1)S(1)} %get-tuple-element.85), channel_id=1, source_target_pairs={{0,2},{2,0},{4,6},{6,4},{1,3},{3,1},{5,7},{7,5},{8,10},{10,8},{12,... | collective-permute-start | bytes 294920 | tf_op jit(solution)/shard_map/ppermute | solution.py:406
  14.3 9.1 %collective-permute-start.4 = (bf16[32,1536]{1,0:T(8,128)(2,1)S(1)}, bf16[32,1536]{1,0:T(8,128)(2,1)S(1)}, u32[]{:S(2)}, u32[]{:S(2)}) collective-permute-start(bf16[32,1536]{1,0:T(8,128)(2,1)S(1)} %get-tuple-element.86), channel_id=1, source_target_pairs={{0,4},{2,6},{4,0},{6,2},{1,5},{3,7},{5,1},{7,3},{8,12},{10,14},{12... | collective-permute-start | bytes 294920 | tf_op jit(solution)/shard_map/ppermute | solution.py:406
  14.9 8.5 %collective-permute-start.5 = (bf16[32,1536]{1,0:T(8,128)(2,1)S(1)}, bf16[32,1536]{1,0:T(8,128)(2,1)S(1)}, u32[]{:S(2)}, u32[]{:S(2)}) collective-permute-start(bf16[32,1536]{1,0:T(8,128)(2,1)S(1)} %get-tuple-element.87), channel_id=1, source_target_pairs={{0,6},{2,4},{4,2},{6,0},{1,7},{3,5},{5,3},{7,1},{8,14},{10,12},{12... | collective-permute-start | bytes 294920 | tf_op jit(solution)/shard_map/ppermute | solution.py:406
  23.4 1.3 %collective-permute-start.8 = (bf16[32,1536]{1,0:T(8,128)(2,1)S(1)}, bf16[32,1536]{1,0:T(8,128)(2,1)S(1)}, u32[]{:S(2)}, u32[]{:S(2)}) collective-permute-start(bf16[32,1536]{1,0:T(8,128)(2,1)S(1)} %collective-permute-done.3.refs_0_), channel_id=1, source_target_pairs={{0,1},{1,0},{2,3},{3,2},{4,5},{5,4},{6,7},{7,6},{8,9},{9,8},{10,11... | collective-permute-start | bytes 294920 | tf_op jit(solution)/shard_map/ppermute | solution.py:425
  23.4 1.5 %collective-permute-start.9 = (bf16[32,1536]{1,0:T(8,128)(2,1)S(1)}, bf16[32,1536]{1,0:T(8,128)(2,1)S(1)}, u32[]{:S(2)}, u32[]{:S(2)}) collective-permute-start(bf16[32,1536]{1,0:T(8,128)(2,1)S(1)} %collective-permute-done.4.refs_1_), channel_id=1, source_target_pairs={{0,1},{1,0},{2,3},{3,2},{4,5},{5,4},{6,7},{7,6},{8,9},{9,8},{10,11... | collective-permute-start | bytes 294920 | tf_op jit(solution)/shard_map/ppermute | solution.py:425
  23.9 1.3 %collective-permute-start.10 = (bf16[32,1536]{1,0:T(8,128)(2,1)S(1)}, bf16[32,1536]{1,0:T(8,128)(2,1)S(1)}, u32[]{:S(2)}, u32[]{:S(2)}) collective-permute-start(bf16[32,1536]{1,0:T(8,128)(2,1)S(1)} %collective-permute-done.5.refs_2_), channel_id=1, source_target_pairs={{0,1},{1,0},{2,3},{3,2},{4,5},{5,4},{6,7},{7,6},{8,9},{9,8},{10,11... | collective-permute-start | bytes 294920 | tf_op jit(solution)/shard_map/ppermute | solution.py:425
  28.6 2.0 %collective-permute-start.11 = (bf16[256,384]{1,0:T(8,128)(2,1)S(1)}, bf16[256,384]{1,0:T(8,128)(2,1)S(1)}, u32[]{:S(2)}, u32[]{:S(2)}) collective-permute-start(bf16[256,384]{1,0:T(8,128)(2,1)S(1)} %get-tuple-element.107.mine), channel_id=1, source_target_pairs={{0,1},{1,0},{2,3},{3,2},{4,5},{5,4},{6,7},{7,6},{8,9},{9,8},{10,11... | collective-permute-start | bytes 589832 | tf_op jit(solution)/shard_map/ppermute | solution.py:459
  32.7 32.1 %collective-permute-start.24 = (bf16[2,2,2,48,1536]{4,3,2,1,0:T(8,128)(2,1)S(1)}, bf16[2,2,2,48,1536]{4,3,2,1,0:T(8,128)(2,1)S(1)}, u32[]{:S(2)}, u32[]{:S(2)}) collective-permute-start(bf16[2,2,2,48,1536]{4,3,2,1,0:T(8,128)(2,1)S(1)} %get-tuple-element.109), channel_id=1, source_target_pairs={{0,2},{2,0},{4,6},{6,4},{1,3},{3,1},{5,7},{7,5},{8,10},{10,8},{12,... | collective-permute-start | bytes 3538952 | tf_op jit(solution)/shard_map/ppermute | solution.py:523
  35.5 9.9 %collective-permute-start.12 = (bf16[2,192,384]{2,1,0:T(8,128)(2,1)S(1)}, bf16[2,192,384]{2,1,0:T(8,128)(2,1)S(1)}, u32[]{:S(2)}, u32[]{:S(2)}) collective-permute-start(bf16[2,192,384]{2,1,0:T(8,128)(2,1)S(1)} %get-tuple-element.112), channel_id=1, source_target_pairs={{0,8},{8,0},{16,24},{24,16},{1,9},{9,1},{17,25},{25,17},{2,10},{10... | collective-permute-start | bytes 884744 | tf_op jit(solution)/shard_map/ppermute | solution.py:476
  37.1 9.9 %collective-permute-start.13 = (bf16[2,192,384]{2,1,0:T(8,128)(2,1)S(1)}, bf16[2,192,384]{2,1,0:T(8,128)(2,1)S(1)}, u32[]{:S(2)}, u32[]{:S(2)}) collective-permute-start(bf16[2,192,384]{2,1,0:T(8,128)(2,1)S(1)} %get-tuple-element.114), channel_id=1, source_target_pairs={{0,16},{8,24},{16,0},{24,8},{1,17},{9,25},{17,1},{25,9},{2,18},{10... | collective-permute-start | bytes 884744 | tf_op jit(solution)/shard_map/ppermute | solution.py:476
  40.2 11.6 %collective-permute-start.14 = (bf16[2,192,384]{2,1,0:T(8,128)(2,1)S(1)}, bf16[2,192,384]{2,1,0:T(8,128)(2,1)S(1)}, u32[]{:S(2)}, u32[]{:S(2)}) collective-permute-start(bf16[2,192,384]{2,1,0:T(8,128)(2,1)S(1)} %get-tuple-element.120), channel_id=1, source_target_pairs={{0,8},{8,0},{16,24},{24,16},{1,9},{9,1},{17,25},{25,17},{2,10},{10... | collective-permute-start | bytes 884744 | tf_op jit(solution)/shard_map/ppermute | solution.py:476
  40.8 12.5 %collective-permute-start.15 = (bf16[2,192,384]{2,1,0:T(8,128)(2,1)S(1)}, bf16[2,192,384]{2,1,0:T(8,128)(2,1)S(1)}, u32[]{:S(2)}, u32[]{:S(2)}) collective-permute-start(bf16[2,192,384]{2,1,0:T(8,128)(2,1)S(1)} %get-tuple-element.122), channel_id=1, source_target_pairs={{0,16},{8,24},{16,0},{24,8},{1,17},{9,25},{17,1},{25,9},{2,18},{10... | collective-permute-start | bytes 884744 | tf_op jit(solution)/shard_map/ppermute | solution.py:476
  47.1 9.4 %collective-permute-start.16 = (bf16[192,384]{1,0:T(8,128)(2,1)S(1)}, bf16[192,384]{1,0:T(8,128)(2,1)S(1)}, u32[]{:S(2)}, u32[]{:S(2)}) collective-permute-start(bf16[192,384]{1,0:T(8,128)(2,1)S(1)} %get-tuple-element.118), channel_id=1, source_target_pairs={{0,16},{8,24},{16,0},{24,8},{1,17},{9,25},{17,1},{25,9},{2,18},{10... | collective-permute-start | bytes 442376 | tf_op jit(solution)/shard_map/ppermute | solution.py:484
  48.7 7.8 %collective-permute-start.17 = (bf16[192,384]{1,0:T(8,128)(2,1)S(1)}, bf16[192,384]{1,0:T(8,128)(2,1)S(1)}, u32[]{:S(2)}, u32[]{:S(2)}) collective-permute-start(bf16[192,384]{1,0:T(8,128)(2,1)S(1)} %get-tuple-element.126), channel_id=1, source_target_pairs={{0,8},{8,0},{16,24},{24,16},{1,9},{9,1},{17,25},{25,17},{2,10},{10... | collective-permute-start | bytes 442376 | tf_op jit(solution)/shard_map/ppermute | solution.py:484
  53.4 5.2 %collective-permute-start.18 = (bf16[192,384]{1,0:T(8,128)(2,1)S(1)}, bf16[192,384]{1,0:T(8,128)(2,1)S(1)}, u32[]{:S(2)}, u32[]{:S(2)}) collective-permute-start(bf16[192,384]{1,0:T(8,128)(2,1)S(1)} %get-tuple-element.123), channel_id=1, source_target_pairs={{0,16},{8,24},{16,0},{24,8},{1,17},{9,25},{17,1},{25,9},{2,18},{10... | collective-permute-start | bytes 442376 | tf_op jit(solution)/shard_map/ppermute | solution.py:484
  55.0 5.1 %collective-permute-start.19 = (bf16[192,384]{1,0:T(8,128)(2,1)S(1)}, bf16[192,384]{1,0:T(8,128)(2,1)S(1)}, u32[]{:S(2)}, u32[]{:S(2)}) collective-permute-start(bf16[192,384]{1,0:T(8,128)(2,1)S(1)} %get-tuple-element.131), channel_id=1, source_target_pairs={{0,8},{8,0},{16,24},{24,16},{1,9},{9,1},{17,25},{25,17},{2,10},{10... | collective-permute-start | bytes 442376 | tf_op jit(solution)/shard_map/ppermute | solution.py:484
  57.1 7.1 %collective-permute-start.20 = (bf16[2,96,384]{2,1,0:T(8,128)(2,1)S(1)}, bf16[2,96,384]{2,1,0:T(8,128)(2,1)S(1)}, u32[]{:S(2)}, u32[]{:S(2)}) collective-permute-start(bf16[2,96,384]{2,1,0:T(8,128)(2,1)S(1)} %get-tuple-element.134), channel_id=1, source_target_pairs={{0,2},{2,0},{4,6},{6,4},{1,3},{3,1},{5,7},{7,5},{8,10},{10,8},{12,... | collective-permute-start | bytes 442376 | tf_op jit(solution)/shard_map/ppermute | solution.py:538
  65.0 16.2 %collective-permute-start.29 = (bf16[2,2,48,768]{3,2,1,0:T(8,128)(2,1)S(1)}, bf16[2,2,48,768]{3,2,1,0:T(8,128)(2,1)S(1)}, u32[]{:S(2)}, u32[]{:S(2)}) collective-permute-start(bf16[2,2,48,768]{3,2,1,0:T(8,128)(2,1)S(1)} %get-tuple-element.141), channel_id=1, source_target_pairs={{0,8},{8,0},{16,24},{24,16},{1,9},{9,1},{17,25},{25,17},{2,10},{10... | collective-permute-start | bytes 884744 | tf_op jit(solution)/shard_map/ppermute | solution.py:476
  66.6 14.6 %collective-permute-start.30 = (bf16[2,2,48,768]{3,2,1,0:T(8,128)(2,1)S(1)}, bf16[2,2,48,768]{3,2,1,0:T(8,128)(2,1)S(1)}, u32[]{:S(2)}, u32[]{:S(2)}) collective-permute-start(bf16[2,2,48,768]{3,2,1,0:T(8,128)(2,1)S(1)} %get-tuple-element.151), channel_id=1, source_target_pairs={{0,16},{8,24},{16,0},{24,8},{1,17},{9,25},{17,1},{25,9},{2,18},{10... | collective-permute-start | bytes 884744 | tf_op jit(solution)/shard_map/ppermute | solution.py:476
  68.1 12.5 %collective-permute-start.25 = (bf16[2,96,384]{2,1,0:T(8,128)(2,1)S(1)}, bf16[2,96,384]{2,1,0:T(8,128)(2,1)S(1)}, u32[]{:S(2)}, u32[]{:S(2)}) collective-permute-start(bf16[2,96,384]{2,1,0:T(8,128)(2,1)S(1)} %get-tuple-element.143), channel_id=1, source_target_pairs={{0,2},{2,0},{4,6},{6,4},{1,3},{3,1},{5,7},{7,5},{8,10},{10,8},{12,... | collective-permute-start | bytes 442376 | tf_op jit(solution)/shard_map/ppermute | solution.py:538
  69.7 5.3 %collective-permute-start.21 = (bf16[48,384]{1,0:T(8,128)(2,1)S(1)}, bf16[48,384]{1,0:T(8,128)(2,1)S(1)}, u32[]{:S(2)}, u32[]{:S(2)}) collective-permute-start(bf16[48,384]{1,0:T(8,128)(2,1)S(1)} %get-tuple-element.136), channel_id=1, source_target_pairs={{0,4},{2,6},{4,0},{6,2},{1,5},{3,7},{5,1},{7,3},{8,12},{10,14},{12... | collective-permute-start | bytes 110600 | tf_op jit(solution)/shard_map/ppermute | solution.py:509
  70.5 8.9 %collective-permute-start.22 = (f32[48,384]{1,0:T(8,128)S(1)}, f32[48,384]{1,0:T(8,128)S(1)}, u32[]{:S(2)}, u32[]{:S(2)}) collective-permute-start(f32[48,384]{1,0:T(8,128)S(1)} %get-tuple-element.137), channel_id=1, source_target_pairs={{0,1},{1,0},{2,3},{3,2},{4,5},{5,4},{6,7},{7,6},{8,9},{9,8},{10,11... | collective-permute-start | bytes 221192 | tf_op jit(solution)/shard_map/ppermute | solution.py:511
  75.0 4.4 %collective-permute-start.23 = (bf16[48,384]{1,0:T(8,128)(2,1)S(1)}, bf16[48,384]{1,0:T(8,128)(2,1)S(1)}, u32[]{:S(2)}, u32[]{:S(2)}) collective-permute-start(bf16[48,384]{1,0:T(8,128)(2,1)S(1)} %get-tuple-element.138), channel_id=1, source_target_pairs={{0,5},{1,4},{2,7},{3,6},{4,1},{5,0},{6,3},{7,2},{8,13},{9,12},{10,... | collective-permute-start | bytes 110600 | tf_op jit(solution)/shard_map/ppermute | solution.py:510
  81.4 7.2 %collective-permute-start.31 = (bf16[2,48,768]{2,1,0:T(8,128)(2,1)S(1)}, bf16[2,48,768]{2,1,0:T(8,128)(2,1)S(1)}, u32[]{:S(2)}, u32[]{:S(2)}) collective-permute-start(bf16[2,48,768]{2,1,0:T(8,128)(2,1)S(1)} %get-tuple-element.154), channel_id=1, source_target_pairs={{0,8},{8,0},{16,24},{24,16},{1,9},{9,1},{17,25},{25,17},{2,10},{10... | collective-permute-start | bytes 442376 | tf_op jit(solution)/shard_map/ppermute | solution.py:484
  82.0 6.6 %collective-permute-start.32 = (bf16[2,48,768]{2,1,0:T(8,128)(2,1)S(1)}, bf16[2,48,768]{2,1,0:T(8,128)(2,1)S(1)}, u32[]{:S(2)}, u32[]{:S(2)}) collective-permute-start(bf16[2,48,768]{2,1,0:T(8,128)(2,1)S(1)} %get-tuple-element.156), channel_id=1, source_target_pairs={{0,16},{8,24},{16,0},{24,8},{1,17},{9,25},{17,1},{25,9},{2,18},{10... | collective-permute-start | bytes 442376 | tf_op jit(solution)/shard_map/ppermute | solution.py:484
  82.5 6.0 %collective-permute-start.26 = (bf16[48,384]{1,0:T(8,128)(2,1)S(1)}, bf16[48,384]{1,0:T(8,128)(2,1)S(1)}, u32[]{:S(2)}, u32[]{:S(2)}) collective-permute-start(bf16[48,384]{1,0:T(8,128)(2,1)S(1)} %get-tuple-element.145), channel_id=1, source_target_pairs={{0,4},{2,6},{4,0},{6,2},{1,5},{3,7},{5,1},{7,3},{8,12},{10,14},{12... | collective-permute-start | bytes 110600 | tf_op jit(solution)/shard_map/ppermute | solution.py:509
  83.5 5.0 %collective-permute-start.28 = (bf16[48,384]{1,0:T(8,128)(2,1)S(1)}, bf16[48,384]{1,0:T(8,128)(2,1)S(1)}, u32[]{:S(2)}, u32[]{:S(2)}) collective-permute-start(bf16[48,384]{1,0:T(8,128)(2,1)S(1)} %get-tuple-element.147), channel_id=1, source_target_pairs={{0,5},{1,4},{2,7},{3,6},{4,1},{5,0},{6,3},{7,2},{8,13},{9,12},{10,... | collective-permute-start | bytes 110600 | tf_op jit(solution)/shard_map/ppermute | solution.py:510
  89.2 9.6 %collective-permute-start.34 = (f32[24,1536]{1,0:T(8,128)S(1)}, f32[24,1536]{1,0:T(8,128)S(1)}, u32[]{:S(2)}, u32[]{:S(2)}) collective-permute-start(f32[24,1536]{1,0:T(8,128)S(1)} %get-tuple-element.160), channel_id=1, source_target_pairs={{0,1},{1,0},{2,3},{3,2},{4,5},{5,4},{6,7},{7,6},{8,9},{9,8},{10,11... | collective-permute-start | bytes 442376 | tf_op jit(solution)/shard_map/ppermute | solution.py:511
  89.4 2.8 %collective-permute-start.27 = (f32[48,384]{1,0:T(8,128)S(1)}, f32[48,384]{1,0:T(8,128)S(1)}, u32[]{:S(2)}, u32[]{:S(2)}) collective-permute-start(f32[48,384]{1,0:T(8,128)S(1)} %get-tuple-element.146), channel_id=1, source_target_pairs={{0,1},{1,0},{2,3},{3,2},{4,5},{5,4},{6,7},{7,6},{8,9},{9,8},{10,11... | collective-permute-start | bytes 221192 | tf_op jit(solution)/shard_map/ppermute | solution.py:511
  89.8 7.8 %collective-permute-start.33 = (bf16[24,1536]{1,0:T(8,128)(2,1)S(1)}, bf16[24,1536]{1,0:T(8,128)(2,1)S(1)}, u32[]{:S(2)}, u32[]{:S(2)}) collective-permute-start(bf16[24,1536]{1,0:T(8,128)(2,1)S(1)} %get-tuple-element.159), channel_id=1, source_target_pairs={{0,4},{2,6},{4,0},{6,2},{1,5},{3,7},{5,1},{7,3},{8,12},{10,14},{12... | collective-permute-start | bytes 221192 | tf_op jit(solution)/shard_map/ppermute | solution.py:509
  90.9 7.9 %collective-permute-start.35 = (bf16[24,1536]{1,0:T(8,128)(2,1)S(1)}, bf16[24,1536]{1,0:T(8,128)(2,1)S(1)}, u32[]{:S(2)}, u32[]{:S(2)}) collective-permute-start(bf16[24,1536]{1,0:T(8,128)(2,1)S(1)} %get-tuple-element.161), channel_id=1, source_target_pairs={{0,5},{1,4},{2,7},{3,6},{4,1},{5,0},{6,3},{7,2},{8,13},{9,12},{10,... | collective-permute-start | bytes 221192 | tf_op jit(solution)/shard_map/ppermute | solution.py:510

commit v12 on v9

--- a/solution.py
+++ b/solution.py
@@ -63,9 +63,43 @@
     return pl.ds(pl.multiple_of(scalars[0] * size, size), size)
 
 
+def stacked(x, views):
+    tokens, pair = x.shape
+    low = (lax.broadcasted_iota(jnp.int32, (1, 1, pair), 2) < pair // 2).astype(x.dtype)
+    x = x.reshape(views, tokens // views, pair)
+    return jnp.concatenate((x * low, x * (1 - low)), axis=1).reshape(2 * tokens, pair)
+
+
+def unstacked(x, views):
+    rows, pair = x.shape
+    low = lax.broadcasted_iota(jnp.int32, (1, 1, pair), 2) < pair // 2
+    x = x.reshape(views, 2, rows // (2 * views), pair)
+    return jnp.where(low, x[:, 0], x[:, 1]).reshape(rows // 2, pair)
+
+
+def view_parts(x, views, axis):
+    size = x.shape[axis] // views
+    return [lax.slice_in_dim(x, u * size, (u + 1) * size, axis=axis) for u in range(views)]
+
+
+def own_nt(a, b, views):
+    pairs = zip(view_parts(a, views, 0), view_parts(b, views, 0))
+    return jnp.concatenate([dot_nt(x, y) for x, y in pairs], axis=1)
+
+
+def own_tn(a, b, views):
+    pairs = zip(view_parts(a, views, 1), view_parts(b, views, 0))
+    return jnp.concatenate([dot_tn(x, y) for x, y in pairs], axis=0)
+
+
+def own_nn(a, b, views):
+    pairs = zip(view_parts(a, views, 1), view_parts(b, views, 0))
+    return jnp.concatenate([dot_nn(x, y) for x, y in pairs], axis=0)
+
+
 def project_kernel(
     scalars, lat_own, lat_other, cot_own, cot_other, gain, taps, w_query, w_key, w_value, w_out,
-    normed, queries, keys, values, out_grad, upstream,
+    normed_t, keys, values, upstream, query_stack, grad_stack, scores_own, dprob_own, normed,
 ):
     views, strip, width = lat_own.shape
     scale = gain[...].reshape(1, width)
@@ -102,52 +136,28 @@
                     total = total + cross[half][b : b + 1] * shifted[1 - half][b]
                 upstream[strip_of(u, half), lanes] = total.astype(jnp.bfloat16)
     rows = normed[...]
-    half = core_half(scalars, queries.shape[1])
-    for weight, result in ((w_query, queries), (w_key, keys), (w_value, values)):
-        result[...] = dot_nn(rows, weight[:, half]).astype(jnp.bfloat16)
-    out_grad[...] = dot_nt(upstream[...], w_out[half, :]).astype(jnp.bfloat16)
-
-
-def stacked(x, views):
-    tokens, pair = x.shape
-    low = (lax.broadcasted_iota(jnp.int32, (1, 1, pair), 2) < pair // 2).astype(x.dtype)
-    x = x.reshape(views, tokens // views, pair)
-    return jnp.concatenate((x * low, x * (1 - low)), axis=1).reshape(2 * tokens, pair)
-
-
-def unstacked(x, views):
-    rows, pair = x.shape
-    low = lax.broadcasted_iota(jnp.int32, (1, 1, pair), 2) < pair // 2
-    x = x.reshape(views, 2, rows // (2 * views), pair)
-    return jnp.where(low, x[:, 0], x[:, 1]).reshape(rows // 2, pair)
-
-
-def view_parts(x, views, axis):
-    size = x.shape[axis] // views
-    return [lax.slice_in_dim(x, u * size, (u + 1) * size, axis=axis) for u in range(views)]
-
-
-def own_nt(a, b, views):
-    pairs = zip(view_parts(a, views, 0), view_parts(b, views, 0))
-    return jnp.concatenate([dot_nt(x, y) for x, y in pairs], axis=1)
-
-
-def own_tn(a, b, views):
-    pairs = zip(view_parts(a, views, 1), view_parts(b, views, 0))
-    return jnp.concatenate([dot_tn(x, y) for x, y in pairs], axis=0)
-
-
-def own_nn(a, b, views):
-    pairs = zip(view_parts(a, views, 1), view_parts(b, views, 0))
-    return jnp.concatenate([dot_nn(x, y) for x, y in pairs], axis=0)
+    normed_t[...] = rows.T
+    part = keys.shape[1]
+    half = core_half(scalars, part)
+    queries = dot_nn(rows, w_query[:, half]).astype(jnp.bfloat16)
+    keys[...] = dot_nn(rows, w_key[:, half]).astype(jnp.bfloat16)
+    values[...] = dot_nn(rows, w_value[:, half]).astype(jnp.bfloat16)
+    out_grad = dot_nt(upstream[...], w_out[half, :]).astype(jnp.bfloat16)
+    pair = 2 * HEAD_DIM
+    for p in range(part // pair):
+        lanes = slice(p * pair, (p + 1) * pair)
+        q, g = stacked(queries[:, lanes], views), stacked(out_grad[:, lanes], views)
+        query_stack[p], grad_stack[p] = q, g
+        scores_own[p] = own_nt(keys[:, lanes], q, views) * SCALE
+        dprob_own[p] = own_nt(values[:, lanes], g, views)
 
 
 def forward_kernel(views, groups, scalars, alive, *refs):
     got_own, got_other, refs = refs[: groups - 1], refs[groups - 1 : 2 * groups - 2], refs[2 * groups - 2 :]
-    queries, keys, values, out_grad, gain, w_key, w_value, *refs = refs
-    normed_far, keys_far, values_far, attention_own, attention_far, mixed, dvalue = refs
+    query_stack, grad_stack, scores_own, values, gain, w_key, w_value, *refs = refs
+    normed_far_t, keys_far, values_far, attention_own, attention_far, mixed_t, dvalue, normed_far = refs
     strip = got_own[0].shape[0]
-    tokens, part = queries.shape
+    tokens, part = values.shape
     view_tokens = tokens // views
     here = scalars[1]
     scale_row = gain[...].reshape(1, normed_far.shape[1])
@@ -165,13 +175,13 @@
             taken = jnp.where(column_view == u, alive[group * views + u], taken)
         slot_alive.append(taken > 0)
     fetched = normed_far[...]
+    normed_far_t[...] = fetched.T
     half = core_half(scalars, part)
     keys_far[...] = dot_nn(fetched, w_key[:, half]).astype(jnp.bfloat16)
     values_far[...] = dot_nn(fetched, w_value[:, half]).astype(jnp.bfloat16)
     for p in range(part // pair):
         lanes = slice(p * pair, (p + 1) * pair)
-        q, g = stacked(queries[:, lanes], views), stacked(out_grad[:, lanes], views)
-        s_own = own_nt(keys[:, lanes], q, views) * SCALE
+        q, g, s_own = query_stack[p], grad_stack[p], scores_own[p]
         s_far = dot_nt(keys_far[:, lanes], q) * SCALE
         s_far = jnp.concatenate(
             [
@@ -188,21 +198,20 @@
         attention_own[p], attention_far[p] = a_own, a_far
         a_own, a_far = a_own.astype(jnp.bfloat16), a_far.astype(jnp.bfloat16)
         mix = own_tn(a_own, values[:, lanes], views) + dot_tn(a_far, values_far[:, lanes])
-        mixed[:, lanes] = unstacked(mix, views).astype(jnp.bfloat16)
+        mixed_t[lanes, :] = unstacked(mix, views).T.astype(jnp.bfloat16)
         dvalue[:tokens, lanes] = own_nn(a_own, g, views).astype(jnp.bfloat16)
         dvalue[tokens:, lanes] = dot_nn(a_far, g).astype(jnp.bfloat16)
 
 
 def backward_kernel(
-    views, queries, keys, values, out_grad, keys_far, values_far, attention_own, attention_far, dquery, dkey
+    views, query_stack, grad_stack, dprob_own, keys, keys_far, values_far, attention_own, attention_far, dquery, dkey
 ):
-    tokens, part = queries.shape
+    tokens, part = keys.shape
     pair = 2 * HEAD_DIM
     for p in range(part // pair):
         lanes = slice(p * pair, (p + 1) * pair)
-        q, g = stacked(queries[:, lanes], views), stacked(out_grad[:, lanes], views)
+        q, g, dp_own = query_stack[p], grad_stack[p], dprob_own[p]
         a_own, a_far = attention_own[p], attention_far[p]
-        dp_own = own_nt(values[:, lanes], g, views)
         dp_far = dot_nt(values_far[:, lanes], g)
         delta = jnp.sum(a_own * dp_own, 0, keepdims=True) + jnp.sum(a_far * dp_far, 0, keepdims=True)
         ds_own = (a_own * (dp_own - delta) * SCALE).astype(jnp.bfloat16)
@@ -213,6 +222,14 @@
         dkey[tokens:, lanes] = dot_nn(ds_far, q).astype(jnp.bfloat16)
 
 
+def times(lefts, right):
+    total, start = 0.0, 0
+    for left in lefts:
+        total = total + dot_nn(left, right[start : start + left.shape[1], :])
+        start += left.shape[1]
+    return total
+
+
 def by_quarters(scalars, lefts, right, send, keep, x_first):
     size = send.shape[1]
     x, y = scalars[3], scalars[4]
@@ -220,45 +237,48 @@
         for second in (1, 0):
             dx, dy = (first, second) if x_first else (second, first)
             block = 2 * lax.bitwise_xor(y, jnp.int32(dy)) + lax.bitwise_xor(x, jnp.int32(dx))
-            columns = pl.ds(pl.multiple_of(block * size, size), size)
-            total, start = 0.0, 0
-            for left in lefts:
-                total = total + dot_tn(left[:, columns], right[start : start + left.shape[0], :])
-                start += left.shape[0]
-            target[second] = total.astype(target.dtype)
-
-
-def query_key_kernel(scalars, normed, normed_far, dquery, dkey, q_send, k_send, q_keep, k_keep):
-    by_quarters(scalars, (normed,), dquery, q_send, q_keep, True)
-    by_quarters(scalars, (normed, normed_far), dkey, k_send, k_keep, False)
-
-
-def value_out_kernel(scalars, normed, normed_far, dvalue, mine, theirs, upstream, send, keep):
+            rows = pl.ds(pl.multiple_of(block * size, size), size)
+            target[second] = times([left[rows, :] for left in lefts], right).astype(target.dtype)
+
+
+def query_key_kernel(scalars, normed_t, normed_far_t, dquery, dkey, q_send, k_send, q_keep, k_keep):
+    by_quarters(scalars, (normed_t,), dquery, q_send, q_keep, True)
+    by_quarters(scalars, (normed_t, normed_far_t), dkey, k_send, k_keep, False)
+
+
+def value_out_kernel(scalars, normed_t, normed_far_t, dvalue, mine, theirs, upstream, send, keep):
     row, x, y = scalars[0], scalars[3], scalars[4]
     odd = lax.rem(scalars[1], jnp.int32(2)) == 1
     _, _, pairs, size, width = send.shape
     half, quarter = width // 2, width // 4
-    right = upstream[:, core_half(scalars, half)]
-    from_mine, from_theirs = dot_tn(mine[...], right), dot_tn(theirs[...], right)
+    places = [(dy, dx, pair) for dy in range(2) for dx in range(2) for pair in range(pairs)]
+    rows = {"send": ([], [], []), "keep": ([], [], [])}
     for dy in range(2):
-        grad_o = jnp.where(row == lax.bitwise_xor(y, jnp.int32(dy)), from_mine, from_theirs)
-        low, high = grad_o[: 2 * pairs * size], grad_o[2 * pairs * size :]
+        to_y = lax.bitwise_xor(y, jnp.int32(dy))
         for dx in range(2):
             to_x = lax.bitwise_xor(x, jnp.int32(dx))
-            o_part = jnp.where(to_x == 0, low, high)
-            block = 2 * lax.bitwise_xor(y, jnp.int32(dy)) + to_x
-            columns = pl.ds(pl.multiple_of(block * quarter, quarter), quarter)
-            tokens = normed.shape[0]
-            v_part = dot_tn(normed[:, columns], dvalue[:tokens, :])
-            v_part = v_part + dot_tn(normed_far[:, columns], dvalue[tokens:, :])
+            out_rows = pl.ds(pl.multiple_of(to_x * (half // 4), half // 4), half // 4)
+            out_block = jnp.where(row == to_y, mine[out_rows, :], theirs[out_rows, :])
+            value_rows = pl.ds(pl.multiple_of((2 * to_y + to_x) * quarter, quarter), quarter)
+            blocks = (normed_t[value_rows, :], normed_far_t[value_rows, :], out_block)
             for pair in range(pairs):
-                tiles = []
-                for view in (2 * pair, 2 * pair + 1):
-                    v_view = v_part[2 * view * size : 2 * (view + 1) * size]
-                    tiles.append((o_part[view * size : (view + 1) * size], v_view[:size], v_view[size:]))
-                for target, take_odd in ((send, jnp.logical_not(odd)), (keep, odd)):
-                    tile = [jnp.where(take_odd, second, first) for first, second in zip(*tiles)]
-                    target[dy, dx, pair] = jnp.concatenate(tile, axis=1).astype(target.dtype)
+                for i, block in enumerate(blocks):
+                    count = size if i == 2 else 2 * size
+                    first = block[2 * pair * count : (2 * pair + 1) * count]
+                    second = block[(2 * pair + 1) * count : (2 * pair + 2) * count]
+                    rows["send"][i].append(jnp.where(odd, first, second))
+                    rows["keep"][i].append(jnp.where(odd, second, first))
+    right = upstream[:, core_half(scalars, half)]
+    for target, name in ((send, "send"), (keep, "keep")):
+        own, far, out = [jnp.concatenate(parts, axis=0) for parts in rows[name]]
+        grad_v = times((own, far), dvalue).astype(target.dtype)
+        grad_o = dot_nn(out, right).astype(target.dtype)
+        for i, place in enumerate(places):
+            target[(*place, slice(None), slice(0, half))] = grad_o[i * size : (i + 1) * size]
+            for core in range(2):
+                columns = slice(half + core * quarter, half + (core + 1) * quarter)
+                part = grad_v[(2 * i + core) * size : (2 * i + core + 1) * size]
+                target[(*place, slice(None), columns)] = part
 
 
 def view_sum_kernel(keep, got, x_send, y_send, x_keep, y_keep):
@@ -399,24 +419,28 @@
         name="pick",
     )(scalars, *granted, lat)
     got_own = [lax.ppermute(part_out, "view", pairs) for part_out, pairs in zip(outgoing, between)]
-    normed, queries, keys, values, out_grad, upstream = pl.pallas_call(
+    head_pairs = part // (2 * HEAD_DIM)
+    normed_t, keys, values, upstream, query_stack, grad_stack, scores_own, dprob_own = pl.pallas_call(
         project_kernel,
         in_specs=[SMEM] + [VMEM] * 10,
-        out_specs=[VMEM] * 6,
+        out_specs=[VMEM] * 8,
         out_shape=[
-            shape((tokens, width), bf16),
-            shape((tokens, part), bf16),
-            shape((tokens, part), bf16),
+            shape((width, tokens), bf16),
             shape((tokens, part), bf16),
             shape((tokens, part), bf16),
             shape((tokens, width), bf16),
+            shape((head_pairs, 2 * tokens, 2 * HEAD_DIM), bf16),
+            shape((head_pairs, 2 * tokens, 2 * HEAD_DIM), bf16),
+            shape((head_pairs, 2 * strip, 2 * tokens), f32),
+            shape((head_pairs, 2 * strip, 2 * tokens), f32),
         ],
+        scratch_shapes=[pltpu.VMEM((tokens, width), bf16)],
         compiler_params=params(28),
         cost_estimate=LITTLE,
         name="project",
     )(scalars, lat, lat_other, cot, cot_other, norm_gain, kernel, w_query, w_key, w_value, w_out)
 
-    got_own, normed = lax.optimization_barrier((got_own, normed))
+    got_own, normed_t = lax.optimization_barrier((got_own, normed_t))
     got_other = [lax.ppermute(got, "row", swap) for got in got_own]
 
     def call(kernel_body, results, operands, name, first=VMEM, mebibytes=16, cost=LITTLE):
@@ -431,31 +455,32 @@
         )(*operands)
         return list(outputs)
 
-    far_tokens, head_pairs = key_tokens - tokens, part // (2 * HEAD_DIM)
-    normed_far, keys_far, values_far, attention_own, attention_far, mixed, dvalue = pl.pallas_call(
+    far_tokens = key_tokens - tokens
+    normed_far_t, keys_far, values_far, attention_own, attention_far, mixed_t, dvalue = pl.pallas_call(
         functools.partial(forward_kernel, views, groups),
         in_specs=[SMEM] * 2 + [VMEM] * (2 * groups - 2 + 7),
         out_specs=[VMEM] * 7,
         out_shape=[
-            shape((far_tokens, width), bf16),
+            shape((width, far_tokens), bf16),
             shape((far_tokens, part), bf16),
             shape((far_tokens, part), bf16),
             shape((head_pairs, 2 * strip, 2 * tokens), f32),
             shape((head_pairs, far_tokens, 2 * tokens), f32),
-            shape((tokens, part), bf16),
+            shape((part, tokens), bf16),
             shape((key_tokens, part), bf16),
         ],
+        scratch_shapes=[pltpu.VMEM((far_tokens, width), bf16)],
         compiler_params=params(28 + groups // 2),
         cost_estimate=LITTLE,
         name="attention_forward",
     )(
-        scalars, alive, *got_own, *got_other, queries, keys, values, out_grad, norm_gain, w_key, w_value
-    )
-    mixed_other = lax.ppermute(mixed, "row", swap)
+        scalars, alive, *got_own, *got_other, query_stack, grad_stack, scores_own, values, norm_gain, w_key, w_value
+    )
+    mixed_other = lax.ppermute(mixed_t, "row", swap)
     dquery, dkey = call(
         functools.partial(backward_kernel, views),
         [shape((tokens, part), bf16), shape((key_tokens, part), bf16)],
-        (queries, keys, values, out_grad, keys_far, values_far, attention_own, attention_far),
+        (query_stack, grad_stack, dprob_own, keys, keys_far, values_far, attention_own, attention_far),
         "attention_backward",
         mebibytes=28 + groups // 2,
     )
@@ -487,7 +512,7 @@
     send, keep = call(
         value_out_kernel,
         [shape((2, 2, pairs, *tile), kind) for kind in (bf16, f32)],
-        (scalars, normed, normed_far, after(dvalue, dkey), mixed, mixed_other, upstream),
+        (scalars, normed_t, normed_far_t, after(dvalue, dkey), mixed_t, mixed_other, upstream),
         "grad_value_out",
         SMEM,
         24,
@@ -495,7 +520,7 @@
     got = lax.ppermute(send, "view", [(i, i ^ 1) for i in range(groups)])
     results = [shape((2, *q_block), bf16)] * 2 + [shape((2, *q_block), f32)] * 2
     qk_parts = call(
-        query_key_kernel, results, (scalars, normed, normed_far, after(dquery, send), dkey), "grad_query_key", SMEM, 24
+        query_key_kernel, results, (scalars, normed_t, normed_far_t, after(dquery, send), dkey), "grad_query_key", SMEM, 24
     )
     qk_got = first_exchange(qk_parts)
     qk_sums = first_sum(qk_parts, qk_got, "first_sum_query_key")

time: 91.6 us -> 90.9 us (level)
  no operation moved by 1% of the time
where the time goes in v12:
time: 90.9 us; the launch traced here: 90.7 us
  waiting for transfers between devices  42 us (46%)
  starting transfers between devices  28.5 us (31%)
  Pallas kernels  18.6 us (20%)
    ppermute x2, waiting for transfers between devices, first_exchange(): lax.ppermute(sends[0], 'scene', along_x)  13.1 us
    pallas_call x10, Pallas kernels, call(): pl.pallas_call(kernel_body, in_specs=[first] + [VMEM] * (len(operands) -...  9.43 us
    all_to_all x1, waiting for transfers between devices, across_views(): lax.all_to_all(packed, ('view', 'row'), split_axis=0, concat_axis=0, tile...  7.43 us
    ppermute x2, waiting for transfers between devices, second_exchange(): lax.ppermute(sums[0], 'scene', along_y)  7.26 us
    ppermute x3, starting transfers between devices, shards(): granted = [lax.ppermute(request, 'view', pairs) for pairs in between]  5.76 us
    ppermute x3, starting transfers between devices, shards(): lax.ppermute(part_out, 'view', pairs)  4.44 us
    ppermute x2, waiting for transfers between devices, second_exchange(): lax.ppermute(sums[1], 'scene', along_x)  4.38 us
    pallas_call x1, Pallas kernels, shards(): pl.pallas_call(project_kernel, in_specs=[SMEM] + [VMEM] * 10, out_specs=[...  4.12 us
  transfers between devices with their start and end apart: 25, of which 17 were waited for; matrix products, arithmetic and copies ran while one was open for 0% of the time, Pallas kernels for 12%

profile of v12, /device:TPU:0, one launch (start us, length us, event | category | flops | bytes accessed | tf_op | source)
XLA Modules:
  0.0 90.7 jit_solution(18384408738224855596)
XLA Ops:
  0.6 0.8 copy.13.partners
  1.4 1.2 %requests.1 = (s32[4]{0:T(128)S(1)}, s32[16]{0:T(128)S(1)}) custom-call(s32[1,4,3]{2,1,0:T(4,128)S(1)} %copy.13.partners), custom_call_target="tpu_custom_call" | custom-call | flops 40000000000 | bytes 1 | tf_op jit(solution)/shard_map/requests/pallas_call | solution.py:395
  2.6 5.1 %collective-permute-start.2 = (s32[4]{0:T(128)S(1)}, s32[4]{0:T(128)S(1)}, u32[]{:S(2)}, u32[]{:S(2)}) collective-permute-start(s32[4]{0:T(128)S(1)} %get-tuple-element.61), channel_id=1, source_target_pairs={{0,6},{2,4},{4,2},{6,0},{1,7},{3,5},{5,3},{7,1},{8,14},{10,12},{12... | collective-permute-start | bytes 56 | tf_op jit(solution)/shard_map/ppermute | solution.py:405
  7.7 0.0 collective-permute-start.1
  7.7 0.6 collective-permute-start
  8.4 0.5 collective-permute-start.7
  8.9 0.1 stack.23.scalars
  9.0 0.0 copy-start.6
  9.0 0.0 copy-start.7
  9.0 0.2 collective-permute-done.2.refs_2_
  9.3 2.9 %collective-permute-done.1.refs_1_ = s32[4]{0:T(128)S(1)} collective-permute-done((s32[4]{0:T(128)S(1)}, s32[4]{0:T(128)S(1)}, u32[]{:S(2)}, u32[]{:S(2)}) %collective-permute-start.1) | collective-permute-done | bytes 48 | tf_op jit(solution)/shard_map/ppermute | solution.py:405
  12.2 0.0 collective-permute-done.refs_0_
  12.2 0.6 pick.1
  12.8 0.1 collective-permute-start.3
  12.9 2.1 %collective-permute-start.4 = (bf16[32,1536]{1,0:T(8,128)(2,1)S(1)}, bf16[32,1536]{1,0:T(8,128)(2,1)S(1)}, u32[]{:S(2)}, u32[]{:S(2)}) collective-permute-start(bf16[32,1536]{1,0:T(8,128)(2,1)S(1)} %get-tuple-element.63), channel_id=1, source_target_pairs={{0,4},{2,6},{4,0},{6,2},{1,5},{3,7},{5,1},{7,3},{8,12},{10,14},{12... | collective-permute-start | bytes 294920 | tf_op jit(solution)/shard_map/ppermute | solution.py:421
  15.0 2.3 %collective-permute-start.5 = (bf16[32,1536]{1,0:T(8,128)(2,1)S(1)}, bf16[32,1536]{1,0:T(8,128)(2,1)S(1)}, u32[]{:S(2)}, u32[]{:S(2)}) collective-permute-start(bf16[32,1536]{1,0:T(8,128)(2,1)S(1)} %get-tuple-element.64), channel_id=1, source_target_pairs={{0,6},{2,4},{4,2},{6,0},{1,7},{3,5},{5,3},{7,1},{8,14},{10,12},{12... | collective-permute-start | bytes 294920 | tf_op jit(solution)/shard_map/ppermute | solution.py:421
  17.2 0.0 collective-permute-done.6.lat_other
  17.2 0.0 collective-permute-done.7.cot_other
  17.3 4.1 %project.1 = (bf16[1536,256]{1,0:T(8,128)(2,1)S(1)}, bf16[256,384]{1,0:T(8,128)(2,1)S(1)}, bf16[256,384]{1,0:T(8,128)(2,1)S(1)}, bf16[256,1536]{1,0:T(8,128)(2,1...) custom-call(s32[5]{0:T(128)S(1)} %stack.23.scalars, ...), custom_call_target="tpu_custom_call" | custom-call | flops 1 | bytes 1 | tf_op jit(solution)/shard_map/project/pallas_call | solution.py:423
  21.4 1.0 %collective-permute-done.4.refs_1_ = bf16[32,1536]{1,0:T(8,128)(2,1)S(1)} collective-permute-done((bf16[32,1536]{1,0:T(8,128)(2,1)S(1)}, bf16[32,1536]{1,0:T(8,128)(2,1)S(1)}, u32[]{:S(2)}, u32[]{:S(2)}) %collective-permute-start.4) | collective-permute-done | bytes 98336 | tf_op jit(solution)/shard_map/ppermute | solution.py:421
  22.4 0.5 collective-permute-start.9
  22.9 0.0 collective-permute-start.10
  22.9 0.8 collective-permute-done.8.refs_3_
  23.7 0.2 collective-permute-done.9.refs_4_
  23.9 0.4 collective-permute-done.10.refs_5_
  24.2 3.2 %attention_forward.1 = (bf16[1536,192]{1,0:T(8,128)(2,1)S(1)}, bf16[192,384]{1,0:T(8,128)(2,1)S(1)}, bf16[192,384]{1,0:T(8,128)(2,1)S(1)}, f32[3,64,512]{2,1,0:T...) custom-call(s32[5]{0:T(128)S(1)} %stack.23.scalars, ...), custom_call_target="tpu_custom_call" | custom-call | flops 1 | bytes 1 | tf_op jit(solution)/shard_map/attention_forward/pallas_call | solution.py:459
  27.4 0.2 collective-permute-start.11
  27.6 1.6 %attention_backward.1 = (bf16[256,384]{1,0:T(8,128)(2,1)S(1)}, bf16[448,384]{1,0:T(8,128)(2,1)S(1)}) custom-call(bf16[3,512,128]{2,1,0:T(8,128)(2,1)S(1)} %get-tuple-element.71.refs_6_.query_stack, bf16[3,512,128]{2,1,0:T(8,128)(2,1)S(1)} %get-tuple-element.72.refs_7_.grad_stack, f32[3,64,512]{2,1,0:T(8,128)S(1)} %get-tuple-element.76.dprob_own, ...), custom_call_target="tpu_custom_call" | custom-call | flops 1 | bytes 1 | tf_op jit(solution)/shard_map/attention_backward/pallas_call | solution.py:447
  29.2 0.0 collective-permute-done.11.theirs
  29.2 1.8 %grad_value_out.1 = (bf16[2,2,2,48,1536]{4,3,2,1,0:T(8,128)(2,1)S(1)}, f32[2,2,2,48,1536]{4,3,2,1,0:T(8,128)S(1)}) custom-call(s32[5]{0:T(128)S(1)} %stack.23.scalars, bf16[1536,256]{1,0:T(8,128)(2,1)S(1)} %get-tuple-element.66.normed_t, bf16[1536,192]{1,0:T(8,128)(2,1)S(1)} %get-tuple-element.75.normed_far_t, ...), custom_call_target="tpu_custom_call" | custom-call | flops 1 | bytes 1 | tf_op jit(solution)/shard_map/grad_value_out/pallas_call | solution.py:447
  31.0 1.7 %collective-permute-start.16 = (bf16[2,2,2,48,1536]{4,3,2,1,0:T(8,128)(2,1)S(1)}, bf16[2,2,2,48,1536]{4,3,2,1,0:T(8,128)(2,1)S(1)}, u32[]{:S(2)}, u32[]{:S(2)}) collective-permute-start(bf16[2,2,2,48,1536]{4,3,2,1,0:T(8,128)(2,1)S(1)} %get-tuple-element.88), channel_id=1, source_target_pairs={{0,2},{2,0},{4,6},{6,4},{1,3},{3,1},{5,7},{7,5},{8,10},{10,8},{12,... | collective-permute-start | bytes 3538952 | tf_op jit(solution)/shard_map/ppermute | solution.py:520
  32.7 1.9 %grad_query_key.1 = (bf16[2,384,384]{2,1,0:T(8,128)(2,1)S(1)}, bf16[2,384,384]{2,1,0:T(8,128)(2,1)S(1)}, f32[2,384,384]{2,1,0:T(8,128)S(1)}, f32[2,384,384]{2,1,0:T(8,128)S(1)}) custom-call(s32[5]{0:T(128)S(1)} %stack.23.scalars, bf16[1536,256]{1,0:T(8,128)(2,1)S(1)} %get-tuple-element.66.normed_t, bf16[1536,192]{1,0:T(8,128)(2,1)S(1)} %get-tuple-element.75.normed_far_t, ...), custom_call_target="tpu_custom_call" | custom-call | flops 1 | bytes 1 | tf_op jit(solution)/shard_map/grad_query_key/pallas_call | solution.py:447
  34.7 1.6 %collective-permute-start.12 = (bf16[2,384,384]{2,1,0:T(8,128)(2,1)S(1)}, bf16[2,384,384]{2,1,0:T(8,128)(2,1)S(1)}, u32[]{:S(2)}, u32[]{:S(2)}) collective-permute-start(bf16[2,384,384]{2,1,0:T(8,128)(2,1)S(1)} %get-tuple-element.91), channel_id=1, source_target_pairs={{0,8},{8,0},{16,24},{24,16},{1,9},{9,1},{17,25},{25,17},{2,10},{10... | collective-permute-start | bytes 1769480 | tf_op jit(solution)/shard_map/ppermute | solution.py:497
  36.2 1.5 %collective-permute-start.13 = (bf16[2,384,384]{2,1,0:T(8,128)(2,1)S(1)}, bf16[2,384,384]{2,1,0:T(8,128)(2,1)S(1)}, u32[]{:S(2)}, u32[]{:S(2)}) collective-permute-start(bf16[2,384,384]{2,1,0:T(8,128)(2,1)S(1)} %get-tuple-element.93), channel_id=1, source_target_pairs={{0,16},{8,24},{16,0},{24,8},{1,17},{9,25},{17,1},{25,9},{2,18},{10... | collective-permute-start | bytes 1769480 | tf_op jit(solution)/shard_map/ppermute | solution.py:497
  37.7 12.3 %collective-permute-done.12.x_got = bf16[2,384,384]{2,1,0:T(8,128)(2,1)S(1)} collective-permute-done((bf16[2,384,384]{2,1,0:T(8,128)(2,1)S(1)}, bf16[2,384,384]{2,1,0:T(8,128)(2,1)S(1)}, u32[]{:S(2)}, u32[]{:S(2)}) %collective-permute-start.12) | collective-permute-done | bytes 589856 | tf_op jit(solution)/shard_map/ppermute | solution.py:497
  50.0 1.2 %collective-permute-done.13.y_got = bf16[2,384,384]{2,1,0:T(8,128)(2,1)S(1)} collective-permute-done((bf16[2,384,384]{2,1,0:T(8,128)(2,1)S(1)}, bf16[2,384,384]{2,1,0:T(8,128)(2,1)S(1)}, u32[]{:S(2)}, u32[]{:S(2)}) %collective-permute-start.13) | collective-permute-done | bytes 589856 | tf_op jit(solution)/shard_map/ppermute | solution.py:497
  51.2 0.2 first_sum_query_key.1
  51.4 1.6 %collective-permute-start.14 = (bf16[384,384]{1,0:T(8,128)(2,1)S(1)}, bf16[384,384]{1,0:T(8,128)(2,1)S(1)}, u32[]{:S(2)}, u32[]{:S(2)}) collective-permute-start(bf16[384,384]{1,0:T(8,128)(2,1)S(1)} %get-tuple-element.95), channel_id=1, source_target_pairs={{0,16},{8,24},{16,0},{24,8},{1,17},{9,25},{17,1},{25,9},{2,18},{10... | collective-permute-start | bytes 884744 | tf_op jit(solution)/shard_map/ppermute | solution.py:505
  53.0 0.5 collective-permute-start.15
  53.6 5.8 %collective-permute-done.14.q_got = bf16[384,384]{1,0:T(8,128)(2,1)S(1)} collective-permute-done((bf16[384,384]{1,0:T(8,128)(2,1)S(1)}, bf16[384,384]{1,0:T(8,128)(2,1)S(1)}, u32[]{:S(2)}, u32[]{:S(2)}) %collective-permute-start.14) | collective-permute-done | bytes 294944 | tf_op jit(solution)/shard_map/ppermute | solution.py:505
  59.3 1.2 %collective-permute-done.15.k_got = bf16[384,384]{1,0:T(8,128)(2,1)S(1)} collective-permute-done((bf16[384,384]{1,0:T(8,128)(2,1)S(1)}, bf16[384,384]{1,0:T(8,128)(2,1)S(1)}, u32[]{:S(2)}, u32[]{:S(2)}) %collective-permute-start.15) | collective-permute-done | bytes 294944 | tf_op jit(solution)/shard_map/ppermute | solution.py:505
  60.6 0.9 %second_sum_query_key.1 = bf16[384,768]{1,0:T(8,128)(2,1)} custom-call(f32[384,384]{1,0:T(8,128)S(1)} %get-tuple-element.94.q_now, bf16[384,384]{1,0:T(8,128)(2,1)S(1)} %collective-permute-done.14.q_got, f32[384,384]{1,0:T(8,128)S(1)} %get-tuple-element.96.k_now, bf16[384,384]{1,0:T(8,128)(2,1)S(1)} %collective-permute-done.15.k_got), custom_call_target="tpu_custom_call" | custom-call | flops 1 | bytes 1 | tf_op jit(solution)/shard_map/second_sum_query_key/pallas_call | solution.py:447
  61.5 0.0 collective-permute-done.16.got
  61.5 0.2 view_sum_value_out.1
  61.7 0.6 collective-permute-start.18
  62.3 0.6 collective-permute-start.17
  62.9 3.9 %all-to-all-start = ((bf16[8,48,768]{2,1,0:T(8,128)(2,1)}), bf16[8,48,768]{2,1,0:T(8,128)(2,1)S(1)}, u32[]{:S(2)}, u32[]{:S(2)}) async-start(bf16[8,48,768]{2,1,0:T(8,128)(2,1)} %bitcast.7), calls=%async_computation | async-start | bytes 1179648 | tf_op jit(solution)/shard_map/all_to_all | solution.py:508
  66.8 1.7 %collective-permute-done.18.y_got = bf16[2,2,48,768]{3,2,1,0:T(8,128)(2,1)S(1)} collective-permute-done((bf16[2,2,48,768]{3,2,1,0:T(8,128)(2,1)S(1)}, bf16[2,2,48,768]{3,2,1,0:T(8,128)(2,1)S(1)}, u32[]{:S(2)}, u32[]{:S(2)}) %collective-permute-start.18) | collective-permute-done | bytes 294944 | tf_op jit(solution)/shard_map/ppermute | solution.py:497
  68.5 0.8 collective-permute-done.17.x_got
  69.3 0.1 first_sum_value_out.1
  69.4 1.6 %collective-permute-start.19 = (bf16[2,48,768]{2,1,0:T(8,128)(2,1)S(1)}, bf16[2,48,768]{2,1,0:T(8,128)(2,1)S(1)}, u32[]{:S(2)}, u32[]{:S(2)}) collective-permute-start(bf16[2,48,768]{2,1,0:T(8,128)(2,1)S(1)} %get-tuple-element.108), channel_id=1, source_target_pairs={{0,8},{8,0},{16,24},{24,16},{1,9},{9,1},{17,25},{25,17},{2,10},{10... | collective-permute-start | bytes 442376 | tf_op jit(solution)/shard_map/ppermute | solution.py:505
  71.0 0.5 collective-permute-start.20
  71.5 3.1 %collective-permute-done.19.refs_1_ = bf16[2,48,768]{2,1,0:T(8,128)(2,1)S(1)} collective-permute-done((bf16[2,48,768]{2,1,0:T(8,128)(2,1)S(1)}, bf16[2,48,768]{2,1,0:T(8,128)(2,1)S(1)}, u32[]{:S(2)}, u32[]{:S(2)}) %collective-permute-start.19) | collective-permute-done | bytes 147488 | tf_op jit(solution)/shard_map/ppermute | solution.py:505
  74.6 1.5 %collective-permute-done.20.refs_3_ = bf16[2,48,768]{2,1,0:T(8,128)(2,1)S(1)} collective-permute-done((bf16[2,48,768]{2,1,0:T(8,128)(2,1)S(1)}, bf16[2,48,768]{2,1,0:T(8,128)(2,1)S(1)}, u32[]{:S(2)}, u32[]{:S(2)}) %collective-permute-start.20) | collective-permute-done | bytes 147488 | tf_op jit(solution)/shard_map/ppermute | solution.py:505
  76.1 0.6 last_parts_value_out.1
  76.8 0.1 collective-permute-start.22
  76.8 2.9 %collective-permute-start.21 = (bf16[24,1536]{1,0:T(8,128)(2,1)S(1)}, bf16[24,1536]{1,0:T(8,128)(2,1)S(1)}, u32[]{:S(2)}, u32[]{:S(2)}) collective-permute-start(bf16[24,1536]{1,0:T(8,128)(2,1)S(1)} %get-tuple-element.113), channel_id=1, source_target_pairs={{0,4},{2,6},{4,0},{6,2},{1,5},{3,7},{5,1},{7,3},{8,12},{10,14},{12... | collective-permute-start | bytes 221192 | tf_op jit(solution)/shard_map/ppermute | solution.py:569
  79.7 0.1 collective-permute-start.23
  79.8 7.4 %all-to-all-done.packed = bf16[8,48,768]{2,1,0:T(8,128)(2,1)S(1)} async-done(((bf16[8,48,768]{2,1,0:T(8,128)(2,1)}), bf16[8,48,768]{2,1,0:T(8,128)(2,1)S(1)}, u32[]{:S(2)}, u32[]{:S(2)}) %all-to-all-start) | async-done | bytes 589856 | tf_op jit(solution)/shard_map/all_to_all | solution.py:508
  87.2 0.8 last_sum_query_key.1
  88.0 0.8 collective-permute-done.21.far_same
  88.8 0.6 collective-permute-done.23.far_cross
  89.4 0.0 collective-permute-done.22.near_cross
  89.4 1.3 %last_sum_value_out.1 = (f32[48,768]{1,0:T(8,128)}, f32[24,1536]{1,0:T(8,128)}) custom-call(s32[5]{0:T(128)S(1)} %stack.23.scalars, f32[24,1536]{1,0:T(8,128)S(1)} %get-tuple-element.112.mine, bf16[24,1536]{1,0:T(8,128)(2,1)S(1)} %collective-permute-done.21.far_same, f32[24,1536]{1,0:T(8,128)S(1)} %collective-permute-done.22.near_cross, ...), custom_call_target="tpu_custom_call" | custom-call | flops 1 | bytes 1 | tf_op jit(solution)/shard_map/last_sum_value_out/pallas_call | solution.py:447
  (18 shorter events, 0.0 us)
Async XLA Ops:
  1.4 7.0 %copy-start.4 = (bf16[1,4,1,32,1536]{4,3,2,1,0:T(8,128)(2,1)S(1)}, bf16[1,4,1,32,1536]{4,3,2,1,0:T(8,128)(2,1)}, u32[]{:S(2)}) copy-start(bf16[1,4,1,32,1536]{4,3,2,1,0:T(8,128)(2,1)} %param.10) | copy-start | bytes 1179652
  1.4 7.0 %copy-start.5 = (bf16[1,4,1,32,1536]{4,3,2,1,0:T(8,128)(2,1)S(1)}, bf16[1,4,1,32,1536]{4,3,2,1,0:T(8,128)(2,1)}, u32[]{:S(2)}) copy-start(bf16[1,4,1,32,1536]{4,3,2,1,0:T(8,128)(2,1)} %param.18) | copy-start | bytes 1179652
  2.6 6.6 %collective-permute-start.2 = (s32[4]{0:T(128)S(1)}, s32[4]{0:T(128)S(1)}, u32[]{:S(2)}, u32[]{:S(2)}) collective-permute-start(s32[4]{0:T(128)S(1)} %get-tuple-element.61), channel_id=1, source_target_pairs={{0,6},{2,4},{4,2},{6,0},{1,7},{3,5},{5,3},{7,1},{8,14},{10,12},{12... | collective-permute-start | bytes 56 | tf_op jit(solution)/shard_map/ppermute | solution.py:405
  7.7 4.4 %collective-permute-start.1 = (s32[4]{0:T(128)S(1)}, s32[4]{0:T(128)S(1)}, u32[]{:S(2)}, u32[]{:S(2)}) collective-permute-start(s32[4]{0:T(128)S(1)} %get-tuple-element.61), channel_id=1, source_target_pairs={{0,4},{2,6},{4,0},{6,2},{1,5},{3,7},{5,1},{7,3},{8,12},{10,14},{12... | collective-permute-start | bytes 56 | tf_op jit(solution)/shard_map/ppermute | solution.py:405
  7.7 4.4 %collective-permute-start = (s32[4]{0:T(128)S(1)}, s32[4]{0:T(128)S(1)}, u32[]{:S(2)}, u32[]{:S(2)}) collective-permute-start(s32[4]{0:T(128)S(1)} %get-tuple-element.61), channel_id=1, source_target_pairs={{0,2},{2,0},{4,6},{6,4},{1,3},{3,1},{5,7},{7,5},{8,10},{10,8},{12,... | collective-permute-start | bytes 56 | tf_op jit(solution)/shard_map/ppermute | solution.py:405
  8.4 8.8 %collective-permute-start.6 = (bf16[4,32,1536]{2,1,0:T(8,128)(2,1)S(1)}, bf16[4,32,1536]{2,1,0:T(8,128)(2,1)S(1)}, u32[]{:S(2)}, u32[]{:S(2)}) collective-permute-start(bf16[4,32,1536]{2,1,0:T(8,128)(2,1)S(1)} %bitcast.8), channel_id=1, source_target_pairs={{0,1},{1,0},{2,3},{3,2},{4,5},{5,4},{6,7},{7,6},{8,9},{9,8},{10,11... | collective-permute-start | bytes 1179656 | tf_op jit(solution)/shard_map/ppermute | solution.py:409
  8.4 8.8 %collective-permute-start.7 = (bf16[4,32,1536]{2,1,0:T(8,128)(2,1)S(1)}, bf16[4,32,1536]{2,1,0:T(8,128)(2,1)S(1)}, u32[]{:S(2)}, u32[]{:S(2)}) collective-permute-start(bf16[4,32,1536]{2,1,0:T(8,128)(2,1)S(1)} %bitcast.11), channel_id=1, source_target_pairs={{0,1},{1,0},{2,3},{3,2},{4,5},{5,4},{6,7},{7,6},{8,9},{9,8},{10,11... | collective-permute-start | bytes 1179656 | tf_op jit(solution)/shard_map/ppermute | solution.py:410
  9.0 8.3 %copy-start = (bf16[1536,768]{1,0:T(8,128)(2,1)S(1)}, bf16[1536,768]{1,0:T(8,128)(2,1)}, u32[]{:S(2)}) copy-start(bf16[1536,768]{1,0:T(8,128)(2,1)} %refs_11_.1) | copy-start | bytes 7077892
  9.0 8.3 %copy-start.1 = (bf16[1536,768]{1,0:T(8,128)(2,1)S(1)}, bf16[1536,768]{1,0:T(8,128)(2,1)}, u32[]{:S(2)}) copy-start(bf16[1536,768]{1,0:T(8,128)(2,1)} %refs_12_.1) | copy-start | bytes 7077892
  9.0 8.3 %copy-start.2 = (bf16[1536,768]{1,0:T(8,128)(2,1)S(1)}, bf16[1536,768]{1,0:T(8,128)(2,1)}, u32[]{:S(2)}) copy-start(bf16[1536,768]{1,0:T(8,128)(2,1)} %w_query.1) | copy-start | bytes 7077892
  9.0 8.3 %copy-start.3 = (bf16[768,1536]{1,0:T(8,128)(2,1)S(1)}, bf16[768,1536]{1,0:T(8,128)(2,1)}, u32[]{:S(2)}) copy-start(bf16[768,1536]{1,0:T(8,128)(2,1)} %w_out.1) | copy-start | bytes 7077892
  9.0 8.3 %copy-start.6 = (bf16[9,1536]{1,0:T(8,128)(2,1)S(1)}, bf16[9,1536]{1,0:T(8,128)(2,1)}, u32[]{:S(2)}) copy-start(bf16[9,1536]{1,0:T(8,128)(2,1)} %taps.1) | copy-start | bytes 82948
  9.0 8.3 %copy-start.7 = (f32[1536]{0:T(1024)S(1)}, f32[1536]{0:T(1024)}, u32[]{:S(2)}) copy-start(f32[1536]{0:T(1024)} %refs_10_.1) | copy-start | bytes 18436
  12.8 8.6 %collective-permute-start.3 = (bf16[32,1536]{1,0:T(8,128)(2,1)S(1)}, bf16[32,1536]{1,0:T(8,128)(2,1)S(1)}, u32[]{:S(2)}, u32[]{:S(2)}) collective-permute-start(bf16[32,1536]{1,0:T(8,128)(2,1)S(1)} %get-tuple-element.62), channel_id=1, source_target_pairs={{0,2},{2,0},{4,6},{6,4},{1,3},{3,1},{5,7},{7,5},{8,10},{10,8},{12,... | collective-permute-start | bytes 294920 | tf_op jit(solution)/shard_map/ppermute | solution.py:421
  12.9 9.5 %collective-permute-start.4 = (bf16[32,1536]{1,0:T(8,128)(2,1)S(1)}, bf16[32,1536]{1,0:T(8,128)(2,1)S(1)}, u32[]{:S(2)}, u32[]{:S(2)}) collective-permute-start(bf16[32,1536]{1,0:T(8,128)(2,1)S(1)} %get-tuple-element.63), channel_id=1, source_target_pairs={{0,4},{2,6},{4,0},{6,2},{1,5},{3,7},{5,1},{7,3},{8,12},{10,14},{12... | collective-permute-start | bytes 294920 | tf_op jit(solution)/shard_map/ppermute | solution.py:421
  15.0 7.5 %collective-permute-start.5 = (bf16[32,1536]{1,0:T(8,128)(2,1)S(1)}, bf16[32,1536]{1,0:T(8,128)(2,1)S(1)}, u32[]{:S(2)}, u32[]{:S(2)}) collective-permute-start(bf16[32,1536]{1,0:T(8,128)(2,1)S(1)} %get-tuple-element.64), channel_id=1, source_target_pairs={{0,6},{2,4},{4,2},{6,0},{1,7},{3,5},{5,3},{7,1},{8,14},{10,12},{12... | collective-permute-start | bytes 294920 | tf_op jit(solution)/shard_map/ppermute | solution.py:421
  22.4 1.3 %collective-permute-start.8 = (bf16[32,1536]{1,0:T(8,128)(2,1)S(1)}, bf16[32,1536]{1,0:T(8,128)(2,1)S(1)}, u32[]{:S(2)}, u32[]{:S(2)}) collective-permute-start(bf16[32,1536]{1,0:T(8,128)(2,1)S(1)} %collective-permute-done.3.refs_0_), channel_id=1, source_target_pairs={{0,1},{1,0},{2,3},{3,2},{4,5},{5,4},{6,7},{7,6},{8,9},{9,8},{10,11... | collective-permute-start | bytes 294920 | tf_op jit(solution)/shard_map/ppermute | solution.py:444
  22.4 1.5 %collective-permute-start.9 = (bf16[32,1536]{1,0:T(8,128)(2,1)S(1)}, bf16[32,1536]{1,0:T(8,128)(2,1)S(1)}, u32[]{:S(2)}, u32[]{:S(2)}) collective-permute-start(bf16[32,1536]{1,0:T(8,128)(2,1)S(1)} %collective-permute-done.4.refs_1_), channel_id=1, source_target_pairs={{0,1},{1,0},{2,3},{3,2},{4,5},{5,4},{6,7},{7,6},{8,9},{9,8},{10,11... | collective-permute-start | bytes 294920 | tf_op jit(solution)/shard_map/ppermute | solution.py:444
  22.9 1.3 %collective-permute-start.10 = (bf16[32,1536]{1,0:T(8,128)(2,1)S(1)}, bf16[32,1536]{1,0:T(8,128)(2,1)S(1)}, u32[]{:S(2)}, u32[]{:S(2)}) collective-permute-start(bf16[32,1536]{1,0:T(8,128)(2,1)S(1)} %collective-permute-done.5.refs_2_), channel_id=1, source_target_pairs={{0,1},{1,0},{2,3},{3,2},{4,5},{5,4},{6,7},{7,6},{8,9},{9,8},{10,11... | collective-permute-start | bytes 294920 | tf_op jit(solution)/shard_map/ppermute | solution.py:444
  27.4 1.8 %collective-permute-start.11 = (bf16[384,256]{1,0:T(8,128)(2,1)S(1)}, bf16[384,256]{1,0:T(8,128)(2,1)S(1)}, u32[]{:S(2)}, u32[]{:S(2)}) collective-permute-start(bf16[384,256]{1,0:T(8,128)(2,1)S(1)} %get-tuple-element.86.mine), channel_id=1, source_target_pairs={{0,1},{1,0},{2,3},{3,2},{4,5},{5,4},{6,7},{7,6},{8,9},{9,8},{10,11... | collective-permute-start | bytes 589832 | tf_op jit(solution)/shard_map/ppermute | solution.py:479
  31.0 30.5 %collective-permute-start.16 = (bf16[2,2,2,48,1536]{4,3,2,1,0:T(8,128)(2,1)S(1)}, bf16[2,2,2,48,1536]{4,3,2,1,0:T(8,128)(2,1)S(1)}, u32[]{:S(2)}, u32[]{:S(2)}) collective-permute-start(bf16[2,2,2,48,1536]{4,3,2,1,0:T(8,128)(2,1)S(1)} %get-tuple-element.88), channel_id=1, source_target_pairs={{0,2},{2,0},{4,6},{6,4},{1,3},{3,1},{5,7},{7,5},{8,10},{10,8},{12,... | collective-permute-start | bytes 3538952 | tf_op jit(solution)/shard_map/ppermute | solution.py:520
  34.7 15.4 %collective-permute-start.12 = (bf16[2,384,384]{2,1,0:T(8,128)(2,1)S(1)}, bf16[2,384,384]{2,1,0:T(8,128)(2,1)S(1)}, u32[]{:S(2)}, u32[]{:S(2)}) collective-permute-start(bf16[2,384,384]{2,1,0:T(8,128)(2,1)S(1)} %get-tuple-element.91), channel_id=1, source_target_pairs={{0,8},{8,0},{16,24},{24,16},{1,9},{9,1},{17,25},{25,17},{2,10},{10... | collective-permute-start | bytes 1769480 | tf_op jit(solution)/shard_map/ppermute | solution.py:497
  36.2 15.0 %collective-permute-start.13 = (bf16[2,384,384]{2,1,0:T(8,128)(2,1)S(1)}, bf16[2,384,384]{2,1,0:T(8,128)(2,1)S(1)}, u32[]{:S(2)}, u32[]{:S(2)}) collective-permute-start(bf16[2,384,384]{2,1,0:T(8,128)(2,1)S(1)} %get-tuple-element.93), channel_id=1, source_target_pairs={{0,16},{8,24},{16,0},{24,8},{1,17},{9,25},{17,1},{25,9},{2,18},{10... | collective-permute-start | bytes 1769480 | tf_op jit(solution)/shard_map/ppermute | solution.py:497
  51.4 7.9 %collective-permute-start.14 = (bf16[384,384]{1,0:T(8,128)(2,1)S(1)}, bf16[384,384]{1,0:T(8,128)(2,1)S(1)}, u32[]{:S(2)}, u32[]{:S(2)}) collective-permute-start(bf16[384,384]{1,0:T(8,128)(2,1)S(1)} %get-tuple-element.95), channel_id=1, source_target_pairs={{0,16},{8,24},{16,0},{24,8},{1,17},{9,25},{17,1},{25,9},{2,18},{10... | collective-permute-start | bytes 884744 | tf_op jit(solution)/shard_map/ppermute | solution.py:505
  53.0 7.5 %collective-permute-start.15 = (bf16[384,384]{1,0:T(8,128)(2,1)S(1)}, bf16[384,384]{1,0:T(8,128)(2,1)S(1)}, u32[]{:S(2)}, u32[]{:S(2)}) collective-permute-start(bf16[384,384]{1,0:T(8,128)(2,1)S(1)} %get-tuple-element.97), channel_id=1, source_target_pairs={{0,8},{8,0},{16,24},{24,16},{1,9},{9,1},{17,25},{25,17},{2,10},{10... | collective-permute-start | bytes 884744 | tf_op jit(solution)/shard_map/ppermute | solution.py:505
  61.7 6.8 %collective-permute-start.18 = (bf16[2,2,48,768]{3,2,1,0:T(8,128)(2,1)S(1)}, bf16[2,2,48,768]{3,2,1,0:T(8,128)(2,1)S(1)}, u32[]{:S(2)}, u32[]{:S(2)}) collective-permute-start(bf16[2,2,48,768]{3,2,1,0:T(8,128)(2,1)S(1)} %get-tuple-element.106), channel_id=1, source_target_pairs={{0,16},{8,24},{16,0},{24,8},{1,17},{9,25},{17,1},{25,9},{2,18},{10... | collective-permute-start | bytes 884744 | tf_op jit(solution)/shard_map/ppermute | solution.py:497
  62.3 7.0 %collective-permute-start.17 = (bf16[2,2,48,768]{3,2,1,0:T(8,128)(2,1)S(1)}, bf16[2,2,48,768]{3,2,1,0:T(8,128)(2,1)S(1)}, u32[]{:S(2)}, u32[]{:S(2)}) collective-permute-start(bf16[2,2,48,768]{3,2,1,0:T(8,128)(2,1)S(1)} %get-tuple-element.100), channel_id=1, source_target_pairs={{0,8},{8,0},{16,24},{24,16},{1,9},{9,1},{17,25},{25,17},{2,10},{10... | collective-permute-start | bytes 884744 | tf_op jit(solution)/shard_map/ppermute | solution.py:497
  62.9 24.3 %all-to-all-start = ((bf16[8,48,768]{2,1,0:T(8,128)(2,1)}), bf16[8,48,768]{2,1,0:T(8,128)(2,1)S(1)}, u32[]{:S(2)}, u32[]{:S(2)}) async-start(bf16[8,48,768]{2,1,0:T(8,128)(2,1)} %bitcast.7), calls=%async_computation | async-start | bytes 1179648 | tf_op jit(solution)/shard_map/all_to_all | solution.py:508
  69.4 5.2 %collective-permute-start.19 = (bf16[2,48,768]{2,1,0:T(8,128)(2,1)S(1)}, bf16[2,48,768]{2,1,0:T(8,128)(2,1)S(1)}, u32[]{:S(2)}, u32[]{:S(2)}) collective-permute-start(bf16[2,48,768]{2,1,0:T(8,128)(2,1)S(1)} %get-tuple-element.108), channel_id=1, source_target_pairs={{0,8},{8,0},{16,24},{24,16},{1,9},{9,1},{17,25},{25,17},{2,10},{10... | collective-permute-start | bytes 442376 | tf_op jit(solution)/shard_map/ppermute | solution.py:505
  71.0 5.1 %collective-permute-start.20 = (bf16[2,48,768]{2,1,0:T(8,128)(2,1)S(1)}, bf16[2,48,768]{2,1,0:T(8,128)(2,1)S(1)}, u32[]{:S(2)}, u32[]{:S(2)}) collective-permute-start(bf16[2,48,768]{2,1,0:T(8,128)(2,1)S(1)} %get-tuple-element.110), channel_id=1, source_target_pairs={{0,16},{8,24},{16,0},{24,8},{1,17},{9,25},{17,1},{25,9},{2,18},{10... | collective-permute-start | bytes 442376 | tf_op jit(solution)/shard_map/ppermute | solution.py:505
  76.8 12.7 %collective-permute-start.22 = (f32[24,1536]{1,0:T(8,128)S(1)}, f32[24,1536]{1,0:T(8,128)S(1)}, u32[]{:S(2)}, u32[]{:S(2)}) collective-permute-start(f32[24,1536]{1,0:T(8,128)S(1)} %get-tuple-element.114), channel_id=1, source_target_pairs={{0,1},{1,0},{2,3},{3,2},{4,5},{5,4},{6,7},{7,6},{8,9},{9,8},{10,11... | collective-permute-start | bytes 442376 | tf_op jit(solution)/shard_map/ppermute | solution.py:571
  76.8 11.9 %collective-permute-start.21 = (bf16[24,1536]{1,0:T(8,128)(2,1)S(1)}, bf16[24,1536]{1,0:T(8,128)(2,1)S(1)}, u32[]{:S(2)}, u32[]{:S(2)}) collective-permute-start(bf16[24,1536]{1,0:T(8,128)(2,1)S(1)} %get-tuple-element.113), channel_id=1, source_target_pairs={{0,4},{2,6},{4,0},{6,2},{1,5},{3,7},{5,1},{7,3},{8,12},{10,14},{12... | collective-permute-start | bytes 221192 | tf_op jit(solution)/shard_map/ppermute | solution.py:569
  79.7 9.7 %collective-permute-start.23 = (bf16[24,1536]{1,0:T(8,128)(2,1)S(1)}, bf16[24,1536]{1,0:T(8,128)(2,1)S(1)}, u32[]{:S(2)}, u32[]{:S(2)}) collective-permute-start(bf16[24,1536]{1,0:T(8,128)(2,1)S(1)} %get-tuple-element.115), channel_id=1, source_target_pairs={{0,5},{1,4},{2,7},{3,6},{4,1},{5,0},{6,3},{7,2},{8,13},{9,12},{10,... | collective-permute-start | bytes 221192 | tf_op jit(solution)/shard_map/ppermute | solution.py:570

commit v13 on v12

--- a/solution.py
+++ b/solution.py
@@ -37,26 +37,29 @@
     return (x * lax.rsqrt(mean + EPSILON) * gain).astype(jnp.bfloat16)
 
 
-def request_kernel(views, slots, groups, partners, request, alive):
-    for g in range(groups):
-        request[g] = 0
-        for u in range(views):
-            alive[g * views + u] = 0
+def alive_kernel(views, groups, partners, alive):
+    for g in range(groups * views):
+        alive[g] = 0
     for u in range(views):
-        for j in range(slots):
+        for j in range(partners.shape[2]):
             partner = partners[0, u, j]
 
             @pl.when(partner >= 0)
             def _():
-                group = lax.div(partner, jnp.int32(views))
-                request[group] = lax.rem(partner, jnp.int32(views))
-                alive[group * views + u] = 1
+                alive[lax.div(partner, jnp.int32(views)) * views + u] = 1
 
 
 def pick_kernel(groups, scalars, *refs):
-    requests, lat, outgoing = refs[: groups - 1], refs[groups - 1], refs[groups:]
-    for request, out in zip(requests, outgoing):
-        out[...] = lat[request[scalars[1]]]
+    tables, lat, outgoing = refs[: groups - 1], refs[groups - 1], refs[groups:]
+    views = lat.shape[0]
+    for table, out in zip(tables, outgoing):
+        wanted = jnp.int32(0)
+        for u in range(table.shape[1]):
+            for j in range(table.shape[2]):
+                partner = table[0, u, j]
+                here = (partner >= 0) & (lax.div(partner, jnp.int32(views)) == scalars[1])
+                wanted = jnp.where(here, lax.rem(partner, jnp.int32(views)), wanted)
+        out[...] = lat[wanted]
 
 
 def core_half(scalars, size):
@@ -166,7 +169,7 @@
     column_view = lax.broadcasted_iota(jnp.int32, (1, views * span), 1) // span
     slot_alive = []
     for j in range(groups - 1):
-        group = lax.bitwise_xor(here, jnp.int32(j + 1))
+        group = lax.bitwise_xor(here, jnp.int32(groups - 1 - j))
         start = 2 * j * strip
         normed_far[start : start + strip, :] = normalized(got_own[j][...], scale_row)
         normed_far[start + strip : start + 2 * strip, :] = normalized(got_other[j][...], scale_row)
@@ -381,7 +384,6 @@
     scenes = lax.axis_size("scene")
     assert (strip_rows, rows, scenes) == (1, 2, 4)
     strip = strip_rows * columns
-    slots = partners.shape[2]
     part = inner // rows
     tokens = views * 2 * strip
     key_tokens = tokens + (groups - 1) * 2 * strip
@@ -392,18 +394,19 @@
     swap = [(0, 1), (1, 0)]
     along_x, along_y = [(i, i ^ 1) for i in range(scenes)], [(i, i ^ 2) for i in range(scenes)]
 
-    request, alive = pl.pallas_call(
-        functools.partial(request_kernel, views, slots, groups),
+    alive = pl.pallas_call(
+        functools.partial(alive_kernel, views, groups),
         in_specs=[SMEM],
-        out_specs=(SMEM, SMEM),
-        out_shape=(shape((groups,), i32), shape((groups * views,), i32)),
+        out_specs=SMEM,
+        out_shape=shape((groups * views,), i32),
         cost_estimate=MUCH,
         compiler_params=params(4),
-        name="requests",
+        name="alive",
     )(partners)
-    between = [[(i, i ^ d) for i in range(groups)] for d in range(1, groups)]
-    granted = [lax.ppermute(request, "view", pairs) for pairs in between]
-
+    between = [[(i, i ^ d) for i in range(groups)] for d in reversed(range(1, groups))]
+    granted = [lax.ppermute(partners, "view", pairs) for pairs in between]
+
+    granted, alive = lax.optimization_barrier((granted, alive))
     lat = latents[0].reshape(views, strip, width)
     cot = cotangent[0].reshape(views, strip, width)
     lat_other = lax.ppermute(lat, "row", swap)

time: 90.9 us -> 90.1 us (level)
    ppermute x1, starting transfers between devices: 2.86 us -> 1.19 us  [shards(): lax.ppermute(far_same, 'view', [(i, i ^ 2) for i in range(groups)])]
    ppermute x1, starting transfers between devices: 0.07 us -> 1.57 us  [shards(): lax.ppermute(far_cross, ('view', 'row'), [(i, i ^ 5) for i in range(targe...]
    ppermute x1, starting transfers between devices: 1.69 us -> 0.39 us  [shards(): got = lax.ppermute(send, 'view', [(i, i ^ 1) for i in range(groups)])]
  transfers between devices with their start and end apart: 25 -> 25, of which waited for: 17 -> 16; matrix products, arithmetic and copies ran while one was open for 0% -> 0% of each run, Pallas kernels for 12% -> 14%
where the time goes in v13:
time: 90.1 us; the launch traced here: 89.8 us
  waiting for transfers between devices  41.8 us (46%)
  starting transfers between devices  27.6 us (31%)
  Pallas kernels  18.7 us (21%)
    ppermute x2, waiting for transfers between devices, first_exchange(): lax.ppermute(sends[0], 'scene', along_x)  13.5 us
    pallas_call x10, Pallas kernels, call(): pl.pallas_call(kernel_body, in_specs=[first] + [VMEM] * (len(operands) -...  9.42 us
    ppermute x2, waiting for transfers between devices, second_exchange(): lax.ppermute(sums[0], 'scene', along_y)  7.27 us
    all_to_all x1, waiting for transfers between devices, across_views(): lax.all_to_all(packed, ('view', 'row'), split_axis=0, concat_axis=0, tile...  6.87 us
    ppermute x3, starting transfers between devices, shards(): granted = [lax.ppermute(partners, 'view', pairs) for pairs in between]  5.62 us
    ppermute x3, starting transfers between devices, shards(): lax.ppermute(part_out, 'view', pairs)  4.45 us
    ppermute x2, waiting for transfers between devices, second_exchange(): lax.ppermute(sums[1], 'scene', along_x)  4.39 us
    pallas_call x1, Pallas kernels, shards(): pl.pallas_call(project_kernel, in_specs=[SMEM] + [VMEM] * 10, out_specs=[...  4.13 us
  transfers between devices with their start and end apart: 25, of which 16 were waited for; matrix products, arithmetic and copies ran while one was open for 0% of the time, Pallas kernels for 14%

profile of v13, /device:TPU:0, one launch (start us, length us, event | category | flops | bytes accessed | tf_op | source)
XLA Modules:
  0.0 89.8 jit_solution(546823717430012859)
XLA Ops:
  0.6 0.8 copy.13.partners
  1.4 3.0 %collective-permute-start.2 = (s32[1,4,3]{2,1,0:T(4,128)S(1)}, s32[1,4,3]{2,1,0:T(4,128)S(1)}, u32[]{:S(2)}, u32[]{:S(2)}) collective-permute-start(s32[1,4,3]{2,1,0:T(4,128)S(1)} %copy.13.partners), channel_id=1, source_target_pairs={{0,2},{2,0},{4,6},{6,4},{1,3},{3,1},{5,7},{7,5},{8,10},{10,8},{12,... | collective-permute-start | bytes 152 | tf_op jit(solution)/shard_map/ppermute | solution.py:407
  4.4 2.6 %collective-permute-start.1 = (s32[1,4,3]{2,1,0:T(4,128)S(1)}, s32[1,4,3]{2,1,0:T(4,128)S(1)}, u32[]{:S(2)}, u32[]{:S(2)}) collective-permute-start(s32[1,4,3]{2,1,0:T(4,128)S(1)} %copy.13.partners), channel_id=1, source_target_pairs={{0,4},{2,6},{4,0},{6,2},{1,5},{3,7},{5,1},{7,3},{8,12},{10,14},{12... | collective-permute-start | bytes 152 | tf_op jit(solution)/shard_map/ppermute | solution.py:407
  7.0 0.0 collective-permute-start
  7.0 0.0 collective-permute-start.6
  7.0 0.5 collective-permute-start.7
  7.5 1.2 %alive.1 = s32[16]{0:T(128)S(1)} custom-call(s32[1,4,3]{2,1,0:T(4,128)S(1)} %copy.13.partners), custom_call_target="tpu_custom_call" | custom-call | flops 40000000000 | bytes 1 | tf_op jit(solution)/shard_map/alive/pallas_call | solution.py:397
  8.8 0.1 stack.23.scalars
  8.9 0.0 copy-start.5
  8.9 0.0 copy-start.6
  8.9 0.0 copy-start.7
  8.9 0.0 collective-permute-done.2.refs_2_
  8.9 3.5 %collective-permute-done.refs_0_ = s32[1,4,3]{2,1,0:T(4,128)S(1)} collective-permute-done((s32[1,4,3]{2,1,0:T(4,128)S(1)}, s32[1,4,3]{2,1,0:T(4,128)S(1)}, u32[]{:S(2)}, u32[]{:S(2)}) %collective-permute-start) | collective-permute-done | bytes 80 | tf_op jit(solution)/shard_map/ppermute | solution.py:407
  12.4 0.8 pick.1
  13.2 0.4 collective-permute-start.3
  13.6 0.0 collective-permute-start.4
  13.6 4.0 %collective-permute-start.5 = (bf16[32,1536]{1,0:T(8,128)(2,1)S(1)}, bf16[32,1536]{1,0:T(8,128)(2,1)S(1)}, u32[]{:S(2)}, u32[]{:S(2)}) collective-permute-start(bf16[32,1536]{1,0:T(8,128)(2,1)S(1)} %get-tuple-element.68), channel_id=1, source_target_pairs={{0,2},{2,0},{4,6},{6,4},{1,3},{3,1},{5,7},{7,5},{8,10},{10,8},{12,... | collective-permute-start | bytes 294920 | tf_op jit(solution)/shard_map/ppermute | solution.py:424
  17.7 4.1 %project.1 = (bf16[1536,256]{1,0:T(8,128)(2,1)S(1)}, bf16[256,384]{1,0:T(8,128)(2,1)S(1)}, bf16[256,384]{1,0:T(8,128)(2,1)S(1)}, bf16[256,1536]{1,0:T(8,128)(2,1...) custom-call(s32[5]{0:T(128)S(1)} %stack.23.scalars, ...), custom_call_target="tpu_custom_call" | custom-call | flops 1 | bytes 1 | tf_op jit(solution)/shard_map/project/pallas_call | solution.py:426
  21.8 0.0 collective-permute-done.3.refs_0_
  21.9 0.4 collective-permute-done.4.refs_1_
  22.3 0.0 collective-permute-done.5.refs_2_
  22.3 0.1 collective-permute-start.8
  22.4 0.4 collective-permute-start.9
  22.8 0.1 collective-permute-start.10
  22.9 0.7 collective-permute-done.8.refs_3_
  23.6 0.2 collective-permute-done.9.refs_4_
  23.7 0.4 collective-permute-done.10.refs_5_
  24.1 3.2 %attention_forward.1 = (bf16[1536,192]{1,0:T(8,128)(2,1)S(1)}, bf16[192,384]{1,0:T(8,128)(2,1)S(1)}, bf16[192,384]{1,0:T(8,128)(2,1)S(1)}, f32[3,64,512]{2,1,0:T...) custom-call(s32[5]{0:T(128)S(1)} %stack.23.scalars, ...), custom_call_target="tpu_custom_call" | custom-call | flops 1 | bytes 1 | tf_op jit(solution)/shard_map/attention_forward/pallas_call | solution.py:462
  27.3 0.2 collective-permute-start.11
  27.5 1.6 %attention_backward.1 = (bf16[256,384]{1,0:T(8,128)(2,1)S(1)}, bf16[448,384]{1,0:T(8,128)(2,1)S(1)}) custom-call(bf16[3,512,128]{2,1,0:T(8,128)(2,1)S(1)} %get-tuple-element.75.refs_6_.query_stack, bf16[3,512,128]{2,1,0:T(8,128)(2,1)S(1)} %get-tuple-element.76.refs_7_.grad_stack, f32[3,64,512]{2,1,0:T(8,128)S(1)} %get-tuple-element.80.dprob_own, ...), custom_call_target="tpu_custom_call" | custom-call | flops 1 | bytes 1 | tf_op jit(solution)/shard_map/attention_backward/pallas_call | solution.py:450
  29.1 0.0 collective-permute-done.11.theirs
  29.1 1.8 %grad_value_out.1 = (bf16[2,2,2,48,1536]{4,3,2,1,0:T(8,128)(2,1)S(1)}, f32[2,2,2,48,1536]{4,3,2,1,0:T(8,128)S(1)}) custom-call(s32[5]{0:T(128)S(1)} %stack.23.scalars, bf16[1536,256]{1,0:T(8,128)(2,1)S(1)} %get-tuple-element.70.normed_t, bf16[1536,192]{1,0:T(8,128)(2,1)S(1)} %get-tuple-element.79.normed_far_t, ...), custom_call_target="tpu_custom_call" | custom-call | flops 1 | bytes 1 | tf_op jit(solution)/shard_map/grad_value_out/pallas_call | solution.py:450
  30.9 0.4 collective-permute-start.16
  31.3 1.9 %grad_query_key.1 = (bf16[2,384,384]{2,1,0:T(8,128)(2,1)S(1)}, bf16[2,384,384]{2,1,0:T(8,128)(2,1)S(1)}, f32[2,384,384]{2,1,0:T(8,128)S(1)}, f32[2,384,384]{2,1,0:T(8,128)S(1)}) custom-call(s32[5]{0:T(128)S(1)} %stack.23.scalars, bf16[1536,256]{1,0:T(8,128)(2,1)S(1)} %get-tuple-element.70.normed_t, bf16[1536,192]{1,0:T(8,128)(2,1)S(1)} %get-tuple-element.79.normed_far_t, ...), custom_call_target="tpu_custom_call" | custom-call | flops 1 | bytes 1 | tf_op jit(solution)/shard_map/grad_query_key/pallas_call | solution.py:450
  33.2 1.6 %collective-permute-start.12 = (bf16[2,384,384]{2,1,0:T(8,128)(2,1)S(1)}, bf16[2,384,384]{2,1,0:T(8,128)(2,1)S(1)}, u32[]{:S(2)}, u32[]{:S(2)}) collective-permute-start(bf16[2,384,384]{2,1,0:T(8,128)(2,1)S(1)} %get-tuple-element.95), channel_id=1, source_target_pairs={{0,8},{8,0},{16,24},{24,16},{1,9},{9,1},{17,25},{25,17},{2,10},{10... | collective-permute-start | bytes 1769480 | tf_op jit(solution)/shard_map/ppermute | solution.py:500
  34.8 1.5 %collective-permute-start.13 = (bf16[2,384,384]{2,1,0:T(8,128)(2,1)S(1)}, bf16[2,384,384]{2,1,0:T(8,128)(2,1)S(1)}, u32[]{:S(2)}, u32[]{:S(2)}) collective-permute-start(bf16[2,384,384]{2,1,0:T(8,128)(2,1)S(1)} %get-tuple-element.97), channel_id=1, source_target_pairs={{0,16},{8,24},{16,0},{24,8},{1,17},{9,25},{17,1},{25,9},{2,18},{10... | collective-permute-start | bytes 1769480 | tf_op jit(solution)/shard_map/ppermute | solution.py:500
  36.3 12.3 %collective-permute-done.12.x_got = bf16[2,384,384]{2,1,0:T(8,128)(2,1)S(1)} collective-permute-done((bf16[2,384,384]{2,1,0:T(8,128)(2,1)S(1)}, bf16[2,384,384]{2,1,0:T(8,128)(2,1)S(1)}, u32[]{:S(2)}, u32[]{:S(2)}) %collective-permute-start.12) | collective-permute-done | bytes 589856 | tf_op jit(solution)/shard_map/ppermute | solution.py:500
  48.6 1.2 %collective-permute-done.13.y_got = bf16[2,384,384]{2,1,0:T(8,128)(2,1)S(1)} collective-permute-done((bf16[2,384,384]{2,1,0:T(8,128)(2,1)S(1)}, bf16[2,384,384]{2,1,0:T(8,128)(2,1)S(1)}, u32[]{:S(2)}, u32[]{:S(2)}) %collective-permute-start.13) | collective-permute-done | bytes 589856 | tf_op jit(solution)/shard_map/ppermute | solution.py:500
  49.8 0.2 first_sum_query_key.1
  50.0 1.6 %collective-permute-start.14 = (bf16[384,384]{1,0:T(8,128)(2,1)S(1)}, bf16[384,384]{1,0:T(8,128)(2,1)S(1)}, u32[]{:S(2)}, u32[]{:S(2)}) collective-permute-start(bf16[384,384]{1,0:T(8,128)(2,1)S(1)} %get-tuple-element.99), channel_id=1, source_target_pairs={{0,16},{8,24},{16,0},{24,8},{1,17},{9,25},{17,1},{25,9},{2,18},{10... | collective-permute-start | bytes 884744 | tf_op jit(solution)/shard_map/ppermute | solution.py:508
  51.6 0.5 collective-permute-start.15
  52.1 5.8 %collective-permute-done.14.q_got = bf16[384,384]{1,0:T(8,128)(2,1)S(1)} collective-permute-done((bf16[384,384]{1,0:T(8,128)(2,1)S(1)}, bf16[384,384]{1,0:T(8,128)(2,1)S(1)}, u32[]{:S(2)}, u32[]{:S(2)}) %collective-permute-start.14) | collective-permute-done | bytes 294944 | tf_op jit(solution)/shard_map/ppermute | solution.py:508
  57.9 1.2 %collective-permute-done.15.k_got = bf16[384,384]{1,0:T(8,128)(2,1)S(1)} collective-permute-done((bf16[384,384]{1,0:T(8,128)(2,1)S(1)}, bf16[384,384]{1,0:T(8,128)(2,1)S(1)}, u32[]{:S(2)}, u32[]{:S(2)}) %collective-permute-start.15) | collective-permute-done | bytes 294944 | tf_op jit(solution)/shard_map/ppermute | solution.py:508
  59.1 0.9 %second_sum_query_key.1 = bf16[384,768]{1,0:T(8,128)(2,1)} custom-call(f32[384,384]{1,0:T(8,128)S(1)} %get-tuple-element.98.q_now, bf16[384,384]{1,0:T(8,128)(2,1)S(1)} %collective-permute-done.14.q_got, f32[384,384]{1,0:T(8,128)S(1)} %get-tuple-element.100.k_now, bf16[384,384]{1,0:T(8,128)(2,1)S(1)} %collective-permute-done.15.k_got), custom_call_target="tpu_custom_call" | custom-call | flops 1 | bytes 1 | tf_op jit(solution)/shard_map/second_sum_query_key/pallas_call | solution.py:450
  60.1 0.2 view_sum_value_out.1
  60.3 0.7 collective-permute-start.18
  61.0 1.5 %collective-permute-start.17 = (bf16[2,2,48,768]{3,2,1,0:T(8,128)(2,1)S(1)}, bf16[2,2,48,768]{3,2,1,0:T(8,128)(2,1)S(1)}, u32[]{:S(2)}, u32[]{:S(2)}) collective-permute-start(bf16[2,2,48,768]{3,2,1,0:T(8,128)(2,1)S(1)} %get-tuple-element.104), channel_id=1, source_target_pairs={{0,8},{8,0},{16,24},{24,16},{1,9},{9,1},{17,25},{25,17},{2,10},{10... | collective-permute-start | bytes 884744 | tf_op jit(solution)/shard_map/ppermute | solution.py:500
  62.5 3.5 %all-to-all-start = ((bf16[8,48,768]{2,1,0:T(8,128)(2,1)}), bf16[8,48,768]{2,1,0:T(8,128)(2,1)S(1)}, u32[]{:S(2)}, u32[]{:S(2)}) async-start(bf16[8,48,768]{2,1,0:T(8,128)(2,1)} %bitcast.7), calls=%async_computation | async-start | bytes 1179648 | tf_op jit(solution)/shard_map/all_to_all | solution.py:511
  66.0 1.9 %collective-permute-done.18.y_got = bf16[2,2,48,768]{3,2,1,0:T(8,128)(2,1)S(1)} collective-permute-done((bf16[2,2,48,768]{3,2,1,0:T(8,128)(2,1)S(1)}, bf16[2,2,48,768]{3,2,1,0:T(8,128)(2,1)S(1)}, u32[]{:S(2)}, u32[]{:S(2)}) %collective-permute-start.18) | collective-permute-done | bytes 294944 | tf_op jit(solution)/shard_map/ppermute | solution.py:500
  67.9 1.2 %collective-permute-done.17.x_got = bf16[2,2,48,768]{3,2,1,0:T(8,128)(2,1)S(1)} collective-permute-done((bf16[2,2,48,768]{3,2,1,0:T(8,128)(2,1)S(1)}, bf16[2,2,48,768]{3,2,1,0:T(8,128)(2,1)S(1)}, u32[]{:S(2)}, u32[]{:S(2)}) %collective-permute-start.17) | collective-permute-done | bytes 294944 | tf_op jit(solution)/shard_map/ppermute | solution.py:500
  69.2 0.1 first_sum_value_out.1
  69.3 1.6 %collective-permute-start.19 = (bf16[2,48,768]{2,1,0:T(8,128)(2,1)S(1)}, bf16[2,48,768]{2,1,0:T(8,128)(2,1)S(1)}, u32[]{:S(2)}, u32[]{:S(2)}) collective-permute-start(bf16[2,48,768]{2,1,0:T(8,128)(2,1)S(1)} %get-tuple-element.112), channel_id=1, source_target_pairs={{0,8},{8,0},{16,24},{24,16},{1,9},{9,1},{17,25},{25,17},{2,10},{10... | collective-permute-start | bytes 442376 | tf_op jit(solution)/shard_map/ppermute | solution.py:508
  70.9 0.5 collective-permute-start.20
  71.3 3.2 %collective-permute-done.19.refs_1_ = bf16[2,48,768]{2,1,0:T(8,128)(2,1)S(1)} collective-permute-done((bf16[2,48,768]{2,1,0:T(8,128)(2,1)S(1)}, bf16[2,48,768]{2,1,0:T(8,128)(2,1)S(1)}, u32[]{:S(2)}, u32[]{:S(2)}) %collective-permute-start.19) | collective-permute-done | bytes 147488 | tf_op jit(solution)/shard_map/ppermute | solution.py:508
  74.5 1.5 %collective-permute-done.20.refs_3_ = bf16[2,48,768]{2,1,0:T(8,128)(2,1)S(1)} collective-permute-done((bf16[2,48,768]{2,1,0:T(8,128)(2,1)S(1)}, bf16[2,48,768]{2,1,0:T(8,128)(2,1)S(1)}, u32[]{:S(2)}, u32[]{:S(2)}) %collective-permute-start.20) | collective-permute-done | bytes 147488 | tf_op jit(solution)/shard_map/ppermute | solution.py:508
  76.0 0.6 last_parts_value_out.1
  76.6 0.1 collective-permute-start.22
  76.7 1.2 %collective-permute-start.21 = (bf16[24,1536]{1,0:T(8,128)(2,1)S(1)}, bf16[24,1536]{1,0:T(8,128)(2,1)S(1)}, u32[]{:S(2)}, u32[]{:S(2)}) collective-permute-start(bf16[24,1536]{1,0:T(8,128)(2,1)S(1)} %get-tuple-element.117), channel_id=1, source_target_pairs={{0,4},{2,6},{4,0},{6,2},{1,5},{3,7},{5,1},{7,3},{8,12},{10,14},{12... | collective-permute-start | bytes 221192 | tf_op jit(solution)/shard_map/ppermute | solution.py:572
  77.9 1.6 %collective-permute-start.23 = (bf16[24,1536]{1,0:T(8,128)(2,1)S(1)}, bf16[24,1536]{1,0:T(8,128)(2,1)S(1)}, u32[]{:S(2)}, u32[]{:S(2)}) collective-permute-start(bf16[24,1536]{1,0:T(8,128)(2,1)S(1)} %get-tuple-element.119), channel_id=1, source_target_pairs={{0,5},{1,4},{2,7},{3,6},{4,1},{5,0},{6,3},{7,2},{8,13},{9,12},{10,... | collective-permute-start | bytes 221192 | tf_op jit(solution)/shard_map/ppermute | solution.py:573
  79.5 6.9 %all-to-all-done.packed = bf16[8,48,768]{2,1,0:T(8,128)(2,1)S(1)} async-done(((bf16[8,48,768]{2,1,0:T(8,128)(2,1)}), bf16[8,48,768]{2,1,0:T(8,128)(2,1)S(1)}, u32[]{:S(2)}, u32[]{:S(2)}) %all-to-all-start) | async-done | bytes 589856 | tf_op jit(solution)/shard_map/all_to_all | solution.py:511
  86.4 0.8 last_sum_query_key.1
  87.1 0.8 collective-permute-done.21.far_same
  87.9 0.6 collective-permute-done.23.far_cross
  88.6 1.3 %last_sum_value_out.1 = (f32[48,768]{1,0:T(8,128)}, f32[24,1536]{1,0:T(8,128)}) custom-call(s32[5]{0:T(128)S(1)} %stack.23.scalars, f32[24,1536]{1,0:T(8,128)S(1)} %get-tuple-element.116.mine, bf16[24,1536]{1,0:T(8,128)(2,1)S(1)} %collective-permute-done.21.far_same, f32[24,1536]{1,0:T(8,128)S(1)} %collective-permute-done.22.near_cross, ...), custom_call_target="tpu_custom_call" | custom-call | flops 1 | bytes 1 | tf_op jit(solution)/shard_map/last_sum_value_out/pallas_call | solution.py:450
  (18 shorter events, 0.0 us)
Async XLA Ops:
  1.4 7.5 %collective-permute-start.2 = (s32[1,4,3]{2,1,0:T(4,128)S(1)}, s32[1,4,3]{2,1,0:T(4,128)S(1)}, u32[]{:S(2)}, u32[]{:S(2)}) collective-permute-start(s32[1,4,3]{2,1,0:T(4,128)S(1)} %copy.13.partners), channel_id=1, source_target_pairs={{0,2},{2,0},{4,6},{6,4},{1,3},{3,1},{5,7},{7,5},{8,10},{10,8},{12,... | collective-permute-start | bytes 152 | tf_op jit(solution)/shard_map/ppermute | solution.py:407
  4.4 4.5 %collective-permute-start.1 = (s32[1,4,3]{2,1,0:T(4,128)S(1)}, s32[1,4,3]{2,1,0:T(4,128)S(1)}, u32[]{:S(2)}, u32[]{:S(2)}) collective-permute-start(s32[1,4,3]{2,1,0:T(4,128)S(1)} %copy.13.partners), channel_id=1, source_target_pairs={{0,4},{2,6},{4,0},{6,2},{1,5},{3,7},{5,1},{7,3},{8,12},{10,14},{12... | collective-permute-start | bytes 152 | tf_op jit(solution)/shard_map/ppermute | solution.py:407
  7.0 5.4 %collective-permute-start = (s32[1,4,3]{2,1,0:T(4,128)S(1)}, s32[1,4,3]{2,1,0:T(4,128)S(1)}, u32[]{:S(2)}, u32[]{:S(2)}) collective-permute-start(s32[1,4,3]{2,1,0:T(4,128)S(1)} %copy.13.partners), channel_id=1, source_target_pairs={{0,6},{2,4},{4,2},{6,0},{1,7},{3,5},{5,3},{7,1},{8,14},{10,12},{12... | collective-permute-start | bytes 152 | tf_op jit(solution)/shard_map/ppermute | solution.py:407
  7.0 10.6 %collective-permute-start.6 = (bf16[4,32,1536]{2,1,0:T(8,128)(2,1)}, bf16[4,32,1536]{2,1,0:T(8,128)(2,1)S(1)}, u32[]{:S(2)}, u32[]{:S(2)}) collective-permute-start(bf16[4,32,1536]{2,1,0:T(8,128)(2,1)} %bitcast.8), channel_id=1, source_target_pairs={{0,1},{1,0},{2,3},{3,2},{4,5},{5,4},{6,7},{7,6},{8,9},{9,8},{10,11... | collective-permute-start | bytes 1179656 | tf_op jit(solution)/shard_map/ppermute | solution.py:412
  7.0 10.6 %collective-permute-start.7 = (bf16[4,32,1536]{2,1,0:T(8,128)(2,1)}, bf16[4,32,1536]{2,1,0:T(8,128)(2,1)S(1)}, u32[]{:S(2)}, u32[]{:S(2)}) collective-permute-start(bf16[4,32,1536]{2,1,0:T(8,128)(2,1)} %bitcast.11), channel_id=1, source_target_pairs={{0,1},{1,0},{2,3},{3,2},{4,5},{5,4},{6,7},{7,6},{8,9},{9,8},{10,11... | collective-permute-start | bytes 1179656 | tf_op jit(solution)/shard_map/ppermute | solution.py:413
  7.5 4.9 %copy-start.4 = (bf16[1,4,1,32,1536]{4,3,2,1,0:T(8,128)(2,1)S(1)}, bf16[1,4,1,32,1536]{4,3,2,1,0:T(8,128)(2,1)}, u32[]{:S(2)}) copy-start(bf16[1,4,1,32,1536]{4,3,2,1,0:T(8,128)(2,1)} %param.10) | copy-start | bytes 1179652
  8.8 8.8 %copy-start = (bf16[1536,768]{1,0:T(8,128)(2,1)S(1)}, bf16[1536,768]{1,0:T(8,128)(2,1)}, u32[]{:S(2)}) copy-start(bf16[1536,768]{1,0:T(8,128)(2,1)} %refs_11_.1) | copy-start | bytes 7077892
  8.9 8.8 %copy-start.1 = (bf16[1536,768]{1,0:T(8,128)(2,1)S(1)}, bf16[1536,768]{1,0:T(8,128)(2,1)}, u32[]{:S(2)}) copy-start(bf16[1536,768]{1,0:T(8,128)(2,1)} %refs_12_.1) | copy-start | bytes 7077892
  8.9 8.8 %copy-start.2 = (bf16[1536,768]{1,0:T(8,128)(2,1)S(1)}, bf16[1536,768]{1,0:T(8,128)(2,1)}, u32[]{:S(2)}) copy-start(bf16[1536,768]{1,0:T(8,128)(2,1)} %w_query.1) | copy-start | bytes 7077892
  8.9 8.8 %copy-start.3 = (bf16[768,1536]{1,0:T(8,128)(2,1)S(1)}, bf16[768,1536]{1,0:T(8,128)(2,1)}, u32[]{:S(2)}) copy-start(bf16[768,1536]{1,0:T(8,128)(2,1)} %w_out.1) | copy-start | bytes 7077892
  8.9 8.8 %copy-start.5 = (bf16[1,4,1,32,1536]{4,3,2,1,0:T(8,128)(2,1)S(1)}, bf16[1,4,1,32,1536]{4,3,2,1,0:T(8,128)(2,1)}, u32[]{:S(2)}) copy-start(bf16[1,4,1,32,1536]{4,3,2,1,0:T(8,128)(2,1)} %param.18) | copy-start | bytes 1179652
  8.9 8.8 %copy-start.6 = (bf16[9,1536]{1,0:T(8,128)(2,1)S(1)}, bf16[9,1536]{1,0:T(8,128)(2,1)}, u32[]{:S(2)}) copy-start(bf16[9,1536]{1,0:T(8,128)(2,1)} %taps.1) | copy-start | bytes 82948
  8.9 8.8 %copy-start.7 = (f32[1536]{0:T(1024)S(1)}, f32[1536]{0:T(1024)}, u32[]{:S(2)}) copy-start(f32[1536]{0:T(1024)} %refs_10_.1) | copy-start | bytes 18436
  13.2 8.7 %collective-permute-start.3 = (bf16[32,1536]{1,0:T(8,128)(2,1)S(1)}, bf16[32,1536]{1,0:T(8,128)(2,1)S(1)}, u32[]{:S(2)}, u32[]{:S(2)}) collective-permute-start(bf16[32,1536]{1,0:T(8,128)(2,1)S(1)} %get-tuple-element.66), channel_id=1, source_target_pairs={{0,6},{2,4},{4,2},{6,0},{1,7},{3,5},{5,3},{7,1},{8,14},{10,12},{12... | collective-permute-start | bytes 294920 | tf_op jit(solution)/shard_map/ppermute | solution.py:424
  13.6 8.7 %collective-permute-start.4 = (bf16[32,1536]{1,0:T(8,128)(2,1)S(1)}, bf16[32,1536]{1,0:T(8,128)(2,1)S(1)}, u32[]{:S(2)}, u32[]{:S(2)}) collective-permute-start(bf16[32,1536]{1,0:T(8,128)(2,1)S(1)} %get-tuple-element.67), channel_id=1, source_target_pairs={{0,4},{2,6},{4,0},{6,2},{1,5},{3,7},{5,1},{7,3},{8,12},{10,14},{12... | collective-permute-start | bytes 294920 | tf_op jit(solution)/shard_map/ppermute | solution.py:424
  13.6 8.7 %collective-permute-start.5 = (bf16[32,1536]{1,0:T(8,128)(2,1)S(1)}, bf16[32,1536]{1,0:T(8,128)(2,1)S(1)}, u32[]{:S(2)}, u32[]{:S(2)}) collective-permute-start(bf16[32,1536]{1,0:T(8,128)(2,1)S(1)} %get-tuple-element.68), channel_id=1, source_target_pairs={{0,2},{2,0},{4,6},{6,4},{1,3},{3,1},{5,7},{7,5},{8,10},{10,8},{12,... | collective-permute-start | bytes 294920 | tf_op jit(solution)/shard_map/ppermute | solution.py:424
  22.3 1.3 %collective-permute-start.8 = (bf16[32,1536]{1,0:T(8,128)(2,1)S(1)}, bf16[32,1536]{1,0:T(8,128)(2,1)S(1)}, u32[]{:S(2)}, u32[]{:S(2)}) collective-permute-start(bf16[32,1536]{1,0:T(8,128)(2,1)S(1)} %collective-permute-done.3.refs_0_), channel_id=1, source_target_pairs={{0,1},{1,0},{2,3},{3,2},{4,5},{5,4},{6,7},{7,6},{8,9},{9,8},{10,11... | collective-permute-start | bytes 294920 | tf_op jit(solution)/shard_map/ppermute | solution.py:447
  22.4 1.4 %collective-permute-start.9 = (bf16[32,1536]{1,0:T(8,128)(2,1)S(1)}, bf16[32,1536]{1,0:T(8,128)(2,1)S(1)}, u32[]{:S(2)}, u32[]{:S(2)}) collective-permute-start(bf16[32,1536]{1,0:T(8,128)(2,1)S(1)} %collective-permute-done.4.refs_1_), channel_id=1, source_target_pairs={{0,1},{1,0},{2,3},{3,2},{4,5},{5,4},{6,7},{7,6},{8,9},{9,8},{10,11... | collective-permute-start | bytes 294920 | tf_op jit(solution)/shard_map/ppermute | solution.py:447
  22.8 1.3 %collective-permute-start.10 = (bf16[32,1536]{1,0:T(8,128)(2,1)S(1)}, bf16[32,1536]{1,0:T(8,128)(2,1)S(1)}, u32[]{:S(2)}, u32[]{:S(2)}) collective-permute-start(bf16[32,1536]{1,0:T(8,128)(2,1)S(1)} %collective-permute-done.5.refs_2_), channel_id=1, source_target_pairs={{0,1},{1,0},{2,3},{3,2},{4,5},{5,4},{6,7},{7,6},{8,9},{9,8},{10,11... | collective-permute-start | bytes 294920 | tf_op jit(solution)/shard_map/ppermute | solution.py:447
  27.3 1.8 %collective-permute-start.11 = (bf16[384,256]{1,0:T(8,128)(2,1)S(1)}, bf16[384,256]{1,0:T(8,128)(2,1)S(1)}, u32[]{:S(2)}, u32[]{:S(2)}) collective-permute-start(bf16[384,256]{1,0:T(8,128)(2,1)S(1)} %get-tuple-element.90.mine), channel_id=1, source_target_pairs={{0,1},{1,0},{2,3},{3,2},{4,5},{5,4},{6,7},{7,6},{8,9},{9,8},{10,11... | collective-permute-start | bytes 589832 | tf_op jit(solution)/shard_map/ppermute | solution.py:482
  30.9 29.2 %collective-permute-start.16 = (bf16[2,2,2,48,1536]{4,3,2,1,0:T(8,128)(2,1)S(1)}, bf16[2,2,2,48,1536]{4,3,2,1,0:T(8,128)(2,1)S(1)}, u32[]{:S(2)}, u32[]{:S(2)}) collective-permute-start(bf16[2,2,2,48,1536]{4,3,2,1,0:T(8,128)(2,1)S(1)} %get-tuple-element.92), channel_id=1, source_target_pairs={{0,2},{2,0},{4,6},{6,4},{1,3},{3,1},{5,7},{7,5},{8,10},{10,8},{12,... | collective-permute-start | bytes 3538952 | tf_op jit(solution)/shard_map/ppermute | solution.py:523
  33.2 15.4 %collective-permute-start.12 = (bf16[2,384,384]{2,1,0:T(8,128)(2,1)S(1)}, bf16[2,384,384]{2,1,0:T(8,128)(2,1)S(1)}, u32[]{:S(2)}, u32[]{:S(2)}) collective-permute-start(bf16[2,384,384]{2,1,0:T(8,128)(2,1)S(1)} %get-tuple-element.95), channel_id=1, source_target_pairs={{0,8},{8,0},{16,24},{24,16},{1,9},{9,1},{17,25},{25,17},{2,10},{10... | collective-permute-start | bytes 1769480 | tf_op jit(solution)/shard_map/ppermute | solution.py:500
  34.8 15.0 %collective-permute-start.13 = (bf16[2,384,384]{2,1,0:T(8,128)(2,1)S(1)}, bf16[2,384,384]{2,1,0:T(8,128)(2,1)S(1)}, u32[]{:S(2)}, u32[]{:S(2)}) collective-permute-start(bf16[2,384,384]{2,1,0:T(8,128)(2,1)S(1)} %get-tuple-element.97), channel_id=1, source_target_pairs={{0,16},{8,24},{16,0},{24,8},{1,17},{9,25},{17,1},{25,9},{2,18},{10... | collective-permute-start | bytes 1769480 | tf_op jit(solution)/shard_map/ppermute | solution.py:500
  50.0 7.9 %collective-permute-start.14 = (bf16[384,384]{1,0:T(8,128)(2,1)S(1)}, bf16[384,384]{1,0:T(8,128)(2,1)S(1)}, u32[]{:S(2)}, u32[]{:S(2)}) collective-permute-start(bf16[384,384]{1,0:T(8,128)(2,1)S(1)} %get-tuple-element.99), channel_id=1, source_target_pairs={{0,16},{8,24},{16,0},{24,8},{1,17},{9,25},{17,1},{25,9},{2,18},{10... | collective-permute-start | bytes 884744 | tf_op jit(solution)/shard_map/ppermute | solution.py:508
  51.6 7.5 %collective-permute-start.15 = (bf16[384,384]{1,0:T(8,128)(2,1)S(1)}, bf16[384,384]{1,0:T(8,128)(2,1)S(1)}, u32[]{:S(2)}, u32[]{:S(2)}) collective-permute-start(bf16[384,384]{1,0:T(8,128)(2,1)S(1)} %get-tuple-element.101), channel_id=1, source_target_pairs={{0,8},{8,0},{16,24},{24,16},{1,9},{9,1},{17,25},{25,17},{2,10},{10... | collective-permute-start | bytes 884744 | tf_op jit(solution)/shard_map/ppermute | solution.py:508
  60.3 7.7 %collective-permute-start.18 = (bf16[2,2,48,768]{3,2,1,0:T(8,128)(2,1)S(1)}, bf16[2,2,48,768]{3,2,1,0:T(8,128)(2,1)S(1)}, u32[]{:S(2)}, u32[]{:S(2)}) collective-permute-start(bf16[2,2,48,768]{3,2,1,0:T(8,128)(2,1)S(1)} %get-tuple-element.110), channel_id=1, source_target_pairs={{0,16},{8,24},{16,0},{24,8},{1,17},{9,25},{17,1},{25,9},{2,18},{10... | collective-permute-start | bytes 884744 | tf_op jit(solution)/shard_map/ppermute | solution.py:500
  61.0 8.2 %collective-permute-start.17 = (bf16[2,2,48,768]{3,2,1,0:T(8,128)(2,1)S(1)}, bf16[2,2,48,768]{3,2,1,0:T(8,128)(2,1)S(1)}, u32[]{:S(2)}, u32[]{:S(2)}) collective-permute-start(bf16[2,2,48,768]{3,2,1,0:T(8,128)(2,1)S(1)} %get-tuple-element.104), channel_id=1, source_target_pairs={{0,8},{8,0},{16,24},{24,16},{1,9},{9,1},{17,25},{25,17},{2,10},{10... | collective-permute-start | bytes 884744 | tf_op jit(solution)/shard_map/ppermute | solution.py:500
  62.5 23.9 %all-to-all-start = ((bf16[8,48,768]{2,1,0:T(8,128)(2,1)}), bf16[8,48,768]{2,1,0:T(8,128)(2,1)S(1)}, u32[]{:S(2)}, u32[]{:S(2)}) async-start(bf16[8,48,768]{2,1,0:T(8,128)(2,1)} %bitcast.7), calls=%async_computation | async-start | bytes 1179648 | tf_op jit(solution)/shard_map/all_to_all | solution.py:511
  69.3 5.2 %collective-permute-start.19 = (bf16[2,48,768]{2,1,0:T(8,128)(2,1)S(1)}, bf16[2,48,768]{2,1,0:T(8,128)(2,1)S(1)}, u32[]{:S(2)}, u32[]{:S(2)}) collective-permute-start(bf16[2,48,768]{2,1,0:T(8,128)(2,1)S(1)} %get-tuple-element.112), channel_id=1, source_target_pairs={{0,8},{8,0},{16,24},{24,16},{1,9},{9,1},{17,25},{25,17},{2,10},{10... | collective-permute-start | bytes 442376 | tf_op jit(solution)/shard_map/ppermute | solution.py:508
  70.9 5.1 %collective-permute-start.20 = (bf16[2,48,768]{2,1,0:T(8,128)(2,1)S(1)}, bf16[2,48,768]{2,1,0:T(8,128)(2,1)S(1)}, u32[]{:S(2)}, u32[]{:S(2)}) collective-permute-start(bf16[2,48,768]{2,1,0:T(8,128)(2,1)S(1)} %get-tuple-element.114), channel_id=1, source_target_pairs={{0,16},{8,24},{16,0},{24,8},{1,17},{9,25},{17,1},{25,9},{2,18},{10... | collective-permute-start | bytes 442376 | tf_op jit(solution)/shard_map/ppermute | solution.py:508
  76.6 11.9 %collective-permute-start.22 = (f32[24,1536]{1,0:T(8,128)S(1)}, f32[24,1536]{1,0:T(8,128)S(1)}, u32[]{:S(2)}, u32[]{:S(2)}) collective-permute-start(f32[24,1536]{1,0:T(8,128)S(1)} %get-tuple-element.118), channel_id=1, source_target_pairs={{0,1},{1,0},{2,3},{3,2},{4,5},{5,4},{6,7},{7,6},{8,9},{9,8},{10,11... | collective-permute-start | bytes 442376 | tf_op jit(solution)/shard_map/ppermute | solution.py:574
  76.7 11.2 %collective-permute-start.21 = (bf16[24,1536]{1,0:T(8,128)(2,1)S(1)}, bf16[24,1536]{1,0:T(8,128)(2,1)S(1)}, u32[]{:S(2)}, u32[]{:S(2)}) collective-permute-start(bf16[24,1536]{1,0:T(8,128)(2,1)S(1)} %get-tuple-element.117), channel_id=1, source_target_pairs={{0,4},{2,6},{4,0},{6,2},{1,5},{3,7},{5,1},{7,3},{8,12},{10,14},{12... | collective-permute-start | bytes 221192 | tf_op jit(solution)/shard_map/ppermute | solution.py:572
  77.9 10.7 %collective-permute-start.23 = (bf16[24,1536]{1,0:T(8,128)(2,1)S(1)}, bf16[24,1536]{1,0:T(8,128)(2,1)S(1)}, u32[]{:S(2)}, u32[]{:S(2)}) collective-permute-start(bf16[24,1536]{1,0:T(8,128)(2,1)S(1)} %get-tuple-element.119), channel_id=1, source_target_pairs={{0,5},{1,4},{2,7},{3,6},{4,1},{5,0},{6,3},{7,2},{8,13},{9,12},{10,... | collective-permute-start | bytes 221192 | tf_op jit(solution)/shard_map/ppermute | solution.py:573

commit v14 on v13

--- a/solution.py
+++ b/solution.py
@@ -233,20 +233,28 @@
     return total
 
 
-def by_quarters(scalars, lefts, right, send, keep, x_first):
-    size = send.shape[1]
+def by_quarters(scalars, lefts, right, sends, keep, x_first):
+    size = keep.shape[1]
     x, y = scalars[3], scalars[4]
-    for target, first in ((send, 1), (keep, 0)):
+    for targets, first in ((sends, 1), ([keep.at[0], keep.at[1]], 0)):
         for second in (1, 0):
             dx, dy = (first, second) if x_first else (second, first)
             block = 2 * lax.bitwise_xor(y, jnp.int32(dy)) + lax.bitwise_xor(x, jnp.int32(dx))
             rows = pl.ds(pl.multiple_of(block * size, size), size)
-            target[second] = times([left[rows, :] for left in lefts], right).astype(target.dtype)
-
-
-def query_key_kernel(scalars, normed_t, normed_far_t, dquery, dkey, q_send, k_send, q_keep, k_keep):
-    by_quarters(scalars, (normed_t,), dquery, q_send, q_keep, True)
-    by_quarters(scalars, (normed_t, normed_far_t), dkey, k_send, k_keep, False)
+            target = targets[second]
+            target[...] = times([left[rows, :] for left in lefts], right).astype(target.dtype)
+
+
+def query_key_kernel(
+    scalars, normed_t, normed_far_t, dquery, dkey, q_later, k_later, q_now, k_now, q_keep, k_keep
+):
+    by_quarters(scalars, (normed_t,), dquery, (q_now, q_later), q_keep, True)
+    by_quarters(scalars, (normed_t, normed_far_t), dkey, (k_now, k_later), k_keep, False)
+
+
+def go_on_kernel(q_keep, q_got, k_keep, k_got, q_later, k_later):
+    for keep, got, later in ((q_keep, q_got, q_later), (k_keep, k_got, k_later)):
+        later[...] = (keep[1] + got[...].astype(jnp.float32)).astype(jnp.bfloat16)
 
 
 def value_out_kernel(scalars, normed_t, normed_far_t, dvalue, mine, theirs, upstream, send, keep):
@@ -301,10 +309,11 @@
         now[...] = keep[0] + got[0].astype(jnp.float32)
 
 
-def pack_query_key_kernel(q_now, q_got, k_now, k_got, packed):
-    size = q_now.shape[1]
-    packed[:, :size] = (q_now[...] + q_got[...].astype(jnp.float32)).astype(jnp.bfloat16)
-    packed[:, size:] = (k_now[...] + k_got[...].astype(jnp.float32)).astype(jnp.bfloat16)
+def pack_query_key_kernel(q_keep, q_first, q_second, k_keep, k_first, k_second, packed):
+    size = q_first.shape[1]
+    for i, (keep, first, second) in enumerate(((q_keep, q_first, q_second), (k_keep, k_first, k_second))):
+        total = keep[0] + first[...].astype(jnp.float32) + second[...].astype(jnp.float32)
+        packed[:, i * size : (i + 1) * size] = total.astype(jnp.bfloat16)
 
 
 def summed_tile(addends, place):
@@ -521,17 +530,24 @@
         24,
     )
     got = lax.ppermute(send, "view", [(i, i ^ 1) for i in range(groups)])
-    results = [shape((2, *q_block), bf16)] * 2 + [shape((2, *q_block), f32)] * 2
-    qk_parts = call(
-        query_key_kernel, results, (scalars, normed_t, normed_far_t, after(dquery, send), dkey), "grad_query_key", SMEM, 24
-    )
-    qk_got = first_exchange(qk_parts)
-    qk_sums = first_sum(qk_parts, qk_got, "first_sum_query_key")
-    qk_got = second_exchange(qk_sums)
+    q_later, k_later, q_now, k_now, q_keep, k_keep = call(
+        query_key_kernel,
+        [shape(q_block, bf16)] * 4 + [shape((2, *q_block), f32)] * 2,
+        (scalars, normed_t, normed_far_t, after(dquery, send), dkey),
+        "grad_query_key",
+        SMEM,
+        24,
+    )
+    q_got, k_got = first_exchange((q_later, k_later))
+    q_first, k_first = first_exchange((q_now, k_now))
+    later = call(
+        go_on_kernel, [shape(q_block, bf16)] * 2, (q_keep, q_got, k_keep, k_got), "first_sum_query_key"
+    )
+    q_second, k_second = second_exchange(later)
     packed = call(
         pack_query_key_kernel,
         [shape((q_size, 2 * part), bf16)],
-        (qk_sums[2], qk_got[0], qk_sums[3], qk_got[1]),
+        (q_keep, q_first, q_second, k_keep, k_first, k_second),
         "second_sum_query_key",
     )[0]
     part_shape = (2, pairs, 2 * o_rows, width // 2)
@@ -540,9 +556,10 @@
         [shape(part_shape, bf16)] * 2 + [shape(part_shape, f32)] * 2,
         (keep, after(got, packed)),
         "view_sum_value_out",
+        cost=MUCH,
     )
     vo_got = first_exchange(vo_parts)
-    packed = across_views(after(packed, vo_parts[0]).reshape(targets, q_rows, 2 * part))
+    packed = across_views(packed.reshape(targets, q_rows, 2 * part))
     grad_query, grad_key = call(
         functools.partial(last_query_key_kernel, rows),
         [shape((q_rows, inner), f32)] * 2,
@@ -550,7 +567,7 @@
         "last_sum_query_key",
     )
 
-    vo_sums = first_sum(vo_parts, vo_got, "first_sum_value_out", MUCH)
+    vo_sums = first_sum(vo_parts, vo_got, "first_sum_value_out")
     v_got, o_got = second_exchange(vo_sums)
     addends = (vo_sums[3], o_got, vo_sums[2], v_got)
     for bit in reversed(range(1, pairs.bit_length() - 1)):

time: 90.1 us -> 91.7 us (1.018)
  waiting for transfers between devices: 41.8 us -> 39.4 us
  Pallas kernels: 18.7 us -> 20.8 us
  starting transfers between devices: 27.6 us -> 29.5 us
    all_to_all x1, waiting for transfers between devices: 6.87 us -> 0.01 us  [across_views(): lax.all_to_all(packed, ('view', 'row'), split_axis=0, concat_axis=0, tile...]
    ppermute x1, waiting for transfers between devices: 0.82 us -> 3.96 us  [shards(): lax.ppermute(far_same, 'view', [(i, i ^ 2) for i in range(groups)])]
    ppermute x2 -> x3, waiting for transfers between devices: 13.5 us -> 15.7 us  [first_exchange(): lax.ppermute(sends[0], 'scene', along_x)]
    ppermute x2, waiting for transfers between devices: 4.39 us -> 2.22 us  [second_exchange(): lax.ppermute(sums[1], 'scene', along_x)]
    pallas_call x10, Pallas kernels: 9.42 us -> 11.5 us  [call(): pl.pallas_call(kernel_body, in_specs=[first] + [VMEM] * (len(operands) -...]
    ppermute x1, waiting for transfers between devices: 0.63 us -> 2.52 us  [shards(): lax.ppermute(far_cross, ('view', 'row'), [(i, i ^ 5) for i in range(targe...]
    ppermute x1, starting transfers between devices: 1.57 us -> 0.13 us  [shards(): lax.ppermute(far_cross, ('view', 'row'), [(i, i ^ 5) for i in range(targe...]
    ppermute x1, starting transfers between devices: 1.19 us -> 2.63 us  [shards(): lax.ppermute(far_same, 'view', [(i, i ^ 2) for i in range(groups)])]
  transfers between devices with their start and end apart: 25 -> 27, of which waited for: 16 -> 16; matrix products, arithmetic and copies ran while one was open for 0% -> 0% of each run, Pallas kernels for 14% -> 15%
where the time goes in v14:
time: 91.7 us; the launch traced here: 91.5 us
  waiting for transfers between devices  39.4 us (43%)
  starting transfers between devices  29.5 us (32%)
  Pallas kernels  20.8 us (23%)
    ppermute x3, waiting for transfers between devices, first_exchange(): lax.ppermute(sends[0], 'scene', along_x)  15.7 us
    pallas_call x10, Pallas kernels, call(): pl.pallas_call(kernel_body, in_specs=[first] + [VMEM] * (len(operands) -...  11.5 us
    ppermute x2, waiting for transfers between devices, second_exchange(): lax.ppermute(sums[0], 'scene', along_y)  6.54 us
    ppermute x3, starting transfers between devices, shards(): granted = [lax.ppermute(partners, 'view', pairs) for pairs in between]  5.62 us
    ppermute x3, starting transfers between devices, shards(): lax.ppermute(part_out, 'view', pairs)  4.45 us
    pallas_call x1, Pallas kernels, shards(): pl.pallas_call(project_kernel, in_specs=[SMEM] + [VMEM] * 10, out_specs=[...  4.13 us
    ppermute x1, waiting for transfers between devices, shards(): lax.ppermute(far_same, 'view', [(i, i ^ 2) for i in range(groups)])  3.96 us
    all_to_all x1, starting transfers between devices, across_views(): lax.all_to_all(packed, ('view', 'row'), split_axis=0, concat_axis=0, tile...  3.6 us
  transfers between devices with their start and end apart: 27, of which 16 were waited for; matrix products, arithmetic and copies ran while one was open for 0% of the time, Pallas kernels for 15%

profile of v14, /device:TPU:0, one launch (start us, length us, event | category | flops | bytes accessed | tf_op | source)
XLA Modules:
  0.0 91.5 jit_solution(9726498380670333356)
XLA Ops:
  0.6 0.8 copy.13.partners
  1.4 3.0 %collective-permute-start.2 = (s32[1,4,3]{2,1,0:T(4,128)S(1)}, s32[1,4,3]{2,1,0:T(4,128)S(1)}, u32[]{:S(2)}, u32[]{:S(2)}) collective-permute-start(s32[1,4,3]{2,1,0:T(4,128)S(1)} %copy.13.partners), channel_id=1, source_target_pairs={{0,2},{2,0},{4,6},{6,4},{1,3},{3,1},{5,7},{7,5},{8,10},{10,8},{12,... | collective-permute-start | bytes 152 | tf_op jit(solution)/shard_map/ppermute | solution.py:416
  4.4 2.6 %collective-permute-start.1 = (s32[1,4,3]{2,1,0:T(4,128)S(1)}, s32[1,4,3]{2,1,0:T(4,128)S(1)}, u32[]{:S(2)}, u32[]{:S(2)}) collective-permute-start(s32[1,4,3]{2,1,0:T(4,128)S(1)} %copy.13.partners), channel_id=1, source_target_pairs={{0,4},{2,6},{4,0},{6,2},{1,5},{3,7},{5,1},{7,3},{8,12},{10,14},{12... | collective-permute-start | bytes 152 | tf_op jit(solution)/shard_map/ppermute | solution.py:416
  7.0 0.0 collective-permute-start
  7.0 0.5 collective-permute-start.7
  7.5 1.2 %alive.1 = s32[16]{0:T(128)S(1)} custom-call(s32[1,4,3]{2,1,0:T(4,128)S(1)} %copy.13.partners), custom_call_target="tpu_custom_call" | custom-call | flops 40000000000 | bytes 1 | tf_op jit(solution)/shard_map/alive/pallas_call | solution.py:406
  8.8 0.1 stack.23.scalars
  8.9 0.0 copy-start.5
  8.9 0.0 copy-start.6
  8.9 0.0 copy-start.7
  8.9 0.0 collective-permute-done.1.refs_1_
  8.9 3.5 %collective-permute-done.refs_0_ = s32[1,4,3]{2,1,0:T(4,128)S(1)} collective-permute-done((s32[1,4,3]{2,1,0:T(4,128)S(1)}, s32[1,4,3]{2,1,0:T(4,128)S(1)}, u32[]{:S(2)}, u32[]{:S(2)}) %collective-permute-start) | collective-permute-done | bytes 80 | tf_op jit(solution)/shard_map/ppermute | solution.py:416
  12.4 0.8 pick.1
  13.2 0.4 collective-permute-start.3
  13.6 0.0 collective-permute-start.4
  13.6 4.0 %collective-permute-start.5 = (bf16[32,1536]{1,0:T(8,128)(2,1)S(1)}, bf16[32,1536]{1,0:T(8,128)(2,1)S(1)}, u32[]{:S(2)}, u32[]{:S(2)}) collective-permute-start(bf16[32,1536]{1,0:T(8,128)(2,1)S(1)} %get-tuple-element.67), channel_id=1, source_target_pairs={{0,2},{2,0},{4,6},{6,4},{1,3},{3,1},{5,7},{7,5},{8,10},{10,8},{12,... | collective-permute-start | bytes 294920 | tf_op jit(solution)/shard_map/ppermute | solution.py:433
  17.6 0.0 collective-permute-done.6.lat_other
  17.7 4.1 %project.1 = (bf16[1536,256]{1,0:T(8,128)(2,1)S(1)}, bf16[256,384]{1,0:T(8,128)(2,1)S(1)}, bf16[256,384]{1,0:T(8,128)(2,1)S(1)}, bf16[256,1536]{1,0:T(8,128)(2,1...) custom-call(s32[5]{0:T(128)S(1)} %stack.23.scalars, ...), custom_call_target="tpu_custom_call" | custom-call | flops 1 | bytes 1 | tf_op jit(solution)/shard_map/project/pallas_call | solution.py:435
  21.9 0.4 collective-permute-done.4.refs_1_
  22.3 0.1 collective-permute-start.8
  22.4 0.4 collective-permute-start.9
  22.8 0.1 collective-permute-start.10
  22.9 0.7 collective-permute-done.8.refs_3_
  23.6 0.2 collective-permute-done.9.refs_4_
  23.7 0.4 collective-permute-done.10.refs_5_
  24.1 3.2 %attention_forward.1 = (bf16[1536,192]{1,0:T(8,128)(2,1)S(1)}, bf16[192,384]{1,0:T(8,128)(2,1)S(1)}, bf16[192,384]{1,0:T(8,128)(2,1)S(1)}, f32[3,64,512]{2,1,0:T...) custom-call(s32[5]{0:T(128)S(1)} %stack.23.scalars, ...), custom_call_target="tpu_custom_call" | custom-call | flops 1 | bytes 1 | tf_op jit(solution)/shard_map/attention_forward/pallas_call | solution.py:471
  27.3 0.2 collective-permute-start.11
  27.5 1.6 %attention_backward.1 = (bf16[256,384]{1,0:T(8,128)(2,1)S(1)}, bf16[448,384]{1,0:T(8,128)(2,1)S(1)}) custom-call(bf16[3,512,128]{2,1,0:T(8,128)(2,1)S(1)} %get-tuple-element.74.refs_6_.query_stack, bf16[3,512,128]{2,1,0:T(8,128)(2,1)S(1)} %get-tuple-element.75.refs_7_.grad_stack, f32[3,64,512]{2,1,0:T(8,128)S(1)} %get-tuple-element.79.dprob_own, ...), custom_call_target="tpu_custom_call" | custom-call | flops 1 | bytes 1 | tf_op jit(solution)/shard_map/attention_backward/pallas_call | solution.py:459
  29.1 2.5 %grad_value_out.1 = (bf16[2,2,2,48,1536]{4,3,2,1,0:T(8,128)(2,1)}, f32[2,2,2,48,1536]{4,3,2,1,0:T(8,128)S(1)}) custom-call(s32[5]{0:T(128)S(1)} %stack.23.scalars, bf16[1536,256]{1,0:T(8,128)(2,1)S(1)} %get-tuple-element.69.normed_t, bf16[1536,192]{1,0:T(8,128)(2,1)S(1)} %get-tuple-element.78.normed_far_t, bf16[448,384]{1,0:T(8,128)(2,1)S(1)} %get-tuple-element.88.dvalue, ...), custom_call_target="tpu_custom_call" | custom-call | flops 1 | bytes 1 | tf_op jit(solution)/shard_map/grad_value_out/pallas_call | solution.py:459
  31.6 0.3 collective-permute-start.18
  31.9 1.9 %grad_query_key.1 = (bf16[384,384]{1,0:T(8,128)(2,1)S(1)}, bf16[384,384]{1,0:T(8,128)(2,1)S(1)}, bf16[384,384]{1,0:T(8,128)(2,1)S(1)}, bf16[384,384]{1,0:T(8,128...) custom-call(s32[5]{0:T(128)S(1)} %stack.23.scalars, ...), custom_call_target="tpu_custom_call" | custom-call | flops 1 | bytes 1 | tf_op jit(solution)/shard_map/grad_query_key/pallas_call | solution.py:459
  33.8 1.6 %collective-permute-start.13 = (bf16[384,384]{1,0:T(8,128)(2,1)S(1)}, bf16[384,384]{1,0:T(8,128)(2,1)S(1)}, u32[]{:S(2)}, u32[]{:S(2)}) collective-permute-start(bf16[384,384]{1,0:T(8,128)(2,1)S(1)} %get-tuple-element.95), channel_id=1, source_target_pairs={{0,8},{8,0},{16,24},{24,16},{1,9},{9,1},{17,25},{25,17},{2,10},{10... | collective-permute-start | bytes 884744 | tf_op jit(solution)/shard_map/ppermute | solution.py:509
  35.4 1.5 %collective-permute-start.14 = (bf16[384,384]{1,0:T(8,128)(2,1)S(1)}, bf16[384,384]{1,0:T(8,128)(2,1)S(1)}, u32[]{:S(2)}, u32[]{:S(2)}) collective-permute-start(bf16[384,384]{1,0:T(8,128)(2,1)S(1)} %get-tuple-element.97), channel_id=1, source_target_pairs={{0,16},{8,24},{16,0},{24,8},{1,17},{9,25},{17,1},{25,9},{2,18},{10... | collective-permute-start | bytes 884744 | tf_op jit(solution)/shard_map/ppermute | solution.py:509
  36.9 0.5 collective-permute-start.12
  37.4 0.5 collective-permute-start.16
  38.0 5.8 %collective-permute-done.13.q_got = bf16[384,384]{1,0:T(8,128)(2,1)S(1)} collective-permute-done((bf16[384,384]{1,0:T(8,128)(2,1)S(1)}, bf16[384,384]{1,0:T(8,128)(2,1)S(1)}, u32[]{:S(2)}, u32[]{:S(2)}) %collective-permute-start.13) | collective-permute-done | bytes 294944 | tf_op jit(solution)/shard_map/ppermute | solution.py:509
  43.8 1.5 %collective-permute-done.14.k_got = bf16[384,384]{1,0:T(8,128)(2,1)S(1)} collective-permute-done((bf16[384,384]{1,0:T(8,128)(2,1)S(1)}, bf16[384,384]{1,0:T(8,128)(2,1)S(1)}, u32[]{:S(2)}, u32[]{:S(2)}) %collective-permute-start.14) | collective-permute-done | bytes 294944 | tf_op jit(solution)/shard_map/ppermute | solution.py:509
  45.3 0.1 first_sum_query_key.1
  45.4 1.6 %collective-permute-start.15 = (bf16[384,384]{1,0:T(8,128)(2,1)S(1)}, bf16[384,384]{1,0:T(8,128)(2,1)S(1)}, u32[]{:S(2)}, u32[]{:S(2)}) collective-permute-start(bf16[384,384]{1,0:T(8,128)(2,1)S(1)} %get-tuple-element.98), channel_id=1, source_target_pairs={{0,16},{8,24},{16,0},{24,8},{1,17},{9,25},{17,1},{25,9},{2,18},{10... | collective-permute-start | bytes 884744 | tf_op jit(solution)/shard_map/ppermute | solution.py:517
  47.0 0.5 collective-permute-start.17
  47.5 2.5 %collective-permute-done.12.q_first = bf16[384,384]{1,0:T(8,128)(2,1)S(1)} collective-permute-done((bf16[384,384]{1,0:T(8,128)(2,1)S(1)}, bf16[384,384]{1,0:T(8,128)(2,1)S(1)}, u32[]{:S(2)}, u32[]{:S(2)}) %collective-permute-start.12) | collective-permute-done | bytes 294944 | tf_op jit(solution)/shard_map/ppermute | solution.py:509
  50.1 1.5 %collective-permute-done.16.k_first = bf16[384,384]{1,0:T(8,128)(2,1)S(1)} collective-permute-done((bf16[384,384]{1,0:T(8,128)(2,1)S(1)}, bf16[384,384]{1,0:T(8,128)(2,1)S(1)}, u32[]{:S(2)}, u32[]{:S(2)}) %collective-permute-start.16) | collective-permute-done | bytes 294944 | tf_op jit(solution)/shard_map/ppermute | solution.py:509
  51.6 5.1 %collective-permute-done.15.q_second = bf16[384,384]{1,0:T(8,128)(2,1)S(1)} collective-permute-done((bf16[384,384]{1,0:T(8,128)(2,1)S(1)}, bf16[384,384]{1,0:T(8,128)(2,1)S(1)}, u32[]{:S(2)}, u32[]{:S(2)}) %collective-permute-start.15) | collective-permute-done | bytes 294944 | tf_op jit(solution)/shard_map/ppermute | solution.py:517
  56.7 0.0 collective-permute-done.17.k_second
  56.7 1.0 %second_sum_query_key.1 = bf16[384,768]{1,0:T(8,128)(2,1)} custom-call(f32[2,384,384]{2,1,0:T(8,128)S(1)} %get-tuple-element.93.q_keep, bf16[384,384]{1,0:T(8,128)(2,1)S(1)} %collective-permute-done.12.q_first, bf16[384,384]{1,0:T(8,128)(2,1)S(1)} %collective-permute-done.15.q_second, f32[2,384,384]{2,1,0:T(8,128)S(1)} %get-tuple-element.96.k_keep, ...), custom_call_target="tpu_custom_call" | custom-call | flops 1 | bytes 1 | tf_op jit(solution)/shard_map/second_sum_query_key/pallas_call | solution.py:459
  57.8 3.6 %all-to-all-start = ((bf16[8,48,768]{2,1,0:T(8,128)(2,1)}), bf16[8,48,768]{2,1,0:T(8,128)(2,1)S(1)}, u32[]{:S(2)}, u32[]{:S(2)}) async-start(bf16[8,48,768]{2,1,0:T(8,128)(2,1)} %bitcast.7), calls=%async_computation | async-start | bytes 1179648 | tf_op jit(solution)/shard_map/all_to_all | solution.py:520
  61.4 1.5 %view_sum_value_out.1 = (bf16[2,2,48,768]{3,2,1,0:T(8,128)(2,1)S(1)}, bf16[2,2,48,768]{3,2,1,0:T(8,128)(2,1)S(1)}, f32[2,2,48,768]{3,2,1,0:T(8,128)S(1)}, f32[2,2,48,768]{3,2,1,0:T(8,128)S(1)}) custom-call(f32[2,2,2,48,1536]{4,3,2,1,0:T(8,128)S(1)} %get-tuple-element.103.keep, bf16[2,2,2,48,1536]{4,3,2,1,0:T(8,128)(2,1)} %collective-permute-done.18.got), custom_call_target="tpu_custom_call" | custom-call | flops 40000000000 | bytes 1 | tf_op jit(solution)/shard_map/view_sum_value_out/pallas_call | solution.py:459
  62.9 0.6 collective-permute-start.19
  63.5 1.5 %collective-permute-start.20 = (bf16[2,2,48,768]{3,2,1,0:T(8,128)(2,1)S(1)}, bf16[2,2,48,768]{3,2,1,0:T(8,128)(2,1)S(1)}, u32[]{:S(2)}, u32[]{:S(2)}) collective-permute-start(bf16[2,2,48,768]{3,2,1,0:T(8,128)(2,1)S(1)} %get-tuple-element.108), channel_id=1, source_target_pairs={{0,16},{8,24},{16,0},{24,8},{1,17},{9,25},{17,1},{25,9},{2,18},{10... | collective-permute-start | bytes 884744 | tf_op jit(solution)/shard_map/ppermute | solution.py:509
  65.0 7.4 %collective-permute-done.19.x_got = bf16[2,2,48,768]{3,2,1,0:T(8,128)(2,1)S(1)} collective-permute-done((bf16[2,2,48,768]{3,2,1,0:T(8,128)(2,1)S(1)}, bf16[2,2,48,768]{3,2,1,0:T(8,128)(2,1)S(1)}, u32[]{:S(2)}, u32[]{:S(2)}) %collective-permute-start.19) | collective-permute-done | bytes 294944 | tf_op jit(solution)/shard_map/ppermute | solution.py:509
  72.4 0.3 collective-permute-done.20.y_got
  72.6 0.1 first_sum_value_out.1
  72.8 1.6 %collective-permute-start.21 = (bf16[2,48,768]{2,1,0:T(8,128)(2,1)S(1)}, bf16[2,48,768]{2,1,0:T(8,128)(2,1)S(1)}, u32[]{:S(2)}, u32[]{:S(2)}) collective-permute-start(bf16[2,48,768]{2,1,0:T(8,128)(2,1)S(1)} %get-tuple-element.110), channel_id=1, source_target_pairs={{0,8},{8,0},{16,24},{24,16},{1,9},{9,1},{17,25},{25,17},{2,10},{10... | collective-permute-start | bytes 442376 | tf_op jit(solution)/shard_map/ppermute | solution.py:517
  74.3 1.5 %collective-permute-start.22 = (bf16[2,48,768]{2,1,0:T(8,128)(2,1)S(1)}, bf16[2,48,768]{2,1,0:T(8,128)(2,1)S(1)}, u32[]{:S(2)}, u32[]{:S(2)}) collective-permute-start(bf16[2,48,768]{2,1,0:T(8,128)(2,1)S(1)} %get-tuple-element.112), channel_id=1, source_target_pairs={{0,16},{8,24},{16,0},{24,8},{1,17},{9,25},{17,1},{25,9},{2,18},{10... | collective-permute-start | bytes 442376 | tf_op jit(solution)/shard_map/ppermute | solution.py:517
  75.8 2.2 %collective-permute-done.21.refs_1_ = bf16[2,48,768]{2,1,0:T(8,128)(2,1)S(1)} collective-permute-done((bf16[2,48,768]{2,1,0:T(8,128)(2,1)S(1)}, bf16[2,48,768]{2,1,0:T(8,128)(2,1)S(1)}, u32[]{:S(2)}, u32[]{:S(2)}) %collective-permute-start.21) | collective-permute-done | bytes 147488 | tf_op jit(solution)/shard_map/ppermute | solution.py:517
  78.0 1.4 %collective-permute-done.22.refs_3_ = bf16[2,48,768]{2,1,0:T(8,128)(2,1)S(1)} collective-permute-done((bf16[2,48,768]{2,1,0:T(8,128)(2,1)S(1)}, bf16[2,48,768]{2,1,0:T(8,128)(2,1)S(1)}, u32[]{:S(2)}, u32[]{:S(2)}) %collective-permute-start.22) | collective-permute-done | bytes 147488 | tf_op jit(solution)/shard_map/ppermute | solution.py:517
  79.5 0.6 last_parts_value_out.1
  80.1 0.1 collective-permute-start.24
  80.2 2.6 %collective-permute-start.23 = (bf16[24,1536]{1,0:T(8,128)(2,1)S(1)}, bf16[24,1536]{1,0:T(8,128)(2,1)S(1)}, u32[]{:S(2)}, u32[]{:S(2)}) collective-permute-start(bf16[24,1536]{1,0:T(8,128)(2,1)S(1)} %get-tuple-element.115), channel_id=1, source_target_pairs={{0,4},{2,6},{4,0},{6,2},{1,5},{3,7},{5,1},{7,3},{8,12},{10,14},{12... | collective-permute-start | bytes 221192 | tf_op jit(solution)/shard_map/ppermute | solution.py:589
  82.8 0.1 collective-permute-start.25
  82.9 0.8 last_sum_query_key.1
  83.7 4.0 %collective-permute-done.23.far_same = bf16[24,1536]{1,0:T(8,128)(2,1)S(1)} collective-permute-done((bf16[24,1536]{1,0:T(8,128)(2,1)S(1)}, bf16[24,1536]{1,0:T(8,128)(2,1)S(1)}, u32[]{:S(2)}, u32[]{:S(2)}) %collective-permute-start.23) | collective-permute-done | bytes 73760 | tf_op jit(solution)/shard_map/ppermute | solution.py:589
  87.7 2.5 %collective-permute-done.25.far_cross = bf16[24,1536]{1,0:T(8,128)(2,1)S(1)} collective-permute-done((bf16[24,1536]{1,0:T(8,128)(2,1)S(1)}, bf16[24,1536]{1,0:T(8,128)(2,1)S(1)}, u32[]{:S(2)}, u32[]{:S(2)}) %collective-permute-start.25) | collective-permute-done | bytes 73760 | tf_op jit(solution)/shard_map/ppermute | solution.py:590
  90.2 1.3 %last_sum_value_out.1 = (f32[48,768]{1,0:T(8,128)}, f32[24,1536]{1,0:T(8,128)}) custom-call(s32[5]{0:T(128)S(1)} %stack.23.scalars, f32[24,1536]{1,0:T(8,128)S(1)} %get-tuple-element.114.mine, bf16[24,1536]{1,0:T(8,128)(2,1)S(1)} %collective-permute-done.23.far_same, f32[24,1536]{1,0:T(8,128)S(1)} %collective-permute-done.24.near_cross, ...), custom_call_target="tpu_custom_call" | custom-call | flops 1 | bytes 1 | tf_op jit(solution)/shard_map/last_sum_value_out/pallas_call | solution.py:459
  (22 shorter events, 0.0 us)
Async XLA Ops:
  1.4 7.5 %collective-permute-start.2 = (s32[1,4,3]{2,1,0:T(4,128)S(1)}, s32[1,4,3]{2,1,0:T(4,128)S(1)}, u32[]{:S(2)}, u32[]{:S(2)}) collective-permute-start(s32[1,4,3]{2,1,0:T(4,128)S(1)} %copy.13.partners), channel_id=1, source_target_pairs={{0,2},{2,0},{4,6},{6,4},{1,3},{3,1},{5,7},{7,5},{8,10},{10,8},{12,... | collective-permute-start | bytes 152 | tf_op jit(solution)/shard_map/ppermute | solution.py:416
  4.4 4.5 %collective-permute-start.1 = (s32[1,4,3]{2,1,0:T(4,128)S(1)}, s32[1,4,3]{2,1,0:T(4,128)S(1)}, u32[]{:S(2)}, u32[]{:S(2)}) collective-permute-start(s32[1,4,3]{2,1,0:T(4,128)S(1)} %copy.13.partners), channel_id=1, source_target_pairs={{0,4},{2,6},{4,0},{6,2},{1,5},{3,7},{5,1},{7,3},{8,12},{10,14},{12... | collective-permute-start | bytes 152 | tf_op jit(solution)/shard_map/ppermute | solution.py:416
  7.0 5.4 %collective-permute-start = (s32[1,4,3]{2,1,0:T(4,128)S(1)}, s32[1,4,3]{2,1,0:T(4,128)S(1)}, u32[]{:S(2)}, u32[]{:S(2)}) collective-permute-start(s32[1,4,3]{2,1,0:T(4,128)S(1)} %copy.13.partners), channel_id=1, source_target_pairs={{0,6},{2,4},{4,2},{6,0},{1,7},{3,5},{5,3},{7,1},{8,14},{10,12},{12... | collective-permute-start | bytes 152 | tf_op jit(solution)/shard_map/ppermute | solution.py:416
  7.0 10.6 %collective-permute-start.6 = (bf16[4,32,1536]{2,1,0:T(8,128)(2,1)}, bf16[4,32,1536]{2,1,0:T(8,128)(2,1)S(1)}, u32[]{:S(2)}, u32[]{:S(2)}) collective-permute-start(bf16[4,32,1536]{2,1,0:T(8,128)(2,1)} %bitcast.8), channel_id=1, source_target_pairs={{0,1},{1,0},{2,3},{3,2},{4,5},{5,4},{6,7},{7,6},{8,9},{9,8},{10,11... | collective-permute-start | bytes 1179656 | tf_op jit(solution)/shard_map/ppermute | solution.py:421
  7.0 10.6 %collective-permute-start.7 = (bf16[4,32,1536]{2,1,0:T(8,128)(2,1)}, bf16[4,32,1536]{2,1,0:T(8,128)(2,1)S(1)}, u32[]{:S(2)}, u32[]{:S(2)}) collective-permute-start(bf16[4,32,1536]{2,1,0:T(8,128)(2,1)} %bitcast.11), channel_id=1, source_target_pairs={{0,1},{1,0},{2,3},{3,2},{4,5},{5,4},{6,7},{7,6},{8,9},{9,8},{10,11... | collective-permute-start | bytes 1179656 | tf_op jit(solution)/shard_map/ppermute | solution.py:422
  7.5 4.9 %copy-start.4 = (bf16[1,4,1,32,1536]{4,3,2,1,0:T(8,128)(2,1)S(1)}, bf16[1,4,1,32,1536]{4,3,2,1,0:T(8,128)(2,1)}, u32[]{:S(2)}) copy-start(bf16[1,4,1,32,1536]{4,3,2,1,0:T(8,128)(2,1)} %param.10) | copy-start | bytes 1179652
  8.8 8.8 %copy-start = (bf16[1536,768]{1,0:T(8,128)(2,1)S(1)}, bf16[1536,768]{1,0:T(8,128)(2,1)}, u32[]{:S(2)}) copy-start(bf16[1536,768]{1,0:T(8,128)(2,1)} %refs_11_.1) | copy-start | bytes 7077892
  8.9 8.8 %copy-start.1 = (bf16[1536,768]{1,0:T(8,128)(2,1)S(1)}, bf16[1536,768]{1,0:T(8,128)(2,1)}, u32[]{:S(2)}) copy-start(bf16[1536,768]{1,0:T(8,128)(2,1)} %refs_12_.1) | copy-start | bytes 7077892
  8.9 8.8 %copy-start.2 = (bf16[1536,768]{1,0:T(8,128)(2,1)S(1)}, bf16[1536,768]{1,0:T(8,128)(2,1)}, u32[]{:S(2)}) copy-start(bf16[1536,768]{1,0:T(8,128)(2,1)} %w_query.1) | copy-start | bytes 7077892
  8.9 8.8 %copy-start.3 = (bf16[768,1536]{1,0:T(8,128)(2,1)S(1)}, bf16[768,1536]{1,0:T(8,128)(2,1)}, u32[]{:S(2)}) copy-start(bf16[768,1536]{1,0:T(8,128)(2,1)} %w_out.1) | copy-start | bytes 7077892
  8.9 8.8 %copy-start.5 = (bf16[1,4,1,32,1536]{4,3,2,1,0:T(8,128)(2,1)S(1)}, bf16[1,4,1,32,1536]{4,3,2,1,0:T(8,128)(2,1)}, u32[]{:S(2)}) copy-start(bf16[1,4,1,32,1536]{4,3,2,1,0:T(8,128)(2,1)} %param.18) | copy-start | bytes 1179652
  8.9 8.8 %copy-start.6 = (bf16[9,1536]{1,0:T(8,128)(2,1)S(1)}, bf16[9,1536]{1,0:T(8,128)(2,1)}, u32[]{:S(2)}) copy-start(bf16[9,1536]{1,0:T(8,128)(2,1)} %taps.1) | copy-start | bytes 82948
  8.9 8.8 %copy-start.7 = (f32[1536]{0:T(1024)S(1)}, f32[1536]{0:T(1024)}, u32[]{:S(2)}) copy-start(f32[1536]{0:T(1024)} %refs_10_.1) | copy-start | bytes 18436
  13.2 8.7 %collective-permute-start.3 = (bf16[32,1536]{1,0:T(8,128)(2,1)S(1)}, bf16[32,1536]{1,0:T(8,128)(2,1)S(1)}, u32[]{:S(2)}, u32[]{:S(2)}) collective-permute-start(bf16[32,1536]{1,0:T(8,128)(2,1)S(1)} %get-tuple-element.65), channel_id=1, source_target_pairs={{0,6},{2,4},{4,2},{6,0},{1,7},{3,5},{5,3},{7,1},{8,14},{10,12},{12... | collective-permute-start | bytes 294920 | tf_op jit(solution)/shard_map/ppermute | solution.py:433
  13.6 8.7 %collective-permute-start.4 = (bf16[32,1536]{1,0:T(8,128)(2,1)S(1)}, bf16[32,1536]{1,0:T(8,128)(2,1)S(1)}, u32[]{:S(2)}, u32[]{:S(2)}) collective-permute-start(bf16[32,1536]{1,0:T(8,128)(2,1)S(1)} %get-tuple-element.66), channel_id=1, source_target_pairs={{0,4},{2,6},{4,0},{6,2},{1,5},{3,7},{5,1},{7,3},{8,12},{10,14},{12... | collective-permute-start | bytes 294920 | tf_op jit(solution)/shard_map/ppermute | solution.py:433
  13.6 8.7 %collective-permute-start.5 = (bf16[32,1536]{1,0:T(8,128)(2,1)S(1)}, bf16[32,1536]{1,0:T(8,128)(2,1)S(1)}, u32[]{:S(2)}, u32[]{:S(2)}) collective-permute-start(bf16[32,1536]{1,0:T(8,128)(2,1)S(1)} %get-tuple-element.67), channel_id=1, source_target_pairs={{0,2},{2,0},{4,6},{6,4},{1,3},{3,1},{5,7},{7,5},{8,10},{10,8},{12,... | collective-permute-start | bytes 294920 | tf_op jit(solution)/shard_map/ppermute | solution.py:433
  22.3 1.3 %collective-permute-start.8 = (bf16[32,1536]{1,0:T(8,128)(2,1)S(1)}, bf16[32,1536]{1,0:T(8,128)(2,1)S(1)}, u32[]{:S(2)}, u32[]{:S(2)}) collective-permute-start(bf16[32,1536]{1,0:T(8,128)(2,1)S(1)} %collective-permute-done.3.refs_0_), channel_id=1, source_target_pairs={{0,1},{1,0},{2,3},{3,2},{4,5},{5,4},{6,7},{7,6},{8,9},{9,8},{10,11... | collective-permute-start | bytes 294920 | tf_op jit(solution)/shard_map/ppermute | solution.py:456
  22.4 1.4 %collective-permute-start.9 = (bf16[32,1536]{1,0:T(8,128)(2,1)S(1)}, bf16[32,1536]{1,0:T(8,128)(2,1)S(1)}, u32[]{:S(2)}, u32[]{:S(2)}) collective-permute-start(bf16[32,1536]{1,0:T(8,128)(2,1)S(1)} %collective-permute-done.4.refs_1_), channel_id=1, source_target_pairs={{0,1},{1,0},{2,3},{3,2},{4,5},{5,4},{6,7},{7,6},{8,9},{9,8},{10,11... | collective-permute-start | bytes 294920 | tf_op jit(solution)/shard_map/ppermute | solution.py:456
  22.8 1.3 %collective-permute-start.10 = (bf16[32,1536]{1,0:T(8,128)(2,1)S(1)}, bf16[32,1536]{1,0:T(8,128)(2,1)S(1)}, u32[]{:S(2)}, u32[]{:S(2)}) collective-permute-start(bf16[32,1536]{1,0:T(8,128)(2,1)S(1)} %collective-permute-done.5.refs_2_), channel_id=1, source_target_pairs={{0,1},{1,0},{2,3},{3,2},{4,5},{5,4},{6,7},{7,6},{8,9},{9,8},{10,11... | collective-permute-start | bytes 294920 | tf_op jit(solution)/shard_map/ppermute | solution.py:456
  27.3 1.8 %collective-permute-start.11 = (bf16[384,256]{1,0:T(8,128)(2,1)S(1)}, bf16[384,256]{1,0:T(8,128)(2,1)S(1)}, u32[]{:S(2)}, u32[]{:S(2)}) collective-permute-start(bf16[384,256]{1,0:T(8,128)(2,1)S(1)} %get-tuple-element.89.mine), channel_id=1, source_target_pairs={{0,1},{1,0},{2,3},{3,2},{4,5},{5,4},{6,7},{7,6},{8,9},{9,8},{10,11... | collective-permute-start | bytes 589832 | tf_op jit(solution)/shard_map/ppermute | solution.py:491
  31.6 29.8 %collective-permute-start.18 = (bf16[2,2,2,48,1536]{4,3,2,1,0:T(8,128)(2,1)}, bf16[2,2,2,48,1536]{4,3,2,1,0:T(8,128)(2,1)}, u32[]{:S(2)}, u32[]{:S(2)}) collective-permute-start(bf16[2,2,2,48,1536]{4,3,2,1,0:T(8,128)(2,1)} %get-tuple-element.91), channel_id=1, source_target_pairs={{0,2},{2,0},{4,6},{6,4},{1,3},{3,1},{5,7},{7,5},{8,10},{10,8},{12,... | collective-permute-start | bytes 3538952 | tf_op jit(solution)/shard_map/ppermute | solution.py:532
  33.8 9.9 %collective-permute-start.13 = (bf16[384,384]{1,0:T(8,128)(2,1)S(1)}, bf16[384,384]{1,0:T(8,128)(2,1)S(1)}, u32[]{:S(2)}, u32[]{:S(2)}) collective-permute-start(bf16[384,384]{1,0:T(8,128)(2,1)S(1)} %get-tuple-element.95), channel_id=1, source_target_pairs={{0,8},{8,0},{16,24},{24,16},{1,9},{9,1},{17,25},{25,17},{2,10},{10... | collective-permute-start | bytes 884744 | tf_op jit(solution)/shard_map/ppermute | solution.py:509
  35.4 9.9 %collective-permute-start.14 = (bf16[384,384]{1,0:T(8,128)(2,1)S(1)}, bf16[384,384]{1,0:T(8,128)(2,1)S(1)}, u32[]{:S(2)}, u32[]{:S(2)}) collective-permute-start(bf16[384,384]{1,0:T(8,128)(2,1)S(1)} %get-tuple-element.97), channel_id=1, source_target_pairs={{0,16},{8,24},{16,0},{24,8},{1,17},{9,25},{17,1},{25,9},{2,18},{10... | collective-permute-start | bytes 884744 | tf_op jit(solution)/shard_map/ppermute | solution.py:509
  36.9 13.2 %collective-permute-start.12 = (bf16[384,384]{1,0:T(8,128)(2,1)S(1)}, bf16[384,384]{1,0:T(8,128)(2,1)S(1)}, u32[]{:S(2)}, u32[]{:S(2)}) collective-permute-start(bf16[384,384]{1,0:T(8,128)(2,1)S(1)} %get-tuple-element.94), channel_id=1, source_target_pairs={{0,8},{8,0},{16,24},{24,16},{1,9},{9,1},{17,25},{25,17},{2,10},{10... | collective-permute-start | bytes 884744 | tf_op jit(solution)/shard_map/ppermute | solution.py:509
  37.4 14.2 %collective-permute-start.16 = (bf16[384,384]{1,0:T(8,128)(2,1)S(1)}, bf16[384,384]{1,0:T(8,128)(2,1)S(1)}, u32[]{:S(2)}, u32[]{:S(2)}) collective-permute-start(bf16[384,384]{1,0:T(8,128)(2,1)S(1)} %get-tuple-element.99), channel_id=1, source_target_pairs={{0,16},{8,24},{16,0},{24,8},{1,17},{9,25},{17,1},{25,9},{2,18},{10... | collective-permute-start | bytes 884744 | tf_op jit(solution)/shard_map/ppermute | solution.py:509
  45.4 11.3 %collective-permute-start.15 = (bf16[384,384]{1,0:T(8,128)(2,1)S(1)}, bf16[384,384]{1,0:T(8,128)(2,1)S(1)}, u32[]{:S(2)}, u32[]{:S(2)}) collective-permute-start(bf16[384,384]{1,0:T(8,128)(2,1)S(1)} %get-tuple-element.98), channel_id=1, source_target_pairs={{0,16},{8,24},{16,0},{24,8},{1,17},{9,25},{17,1},{25,9},{2,18},{10... | collective-permute-start | bytes 884744 | tf_op jit(solution)/shard_map/ppermute | solution.py:517
  47.0 9.7 %collective-permute-start.17 = (bf16[384,384]{1,0:T(8,128)(2,1)S(1)}, bf16[384,384]{1,0:T(8,128)(2,1)S(1)}, u32[]{:S(2)}, u32[]{:S(2)}) collective-permute-start(bf16[384,384]{1,0:T(8,128)(2,1)S(1)} %get-tuple-element.100), channel_id=1, source_target_pairs={{0,8},{8,0},{16,24},{24,16},{1,9},{9,1},{17,25},{25,17},{2,10},{10... | collective-permute-start | bytes 884744 | tf_op jit(solution)/shard_map/ppermute | solution.py:517
  57.8 25.2 %all-to-all-start = ((bf16[8,48,768]{2,1,0:T(8,128)(2,1)}), bf16[8,48,768]{2,1,0:T(8,128)(2,1)S(1)}, u32[]{:S(2)}, u32[]{:S(2)}) async-start(bf16[8,48,768]{2,1,0:T(8,128)(2,1)} %bitcast.7), calls=%async_computation | async-start | bytes 1179648 | tf_op jit(solution)/shard_map/all_to_all | solution.py:520
  62.9 9.5 %collective-permute-start.19 = (bf16[2,2,48,768]{3,2,1,0:T(8,128)(2,1)S(1)}, bf16[2,2,48,768]{3,2,1,0:T(8,128)(2,1)S(1)}, u32[]{:S(2)}, u32[]{:S(2)}) collective-permute-start(bf16[2,2,48,768]{3,2,1,0:T(8,128)(2,1)S(1)} %get-tuple-element.106), channel_id=1, source_target_pairs={{0,8},{8,0},{16,24},{24,16},{1,9},{9,1},{17,25},{25,17},{2,10},{10... | collective-permute-start | bytes 884744 | tf_op jit(solution)/shard_map/ppermute | solution.py:509
  63.5 9.1 %collective-permute-start.20 = (bf16[2,2,48,768]{3,2,1,0:T(8,128)(2,1)S(1)}, bf16[2,2,48,768]{3,2,1,0:T(8,128)(2,1)S(1)}, u32[]{:S(2)}, u32[]{:S(2)}) collective-permute-start(bf16[2,2,48,768]{3,2,1,0:T(8,128)(2,1)S(1)} %get-tuple-element.108), channel_id=1, source_target_pairs={{0,16},{8,24},{16,0},{24,8},{1,17},{9,25},{17,1},{25,9},{2,18},{10... | collective-permute-start | bytes 884744 | tf_op jit(solution)/shard_map/ppermute | solution.py:509
  72.8 5.3 %collective-permute-start.21 = (bf16[2,48,768]{2,1,0:T(8,128)(2,1)S(1)}, bf16[2,48,768]{2,1,0:T(8,128)(2,1)S(1)}, u32[]{:S(2)}, u32[]{:S(2)}) collective-permute-start(bf16[2,48,768]{2,1,0:T(8,128)(2,1)S(1)} %get-tuple-element.110), channel_id=1, source_target_pairs={{0,8},{8,0},{16,24},{24,16},{1,9},{9,1},{17,25},{25,17},{2,10},{10... | collective-permute-start | bytes 442376 | tf_op jit(solution)/shard_map/ppermute | solution.py:517
  74.3 5.1 %collective-permute-start.22 = (bf16[2,48,768]{2,1,0:T(8,128)(2,1)S(1)}, bf16[2,48,768]{2,1,0:T(8,128)(2,1)S(1)}, u32[]{:S(2)}, u32[]{:S(2)}) collective-permute-start(bf16[2,48,768]{2,1,0:T(8,128)(2,1)S(1)} %get-tuple-element.112), channel_id=1, source_target_pairs={{0,16},{8,24},{16,0},{24,8},{1,17},{9,25},{17,1},{25,9},{2,18},{10... | collective-permute-start | bytes 442376 | tf_op jit(solution)/shard_map/ppermute | solution.py:517
  80.1 10.1 %collective-permute-start.24 = (f32[24,1536]{1,0:T(8,128)S(1)}, f32[24,1536]{1,0:T(8,128)S(1)}, u32[]{:S(2)}, u32[]{:S(2)}) collective-permute-start(f32[24,1536]{1,0:T(8,128)S(1)} %get-tuple-element.116), channel_id=1, source_target_pairs={{0,1},{1,0},{2,3},{3,2},{4,5},{5,4},{6,7},{7,6},{8,9},{9,8},{10,11... | collective-permute-start | bytes 442376 | tf_op jit(solution)/shard_map/ppermute | solution.py:591
  80.2 7.5 %collective-permute-start.23 = (bf16[24,1536]{1,0:T(8,128)(2,1)S(1)}, bf16[24,1536]{1,0:T(8,128)(2,1)S(1)}, u32[]{:S(2)}, u32[]{:S(2)}) collective-permute-start(bf16[24,1536]{1,0:T(8,128)(2,1)S(1)} %get-tuple-element.115), channel_id=1, source_target_pairs={{0,4},{2,6},{4,0},{6,2},{1,5},{3,7},{5,1},{7,3},{8,12},{10,14},{12... | collective-permute-start | bytes 221192 | tf_op jit(solution)/shard_map/ppermute | solution.py:589
  82.8 7.4 %collective-permute-start.25 = (bf16[24,1536]{1,0:T(8,128)(2,1)S(1)}, bf16[24,1536]{1,0:T(8,128)(2,1)S(1)}, u32[]{:S(2)}, u32[]{:S(2)}) collective-permute-start(bf16[24,1536]{1,0:T(8,128)(2,1)S(1)} %get-tuple-element.117), channel_id=1, source_target_pairs={{0,5},{1,4},{2,7},{3,6},{4,1},{5,0},{6,3},{7,2},{8,13},{9,12},{10,... | collective-permute-start | bytes 221192 | tf_op jit(solution)/shard_map/ppermute | solution.py:590

commit v15 on v14

--- a/solution.py
+++ b/solution.py
@@ -556,10 +556,9 @@
         [shape(part_shape, bf16)] * 2 + [shape(part_shape, f32)] * 2,
         (keep, after(got, packed)),
         "view_sum_value_out",
-        cost=MUCH,
     )
     vo_got = first_exchange(vo_parts)
-    packed = across_views(packed.reshape(targets, q_rows, 2 * part))
+    packed = across_views(after(packed, vo_parts[0]).reshape(targets, q_rows, 2 * part))
     grad_query, grad_key = call(
         functools.partial(last_query_key_kernel, rows),
         [shape((q_rows, inner), f32)] * 2,
@@ -567,7 +566,7 @@
         "last_sum_query_key",
     )
 
-    vo_sums = first_sum(vo_parts, vo_got, "first_sum_value_out")
+    vo_sums = first_sum(vo_parts, vo_got, "first_sum_value_out", MUCH)
     v_got, o_got = second_exchange(vo_sums)
     addends = (vo_sums[3], o_got, vo_sums[2], v_got)
     for bit in reversed(range(1, pairs.bit_length() - 1)):

time: 91.7 us -> 90.1 us (0.983)
  Pallas kernels: 20.8 us -> 18.7 us
    all_to_all x1, waiting for transfers between devices: 0.01 us -> 6.87 us  [across_views(): lax.all_to_all(packed, ('view', 'row'), split_axis=0, concat_axis=0, tile...]
    ppermute x3, waiting for transfers between devices: 15.7 us -> 9.62 us  [first_exchange(): lax.ppermute(sends[0], 'scene', along_x)]
    ppermute x1, waiting for transfers between devices: 3.96 us -> 0.82 us  [shards(): lax.ppermute(far_same, 'view', [(i, i ^ 2) for i in range(groups)])]
    ppermute x1, waiting for transfers between devices: 0.01 us -> 2.08 us  [shards(): got = lax.ppermute(send, 'view', [(i, i ^ 1) for i in range(groups)])]
    pallas_call x10, Pallas kernels: 11.5 us -> 9.4 us  [call(): pl.pallas_call(kernel_body, in_specs=[first] + [VMEM] * (len(operands) -...]
    ppermute x1, waiting for transfers between devices: 2.52 us -> 0.63 us  [shards(): lax.ppermute(far_cross, ('view', 'row'), [(i, i ^ 5) for i in range(targe...]
    ppermute x3, waiting for transfers between devices: 3.31 us -> 4.95 us  [first_exchange(): lax.ppermute(sends[1], 'scene', along_y)]
    ppermute x1, starting transfers between devices: 0.13 us -> 1.57 us  [shards(): lax.ppermute(far_cross, ('view', 'row'), [(i, i ^ 5) for i in range(targe...]
  transfers between devices with their start and end apart: 27 -> 27, of which waited for: 16 -> 18; matrix products, arithmetic and copies ran while one was open for 0% -> 0% of each run, Pallas kernels for 15% -> 14%
where the time goes in v15:
time: 90.1 us; the launch traced here: 89.8 us
  waiting for transfers between devices  39.9 us (44%)
  starting transfers between devices  29.5 us (33%)
  Pallas kernels  18.7 us (21%)
    ppermute x3, waiting for transfers between devices, first_exchange(): lax.ppermute(sends[0], 'scene', along_x)  9.62 us
    pallas_call x10, Pallas kernels, call(): pl.pallas_call(kernel_body, in_specs=[first] + [VMEM] * (len(operands) -...  9.4 us
    all_to_all x1, waiting for transfers between devices, across_views(): lax.all_to_all(packed, ('view', 'row'), split_axis=0, concat_axis=0, tile...  6.87 us
    ppermute x2, waiting for transfers between devices, second_exchange(): lax.ppermute(sums[0], 'scene', along_y)  6.62 us
    ppermute x3, starting transfers between devices, shards(): granted = [lax.ppermute(partners, 'view', pairs) for pairs in between]  5.62 us
    ppermute x3, waiting for transfers between devices, first_exchange(): lax.ppermute(sends[1], 'scene', along_y)  4.95 us
    ppermute x3, starting transfers between devices, shards(): lax.ppermute(part_out, 'view', pairs)  4.45 us
    pallas_call x1, Pallas kernels, shards(): pl.pallas_call(project_kernel, in_specs=[SMEM] + [VMEM] * 10, out_specs=[...  4.13 us
  transfers between devices with their start and end apart: 27, of which 18 were waited for; matrix products, arithmetic and copies ran while one was open for 0% of the time, Pallas kernels for 14%

profile of v15, /device:TPU:0, one launch (start us, length us, event | category | flops | bytes accessed | tf_op | source)
XLA Modules:
  0.0 89.8 jit_solution(2585585950230405090)
XLA Ops:
  0.6 0.8 copy.13.partners
  1.4 3.0 %collective-permute-start.2 = (s32[1,4,3]{2,1,0:T(4,128)S(1)}, s32[1,4,3]{2,1,0:T(4,128)S(1)}, u32[]{:S(2)}, u32[]{:S(2)}) collective-permute-start(s32[1,4,3]{2,1,0:T(4,128)S(1)} %copy.13.partners), channel_id=1, source_target_pairs={{0,2},{2,0},{4,6},{6,4},{1,3},{3,1},{5,7},{7,5},{8,10},{10,8},{12,... | collective-permute-start | bytes 152 | tf_op jit(solution)/shard_map/ppermute | solution.py:416
  4.4 2.6 %collective-permute-start.1 = (s32[1,4,3]{2,1,0:T(4,128)S(1)}, s32[1,4,3]{2,1,0:T(4,128)S(1)}, u32[]{:S(2)}, u32[]{:S(2)}) collective-permute-start(s32[1,4,3]{2,1,0:T(4,128)S(1)} %copy.13.partners), channel_id=1, source_target_pairs={{0,4},{2,6},{4,0},{6,2},{1,5},{3,7},{5,1},{7,3},{8,12},{10,14},{12... | collective-permute-start | bytes 152 | tf_op jit(solution)/shard_map/ppermute | solution.py:416
  7.0 0.0 collective-permute-start
  7.0 0.0 collective-permute-start.6
  7.0 0.5 collective-permute-start.7
  7.5 1.2 %alive.1 = s32[16]{0:T(128)S(1)} custom-call(s32[1,4,3]{2,1,0:T(4,128)S(1)} %copy.13.partners), custom_call_target="tpu_custom_call" | custom-call | flops 40000000000 | bytes 1 | tf_op jit(solution)/shard_map/alive/pallas_call | solution.py:406
  8.8 0.1 stack.23.scalars
  8.9 0.0 copy-start.5
  8.9 0.0 copy-start.6
  8.9 0.0 copy-start.7
  8.9 0.0 collective-permute-done.1.refs_1_
  8.9 3.5 %collective-permute-done.refs_0_ = s32[1,4,3]{2,1,0:T(4,128)S(1)} collective-permute-done((s32[1,4,3]{2,1,0:T(4,128)S(1)}, s32[1,4,3]{2,1,0:T(4,128)S(1)}, u32[]{:S(2)}, u32[]{:S(2)}) %collective-permute-start) | collective-permute-done | bytes 80 | tf_op jit(solution)/shard_map/ppermute | solution.py:416
  12.4 0.8 pick.1
  13.2 0.4 collective-permute-start.3
  13.6 4.0 %collective-permute-start.5 = (bf16[32,1536]{1,0:T(8,128)(2,1)S(1)}, bf16[32,1536]{1,0:T(8,128)(2,1)S(1)}, u32[]{:S(2)}, u32[]{:S(2)}) collective-permute-start(bf16[32,1536]{1,0:T(8,128)(2,1)S(1)} %get-tuple-element.68), channel_id=1, source_target_pairs={{0,2},{2,0},{4,6},{6,4},{1,3},{3,1},{5,7},{7,5},{8,10},{10,8},{12,... | collective-permute-start | bytes 294920 | tf_op jit(solution)/shard_map/ppermute | solution.py:433
  17.7 4.1 %project.1 = (bf16[1536,256]{1,0:T(8,128)(2,1)S(1)}, bf16[256,384]{1,0:T(8,128)(2,1)S(1)}, bf16[256,384]{1,0:T(8,128)(2,1)S(1)}, bf16[256,1536]{1,0:T(8,128)(2,1...) custom-call(s32[5]{0:T(128)S(1)} %stack.23.scalars, ...), custom_call_target="tpu_custom_call" | custom-call | flops 1 | bytes 1 | tf_op jit(solution)/shard_map/project/pallas_call | solution.py:435
  21.9 0.4 collective-permute-done.4.refs_1_
  22.3 0.1 collective-permute-start.8
  22.4 0.4 collective-permute-start.9
  22.8 0.1 collective-permute-start.10
  22.9 0.7 collective-permute-done.8.refs_3_
  23.6 0.2 collective-permute-done.9.refs_4_
  23.7 0.4 collective-permute-done.10.refs_5_
  24.1 3.2 %attention_forward.1 = (bf16[1536,192]{1,0:T(8,128)(2,1)S(1)}, bf16[192,384]{1,0:T(8,128)(2,1)S(1)}, bf16[192,384]{1,0:T(8,128)(2,1)S(1)}, f32[3,64,512]{2,1,0:T...) custom-call(s32[5]{0:T(128)S(1)} %stack.23.scalars, ...), custom_call_target="tpu_custom_call" | custom-call | flops 1 | bytes 1 | tf_op jit(solution)/shard_map/attention_forward/pallas_call | solution.py:471
  27.3 0.2 collective-permute-start.11
  27.5 1.6 %attention_backward.1 = (bf16[256,384]{1,0:T(8,128)(2,1)S(1)}, bf16[448,384]{1,0:T(8,128)(2,1)S(1)}) custom-call(bf16[3,512,128]{2,1,0:T(8,128)(2,1)S(1)} %get-tuple-element.75.refs_6_.query_stack, bf16[3,512,128]{2,1,0:T(8,128)(2,1)S(1)} %get-tuple-element.76.refs_7_.grad_stack, f32[3,64,512]{2,1,0:T(8,128)S(1)} %get-tuple-element.80.dprob_own, ...), custom_call_target="tpu_custom_call" | custom-call | flops 1 | bytes 1 | tf_op jit(solution)/shard_map/attention_backward/pallas_call | solution.py:459
  29.1 1.8 %grad_value_out.1 = (bf16[2,2,2,48,1536]{4,3,2,1,0:T(8,128)(2,1)S(1)}, f32[2,2,2,48,1536]{4,3,2,1,0:T(8,128)S(1)}) custom-call(s32[5]{0:T(128)S(1)} %stack.23.scalars, bf16[1536,256]{1,0:T(8,128)(2,1)S(1)} %get-tuple-element.70.normed_t, bf16[1536,192]{1,0:T(8,128)(2,1)S(1)} %get-tuple-element.79.normed_far_t, ...), custom_call_target="tpu_custom_call" | custom-call | flops 1 | bytes 1 | tf_op jit(solution)/shard_map/grad_value_out/pallas_call | solution.py:459
  30.9 0.4 collective-permute-start.18
  31.3 1.9 %grad_query_key.1 = (bf16[384,384]{1,0:T(8,128)(2,1)S(1)}, bf16[384,384]{1,0:T(8,128)(2,1)S(1)}, bf16[384,384]{1,0:T(8,128)(2,1)S(1)}, bf16[384,384]{1,0:T(8,128...) custom-call(s32[5]{0:T(128)S(1)} %stack.23.scalars, ...), custom_call_target="tpu_custom_call" | custom-call | flops 1 | bytes 1 | tf_op jit(solution)/shard_map/grad_query_key/pallas_call | solution.py:459
  33.2 1.6 %collective-permute-start.13 = (bf16[384,384]{1,0:T(8,128)(2,1)S(1)}, bf16[384,384]{1,0:T(8,128)(2,1)S(1)}, u32[]{:S(2)}, u32[]{:S(2)}) collective-permute-start(bf16[384,384]{1,0:T(8,128)(2,1)S(1)} %get-tuple-element.96), channel_id=1, source_target_pairs={{0,8},{8,0},{16,24},{24,16},{1,9},{9,1},{17,25},{25,17},{2,10},{10... | collective-permute-start | bytes 884744 | tf_op jit(solution)/shard_map/ppermute | solution.py:509
  34.8 1.5 %collective-permute-start.14 = (bf16[384,384]{1,0:T(8,128)(2,1)S(1)}, bf16[384,384]{1,0:T(8,128)(2,1)S(1)}, u32[]{:S(2)}, u32[]{:S(2)}) collective-permute-start(bf16[384,384]{1,0:T(8,128)(2,1)S(1)} %get-tuple-element.98), channel_id=1, source_target_pairs={{0,16},{8,24},{16,0},{24,8},{1,17},{9,25},{17,1},{25,9},{2,18},{10... | collective-permute-start | bytes 884744 | tf_op jit(solution)/shard_map/ppermute | solution.py:509
  36.3 0.5 collective-permute-start.12
  36.8 0.5 collective-permute-start.16
  37.4 5.8 %collective-permute-done.13.q_got = bf16[384,384]{1,0:T(8,128)(2,1)S(1)} collective-permute-done((bf16[384,384]{1,0:T(8,128)(2,1)S(1)}, bf16[384,384]{1,0:T(8,128)(2,1)S(1)}, u32[]{:S(2)}, u32[]{:S(2)}) %collective-permute-start.13) | collective-permute-done | bytes 294944 | tf_op jit(solution)/shard_map/ppermute | solution.py:509
  43.2 1.5 %collective-permute-done.14.k_got = bf16[384,384]{1,0:T(8,128)(2,1)S(1)} collective-permute-done((bf16[384,384]{1,0:T(8,128)(2,1)S(1)}, bf16[384,384]{1,0:T(8,128)(2,1)S(1)}, u32[]{:S(2)}, u32[]{:S(2)}) %collective-permute-start.14) | collective-permute-done | bytes 294944 | tf_op jit(solution)/shard_map/ppermute | solution.py:509
  44.7 0.1 first_sum_query_key.1
  44.8 1.6 %collective-permute-start.15 = (bf16[384,384]{1,0:T(8,128)(2,1)S(1)}, bf16[384,384]{1,0:T(8,128)(2,1)S(1)}, u32[]{:S(2)}, u32[]{:S(2)}) collective-permute-start(bf16[384,384]{1,0:T(8,128)(2,1)S(1)} %get-tuple-element.99), channel_id=1, source_target_pairs={{0,16},{8,24},{16,0},{24,8},{1,17},{9,25},{17,1},{25,9},{2,18},{10... | collective-permute-start | bytes 884744 | tf_op jit(solution)/shard_map/ppermute | solution.py:517
  46.4 0.5 collective-permute-start.17
  46.9 2.6 %collective-permute-done.12.q_first = bf16[384,384]{1,0:T(8,128)(2,1)S(1)} collective-permute-done((bf16[384,384]{1,0:T(8,128)(2,1)S(1)}, bf16[384,384]{1,0:T(8,128)(2,1)S(1)}, u32[]{:S(2)}, u32[]{:S(2)}) %collective-permute-start.12) | collective-permute-done | bytes 294944 | tf_op jit(solution)/shard_map/ppermute | solution.py:509
  49.5 1.5 %collective-permute-done.16.k_first = bf16[384,384]{1,0:T(8,128)(2,1)S(1)} collective-permute-done((bf16[384,384]{1,0:T(8,128)(2,1)S(1)}, bf16[384,384]{1,0:T(8,128)(2,1)S(1)}, u32[]{:S(2)}, u32[]{:S(2)}) %collective-permute-start.16) | collective-permute-done | bytes 294944 | tf_op jit(solution)/shard_map/ppermute | solution.py:509
  51.0 5.1 %collective-permute-done.15.q_second = bf16[384,384]{1,0:T(8,128)(2,1)S(1)} collective-permute-done((bf16[384,384]{1,0:T(8,128)(2,1)S(1)}, bf16[384,384]{1,0:T(8,128)(2,1)S(1)}, u32[]{:S(2)}, u32[]{:S(2)}) %collective-permute-start.15) | collective-permute-done | bytes 294944 | tf_op jit(solution)/shard_map/ppermute | solution.py:517
  56.1 1.0 %second_sum_query_key.1 = bf16[384,768]{1,0:T(8,128)(2,1)} custom-call(f32[2,384,384]{2,1,0:T(8,128)S(1)} %get-tuple-element.94.q_keep, bf16[384,384]{1,0:T(8,128)(2,1)S(1)} %collective-permute-done.12.q_first, bf16[384,384]{1,0:T(8,128)(2,1)S(1)} %collective-permute-done.15.q_second, f32[2,384,384]{2,1,0:T(8,128)S(1)} %get-tuple-element.97.k_keep, ...), custom_call_target="tpu_custom_call" | custom-call | flops 1 | bytes 1 | tf_op jit(solution)/shard_map/second_sum_query_key/pallas_call | solution.py:459
  57.1 2.1 %collective-permute-done.18.got = bf16[2,2,2,48,1536]{4,3,2,1,0:T(8,128)(2,1)S(1)} collective-permute-done((bf16[2,2,2,48,1536]{4,3,2,1,0:T(8,128)(2,1)S(1)}, bf16[2,2,2,48,1536]{4,3,2,1,0:T(8,128)(2,1)S(1)}, u32[]{:S(2)}, u32[]{:S(2)}) %collective-permute-start.18) | collective-permute-done | bytes 1179680 | tf_op jit(solution)/shard_map/ppermute | solution.py:532
  59.2 0.2 view_sum_value_out.1
  59.4 1.6 %collective-permute-start.20 = (bf16[2,2,48,768]{3,2,1,0:T(8,128)(2,1)S(1)}, bf16[2,2,48,768]{3,2,1,0:T(8,128)(2,1)S(1)}, u32[]{:S(2)}, u32[]{:S(2)}) collective-permute-start(bf16[2,2,48,768]{3,2,1,0:T(8,128)(2,1)S(1)} %get-tuple-element.110), channel_id=1, source_target_pairs={{0,16},{8,24},{16,0},{24,8},{1,17},{9,25},{17,1},{25,9},{2,18},{10... | collective-permute-start | bytes 884744 | tf_op jit(solution)/shard_map/ppermute | solution.py:509
  61.0 1.5 %collective-permute-start.19 = (bf16[2,2,48,768]{3,2,1,0:T(8,128)(2,1)S(1)}, bf16[2,2,48,768]{3,2,1,0:T(8,128)(2,1)S(1)}, u32[]{:S(2)}, u32[]{:S(2)}) collective-permute-start(bf16[2,2,48,768]{3,2,1,0:T(8,128)(2,1)S(1)} %get-tuple-element.104), channel_id=1, source_target_pairs={{0,8},{8,0},{16,24},{24,16},{1,9},{9,1},{17,25},{25,17},{2,10},{10... | collective-permute-start | bytes 884744 | tf_op jit(solution)/shard_map/ppermute | solution.py:509
  62.5 3.5 %all-to-all-start = ((bf16[8,48,768]{2,1,0:T(8,128)(2,1)}), bf16[8,48,768]{2,1,0:T(8,128)(2,1)S(1)}, u32[]{:S(2)}, u32[]{:S(2)}) async-start(bf16[8,48,768]{2,1,0:T(8,128)(2,1)} %bitcast.7), calls=%async_computation | async-start | bytes 1179648 | tf_op jit(solution)/shard_map/all_to_all | solution.py:520
  66.0 1.9 %collective-permute-done.20.y_got = bf16[2,2,48,768]{3,2,1,0:T(8,128)(2,1)S(1)} collective-permute-done((bf16[2,2,48,768]{3,2,1,0:T(8,128)(2,1)S(1)}, bf16[2,2,48,768]{3,2,1,0:T(8,128)(2,1)S(1)}, u32[]{:S(2)}, u32[]{:S(2)}) %collective-permute-start.20) | collective-permute-done | bytes 294944 | tf_op jit(solution)/shard_map/ppermute | solution.py:509
  67.9 1.2 %collective-permute-done.19.x_got = bf16[2,2,48,768]{3,2,1,0:T(8,128)(2,1)S(1)} collective-permute-done((bf16[2,2,48,768]{3,2,1,0:T(8,128)(2,1)S(1)}, bf16[2,2,48,768]{3,2,1,0:T(8,128)(2,1)S(1)}, u32[]{:S(2)}, u32[]{:S(2)}) %collective-permute-start.19) | collective-permute-done | bytes 294944 | tf_op jit(solution)/shard_map/ppermute | solution.py:509
  69.2 0.1 first_sum_value_out.1
  69.3 1.6 %collective-permute-start.21 = (bf16[2,48,768]{2,1,0:T(8,128)(2,1)S(1)}, bf16[2,48,768]{2,1,0:T(8,128)(2,1)S(1)}, u32[]{:S(2)}, u32[]{:S(2)}) collective-permute-start(bf16[2,48,768]{2,1,0:T(8,128)(2,1)S(1)} %get-tuple-element.112), channel_id=1, source_target_pairs={{0,8},{8,0},{16,24},{24,16},{1,9},{9,1},{17,25},{25,17},{2,10},{10... | collective-permute-start | bytes 442376 | tf_op jit(solution)/shard_map/ppermute | solution.py:517
  70.9 0.5 collective-permute-start.22
  71.3 3.2 %collective-permute-done.21.refs_1_ = bf16[2,48,768]{2,1,0:T(8,128)(2,1)S(1)} collective-permute-done((bf16[2,48,768]{2,1,0:T(8,128)(2,1)S(1)}, bf16[2,48,768]{2,1,0:T(8,128)(2,1)S(1)}, u32[]{:S(2)}, u32[]{:S(2)}) %collective-permute-start.21) | collective-permute-done | bytes 147488 | tf_op jit(solution)/shard_map/ppermute | solution.py:517
  74.5 1.5 %collective-permute-done.22.refs_3_ = bf16[2,48,768]{2,1,0:T(8,128)(2,1)S(1)} collective-permute-done((bf16[2,48,768]{2,1,0:T(8,128)(2,1)S(1)}, bf16[2,48,768]{2,1,0:T(8,128)(2,1)S(1)}, u32[]{:S(2)}, u32[]{:S(2)}) %collective-permute-start.22) | collective-permute-done | bytes 147488 | tf_op jit(solution)/shard_map/ppermute | solution.py:517
  76.0 0.6 last_parts_value_out.1
  76.6 0.1 collective-permute-start.24
  76.7 1.2 %collective-permute-start.23 = (bf16[24,1536]{1,0:T(8,128)(2,1)S(1)}, bf16[24,1536]{1,0:T(8,128)(2,1)S(1)}, u32[]{:S(2)}, u32[]{:S(2)}) collective-permute-start(bf16[24,1536]{1,0:T(8,128)(2,1)S(1)} %get-tuple-element.117), channel_id=1, source_target_pairs={{0,4},{2,6},{4,0},{6,2},{1,5},{3,7},{5,1},{7,3},{8,12},{10,14},{12... | collective-permute-start | bytes 221192 | tf_op jit(solution)/shard_map/ppermute | solution.py:588
  77.9 1.6 %collective-permute-start.25 = (bf16[24,1536]{1,0:T(8,128)(2,1)S(1)}, bf16[24,1536]{1,0:T(8,128)(2,1)S(1)}, u32[]{:S(2)}, u32[]{:S(2)}) collective-permute-start(bf16[24,1536]{1,0:T(8,128)(2,1)S(1)} %get-tuple-element.119), channel_id=1, source_target_pairs={{0,5},{1,4},{2,7},{3,6},{4,1},{5,0},{6,3},{7,2},{8,13},{9,12},{10,... | collective-permute-start | bytes 221192 | tf_op jit(solution)/shard_map/ppermute | solution.py:589
  79.5 6.9 %all-to-all-done.packed = bf16[8,48,768]{2,1,0:T(8,128)(2,1)S(1)} async-done(((bf16[8,48,768]{2,1,0:T(8,128)(2,1)}), bf16[8,48,768]{2,1,0:T(8,128)(2,1)S(1)}, u32[]{:S(2)}, u32[]{:S(2)}) %all-to-all-start) | async-done | bytes 589856 | tf_op jit(solution)/shard_map/all_to_all | solution.py:520
  86.4 0.8 last_sum_query_key.1
  87.1 0.8 collective-permute-done.23.far_same
  87.9 0.6 collective-permute-done.25.far_cross
  88.6 1.3 %last_sum_value_out.1 = (f32[48,768]{1,0:T(8,128)}, f32[24,1536]{1,0:T(8,128)}) custom-call(s32[5]{0:T(128)S(1)} %stack.23.scalars, f32[24,1536]{1,0:T(8,128)S(1)} %get-tuple-element.116.mine, bf16[24,1536]{1,0:T(8,128)(2,1)S(1)} %collective-permute-done.23.far_same, f32[24,1536]{1,0:T(8,128)S(1)} %collective-permute-done.24.near_cross, ...), custom_call_target="tpu_custom_call" | custom-call | flops 1 | bytes 1 | tf_op jit(solution)/shard_map/last_sum_value_out/pallas_call | solution.py:459
  (22 shorter events, 0.0 us)
Async XLA Ops:
  1.4 7.5 %collective-permute-start.2 = (s32[1,4,3]{2,1,0:T(4,128)S(1)}, s32[1,4,3]{2,1,0:T(4,128)S(1)}, u32[]{:S(2)}, u32[]{:S(2)}) collective-permute-start(s32[1,4,3]{2,1,0:T(4,128)S(1)} %copy.13.partners), channel_id=1, source_target_pairs={{0,2},{2,0},{4,6},{6,4},{1,3},{3,1},{5,7},{7,5},{8,10},{10,8},{12,... | collective-permute-start | bytes 152 | tf_op jit(solution)/shard_map/ppermute | solution.py:416
  4.4 4.5 %collective-permute-start.1 = (s32[1,4,3]{2,1,0:T(4,128)S(1)}, s32[1,4,3]{2,1,0:T(4,128)S(1)}, u32[]{:S(2)}, u32[]{:S(2)}) collective-permute-start(s32[1,4,3]{2,1,0:T(4,128)S(1)} %copy.13.partners), channel_id=1, source_target_pairs={{0,4},{2,6},{4,0},{6,2},{1,5},{3,7},{5,1},{7,3},{8,12},{10,14},{12... | collective-permute-start | bytes 152 | tf_op jit(solution)/shard_map/ppermute | solution.py:416
  7.0 5.4 %collective-permute-start = (s32[1,4,3]{2,1,0:T(4,128)S(1)}, s32[1,4,3]{2,1,0:T(4,128)S(1)}, u32[]{:S(2)}, u32[]{:S(2)}) collective-permute-start(s32[1,4,3]{2,1,0:T(4,128)S(1)} %copy.13.partners), channel_id=1, source_target_pairs={{0,6},{2,4},{4,2},{6,0},{1,7},{3,5},{5,3},{7,1},{8,14},{10,12},{12... | collective-permute-start | bytes 152 | tf_op jit(solution)/shard_map/ppermute | solution.py:416
  7.0 10.6 %collective-permute-start.6 = (bf16[4,32,1536]{2,1,0:T(8,128)(2,1)}, bf16[4,32,1536]{2,1,0:T(8,128)(2,1)S(1)}, u32[]{:S(2)}, u32[]{:S(2)}) collective-permute-start(bf16[4,32,1536]{2,1,0:T(8,128)(2,1)} %bitcast.8), channel_id=1, source_target_pairs={{0,1},{1,0},{2,3},{3,2},{4,5},{5,4},{6,7},{7,6},{8,9},{9,8},{10,11... | collective-permute-start | bytes 1179656 | tf_op jit(solution)/shard_map/ppermute | solution.py:421
  7.0 10.6 %collective-permute-start.7 = (bf16[4,32,1536]{2,1,0:T(8,128)(2,1)}, bf16[4,32,1536]{2,1,0:T(8,128)(2,1)S(1)}, u32[]{:S(2)}, u32[]{:S(2)}) collective-permute-start(bf16[4,32,1536]{2,1,0:T(8,128)(2,1)} %bitcast.11), channel_id=1, source_target_pairs={{0,1},{1,0},{2,3},{3,2},{4,5},{5,4},{6,7},{7,6},{8,9},{9,8},{10,11... | collective-permute-start | bytes 1179656 | tf_op jit(solution)/shard_map/ppermute | solution.py:422
  7.5 4.9 %copy-start.4 = (bf16[1,4,1,32,1536]{4,3,2,1,0:T(8,128)(2,1)S(1)}, bf16[1,4,1,32,1536]{4,3,2,1,0:T(8,128)(2,1)}, u32[]{:S(2)}) copy-start(bf16[1,4,1,32,1536]{4,3,2,1,0:T(8,128)(2,1)} %param.10) | copy-start | bytes 1179652
  8.8 8.8 %copy-start = (bf16[1536,768]{1,0:T(8,128)(2,1)S(1)}, bf16[1536,768]{1,0:T(8,128)(2,1)}, u32[]{:S(2)}) copy-start(bf16[1536,768]{1,0:T(8,128)(2,1)} %refs_11_.1) | copy-start | bytes 7077892
  8.9 8.8 %copy-start.1 = (bf16[1536,768]{1,0:T(8,128)(2,1)S(1)}, bf16[1536,768]{1,0:T(8,128)(2,1)}, u32[]{:S(2)}) copy-start(bf16[1536,768]{1,0:T(8,128)(2,1)} %refs_12_.1) | copy-start | bytes 7077892
  8.9 8.8 %copy-start.2 = (bf16[1536,768]{1,0:T(8,128)(2,1)S(1)}, bf16[1536,768]{1,0:T(8,128)(2,1)}, u32[]{:S(2)}) copy-start(bf16[1536,768]{1,0:T(8,128)(2,1)} %w_query.1) | copy-start | bytes 7077892
  8.9 8.8 %copy-start.3 = (bf16[768,1536]{1,0:T(8,128)(2,1)S(1)}, bf16[768,1536]{1,0:T(8,128)(2,1)}, u32[]{:S(2)}) copy-start(bf16[768,1536]{1,0:T(8,128)(2,1)} %w_out.1) | copy-start | bytes 7077892
  8.9 8.8 %copy-start.5 = (bf16[1,4,1,32,1536]{4,3,2,1,0:T(8,128)(2,1)S(1)}, bf16[1,4,1,32,1536]{4,3,2,1,0:T(8,128)(2,1)}, u32[]{:S(2)}) copy-start(bf16[1,4,1,32,1536]{4,3,2,1,0:T(8,128)(2,1)} %param.18) | copy-start | bytes 1179652
  8.9 8.8 %copy-start.6 = (bf16[9,1536]{1,0:T(8,128)(2,1)S(1)}, bf16[9,1536]{1,0:T(8,128)(2,1)}, u32[]{:S(2)}) copy-start(bf16[9,1536]{1,0:T(8,128)(2,1)} %taps.1) | copy-start | bytes 82948
  8.9 8.8 %copy-start.7 = (f32[1536]{0:T(1024)S(1)}, f32[1536]{0:T(1024)}, u32[]{:S(2)}) copy-start(f32[1536]{0:T(1024)} %refs_10_.1) | copy-start | bytes 18436
  13.2 8.7 %collective-permute-start.3 = (bf16[32,1536]{1,0:T(8,128)(2,1)S(1)}, bf16[32,1536]{1,0:T(8,128)(2,1)S(1)}, u32[]{:S(2)}, u32[]{:S(2)}) collective-permute-start(bf16[32,1536]{1,0:T(8,128)(2,1)S(1)} %get-tuple-element.66), channel_id=1, source_target_pairs={{0,6},{2,4},{4,2},{6,0},{1,7},{3,5},{5,3},{7,1},{8,14},{10,12},{12... | collective-permute-start | bytes 294920 | tf_op jit(solution)/shard_map/ppermute | solution.py:433
  13.6 8.7 %collective-permute-start.4 = (bf16[32,1536]{1,0:T(8,128)(2,1)S(1)}, bf16[32,1536]{1,0:T(8,128)(2,1)S(1)}, u32[]{:S(2)}, u32[]{:S(2)}) collective-permute-start(bf16[32,1536]{1,0:T(8,128)(2,1)S(1)} %get-tuple-element.67), channel_id=1, source_target_pairs={{0,4},{2,6},{4,0},{6,2},{1,5},{3,7},{5,1},{7,3},{8,12},{10,14},{12... | collective-permute-start | bytes 294920 | tf_op jit(solution)/shard_map/ppermute | solution.py:433
  13.6 8.7 %collective-permute-start.5 = (bf16[32,1536]{1,0:T(8,128)(2,1)S(1)}, bf16[32,1536]{1,0:T(8,128)(2,1)S(1)}, u32[]{:S(2)}, u32[]{:S(2)}) collective-permute-start(bf16[32,1536]{1,0:T(8,128)(2,1)S(1)} %get-tuple-element.68), channel_id=1, source_target_pairs={{0,2},{2,0},{4,6},{6,4},{1,3},{3,1},{5,7},{7,5},{8,10},{10,8},{12,... | collective-permute-start | bytes 294920 | tf_op jit(solution)/shard_map/ppermute | solution.py:433
  22.3 1.3 %collective-permute-start.8 = (bf16[32,1536]{1,0:T(8,128)(2,1)S(1)}, bf16[32,1536]{1,0:T(8,128)(2,1)S(1)}, u32[]{:S(2)}, u32[]{:S(2)}) collective-permute-start(bf16[32,1536]{1,0:T(8,128)(2,1)S(1)} %collective-permute-done.3.refs_0_), channel_id=1, source_target_pairs={{0,1},{1,0},{2,3},{3,2},{4,5},{5,4},{6,7},{7,6},{8,9},{9,8},{10,11... | collective-permute-start | bytes 294920 | tf_op jit(solution)/shard_map/ppermute | solution.py:456
  22.4 1.4 %collective-permute-start.9 = (bf16[32,1536]{1,0:T(8,128)(2,1)S(1)}, bf16[32,1536]{1,0:T(8,128)(2,1)S(1)}, u32[]{:S(2)}, u32[]{:S(2)}) collective-permute-start(bf16[32,1536]{1,0:T(8,128)(2,1)S(1)} %collective-permute-done.4.refs_1_), channel_id=1, source_target_pairs={{0,1},{1,0},{2,3},{3,2},{4,5},{5,4},{6,7},{7,6},{8,9},{9,8},{10,11... | collective-permute-start | bytes 294920 | tf_op jit(solution)/shard_map/ppermute | solution.py:456
  22.8 1.3 %collective-permute-start.10 = (bf16[32,1536]{1,0:T(8,128)(2,1)S(1)}, bf16[32,1536]{1,0:T(8,128)(2,1)S(1)}, u32[]{:S(2)}, u32[]{:S(2)}) collective-permute-start(bf16[32,1536]{1,0:T(8,128)(2,1)S(1)} %collective-permute-done.5.refs_2_), channel_id=1, source_target_pairs={{0,1},{1,0},{2,3},{3,2},{4,5},{5,4},{6,7},{7,6},{8,9},{9,8},{10,11... | collective-permute-start | bytes 294920 | tf_op jit(solution)/shard_map/ppermute | solution.py:456
  27.3 1.8 %collective-permute-start.11 = (bf16[384,256]{1,0:T(8,128)(2,1)S(1)}, bf16[384,256]{1,0:T(8,128)(2,1)S(1)}, u32[]{:S(2)}, u32[]{:S(2)}) collective-permute-start(bf16[384,256]{1,0:T(8,128)(2,1)S(1)} %get-tuple-element.90.mine), channel_id=1, source_target_pairs={{0,1},{1,0},{2,3},{3,2},{4,5},{5,4},{6,7},{7,6},{8,9},{9,8},{10,11... | collective-permute-start | bytes 589832 | tf_op jit(solution)/shard_map/ppermute | solution.py:491
  30.9 28.3 %collective-permute-start.18 = (bf16[2,2,2,48,1536]{4,3,2,1,0:T(8,128)(2,1)S(1)}, bf16[2,2,2,48,1536]{4,3,2,1,0:T(8,128)(2,1)S(1)}, u32[]{:S(2)}, u32[]{:S(2)}) collective-permute-start(bf16[2,2,2,48,1536]{4,3,2,1,0:T(8,128)(2,1)S(1)} %get-tuple-element.92), channel_id=1, source_target_pairs={{0,2},{2,0},{4,6},{6,4},{1,3},{3,1},{5,7},{7,5},{8,10},{10,8},{12,... | collective-permute-start | bytes 3538952 | tf_op jit(solution)/shard_map/ppermute | solution.py:532
  33.2 9.9 %collective-permute-start.13 = (bf16[384,384]{1,0:T(8,128)(2,1)S(1)}, bf16[384,384]{1,0:T(8,128)(2,1)S(1)}, u32[]{:S(2)}, u32[]{:S(2)}) collective-permute-start(bf16[384,384]{1,0:T(8,128)(2,1)S(1)} %get-tuple-element.96), channel_id=1, source_target_pairs={{0,8},{8,0},{16,24},{24,16},{1,9},{9,1},{17,25},{25,17},{2,10},{10... | collective-permute-start | bytes 884744 | tf_op jit(solution)/shard_map/ppermute | solution.py:509
  34.8 9.9 %collective-permute-start.14 = (bf16[384,384]{1,0:T(8,128)(2,1)S(1)}, bf16[384,384]{1,0:T(8,128)(2,1)S(1)}, u32[]{:S(2)}, u32[]{:S(2)}) collective-permute-start(bf16[384,384]{1,0:T(8,128)(2,1)S(1)} %get-tuple-element.98), channel_id=1, source_target_pairs={{0,16},{8,24},{16,0},{24,8},{1,17},{9,25},{17,1},{25,9},{2,18},{10... | collective-permute-start | bytes 884744 | tf_op jit(solution)/shard_map/ppermute | solution.py:509
  36.3 13.2 %collective-permute-start.12 = (bf16[384,384]{1,0:T(8,128)(2,1)S(1)}, bf16[384,384]{1,0:T(8,128)(2,1)S(1)}, u32[]{:S(2)}, u32[]{:S(2)}) collective-permute-start(bf16[384,384]{1,0:T(8,128)(2,1)S(1)} %get-tuple-element.95), channel_id=1, source_target_pairs={{0,8},{8,0},{16,24},{24,16},{1,9},{9,1},{17,25},{25,17},{2,10},{10... | collective-permute-start | bytes 884744 | tf_op jit(solution)/shard_map/ppermute | solution.py:509
  36.8 14.2 %collective-permute-start.16 = (bf16[384,384]{1,0:T(8,128)(2,1)S(1)}, bf16[384,384]{1,0:T(8,128)(2,1)S(1)}, u32[]{:S(2)}, u32[]{:S(2)}) collective-permute-start(bf16[384,384]{1,0:T(8,128)(2,1)S(1)} %get-tuple-element.100), channel_id=1, source_target_pairs={{0,16},{8,24},{16,0},{24,8},{1,17},{9,25},{17,1},{25,9},{2,18},{10... | collective-permute-start | bytes 884744 | tf_op jit(solution)/shard_map/ppermute | solution.py:509
  44.8 11.3 %collective-permute-start.15 = (bf16[384,384]{1,0:T(8,128)(2,1)S(1)}, bf16[384,384]{1,0:T(8,128)(2,1)S(1)}, u32[]{:S(2)}, u32[]{:S(2)}) collective-permute-start(bf16[384,384]{1,0:T(8,128)(2,1)S(1)} %get-tuple-element.99), channel_id=1, source_target_pairs={{0,16},{8,24},{16,0},{24,8},{1,17},{9,25},{17,1},{25,9},{2,18},{10... | collective-permute-start | bytes 884744 | tf_op jit(solution)/shard_map/ppermute | solution.py:517
  46.4 9.8 %collective-permute-start.17 = (bf16[384,384]{1,0:T(8,128)(2,1)S(1)}, bf16[384,384]{1,0:T(8,128)(2,1)S(1)}, u32[]{:S(2)}, u32[]{:S(2)}) collective-permute-start(bf16[384,384]{1,0:T(8,128)(2,1)S(1)} %get-tuple-element.101), channel_id=1, source_target_pairs={{0,8},{8,0},{16,24},{24,16},{1,9},{9,1},{17,25},{25,17},{2,10},{10... | collective-permute-start | bytes 884744 | tf_op jit(solution)/shard_map/ppermute | solution.py:517
  59.4 8.5 %collective-permute-start.20 = (bf16[2,2,48,768]{3,2,1,0:T(8,128)(2,1)S(1)}, bf16[2,2,48,768]{3,2,1,0:T(8,128)(2,1)S(1)}, u32[]{:S(2)}, u32[]{:S(2)}) collective-permute-start(bf16[2,2,48,768]{3,2,1,0:T(8,128)(2,1)S(1)} %get-tuple-element.110), channel_id=1, source_target_pairs={{0,16},{8,24},{16,0},{24,8},{1,17},{9,25},{17,1},{25,9},{2,18},{10... | collective-permute-start | bytes 884744 | tf_op jit(solution)/shard_map/ppermute | solution.py:509
  61.0 8.2 %collective-permute-start.19 = (bf16[2,2,48,768]{3,2,1,0:T(8,128)(2,1)S(1)}, bf16[2,2,48,768]{3,2,1,0:T(8,128)(2,1)S(1)}, u32[]{:S(2)}, u32[]{:S(2)}) collective-permute-start(bf16[2,2,48,768]{3,2,1,0:T(8,128)(2,1)S(1)} %get-tuple-element.104), channel_id=1, source_target_pairs={{0,8},{8,0},{16,24},{24,16},{1,9},{9,1},{17,25},{25,17},{2,10},{10... | collective-permute-start | bytes 884744 | tf_op jit(solution)/shard_map/ppermute | solution.py:509
  62.5 23.9 %all-to-all-start = ((bf16[8,48,768]{2,1,0:T(8,128)(2,1)}), bf16[8,48,768]{2,1,0:T(8,128)(2,1)S(1)}, u32[]{:S(2)}, u32[]{:S(2)}) async-start(bf16[8,48,768]{2,1,0:T(8,128)(2,1)} %bitcast.7), calls=%async_computation | async-start | bytes 1179648 | tf_op jit(solution)/shard_map/all_to_all | solution.py:520
  69.3 5.2 %collective-permute-start.21 = (bf16[2,48,768]{2,1,0:T(8,128)(2,1)S(1)}, bf16[2,48,768]{2,1,0:T(8,128)(2,1)S(1)}, u32[]{:S(2)}, u32[]{:S(2)}) collective-permute-start(bf16[2,48,768]{2,1,0:T(8,128)(2,1)S(1)} %get-tuple-element.112), channel_id=1, source_target_pairs={{0,8},{8,0},{16,24},{24,16},{1,9},{9,1},{17,25},{25,17},{2,10},{10... | collective-permute-start | bytes 442376 | tf_op jit(solution)/shard_map/ppermute | solution.py:517
  70.9 5.1 %collective-permute-start.22 = (bf16[2,48,768]{2,1,0:T(8,128)(2,1)S(1)}, bf16[2,48,768]{2,1,0:T(8,128)(2,1)S(1)}, u32[]{:S(2)}, u32[]{:S(2)}) collective-permute-start(bf16[2,48,768]{2,1,0:T(8,128)(2,1)S(1)} %get-tuple-element.114), channel_id=1, source_target_pairs={{0,16},{8,24},{16,0},{24,8},{1,17},{9,25},{17,1},{25,9},{2,18},{10... | collective-permute-start | bytes 442376 | tf_op jit(solution)/shard_map/ppermute | solution.py:517
  76.6 11.9 %collective-permute-start.24 = (f32[24,1536]{1,0:T(8,128)S(1)}, f32[24,1536]{1,0:T(8,128)S(1)}, u32[]{:S(2)}, u32[]{:S(2)}) collective-permute-start(f32[24,1536]{1,0:T(8,128)S(1)} %get-tuple-element.118), channel_id=1, source_target_pairs={{0,1},{1,0},{2,3},{3,2},{4,5},{5,4},{6,7},{7,6},{8,9},{9,8},{10,11... | collective-permute-start | bytes 442376 | tf_op jit(solution)/shard_map/ppermute | solution.py:590
  76.7 11.2 %collective-permute-start.23 = (bf16[24,1536]{1,0:T(8,128)(2,1)S(1)}, bf16[24,1536]{1,0:T(8,128)(2,1)S(1)}, u32[]{:S(2)}, u32[]{:S(2)}) collective-permute-start(bf16[24,1536]{1,0:T(8,128)(2,1)S(1)} %get-tuple-element.117), channel_id=1, source_target_pairs={{0,4},{2,6},{4,0},{6,2},{1,5},{3,7},{5,1},{7,3},{8,12},{10,14},{12... | collective-permute-start | bytes 221192 | tf_op jit(solution)/shard_map/ppermute | solution.py:588
  77.9 10.7 %collective-permute-start.25 = (bf16[24,1536]{1,0:T(8,128)(2,1)S(1)}, bf16[24,1536]{1,0:T(8,128)(2,1)S(1)}, u32[]{:S(2)}, u32[]{:S(2)}) collective-permute-start(bf16[24,1536]{1,0:T(8,128)(2,1)S(1)} %get-tuple-element.119), channel_id=1, source_target_pairs={{0,5},{1,4},{2,7},{3,6},{4,1},{5,0},{6,3},{7,2},{8,13},{9,12},{10,... | collective-permute-start | bytes 221192 | tf_op jit(solution)/shard_map/ppermute | solution.py:589

commit v16 on v14

--- a/solution.py
+++ b/solution.py
@@ -11,6 +11,7 @@
 EPSILON = 1e-06
 SCALE = HEAD_DIM ** (-0.5)
 MASKED = -1e30
+PAIR = 2 * HEAD_DIM
 MIB = 1024 * 1024
 LITTLE = pl.CostEstimate(flops=1, bytes_accessed=1, transcendentals=0)
 MUCH = pl.CostEstimate(flops=40_000_000_000, bytes_accessed=1, transcendentals=0)
@@ -246,10 +247,11 @@
 
 
 def query_key_kernel(
-    scalars, normed_t, normed_far_t, dquery, dkey, q_later, k_later, q_now, k_now, q_keep, k_keep
+    scalars, normed_t, normed_far_t, dquery, dkey, dvalue, q_later, k_later, q_now, k_now, q_keep, k_keep
 ):
-    by_quarters(scalars, (normed_t,), dquery, (q_now, q_later), q_keep, True)
-    by_quarters(scalars, (normed_t, normed_far_t), dkey, (k_now, k_later), k_keep, False)
+    by_quarters(scalars, (normed_t,), dquery[...], (q_now, q_later), q_keep, True)
+    right = jnp.concatenate((dkey[...], dvalue[:, :PAIR]), axis=1)
+    by_quarters(scalars, (normed_t, normed_far_t), right, (k_now, k_later), k_keep, False)
 
 
 def go_on_kernel(q_keep, q_got, k_keep, k_got, q_later, k_later):
@@ -260,8 +262,10 @@
 def value_out_kernel(scalars, normed_t, normed_far_t, dvalue, mine, theirs, upstream, send, keep):
     row, x, y = scalars[0], scalars[3], scalars[4]
     odd = lax.rem(scalars[1], jnp.int32(2)) == 1
-    _, _, pairs, size, width = send.shape
-    half, quarter = width // 2, width // 4
+    _, _, pairs, size, _ = send.shape
+    half, quarter = upstream.shape[1] // 2, normed_t.shape[0] // 4
+    value_right = dvalue[:, PAIR:]
+    lanes = value_right.shape[1]
     places = [(dy, dx, pair) for dy in range(2) for dx in range(2) for pair in range(pairs)]
     rows = {"send": ([], [], []), "keep": ([], [], [])}
     for dy in range(2):
@@ -282,18 +286,18 @@
     right = upstream[:, core_half(scalars, half)]
     for target, name in ((send, "send"), (keep, "keep")):
         own, far, out = [jnp.concatenate(parts, axis=0) for parts in rows[name]]
-        grad_v = times((own, far), dvalue).astype(target.dtype)
+        grad_v = times((own, far), value_right).astype(target.dtype)
         grad_o = dot_nn(out, right).astype(target.dtype)
         for i, place in enumerate(places):
             target[(*place, slice(None), slice(0, half))] = grad_o[i * size : (i + 1) * size]
             for core in range(2):
-                columns = slice(half + core * quarter, half + (core + 1) * quarter)
+                columns = slice(half + core * lanes, half + (core + 1) * lanes)
                 part = grad_v[(2 * i + core) * size : (2 * i + core + 1) * size]
                 target[(*place, slice(None), columns)] = part
 
 
 def view_sum_kernel(keep, got, x_send, y_send, x_keep, y_keep):
-    half = keep.shape[4] // 2
+    half = y_send.shape[3]
     for second in range(2):
         for target, first in ((x_send, 1), (x_keep, 0)):
             total = keep[second, first, :, :, half:] + got[second, first, :, :, half:].astype(jnp.float32)
@@ -309,11 +313,19 @@
         now[...] = keep[0] + got[0].astype(jnp.float32)
 
 
-def pack_query_key_kernel(q_keep, q_first, q_second, k_keep, k_first, k_second, packed):
-    size = q_first.shape[1]
-    for i, (keep, first, second) in enumerate(((q_keep, q_first, q_second), (k_keep, k_first, k_second))):
-        total = keep[0] + first[...].astype(jnp.float32) + second[...].astype(jnp.float32)
-        packed[:, i * size : (i + 1) * size] = total.astype(jnp.bfloat16)
+def query_key_tiles_kernel(scalars, q_keep, q_first, q_second, k_keep, k_first, k_second, send, keep):
+    odd = lax.rem(scalars[1], jnp.int32(2)) == 1
+    total = [
+        kept[0] + first[...].astype(jnp.float32) + second[...].astype(jnp.float32)
+        for kept, first, second in ((q_keep, q_first, q_second), (k_keep, k_first, k_second))
+    ]
+    total = jnp.concatenate(total, axis=1)
+    pairs, size, _ = send.shape
+    for pair in range(pairs):
+        first = total[2 * pair * size : (2 * pair + 1) * size]
+        second = total[(2 * pair + 1) * size : (2 * pair + 2) * size]
+        send[pair] = jnp.where(odd, first, second).astype(send.dtype)
+        keep[pair] = jnp.where(odd, second, first)
 
 
 def summed_tile(addends, place):
@@ -335,47 +347,55 @@
             target[i] = summed_tile(addends, part * count + i).astype(target.dtype)
 
 
-def tile_cores_kernel(scalars, *refs):
+def query_key_cores(tile, half):
+    size = tile.shape[0] // 2
+    return tile[:size], tile[size:]
+
+
+def value_out_cores(tile, half):
+    size, lanes = tile.shape[0] // 2, (tile.shape[1] - half) // 2
+    parts = []
+    for core in range(2):
+        value = tile[:, half + core * lanes : half + (core + 1) * lanes]
+        out = tile[core * size : (core + 1) * size, :half]
+        parts.append(jnp.concatenate((out, value[:size], value[size:]), axis=1))
+    return parts
+
+
+def tile_cores_kernel(split, half, scalars, *refs):
     addends, (far_same, far_cross, near_cross, mine) = refs[:-4], refs[-4:]
-    size, width = mine.shape
-    half, quarter = width // 2, width // 4
     bit = view_bit(scalars, 0)
     for place, same, cross in ((1 - bit, far_same, far_cross), (bit, mine, near_cross)):
-        total = summed_tile(addends, place)
-        parts = []
-        for core in range(2):
-            value = total[:, half + core * quarter : half + (core + 1) * quarter]
-            out = total[core * size : (core + 1) * size, :half]
-            parts.append(jnp.concatenate((out, value[:size], value[size:]), axis=1))
+        parts = split(summed_tile(addends, place), half)
         same[...] = jnp.where(scalars[0] == 0, parts[0], parts[1]).astype(same.dtype)
         cross[...] = jnp.where(scalars[0] == 0, parts[1], parts[0]).astype(cross.dtype)
 
 
-def place_kernel(scalars, mine, far_same, near_cross, far_cross, value, out):
+def last_sums(scalars, mine, far_same, near_cross, far_cross):
+    for near, far, core in ((mine, far_same, scalars[0]), (near_cross, far_cross, 1 - scalars[0])):
+        yield near[...] + far[...].astype(jnp.float32), core
+
+
+def place_query_key_kernel(scalars, mine, far_same, near_cross, far_cross, query, key, value):
+    size = query.shape[1] // 2
+    for total, core in last_sums(scalars, mine, far_same, near_cross, far_cross):
+        columns = pl.ds(pl.multiple_of(core * size, size), size)
+        query[:, columns] = total[:, :size]
+        key[:, columns] = total[:, size : 2 * size]
+        value[:, pl.ds(pl.multiple_of(core * PAIR, PAIR), PAIR)] = total[:, 2 * size :]
+
+
+def place_value_out_kernel(scalars, mine, far_same, near_cross, far_cross, first_pairs, value, out):
     size, width = mine.shape
-    half, quarter = width // 2, width // 4
-    for near, far, core in ((mine, far_same, scalars[0]), (near_cross, far_cross, 1 - scalars[0])):
-        total = near[...] + far[...].astype(jnp.float32)
+    half, part = out.shape[1] // 2, value.shape[1] // 2
+    lanes = part - PAIR
+    for core in range(2):
+        value[:, core * part : core * part + PAIR] = first_pairs[:, core * PAIR : (core + 1) * PAIR]
+    for total, core in last_sums(scalars, mine, far_same, near_cross, far_cross):
         out[:, pl.ds(pl.multiple_of(core * half, half), half)] = total[:, :half]
-        columns = pl.ds(pl.multiple_of(core * quarter, quarter), quarter)
-        value[:size, columns] = total[:, half : half + quarter]
-        value[size:, columns] = total[:, half + quarter :]
-
-
-def summed_views(rows, packed):
-    for r in range(rows):
-        total = packed[r].astype(jnp.float32)
-        for i in range(r + rows, packed.shape[0], rows):
-            total = total + packed[i].astype(jnp.float32)
-        yield r, total
-
-
-def last_query_key_kernel(rows, packed, query, key):
-    size = packed.shape[2] // 2
-    for r, total in summed_views(rows, packed):
-        columns = slice(r * size, (r + 1) * size)
-        query[:, columns] = total[:, :size]
-        key[:, columns] = total[:, size:]
+        columns = pl.ds(pl.multiple_of(core * part + PAIR, PAIR), lanes)
+        value[:size, columns] = total[:, half : half + lanes]
+        value[size:, columns] = total[:, half + lanes :]
 
 
 def params(mebibytes):
@@ -516,11 +536,37 @@
     def second_exchange(sums):
         return lax.ppermute(sums[0], "scene", along_y), lax.ppermute(sums[1], "scene", along_x)
 
-    def across_views(packed):
-        return lax.all_to_all(packed, ("view", "row"), split_axis=0, concat_axis=0, tiled=True)
-
     pairs = groups // 2
-    tile = (2 * o_rows, width)
+    neighbours = [(i, i ^ 1) for i in range(groups)]
+    split_rows = {"query_key": q_rows, "value_out": o_rows}
+
+    def last_parts(addends, split, name):
+        tile = (addends[0].shape[1], sum(now.shape[2] for now in addends[::2]))
+        for bit in reversed(range(1, pairs.bit_length() - 1)):
+            send, keep = call(
+                functools.partial(tile_halves_kernel, bit),
+                [shape((1 << bit, *tile), kind) for kind in (bf16, f32)],
+                (scalars, *addends),
+                "view_bit_" + name,
+                SMEM,
+            )
+            addends = (keep, lax.ppermute(send, "view", [(i, i ^ (2 << bit)) for i in range(groups)]))
+        lanes = tile[0] * tile[1] // (2 * split_rows[name])
+        columns = width // 2
+        far_same, far_cross, near_cross, mine = call(
+            functools.partial(tile_cores_kernel, split, columns),
+            [shape((split_rows[name], lanes), kind) for kind in (bf16, bf16, f32, f32)],
+            (scalars, *addends),
+            "last_parts_" + name,
+            SMEM,
+        )
+        far_same = lax.ppermute(far_same, "view", [(i, i ^ 2) for i in range(groups)])
+        far_cross = lax.ppermute(far_cross, ("view", "row"), [(i, i ^ 5) for i in range(targets)])
+        near_cross = lax.ppermute(near_cross, "row", swap)
+        return mine, far_same, near_cross, far_cross
+
+    rest = part - PAIR
+    tile = (2 * o_rows, width // 2 + 2 * rest)
     send, keep = call(
         value_out_kernel,
         [shape((2, 2, pairs, *tile), kind) for kind in (bf16, f32)],
@@ -529,11 +575,13 @@
         SMEM,
         24,
     )
-    got = lax.ppermute(send, "view", [(i, i ^ 1) for i in range(groups)])
+    got = lax.ppermute(send, "view", neighbours)
+    k_block = (q_size, part + PAIR)
     q_later, k_later, q_now, k_now, q_keep, k_keep = call(
         query_key_kernel,
-        [shape(q_block, bf16)] * 4 + [shape((2, *q_block), f32)] * 2,
-        (scalars, normed_t, normed_far_t, after(dquery, send), dkey),
+        [shape(block, bf16) for block in (q_block, k_block, q_block, k_block)]
+        + [shape((2, *block), f32) for block in (q_block, k_block)],
+        (scalars, normed_t, normed_far_t, after(dquery, send), dkey, dvalue),
         "grad_query_key",
         SMEM,
         24,
@@ -541,58 +589,43 @@
     q_got, k_got = first_exchange((q_later, k_later))
     q_first, k_first = first_exchange((q_now, k_now))
     later = call(
-        go_on_kernel, [shape(q_block, bf16)] * 2, (q_keep, q_got, k_keep, k_got), "first_sum_query_key"
+        go_on_kernel, [shape(q_block, bf16), shape(k_block, bf16)], (q_keep, q_got, k_keep, k_got), "first_sum_query_key"
     )
     q_second, k_second = second_exchange(later)
-    packed = call(
-        pack_query_key_kernel,
-        [shape((q_size, 2 * part), bf16)],
-        (q_keep, q_first, q_second, k_keep, k_first, k_second),
-        "second_sum_query_key",
-    )[0]
-    part_shape = (2, pairs, 2 * o_rows, width // 2)
+    x_shape, y_shape = (2, pairs, 2 * o_rows, 2 * rest), (2, pairs, 2 * o_rows, width // 2)
     vo_parts = call(
         view_sum_kernel,
-        [shape(part_shape, bf16)] * 2 + [shape(part_shape, f32)] * 2,
-        (keep, after(got, packed)),
+        [shape(x_shape, bf16), shape(y_shape, bf16), shape(x_shape, f32), shape(y_shape, f32)],
+        (keep, after(got, later[0], q_first, k_first)),
         "view_sum_value_out",
-        cost=MUCH,
     )
     vo_got = first_exchange(vo_parts)
-    packed = across_views(packed.reshape(targets, q_rows, 2 * part))
-    grad_query, grad_key = call(
-        functools.partial(last_query_key_kernel, rows),
-        [shape((q_rows, inner), f32)] * 2,
-        (packed,),
-        "last_sum_query_key",
-    )
-
+    qk_tile = (2 * q_rows, 2 * part + PAIR)
+    qk_send, qk_keep = call(
+        query_key_tiles_kernel,
+        [shape((pairs, *qk_tile), kind) for kind in (bf16, f32)],
+        (scalars, after(q_keep, vo_parts[0]), q_first, q_second, k_keep, k_first, k_second),
+        "second_sum_query_key",
+        SMEM,
+    )
+    qk_addends = (qk_keep, lax.ppermute(qk_send, "view", neighbours))
+    vo_parts[2] = after(vo_parts[2], qk_send)
     vo_sums = first_sum(vo_parts, vo_got, "first_sum_value_out")
     v_got, o_got = second_exchange(vo_sums)
     addends = (vo_sums[3], o_got, vo_sums[2], v_got)
-    for bit in reversed(range(1, pairs.bit_length() - 1)):
-        send, keep = call(
-            functools.partial(tile_halves_kernel, bit),
-            [shape((1 << bit, *tile), kind) for kind in (bf16, f32)],
-            (scalars, *addends),
-            "view_bit_value_out",
-            SMEM,
-        )
-        addends = (keep, lax.ppermute(send, "view", [(i, i ^ (2 << bit)) for i in range(groups)]))
-    far_same, far_cross, near_cross, mine = call(
-        tile_cores_kernel,
-        [shape((o_rows, width), kind) for kind in (bf16, bf16, f32, f32)],
-        (scalars, *addends),
-        "last_parts_value_out",
+    qk_last = last_parts((after(qk_addends[0], vo_sums[0]), qk_addends[1]), query_key_cores, "query_key")
+    vo_last = last_parts((after(addends[0], qk_last[0]), *addends[1:]), value_out_cores, "value_out")
+    grad_query, grad_key, first_pairs = call(
+        place_query_key_kernel,
+        [shape((q_rows, inner), f32)] * 2 + [shape((q_rows, rows * PAIR), f32)],
+        (scalars, *qk_last),
+        "last_sum_query_key",
         SMEM,
     )
-    far_same = lax.ppermute(far_same, "view", [(i, i ^ 2) for i in range(groups)])
-    far_cross = lax.ppermute(far_cross, ("view", "row"), [(i, i ^ 5) for i in range(targets)])
-    near_cross = lax.ppermute(near_cross, "row", swap)
     grad_value, grad_out = call(
-        place_kernel,
+        place_value_out_kernel,
         [shape((q_rows, inner), f32), shape((o_rows, width), f32)],
-        (scalars, after(mine, grad_key), far_same, near_cross, far_cross),
+        (scalars, *vo_last, first_pairs),
         "last_sum_value_out",
         SMEM,
     )

time: 91.7 us -> 93.2 us (1.016)
  waiting for transfers between devices: 39.4 us -> 42.2 us
  Pallas kernels: 20.8 us -> 19.4 us
    ppermute x3, waiting for transfers between devices: 15.7 us -> 24.3 us  [first_exchange(): lax.ppermute(sends[0], 'scene', along_x)]
    ppermute x2, waiting for transfers between devices: 6.54 us -> 2.84 us  [second_exchange(): lax.ppermute(sums[0], 'scene', along_y)]
    all_to_all x1 -> x0, starting transfers between devices: 3.6 us -> none  [across_views(): lax.all_to_all(packed, ('view', 'row'), split_axis=0, concat_axis=0, tile...]
    ppermute x4 -> x8, starting transfers between devices: 3.15 us -> 5.92 us  [the longest x2 2.99 us: last_parts(): lax.ppermute(far_same, 'view', [(i, i ^ 2) for i in range(groups)])]
    ppermute x2, waiting for transfers between devices: 2.22 us -> 0.01 us  [second_exchange(): lax.ppermute(sums[1], 'scene', along_x)]
    ppermute x4 -> x8, waiting for transfers between devices: 6.48 us -> 8.22 us  [the longest x2 7.52 us: last_parts(): lax.ppermute(far_cross, ('view', 'row'), [(i, i ^ 5) for i in range(targe...]
    ppermute x3, waiting for transfers between devices: 3.31 us -> 1.75 us  [first_exchange(): lax.ppermute(sends[1], 'scene', along_y)]
    pallas_call x10 -> x11, Pallas kernels: 11.5 us -> 10.1 us  [call(): pl.pallas_call(kernel_body, in_specs=[first] + [VMEM] * (len(operands) -...]
  transfers between devices with their start and end apart: 27 -> 30, of which waited for: 16 -> 14; matrix products, arithmetic and copies ran while one was open for 0% -> 0% of each run, Pallas kernels for 15% -> 14%
where the time goes in v16:
time: 93.2 us; the launch traced here: 93 us
  waiting for transfers between devices  42.2 us (45%)
  starting transfers between devices  29.6 us (32%)
  Pallas kernels  19.4 us (21%)
    ppermute x3, waiting for transfers between devices, first_exchange(): lax.ppermute(sends[0], 'scene', along_x)  24.3 us
    pallas_call x11, Pallas kernels, call(): pl.pallas_call(kernel_body, in_specs=[first] + [VMEM] * (len(operands) -...  10.1 us
    ppermute x2, waiting for transfers between devices, last_parts(): lax.ppermute(far_cross, ('view', 'row'), [(i, i ^ 5) for i in range(targe...  7.52 us
    ppermute x3, starting transfers between devices, shards(): granted = [lax.ppermute(partners, 'view', pairs) for pairs in between]  5.62 us
    ppermute x3, starting transfers between devices, shards(): lax.ppermute(part_out, 'view', pairs)  4.45 us
    pallas_call x1, Pallas kernels, shards(): pl.pallas_call(project_kernel, in_specs=[SMEM] + [VMEM] * 10, out_specs=[...  4.13 us
    ppermute x3, starting transfers between devices, first_exchange(): lax.ppermute(sends[1], 'scene', along_y)  3.66 us
    ppermute x3, starting transfers between devices, first_exchange(): lax.ppermute(sends[0], 'scene', along_x)  3.5 us
  transfers between devices with their start and end apart: 30, of which 14 were waited for; matrix products, arithmetic and copies ran while one was open for 0% of the time, Pallas kernels for 14%

profile of v16, /device:TPU:0, one launch (start us, length us, event | category | flops | bytes accessed | tf_op | source)
XLA Modules:
  0.0 93.0 jit_solution(14158074426868325908)
XLA Ops:
  0.6 0.8 copy.13.partners
  1.4 3.0 %collective-permute-start.2 = (s32[1,4,3]{2,1,0:T(4,128)S(1)}, s32[1,4,3]{2,1,0:T(4,128)S(1)}, u32[]{:S(2)}, u32[]{:S(2)}) collective-permute-start(s32[1,4,3]{2,1,0:T(4,128)S(1)} %copy.13.partners), channel_id=1, source_target_pairs={{0,2},{2,0},{4,6},{6,4},{1,3},{3,1},{5,7},{7,5},{8,10},{10,8},{12,... | collective-permute-start | bytes 152 | tf_op jit(solution)/shard_map/ppermute | solution.py:436
  4.4 2.6 %collective-permute-start.1 = (s32[1,4,3]{2,1,0:T(4,128)S(1)}, s32[1,4,3]{2,1,0:T(4,128)S(1)}, u32[]{:S(2)}, u32[]{:S(2)}) collective-permute-start(s32[1,4,3]{2,1,0:T(4,128)S(1)} %copy.13.partners), channel_id=1, source_target_pairs={{0,4},{2,6},{4,0},{6,2},{1,5},{3,7},{5,1},{7,3},{8,12},{10,14},{12... | collective-permute-start | bytes 152 | tf_op jit(solution)/shard_map/ppermute | solution.py:436
  7.0 0.5 collective-permute-start.7
  7.5 1.2 %alive.1 = s32[16]{0:T(128)S(1)} custom-call(s32[1,4,3]{2,1,0:T(4,128)S(1)} %copy.13.partners), custom_call_target="tpu_custom_call" | custom-call | flops 40000000000 | bytes 1 | tf_op jit(solution)/shard_map/alive/pallas_call | solution.py:426
  8.8 0.1 stack.23.scalars
  8.9 0.0 copy-start.5
  8.9 0.0 copy-start.6
  8.9 0.0 copy-start.7
  8.9 0.0 collective-permute-done.2.refs_2_
  8.9 3.5 %collective-permute-done.refs_0_ = s32[1,4,3]{2,1,0:T(4,128)S(1)} collective-permute-done((s32[1,4,3]{2,1,0:T(4,128)S(1)}, s32[1,4,3]{2,1,0:T(4,128)S(1)}, u32[]{:S(2)}, u32[]{:S(2)}) %collective-permute-start) | collective-permute-done | bytes 80 | tf_op jit(solution)/shard_map/ppermute | solution.py:436
  12.4 0.8 pick.1
  13.2 0.4 collective-permute-start.3
  13.6 0.0 collective-permute-start.4
  13.6 4.0 %collective-permute-start.5 = (bf16[32,1536]{1,0:T(8,128)(2,1)S(1)}, bf16[32,1536]{1,0:T(8,128)(2,1)S(1)}, u32[]{:S(2)}, u32[]{:S(2)}) collective-permute-start(bf16[32,1536]{1,0:T(8,128)(2,1)S(1)} %get-tuple-element.77), channel_id=1, source_target_pairs={{0,2},{2,0},{4,6},{6,4},{1,3},{3,1},{5,7},{7,5},{8,10},{10,8},{12,... | collective-permute-start | bytes 294920 | tf_op jit(solution)/shard_map/ppermute | solution.py:453
  17.7 4.1 %project.1 = (bf16[1536,256]{1,0:T(8,128)(2,1)S(1)}, bf16[256,384]{1,0:T(8,128)(2,1)S(1)}, bf16[256,384]{1,0:T(8,128)(2,1)S(1)}, bf16[256,1536]{1,0:T(8,128)(2,1...) custom-call(s32[5]{0:T(128)S(1)} %stack.23.scalars, ...), custom_call_target="tpu_custom_call" | custom-call | flops 1 | bytes 1 | tf_op jit(solution)/shard_map/project/pallas_call | solution.py:455
  21.8 0.0 collective-permute-done.3.refs_0_
  21.9 0.4 collective-permute-done.4.refs_1_
  22.3 0.1 collective-permute-start.8
  22.4 0.4 collective-permute-start.9
  22.8 0.1 collective-permute-start.10
  22.9 0.7 collective-permute-done.8.refs_3_
  23.6 0.2 collective-permute-done.9.refs_4_
  23.7 0.4 collective-permute-done.10.refs_5_
  24.1 3.2 %attention_forward.1 = (bf16[1536,192]{1,0:T(8,128)(2,1)S(1)}, bf16[192,384]{1,0:T(8,128)(2,1)S(1)}, bf16[192,384]{1,0:T(8,128)(2,1)S(1)}, f32[3,64,512]{2,1,0:T...) custom-call(s32[5]{0:T(128)S(1)} %stack.23.scalars, ...), custom_call_target="tpu_custom_call" | custom-call | flops 1 | bytes 1 | tf_op jit(solution)/shard_map/attention_forward/pallas_call | solution.py:491
  27.3 0.2 collective-permute-start.11
  27.5 1.6 %attention_backward.1 = (bf16[256,384]{1,0:T(8,128)(2,1)S(1)}, bf16[448,384]{1,0:T(8,128)(2,1)S(1)}) custom-call(bf16[3,512,128]{2,1,0:T(8,128)(2,1)S(1)} %get-tuple-element.84.refs_6_.query_stack, bf16[3,512,128]{2,1,0:T(8,128)(2,1)S(1)} %get-tuple-element.85.refs_7_.grad_stack, f32[3,64,512]{2,1,0:T(8,128)S(1)} %get-tuple-element.89.dprob_own, ...), custom_call_target="tpu_custom_call" | custom-call | flops 1 | bytes 1 | tf_op jit(solution)/shard_map/attention_backward/pallas_call | solution.py:479
  29.1 1.4 %grad_value_out.1 = (bf16[2,2,2,48,1280]{4,3,2,1,0:T(8,128)(2,1)S(1)}, f32[2,2,2,48,1280]{4,3,2,1,0:T(8,128)S(1)}) custom-call(s32[5]{0:T(128)S(1)} %stack.23.scalars, bf16[1536,256]{1,0:T(8,128)(2,1)S(1)} %get-tuple-element.79.normed_t, bf16[1536,192]{1,0:T(8,128)(2,1)S(1)} %get-tuple-element.88.normed_far_t, ...), custom_call_target="tpu_custom_call" | custom-call | flops 1 | bytes 1 | tf_op jit(solution)/shard_map/grad_value_out/pallas_call | solution.py:479
  30.5 0.4 collective-permute-start.12
  30.9 1.9 %grad_query_key.1 = (bf16[384,384]{1,0:T(8,128)(2,1)S(1)}, bf16[384,512]{1,0:T(8,128)(2,1)S(1)}, bf16[384,384]{1,0:T(8,128)(2,1)S(1)}, bf16[384,512]{1,0:T(8,128...) custom-call(s32[5]{0:T(128)S(1)} %stack.23.scalars, ...), custom_call_target="tpu_custom_call" | custom-call | flops 1 | bytes 1 | tf_op jit(solution)/shard_map/grad_query_key/pallas_call | solution.py:479
  32.8 1.6 %collective-permute-start.14 = (bf16[384,512]{1,0:T(8,128)(2,1)S(1)}, bf16[384,512]{1,0:T(8,128)(2,1)S(1)}, u32[]{:S(2)}, u32[]{:S(2)}) collective-permute-start(bf16[384,512]{1,0:T(8,128)(2,1)S(1)} %get-tuple-element.107), channel_id=1, source_target_pairs={{0,16},{8,24},{16,0},{24,8},{1,17},{9,25},{17,1},{25,9},{2,18},{10... | collective-permute-start | bytes 1179656 | tf_op jit(solution)/shard_map/ppermute | solution.py:529
  34.4 1.5 %collective-permute-start.13 = (bf16[384,384]{1,0:T(8,128)(2,1)S(1)}, bf16[384,384]{1,0:T(8,128)(2,1)S(1)}, u32[]{:S(2)}, u32[]{:S(2)}) collective-permute-start(bf16[384,384]{1,0:T(8,128)(2,1)S(1)} %get-tuple-element.105), channel_id=1, source_target_pairs={{0,8},{8,0},{16,24},{24,16},{1,9},{9,1},{17,25},{25,17},{2,10},{10... | collective-permute-start | bytes 884744 | tf_op jit(solution)/shard_map/ppermute | solution.py:529
  35.9 0.5 collective-permute-start.16
  36.4 6.7 %collective-permute-done.13.q_got = bf16[384,384]{1,0:T(8,128)(2,1)S(1)} collective-permute-done((bf16[384,384]{1,0:T(8,128)(2,1)S(1)}, bf16[384,384]{1,0:T(8,128)(2,1)S(1)}, u32[]{:S(2)}, u32[]{:S(2)}) %collective-permute-start.13) | collective-permute-done | bytes 294944 | tf_op jit(solution)/shard_map/ppermute | solution.py:529
  43.1 1.7 %collective-permute-done.14.k_got = bf16[384,512]{1,0:T(8,128)(2,1)S(1)} collective-permute-done((bf16[384,512]{1,0:T(8,128)(2,1)S(1)}, bf16[384,512]{1,0:T(8,128)(2,1)S(1)}, u32[]{:S(2)}, u32[]{:S(2)}) %collective-permute-start.14) | collective-permute-done | bytes 393248 | tf_op jit(solution)/shard_map/ppermute | solution.py:529
  44.9 0.1 first_sum_query_key.1
  45.0 1.6 %collective-permute-start.18 = (bf16[384,512]{1,0:T(8,128)(2,1)S(1)}, bf16[384,512]{1,0:T(8,128)(2,1)S(1)}, u32[]{:S(2)}, u32[]{:S(2)}) collective-permute-start(bf16[384,512]{1,0:T(8,128)(2,1)S(1)} %get-tuple-element.114), channel_id=1, source_target_pairs={{0,8},{8,0},{16,24},{24,16},{1,9},{9,1},{17,25},{25,17},{2,10},{10... | collective-permute-start | bytes 1179656 | tf_op jit(solution)/shard_map/ppermute | solution.py:537
  46.6 0.5 collective-permute-start.15
  47.1 1.5 %collective-permute-start.17 = (bf16[384,384]{1,0:T(8,128)(2,1)S(1)}, bf16[384,384]{1,0:T(8,128)(2,1)S(1)}, u32[]{:S(2)}, u32[]{:S(2)}) collective-permute-start(bf16[384,384]{1,0:T(8,128)(2,1)S(1)} %get-tuple-element.108), channel_id=1, source_target_pairs={{0,16},{8,24},{16,0},{24,8},{1,17},{9,25},{17,1},{25,9},{2,18},{10... | collective-permute-start | bytes 884744 | tf_op jit(solution)/shard_map/ppermute | solution.py:537
  48.7 12.2 %collective-permute-done.15.q_first = bf16[384,384]{1,0:T(8,128)(2,1)S(1)} collective-permute-done((bf16[384,384]{1,0:T(8,128)(2,1)S(1)}, bf16[384,384]{1,0:T(8,128)(2,1)S(1)}, u32[]{:S(2)}, u32[]{:S(2)}) %collective-permute-start.15) | collective-permute-done | bytes 294944 | tf_op jit(solution)/shard_map/ppermute | solution.py:529
  60.8 0.0 collective-permute-done.16.k_first
  60.8 0.2 view_sum_value_out.1
  61.0 1.6 %collective-permute-start.20 = (bf16[2,2,48,768]{3,2,1,0:T(8,128)(2,1)S(1)}, bf16[2,2,48,768]{3,2,1,0:T(8,128)(2,1)S(1)}, u32[]{:S(2)}, u32[]{:S(2)}) collective-permute-start(bf16[2,2,48,768]{3,2,1,0:T(8,128)(2,1)S(1)} %get-tuple-element.120), channel_id=1, source_target_pairs={{0,16},{8,24},{16,0},{24,8},{1,17},{9,25},{17,1},{25,9},{2,18},{10... | collective-permute-start | bytes 884744 | tf_op jit(solution)/shard_map/ppermute | solution.py:529
  62.6 0.9 second_sum_query_key.1
  63.4 1.8 %collective-permute-start.21 = (bf16[2,96,896]{2,1,0:T(8,128)(2,1)S(1)}, bf16[2,96,896]{2,1,0:T(8,128)(2,1)S(1)}, u32[]{:S(2)}, u32[]{:S(2)}) collective-permute-start(bf16[2,96,896]{2,1,0:T(8,128)(2,1)S(1)} %get-tuple-element.117), channel_id=1, source_target_pairs={{0,2},{2,0},{4,6},{6,4},{1,3},{3,1},{5,7},{7,5},{8,10},{10,8},{12,... | collective-permute-start | bytes 1032200 | tf_op jit(solution)/shard_map/ppermute | solution.py:611
  65.2 1.5 %collective-permute-start.19 = (bf16[2,2,48,512]{3,2,1,0:T(8,128)(2,1)S(1)}, bf16[2,2,48,512]{3,2,1,0:T(8,128)(2,1)S(1)}, u32[]{:S(2)}, u32[]{:S(2)}) collective-permute-start(bf16[2,2,48,512]{3,2,1,0:T(8,128)(2,1)S(1)} %get-tuple-element.112), channel_id=1, source_target_pairs={{0,8},{8,0},{16,24},{24,16},{1,9},{9,1},{17,25},{25,17},{2,10},{10... | collective-permute-start | bytes 589832 | tf_op jit(solution)/shard_map/ppermute | solution.py:529
  66.7 5.4 %collective-permute-done.19.x_got = bf16[2,2,48,512]{3,2,1,0:T(8,128)(2,1)S(1)} collective-permute-done((bf16[2,2,48,512]{3,2,1,0:T(8,128)(2,1)S(1)}, bf16[2,2,48,512]{3,2,1,0:T(8,128)(2,1)S(1)}, u32[]{:S(2)}, u32[]{:S(2)}) %collective-permute-start.19) | collective-permute-done | bytes 196640 | tf_op jit(solution)/shard_map/ppermute | solution.py:529
  72.2 0.1 first_sum_value_out.1
  72.3 1.6 %collective-permute-start.25 = (bf16[2,48,768]{2,1,0:T(8,128)(2,1)S(1)}, bf16[2,48,768]{2,1,0:T(8,128)(2,1)S(1)}, u32[]{:S(2)}, u32[]{:S(2)}) collective-permute-start(bf16[2,48,768]{2,1,0:T(8,128)(2,1)S(1)} %get-tuple-element.131), channel_id=1, source_target_pairs={{0,8},{8,0},{16,24},{24,16},{1,9},{9,1},{17,25},{25,17},{2,10},{10... | collective-permute-start | bytes 442376 | tf_op jit(solution)/shard_map/ppermute | solution.py:537
  73.8 0.5 collective-permute-start.26
  74.3 0.6 last_parts_query_key.1
  75.0 0.1 collective-permute-start.23
  75.0 0.6 collective-permute-start.22
  75.6 2.8 %collective-permute-done.26.refs_3_ = bf16[2,48,512]{2,1,0:T(8,128)(2,1)S(1)} collective-permute-done((bf16[2,48,512]{2,1,0:T(8,128)(2,1)S(1)}, bf16[2,48,512]{2,1,0:T(8,128)(2,1)S(1)}, u32[]{:S(2)}, u32[]{:S(2)}) %collective-permute-start.26) | collective-permute-done | bytes 98336 | tf_op jit(solution)/shard_map/ppermute | solution.py:537
  78.4 0.6 last_parts_value_out.1
  79.1 0.1 collective-permute-start.28
  79.1 0.6 collective-permute-start.24
  79.7 2.4 %collective-permute-start.27 = (bf16[24,1280]{1,0:T(8,128)(2,1)S(1)}, bf16[24,1280]{1,0:T(8,128)(2,1)S(1)}, u32[]{:S(2)}, u32[]{:S(2)}) collective-permute-start(bf16[24,1280]{1,0:T(8,128)(2,1)S(1)} %get-tuple-element.134), channel_id=1, source_target_pairs={{0,4},{2,6},{4,0},{6,2},{1,5},{3,7},{5,1},{7,3},{8,12},{10,14},{12... | collective-permute-start | bytes 184328 | tf_op jit(solution)/shard_map/ppermute | solution.py:563
  82.2 0.6 collective-permute-done.22.far_same
  82.7 6.3 %collective-permute-done.24.far_cross = bf16[48,896]{1,0:T(8,128)(2,1)S(1)} collective-permute-done((bf16[48,896]{1,0:T(8,128)(2,1)S(1)}, bf16[48,896]{1,0:T(8,128)(2,1)S(1)}, u32[]{:S(2)}, u32[]{:S(2)}) %collective-permute-start.24) | collective-permute-done | bytes 86048 | tf_op jit(solution)/shard_map/ppermute | solution.py:564
  89.1 1.3 %last_sum_query_key.1 = (f32[48,768]{1,0:T(8,128)}, f32[48,768]{1,0:T(8,128)}, f32[48,256]{1,0:T(8,128)S(1)}) custom-call(s32[5]{0:T(128)S(1)} %stack.23.scalars, f32[48,896]{1,0:T(8,128)S(1)} %get-tuple-element.123.mine, bf16[48,896]{1,0:T(8,128)(2,1)S(1)} %collective-permute-done.22.far_same, f32[48,896]{1,0:T(8,128)S(1)} %collective-permute-done.23.near_cross, ...), custom_call_target="tpu_custom_call" | custom-call | flops 1 | bytes 1 | tf_op jit(solution)/shard_map/last_sum_query_key/pallas_call | solution.py:479
  90.4 0.1 collective-permute-done.27.far_same
  90.5 1.2 %collective-permute-done.29.far_cross = bf16[24,1280]{1,0:T(8,128)(2,1)S(1)} collective-permute-done((bf16[24,1280]{1,0:T(8,128)(2,1)S(1)}, bf16[24,1280]{1,0:T(8,128)(2,1)S(1)}, u32[]{:S(2)}, u32[]{:S(2)}) %collective-permute-start.29) | collective-permute-done | bytes 61472 | tf_op jit(solution)/shard_map/ppermute | solution.py:564
  91.7 1.3 %last_sum_value_out.1 = (f32[48,768]{1,0:T(8,128)}, f32[24,1536]{1,0:T(8,128)}) custom-call(s32[5]{0:T(128)S(1)} %stack.23.scalars, f32[24,1280]{1,0:T(8,128)S(1)} %get-tuple-element.133.mine, bf16[24,1280]{1,0:T(8,128)(2,1)S(1)} %collective-permute-done.27.far_same, f32[24,1280]{1,0:T(8,128)S(1)} %collective-permute-done.28.near_cross, ...), custom_call_target="tpu_custom_call" | custom-call | flops 1 | bytes 1 | tf_op jit(solution)/shard_map/last_sum_value_out/pallas_call | solution.py:479
  (29 shorter events, 0.1 us)
Async XLA Ops:
  1.4 7.5 %collective-permute-start.2 = (s32[1,4,3]{2,1,0:T(4,128)S(1)}, s32[1,4,3]{2,1,0:T(4,128)S(1)}, u32[]{:S(2)}, u32[]{:S(2)}) collective-permute-start(s32[1,4,3]{2,1,0:T(4,128)S(1)} %copy.13.partners), channel_id=1, source_target_pairs={{0,2},{2,0},{4,6},{6,4},{1,3},{3,1},{5,7},{7,5},{8,10},{10,8},{12,... | collective-permute-start | bytes 152 | tf_op jit(solution)/shard_map/ppermute | solution.py:436
  4.4 4.5 %collective-permute-start.1 = (s32[1,4,3]{2,1,0:T(4,128)S(1)}, s32[1,4,3]{2,1,0:T(4,128)S(1)}, u32[]{:S(2)}, u32[]{:S(2)}) collective-permute-start(s32[1,4,3]{2,1,0:T(4,128)S(1)} %copy.13.partners), channel_id=1, source_target_pairs={{0,4},{2,6},{4,0},{6,2},{1,5},{3,7},{5,1},{7,3},{8,12},{10,14},{12... | collective-permute-start | bytes 152 | tf_op jit(solution)/shard_map/ppermute | solution.py:436
  7.0 5.4 %collective-permute-start = (s32[1,4,3]{2,1,0:T(4,128)S(1)}, s32[1,4,3]{2,1,0:T(4,128)S(1)}, u32[]{:S(2)}, u32[]{:S(2)}) collective-permute-start(s32[1,4,3]{2,1,0:T(4,128)S(1)} %copy.13.partners), channel_id=1, source_target_pairs={{0,6},{2,4},{4,2},{6,0},{1,7},{3,5},{5,3},{7,1},{8,14},{10,12},{12... | collective-permute-start | bytes 152 | tf_op jit(solution)/shard_map/ppermute | solution.py:436
  7.0 10.6 %collective-permute-start.6 = (bf16[4,32,1536]{2,1,0:T(8,128)(2,1)}, bf16[4,32,1536]{2,1,0:T(8,128)(2,1)S(1)}, u32[]{:S(2)}, u32[]{:S(2)}) collective-permute-start(bf16[4,32,1536]{2,1,0:T(8,128)(2,1)} %bitcast.7), channel_id=1, source_target_pairs={{0,1},{1,0},{2,3},{3,2},{4,5},{5,4},{6,7},{7,6},{8,9},{9,8},{10,11... | collective-permute-start | bytes 1179656 | tf_op jit(solution)/shard_map/ppermute | solution.py:441
  7.0 10.6 %collective-permute-start.7 = (bf16[4,32,1536]{2,1,0:T(8,128)(2,1)}, bf16[4,32,1536]{2,1,0:T(8,128)(2,1)S(1)}, u32[]{:S(2)}, u32[]{:S(2)}) collective-permute-start(bf16[4,32,1536]{2,1,0:T(8,128)(2,1)} %bitcast.10), channel_id=1, source_target_pairs={{0,1},{1,0},{2,3},{3,2},{4,5},{5,4},{6,7},{7,6},{8,9},{9,8},{10,11... | collective-permute-start | bytes 1179656 | tf_op jit(solution)/shard_map/ppermute | solution.py:442
  7.5 4.9 %copy-start.4 = (bf16[1,4,1,32,1536]{4,3,2,1,0:T(8,128)(2,1)S(1)}, bf16[1,4,1,32,1536]{4,3,2,1,0:T(8,128)(2,1)}, u32[]{:S(2)}) copy-start(bf16[1,4,1,32,1536]{4,3,2,1,0:T(8,128)(2,1)} %param.10) | copy-start | bytes 1179652
  8.8 8.8 %copy-start = (bf16[1536,768]{1,0:T(8,128)(2,1)S(1)}, bf16[1536,768]{1,0:T(8,128)(2,1)}, u32[]{:S(2)}) copy-start(bf16[1536,768]{1,0:T(8,128)(2,1)} %refs_11_.1) | copy-start | bytes 7077892
  8.9 8.8 %copy-start.1 = (bf16[1536,768]{1,0:T(8,128)(2,1)S(1)}, bf16[1536,768]{1,0:T(8,128)(2,1)}, u32[]{:S(2)}) copy-start(bf16[1536,768]{1,0:T(8,128)(2,1)} %refs_12_.1) | copy-start | bytes 7077892
  8.9 8.8 %copy-start.2 = (bf16[1536,768]{1,0:T(8,128)(2,1)S(1)}, bf16[1536,768]{1,0:T(8,128)(2,1)}, u32[]{:S(2)}) copy-start(bf16[1536,768]{1,0:T(8,128)(2,1)} %w_query.1) | copy-start | bytes 7077892
  8.9 8.8 %copy-start.3 = (bf16[768,1536]{1,0:T(8,128)(2,1)S(1)}, bf16[768,1536]{1,0:T(8,128)(2,1)}, u32[]{:S(2)}) copy-start(bf16[768,1536]{1,0:T(8,128)(2,1)} %w_out.1) | copy-start | bytes 7077892
  8.9 8.8 %copy-start.5 = (bf16[1,4,1,32,1536]{4,3,2,1,0:T(8,128)(2,1)S(1)}, bf16[1,4,1,32,1536]{4,3,2,1,0:T(8,128)(2,1)}, u32[]{:S(2)}) copy-start(bf16[1,4,1,32,1536]{4,3,2,1,0:T(8,128)(2,1)} %param.18) | copy-start | bytes 1179652
  8.9 8.8 %copy-start.6 = (bf16[9,1536]{1,0:T(8,128)(2,1)S(1)}, bf16[9,1536]{1,0:T(8,128)(2,1)}, u32[]{:S(2)}) copy-start(bf16[9,1536]{1,0:T(8,128)(2,1)} %taps.1) | copy-start | bytes 82948
  8.9 8.8 %copy-start.7 = (f32[1536]{0:T(1024)S(1)}, f32[1536]{0:T(1024)}, u32[]{:S(2)}) copy-start(f32[1536]{0:T(1024)} %refs_10_.1) | copy-start | bytes 18436
  13.2 8.7 %collective-permute-start.3 = (bf16[32,1536]{1,0:T(8,128)(2,1)S(1)}, bf16[32,1536]{1,0:T(8,128)(2,1)S(1)}, u32[]{:S(2)}, u32[]{:S(2)}) collective-permute-start(bf16[32,1536]{1,0:T(8,128)(2,1)S(1)} %get-tuple-element.75), channel_id=1, source_target_pairs={{0,6},{2,4},{4,2},{6,0},{1,7},{3,5},{5,3},{7,1},{8,14},{10,12},{12... | collective-permute-start | bytes 294920 | tf_op jit(solution)/shard_map/ppermute | solution.py:453
  13.6 8.7 %collective-permute-start.4 = (bf16[32,1536]{1,0:T(8,128)(2,1)S(1)}, bf16[32,1536]{1,0:T(8,128)(2,1)S(1)}, u32[]{:S(2)}, u32[]{:S(2)}) collective-permute-start(bf16[32,1536]{1,0:T(8,128)(2,1)S(1)} %get-tuple-element.76), channel_id=1, source_target_pairs={{0,4},{2,6},{4,0},{6,2},{1,5},{3,7},{5,1},{7,3},{8,12},{10,14},{12... | collective-permute-start | bytes 294920 | tf_op jit(solution)/shard_map/ppermute | solution.py:453
  13.6 8.7 %collective-permute-start.5 = (bf16[32,1536]{1,0:T(8,128)(2,1)S(1)}, bf16[32,1536]{1,0:T(8,128)(2,1)S(1)}, u32[]{:S(2)}, u32[]{:S(2)}) collective-permute-start(bf16[32,1536]{1,0:T(8,128)(2,1)S(1)} %get-tuple-element.77), channel_id=1, source_target_pairs={{0,2},{2,0},{4,6},{6,4},{1,3},{3,1},{5,7},{7,5},{8,10},{10,8},{12,... | collective-permute-start | bytes 294920 | tf_op jit(solution)/shard_map/ppermute | solution.py:453
  22.3 1.3 %collective-permute-start.8 = (bf16[32,1536]{1,0:T(8,128)(2,1)S(1)}, bf16[32,1536]{1,0:T(8,128)(2,1)S(1)}, u32[]{:S(2)}, u32[]{:S(2)}) collective-permute-start(bf16[32,1536]{1,0:T(8,128)(2,1)S(1)} %collective-permute-done.3.refs_0_), channel_id=1, source_target_pairs={{0,1},{1,0},{2,3},{3,2},{4,5},{5,4},{6,7},{7,6},{8,9},{9,8},{10,11... | collective-permute-start | bytes 294920 | tf_op jit(solution)/shard_map/ppermute | solution.py:476
  22.4 1.4 %collective-permute-start.9 = (bf16[32,1536]{1,0:T(8,128)(2,1)S(1)}, bf16[32,1536]{1,0:T(8,128)(2,1)S(1)}, u32[]{:S(2)}, u32[]{:S(2)}) collective-permute-start(bf16[32,1536]{1,0:T(8,128)(2,1)S(1)} %collective-permute-done.4.refs_1_), channel_id=1, source_target_pairs={{0,1},{1,0},{2,3},{3,2},{4,5},{5,4},{6,7},{7,6},{8,9},{9,8},{10,11... | collective-permute-start | bytes 294920 | tf_op jit(solution)/shard_map/ppermute | solution.py:476
  22.8 1.3 %collective-permute-start.10 = (bf16[32,1536]{1,0:T(8,128)(2,1)S(1)}, bf16[32,1536]{1,0:T(8,128)(2,1)S(1)}, u32[]{:S(2)}, u32[]{:S(2)}) collective-permute-start(bf16[32,1536]{1,0:T(8,128)(2,1)S(1)} %collective-permute-done.5.refs_2_), channel_id=1, source_target_pairs={{0,1},{1,0},{2,3},{3,2},{4,5},{5,4},{6,7},{7,6},{8,9},{9,8},{10,11... | collective-permute-start | bytes 294920 | tf_op jit(solution)/shard_map/ppermute | solution.py:476
  27.3 1.8 %collective-permute-start.11 = (bf16[384,256]{1,0:T(8,128)(2,1)S(1)}, bf16[384,256]{1,0:T(8,128)(2,1)S(1)}, u32[]{:S(2)}, u32[]{:S(2)}) collective-permute-start(bf16[384,256]{1,0:T(8,128)(2,1)S(1)} %get-tuple-element.99.mine), channel_id=1, source_target_pairs={{0,1},{1,0},{2,3},{3,2},{4,5},{5,4},{6,7},{7,6},{8,9},{9,8},{10,11... | collective-permute-start | bytes 589832 | tf_op jit(solution)/shard_map/ppermute | solution.py:511
  30.5 30.3 %collective-permute-start.12 = (bf16[2,2,2,48,1280]{4,3,2,1,0:T(8,128)(2,1)S(1)}, bf16[2,2,2,48,1280]{4,3,2,1,0:T(8,128)(2,1)S(1)}, u32[]{:S(2)}, u32[]{:S(2)}) collective-permute-start(bf16[2,2,2,48,1280]{4,3,2,1,0:T(8,128)(2,1)S(1)} %get-tuple-element.101), channel_id=1, source_target_pairs={{0,2},{2,0},{4,6},{6,4},{1,3},{3,1},{5,7},{7,5},{8,10},{10,8},{12,... | collective-permute-start | bytes 2949128 | tf_op jit(solution)/shard_map/ppermute | solution.py:578
  32.8 12.0 %collective-permute-start.14 = (bf16[384,512]{1,0:T(8,128)(2,1)S(1)}, bf16[384,512]{1,0:T(8,128)(2,1)S(1)}, u32[]{:S(2)}, u32[]{:S(2)}) collective-permute-start(bf16[384,512]{1,0:T(8,128)(2,1)S(1)} %get-tuple-element.107), channel_id=1, source_target_pairs={{0,16},{8,24},{16,0},{24,8},{1,17},{9,25},{17,1},{25,9},{2,18},{10... | collective-permute-start | bytes 1179656 | tf_op jit(solution)/shard_map/ppermute | solution.py:529
  34.4 8.7 %collective-permute-start.13 = (bf16[384,384]{1,0:T(8,128)(2,1)S(1)}, bf16[384,384]{1,0:T(8,128)(2,1)S(1)}, u32[]{:S(2)}, u32[]{:S(2)}) collective-permute-start(bf16[384,384]{1,0:T(8,128)(2,1)S(1)} %get-tuple-element.105), channel_id=1, source_target_pairs={{0,8},{8,0},{16,24},{24,16},{1,9},{9,1},{17,25},{25,17},{2,10},{10... | collective-permute-start | bytes 884744 | tf_op jit(solution)/shard_map/ppermute | solution.py:529
  35.9 24.9 %collective-permute-start.16 = (bf16[384,512]{1,0:T(8,128)(2,1)S(1)}, bf16[384,512]{1,0:T(8,128)(2,1)S(1)}, u32[]{:S(2)}, u32[]{:S(2)}) collective-permute-start(bf16[384,512]{1,0:T(8,128)(2,1)S(1)} %get-tuple-element.110), channel_id=1, source_target_pairs={{0,16},{8,24},{16,0},{24,8},{1,17},{9,25},{17,1},{25,9},{2,18},{10... | collective-permute-start | bytes 1179656 | tf_op jit(solution)/shard_map/ppermute | solution.py:529
  45.0 17.6 %collective-permute-start.18 = (bf16[384,512]{1,0:T(8,128)(2,1)S(1)}, bf16[384,512]{1,0:T(8,128)(2,1)S(1)}, u32[]{:S(2)}, u32[]{:S(2)}) collective-permute-start(bf16[384,512]{1,0:T(8,128)(2,1)S(1)} %get-tuple-element.114), channel_id=1, source_target_pairs={{0,8},{8,0},{16,24},{24,16},{1,9},{9,1},{17,25},{25,17},{2,10},{10... | collective-permute-start | bytes 1179656 | tf_op jit(solution)/shard_map/ppermute | solution.py:537
  46.6 14.2 %collective-permute-start.15 = (bf16[384,384]{1,0:T(8,128)(2,1)S(1)}, bf16[384,384]{1,0:T(8,128)(2,1)S(1)}, u32[]{:S(2)}, u32[]{:S(2)}) collective-permute-start(bf16[384,384]{1,0:T(8,128)(2,1)S(1)} %get-tuple-element.109), channel_id=1, source_target_pairs={{0,8},{8,0},{16,24},{24,16},{1,9},{9,1},{17,25},{25,17},{2,10},{10... | collective-permute-start | bytes 884744 | tf_op jit(solution)/shard_map/ppermute | solution.py:529
  47.1 15.5 %collective-permute-start.17 = (bf16[384,384]{1,0:T(8,128)(2,1)S(1)}, bf16[384,384]{1,0:T(8,128)(2,1)S(1)}, u32[]{:S(2)}, u32[]{:S(2)}) collective-permute-start(bf16[384,384]{1,0:T(8,128)(2,1)S(1)} %get-tuple-element.108), channel_id=1, source_target_pairs={{0,16},{8,24},{16,0},{24,8},{1,17},{9,25},{17,1},{25,9},{2,18},{10... | collective-permute-start | bytes 884744 | tf_op jit(solution)/shard_map/ppermute | solution.py:537
  61.0 11.2 %collective-permute-start.20 = (bf16[2,2,48,768]{3,2,1,0:T(8,128)(2,1)S(1)}, bf16[2,2,48,768]{3,2,1,0:T(8,128)(2,1)S(1)}, u32[]{:S(2)}, u32[]{:S(2)}) collective-permute-start(bf16[2,2,48,768]{3,2,1,0:T(8,128)(2,1)S(1)} %get-tuple-element.120), channel_id=1, source_target_pairs={{0,16},{8,24},{16,0},{24,8},{1,17},{9,25},{17,1},{25,9},{2,18},{10... | collective-permute-start | bytes 884744 | tf_op jit(solution)/shard_map/ppermute | solution.py:529
  63.4 10.9 %collective-permute-start.21 = (bf16[2,96,896]{2,1,0:T(8,128)(2,1)S(1)}, bf16[2,96,896]{2,1,0:T(8,128)(2,1)S(1)}, u32[]{:S(2)}, u32[]{:S(2)}) collective-permute-start(bf16[2,96,896]{2,1,0:T(8,128)(2,1)S(1)} %get-tuple-element.117), channel_id=1, source_target_pairs={{0,2},{2,0},{4,6},{6,4},{1,3},{3,1},{5,7},{7,5},{8,10},{10,8},{12,... | collective-permute-start | bytes 1032200 | tf_op jit(solution)/shard_map/ppermute | solution.py:611
  65.2 6.9 %collective-permute-start.19 = (bf16[2,2,48,512]{3,2,1,0:T(8,128)(2,1)S(1)}, bf16[2,2,48,512]{3,2,1,0:T(8,128)(2,1)S(1)}, u32[]{:S(2)}, u32[]{:S(2)}) collective-permute-start(bf16[2,2,48,512]{3,2,1,0:T(8,128)(2,1)S(1)} %get-tuple-element.112), channel_id=1, source_target_pairs={{0,8},{8,0},{16,24},{24,16},{1,9},{9,1},{17,25},{25,17},{2,10},{10... | collective-permute-start | bytes 589832 | tf_op jit(solution)/shard_map/ppermute | solution.py:529
  72.3 6.2 %collective-permute-start.25 = (bf16[2,48,768]{2,1,0:T(8,128)(2,1)S(1)}, bf16[2,48,768]{2,1,0:T(8,128)(2,1)S(1)}, u32[]{:S(2)}, u32[]{:S(2)}) collective-permute-start(bf16[2,48,768]{2,1,0:T(8,128)(2,1)S(1)} %get-tuple-element.131), channel_id=1, source_target_pairs={{0,8},{8,0},{16,24},{24,16},{1,9},{9,1},{17,25},{25,17},{2,10},{10... | collective-permute-start | bytes 442376 | tf_op jit(solution)/shard_map/ppermute | solution.py:537
  73.8 4.6 %collective-permute-start.26 = (bf16[2,48,512]{2,1,0:T(8,128)(2,1)S(1)}, bf16[2,48,512]{2,1,0:T(8,128)(2,1)S(1)}, u32[]{:S(2)}, u32[]{:S(2)}) collective-permute-start(bf16[2,48,512]{2,1,0:T(8,128)(2,1)S(1)} %get-tuple-element.121), channel_id=1, source_target_pairs={{0,16},{8,24},{16,0},{24,8},{1,17},{9,25},{17,1},{25,9},{2,18},{10... | collective-permute-start | bytes 294920 | tf_op jit(solution)/shard_map/ppermute | solution.py:537
  75.0 14.1 %collective-permute-start.23 = (f32[48,896]{1,0:T(8,128)S(1)}, f32[48,896]{1,0:T(8,128)S(1)}, u32[]{:S(2)}, u32[]{:S(2)}) collective-permute-start(f32[48,896]{1,0:T(8,128)S(1)} %get-tuple-element.125), channel_id=1, source_target_pairs={{0,1},{1,0},{2,3},{3,2},{4,5},{5,4},{6,7},{7,6},{8,9},{9,8},{10,11... | collective-permute-start | bytes 516104 | tf_op jit(solution)/shard_map/ppermute | solution.py:565
  75.0 7.7 %collective-permute-start.22 = (bf16[48,896]{1,0:T(8,128)(2,1)S(1)}, bf16[48,896]{1,0:T(8,128)(2,1)S(1)}, u32[]{:S(2)}, u32[]{:S(2)}) collective-permute-start(bf16[48,896]{1,0:T(8,128)(2,1)S(1)} %get-tuple-element.124), channel_id=1, source_target_pairs={{0,4},{2,6},{4,0},{6,2},{1,5},{3,7},{5,1},{7,3},{8,12},{10,14},{12... | collective-permute-start | bytes 258056 | tf_op jit(solution)/shard_map/ppermute | solution.py:563
  79.1 12.6 %collective-permute-start.28 = (f32[24,1280]{1,0:T(8,128)S(1)}, f32[24,1280]{1,0:T(8,128)S(1)}, u32[]{:S(2)}, u32[]{:S(2)}) collective-permute-start(f32[24,1280]{1,0:T(8,128)S(1)} %get-tuple-element.135), channel_id=1, source_target_pairs={{0,1},{1,0},{2,3},{3,2},{4,5},{5,4},{6,7},{7,6},{8,9},{9,8},{10,11... | collective-permute-start | bytes 368648 | tf_op jit(solution)/shard_map/ppermute | solution.py:565
  79.1 9.9 %collective-permute-start.24 = (bf16[48,896]{1,0:T(8,128)(2,1)S(1)}, bf16[48,896]{1,0:T(8,128)(2,1)S(1)}, u32[]{:S(2)}, u32[]{:S(2)}) collective-permute-start(bf16[48,896]{1,0:T(8,128)(2,1)S(1)} %get-tuple-element.126), channel_id=1, source_target_pairs={{0,5},{1,4},{2,7},{3,6},{4,1},{5,0},{6,3},{7,2},{8,13},{9,12},{10,... | collective-permute-start | bytes 258056 | tf_op jit(solution)/shard_map/ppermute | solution.py:564
  79.7 10.8 %collective-permute-start.27 = (bf16[24,1280]{1,0:T(8,128)(2,1)S(1)}, bf16[24,1280]{1,0:T(8,128)(2,1)S(1)}, u32[]{:S(2)}, u32[]{:S(2)}) collective-permute-start(bf16[24,1280]{1,0:T(8,128)(2,1)S(1)} %get-tuple-element.134), channel_id=1, source_target_pairs={{0,4},{2,6},{4,0},{6,2},{1,5},{3,7},{5,1},{7,3},{8,12},{10,14},{12... | collective-permute-start | bytes 184328 | tf_op jit(solution)/shard_map/ppermute | solution.py:563
  82.7 9.0 %collective-permute-start.29 = (bf16[24,1280]{1,0:T(8,128)(2,1)S(1)}, bf16[24,1280]{1,0:T(8,128)(2,1)S(1)}, u32[]{:S(2)}, u32[]{:S(2)}) collective-permute-start(bf16[24,1280]{1,0:T(8,128)(2,1)S(1)} %get-tuple-element.136), channel_id=1, source_target_pairs={{0,5},{1,4},{2,7},{3,6},{4,1},{5,0},{6,3},{7,2},{8,13},{9,12},{10,... | collective-permute-start | bytes 184328 | tf_op jit(solution)/shard_map/ppermute | solution.py:564

commit v17 on v16

--- a/solution.py
+++ b/solution.py
@@ -11,7 +11,6 @@
 EPSILON = 1e-06
 SCALE = HEAD_DIM ** (-0.5)
 MASKED = -1e30
-PAIR = 2 * HEAD_DIM
 MIB = 1024 * 1024
 LITTLE = pl.CostEstimate(flops=1, bytes_accessed=1, transcendentals=0)
 MUCH = pl.CostEstimate(flops=40_000_000_000, bytes_accessed=1, transcendentals=0)
@@ -247,11 +246,10 @@
 
 
 def query_key_kernel(
-    scalars, normed_t, normed_far_t, dquery, dkey, dvalue, q_later, k_later, q_now, k_now, q_keep, k_keep
+    scalars, normed_t, normed_far_t, dquery, dkey, q_later, k_later, q_now, k_now, q_keep, k_keep
 ):
     by_quarters(scalars, (normed_t,), dquery[...], (q_now, q_later), q_keep, True)
-    right = jnp.concatenate((dkey[...], dvalue[:, :PAIR]), axis=1)
-    by_quarters(scalars, (normed_t, normed_far_t), right, (k_now, k_later), k_keep, False)
+    by_quarters(scalars, (normed_t, normed_far_t), dkey[...], (k_now, k_later), k_keep, False)
 
 
 def go_on_kernel(q_keep, q_got, k_keep, k_got, q_later, k_later):
@@ -264,7 +262,7 @@
     odd = lax.rem(scalars[1], jnp.int32(2)) == 1
     _, _, pairs, size, _ = send.shape
     half, quarter = upstream.shape[1] // 2, normed_t.shape[0] // 4
-    value_right = dvalue[:, PAIR:]
+    value_right = dvalue[...]
     lanes = value_right.shape[1]
     places = [(dy, dx, pair) for dy in range(2) for dx in range(2) for pair in range(pairs)]
     rows = {"send": ([], [], []), "keep": ([], [], [])}
@@ -376,26 +374,22 @@
         yield near[...] + far[...].astype(jnp.float32), core
 
 
-def place_query_key_kernel(scalars, mine, far_same, near_cross, far_cross, query, key, value):
+def place_query_key_kernel(scalars, mine, far_same, near_cross, far_cross, query, key):
     size = query.shape[1] // 2
     for total, core in last_sums(scalars, mine, far_same, near_cross, far_cross):
         columns = pl.ds(pl.multiple_of(core * size, size), size)
         query[:, columns] = total[:, :size]
-        key[:, columns] = total[:, size : 2 * size]
-        value[:, pl.ds(pl.multiple_of(core * PAIR, PAIR), PAIR)] = total[:, 2 * size :]
-
-
-def place_value_out_kernel(scalars, mine, far_same, near_cross, far_cross, first_pairs, value, out):
+        key[:, columns] = total[:, size:]
+
+
+def place_value_out_kernel(scalars, mine, far_same, near_cross, far_cross, value, out):
     size, width = mine.shape
     half, part = out.shape[1] // 2, value.shape[1] // 2
-    lanes = part - PAIR
-    for core in range(2):
-        value[:, core * part : core * part + PAIR] = first_pairs[:, core * PAIR : (core + 1) * PAIR]
     for total, core in last_sums(scalars, mine, far_same, near_cross, far_cross):
         out[:, pl.ds(pl.multiple_of(core * half, half), half)] = total[:, :half]
-        columns = pl.ds(pl.multiple_of(core * part + PAIR, PAIR), lanes)
-        value[:size, columns] = total[:, half : half + lanes]
-        value[size:, columns] = total[:, half + lanes :]
+        columns = pl.ds(pl.multiple_of(core * part, part), part)
+        value[:size, columns] = total[:, half : half + part]
+        value[size:, columns] = total[:, half + part :]
 
 
 def params(mebibytes):
@@ -565,8 +559,7 @@
         near_cross = lax.ppermute(near_cross, "row", swap)
         return mine, far_same, near_cross, far_cross
 
-    rest = part - PAIR
-    tile = (2 * o_rows, width // 2 + 2 * rest)
+    tile = (2 * o_rows, width // 2 + 2 * part)
     send, keep = call(
         value_out_kernel,
         [shape((2, 2, pairs, *tile), kind) for kind in (bf16, f32)],
@@ -576,12 +569,11 @@
         24,
     )
     got = lax.ppermute(send, "view", neighbours)
-    k_block = (q_size, part + PAIR)
     q_later, k_later, q_now, k_now, q_keep, k_keep = call(
         query_key_kernel,
-        [shape(block, bf16) for block in (q_block, k_block, q_block, k_block)]
-        + [shape((2, *block), f32) for block in (q_block, k_block)],
-        (scalars, normed_t, normed_far_t, after(dquery, send), dkey, dvalue),
+        [shape(block, bf16) for block in (q_block, q_block, q_block, q_block)]
+        + [shape((2, *block), f32) for block in (q_block, q_block)],
+        (scalars, normed_t, normed_far_t, after(dquery, send), dkey),
         "grad_query_key",
         SMEM,
         24,
@@ -589,35 +581,35 @@
     q_got, k_got = first_exchange((q_later, k_later))
     q_first, k_first = first_exchange((q_now, k_now))
     later = call(
-        go_on_kernel, [shape(q_block, bf16), shape(k_block, bf16)], (q_keep, q_got, k_keep, k_got), "first_sum_query_key"
+        go_on_kernel, [shape(q_block, bf16), shape(q_block, bf16)], (q_keep, q_got, k_keep, k_got), "first_sum_query_key"
     )
     q_second, k_second = second_exchange(later)
-    x_shape, y_shape = (2, pairs, 2 * o_rows, 2 * rest), (2, pairs, 2 * o_rows, width // 2)
+    qk_tile = (2 * q_rows, 2 * part)
+    qk_send, qk_keep = call(
+        query_key_tiles_kernel,
+        [shape((pairs, *qk_tile), kind) for kind in (bf16, f32)],
+        (scalars, q_keep, q_first, q_second, k_keep, k_first, k_second),
+        "second_sum_query_key",
+        SMEM,
+    )
+    qk_addends = (qk_keep, lax.ppermute(qk_send, "view", neighbours))
+    x_shape, y_shape = (2, pairs, 2 * o_rows, 2 * part), (2, pairs, 2 * o_rows, width // 2)
     vo_parts = call(
         view_sum_kernel,
         [shape(x_shape, bf16), shape(y_shape, bf16), shape(x_shape, f32), shape(y_shape, f32)],
-        (keep, after(got, later[0], q_first, k_first)),
+        (keep, after(got, qk_send)),
         "view_sum_value_out",
     )
     vo_got = first_exchange(vo_parts)
-    qk_tile = (2 * q_rows, 2 * part + PAIR)
-    qk_send, qk_keep = call(
-        query_key_tiles_kernel,
-        [shape((pairs, *qk_tile), kind) for kind in (bf16, f32)],
-        (scalars, after(q_keep, vo_parts[0]), q_first, q_second, k_keep, k_first, k_second),
-        "second_sum_query_key",
-        SMEM,
-    )
-    qk_addends = (qk_keep, lax.ppermute(qk_send, "view", neighbours))
-    vo_parts[2] = after(vo_parts[2], qk_send)
+    qk_last = last_parts(qk_addends, query_key_cores, "query_key")
+    vo_parts[2] = after(vo_parts[2], qk_last[0])
     vo_sums = first_sum(vo_parts, vo_got, "first_sum_value_out")
     v_got, o_got = second_exchange(vo_sums)
     addends = (vo_sums[3], o_got, vo_sums[2], v_got)
-    qk_last = last_parts((after(qk_addends[0], vo_sums[0]), qk_addends[1]), query_key_cores, "query_key")
-    vo_last = last_parts((after(addends[0], qk_last[0]), *addends[1:]), value_out_cores, "value_out")
-    grad_query, grad_key, first_pairs = call(
+    vo_last = last_parts((after(addends[0], qk_last[1], qk_last[3]), *addends[1:]), value_out_cores, "value_out")
+    grad_query, grad_key = call(
         place_query_key_kernel,
-        [shape((q_rows, inner), f32)] * 2 + [shape((q_rows, rows * PAIR), f32)],
+        [shape((q_rows, inner), f32)] * 2,
         (scalars, *qk_last),
         "last_sum_query_key",
         SMEM,
@@ -625,7 +617,7 @@
     grad_value, grad_out = call(
         place_value_out_kernel,
         [shape((q_rows, inner), f32), shape((o_rows, width), f32)],
-        (scalars, *vo_last, first_pairs),
+        (scalars, after(vo_last[0], grad_query), *vo_last[1:]),
         "last_sum_value_out",
         SMEM,
     )

time: 93.2 us -> 91.8 us (0.985)
  waiting for transfers between devices: 42.2 us -> 39.2 us
  starting transfers between devices: 29.6 us -> 31 us
    ppermute x3, waiting for transfers between devices: 24.3 us -> 10.1 us  [first_exchange(): lax.ppermute(sends[0], 'scene', along_x)]
    ppermute x2, waiting for transfers between devices: 0.69 us -> 9.49 us  [last_parts(): lax.ppermute(far_same, 'view', [(i, i ^ 2) for i in range(groups)])]
    ppermute x2, waiting for transfers between devices: 7.52 us -> 1.5 us  [last_parts(): lax.ppermute(far_cross, ('view', 'row'), [(i, i ^ 5) for i in range(targe...]
    ppermute x1, waiting for transfers between devices: 0.01 us -> 2.5 us  [shards(): qk_addends = (qk_keep, lax.ppermute(qk_send, 'view', neighbours))]
    ppermute x3, waiting for transfers between devices: 1.75 us -> 4.25 us  [first_exchange(): lax.ppermute(sends[1], 'scene', along_y)]
    ppermute x2, starting transfers between devices: 0.14 us -> 2.55 us  [last_parts(): near_cross = lax.ppermute(near_cross, 'row', swap)]
    ppermute x2, waiting for transfers between devices: 2.84 us -> 5.13 us  [second_exchange(): lax.ppermute(sums[0], 'scene', along_y)]
    ppermute x2, starting transfers between devices: 3.12 us -> 1.15 us  [second_exchange(): lax.ppermute(sums[1], 'scene', along_x)]
  transfers between devices with their start and end apart: 30 -> 30, of which waited for: 14 -> 18; matrix products, arithmetic and copies ran while one was open for 0% -> 0% of each run, Pallas kernels for 14% -> 14%
where the time goes in v17:
time: 91.8 us; the launch traced here: 91.6 us
  waiting for transfers between devices  39.2 us (43%)
  starting transfers between devices  31 us (34%)
  Pallas kernels  19.6 us (21%)
    pallas_call x11, Pallas kernels, call(): pl.pallas_call(kernel_body, in_specs=[first] + [VMEM] * (len(operands) -...  10.3 us
    ppermute x3, waiting for transfers between devices, first_exchange(): lax.ppermute(sends[0], 'scene', along_x)  10.1 us
    ppermute x2, waiting for transfers between devices, last_parts(): lax.ppermute(far_same, 'view', [(i, i ^ 2) for i in range(groups)])  9.49 us
    ppermute x3, starting transfers between devices, shards(): granted = [lax.ppermute(partners, 'view', pairs) for pairs in between]  5.62 us
    ppermute x2, waiting for transfers between devices, second_exchange(): lax.ppermute(sums[0], 'scene', along_y)  5.13 us
    ppermute x3, starting transfers between devices, shards(): lax.ppermute(part_out, 'view', pairs)  4.45 us
    ppermute x3, waiting for transfers between devices, first_exchange(): lax.ppermute(sends[1], 'scene', along_y)  4.25 us
    pallas_call x1, Pallas kernels, shards(): pl.pallas_call(project_kernel, in_specs=[SMEM] + [VMEM] * 10, out_specs=[...  4.13 us
  transfers between devices with their start and end apart: 30, of which 18 were waited for; matrix products, arithmetic and copies ran while one was open for 0% of the time, Pallas kernels for 14%

profile of v17, /device:TPU:0, one launch (start us, length us, event | category | flops | bytes accessed | tf_op | source)
XLA Modules:
  0.0 91.6 jit_solution(3619777649209948564)
XLA Ops:
  0.6 0.8 copy.13.partners
  1.4 3.0 %collective-permute-start.2 = (s32[1,4,3]{2,1,0:T(4,128)S(1)}, s32[1,4,3]{2,1,0:T(4,128)S(1)}, u32[]{:S(2)}, u32[]{:S(2)}) collective-permute-start(s32[1,4,3]{2,1,0:T(4,128)S(1)} %copy.13.partners), channel_id=1, source_target_pairs={{0,2},{2,0},{4,6},{6,4},{1,3},{3,1},{5,7},{7,5},{8,10},{10,8},{12,... | collective-permute-start | bytes 152 | tf_op jit(solution)/shard_map/ppermute | solution.py:430
  4.4 2.6 %collective-permute-start.1 = (s32[1,4,3]{2,1,0:T(4,128)S(1)}, s32[1,4,3]{2,1,0:T(4,128)S(1)}, u32[]{:S(2)}, u32[]{:S(2)}) collective-permute-start(s32[1,4,3]{2,1,0:T(4,128)S(1)} %copy.13.partners), channel_id=1, source_target_pairs={{0,4},{2,6},{4,0},{6,2},{1,5},{3,7},{5,1},{7,3},{8,12},{10,14},{12... | collective-permute-start | bytes 152 | tf_op jit(solution)/shard_map/ppermute | solution.py:430
  7.0 0.0 collective-permute-start
  7.0 0.5 collective-permute-start.7
  7.5 1.2 %alive.1 = s32[16]{0:T(128)S(1)} custom-call(s32[1,4,3]{2,1,0:T(4,128)S(1)} %copy.13.partners), custom_call_target="tpu_custom_call" | custom-call | flops 40000000000 | bytes 1 | tf_op jit(solution)/shard_map/alive/pallas_call | solution.py:420
  8.8 0.1 stack.23.scalars
  8.9 0.0 copy-start.5
  8.9 0.0 copy-start.6
  8.9 0.0 copy-start.7
  8.9 3.5 %collective-permute-done.refs_0_ = s32[1,4,3]{2,1,0:T(4,128)S(1)} collective-permute-done((s32[1,4,3]{2,1,0:T(4,128)S(1)}, s32[1,4,3]{2,1,0:T(4,128)S(1)}, u32[]{:S(2)}, u32[]{:S(2)}) %collective-permute-start) | collective-permute-done | bytes 80 | tf_op jit(solution)/shard_map/ppermute | solution.py:430
  12.4 0.8 pick.1
  13.2 0.4 collective-permute-start.3
  13.6 4.0 %collective-permute-start.5 = (bf16[32,1536]{1,0:T(8,128)(2,1)S(1)}, bf16[32,1536]{1,0:T(8,128)(2,1)S(1)}, u32[]{:S(2)}, u32[]{:S(2)}) collective-permute-start(bf16[32,1536]{1,0:T(8,128)(2,1)S(1)} %get-tuple-element.75), channel_id=1, source_target_pairs={{0,2},{2,0},{4,6},{6,4},{1,3},{3,1},{5,7},{7,5},{8,10},{10,8},{12,... | collective-permute-start | bytes 294920 | tf_op jit(solution)/shard_map/ppermute | solution.py:447
  17.7 4.1 %project.1 = (bf16[1536,256]{1,0:T(8,128)(2,1)S(1)}, bf16[256,384]{1,0:T(8,128)(2,1)S(1)}, bf16[256,384]{1,0:T(8,128)(2,1)S(1)}, bf16[256,1536]{1,0:T(8,128)(2,1...) custom-call(s32[5]{0:T(128)S(1)} %stack.23.scalars, ...), custom_call_target="tpu_custom_call" | custom-call | flops 1 | bytes 1 | tf_op jit(solution)/shard_map/project/pallas_call | solution.py:449
  21.9 0.4 collective-permute-done.4.refs_1_
  22.3 0.1 collective-permute-start.8
  22.4 0.4 collective-permute-start.9
  22.8 0.1 collective-permute-start.10
  22.9 0.7 collective-permute-done.8.refs_3_
  23.6 0.2 collective-permute-done.9.refs_4_
  23.7 0.4 collective-permute-done.10.refs_5_
  24.1 3.2 %attention_forward.1 = (bf16[1536,192]{1,0:T(8,128)(2,1)S(1)}, bf16[192,384]{1,0:T(8,128)(2,1)S(1)}, bf16[192,384]{1,0:T(8,128)(2,1)S(1)}, f32[3,64,512]{2,1,0:T...) custom-call(s32[5]{0:T(128)S(1)} %stack.23.scalars, ...), custom_call_target="tpu_custom_call" | custom-call | flops 1 | bytes 1 | tf_op jit(solution)/shard_map/attention_forward/pallas_call | solution.py:485
  27.3 0.2 collective-permute-start.11
  27.5 1.6 %attention_backward.1 = (bf16[256,384]{1,0:T(8,128)(2,1)S(1)}, bf16[448,384]{1,0:T(8,128)(2,1)S(1)}) custom-call(bf16[3,512,128]{2,1,0:T(8,128)(2,1)S(1)} %get-tuple-element.82.refs_6_.query_stack, bf16[3,512,128]{2,1,0:T(8,128)(2,1)S(1)} %get-tuple-element.83.refs_7_.grad_stack, f32[3,64,512]{2,1,0:T(8,128)S(1)} %get-tuple-element.87.dprob_own, ...), custom_call_target="tpu_custom_call" | custom-call | flops 1 | bytes 1 | tf_op jit(solution)/shard_map/attention_backward/pallas_call | solution.py:473
  29.1 1.8 %grad_value_out.1 = (bf16[2,2,2,48,1536]{4,3,2,1,0:T(8,128)(2,1)S(1)}, f32[2,2,2,48,1536]{4,3,2,1,0:T(8,128)S(1)}) custom-call(s32[5]{0:T(128)S(1)} %stack.23.scalars, bf16[1536,256]{1,0:T(8,128)(2,1)S(1)} %get-tuple-element.77.normed_t, bf16[1536,192]{1,0:T(8,128)(2,1)S(1)} %get-tuple-element.86.normed_far_t, ...), custom_call_target="tpu_custom_call" | custom-call | flops 1 | bytes 1 | tf_op jit(solution)/shard_map/grad_value_out/pallas_call | solution.py:473
  30.9 0.4 collective-permute-start.22
  31.3 1.9 %grad_query_key.1 = (bf16[384,384]{1,0:T(8,128)(2,1)S(1)}, bf16[384,384]{1,0:T(8,128)(2,1)S(1)}, bf16[384,384]{1,0:T(8,128)(2,1)S(1)}, bf16[384,384]{1,0:T(8,128...) custom-call(s32[5]{0:T(128)S(1)} %stack.23.scalars, ...), custom_call_target="tpu_custom_call" | custom-call | flops 1 | bytes 1 | tf_op jit(solution)/shard_map/grad_query_key/pallas_call | solution.py:473
  33.2 1.6 %collective-permute-start.13 = (bf16[384,384]{1,0:T(8,128)(2,1)S(1)}, bf16[384,384]{1,0:T(8,128)(2,1)S(1)}, u32[]{:S(2)}, u32[]{:S(2)}) collective-permute-start(bf16[384,384]{1,0:T(8,128)(2,1)S(1)} %get-tuple-element.103), channel_id=1, source_target_pairs={{0,8},{8,0},{16,24},{24,16},{1,9},{9,1},{17,25},{25,17},{2,10},{10... | collective-permute-start | bytes 884744 | tf_op jit(solution)/shard_map/ppermute | solution.py:523
  34.8 1.5 %collective-permute-start.14 = (bf16[384,384]{1,0:T(8,128)(2,1)S(1)}, bf16[384,384]{1,0:T(8,128)(2,1)S(1)}, u32[]{:S(2)}, u32[]{:S(2)}) collective-permute-start(bf16[384,384]{1,0:T(8,128)(2,1)S(1)} %get-tuple-element.105), channel_id=1, source_target_pairs={{0,16},{8,24},{16,0},{24,8},{1,17},{9,25},{17,1},{25,9},{2,18},{10... | collective-permute-start | bytes 884744 | tf_op jit(solution)/shard_map/ppermute | solution.py:523
  36.3 0.5 collective-permute-start.12
  36.8 0.5 collective-permute-start.16
  37.3 5.8 %collective-permute-done.13.q_got = bf16[384,384]{1,0:T(8,128)(2,1)S(1)} collective-permute-done((bf16[384,384]{1,0:T(8,128)(2,1)S(1)}, bf16[384,384]{1,0:T(8,128)(2,1)S(1)}, u32[]{:S(2)}, u32[]{:S(2)}) %collective-permute-start.13) | collective-permute-done | bytes 294944 | tf_op jit(solution)/shard_map/ppermute | solution.py:523
  43.2 1.5 %collective-permute-done.14.k_got = bf16[384,384]{1,0:T(8,128)(2,1)S(1)} collective-permute-done((bf16[384,384]{1,0:T(8,128)(2,1)S(1)}, bf16[384,384]{1,0:T(8,128)(2,1)S(1)}, u32[]{:S(2)}, u32[]{:S(2)}) %collective-permute-start.14) | collective-permute-done | bytes 294944 | tf_op jit(solution)/shard_map/ppermute | solution.py:523
  44.7 0.1 first_sum_query_key.1
  44.8 1.6 %collective-permute-start.15 = (bf16[384,384]{1,0:T(8,128)(2,1)S(1)}, bf16[384,384]{1,0:T(8,128)(2,1)S(1)}, u32[]{:S(2)}, u32[]{:S(2)}) collective-permute-start(bf16[384,384]{1,0:T(8,128)(2,1)S(1)} %get-tuple-element.106), channel_id=1, source_target_pairs={{0,16},{8,24},{16,0},{24,8},{1,17},{9,25},{17,1},{25,9},{2,18},{10... | collective-permute-start | bytes 884744 | tf_op jit(solution)/shard_map/ppermute | solution.py:531
  46.4 0.5 collective-permute-start.17
  46.9 2.6 %collective-permute-done.12.q_first = bf16[384,384]{1,0:T(8,128)(2,1)S(1)} collective-permute-done((bf16[384,384]{1,0:T(8,128)(2,1)S(1)}, bf16[384,384]{1,0:T(8,128)(2,1)S(1)}, u32[]{:S(2)}, u32[]{:S(2)}) %collective-permute-start.12) | collective-permute-done | bytes 294944 | tf_op jit(solution)/shard_map/ppermute | solution.py:523
  49.5 1.5 %collective-permute-done.16.k_first = bf16[384,384]{1,0:T(8,128)(2,1)S(1)} collective-permute-done((bf16[384,384]{1,0:T(8,128)(2,1)S(1)}, bf16[384,384]{1,0:T(8,128)(2,1)S(1)}, u32[]{:S(2)}, u32[]{:S(2)}) %collective-permute-start.16) | collective-permute-done | bytes 294944 | tf_op jit(solution)/shard_map/ppermute | solution.py:523
  51.0 5.1 %collective-permute-done.15.q_second = bf16[384,384]{1,0:T(8,128)(2,1)S(1)} collective-permute-done((bf16[384,384]{1,0:T(8,128)(2,1)S(1)}, bf16[384,384]{1,0:T(8,128)(2,1)S(1)}, u32[]{:S(2)}, u32[]{:S(2)}) %collective-permute-start.15) | collective-permute-done | bytes 294944 | tf_op jit(solution)/shard_map/ppermute | solution.py:531
  56.1 0.8 second_sum_query_key.1
  56.9 1.8 %collective-permute-start.18 = (bf16[2,96,768]{2,1,0:T(8,128)(2,1)S(1)}, bf16[2,96,768]{2,1,0:T(8,128)(2,1)S(1)}, u32[]{:S(2)}, u32[]{:S(2)}) collective-permute-start(bf16[2,96,768]{2,1,0:T(8,128)(2,1)S(1)} %get-tuple-element.110), channel_id=1, source_target_pairs={{0,2},{2,0},{4,6},{6,4},{1,3},{3,1},{5,7},{7,5},{8,10},{10,8},{12,... | collective-permute-start | bytes 884744 | tf_op jit(solution)/shard_map/ppermute | solution.py:595
  58.7 1.1 %collective-permute-done.22.got = bf16[2,2,2,48,1536]{4,3,2,1,0:T(8,128)(2,1)S(1)} collective-permute-done((bf16[2,2,2,48,1536]{4,3,2,1,0:T(8,128)(2,1)S(1)}, bf16[2,2,2,48,1536]{4,3,2,1,0:T(8,128)(2,1)S(1)}, u32[]{:S(2)}, u32[]{:S(2)}) %collective-permute-start.22) | collective-permute-done | bytes 1179680 | tf_op jit(solution)/shard_map/ppermute | solution.py:571
  59.8 0.2 view_sum_value_out.1
  60.0 1.6 %collective-permute-start.23 = (bf16[2,2,48,768]{3,2,1,0:T(8,128)(2,1)S(1)}, bf16[2,2,48,768]{3,2,1,0:T(8,128)(2,1)S(1)}, u32[]{:S(2)}, u32[]{:S(2)}) collective-permute-start(bf16[2,2,48,768]{3,2,1,0:T(8,128)(2,1)S(1)} %get-tuple-element.121), channel_id=1, source_target_pairs={{0,8},{8,0},{16,24},{24,16},{1,9},{9,1},{17,25},{25,17},{2,10},{10... | collective-permute-start | bytes 884744 | tf_op jit(solution)/shard_map/ppermute | solution.py:523
  61.5 1.5 %collective-permute-start.24 = (bf16[2,2,48,768]{3,2,1,0:T(8,128)(2,1)S(1)}, bf16[2,2,48,768]{3,2,1,0:T(8,128)(2,1)S(1)}, u32[]{:S(2)}, u32[]{:S(2)}) collective-permute-start(bf16[2,2,48,768]{3,2,1,0:T(8,128)(2,1)S(1)} %get-tuple-element.123), channel_id=1, source_target_pairs={{0,16},{8,24},{16,0},{24,8},{1,17},{9,25},{17,1},{25,9},{2,18},{10... | collective-permute-start | bytes 884744 | tf_op jit(solution)/shard_map/ppermute | solution.py:523
  63.0 2.5 %collective-permute-done.18.refs_1_ = bf16[2,96,768]{2,1,0:T(8,128)(2,1)S(1)} collective-permute-done((bf16[2,96,768]{2,1,0:T(8,128)(2,1)S(1)}, bf16[2,96,768]{2,1,0:T(8,128)(2,1)S(1)}, u32[]{:S(2)}, u32[]{:S(2)}) %collective-permute-start.18) | collective-permute-done | bytes 294944 | tf_op jit(solution)/shard_map/ppermute | solution.py:595
  65.5 0.6 last_parts_query_key.1
  66.2 1.8 %collective-permute-done.23.x_got = bf16[2,2,48,768]{3,2,1,0:T(8,128)(2,1)S(1)} collective-permute-done((bf16[2,2,48,768]{3,2,1,0:T(8,128)(2,1)S(1)}, bf16[2,2,48,768]{3,2,1,0:T(8,128)(2,1)S(1)}, u32[]{:S(2)}, u32[]{:S(2)}) %collective-permute-start.23) | collective-permute-done | bytes 294944 | tf_op jit(solution)/shard_map/ppermute | solution.py:523
  67.9 1.2 %collective-permute-done.24.y_got = bf16[2,2,48,768]{3,2,1,0:T(8,128)(2,1)S(1)} collective-permute-done((bf16[2,2,48,768]{3,2,1,0:T(8,128)(2,1)S(1)}, bf16[2,2,48,768]{3,2,1,0:T(8,128)(2,1)S(1)}, u32[]{:S(2)}, u32[]{:S(2)}) %collective-permute-start.24) | collective-permute-done | bytes 294944 | tf_op jit(solution)/shard_map/ppermute | solution.py:523
  69.1 0.1 first_sum_value_out.1
  69.3 0.6 collective-permute-start.25
  69.9 1.5 %collective-permute-start.26 = (bf16[2,48,768]{2,1,0:T(8,128)(2,1)S(1)}, bf16[2,48,768]{2,1,0:T(8,128)(2,1)S(1)}, u32[]{:S(2)}, u32[]{:S(2)}) collective-permute-start(bf16[2,48,768]{2,1,0:T(8,128)(2,1)S(1)} %get-tuple-element.128), channel_id=1, source_target_pairs={{0,16},{8,24},{16,0},{24,8},{1,17},{9,25},{17,1},{25,9},{2,18},{10... | collective-permute-start | bytes 442376 | tf_op jit(solution)/shard_map/ppermute | solution.py:531
  71.4 1.1 %collective-permute-start.19 = (bf16[48,768]{1,0:T(8,128)(2,1)S(1)}, bf16[48,768]{1,0:T(8,128)(2,1)S(1)}, u32[]{:S(2)}, u32[]{:S(2)}) collective-permute-start(bf16[48,768]{1,0:T(8,128)(2,1)S(1)} %get-tuple-element.112), channel_id=1, source_target_pairs={{0,4},{2,6},{4,0},{6,2},{1,5},{3,7},{5,1},{7,3},{8,12},{10,14},{12... | collective-permute-start | bytes 221192 | tf_op jit(solution)/shard_map/ppermute | solution.py:557
  72.5 1.9 %collective-permute-start.20 = (f32[48,768]{1,0:T(8,128)S(1)}, f32[48,768]{1,0:T(8,128)S(1)}, u32[]{:S(2)}, u32[]{:S(2)}) collective-permute-start(f32[48,768]{1,0:T(8,128)S(1)} %get-tuple-element.113), channel_id=1, source_target_pairs={{0,1},{1,0},{2,3},{3,2},{4,5},{5,4},{6,7},{7,6},{8,9},{9,8},{10,11... | collective-permute-start | bytes 442376 | tf_op jit(solution)/shard_map/ppermute | solution.py:559
  74.4 5.1 %collective-permute-done.19.far_same = bf16[48,768]{1,0:T(8,128)(2,1)S(1)} collective-permute-done((bf16[48,768]{1,0:T(8,128)(2,1)S(1)}, bf16[48,768]{1,0:T(8,128)(2,1)S(1)}, u32[]{:S(2)}, u32[]{:S(2)}) %collective-permute-start.19) | collective-permute-done | bytes 73760 | tf_op jit(solution)/shard_map/ppermute | solution.py:557
  79.5 0.1 collective-permute-done.21.far_cross
  79.6 0.6 last_parts_value_out.1
  80.2 0.6 collective-permute-start.28
  80.9 2.3 %collective-permute-start.29 = (bf16[24,1536]{1,0:T(8,128)(2,1)S(1)}, bf16[24,1536]{1,0:T(8,128)(2,1)S(1)}, u32[]{:S(2)}, u32[]{:S(2)}) collective-permute-start(bf16[24,1536]{1,0:T(8,128)(2,1)S(1)} %get-tuple-element.133), channel_id=1, source_target_pairs={{0,5},{1,4},{2,7},{3,6},{4,1},{5,0},{6,3},{7,2},{8,13},{9,12},{10,... | collective-permute-start | bytes 221192 | tf_op jit(solution)/shard_map/ppermute | solution.py:558
  83.2 1.3 %last_sum_query_key.1 = (f32[48,768]{1,0:T(8,128)}, f32[48,768]{1,0:T(8,128)}) custom-call(s32[5]{0:T(128)S(1)} %stack.23.scalars, f32[48,768]{1,0:T(8,128)S(1)} %get-tuple-element.111.mine, bf16[48,768]{1,0:T(8,128)(2,1)S(1)} %collective-permute-done.19.far_same, f32[48,768]{1,0:T(8,128)S(1)} %collective-permute-done.20.near_cross, ...), custom_call_target="tpu_custom_call" | custom-call | flops 1 | bytes 1 | tf_op jit(solution)/shard_map/last_sum_query_key/pallas_call | solution.py:473
  84.5 4.4 %collective-permute-done.27.far_same = bf16[24,1536]{1,0:T(8,128)(2,1)S(1)} collective-permute-done((bf16[24,1536]{1,0:T(8,128)(2,1)S(1)}, bf16[24,1536]{1,0:T(8,128)(2,1)S(1)}, u32[]{:S(2)}, u32[]{:S(2)}) %collective-permute-start.27) | collective-permute-done | bytes 73760 | tf_op jit(solution)/shard_map/ppermute | solution.py:557
  88.9 1.4 %collective-permute-done.29.far_cross = bf16[24,1536]{1,0:T(8,128)(2,1)S(1)} collective-permute-done((bf16[24,1536]{1,0:T(8,128)(2,1)S(1)}, bf16[24,1536]{1,0:T(8,128)(2,1)S(1)}, u32[]{:S(2)}, u32[]{:S(2)}) %collective-permute-start.29) | collective-permute-done | bytes 73760 | tf_op jit(solution)/shard_map/ppermute | solution.py:558
  90.3 1.3 %last_sum_value_out.1 = (f32[48,768]{1,0:T(8,128)}, f32[24,1536]{1,0:T(8,128)}) custom-call(s32[5]{0:T(128)S(1)} %stack.23.scalars, f32[24,1536]{1,0:T(8,128)S(1)} %get-tuple-element.130.mine, bf16[24,1536]{1,0:T(8,128)(2,1)S(1)} %collective-permute-done.27.far_same, f32[24,1536]{1,0:T(8,128)S(1)} %collective-permute-done.28.near_cross, ...), custom_call_target="tpu_custom_call" | custom-call | flops 1 | bytes 1 | tf_op jit(solution)/shard_map/last_sum_value_out/pallas_call | solution.py:473
  (29 shorter events, 0.1 us)
Async XLA Ops:
  1.4 7.5 %collective-permute-start.2 = (s32[1,4,3]{2,1,0:T(4,128)S(1)}, s32[1,4,3]{2,1,0:T(4,128)S(1)}, u32[]{:S(2)}, u32[]{:S(2)}) collective-permute-start(s32[1,4,3]{2,1,0:T(4,128)S(1)} %copy.13.partners), channel_id=1, source_target_pairs={{0,2},{2,0},{4,6},{6,4},{1,3},{3,1},{5,7},{7,5},{8,10},{10,8},{12,... | collective-permute-start | bytes 152 | tf_op jit(solution)/shard_map/ppermute | solution.py:430
  4.4 4.5 %collective-permute-start.1 = (s32[1,4,3]{2,1,0:T(4,128)S(1)}, s32[1,4,3]{2,1,0:T(4,128)S(1)}, u32[]{:S(2)}, u32[]{:S(2)}) collective-permute-start(s32[1,4,3]{2,1,0:T(4,128)S(1)} %copy.13.partners), channel_id=1, source_target_pairs={{0,4},{2,6},{4,0},{6,2},{1,5},{3,7},{5,1},{7,3},{8,12},{10,14},{12... | collective-permute-start | bytes 152 | tf_op jit(solution)/shard_map/ppermute | solution.py:430
  7.0 5.4 %collective-permute-start = (s32[1,4,3]{2,1,0:T(4,128)S(1)}, s32[1,4,3]{2,1,0:T(4,128)S(1)}, u32[]{:S(2)}, u32[]{:S(2)}) collective-permute-start(s32[1,4,3]{2,1,0:T(4,128)S(1)} %copy.13.partners), channel_id=1, source_target_pairs={{0,6},{2,4},{4,2},{6,0},{1,7},{3,5},{5,3},{7,1},{8,14},{10,12},{12... | collective-permute-start | bytes 152 | tf_op jit(solution)/shard_map/ppermute | solution.py:430
  7.0 10.6 %collective-permute-start.6 = (bf16[4,32,1536]{2,1,0:T(8,128)(2,1)}, bf16[4,32,1536]{2,1,0:T(8,128)(2,1)S(1)}, u32[]{:S(2)}, u32[]{:S(2)}) collective-permute-start(bf16[4,32,1536]{2,1,0:T(8,128)(2,1)} %bitcast.7), channel_id=1, source_target_pairs={{0,1},{1,0},{2,3},{3,2},{4,5},{5,4},{6,7},{7,6},{8,9},{9,8},{10,11... | collective-permute-start | bytes 1179656 | tf_op jit(solution)/shard_map/ppermute | solution.py:435
  7.0 10.6 %collective-permute-start.7 = (bf16[4,32,1536]{2,1,0:T(8,128)(2,1)}, bf16[4,32,1536]{2,1,0:T(8,128)(2,1)S(1)}, u32[]{:S(2)}, u32[]{:S(2)}) collective-permute-start(bf16[4,32,1536]{2,1,0:T(8,128)(2,1)} %bitcast.10), channel_id=1, source_target_pairs={{0,1},{1,0},{2,3},{3,2},{4,5},{5,4},{6,7},{7,6},{8,9},{9,8},{10,11... | collective-permute-start | bytes 1179656 | tf_op jit(solution)/shard_map/ppermute | solution.py:436
  7.5 4.9 %copy-start.4 = (bf16[1,4,1,32,1536]{4,3,2,1,0:T(8,128)(2,1)S(1)}, bf16[1,4,1,32,1536]{4,3,2,1,0:T(8,128)(2,1)}, u32[]{:S(2)}) copy-start(bf16[1,4,1,32,1536]{4,3,2,1,0:T(8,128)(2,1)} %param.10) | copy-start | bytes 1179652
  8.8 8.8 %copy-start = (bf16[1536,768]{1,0:T(8,128)(2,1)S(1)}, bf16[1536,768]{1,0:T(8,128)(2,1)}, u32[]{:S(2)}) copy-start(bf16[1536,768]{1,0:T(8,128)(2,1)} %refs_11_.1) | copy-start | bytes 7077892
  8.9 8.8 %copy-start.1 = (bf16[1536,768]{1,0:T(8,128)(2,1)S(1)}, bf16[1536,768]{1,0:T(8,128)(2,1)}, u32[]{:S(2)}) copy-start(bf16[1536,768]{1,0:T(8,128)(2,1)} %refs_12_.1) | copy-start | bytes 7077892
  8.9 8.8 %copy-start.2 = (bf16[1536,768]{1,0:T(8,128)(2,1)S(1)}, bf16[1536,768]{1,0:T(8,128)(2,1)}, u32[]{:S(2)}) copy-start(bf16[1536,768]{1,0:T(8,128)(2,1)} %w_query.1) | copy-start | bytes 7077892
  8.9 8.8 %copy-start.3 = (bf16[768,1536]{1,0:T(8,128)(2,1)S(1)}, bf16[768,1536]{1,0:T(8,128)(2,1)}, u32[]{:S(2)}) copy-start(bf16[768,1536]{1,0:T(8,128)(2,1)} %w_out.1) | copy-start | bytes 7077892
  8.9 8.8 %copy-start.5 = (bf16[1,4,1,32,1536]{4,3,2,1,0:T(8,128)(2,1)S(1)}, bf16[1,4,1,32,1536]{4,3,2,1,0:T(8,128)(2,1)}, u32[]{:S(2)}) copy-start(bf16[1,4,1,32,1536]{4,3,2,1,0:T(8,128)(2,1)} %param.18) | copy-start | bytes 1179652
  8.9 8.8 %copy-start.6 = (bf16[9,1536]{1,0:T(8,128)(2,1)S(1)}, bf16[9,1536]{1,0:T(8,128)(2,1)}, u32[]{:S(2)}) copy-start(bf16[9,1536]{1,0:T(8,128)(2,1)} %taps.1) | copy-start | bytes 82948
  8.9 8.8 %copy-start.7 = (f32[1536]{0:T(1024)S(1)}, f32[1536]{0:T(1024)}, u32[]{:S(2)}) copy-start(f32[1536]{0:T(1024)} %refs_10_.1) | copy-start | bytes 18436
  13.2 8.7 %collective-permute-start.3 = (bf16[32,1536]{1,0:T(8,128)(2,1)S(1)}, bf16[32,1536]{1,0:T(8,128)(2,1)S(1)}, u32[]{:S(2)}, u32[]{:S(2)}) collective-permute-start(bf16[32,1536]{1,0:T(8,128)(2,1)S(1)} %get-tuple-element.73), channel_id=1, source_target_pairs={{0,6},{2,4},{4,2},{6,0},{1,7},{3,5},{5,3},{7,1},{8,14},{10,12},{12... | collective-permute-start | bytes 294920 | tf_op jit(solution)/shard_map/ppermute | solution.py:447
  13.6 8.7 %collective-permute-start.4 = (bf16[32,1536]{1,0:T(8,128)(2,1)S(1)}, bf16[32,1536]{1,0:T(8,128)(2,1)S(1)}, u32[]{:S(2)}, u32[]{:S(2)}) collective-permute-start(bf16[32,1536]{1,0:T(8,128)(2,1)S(1)} %get-tuple-element.74), channel_id=1, source_target_pairs={{0,4},{2,6},{4,0},{6,2},{1,5},{3,7},{5,1},{7,3},{8,12},{10,14},{12... | collective-permute-start | bytes 294920 | tf_op jit(solution)/shard_map/ppermute | solution.py:447
  13.6 8.7 %collective-permute-start.5 = (bf16[32,1536]{1,0:T(8,128)(2,1)S(1)}, bf16[32,1536]{1,0:T(8,128)(2,1)S(1)}, u32[]{:S(2)}, u32[]{:S(2)}) collective-permute-start(bf16[32,1536]{1,0:T(8,128)(2,1)S(1)} %get-tuple-element.75), channel_id=1, source_target_pairs={{0,2},{2,0},{4,6},{6,4},{1,3},{3,1},{5,7},{7,5},{8,10},{10,8},{12,... | collective-permute-start | bytes 294920 | tf_op jit(solution)/shard_map/ppermute | solution.py:447
  22.3 1.3 %collective-permute-start.8 = (bf16[32,1536]{1,0:T(8,128)(2,1)S(1)}, bf16[32,1536]{1,0:T(8,128)(2,1)S(1)}, u32[]{:S(2)}, u32[]{:S(2)}) collective-permute-start(bf16[32,1536]{1,0:T(8,128)(2,1)S(1)} %collective-permute-done.3.refs_0_), channel_id=1, source_target_pairs={{0,1},{1,0},{2,3},{3,2},{4,5},{5,4},{6,7},{7,6},{8,9},{9,8},{10,11... | collective-permute-start | bytes 294920 | tf_op jit(solution)/shard_map/ppermute | solution.py:470
  22.4 1.4 %collective-permute-start.9 = (bf16[32,1536]{1,0:T(8,128)(2,1)S(1)}, bf16[32,1536]{1,0:T(8,128)(2,1)S(1)}, u32[]{:S(2)}, u32[]{:S(2)}) collective-permute-start(bf16[32,1536]{1,0:T(8,128)(2,1)S(1)} %collective-permute-done.4.refs_1_), channel_id=1, source_target_pairs={{0,1},{1,0},{2,3},{3,2},{4,5},{5,4},{6,7},{7,6},{8,9},{9,8},{10,11... | collective-permute-start | bytes 294920 | tf_op jit(solution)/shard_map/ppermute | solution.py:470
  22.8 1.3 %collective-permute-start.10 = (bf16[32,1536]{1,0:T(8,128)(2,1)S(1)}, bf16[32,1536]{1,0:T(8,128)(2,1)S(1)}, u32[]{:S(2)}, u32[]{:S(2)}) collective-permute-start(bf16[32,1536]{1,0:T(8,128)(2,1)S(1)} %collective-permute-done.5.refs_2_), channel_id=1, source_target_pairs={{0,1},{1,0},{2,3},{3,2},{4,5},{5,4},{6,7},{7,6},{8,9},{9,8},{10,11... | collective-permute-start | bytes 294920 | tf_op jit(solution)/shard_map/ppermute | solution.py:470
  27.3 1.8 %collective-permute-start.11 = (bf16[384,256]{1,0:T(8,128)(2,1)S(1)}, bf16[384,256]{1,0:T(8,128)(2,1)S(1)}, u32[]{:S(2)}, u32[]{:S(2)}) collective-permute-start(bf16[384,256]{1,0:T(8,128)(2,1)S(1)} %get-tuple-element.97.mine), channel_id=1, source_target_pairs={{0,1},{1,0},{2,3},{3,2},{4,5},{5,4},{6,7},{7,6},{8,9},{9,8},{10,11... | collective-permute-start | bytes 589832 | tf_op jit(solution)/shard_map/ppermute | solution.py:505
  30.9 28.9 %collective-permute-start.22 = (bf16[2,2,2,48,1536]{4,3,2,1,0:T(8,128)(2,1)S(1)}, bf16[2,2,2,48,1536]{4,3,2,1,0:T(8,128)(2,1)S(1)}, u32[]{:S(2)}, u32[]{:S(2)}) collective-permute-start(bf16[2,2,2,48,1536]{4,3,2,1,0:T(8,128)(2,1)S(1)} %get-tuple-element.99), channel_id=1, source_target_pairs={{0,2},{2,0},{4,6},{6,4},{1,3},{3,1},{5,7},{7,5},{8,10},{10,8},{12,... | collective-permute-start | bytes 3538952 | tf_op jit(solution)/shard_map/ppermute | solution.py:571
  33.2 9.9 %collective-permute-start.13 = (bf16[384,384]{1,0:T(8,128)(2,1)S(1)}, bf16[384,384]{1,0:T(8,128)(2,1)S(1)}, u32[]{:S(2)}, u32[]{:S(2)}) collective-permute-start(bf16[384,384]{1,0:T(8,128)(2,1)S(1)} %get-tuple-element.103), channel_id=1, source_target_pairs={{0,8},{8,0},{16,24},{24,16},{1,9},{9,1},{17,25},{25,17},{2,10},{10... | collective-permute-start | bytes 884744 | tf_op jit(solution)/shard_map/ppermute | solution.py:523
  34.8 9.9 %collective-permute-start.14 = (bf16[384,384]{1,0:T(8,128)(2,1)S(1)}, bf16[384,384]{1,0:T(8,128)(2,1)S(1)}, u32[]{:S(2)}, u32[]{:S(2)}) collective-permute-start(bf16[384,384]{1,0:T(8,128)(2,1)S(1)} %get-tuple-element.105), channel_id=1, source_target_pairs={{0,16},{8,24},{16,0},{24,8},{1,17},{9,25},{17,1},{25,9},{2,18},{10... | collective-permute-start | bytes 884744 | tf_op jit(solution)/shard_map/ppermute | solution.py:523
  36.3 13.2 %collective-permute-start.12 = (bf16[384,384]{1,0:T(8,128)(2,1)S(1)}, bf16[384,384]{1,0:T(8,128)(2,1)S(1)}, u32[]{:S(2)}, u32[]{:S(2)}) collective-permute-start(bf16[384,384]{1,0:T(8,128)(2,1)S(1)} %get-tuple-element.102), channel_id=1, source_target_pairs={{0,8},{8,0},{16,24},{24,16},{1,9},{9,1},{17,25},{25,17},{2,10},{10... | collective-permute-start | bytes 884744 | tf_op jit(solution)/shard_map/ppermute | solution.py:523
  36.8 14.2 %collective-permute-start.16 = (bf16[384,384]{1,0:T(8,128)(2,1)S(1)}, bf16[384,384]{1,0:T(8,128)(2,1)S(1)}, u32[]{:S(2)}, u32[]{:S(2)}) collective-permute-start(bf16[384,384]{1,0:T(8,128)(2,1)S(1)} %get-tuple-element.107), channel_id=1, source_target_pairs={{0,16},{8,24},{16,0},{24,8},{1,17},{9,25},{17,1},{25,9},{2,18},{10... | collective-permute-start | bytes 884744 | tf_op jit(solution)/shard_map/ppermute | solution.py:523
  44.8 11.3 %collective-permute-start.15 = (bf16[384,384]{1,0:T(8,128)(2,1)S(1)}, bf16[384,384]{1,0:T(8,128)(2,1)S(1)}, u32[]{:S(2)}, u32[]{:S(2)}) collective-permute-start(bf16[384,384]{1,0:T(8,128)(2,1)S(1)} %get-tuple-element.106), channel_id=1, source_target_pairs={{0,16},{8,24},{16,0},{24,8},{1,17},{9,25},{17,1},{25,9},{2,18},{10... | collective-permute-start | bytes 884744 | tf_op jit(solution)/shard_map/ppermute | solution.py:531
  46.4 9.8 %collective-permute-start.17 = (bf16[384,384]{1,0:T(8,128)(2,1)S(1)}, bf16[384,384]{1,0:T(8,128)(2,1)S(1)}, u32[]{:S(2)}, u32[]{:S(2)}) collective-permute-start(bf16[384,384]{1,0:T(8,128)(2,1)S(1)} %get-tuple-element.108), channel_id=1, source_target_pairs={{0,8},{8,0},{16,24},{24,16},{1,9},{9,1},{17,25},{25,17},{2,10},{10... | collective-permute-start | bytes 884744 | tf_op jit(solution)/shard_map/ppermute | solution.py:531
  56.9 8.6 %collective-permute-start.18 = (bf16[2,96,768]{2,1,0:T(8,128)(2,1)S(1)}, bf16[2,96,768]{2,1,0:T(8,128)(2,1)S(1)}, u32[]{:S(2)}, u32[]{:S(2)}) collective-permute-start(bf16[2,96,768]{2,1,0:T(8,128)(2,1)S(1)} %get-tuple-element.110), channel_id=1, source_target_pairs={{0,2},{2,0},{4,6},{6,4},{1,3},{3,1},{5,7},{7,5},{8,10},{10,8},{12,... | collective-permute-start | bytes 884744 | tf_op jit(solution)/shard_map/ppermute | solution.py:595
  60.0 8.0 %collective-permute-start.23 = (bf16[2,2,48,768]{3,2,1,0:T(8,128)(2,1)S(1)}, bf16[2,2,48,768]{3,2,1,0:T(8,128)(2,1)S(1)}, u32[]{:S(2)}, u32[]{:S(2)}) collective-permute-start(bf16[2,2,48,768]{3,2,1,0:T(8,128)(2,1)S(1)} %get-tuple-element.121), channel_id=1, source_target_pairs={{0,8},{8,0},{16,24},{24,16},{1,9},{9,1},{17,25},{25,17},{2,10},{10... | collective-permute-start | bytes 884744 | tf_op jit(solution)/shard_map/ppermute | solution.py:523
  61.5 7.6 %collective-permute-start.24 = (bf16[2,2,48,768]{3,2,1,0:T(8,128)(2,1)S(1)}, bf16[2,2,48,768]{3,2,1,0:T(8,128)(2,1)S(1)}, u32[]{:S(2)}, u32[]{:S(2)}) collective-permute-start(bf16[2,2,48,768]{3,2,1,0:T(8,128)(2,1)S(1)} %get-tuple-element.123), channel_id=1, source_target_pairs={{0,16},{8,24},{16,0},{24,8},{1,17},{9,25},{17,1},{25,9},{2,18},{10... | collective-permute-start | bytes 884744 | tf_op jit(solution)/shard_map/ppermute | solution.py:523
  69.3 10.3 %collective-permute-start.25 = (bf16[2,48,768]{2,1,0:T(8,128)(2,1)S(1)}, bf16[2,48,768]{2,1,0:T(8,128)(2,1)S(1)}, u32[]{:S(2)}, u32[]{:S(2)}) collective-permute-start(bf16[2,48,768]{2,1,0:T(8,128)(2,1)S(1)} %get-tuple-element.126), channel_id=1, source_target_pairs={{0,8},{8,0},{16,24},{24,16},{1,9},{9,1},{17,25},{25,17},{2,10},{10... | collective-permute-start | bytes 442376 | tf_op jit(solution)/shard_map/ppermute | solution.py:531
  69.9 9.7 %collective-permute-start.26 = (bf16[2,48,768]{2,1,0:T(8,128)(2,1)S(1)}, bf16[2,48,768]{2,1,0:T(8,128)(2,1)S(1)}, u32[]{:S(2)}, u32[]{:S(2)}) collective-permute-start(bf16[2,48,768]{2,1,0:T(8,128)(2,1)S(1)} %get-tuple-element.128), channel_id=1, source_target_pairs={{0,16},{8,24},{16,0},{24,8},{1,17},{9,25},{17,1},{25,9},{2,18},{10... | collective-permute-start | bytes 442376 | tf_op jit(solution)/shard_map/ppermute | solution.py:531
  71.4 8.1 %collective-permute-start.19 = (bf16[48,768]{1,0:T(8,128)(2,1)S(1)}, bf16[48,768]{1,0:T(8,128)(2,1)S(1)}, u32[]{:S(2)}, u32[]{:S(2)}) collective-permute-start(bf16[48,768]{1,0:T(8,128)(2,1)S(1)} %get-tuple-element.112), channel_id=1, source_target_pairs={{0,4},{2,6},{4,0},{6,2},{1,5},{3,7},{5,1},{7,3},{8,12},{10,14},{12... | collective-permute-start | bytes 221192 | tf_op jit(solution)/shard_map/ppermute | solution.py:557
  72.5 7.1 %collective-permute-start.21 = (bf16[48,768]{1,0:T(8,128)(2,1)S(1)}, bf16[48,768]{1,0:T(8,128)(2,1)S(1)}, u32[]{:S(2)}, u32[]{:S(2)}) collective-permute-start(bf16[48,768]{1,0:T(8,128)(2,1)S(1)} %get-tuple-element.114), channel_id=1, source_target_pairs={{0,5},{1,4},{2,7},{3,6},{4,1},{5,0},{6,3},{7,2},{8,13},{9,12},{10,... | collective-permute-start | bytes 221192 | tf_op jit(solution)/shard_map/ppermute | solution.py:558
  72.5 10.7 %collective-permute-start.20 = (f32[48,768]{1,0:T(8,128)S(1)}, f32[48,768]{1,0:T(8,128)S(1)}, u32[]{:S(2)}, u32[]{:S(2)}) collective-permute-start(f32[48,768]{1,0:T(8,128)S(1)} %get-tuple-element.113), channel_id=1, source_target_pairs={{0,1},{1,0},{2,3},{3,2},{4,5},{5,4},{6,7},{7,6},{8,9},{9,8},{10,11... | collective-permute-start | bytes 442376 | tf_op jit(solution)/shard_map/ppermute | solution.py:559
  80.2 10.1 %collective-permute-start.28 = (f32[24,1536]{1,0:T(8,128)S(1)}, f32[24,1536]{1,0:T(8,128)S(1)}, u32[]{:S(2)}, u32[]{:S(2)}) collective-permute-start(f32[24,1536]{1,0:T(8,128)S(1)} %get-tuple-element.132), channel_id=1, source_target_pairs={{0,1},{1,0},{2,3},{3,2},{4,5},{5,4},{6,7},{7,6},{8,9},{9,8},{10,11... | collective-permute-start | bytes 442376 | tf_op jit(solution)/shard_map/ppermute | solution.py:559
  80.9 8.0 %collective-permute-start.27 = (bf16[24,1536]{1,0:T(8,128)(2,1)S(1)}, bf16[24,1536]{1,0:T(8,128)(2,1)S(1)}, u32[]{:S(2)}, u32[]{:S(2)}) collective-permute-start(bf16[24,1536]{1,0:T(8,128)(2,1)S(1)} %get-tuple-element.131), channel_id=1, source_target_pairs={{0,4},{2,6},{4,0},{6,2},{1,5},{3,7},{5,1},{7,3},{8,12},{10,14},{12... | collective-permute-start | bytes 221192 | tf_op jit(solution)/shard_map/ppermute | solution.py:557
  80.9 9.4 %collective-permute-start.29 = (bf16[24,1536]{1,0:T(8,128)(2,1)S(1)}, bf16[24,1536]{1,0:T(8,128)(2,1)S(1)}, u32[]{:S(2)}, u32[]{:S(2)}) collective-permute-start(bf16[24,1536]{1,0:T(8,128)(2,1)S(1)} %get-tuple-element.133), channel_id=1, source_target_pairs={{0,5},{1,4},{2,7},{3,6},{4,1},{5,0},{6,3},{7,2},{8,13},{9,12},{10,... | collective-permute-start | bytes 221192 | tf_op jit(solution)/shard_map/ppermute | solution.py:558

commit v18 on v17

--- a/solution.py
+++ b/solution.py
@@ -606,18 +606,19 @@
     vo_sums = first_sum(vo_parts, vo_got, "first_sum_value_out")
     v_got, o_got = second_exchange(vo_sums)
     addends = (vo_sums[3], o_got, vo_sums[2], v_got)
-    vo_last = last_parts((after(addends[0], qk_last[1], qk_last[3]), *addends[1:]), value_out_cores, "value_out")
     grad_query, grad_key = call(
         place_query_key_kernel,
         [shape((q_rows, inner), f32)] * 2,
         (scalars, *qk_last),
         "last_sum_query_key",
         SMEM,
-    )
+        cost=MUCH,
+    )
+    vo_last = last_parts((after(addends[0], grad_query), *addends[1:]), value_out_cores, "value_out")
     grad_value, grad_out = call(
         place_value_out_kernel,
         [shape((q_rows, inner), f32), shape((o_rows, width), f32)],
-        (scalars, after(vo_last[0], grad_query), *vo_last[1:]),
+        (scalars, *vo_last),
         "last_sum_value_out",
         SMEM,
     )

time: 91.8 us -> 89.3 us (0.973)
  waiting for transfers between devices: 39.2 us -> 36.2 us
    ppermute x2, starting transfers between devices: 2.55 us -> 0.4 us  [last_parts(): near_cross = lax.ppermute(near_cross, 'row', swap)]
    ppermute x3, waiting for transfers between devices: 10.1 us -> 8.38 us  [first_exchange(): lax.ppermute(sends[0], 'scene', along_x)]
    ppermute x2, starting transfers between devices: 2.33 us -> 3.61 us  [last_parts(): lax.ppermute(far_cross, ('view', 'row'), [(i, i ^ 5) for i in range(targe...]
    ppermute x3, waiting for transfers between devices: 4.25 us -> 3.17 us  [first_exchange(): lax.ppermute(sends[1], 'scene', along_y)]
  transfers between devices with their start and end apart: 30 -> 30, of which waited for: 18 -> 17; matrix products, arithmetic and copies ran while one was open for 0% -> 0% of each run, Pallas kernels for 14% -> 14%
where the time goes in v18:
time: 89.3 us; the launch traced here: 89.1 us
  waiting for transfers between devices  36.2 us (41%)
  starting transfers between devices  31.5 us (35%)
  Pallas kernels  19.6 us (22%)
    pallas_call x11, Pallas kernels, call(): pl.pallas_call(kernel_body, in_specs=[first] + [VMEM] * (len(operands) -...  10.3 us
    ppermute x2, waiting for transfers between devices, last_parts(): lax.ppermute(far_same, 'view', [(i, i ^ 2) for i in range(groups)])  8.69 us
    ppermute x3, waiting for transfers between devices, first_exchange(): lax.ppermute(sends[0], 'scene', along_x)  8.38 us
    ppermute x3, starting transfers between devices, shards(): granted = [lax.ppermute(partners, 'view', pairs) for pairs in between]  5.62 us
    ppermute x2, waiting for transfers between devices, second_exchange(): lax.ppermute(sums[0], 'scene', along_y)  5.13 us
    ppermute x3, starting transfers between devices, shards(): lax.ppermute(part_out, 'view', pairs)  4.45 us
    pallas_call x1, Pallas kernels, shards(): pl.pallas_call(project_kernel, in_specs=[SMEM] + [VMEM] * 10, out_specs=[...  4.13 us
    ppermute x3, starting transfers between devices, first_exchange(): lax.ppermute(sends[0], 'scene', along_x)  3.66 us
  transfers between devices with their start and end apart: 30, of which 17 were waited for; matrix products, arithmetic and copies ran while one was open for 0% of the time, Pallas kernels for 14%

profile of v18, /device:TPU:0, one launch (start us, length us, event | category | flops | bytes accessed | tf_op | source)
XLA Modules:
  0.0 89.1 jit_solution(6273366401274935623)
XLA Ops:
  0.6 0.8 copy.13.partners
  1.4 3.0 %collective-permute-start.2 = (s32[1,4,3]{2,1,0:T(4,128)S(1)}, s32[1,4,3]{2,1,0:T(4,128)S(1)}, u32[]{:S(2)}, u32[]{:S(2)}) collective-permute-start(s32[1,4,3]{2,1,0:T(4,128)S(1)} %copy.13.partners), channel_id=1, source_target_pairs={{0,2},{2,0},{4,6},{6,4},{1,3},{3,1},{5,7},{7,5},{8,10},{10,8},{12,... | collective-permute-start | bytes 152 | tf_op jit(solution)/shard_map/ppermute | solution.py:430
  4.4 2.6 %collective-permute-start.1 = (s32[1,4,3]{2,1,0:T(4,128)S(1)}, s32[1,4,3]{2,1,0:T(4,128)S(1)}, u32[]{:S(2)}, u32[]{:S(2)}) collective-permute-start(s32[1,4,3]{2,1,0:T(4,128)S(1)} %copy.13.partners), channel_id=1, source_target_pairs={{0,4},{2,6},{4,0},{6,2},{1,5},{3,7},{5,1},{7,3},{8,12},{10,14},{12... | collective-permute-start | bytes 152 | tf_op jit(solution)/shard_map/ppermute | solution.py:430
  7.0 0.0 collective-permute-start
  7.0 0.5 collective-permute-start.7
  7.5 1.2 %alive.1 = s32[16]{0:T(128)S(1)} custom-call(s32[1,4,3]{2,1,0:T(4,128)S(1)} %copy.13.partners), custom_call_target="tpu_custom_call" | custom-call | flops 40000000000 | bytes 1 | tf_op jit(solution)/shard_map/alive/pallas_call | solution.py:420
  8.8 0.1 stack.23.scalars
  8.9 0.0 copy-start.5
  8.9 0.0 copy-start.6
  8.9 0.0 copy-start.7
  8.9 3.5 %collective-permute-done.refs_0_ = s32[1,4,3]{2,1,0:T(4,128)S(1)} collective-permute-done((s32[1,4,3]{2,1,0:T(4,128)S(1)}, s32[1,4,3]{2,1,0:T(4,128)S(1)}, u32[]{:S(2)}, u32[]{:S(2)}) %collective-permute-start) | collective-permute-done | bytes 80 | tf_op jit(solution)/shard_map/ppermute | solution.py:430
  12.4 0.8 pick.1
  13.2 0.4 collective-permute-start.3
  13.6 4.0 %collective-permute-start.5 = (bf16[32,1536]{1,0:T(8,128)(2,1)S(1)}, bf16[32,1536]{1,0:T(8,128)(2,1)S(1)}, u32[]{:S(2)}, u32[]{:S(2)}) collective-permute-start(bf16[32,1536]{1,0:T(8,128)(2,1)S(1)} %get-tuple-element.74), channel_id=1, source_target_pairs={{0,2},{2,0},{4,6},{6,4},{1,3},{3,1},{5,7},{7,5},{8,10},{10,8},{12,... | collective-permute-start | bytes 294920 | tf_op jit(solution)/shard_map/ppermute | solution.py:447
  17.7 4.1 %project.1 = (bf16[1536,256]{1,0:T(8,128)(2,1)S(1)}, bf16[256,384]{1,0:T(8,128)(2,1)S(1)}, bf16[256,384]{1,0:T(8,128)(2,1)S(1)}, bf16[256,1536]{1,0:T(8,128)(2,1...) custom-call(s32[5]{0:T(128)S(1)} %stack.23.scalars, ...), custom_call_target="tpu_custom_call" | custom-call | flops 1 | bytes 1 | tf_op jit(solution)/shard_map/project/pallas_call | solution.py:449
  21.9 0.4 collective-permute-done.4.refs_1_
  22.3 0.1 collective-permute-start.8
  22.4 0.4 collective-permute-start.9
  22.8 0.1 collective-permute-start.10
  22.9 0.7 collective-permute-done.8.refs_3_
  23.6 0.2 collective-permute-done.9.refs_4_
  23.7 0.4 collective-permute-done.10.refs_5_
  24.1 3.2 %attention_forward.1 = (bf16[1536,192]{1,0:T(8,128)(2,1)S(1)}, bf16[192,384]{1,0:T(8,128)(2,1)S(1)}, bf16[192,384]{1,0:T(8,128)(2,1)S(1)}, f32[3,64,512]{2,1,0:T...) custom-call(s32[5]{0:T(128)S(1)} %stack.23.scalars, ...), custom_call_target="tpu_custom_call" | custom-call | flops 1 | bytes 1 | tf_op jit(solution)/shard_map/attention_forward/pallas_call | solution.py:485
  27.3 0.2 collective-permute-start.11
  27.5 1.6 %attention_backward.1 = (bf16[256,384]{1,0:T(8,128)(2,1)S(1)}, bf16[448,384]{1,0:T(8,128)(2,1)S(1)}) custom-call(bf16[3,512,128]{2,1,0:T(8,128)(2,1)S(1)} %get-tuple-element.81.refs_6_.query_stack, bf16[3,512,128]{2,1,0:T(8,128)(2,1)S(1)} %get-tuple-element.82.refs_7_.grad_stack, f32[3,64,512]{2,1,0:T(8,128)S(1)} %get-tuple-element.86.dprob_own, ...), custom_call_target="tpu_custom_call" | custom-call | flops 1 | bytes 1 | tf_op jit(solution)/shard_map/attention_backward/pallas_call | solution.py:473
  29.1 1.8 %grad_value_out.1 = (bf16[2,2,2,48,1536]{4,3,2,1,0:T(8,128)(2,1)S(1)}, f32[2,2,2,48,1536]{4,3,2,1,0:T(8,128)S(1)}) custom-call(s32[5]{0:T(128)S(1)} %stack.23.scalars, bf16[1536,256]{1,0:T(8,128)(2,1)S(1)} %get-tuple-element.76.normed_t, bf16[1536,192]{1,0:T(8,128)(2,1)S(1)} %get-tuple-element.85.normed_far_t, ...), custom_call_target="tpu_custom_call" | custom-call | flops 1 | bytes 1 | tf_op jit(solution)/shard_map/grad_value_out/pallas_call | solution.py:473
  30.9 0.4 collective-permute-start.22
  31.3 1.9 %grad_query_key.1 = (bf16[384,384]{1,0:T(8,128)(2,1)S(1)}, bf16[384,384]{1,0:T(8,128)(2,1)S(1)}, bf16[384,384]{1,0:T(8,128)(2,1)S(1)}, bf16[384,384]{1,0:T(8,128...) custom-call(s32[5]{0:T(128)S(1)} %stack.23.scalars, ...), custom_call_target="tpu_custom_call" | custom-call | flops 1 | bytes 1 | tf_op jit(solution)/shard_map/grad_query_key/pallas_call | solution.py:473
  33.2 1.6 %collective-permute-start.13 = (bf16[384,384]{1,0:T(8,128)(2,1)S(1)}, bf16[384,384]{1,0:T(8,128)(2,1)S(1)}, u32[]{:S(2)}, u32[]{:S(2)}) collective-permute-start(bf16[384,384]{1,0:T(8,128)(2,1)S(1)} %get-tuple-element.102), channel_id=1, source_target_pairs={{0,8},{8,0},{16,24},{24,16},{1,9},{9,1},{17,25},{25,17},{2,10},{10... | collective-permute-start | bytes 884744 | tf_op jit(solution)/shard_map/ppermute | solution.py:523
  34.8 1.5 %collective-permute-start.14 = (bf16[384,384]{1,0:T(8,128)(2,1)S(1)}, bf16[384,384]{1,0:T(8,128)(2,1)S(1)}, u32[]{:S(2)}, u32[]{:S(2)}) collective-permute-start(bf16[384,384]{1,0:T(8,128)(2,1)S(1)} %get-tuple-element.104), channel_id=1, source_target_pairs={{0,16},{8,24},{16,0},{24,8},{1,17},{9,25},{17,1},{25,9},{2,18},{10... | collective-permute-start | bytes 884744 | tf_op jit(solution)/shard_map/ppermute | solution.py:523
  36.3 0.5 collective-permute-start.12
  36.8 0.5 collective-permute-start.16
  37.3 5.8 %collective-permute-done.13.q_got = bf16[384,384]{1,0:T(8,128)(2,1)S(1)} collective-permute-done((bf16[384,384]{1,0:T(8,128)(2,1)S(1)}, bf16[384,384]{1,0:T(8,128)(2,1)S(1)}, u32[]{:S(2)}, u32[]{:S(2)}) %collective-permute-start.13) | collective-permute-done | bytes 294944 | tf_op jit(solution)/shard_map/ppermute | solution.py:523
  43.2 1.5 %collective-permute-done.14.k_got = bf16[384,384]{1,0:T(8,128)(2,1)S(1)} collective-permute-done((bf16[384,384]{1,0:T(8,128)(2,1)S(1)}, bf16[384,384]{1,0:T(8,128)(2,1)S(1)}, u32[]{:S(2)}, u32[]{:S(2)}) %collective-permute-start.14) | collective-permute-done | bytes 294944 | tf_op jit(solution)/shard_map/ppermute | solution.py:523
  44.7 0.1 first_sum_query_key.1
  44.8 1.6 %collective-permute-start.15 = (bf16[384,384]{1,0:T(8,128)(2,1)S(1)}, bf16[384,384]{1,0:T(8,128)(2,1)S(1)}, u32[]{:S(2)}, u32[]{:S(2)}) collective-permute-start(bf16[384,384]{1,0:T(8,128)(2,1)S(1)} %get-tuple-element.105), channel_id=1, source_target_pairs={{0,16},{8,24},{16,0},{24,8},{1,17},{9,25},{17,1},{25,9},{2,18},{10... | collective-permute-start | bytes 884744 | tf_op jit(solution)/shard_map/ppermute | solution.py:531
  46.4 0.5 collective-permute-start.17
  46.9 2.6 %collective-permute-done.12.q_first = bf16[384,384]{1,0:T(8,128)(2,1)S(1)} collective-permute-done((bf16[384,384]{1,0:T(8,128)(2,1)S(1)}, bf16[384,384]{1,0:T(8,128)(2,1)S(1)}, u32[]{:S(2)}, u32[]{:S(2)}) %collective-permute-start.12) | collective-permute-done | bytes 294944 | tf_op jit(solution)/shard_map/ppermute | solution.py:523
  49.5 1.5 %collective-permute-done.16.k_first = bf16[384,384]{1,0:T(8,128)(2,1)S(1)} collective-permute-done((bf16[384,384]{1,0:T(8,128)(2,1)S(1)}, bf16[384,384]{1,0:T(8,128)(2,1)S(1)}, u32[]{:S(2)}, u32[]{:S(2)}) %collective-permute-start.16) | collective-permute-done | bytes 294944 | tf_op jit(solution)/shard_map/ppermute | solution.py:523
  51.0 5.1 %collective-permute-done.15.q_second = bf16[384,384]{1,0:T(8,128)(2,1)S(1)} collective-permute-done((bf16[384,384]{1,0:T(8,128)(2,1)S(1)}, bf16[384,384]{1,0:T(8,128)(2,1)S(1)}, u32[]{:S(2)}, u32[]{:S(2)}) %collective-permute-start.15) | collective-permute-done | bytes 294944 | tf_op jit(solution)/shard_map/ppermute | solution.py:531
  56.1 0.8 second_sum_query_key.1
  56.9 1.8 %collective-permute-start.18 = (bf16[2,96,768]{2,1,0:T(8,128)(2,1)S(1)}, bf16[2,96,768]{2,1,0:T(8,128)(2,1)S(1)}, u32[]{:S(2)}, u32[]{:S(2)}) collective-permute-start(bf16[2,96,768]{2,1,0:T(8,128)(2,1)S(1)} %get-tuple-element.109), channel_id=1, source_target_pairs={{0,2},{2,0},{4,6},{6,4},{1,3},{3,1},{5,7},{7,5},{8,10},{10,8},{12,... | collective-permute-start | bytes 884744 | tf_op jit(solution)/shard_map/ppermute | solution.py:595
  58.7 1.1 %collective-permute-done.22.got = bf16[2,2,2,48,1536]{4,3,2,1,0:T(8,128)(2,1)S(1)} collective-permute-done((bf16[2,2,2,48,1536]{4,3,2,1,0:T(8,128)(2,1)S(1)}, bf16[2,2,2,48,1536]{4,3,2,1,0:T(8,128)(2,1)S(1)}, u32[]{:S(2)}, u32[]{:S(2)}) %collective-permute-start.22) | collective-permute-done | bytes 1179680 | tf_op jit(solution)/shard_map/ppermute | solution.py:571
  59.8 0.2 view_sum_value_out.1
  60.0 1.6 %collective-permute-start.23 = (bf16[2,2,48,768]{3,2,1,0:T(8,128)(2,1)S(1)}, bf16[2,2,48,768]{3,2,1,0:T(8,128)(2,1)S(1)}, u32[]{:S(2)}, u32[]{:S(2)}) collective-permute-start(bf16[2,2,48,768]{3,2,1,0:T(8,128)(2,1)S(1)} %get-tuple-element.120), channel_id=1, source_target_pairs={{0,8},{8,0},{16,24},{24,16},{1,9},{9,1},{17,25},{25,17},{2,10},{10... | collective-permute-start | bytes 884744 | tf_op jit(solution)/shard_map/ppermute | solution.py:523
  61.5 1.5 %collective-permute-start.24 = (bf16[2,2,48,768]{3,2,1,0:T(8,128)(2,1)S(1)}, bf16[2,2,48,768]{3,2,1,0:T(8,128)(2,1)S(1)}, u32[]{:S(2)}, u32[]{:S(2)}) collective-permute-start(bf16[2,2,48,768]{3,2,1,0:T(8,128)(2,1)S(1)} %get-tuple-element.122), channel_id=1, source_target_pairs={{0,16},{8,24},{16,0},{24,8},{1,17},{9,25},{17,1},{25,9},{2,18},{10... | collective-permute-start | bytes 884744 | tf_op jit(solution)/shard_map/ppermute | solution.py:523
  63.0 2.5 %collective-permute-done.18.refs_1_ = bf16[2,96,768]{2,1,0:T(8,128)(2,1)S(1)} collective-permute-done((bf16[2,96,768]{2,1,0:T(8,128)(2,1)S(1)}, bf16[2,96,768]{2,1,0:T(8,128)(2,1)S(1)}, u32[]{:S(2)}, u32[]{:S(2)}) %collective-permute-start.18) | collective-permute-done | bytes 294944 | tf_op jit(solution)/shard_map/ppermute | solution.py:595
  65.5 0.6 last_parts_query_key.1
  66.2 0.1 collective-permute-start.20
  66.3 1.7 %collective-permute-start.19 = (bf16[48,768]{1,0:T(8,128)(2,1)S(1)}, bf16[48,768]{1,0:T(8,128)(2,1)S(1)}, u32[]{:S(2)}, u32[]{:S(2)}) collective-permute-start(bf16[48,768]{1,0:T(8,128)(2,1)S(1)} %get-tuple-element.111), channel_id=1, source_target_pairs={{0,4},{2,6},{4,0},{6,2},{1,5},{3,7},{5,1},{7,3},{8,12},{10,14},{12... | collective-permute-start | bytes 221192 | tf_op jit(solution)/shard_map/ppermute | solution.py:557
  67.9 1.1 %collective-permute-start.21 = (bf16[48,768]{1,0:T(8,128)(2,1)S(1)}, bf16[48,768]{1,0:T(8,128)(2,1)S(1)}, u32[]{:S(2)}, u32[]{:S(2)}) collective-permute-start(bf16[48,768]{1,0:T(8,128)(2,1)S(1)} %get-tuple-element.113), channel_id=1, source_target_pairs={{0,5},{1,4},{2,7},{3,6},{4,1},{5,0},{6,3},{7,2},{8,13},{9,12},{10,... | collective-permute-start | bytes 221192 | tf_op jit(solution)/shard_map/ppermute | solution.py:558
  69.0 0.1 collective-permute-done.24.y_got
  69.1 0.1 first_sum_value_out.1
  69.2 1.4 %collective-permute-start.25 = (bf16[2,48,768]{2,1,0:T(8,128)(2,1)S(1)}, bf16[2,48,768]{2,1,0:T(8,128)(2,1)S(1)}, u32[]{:S(2)}, u32[]{:S(2)}) collective-permute-start(bf16[2,48,768]{2,1,0:T(8,128)(2,1)S(1)} %get-tuple-element.125), channel_id=1, source_target_pairs={{0,8},{8,0},{16,24},{24,16},{1,9},{9,1},{17,25},{25,17},{2,10},{10... | collective-permute-start | bytes 442376 | tf_op jit(solution)/shard_map/ppermute | solution.py:531
  70.7 1.5 %collective-permute-start.26 = (bf16[2,48,768]{2,1,0:T(8,128)(2,1)S(1)}, bf16[2,48,768]{2,1,0:T(8,128)(2,1)S(1)}, u32[]{:S(2)}, u32[]{:S(2)}) collective-permute-start(bf16[2,48,768]{2,1,0:T(8,128)(2,1)S(1)} %get-tuple-element.127), channel_id=1, source_target_pairs={{0,16},{8,24},{16,0},{24,8},{1,17},{9,25},{17,1},{25,9},{2,18},{10... | collective-permute-start | bytes 442376 | tf_op jit(solution)/shard_map/ppermute | solution.py:531
  72.2 3.2 %collective-permute-done.19.far_same = bf16[48,768]{1,0:T(8,128)(2,1)S(1)} collective-permute-done((bf16[48,768]{1,0:T(8,128)(2,1)S(1)}, bf16[48,768]{1,0:T(8,128)(2,1)S(1)}, u32[]{:S(2)}, u32[]{:S(2)}) %collective-permute-start.19) | collective-permute-done | bytes 73760 | tf_op jit(solution)/shard_map/ppermute | solution.py:557
  75.4 0.7 collective-permute-done.21.far_cross
  76.1 1.3 %last_sum_query_key.1 = (f32[48,768]{1,0:T(8,128)}, f32[48,768]{1,0:T(8,128)}) custom-call(s32[5]{0:T(128)S(1)} %stack.23.scalars, f32[48,768]{1,0:T(8,128)S(1)} %get-tuple-element.110.mine, bf16[48,768]{1,0:T(8,128)(2,1)S(1)} %collective-permute-done.19.far_same, f32[48,768]{1,0:T(8,128)S(1)} %collective-permute-done.20.near_cross, ...), custom_call_target="tpu_custom_call" | custom-call | flops 40000000000 | bytes 1 | tf_op jit(solution)/shard_map/last_sum_query_key/pallas_call | solution.py:473
  77.4 0.6 last_parts_value_out.1
  78.1 0.3 collective-permute-start.28
  78.4 2.5 %collective-permute-start.29 = (bf16[24,1536]{1,0:T(8,128)(2,1)S(1)}, bf16[24,1536]{1,0:T(8,128)(2,1)S(1)}, u32[]{:S(2)}, u32[]{:S(2)}) collective-permute-start(bf16[24,1536]{1,0:T(8,128)(2,1)S(1)} %get-tuple-element.131), channel_id=1, source_target_pairs={{0,5},{1,4},{2,7},{3,6},{4,1},{5,0},{6,3},{7,2},{8,13},{9,12},{10,... | collective-permute-start | bytes 221192 | tf_op jit(solution)/shard_map/ppermute | solution.py:558
  80.9 5.5 %collective-permute-done.27.far_same = bf16[24,1536]{1,0:T(8,128)(2,1)S(1)} collective-permute-done((bf16[24,1536]{1,0:T(8,128)(2,1)S(1)}, bf16[24,1536]{1,0:T(8,128)(2,1)S(1)}, u32[]{:S(2)}, u32[]{:S(2)}) %collective-permute-start.27) | collective-permute-done | bytes 73760 | tf_op jit(solution)/shard_map/ppermute | solution.py:557
  86.4 1.4 %collective-permute-done.29.far_cross = bf16[24,1536]{1,0:T(8,128)(2,1)S(1)} collective-permute-done((bf16[24,1536]{1,0:T(8,128)(2,1)S(1)}, bf16[24,1536]{1,0:T(8,128)(2,1)S(1)}, u32[]{:S(2)}, u32[]{:S(2)}) %collective-permute-start.29) | collective-permute-done | bytes 73760 | tf_op jit(solution)/shard_map/ppermute | solution.py:558
  87.8 1.3 %last_sum_value_out.1 = (f32[48,768]{1,0:T(8,128)}, f32[24,1536]{1,0:T(8,128)}) custom-call(s32[5]{0:T(128)S(1)} %stack.23.scalars, f32[24,1536]{1,0:T(8,128)S(1)} %get-tuple-element.128.mine, bf16[24,1536]{1,0:T(8,128)(2,1)S(1)} %collective-permute-done.27.far_same, f32[24,1536]{1,0:T(8,128)S(1)} %collective-permute-done.28.near_cross, ...), custom_call_target="tpu_custom_call" | custom-call | flops 1 | bytes 1 | tf_op jit(solution)/shard_map/last_sum_value_out/pallas_call | solution.py:473
  (29 shorter events, 0.1 us)
Async XLA Ops:
  1.4 7.5 %collective-permute-start.2 = (s32[1,4,3]{2,1,0:T(4,128)S(1)}, s32[1,4,3]{2,1,0:T(4,128)S(1)}, u32[]{:S(2)}, u32[]{:S(2)}) collective-permute-start(s32[1,4,3]{2,1,0:T(4,128)S(1)} %copy.13.partners), channel_id=1, source_target_pairs={{0,2},{2,0},{4,6},{6,4},{1,3},{3,1},{5,7},{7,5},{8,10},{10,8},{12,... | collective-permute-start | bytes 152 | tf_op jit(solution)/shard_map/ppermute | solution.py:430
  4.4 4.5 %collective-permute-start.1 = (s32[1,4,3]{2,1,0:T(4,128)S(1)}, s32[1,4,3]{2,1,0:T(4,128)S(1)}, u32[]{:S(2)}, u32[]{:S(2)}) collective-permute-start(s32[1,4,3]{2,1,0:T(4,128)S(1)} %copy.13.partners), channel_id=1, source_target_pairs={{0,4},{2,6},{4,0},{6,2},{1,5},{3,7},{5,1},{7,3},{8,12},{10,14},{12... | collective-permute-start | bytes 152 | tf_op jit(solution)/shard_map/ppermute | solution.py:430
  7.0 5.4 %collective-permute-start = (s32[1,4,3]{2,1,0:T(4,128)S(1)}, s32[1,4,3]{2,1,0:T(4,128)S(1)}, u32[]{:S(2)}, u32[]{:S(2)}) collective-permute-start(s32[1,4,3]{2,1,0:T(4,128)S(1)} %copy.13.partners), channel_id=1, source_target_pairs={{0,6},{2,4},{4,2},{6,0},{1,7},{3,5},{5,3},{7,1},{8,14},{10,12},{12... | collective-permute-start | bytes 152 | tf_op jit(solution)/shard_map/ppermute | solution.py:430
  7.0 10.6 %collective-permute-start.6 = (bf16[4,32,1536]{2,1,0:T(8,128)(2,1)}, bf16[4,32,1536]{2,1,0:T(8,128)(2,1)S(1)}, u32[]{:S(2)}, u32[]{:S(2)}) collective-permute-start(bf16[4,32,1536]{2,1,0:T(8,128)(2,1)} %bitcast.7), channel_id=1, source_target_pairs={{0,1},{1,0},{2,3},{3,2},{4,5},{5,4},{6,7},{7,6},{8,9},{9,8},{10,11... | collective-permute-start | bytes 1179656 | tf_op jit(solution)/shard_map/ppermute | solution.py:435
  7.0 10.6 %collective-permute-start.7 = (bf16[4,32,1536]{2,1,0:T(8,128)(2,1)}, bf16[4,32,1536]{2,1,0:T(8,128)(2,1)S(1)}, u32[]{:S(2)}, u32[]{:S(2)}) collective-permute-start(bf16[4,32,1536]{2,1,0:T(8,128)(2,1)} %bitcast.10), channel_id=1, source_target_pairs={{0,1},{1,0},{2,3},{3,2},{4,5},{5,4},{6,7},{7,6},{8,9},{9,8},{10,11... | collective-permute-start | bytes 1179656 | tf_op jit(solution)/shard_map/ppermute | solution.py:436
  7.5 4.9 %copy-start.4 = (bf16[1,4,1,32,1536]{4,3,2,1,0:T(8,128)(2,1)S(1)}, bf16[1,4,1,32,1536]{4,3,2,1,0:T(8,128)(2,1)}, u32[]{:S(2)}) copy-start(bf16[1,4,1,32,1536]{4,3,2,1,0:T(8,128)(2,1)} %param.10) | copy-start | bytes 1179652
  8.8 8.8 %copy-start = (bf16[1536,768]{1,0:T(8,128)(2,1)S(1)}, bf16[1536,768]{1,0:T(8,128)(2,1)}, u32[]{:S(2)}) copy-start(bf16[1536,768]{1,0:T(8,128)(2,1)} %refs_11_.1) | copy-start | bytes 7077892
  8.9 8.8 %copy-start.1 = (bf16[1536,768]{1,0:T(8,128)(2,1)S(1)}, bf16[1536,768]{1,0:T(8,128)(2,1)}, u32[]{:S(2)}) copy-start(bf16[1536,768]{1,0:T(8,128)(2,1)} %refs_12_.1) | copy-start | bytes 7077892
  8.9 8.8 %copy-start.2 = (bf16[1536,768]{1,0:T(8,128)(2,1)S(1)}, bf16[1536,768]{1,0:T(8,128)(2,1)}, u32[]{:S(2)}) copy-start(bf16[1536,768]{1,0:T(8,128)(2,1)} %w_query.1) | copy-start | bytes 7077892
  8.9 8.8 %copy-start.3 = (bf16[768,1536]{1,0:T(8,128)(2,1)S(1)}, bf16[768,1536]{1,0:T(8,128)(2,1)}, u32[]{:S(2)}) copy-start(bf16[768,1536]{1,0:T(8,128)(2,1)} %w_out.1) | copy-start | bytes 7077892
  8.9 8.8 %copy-start.5 = (bf16[1,4,1,32,1536]{4,3,2,1,0:T(8,128)(2,1)S(1)}, bf16[1,4,1,32,1536]{4,3,2,1,0:T(8,128)(2,1)}, u32[]{:S(2)}) copy-start(bf16[1,4,1,32,1536]{4,3,2,1,0:T(8,128)(2,1)} %param.18) | copy-start | bytes 1179652
  8.9 8.8 %copy-start.6 = (bf16[9,1536]{1,0:T(8,128)(2,1)S(1)}, bf16[9,1536]{1,0:T(8,128)(2,1)}, u32[]{:S(2)}) copy-start(bf16[9,1536]{1,0:T(8,128)(2,1)} %taps.1) | copy-start | bytes 82948
  8.9 8.8 %copy-start.7 = (f32[1536]{0:T(1024)S(1)}, f32[1536]{0:T(1024)}, u32[]{:S(2)}) copy-start(f32[1536]{0:T(1024)} %refs_10_.1) | copy-start | bytes 18436
  13.2 8.7 %collective-permute-start.3 = (bf16[32,1536]{1,0:T(8,128)(2,1)S(1)}, bf16[32,1536]{1,0:T(8,128)(2,1)S(1)}, u32[]{:S(2)}, u32[]{:S(2)}) collective-permute-start(bf16[32,1536]{1,0:T(8,128)(2,1)S(1)} %get-tuple-element.72), channel_id=1, source_target_pairs={{0,6},{2,4},{4,2},{6,0},{1,7},{3,5},{5,3},{7,1},{8,14},{10,12},{12... | collective-permute-start | bytes 294920 | tf_op jit(solution)/shard_map/ppermute | solution.py:447
  13.6 8.7 %collective-permute-start.4 = (bf16[32,1536]{1,0:T(8,128)(2,1)S(1)}, bf16[32,1536]{1,0:T(8,128)(2,1)S(1)}, u32[]{:S(2)}, u32[]{:S(2)}) collective-permute-start(bf16[32,1536]{1,0:T(8,128)(2,1)S(1)} %get-tuple-element.73), channel_id=1, source_target_pairs={{0,4},{2,6},{4,0},{6,2},{1,5},{3,7},{5,1},{7,3},{8,12},{10,14},{12... | collective-permute-start | bytes 294920 | tf_op jit(solution)/shard_map/ppermute | solution.py:447
  13.6 8.7 %collective-permute-start.5 = (bf16[32,1536]{1,0:T(8,128)(2,1)S(1)}, bf16[32,1536]{1,0:T(8,128)(2,1)S(1)}, u32[]{:S(2)}, u32[]{:S(2)}) collective-permute-start(bf16[32,1536]{1,0:T(8,128)(2,1)S(1)} %get-tuple-element.74), channel_id=1, source_target_pairs={{0,2},{2,0},{4,6},{6,4},{1,3},{3,1},{5,7},{7,5},{8,10},{10,8},{12,... | collective-permute-start | bytes 294920 | tf_op jit(solution)/shard_map/ppermute | solution.py:447
  22.3 1.3 %collective-permute-start.8 = (bf16[32,1536]{1,0:T(8,128)(2,1)S(1)}, bf16[32,1536]{1,0:T(8,128)(2,1)S(1)}, u32[]{:S(2)}, u32[]{:S(2)}) collective-permute-start(bf16[32,1536]{1,0:T(8,128)(2,1)S(1)} %collective-permute-done.3.refs_0_), channel_id=1, source_target_pairs={{0,1},{1,0},{2,3},{3,2},{4,5},{5,4},{6,7},{7,6},{8,9},{9,8},{10,11... | collective-permute-start | bytes 294920 | tf_op jit(solution)/shard_map/ppermute | solution.py:470
  22.4 1.4 %collective-permute-start.9 = (bf16[32,1536]{1,0:T(8,128)(2,1)S(1)}, bf16[32,1536]{1,0:T(8,128)(2,1)S(1)}, u32[]{:S(2)}, u32[]{:S(2)}) collective-permute-start(bf16[32,1536]{1,0:T(8,128)(2,1)S(1)} %collective-permute-done.4.refs_1_), channel_id=1, source_target_pairs={{0,1},{1,0},{2,3},{3,2},{4,5},{5,4},{6,7},{7,6},{8,9},{9,8},{10,11... | collective-permute-start | bytes 294920 | tf_op jit(solution)/shard_map/ppermute | solution.py:470
  22.8 1.3 %collective-permute-start.10 = (bf16[32,1536]{1,0:T(8,128)(2,1)S(1)}, bf16[32,1536]{1,0:T(8,128)(2,1)S(1)}, u32[]{:S(2)}, u32[]{:S(2)}) collective-permute-start(bf16[32,1536]{1,0:T(8,128)(2,1)S(1)} %collective-permute-done.5.refs_2_), channel_id=1, source_target_pairs={{0,1},{1,0},{2,3},{3,2},{4,5},{5,4},{6,7},{7,6},{8,9},{9,8},{10,11... | collective-permute-start | bytes 294920 | tf_op jit(solution)/shard_map/ppermute | solution.py:470
  27.3 1.8 %collective-permute-start.11 = (bf16[384,256]{1,0:T(8,128)(2,1)S(1)}, bf16[384,256]{1,0:T(8,128)(2,1)S(1)}, u32[]{:S(2)}, u32[]{:S(2)}) collective-permute-start(bf16[384,256]{1,0:T(8,128)(2,1)S(1)} %get-tuple-element.96.mine), channel_id=1, source_target_pairs={{0,1},{1,0},{2,3},{3,2},{4,5},{5,4},{6,7},{7,6},{8,9},{9,8},{10,11... | collective-permute-start | bytes 589832 | tf_op jit(solution)/shard_map/ppermute | solution.py:505
  30.9 28.9 %collective-permute-start.22 = (bf16[2,2,2,48,1536]{4,3,2,1,0:T(8,128)(2,1)S(1)}, bf16[2,2,2,48,1536]{4,3,2,1,0:T(8,128)(2,1)S(1)}, u32[]{:S(2)}, u32[]{:S(2)}) collective-permute-start(bf16[2,2,2,48,1536]{4,3,2,1,0:T(8,128)(2,1)S(1)} %get-tuple-element.98), channel_id=1, source_target_pairs={{0,2},{2,0},{4,6},{6,4},{1,3},{3,1},{5,7},{7,5},{8,10},{10,8},{12,... | collective-permute-start | bytes 3538952 | tf_op jit(solution)/shard_map/ppermute | solution.py:571
  33.2 9.9 %collective-permute-start.13 = (bf16[384,384]{1,0:T(8,128)(2,1)S(1)}, bf16[384,384]{1,0:T(8,128)(2,1)S(1)}, u32[]{:S(2)}, u32[]{:S(2)}) collective-permute-start(bf16[384,384]{1,0:T(8,128)(2,1)S(1)} %get-tuple-element.102), channel_id=1, source_target_pairs={{0,8},{8,0},{16,24},{24,16},{1,9},{9,1},{17,25},{25,17},{2,10},{10... | collective-permute-start | bytes 884744 | tf_op jit(solution)/shard_map/ppermute | solution.py:523
  34.8 9.9 %collective-permute-start.14 = (bf16[384,384]{1,0:T(8,128)(2,1)S(1)}, bf16[384,384]{1,0:T(8,128)(2,1)S(1)}, u32[]{:S(2)}, u32[]{:S(2)}) collective-permute-start(bf16[384,384]{1,0:T(8,128)(2,1)S(1)} %get-tuple-element.104), channel_id=1, source_target_pairs={{0,16},{8,24},{16,0},{24,8},{1,17},{9,25},{17,1},{25,9},{2,18},{10... | collective-permute-start | bytes 884744 | tf_op jit(solution)/shard_map/ppermute | solution.py:523
  36.3 13.2 %collective-permute-start.12 = (bf16[384,384]{1,0:T(8,128)(2,1)S(1)}, bf16[384,384]{1,0:T(8,128)(2,1)S(1)}, u32[]{:S(2)}, u32[]{:S(2)}) collective-permute-start(bf16[384,384]{1,0:T(8,128)(2,1)S(1)} %get-tuple-element.101), channel_id=1, source_target_pairs={{0,8},{8,0},{16,24},{24,16},{1,9},{9,1},{17,25},{25,17},{2,10},{10... | collective-permute-start | bytes 884744 | tf_op jit(solution)/shard_map/ppermute | solution.py:523
  36.8 14.2 %collective-permute-start.16 = (bf16[384,384]{1,0:T(8,128)(2,1)S(1)}, bf16[384,384]{1,0:T(8,128)(2,1)S(1)}, u32[]{:S(2)}, u32[]{:S(2)}) collective-permute-start(bf16[384,384]{1,0:T(8,128)(2,1)S(1)} %get-tuple-element.106), channel_id=1, source_target_pairs={{0,16},{8,24},{16,0},{24,8},{1,17},{9,25},{17,1},{25,9},{2,18},{10... | collective-permute-start | bytes 884744 | tf_op jit(solution)/shard_map/ppermute | solution.py:523
  44.8 11.3 %collective-permute-start.15 = (bf16[384,384]{1,0:T(8,128)(2,1)S(1)}, bf16[384,384]{1,0:T(8,128)(2,1)S(1)}, u32[]{:S(2)}, u32[]{:S(2)}) collective-permute-start(bf16[384,384]{1,0:T(8,128)(2,1)S(1)} %get-tuple-element.105), channel_id=1, source_target_pairs={{0,16},{8,24},{16,0},{24,8},{1,17},{9,25},{17,1},{25,9},{2,18},{10... | collective-permute-start | bytes 884744 | tf_op jit(solution)/shard_map/ppermute | solution.py:531
  46.4 9.8 %collective-permute-start.17 = (bf16[384,384]{1,0:T(8,128)(2,1)S(1)}, bf16[384,384]{1,0:T(8,128)(2,1)S(1)}, u32[]{:S(2)}, u32[]{:S(2)}) collective-permute-start(bf16[384,384]{1,0:T(8,128)(2,1)S(1)} %get-tuple-element.107), channel_id=1, source_target_pairs={{0,8},{8,0},{16,24},{24,16},{1,9},{9,1},{17,25},{25,17},{2,10},{10... | collective-permute-start | bytes 884744 | tf_op jit(solution)/shard_map/ppermute | solution.py:531
  56.9 8.6 %collective-permute-start.18 = (bf16[2,96,768]{2,1,0:T(8,128)(2,1)S(1)}, bf16[2,96,768]{2,1,0:T(8,128)(2,1)S(1)}, u32[]{:S(2)}, u32[]{:S(2)}) collective-permute-start(bf16[2,96,768]{2,1,0:T(8,128)(2,1)S(1)} %get-tuple-element.109), channel_id=1, source_target_pairs={{0,2},{2,0},{4,6},{6,4},{1,3},{3,1},{5,7},{7,5},{8,10},{10,8},{12,... | collective-permute-start | bytes 884744 | tf_op jit(solution)/shard_map/ppermute | solution.py:595
  60.0 9.1 %collective-permute-start.23 = (bf16[2,2,48,768]{3,2,1,0:T(8,128)(2,1)S(1)}, bf16[2,2,48,768]{3,2,1,0:T(8,128)(2,1)S(1)}, u32[]{:S(2)}, u32[]{:S(2)}) collective-permute-start(bf16[2,2,48,768]{3,2,1,0:T(8,128)(2,1)S(1)} %get-tuple-element.120), channel_id=1, source_target_pairs={{0,8},{8,0},{16,24},{24,16},{1,9},{9,1},{17,25},{25,17},{2,10},{10... | collective-permute-start | bytes 884744 | tf_op jit(solution)/shard_map/ppermute | solution.py:523
  61.5 7.6 %collective-permute-start.24 = (bf16[2,2,48,768]{3,2,1,0:T(8,128)(2,1)S(1)}, bf16[2,2,48,768]{3,2,1,0:T(8,128)(2,1)S(1)}, u32[]{:S(2)}, u32[]{:S(2)}) collective-permute-start(bf16[2,2,48,768]{3,2,1,0:T(8,128)(2,1)S(1)} %get-tuple-element.122), channel_id=1, source_target_pairs={{0,16},{8,24},{16,0},{24,8},{1,17},{9,25},{17,1},{25,9},{2,18},{10... | collective-permute-start | bytes 884744 | tf_op jit(solution)/shard_map/ppermute | solution.py:523
  66.2 10.0 %collective-permute-start.20 = (f32[48,768]{1,0:T(8,128)S(1)}, f32[48,768]{1,0:T(8,128)S(1)}, u32[]{:S(2)}, u32[]{:S(2)}) collective-permute-start(f32[48,768]{1,0:T(8,128)S(1)} %get-tuple-element.112), channel_id=1, source_target_pairs={{0,1},{1,0},{2,3},{3,2},{4,5},{5,4},{6,7},{7,6},{8,9},{9,8},{10,11... | collective-permute-start | bytes 442376 | tf_op jit(solution)/shard_map/ppermute | solution.py:559
  66.3 9.2 %collective-permute-start.19 = (bf16[48,768]{1,0:T(8,128)(2,1)S(1)}, bf16[48,768]{1,0:T(8,128)(2,1)S(1)}, u32[]{:S(2)}, u32[]{:S(2)}) collective-permute-start(bf16[48,768]{1,0:T(8,128)(2,1)S(1)} %get-tuple-element.111), channel_id=1, source_target_pairs={{0,4},{2,6},{4,0},{6,2},{1,5},{3,7},{5,1},{7,3},{8,12},{10,14},{12... | collective-permute-start | bytes 221192 | tf_op jit(solution)/shard_map/ppermute | solution.py:557
  67.9 8.2 %collective-permute-start.21 = (bf16[48,768]{1,0:T(8,128)(2,1)S(1)}, bf16[48,768]{1,0:T(8,128)(2,1)S(1)}, u32[]{:S(2)}, u32[]{:S(2)}) collective-permute-start(bf16[48,768]{1,0:T(8,128)(2,1)S(1)} %get-tuple-element.113), channel_id=1, source_target_pairs={{0,5},{1,4},{2,7},{3,6},{4,1},{5,0},{6,3},{7,2},{8,13},{9,12},{10,... | collective-permute-start | bytes 221192 | tf_op jit(solution)/shard_map/ppermute | solution.py:558
  69.2 8.2 %collective-permute-start.25 = (bf16[2,48,768]{2,1,0:T(8,128)(2,1)S(1)}, bf16[2,48,768]{2,1,0:T(8,128)(2,1)S(1)}, u32[]{:S(2)}, u32[]{:S(2)}) collective-permute-start(bf16[2,48,768]{2,1,0:T(8,128)(2,1)S(1)} %get-tuple-element.125), channel_id=1, source_target_pairs={{0,8},{8,0},{16,24},{24,16},{1,9},{9,1},{17,25},{25,17},{2,10},{10... | collective-permute-start | bytes 442376 | tf_op jit(solution)/shard_map/ppermute | solution.py:531
  70.7 6.8 %collective-permute-start.26 = (bf16[2,48,768]{2,1,0:T(8,128)(2,1)S(1)}, bf16[2,48,768]{2,1,0:T(8,128)(2,1)S(1)}, u32[]{:S(2)}, u32[]{:S(2)}) collective-permute-start(bf16[2,48,768]{2,1,0:T(8,128)(2,1)S(1)} %get-tuple-element.127), channel_id=1, source_target_pairs={{0,16},{8,24},{16,0},{24,8},{1,17},{9,25},{17,1},{25,9},{2,18},{10... | collective-permute-start | bytes 442376 | tf_op jit(solution)/shard_map/ppermute | solution.py:531
  78.1 9.7 %collective-permute-start.28 = (f32[24,1536]{1,0:T(8,128)S(1)}, f32[24,1536]{1,0:T(8,128)S(1)}, u32[]{:S(2)}, u32[]{:S(2)}) collective-permute-start(f32[24,1536]{1,0:T(8,128)S(1)} %get-tuple-element.130), channel_id=1, source_target_pairs={{0,1},{1,0},{2,3},{3,2},{4,5},{5,4},{6,7},{7,6},{8,9},{9,8},{10,11... | collective-permute-start | bytes 442376 | tf_op jit(solution)/shard_map/ppermute | solution.py:559
  78.4 8.0 %collective-permute-start.27 = (bf16[24,1536]{1,0:T(8,128)(2,1)S(1)}, bf16[24,1536]{1,0:T(8,128)(2,1)S(1)}, u32[]{:S(2)}, u32[]{:S(2)}) collective-permute-start(bf16[24,1536]{1,0:T(8,128)(2,1)S(1)} %get-tuple-element.129), channel_id=1, source_target_pairs={{0,4},{2,6},{4,0},{6,2},{1,5},{3,7},{5,1},{7,3},{8,12},{10,14},{12... | collective-permute-start | bytes 221192 | tf_op jit(solution)/shard_map/ppermute | solution.py:557
  78.4 9.4 %collective-permute-start.29 = (bf16[24,1536]{1,0:T(8,128)(2,1)S(1)}, bf16[24,1536]{1,0:T(8,128)(2,1)S(1)}, u32[]{:S(2)}, u32[]{:S(2)}) collective-permute-start(bf16[24,1536]{1,0:T(8,128)(2,1)S(1)} %get-tuple-element.131), channel_id=1, source_target_pairs={{0,5},{1,4},{2,7},{3,6},{4,1},{5,0},{6,3},{7,2},{8,13},{9,12},{10,... | collective-permute-start | bytes 221192 | tf_op jit(solution)/shard_map/ppermute | solution.py:558

commit v19 on v17

--- a/solution.py
+++ b/solution.py
@@ -374,9 +374,14 @@
         yield near[...] + far[...].astype(jnp.float32), core
 
 
-def place_query_key_kernel(scalars, mine, far_same, near_cross, far_cross, query, key):
+def add_kernel(mine, far_same, near_cross, far_cross, same, cross):
+    same[...] = mine[...] + far_same[...].astype(jnp.float32)
+    cross[...] = near_cross[...] + far_cross[...].astype(jnp.float32)
+
+
+def place_query_key_kernel(scalars, same, cross, query, key):
     size = query.shape[1] // 2
-    for total, core in last_sums(scalars, mine, far_same, near_cross, far_cross):
+    for total, core in ((same, scalars[0]), (cross, 1 - scalars[0])):
         columns = pl.ds(pl.multiple_of(core * size, size), size)
         query[:, columns] = total[:, :size]
         key[:, columns] = total[:, size:]
@@ -606,12 +611,15 @@
     vo_sums = first_sum(vo_parts, vo_got, "first_sum_value_out")
     v_got, o_got = second_exchange(vo_sums)
     addends = (vo_sums[3], o_got, vo_sums[2], v_got)
-    vo_last = last_parts((after(addends[0], qk_last[1], qk_last[3]), *addends[1:]), value_out_cores, "value_out")
+    qk_total = call(
+        add_kernel, [shape((q_rows, 2 * part), f32)] * 2, qk_last, "last_sum_query_key", cost=MUCH
+    )
+    vo_last = last_parts((after(addends[0], qk_total[0]), *addends[1:]), value_out_cores, "value_out")
     grad_query, grad_key = call(
         place_query_key_kernel,
         [shape((q_rows, inner), f32)] * 2,
-        (scalars, *qk_last),
-        "last_sum_query_key",
+        (scalars, *qk_total),
+        "place_query_key",
         SMEM,
     )
     grad_value, grad_out = call(

time: 91.8 us -> 88.7 us (0.966)
  waiting for transfers between devices: 39.2 us -> 35.6 us
    ppermute x2, starting transfers between devices: 2.55 us -> 0.14 us  [last_parts(): near_cross = lax.ppermute(near_cross, 'row', swap)]
    ppermute x2, waiting for transfers between devices: 9.49 us -> 7.72 us  [last_parts(): lax.ppermute(far_same, 'view', [(i, i ^ 2) for i in range(groups)])]
    ppermute x3, waiting for transfers between devices: 10.1 us -> 8.38 us  [first_exchange(): lax.ppermute(sends[0], 'scene', along_x)]
    ppermute x2, starting transfers between devices: 1.13 us -> 2.61 us  [last_parts(): lax.ppermute(far_same, 'view', [(i, i ^ 2) for i in range(groups)])]
    ppermute x3, waiting for transfers between devices: 4.25 us -> 3.17 us  [first_exchange(): lax.ppermute(sends[1], 'scene', along_y)]
    pallas_call x11 -> x12, Pallas kernels: 10.3 us -> 10.3 us  [call(): pl.pallas_call(kernel_body, in_specs=[first] + [VMEM] * (len(operands) -...]
where the time goes in v19:
time: 88.7 us; the launch traced here: 88.5 us
  waiting for transfers between devices  35.6 us (40%)
  starting transfers between devices  31.5 us (36%)
  Pallas kernels  19.6 us (22%)
  between operations  0.9 us (1%)
  local copies, waits for them, and re-layouts  0.89 us (1%)
    pallas_call x12, Pallas kernels, call(): pl.pallas_call(kernel_body, in_specs=[first] + [VMEM] * (len(operands) -...  10.3 us
    ppermute x3, waiting for transfers between devices, first_exchange(): lax.ppermute(sends[0], 'scene', along_x)  8.38 us
    ppermute x2, waiting for transfers between devices, last_parts(): lax.ppermute(far_same, 'view', [(i, i ^ 2) for i in range(groups)])  7.72 us
    ppermute x3, starting transfers between devices, shards(): granted = [lax.ppermute(partners, 'view', pairs) for pairs in between]  5.62 us
    ppermute x2, waiting for transfers between devices, second_exchange(): lax.ppermute(sums[0], 'scene', along_y)  5.43 us
    ppermute x3, starting transfers between devices, shards(): lax.ppermute(part_out, 'view', pairs)  4.45 us
    pallas_call x1, Pallas kernels, shards(): pl.pallas_call(project_kernel, in_specs=[SMEM] + [VMEM] * 10, out_specs=[...  4.13 us
    ppermute x3, starting transfers between devices, first_exchange(): lax.ppermute(sends[0], 'scene', along_x)  3.66 us
  transfers between devices with their start and end apart: 30, of which 18 were waited for; matrix products, arithmetic and copies ran while one was open for 0% of the time, Pallas kernels for 14%

profile of v19, /device:TPU:0, one launch (start us, length us, event | category | flops | bytes accessed | tf_op | source)
XLA Modules:
  0.0 88.5 jit_solution(13139055539650175133)
XLA Ops:
  0.6 0.8 copy.13.partners
  1.4 3.0 %collective-permute-start.2 = (s32[1,4,3]{2,1,0:T(4,128)S(1)}, s32[1,4,3]{2,1,0:T(4,128)S(1)}, u32[]{:S(2)}, u32[]{:S(2)}) collective-permute-start(s32[1,4,3]{2,1,0:T(4,128)S(1)} %copy.13.partners), channel_id=1, source_target_pairs={{0,2},{2,0},{4,6},{6,4},{1,3},{3,1},{5,7},{7,5},{8,10},{10,8},{12,... | collective-permute-start | bytes 152 | tf_op jit(solution)/shard_map/ppermute | solution.py:435
  4.4 2.6 %collective-permute-start.1 = (s32[1,4,3]{2,1,0:T(4,128)S(1)}, s32[1,4,3]{2,1,0:T(4,128)S(1)}, u32[]{:S(2)}, u32[]{:S(2)}) collective-permute-start(s32[1,4,3]{2,1,0:T(4,128)S(1)} %copy.13.partners), channel_id=1, source_target_pairs={{0,4},{2,6},{4,0},{6,2},{1,5},{3,7},{5,1},{7,3},{8,12},{10,14},{12... | collective-permute-start | bytes 152 | tf_op jit(solution)/shard_map/ppermute | solution.py:435
  7.0 0.5 collective-permute-start.7
  7.5 1.2 %alive.1 = s32[16]{0:T(128)S(1)} custom-call(s32[1,4,3]{2,1,0:T(4,128)S(1)} %copy.13.partners), custom_call_target="tpu_custom_call" | custom-call | flops 40000000000 | bytes 1 | tf_op jit(solution)/shard_map/alive/pallas_call | solution.py:425
  8.8 0.1 stack.23.scalars
  8.9 0.0 copy-start.5
  8.9 0.0 copy-start.6
  8.9 3.5 %collective-permute-done.refs_0_ = s32[1,4,3]{2,1,0:T(4,128)S(1)} collective-permute-done((s32[1,4,3]{2,1,0:T(4,128)S(1)}, s32[1,4,3]{2,1,0:T(4,128)S(1)}, u32[]{:S(2)}, u32[]{:S(2)}) %collective-permute-start) | collective-permute-done | bytes 80 | tf_op jit(solution)/shard_map/ppermute | solution.py:435
  12.4 0.8 pick.1
  13.2 0.4 collective-permute-start.3
  13.6 4.0 %collective-permute-start.5 = (bf16[32,1536]{1,0:T(8,128)(2,1)S(1)}, bf16[32,1536]{1,0:T(8,128)(2,1)S(1)}, u32[]{:S(2)}, u32[]{:S(2)}) collective-permute-start(bf16[32,1536]{1,0:T(8,128)(2,1)S(1)} %get-tuple-element.77), channel_id=1, source_target_pairs={{0,2},{2,0},{4,6},{6,4},{1,3},{3,1},{5,7},{7,5},{8,10},{10,8},{12,... | collective-permute-start | bytes 294920 | tf_op jit(solution)/shard_map/ppermute | solution.py:452
  17.7 4.1 %project.1 = (bf16[1536,256]{1,0:T(8,128)(2,1)S(1)}, bf16[256,384]{1,0:T(8,128)(2,1)S(1)}, bf16[256,384]{1,0:T(8,128)(2,1)S(1)}, bf16[256,1536]{1,0:T(8,128)(2,1...) custom-call(s32[5]{0:T(128)S(1)} %stack.23.scalars, ...), custom_call_target="tpu_custom_call" | custom-call | flops 1 | bytes 1 | tf_op jit(solution)/shard_map/project/pallas_call | solution.py:454
  21.9 0.4 collective-permute-done.4.refs_1_
  22.3 0.1 collective-permute-start.8
  22.4 0.4 collective-permute-start.9
  22.8 0.1 collective-permute-start.10
  22.9 0.7 collective-permute-done.8.refs_3_
  23.6 0.2 collective-permute-done.9.refs_4_
  23.7 0.4 collective-permute-done.10.refs_5_
  24.1 3.2 %attention_forward.1 = (bf16[1536,192]{1,0:T(8,128)(2,1)S(1)}, bf16[192,384]{1,0:T(8,128)(2,1)S(1)}, bf16[192,384]{1,0:T(8,128)(2,1)S(1)}, f32[3,64,512]{2,1,0:T...) custom-call(s32[5]{0:T(128)S(1)} %stack.23.scalars, ...), custom_call_target="tpu_custom_call" | custom-call | flops 1 | bytes 1 | tf_op jit(solution)/shard_map/attention_forward/pallas_call | solution.py:490
  27.3 0.2 collective-permute-start.11
  27.5 1.6 %attention_backward.1 = (bf16[256,384]{1,0:T(8,128)(2,1)S(1)}, bf16[448,384]{1,0:T(8,128)(2,1)S(1)}) custom-call(bf16[3,512,128]{2,1,0:T(8,128)(2,1)S(1)} %get-tuple-element.84.refs_6_.query_stack, bf16[3,512,128]{2,1,0:T(8,128)(2,1)S(1)} %get-tuple-element.85.refs_7_.grad_stack, f32[3,64,512]{2,1,0:T(8,128)S(1)} %get-tuple-element.89.dprob_own, ...), custom_call_target="tpu_custom_call" | custom-call | flops 1 | bytes 1 | tf_op jit(solution)/shard_map/attention_backward/pallas_call | solution.py:478
  29.1 1.8 %grad_value_out.1 = (bf16[2,2,2,48,1536]{4,3,2,1,0:T(8,128)(2,1)S(1)}, f32[2,2,2,48,1536]{4,3,2,1,0:T(8,128)S(1)}) custom-call(s32[5]{0:T(128)S(1)} %stack.23.scalars, bf16[1536,256]{1,0:T(8,128)(2,1)S(1)} %get-tuple-element.79.normed_t, bf16[1536,192]{1,0:T(8,128)(2,1)S(1)} %get-tuple-element.88.normed_far_t, ...), custom_call_target="tpu_custom_call" | custom-call | flops 1 | bytes 1 | tf_op jit(solution)/shard_map/grad_value_out/pallas_call | solution.py:478
  30.9 0.4 collective-permute-start.22
  31.3 1.9 %grad_query_key.1 = (bf16[384,384]{1,0:T(8,128)(2,1)S(1)}, bf16[384,384]{1,0:T(8,128)(2,1)S(1)}, bf16[384,384]{1,0:T(8,128)(2,1)S(1)}, bf16[384,384]{1,0:T(8,128...) custom-call(s32[5]{0:T(128)S(1)} %stack.23.scalars, ...), custom_call_target="tpu_custom_call" | custom-call | flops 1 | bytes 1 | tf_op jit(solution)/shard_map/grad_query_key/pallas_call | solution.py:478
  33.2 1.6 %collective-permute-start.13 = (bf16[384,384]{1,0:T(8,128)(2,1)S(1)}, bf16[384,384]{1,0:T(8,128)(2,1)S(1)}, u32[]{:S(2)}, u32[]{:S(2)}) collective-permute-start(bf16[384,384]{1,0:T(8,128)(2,1)S(1)} %get-tuple-element.105), channel_id=1, source_target_pairs={{0,8},{8,0},{16,24},{24,16},{1,9},{9,1},{17,25},{25,17},{2,10},{10... | collective-permute-start | bytes 884744 | tf_op jit(solution)/shard_map/ppermute | solution.py:528
  34.8 1.5 %collective-permute-start.14 = (bf16[384,384]{1,0:T(8,128)(2,1)S(1)}, bf16[384,384]{1,0:T(8,128)(2,1)S(1)}, u32[]{:S(2)}, u32[]{:S(2)}) collective-permute-start(bf16[384,384]{1,0:T(8,128)(2,1)S(1)} %get-tuple-element.107), channel_id=1, source_target_pairs={{0,16},{8,24},{16,0},{24,8},{1,17},{9,25},{17,1},{25,9},{2,18},{10... | collective-permute-start | bytes 884744 | tf_op jit(solution)/shard_map/ppermute | solution.py:528
  36.3 0.5 collective-permute-start.12
  36.8 0.5 collective-permute-start.16
  37.3 5.8 %collective-permute-done.13.q_got = bf16[384,384]{1,0:T(8,128)(2,1)S(1)} collective-permute-done((bf16[384,384]{1,0:T(8,128)(2,1)S(1)}, bf16[384,384]{1,0:T(8,128)(2,1)S(1)}, u32[]{:S(2)}, u32[]{:S(2)}) %collective-permute-start.13) | collective-permute-done | bytes 294944 | tf_op jit(solution)/shard_map/ppermute | solution.py:528
  43.2 1.5 %collective-permute-done.14.k_got = bf16[384,384]{1,0:T(8,128)(2,1)S(1)} collective-permute-done((bf16[384,384]{1,0:T(8,128)(2,1)S(1)}, bf16[384,384]{1,0:T(8,128)(2,1)S(1)}, u32[]{:S(2)}, u32[]{:S(2)}) %collective-permute-start.14) | collective-permute-done | bytes 294944 | tf_op jit(solution)/shard_map/ppermute | solution.py:528
  44.7 0.1 first_sum_query_key.1
  44.8 1.6 %collective-permute-start.15 = (bf16[384,384]{1,0:T(8,128)(2,1)S(1)}, bf16[384,384]{1,0:T(8,128)(2,1)S(1)}, u32[]{:S(2)}, u32[]{:S(2)}) collective-permute-start(bf16[384,384]{1,0:T(8,128)(2,1)S(1)} %get-tuple-element.108), channel_id=1, source_target_pairs={{0,16},{8,24},{16,0},{24,8},{1,17},{9,25},{17,1},{25,9},{2,18},{10... | collective-permute-start | bytes 884744 | tf_op jit(solution)/shard_map/ppermute | solution.py:536
  46.4 0.5 collective-permute-start.17
  46.9 2.6 %collective-permute-done.12.q_first = bf16[384,384]{1,0:T(8,128)(2,1)S(1)} collective-permute-done((bf16[384,384]{1,0:T(8,128)(2,1)S(1)}, bf16[384,384]{1,0:T(8,128)(2,1)S(1)}, u32[]{:S(2)}, u32[]{:S(2)}) %collective-permute-start.12) | collective-permute-done | bytes 294944 | tf_op jit(solution)/shard_map/ppermute | solution.py:528
  49.5 1.5 %collective-permute-done.16.k_first = bf16[384,384]{1,0:T(8,128)(2,1)S(1)} collective-permute-done((bf16[384,384]{1,0:T(8,128)(2,1)S(1)}, bf16[384,384]{1,0:T(8,128)(2,1)S(1)}, u32[]{:S(2)}, u32[]{:S(2)}) %collective-permute-start.16) | collective-permute-done | bytes 294944 | tf_op jit(solution)/shard_map/ppermute | solution.py:528
  51.0 5.1 %collective-permute-done.15.q_second = bf16[384,384]{1,0:T(8,128)(2,1)S(1)} collective-permute-done((bf16[384,384]{1,0:T(8,128)(2,1)S(1)}, bf16[384,384]{1,0:T(8,128)(2,1)S(1)}, u32[]{:S(2)}, u32[]{:S(2)}) %collective-permute-start.15) | collective-permute-done | bytes 294944 | tf_op jit(solution)/shard_map/ppermute | solution.py:536
  56.1 0.8 second_sum_query_key.1
  56.9 1.8 %collective-permute-start.18 = (bf16[2,96,768]{2,1,0:T(8,128)(2,1)S(1)}, bf16[2,96,768]{2,1,0:T(8,128)(2,1)S(1)}, u32[]{:S(2)}, u32[]{:S(2)}) collective-permute-start(bf16[2,96,768]{2,1,0:T(8,128)(2,1)S(1)} %get-tuple-element.112), channel_id=1, source_target_pairs={{0,2},{2,0},{4,6},{6,4},{1,3},{3,1},{5,7},{7,5},{8,10},{10,8},{12,... | collective-permute-start | bytes 884744 | tf_op jit(solution)/shard_map/ppermute | solution.py:600
  58.7 1.1 %collective-permute-done.22.got = bf16[2,2,2,48,1536]{4,3,2,1,0:T(8,128)(2,1)S(1)} collective-permute-done((bf16[2,2,2,48,1536]{4,3,2,1,0:T(8,128)(2,1)S(1)}, bf16[2,2,2,48,1536]{4,3,2,1,0:T(8,128)(2,1)S(1)}, u32[]{:S(2)}, u32[]{:S(2)}) %collective-permute-start.22) | collective-permute-done | bytes 1179680 | tf_op jit(solution)/shard_map/ppermute | solution.py:576
  59.8 0.2 view_sum_value_out.1
  60.0 1.6 %collective-permute-start.23 = (bf16[2,2,48,768]{3,2,1,0:T(8,128)(2,1)S(1)}, bf16[2,2,48,768]{3,2,1,0:T(8,128)(2,1)S(1)}, u32[]{:S(2)}, u32[]{:S(2)}) collective-permute-start(bf16[2,2,48,768]{3,2,1,0:T(8,128)(2,1)S(1)} %get-tuple-element.125), channel_id=1, source_target_pairs={{0,8},{8,0},{16,24},{24,16},{1,9},{9,1},{17,25},{25,17},{2,10},{10... | collective-permute-start | bytes 884744 | tf_op jit(solution)/shard_map/ppermute | solution.py:528
  61.5 1.5 %collective-permute-start.24 = (bf16[2,2,48,768]{3,2,1,0:T(8,128)(2,1)S(1)}, bf16[2,2,48,768]{3,2,1,0:T(8,128)(2,1)S(1)}, u32[]{:S(2)}, u32[]{:S(2)}) collective-permute-start(bf16[2,2,48,768]{3,2,1,0:T(8,128)(2,1)S(1)} %get-tuple-element.127), channel_id=1, source_target_pairs={{0,16},{8,24},{16,0},{24,8},{1,17},{9,25},{17,1},{25,9},{2,18},{10... | collective-permute-start | bytes 884744 | tf_op jit(solution)/shard_map/ppermute | solution.py:528
  63.0 2.5 %collective-permute-done.18.refs_1_ = bf16[2,96,768]{2,1,0:T(8,128)(2,1)S(1)} collective-permute-done((bf16[2,96,768]{2,1,0:T(8,128)(2,1)S(1)}, bf16[2,96,768]{2,1,0:T(8,128)(2,1)S(1)}, u32[]{:S(2)}, u32[]{:S(2)}) %collective-permute-start.18) | collective-permute-done | bytes 294944 | tf_op jit(solution)/shard_map/ppermute | solution.py:600
  65.5 0.6 last_parts_query_key.1
  66.2 0.1 collective-permute-start.20
  66.3 1.7 %collective-permute-start.19 = (bf16[48,768]{1,0:T(8,128)(2,1)S(1)}, bf16[48,768]{1,0:T(8,128)(2,1)S(1)}, u32[]{:S(2)}, u32[]{:S(2)}) collective-permute-start(bf16[48,768]{1,0:T(8,128)(2,1)S(1)} %get-tuple-element.114), channel_id=1, source_target_pairs={{0,4},{2,6},{4,0},{6,2},{1,5},{3,7},{5,1},{7,3},{8,12},{10,14},{12... | collective-permute-start | bytes 221192 | tf_op jit(solution)/shard_map/ppermute | solution.py:562
  67.9 1.1 %collective-permute-start.21 = (bf16[48,768]{1,0:T(8,128)(2,1)S(1)}, bf16[48,768]{1,0:T(8,128)(2,1)S(1)}, u32[]{:S(2)}, u32[]{:S(2)}) collective-permute-start(bf16[48,768]{1,0:T(8,128)(2,1)S(1)} %get-tuple-element.116), channel_id=1, source_target_pairs={{0,5},{1,4},{2,7},{3,6},{4,1},{5,0},{6,3},{7,2},{8,13},{9,12},{10,... | collective-permute-start | bytes 221192 | tf_op jit(solution)/shard_map/ppermute | solution.py:563
  69.0 0.1 collective-permute-done.24.y_got
  69.1 0.1 first_sum_value_out.1
  69.2 1.4 %collective-permute-start.25 = (bf16[2,48,768]{2,1,0:T(8,128)(2,1)S(1)}, bf16[2,48,768]{2,1,0:T(8,128)(2,1)S(1)}, u32[]{:S(2)}, u32[]{:S(2)}) collective-permute-start(bf16[2,48,768]{2,1,0:T(8,128)(2,1)S(1)} %get-tuple-element.130), channel_id=1, source_target_pairs={{0,8},{8,0},{16,24},{24,16},{1,9},{9,1},{17,25},{25,17},{2,10},{10... | collective-permute-start | bytes 442376 | tf_op jit(solution)/shard_map/ppermute | solution.py:536
  70.7 1.5 %collective-permute-start.26 = (bf16[2,48,768]{2,1,0:T(8,128)(2,1)S(1)}, bf16[2,48,768]{2,1,0:T(8,128)(2,1)S(1)}, u32[]{:S(2)}, u32[]{:S(2)}) collective-permute-start(bf16[2,48,768]{2,1,0:T(8,128)(2,1)S(1)} %get-tuple-element.132), channel_id=1, source_target_pairs={{0,16},{8,24},{16,0},{24,8},{1,17},{9,25},{17,1},{25,9},{2,18},{10... | collective-permute-start | bytes 442376 | tf_op jit(solution)/shard_map/ppermute | solution.py:536
  72.2 3.2 %collective-permute-done.19.far_same = bf16[48,768]{1,0:T(8,128)(2,1)S(1)} collective-permute-done((bf16[48,768]{1,0:T(8,128)(2,1)S(1)}, bf16[48,768]{1,0:T(8,128)(2,1)S(1)}, u32[]{:S(2)}, u32[]{:S(2)}) %collective-permute-start.19) | collective-permute-done | bytes 73760 | tf_op jit(solution)/shard_map/ppermute | solution.py:562
  75.4 0.7 collective-permute-done.21.far_cross
  76.2 0.3 collective-permute-done.26.refs_3_
  76.5 0.6 last_parts_value_out.1
  77.1 0.1 collective-permute-start.28
  77.2 1.0 %collective-permute-start.27 = (bf16[24,1536]{1,0:T(8,128)(2,1)S(1)}, bf16[24,1536]{1,0:T(8,128)(2,1)S(1)}, u32[]{:S(2)}, u32[]{:S(2)}) collective-permute-start(bf16[24,1536]{1,0:T(8,128)(2,1)S(1)} %get-tuple-element.135), channel_id=1, source_target_pairs={{0,4},{2,6},{4,0},{6,2},{1,5},{3,7},{5,1},{7,3},{8,12},{10,14},{12... | collective-permute-start | bytes 221192 | tf_op jit(solution)/shard_map/ppermute | solution.py:562
  78.2 1.8 %collective-permute-start.29 = (bf16[24,1536]{1,0:T(8,128)(2,1)S(1)}, bf16[24,1536]{1,0:T(8,128)(2,1)S(1)}, u32[]{:S(2)}, u32[]{:S(2)}) collective-permute-start(bf16[24,1536]{1,0:T(8,128)(2,1)S(1)} %get-tuple-element.137), channel_id=1, source_target_pairs={{0,5},{1,4},{2,7},{3,6},{4,1},{5,0},{6,3},{7,2},{8,13},{9,12},{10,... | collective-permute-start | bytes 221192 | tf_op jit(solution)/shard_map/ppermute | solution.py:563
  80.0 1.3 %place_query_key.1 = (f32[48,768]{1,0:T(8,128)}, f32[48,768]{1,0:T(8,128)}) custom-call(s32[5]{0:T(128)S(1)} %stack.23.scalars, f32[48,768]{1,0:T(8,128)S(1)} %get-tuple-element.117.same, f32[48,768]{1,0:T(8,128)S(1)} %get-tuple-element.118.cross), custom_call_target="tpu_custom_call" | custom-call | flops 1 | bytes 1 | tf_op jit(solution)/shard_map/place_query_key/pallas_call | solution.py:478
  81.2 4.5 %collective-permute-done.27.far_same = bf16[24,1536]{1,0:T(8,128)(2,1)S(1)} collective-permute-done((bf16[24,1536]{1,0:T(8,128)(2,1)S(1)}, bf16[24,1536]{1,0:T(8,128)(2,1)S(1)}, u32[]{:S(2)}, u32[]{:S(2)}) %collective-permute-start.27) | collective-permute-done | bytes 73760 | tf_op jit(solution)/shard_map/ppermute | solution.py:562
  85.7 1.5 %collective-permute-done.29.far_cross = bf16[24,1536]{1,0:T(8,128)(2,1)S(1)} collective-permute-done((bf16[24,1536]{1,0:T(8,128)(2,1)S(1)}, bf16[24,1536]{1,0:T(8,128)(2,1)S(1)}, u32[]{:S(2)}, u32[]{:S(2)}) %collective-permute-start.29) | collective-permute-done | bytes 73760 | tf_op jit(solution)/shard_map/ppermute | solution.py:563
  87.2 1.3 %last_sum_value_out.1 = (f32[48,768]{1,0:T(8,128)}, f32[24,1536]{1,0:T(8,128)}) custom-call(s32[5]{0:T(128)S(1)} %stack.23.scalars, f32[24,1536]{1,0:T(8,128)S(1)} %get-tuple-element.134.mine, bf16[24,1536]{1,0:T(8,128)(2,1)S(1)} %collective-permute-done.27.far_same, f32[24,1536]{1,0:T(8,128)S(1)} %collective-permute-done.28.near_cross, ...), custom_call_target="tpu_custom_call" | custom-call | flops 1 | bytes 1 | tf_op jit(solution)/shard_map/last_sum_value_out/pallas_call | solution.py:478
  (30 shorter events, 0.1 us)
Async XLA Ops:
  1.4 7.5 %collective-permute-start.2 = (s32[1,4,3]{2,1,0:T(4,128)S(1)}, s32[1,4,3]{2,1,0:T(4,128)S(1)}, u32[]{:S(2)}, u32[]{:S(2)}) collective-permute-start(s32[1,4,3]{2,1,0:T(4,128)S(1)} %copy.13.partners), channel_id=1, source_target_pairs={{0,2},{2,0},{4,6},{6,4},{1,3},{3,1},{5,7},{7,5},{8,10},{10,8},{12,... | collective-permute-start | bytes 152 | tf_op jit(solution)/shard_map/ppermute | solution.py:435
  4.4 4.5 %collective-permute-start.1 = (s32[1,4,3]{2,1,0:T(4,128)S(1)}, s32[1,4,3]{2,1,0:T(4,128)S(1)}, u32[]{:S(2)}, u32[]{:S(2)}) collective-permute-start(s32[1,4,3]{2,1,0:T(4,128)S(1)} %copy.13.partners), channel_id=1, source_target_pairs={{0,4},{2,6},{4,0},{6,2},{1,5},{3,7},{5,1},{7,3},{8,12},{10,14},{12... | collective-permute-start | bytes 152 | tf_op jit(solution)/shard_map/ppermute | solution.py:435
  7.0 5.4 %collective-permute-start = (s32[1,4,3]{2,1,0:T(4,128)S(1)}, s32[1,4,3]{2,1,0:T(4,128)S(1)}, u32[]{:S(2)}, u32[]{:S(2)}) collective-permute-start(s32[1,4,3]{2,1,0:T(4,128)S(1)} %copy.13.partners), channel_id=1, source_target_pairs={{0,6},{2,4},{4,2},{6,0},{1,7},{3,5},{5,3},{7,1},{8,14},{10,12},{12... | collective-permute-start | bytes 152 | tf_op jit(solution)/shard_map/ppermute | solution.py:435
  7.0 10.6 %collective-permute-start.6 = (bf16[4,32,1536]{2,1,0:T(8,128)(2,1)}, bf16[4,32,1536]{2,1,0:T(8,128)(2,1)S(1)}, u32[]{:S(2)}, u32[]{:S(2)}) collective-permute-start(bf16[4,32,1536]{2,1,0:T(8,128)(2,1)} %bitcast.7), channel_id=1, source_target_pairs={{0,1},{1,0},{2,3},{3,2},{4,5},{5,4},{6,7},{7,6},{8,9},{9,8},{10,11... | collective-permute-start | bytes 1179656 | tf_op jit(solution)/shard_map/ppermute | solution.py:440
  7.0 10.6 %collective-permute-start.7 = (bf16[4,32,1536]{2,1,0:T(8,128)(2,1)}, bf16[4,32,1536]{2,1,0:T(8,128)(2,1)S(1)}, u32[]{:S(2)}, u32[]{:S(2)}) collective-permute-start(bf16[4,32,1536]{2,1,0:T(8,128)(2,1)} %bitcast.10), channel_id=1, source_target_pairs={{0,1},{1,0},{2,3},{3,2},{4,5},{5,4},{6,7},{7,6},{8,9},{9,8},{10,11... | collective-permute-start | bytes 1179656 | tf_op jit(solution)/shard_map/ppermute | solution.py:441
  7.5 4.9 %copy-start.4 = (bf16[1,4,1,32,1536]{4,3,2,1,0:T(8,128)(2,1)S(1)}, bf16[1,4,1,32,1536]{4,3,2,1,0:T(8,128)(2,1)}, u32[]{:S(2)}) copy-start(bf16[1,4,1,32,1536]{4,3,2,1,0:T(8,128)(2,1)} %param.10) | copy-start | bytes 1179652
  8.8 8.8 %copy-start = (bf16[1536,768]{1,0:T(8,128)(2,1)S(1)}, bf16[1536,768]{1,0:T(8,128)(2,1)}, u32[]{:S(2)}) copy-start(bf16[1536,768]{1,0:T(8,128)(2,1)} %refs_11_.1) | copy-start | bytes 7077892
  8.9 8.8 %copy-start.1 = (bf16[1536,768]{1,0:T(8,128)(2,1)S(1)}, bf16[1536,768]{1,0:T(8,128)(2,1)}, u32[]{:S(2)}) copy-start(bf16[1536,768]{1,0:T(8,128)(2,1)} %refs_12_.1) | copy-start | bytes 7077892
  8.9 8.8 %copy-start.2 = (bf16[1536,768]{1,0:T(8,128)(2,1)S(1)}, bf16[1536,768]{1,0:T(8,128)(2,1)}, u32[]{:S(2)}) copy-start(bf16[1536,768]{1,0:T(8,128)(2,1)} %w_query.1) | copy-start | bytes 7077892
  8.9 8.8 %copy-start.3 = (bf16[768,1536]{1,0:T(8,128)(2,1)S(1)}, bf16[768,1536]{1,0:T(8,128)(2,1)}, u32[]{:S(2)}) copy-start(bf16[768,1536]{1,0:T(8,128)(2,1)} %w_out.1) | copy-start | bytes 7077892
  8.9 8.8 %copy-start.5 = (bf16[1,4,1,32,1536]{4,3,2,1,0:T(8,128)(2,1)S(1)}, bf16[1,4,1,32,1536]{4,3,2,1,0:T(8,128)(2,1)}, u32[]{:S(2)}) copy-start(bf16[1,4,1,32,1536]{4,3,2,1,0:T(8,128)(2,1)} %param.18) | copy-start | bytes 1179652
  8.9 8.8 %copy-start.6 = (bf16[9,1536]{1,0:T(8,128)(2,1)S(1)}, bf16[9,1536]{1,0:T(8,128)(2,1)}, u32[]{:S(2)}) copy-start(bf16[9,1536]{1,0:T(8,128)(2,1)} %taps.1) | copy-start | bytes 82948
  8.9 8.8 %copy-start.7 = (f32[1536]{0:T(1024)S(1)}, f32[1536]{0:T(1024)}, u32[]{:S(2)}) copy-start(f32[1536]{0:T(1024)} %refs_10_.1) | copy-start | bytes 18436
  13.2 8.7 %collective-permute-start.3 = (bf16[32,1536]{1,0:T(8,128)(2,1)S(1)}, bf16[32,1536]{1,0:T(8,128)(2,1)S(1)}, u32[]{:S(2)}, u32[]{:S(2)}) collective-permute-start(bf16[32,1536]{1,0:T(8,128)(2,1)S(1)} %get-tuple-element.75), channel_id=1, source_target_pairs={{0,6},{2,4},{4,2},{6,0},{1,7},{3,5},{5,3},{7,1},{8,14},{10,12},{12... | collective-permute-start | bytes 294920 | tf_op jit(solution)/shard_map/ppermute | solution.py:452
  13.6 8.7 %collective-permute-start.4 = (bf16[32,1536]{1,0:T(8,128)(2,1)S(1)}, bf16[32,1536]{1,0:T(8,128)(2,1)S(1)}, u32[]{:S(2)}, u32[]{:S(2)}) collective-permute-start(bf16[32,1536]{1,0:T(8,128)(2,1)S(1)} %get-tuple-element.76), channel_id=1, source_target_pairs={{0,4},{2,6},{4,0},{6,2},{1,5},{3,7},{5,1},{7,3},{8,12},{10,14},{12... | collective-permute-start | bytes 294920 | tf_op jit(solution)/shard_map/ppermute | solution.py:452
  13.6 8.7 %collective-permute-start.5 = (bf16[32,1536]{1,0:T(8,128)(2,1)S(1)}, bf16[32,1536]{1,0:T(8,128)(2,1)S(1)}, u32[]{:S(2)}, u32[]{:S(2)}) collective-permute-start(bf16[32,1536]{1,0:T(8,128)(2,1)S(1)} %get-tuple-element.77), channel_id=1, source_target_pairs={{0,2},{2,0},{4,6},{6,4},{1,3},{3,1},{5,7},{7,5},{8,10},{10,8},{12,... | collective-permute-start | bytes 294920 | tf_op jit(solution)/shard_map/ppermute | solution.py:452
  22.3 1.3 %collective-permute-start.8 = (bf16[32,1536]{1,0:T(8,128)(2,1)S(1)}, bf16[32,1536]{1,0:T(8,128)(2,1)S(1)}, u32[]{:S(2)}, u32[]{:S(2)}) collective-permute-start(bf16[32,1536]{1,0:T(8,128)(2,1)S(1)} %collective-permute-done.3.refs_0_), channel_id=1, source_target_pairs={{0,1},{1,0},{2,3},{3,2},{4,5},{5,4},{6,7},{7,6},{8,9},{9,8},{10,11... | collective-permute-start | bytes 294920 | tf_op jit(solution)/shard_map/ppermute | solution.py:475
  22.4 1.4 %collective-permute-start.9 = (bf16[32,1536]{1,0:T(8,128)(2,1)S(1)}, bf16[32,1536]{1,0:T(8,128)(2,1)S(1)}, u32[]{:S(2)}, u32[]{:S(2)}) collective-permute-start(bf16[32,1536]{1,0:T(8,128)(2,1)S(1)} %collective-permute-done.4.refs_1_), channel_id=1, source_target_pairs={{0,1},{1,0},{2,3},{3,2},{4,5},{5,4},{6,7},{7,6},{8,9},{9,8},{10,11... | collective-permute-start | bytes 294920 | tf_op jit(solution)/shard_map/ppermute | solution.py:475
  22.8 1.3 %collective-permute-start.10 = (bf16[32,1536]{1,0:T(8,128)(2,1)S(1)}, bf16[32,1536]{1,0:T(8,128)(2,1)S(1)}, u32[]{:S(2)}, u32[]{:S(2)}) collective-permute-start(bf16[32,1536]{1,0:T(8,128)(2,1)S(1)} %collective-permute-done.5.refs_2_), channel_id=1, source_target_pairs={{0,1},{1,0},{2,3},{3,2},{4,5},{5,4},{6,7},{7,6},{8,9},{9,8},{10,11... | collective-permute-start | bytes 294920 | tf_op jit(solution)/shard_map/ppermute | solution.py:475
  27.3 1.8 %collective-permute-start.11 = (bf16[384,256]{1,0:T(8,128)(2,1)S(1)}, bf16[384,256]{1,0:T(8,128)(2,1)S(1)}, u32[]{:S(2)}, u32[]{:S(2)}) collective-permute-start(bf16[384,256]{1,0:T(8,128)(2,1)S(1)} %get-tuple-element.99.mine), channel_id=1, source_target_pairs={{0,1},{1,0},{2,3},{3,2},{4,5},{5,4},{6,7},{7,6},{8,9},{9,8},{10,11... | collective-permute-start | bytes 589832 | tf_op jit(solution)/shard_map/ppermute | solution.py:510
  30.9 28.9 %collective-permute-start.22 = (bf16[2,2,2,48,1536]{4,3,2,1,0:T(8,128)(2,1)S(1)}, bf16[2,2,2,48,1536]{4,3,2,1,0:T(8,128)(2,1)S(1)}, u32[]{:S(2)}, u32[]{:S(2)}) collective-permute-start(bf16[2,2,2,48,1536]{4,3,2,1,0:T(8,128)(2,1)S(1)} %get-tuple-element.101), channel_id=1, source_target_pairs={{0,2},{2,0},{4,6},{6,4},{1,3},{3,1},{5,7},{7,5},{8,10},{10,8},{12,... | collective-permute-start | bytes 3538952 | tf_op jit(solution)/shard_map/ppermute | solution.py:576
  33.2 9.9 %collective-permute-start.13 = (bf16[384,384]{1,0:T(8,128)(2,1)S(1)}, bf16[384,384]{1,0:T(8,128)(2,1)S(1)}, u32[]{:S(2)}, u32[]{:S(2)}) collective-permute-start(bf16[384,384]{1,0:T(8,128)(2,1)S(1)} %get-tuple-element.105), channel_id=1, source_target_pairs={{0,8},{8,0},{16,24},{24,16},{1,9},{9,1},{17,25},{25,17},{2,10},{10... | collective-permute-start | bytes 884744 | tf_op jit(solution)/shard_map/ppermute | solution.py:528
  34.8 9.9 %collective-permute-start.14 = (bf16[384,384]{1,0:T(8,128)(2,1)S(1)}, bf16[384,384]{1,0:T(8,128)(2,1)S(1)}, u32[]{:S(2)}, u32[]{:S(2)}) collective-permute-start(bf16[384,384]{1,0:T(8,128)(2,1)S(1)} %get-tuple-element.107), channel_id=1, source_target_pairs={{0,16},{8,24},{16,0},{24,8},{1,17},{9,25},{17,1},{25,9},{2,18},{10... | collective-permute-start | bytes 884744 | tf_op jit(solution)/shard_map/ppermute | solution.py:528
  36.3 13.2 %collective-permute-start.12 = (bf16[384,384]{1,0:T(8,128)(2,1)S(1)}, bf16[384,384]{1,0:T(8,128)(2,1)S(1)}, u32[]{:S(2)}, u32[]{:S(2)}) collective-permute-start(bf16[384,384]{1,0:T(8,128)(2,1)S(1)} %get-tuple-element.104), channel_id=1, source_target_pairs={{0,8},{8,0},{16,24},{24,16},{1,9},{9,1},{17,25},{25,17},{2,10},{10... | collective-permute-start | bytes 884744 | tf_op jit(solution)/shard_map/ppermute | solution.py:528
  36.8 14.2 %collective-permute-start.16 = (bf16[384,384]{1,0:T(8,128)(2,1)S(1)}, bf16[384,384]{1,0:T(8,128)(2,1)S(1)}, u32[]{:S(2)}, u32[]{:S(2)}) collective-permute-start(bf16[384,384]{1,0:T(8,128)(2,1)S(1)} %get-tuple-element.109), channel_id=1, source_target_pairs={{0,16},{8,24},{16,0},{24,8},{1,17},{9,25},{17,1},{25,9},{2,18},{10... | collective-permute-start | bytes 884744 | tf_op jit(solution)/shard_map/ppermute | solution.py:528
  44.8 11.3 %collective-permute-start.15 = (bf16[384,384]{1,0:T(8,128)(2,1)S(1)}, bf16[384,384]{1,0:T(8,128)(2,1)S(1)}, u32[]{:S(2)}, u32[]{:S(2)}) collective-permute-start(bf16[384,384]{1,0:T(8,128)(2,1)S(1)} %get-tuple-element.108), channel_id=1, source_target_pairs={{0,16},{8,24},{16,0},{24,8},{1,17},{9,25},{17,1},{25,9},{2,18},{10... | collective-permute-start | bytes 884744 | tf_op jit(solution)/shard_map/ppermute | solution.py:536
  46.4 9.8 %collective-permute-start.17 = (bf16[384,384]{1,0:T(8,128)(2,1)S(1)}, bf16[384,384]{1,0:T(8,128)(2,1)S(1)}, u32[]{:S(2)}, u32[]{:S(2)}) collective-permute-start(bf16[384,384]{1,0:T(8,128)(2,1)S(1)} %get-tuple-element.110), channel_id=1, source_target_pairs={{0,8},{8,0},{16,24},{24,16},{1,9},{9,1},{17,25},{25,17},{2,10},{10... | collective-permute-start | bytes 884744 | tf_op jit(solution)/shard_map/ppermute | solution.py:536
  56.9 8.6 %collective-permute-start.18 = (bf16[2,96,768]{2,1,0:T(8,128)(2,1)S(1)}, bf16[2,96,768]{2,1,0:T(8,128)(2,1)S(1)}, u32[]{:S(2)}, u32[]{:S(2)}) collective-permute-start(bf16[2,96,768]{2,1,0:T(8,128)(2,1)S(1)} %get-tuple-element.112), channel_id=1, source_target_pairs={{0,2},{2,0},{4,6},{6,4},{1,3},{3,1},{5,7},{7,5},{8,10},{10,8},{12,... | collective-permute-start | bytes 884744 | tf_op jit(solution)/shard_map/ppermute | solution.py:600
  60.0 9.1 %collective-permute-start.23 = (bf16[2,2,48,768]{3,2,1,0:T(8,128)(2,1)S(1)}, bf16[2,2,48,768]{3,2,1,0:T(8,128)(2,1)S(1)}, u32[]{:S(2)}, u32[]{:S(2)}) collective-permute-start(bf16[2,2,48,768]{3,2,1,0:T(8,128)(2,1)S(1)} %get-tuple-element.125), channel_id=1, source_target_pairs={{0,8},{8,0},{16,24},{24,16},{1,9},{9,1},{17,25},{25,17},{2,10},{10... | collective-permute-start | bytes 884744 | tf_op jit(solution)/shard_map/ppermute | solution.py:528
  61.5 7.6 %collective-permute-start.24 = (bf16[2,2,48,768]{3,2,1,0:T(8,128)(2,1)S(1)}, bf16[2,2,48,768]{3,2,1,0:T(8,128)(2,1)S(1)}, u32[]{:S(2)}, u32[]{:S(2)}) collective-permute-start(bf16[2,2,48,768]{3,2,1,0:T(8,128)(2,1)S(1)} %get-tuple-element.127), channel_id=1, source_target_pairs={{0,16},{8,24},{16,0},{24,8},{1,17},{9,25},{17,1},{25,9},{2,18},{10... | collective-permute-start | bytes 884744 | tf_op jit(solution)/shard_map/ppermute | solution.py:528
  66.2 10.0 %collective-permute-start.20 = (f32[48,768]{1,0:T(8,128)S(1)}, f32[48,768]{1,0:T(8,128)S(1)}, u32[]{:S(2)}, u32[]{:S(2)}) collective-permute-start(f32[48,768]{1,0:T(8,128)S(1)} %get-tuple-element.115), channel_id=1, source_target_pairs={{0,1},{1,0},{2,3},{3,2},{4,5},{5,4},{6,7},{7,6},{8,9},{9,8},{10,11... | collective-permute-start | bytes 442376 | tf_op jit(solution)/shard_map/ppermute | solution.py:564
  66.3 9.2 %collective-permute-start.19 = (bf16[48,768]{1,0:T(8,128)(2,1)S(1)}, bf16[48,768]{1,0:T(8,128)(2,1)S(1)}, u32[]{:S(2)}, u32[]{:S(2)}) collective-permute-start(bf16[48,768]{1,0:T(8,128)(2,1)S(1)} %get-tuple-element.114), channel_id=1, source_target_pairs={{0,4},{2,6},{4,0},{6,2},{1,5},{3,7},{5,1},{7,3},{8,12},{10,14},{12... | collective-permute-start | bytes 221192 | tf_op jit(solution)/shard_map/ppermute | solution.py:562
  67.9 8.2 %collective-permute-start.21 = (bf16[48,768]{1,0:T(8,128)(2,1)S(1)}, bf16[48,768]{1,0:T(8,128)(2,1)S(1)}, u32[]{:S(2)}, u32[]{:S(2)}) collective-permute-start(bf16[48,768]{1,0:T(8,128)(2,1)S(1)} %get-tuple-element.116), channel_id=1, source_target_pairs={{0,5},{1,4},{2,7},{3,6},{4,1},{5,0},{6,3},{7,2},{8,13},{9,12},{10,... | collective-permute-start | bytes 221192 | tf_op jit(solution)/shard_map/ppermute | solution.py:563
  69.2 6.9 %collective-permute-start.25 = (bf16[2,48,768]{2,1,0:T(8,128)(2,1)S(1)}, bf16[2,48,768]{2,1,0:T(8,128)(2,1)S(1)}, u32[]{:S(2)}, u32[]{:S(2)}) collective-permute-start(bf16[2,48,768]{2,1,0:T(8,128)(2,1)S(1)} %get-tuple-element.130), channel_id=1, source_target_pairs={{0,8},{8,0},{16,24},{24,16},{1,9},{9,1},{17,25},{25,17},{2,10},{10... | collective-permute-start | bytes 442376 | tf_op jit(solution)/shard_map/ppermute | solution.py:536
  70.7 5.8 %collective-permute-start.26 = (bf16[2,48,768]{2,1,0:T(8,128)(2,1)S(1)}, bf16[2,48,768]{2,1,0:T(8,128)(2,1)S(1)}, u32[]{:S(2)}, u32[]{:S(2)}) collective-permute-start(bf16[2,48,768]{2,1,0:T(8,128)(2,1)S(1)} %get-tuple-element.132), channel_id=1, source_target_pairs={{0,16},{8,24},{16,0},{24,8},{1,17},{9,25},{17,1},{25,9},{2,18},{10... | collective-permute-start | bytes 442376 | tf_op jit(solution)/shard_map/ppermute | solution.py:536
  77.1 10.1 %collective-permute-start.28 = (f32[24,1536]{1,0:T(8,128)S(1)}, f32[24,1536]{1,0:T(8,128)S(1)}, u32[]{:S(2)}, u32[]{:S(2)}) collective-permute-start(f32[24,1536]{1,0:T(8,128)S(1)} %get-tuple-element.136), channel_id=1, source_target_pairs={{0,1},{1,0},{2,3},{3,2},{4,5},{5,4},{6,7},{7,6},{8,9},{9,8},{10,11... | collective-permute-start | bytes 442376 | tf_op jit(solution)/shard_map/ppermute | solution.py:564
  77.2 8.5 %collective-permute-start.27 = (bf16[24,1536]{1,0:T(8,128)(2,1)S(1)}, bf16[24,1536]{1,0:T(8,128)(2,1)S(1)}, u32[]{:S(2)}, u32[]{:S(2)}) collective-permute-start(bf16[24,1536]{1,0:T(8,128)(2,1)S(1)} %get-tuple-element.135), channel_id=1, source_target_pairs={{0,4},{2,6},{4,0},{6,2},{1,5},{3,7},{5,1},{7,3},{8,12},{10,14},{12... | collective-permute-start | bytes 221192 | tf_op jit(solution)/shard_map/ppermute | solution.py:562
  78.2 9.1 %collective-permute-start.29 = (bf16[24,1536]{1,0:T(8,128)(2,1)S(1)}, bf16[24,1536]{1,0:T(8,128)(2,1)S(1)}, u32[]{:S(2)}, u32[]{:S(2)}) collective-permute-start(bf16[24,1536]{1,0:T(8,128)(2,1)S(1)} %get-tuple-element.137), channel_id=1, source_target_pairs={{0,5},{1,4},{2,7},{3,6},{4,1},{5,0},{6,3},{7,2},{8,13},{9,12},{10,... | collective-permute-start | bytes 221192 | tf_op jit(solution)/shard_map/ppermute | solution.py:563

commit v20 on v19

--- a/solution.py
+++ b/solution.py
@@ -257,15 +257,15 @@
         later[...] = (keep[1] + got[...].astype(jnp.float32)).astype(jnp.bfloat16)
 
 
-def value_out_kernel(scalars, normed_t, normed_far_t, dvalue, mine, theirs, upstream, send, keep):
+def value_out_kernel(sent, scalars, normed_t, normed_far_t, dvalue, mine, theirs, upstream, target):
     row, x, y = scalars[0], scalars[3], scalars[4]
-    odd = lax.rem(scalars[1], jnp.int32(2)) == 1
-    _, _, pairs, size, _ = send.shape
+    take_second = lax.rem(scalars[1], jnp.int32(2)) == (0 if sent else 1)
+    _, _, pairs, size, _ = target.shape
     half, quarter = upstream.shape[1] // 2, normed_t.shape[0] // 4
     value_right = dvalue[...]
     lanes = value_right.shape[1]
     places = [(dy, dx, pair) for dy in range(2) for dx in range(2) for pair in range(pairs)]
-    rows = {"send": ([], [], []), "keep": ([], [], [])}
+    rows = ([], [], [])
     for dy in range(2):
         to_y = lax.bitwise_xor(y, jnp.int32(dy))
         for dx in range(2):
@@ -279,19 +279,17 @@
                     count = size if i == 2 else 2 * size
                     first = block[2 * pair * count : (2 * pair + 1) * count]
                     second = block[(2 * pair + 1) * count : (2 * pair + 2) * count]
-                    rows["send"][i].append(jnp.where(odd, first, second))
-                    rows["keep"][i].append(jnp.where(odd, second, first))
+                    rows[i].append(jnp.where(take_second, second, first))
     right = upstream[:, core_half(scalars, half)]
-    for target, name in ((send, "send"), (keep, "keep")):
-        own, far, out = [jnp.concatenate(parts, axis=0) for parts in rows[name]]
-        grad_v = times((own, far), value_right).astype(target.dtype)
-        grad_o = dot_nn(out, right).astype(target.dtype)
-        for i, place in enumerate(places):
-            target[(*place, slice(None), slice(0, half))] = grad_o[i * size : (i + 1) * size]
-            for core in range(2):
-                columns = slice(half + core * lanes, half + (core + 1) * lanes)
-                part = grad_v[(2 * i + core) * size : (2 * i + core + 1) * size]
-                target[(*place, slice(None), columns)] = part
+    own, far, out = [jnp.concatenate(parts, axis=0) for parts in rows]
+    grad_v = times((own, far), value_right).astype(target.dtype)
+    grad_o = dot_nn(out, right).astype(target.dtype)
+    for i, place in enumerate(places):
+        target[(*place, slice(None), slice(0, half))] = grad_o[i * size : (i + 1) * size]
+        for core in range(2):
+            columns = slice(half + core * lanes, half + (core + 1) * lanes)
+            part = grad_v[(2 * i + core) * size : (2 * i + core + 1) * size]
+            target[(*place, slice(None), columns)] = part
 
 
 def view_sum_kernel(keep, got, x_send, y_send, x_keep, y_keep):
@@ -565,13 +563,17 @@
         return mine, far_same, near_cross, far_cross
 
     tile = (2 * o_rows, width // 2 + 2 * part)
-    send, keep = call(
-        value_out_kernel,
-        [shape((2, 2, pairs, *tile), kind) for kind in (bf16, f32)],
-        (scalars, normed_t, normed_far_t, after(dvalue, dkey), mixed_t, mixed_other, upstream),
-        "grad_value_out",
-        SMEM,
-        24,
+    operands = (scalars, normed_t, normed_far_t, after(dvalue, dkey), mixed_t, mixed_other, upstream)
+    send, keep = (
+        call(
+            functools.partial(value_out_kernel, sent),
+            [shape((2, 2, pairs, *tile), kind)],
+            operands,
+            name,
+            SMEM,
+            24,
+        )[0]
+        for sent, kind, name in ((True, bf16, "grad_value_out_sent"), (False, f32, "grad_value_out_kept"))
     )
     got = lax.ppermute(send, "view", neighbours)
     q_later, k_later, q_now, k_now, q_keep, k_keep = call(
@@ -586,7 +588,7 @@
     q_got, k_got = first_exchange((q_later, k_later))
     q_first, k_first = first_exchange((q_now, k_now))
     later = call(
-        go_on_kernel, [shape(q_block, bf16), shape(q_block, bf16)], (q_keep, q_got, k_keep, k_got), "first_sum_query_key"
+        go_on_kernel, [shape(q_block, bf16), shape(q_block, bf16)], (after(q_keep, keep), q_got, k_keep, k_got), "first_sum_query_key"
     )
     q_second, k_second = second_exchange(later)
     qk_tile = (2 * q_rows, 2 * part)

time: 88.7 us -> 88.1 us (level)
  waiting for transfers between devices: 35.6 us -> 34.3 us
    ppermute x3, waiting for transfers between devices: 8.38 us -> 7.03 us  [first_exchange(): lax.ppermute(sends[0], 'scene', along_x)]
    pallas_call x12 -> x13, Pallas kernels: 10.3 us -> 11 us  [call(): pl.pallas_call(kernel_body, in_specs=[first] + [VMEM] * (len(operands) -...]
  transfers between devices with their start and end apart: 30 -> 30, of which waited for: 18 -> 18; matrix products, arithmetic and copies ran while one was open for 0% -> 0% of each run, Pallas kernels for 14% -> 16%
where the time goes in v20:
time: 88.1 us; the launch traced here: 88 us
  waiting for transfers between devices  34.3 us (39%)
  starting transfers between devices  31.5 us (36%)
  Pallas kernels  20.4 us (23%)
  between operations  0.9 us (1%)
  local copies, waits for them, and re-layouts  0.89 us (1%)
    pallas_call x13, Pallas kernels, call(): pl.pallas_call(kernel_body, in_specs=[first] + [VMEM] * (len(operands) -...  11 us
    ppermute x2, waiting for transfers between devices, last_parts(): lax.ppermute(far_same, 'view', [(i, i ^ 2) for i in range(groups)])  7.72 us
    ppermute x3, waiting for transfers between devices, first_exchange(): lax.ppermute(sends[0], 'scene', along_x)  7.03 us
    ppermute x3, starting transfers between devices, shards(): granted = [lax.ppermute(partners, 'view', pairs) for pairs in between]  5.62 us
    ppermute x2, waiting for transfers between devices, second_exchange(): lax.ppermute(sums[0], 'scene', along_y)  5.46 us
    ppermute x3, starting transfers between devices, shards(): lax.ppermute(part_out, 'view', pairs)  4.45 us
    pallas_call x1, Pallas kernels, shards(): pl.pallas_call(project_kernel, in_specs=[SMEM] + [VMEM] * 10, out_specs=[...  4.13 us
    ppermute x3, starting transfers between devices, first_exchange(): lax.ppermute(sends[0], 'scene', along_x)  3.7 us
  transfers between devices with their start and end apart: 30, of which 18 were waited for; matrix products, arithmetic and copies ran while one was open for 0% of the time, Pallas kernels for 16%

profile of v20, /device:TPU:0, one launch (start us, length us, event | category | flops | bytes accessed | tf_op | source)
XLA Modules:
  0.0 88.0 jit_solution(12346382539687659952)
XLA Ops:
  0.6 0.8 copy.13.partners
  1.4 3.0 %collective-permute-start.2 = (s32[1,4,3]{2,1,0:T(4,128)S(1)}, s32[1,4,3]{2,1,0:T(4,128)S(1)}, u32[]{:S(2)}, u32[]{:S(2)}) collective-permute-start(s32[1,4,3]{2,1,0:T(4,128)S(1)} %copy.13.partners), channel_id=1, source_target_pairs={{0,2},{2,0},{4,6},{6,4},{1,3},{3,1},{5,7},{7,5},{8,10},{10,8},{12,... | collective-permute-start | bytes 152 | tf_op jit(solution)/shard_map/ppermute | solution.py:433
  4.4 2.6 %collective-permute-start.1 = (s32[1,4,3]{2,1,0:T(4,128)S(1)}, s32[1,4,3]{2,1,0:T(4,128)S(1)}, u32[]{:S(2)}, u32[]{:S(2)}) collective-permute-start(s32[1,4,3]{2,1,0:T(4,128)S(1)} %copy.13.partners), channel_id=1, source_target_pairs={{0,4},{2,6},{4,0},{6,2},{1,5},{3,7},{5,1},{7,3},{8,12},{10,14},{12... | collective-permute-start | bytes 152 | tf_op jit(solution)/shard_map/ppermute | solution.py:433
  7.0 0.5 collective-permute-start.7
  7.5 1.2 %alive.1 = s32[16]{0:T(128)S(1)} custom-call(s32[1,4,3]{2,1,0:T(4,128)S(1)} %copy.13.partners), custom_call_target="tpu_custom_call" | custom-call | flops 40000000000 | bytes 1 | tf_op jit(solution)/shard_map/alive/pallas_call | solution.py:423
  8.8 0.1 stack.23.scalars
  8.9 0.0 copy-start.6
  8.9 3.5 %collective-permute-done.refs_0_ = s32[1,4,3]{2,1,0:T(4,128)S(1)} collective-permute-done((s32[1,4,3]{2,1,0:T(4,128)S(1)}, s32[1,4,3]{2,1,0:T(4,128)S(1)}, u32[]{:S(2)}, u32[]{:S(2)}) %collective-permute-start) | collective-permute-done | bytes 80 | tf_op jit(solution)/shard_map/ppermute | solution.py:433
  12.4 0.8 pick.1
  13.2 0.4 collective-permute-start.3
  13.6 4.0 %collective-permute-start.5 = (bf16[32,1536]{1,0:T(8,128)(2,1)S(1)}, bf16[32,1536]{1,0:T(8,128)(2,1)S(1)}, u32[]{:S(2)}, u32[]{:S(2)}) collective-permute-start(bf16[32,1536]{1,0:T(8,128)(2,1)S(1)} %get-tuple-element.76), channel_id=1, source_target_pairs={{0,2},{2,0},{4,6},{6,4},{1,3},{3,1},{5,7},{7,5},{8,10},{10,8},{12,... | collective-permute-start | bytes 294920 | tf_op jit(solution)/shard_map/ppermute | solution.py:450
  17.7 4.1 %project.1 = (bf16[1536,256]{1,0:T(8,128)(2,1)S(1)}, bf16[256,384]{1,0:T(8,128)(2,1)S(1)}, bf16[256,384]{1,0:T(8,128)(2,1)S(1)}, bf16[256,1536]{1,0:T(8,128)(2,1...) custom-call(s32[5]{0:T(128)S(1)} %stack.23.scalars, ...), custom_call_target="tpu_custom_call" | custom-call | flops 1 | bytes 1 | tf_op jit(solution)/shard_map/project/pallas_call | solution.py:452
  21.9 0.4 collective-permute-done.4.refs_1_
  22.3 0.1 collective-permute-start.8
  22.4 0.4 collective-permute-start.9
  22.8 0.1 collective-permute-start.10
  22.9 0.7 collective-permute-done.8.refs_3_
  23.6 0.2 collective-permute-done.9.refs_4_
  23.7 0.4 collective-permute-done.10.refs_5_
  24.1 3.2 %attention_forward.1 = (bf16[1536,192]{1,0:T(8,128)(2,1)S(1)}, bf16[192,384]{1,0:T(8,128)(2,1)S(1)}, bf16[192,384]{1,0:T(8,128)(2,1)S(1)}, f32[3,64,512]{2,1,0:T...) custom-call(s32[5]{0:T(128)S(1)} %stack.23.scalars, ...), custom_call_target="tpu_custom_call" | custom-call | flops 1 | bytes 1 | tf_op jit(solution)/shard_map/attention_forward/pallas_call | solution.py:488
  27.3 0.2 collective-permute-start.11
  27.5 1.6 %attention_backward.1 = (bf16[256,384]{1,0:T(8,128)(2,1)S(1)}, bf16[448,384]{1,0:T(8,128)(2,1)S(1)}) custom-call(bf16[3,512,128]{2,1,0:T(8,128)(2,1)S(1)} %get-tuple-element.83.refs_6_.query_stack, bf16[3,512,128]{2,1,0:T(8,128)(2,1)S(1)} %get-tuple-element.84.refs_7_.grad_stack, f32[3,64,512]{2,1,0:T(8,128)S(1)} %get-tuple-element.88.dprob_own, ...), custom_call_target="tpu_custom_call" | custom-call | flops 1 | bytes 1 | tf_op jit(solution)/shard_map/attention_backward/pallas_call | solution.py:476
  29.1 1.3 %grad_value_out_sent.1 = bf16[2,2,2,48,1536]{4,3,2,1,0:T(8,128)(2,1)S(1)} custom-call(s32[5]{0:T(128)S(1)} %stack.23.scalars, bf16[1536,256]{1,0:T(8,128)(2,1)S(1)} %get-tuple-element.78.normed_t, bf16[1536,192]{1,0:T(8,128)(2,1)S(1)} %get-tuple-element.87.normed_far_t, bf16[448,384]{1,0:T(8,128)(2,1)S(1)} %get-tuple-element.97.dvalue, ...), custom_call_target="tpu_custom_call" | custom-call | flops 1 | bytes 1 | tf_op jit(solution)/shard_map/grad_value_out_sent/pallas_call | solution.py:476
  30.4 0.4 collective-permute-start.22
  30.7 1.9 %grad_query_key.1 = (bf16[384,384]{1,0:T(8,128)(2,1)S(1)}, bf16[384,384]{1,0:T(8,128)(2,1)S(1)}, bf16[384,384]{1,0:T(8,128)(2,1)S(1)}, bf16[384,384]{1,0:T(8,128...) custom-call(s32[5]{0:T(128)S(1)} %stack.23.scalars, ...), custom_call_target="tpu_custom_call" | custom-call | flops 1 | bytes 1 | tf_op jit(solution)/shard_map/grad_query_key/pallas_call | solution.py:476
  32.7 1.5 %collective-permute-start.13 = (bf16[384,384]{1,0:T(8,128)(2,1)S(1)}, bf16[384,384]{1,0:T(8,128)(2,1)S(1)}, u32[]{:S(2)}, u32[]{:S(2)}) collective-permute-start(bf16[384,384]{1,0:T(8,128)(2,1)S(1)} %get-tuple-element.104), channel_id=1, source_target_pairs={{0,8},{8,0},{16,24},{24,16},{1,9},{9,1},{17,25},{25,17},{2,10},{10... | collective-permute-start | bytes 884744 | tf_op jit(solution)/shard_map/ppermute | solution.py:526
  34.2 1.5 %collective-permute-start.14 = (bf16[384,384]{1,0:T(8,128)(2,1)S(1)}, bf16[384,384]{1,0:T(8,128)(2,1)S(1)}, u32[]{:S(2)}, u32[]{:S(2)}) collective-permute-start(bf16[384,384]{1,0:T(8,128)(2,1)S(1)} %get-tuple-element.106), channel_id=1, source_target_pairs={{0,16},{8,24},{16,0},{24,8},{1,17},{9,25},{17,1},{25,9},{2,18},{10... | collective-permute-start | bytes 884744 | tf_op jit(solution)/shard_map/ppermute | solution.py:526
  35.7 1.3 %grad_value_out_kept.1.keep = f32[2,2,2,48,1536]{4,3,2,1,0:T(8,128)S(1)} custom-call(s32[5]{0:T(128)S(1)} %stack.23.scalars, bf16[1536,256]{1,0:T(8,128)(2,1)S(1)} %get-tuple-element.78.normed_t, bf16[1536,192]{1,0:T(8,128)(2,1)S(1)} %get-tuple-element.87.normed_far_t, bf16[448,384]{1,0:T(8,128)(2,1)S(1)} %get-tuple-element.97.dvalue, ...), custom_call_target="tpu_custom_call" | custom-call | flops 1 | bytes 1 | tf_op jit(solution)/shard_map/grad_value_out_kept/pallas_call | solution.py:476
  37.0 0.6 collective-permute-start.12
  37.6 0.5 collective-permute-start.16
  38.1 4.5 %collective-permute-done.13.q_got = bf16[384,384]{1,0:T(8,128)(2,1)S(1)} collective-permute-done((bf16[384,384]{1,0:T(8,128)(2,1)S(1)}, bf16[384,384]{1,0:T(8,128)(2,1)S(1)}, u32[]{:S(2)}, u32[]{:S(2)}) %collective-permute-start.13) | collective-permute-done | bytes 294944 | tf_op jit(solution)/shard_map/ppermute | solution.py:526
  42.6 1.5 %collective-permute-done.14.k_got = bf16[384,384]{1,0:T(8,128)(2,1)S(1)} collective-permute-done((bf16[384,384]{1,0:T(8,128)(2,1)S(1)}, bf16[384,384]{1,0:T(8,128)(2,1)S(1)}, u32[]{:S(2)}, u32[]{:S(2)}) %collective-permute-start.14) | collective-permute-done | bytes 294944 | tf_op jit(solution)/shard_map/ppermute | solution.py:526
  44.1 0.1 first_sum_query_key.1
  44.3 1.6 %collective-permute-start.15 = (bf16[384,384]{1,0:T(8,128)(2,1)S(1)}, bf16[384,384]{1,0:T(8,128)(2,1)S(1)}, u32[]{:S(2)}, u32[]{:S(2)}) collective-permute-start(bf16[384,384]{1,0:T(8,128)(2,1)S(1)} %get-tuple-element.107), channel_id=1, source_target_pairs={{0,16},{8,24},{16,0},{24,8},{1,17},{9,25},{17,1},{25,9},{2,18},{10... | collective-permute-start | bytes 884744 | tf_op jit(solution)/shard_map/ppermute | solution.py:534
  45.8 0.5 collective-permute-start.17
  46.4 2.5 %collective-permute-done.12.q_first = bf16[384,384]{1,0:T(8,128)(2,1)S(1)} collective-permute-done((bf16[384,384]{1,0:T(8,128)(2,1)S(1)}, bf16[384,384]{1,0:T(8,128)(2,1)S(1)}, u32[]{:S(2)}, u32[]{:S(2)}) %collective-permute-start.12) | collective-permute-done | bytes 294944 | tf_op jit(solution)/shard_map/ppermute | solution.py:526
  48.9 1.5 %collective-permute-done.16.k_first = bf16[384,384]{1,0:T(8,128)(2,1)S(1)} collective-permute-done((bf16[384,384]{1,0:T(8,128)(2,1)S(1)}, bf16[384,384]{1,0:T(8,128)(2,1)S(1)}, u32[]{:S(2)}, u32[]{:S(2)}) %collective-permute-start.16) | collective-permute-done | bytes 294944 | tf_op jit(solution)/shard_map/ppermute | solution.py:526
  50.5 5.1 %collective-permute-done.15.q_second = bf16[384,384]{1,0:T(8,128)(2,1)S(1)} collective-permute-done((bf16[384,384]{1,0:T(8,128)(2,1)S(1)}, bf16[384,384]{1,0:T(8,128)(2,1)S(1)}, u32[]{:S(2)}, u32[]{:S(2)}) %collective-permute-start.15) | collective-permute-done | bytes 294944 | tf_op jit(solution)/shard_map/ppermute | solution.py:534
  55.6 0.8 second_sum_query_key.1
  56.4 1.8 %collective-permute-start.18 = (bf16[2,96,768]{2,1,0:T(8,128)(2,1)S(1)}, bf16[2,96,768]{2,1,0:T(8,128)(2,1)S(1)}, u32[]{:S(2)}, u32[]{:S(2)}) collective-permute-start(bf16[2,96,768]{2,1,0:T(8,128)(2,1)S(1)} %get-tuple-element.111), channel_id=1, source_target_pairs={{0,2},{2,0},{4,6},{6,4},{1,3},{3,1},{5,7},{7,5},{8,10},{10,8},{12,... | collective-permute-start | bytes 884744 | tf_op jit(solution)/shard_map/ppermute | solution.py:602
  58.2 1.0 %collective-permute-done.22.got = bf16[2,2,2,48,1536]{4,3,2,1,0:T(8,128)(2,1)S(1)} collective-permute-done((bf16[2,2,2,48,1536]{4,3,2,1,0:T(8,128)(2,1)S(1)}, bf16[2,2,2,48,1536]{4,3,2,1,0:T(8,128)(2,1)S(1)}, u32[]{:S(2)}, u32[]{:S(2)}) %collective-permute-start.22) | collective-permute-done | bytes 1179680 | tf_op jit(solution)/shard_map/ppermute | solution.py:578
  59.2 0.2 view_sum_value_out.1
  59.4 1.6 %collective-permute-start.23 = (bf16[2,2,48,768]{3,2,1,0:T(8,128)(2,1)S(1)}, bf16[2,2,48,768]{3,2,1,0:T(8,128)(2,1)S(1)}, u32[]{:S(2)}, u32[]{:S(2)}) collective-permute-start(bf16[2,2,48,768]{3,2,1,0:T(8,128)(2,1)S(1)} %get-tuple-element.123), channel_id=1, source_target_pairs={{0,8},{8,0},{16,24},{24,16},{1,9},{9,1},{17,25},{25,17},{2,10},{10... | collective-permute-start | bytes 884744 | tf_op jit(solution)/shard_map/ppermute | solution.py:526
  61.0 1.5 %collective-permute-start.24 = (bf16[2,2,48,768]{3,2,1,0:T(8,128)(2,1)S(1)}, bf16[2,2,48,768]{3,2,1,0:T(8,128)(2,1)S(1)}, u32[]{:S(2)}, u32[]{:S(2)}) collective-permute-start(bf16[2,2,48,768]{3,2,1,0:T(8,128)(2,1)S(1)} %get-tuple-element.125), channel_id=1, source_target_pairs={{0,16},{8,24},{16,0},{24,8},{1,17},{9,25},{17,1},{25,9},{2,18},{10... | collective-permute-start | bytes 884744 | tf_op jit(solution)/shard_map/ppermute | solution.py:526
  62.5 2.5 %collective-permute-done.18.refs_1_ = bf16[2,96,768]{2,1,0:T(8,128)(2,1)S(1)} collective-permute-done((bf16[2,96,768]{2,1,0:T(8,128)(2,1)S(1)}, bf16[2,96,768]{2,1,0:T(8,128)(2,1)S(1)}, u32[]{:S(2)}, u32[]{:S(2)}) %collective-permute-start.18) | collective-permute-done | bytes 294944 | tf_op jit(solution)/shard_map/ppermute | solution.py:602
  65.0 0.6 last_parts_query_key.1
  65.6 0.1 collective-permute-start.20
  65.7 1.7 %collective-permute-start.19 = (bf16[48,768]{1,0:T(8,128)(2,1)S(1)}, bf16[48,768]{1,0:T(8,128)(2,1)S(1)}, u32[]{:S(2)}, u32[]{:S(2)}) collective-permute-start(bf16[48,768]{1,0:T(8,128)(2,1)S(1)} %get-tuple-element.113), channel_id=1, source_target_pairs={{0,4},{2,6},{4,0},{6,2},{1,5},{3,7},{5,1},{7,3},{8,12},{10,14},{12... | collective-permute-start | bytes 221192 | tf_op jit(solution)/shard_map/ppermute | solution.py:560
  67.4 1.1 %collective-permute-start.21 = (bf16[48,768]{1,0:T(8,128)(2,1)S(1)}, bf16[48,768]{1,0:T(8,128)(2,1)S(1)}, u32[]{:S(2)}, u32[]{:S(2)}) collective-permute-start(bf16[48,768]{1,0:T(8,128)(2,1)S(1)} %get-tuple-element.115), channel_id=1, source_target_pairs={{0,5},{1,4},{2,7},{3,6},{4,1},{5,0},{6,3},{7,2},{8,13},{9,12},{10,... | collective-permute-start | bytes 221192 | tf_op jit(solution)/shard_map/ppermute | solution.py:561
  68.5 0.2 collective-permute-done.24.y_got
  68.6 0.1 first_sum_value_out.1
  68.7 1.4 %collective-permute-start.25 = (bf16[2,48,768]{2,1,0:T(8,128)(2,1)S(1)}, bf16[2,48,768]{2,1,0:T(8,128)(2,1)S(1)}, u32[]{:S(2)}, u32[]{:S(2)}) collective-permute-start(bf16[2,48,768]{2,1,0:T(8,128)(2,1)S(1)} %get-tuple-element.128), channel_id=1, source_target_pairs={{0,8},{8,0},{16,24},{24,16},{1,9},{9,1},{17,25},{25,17},{2,10},{10... | collective-permute-start | bytes 442376 | tf_op jit(solution)/shard_map/ppermute | solution.py:534
  70.1 1.5 %collective-permute-start.26 = (bf16[2,48,768]{2,1,0:T(8,128)(2,1)S(1)}, bf16[2,48,768]{2,1,0:T(8,128)(2,1)S(1)}, u32[]{:S(2)}, u32[]{:S(2)}) collective-permute-start(bf16[2,48,768]{2,1,0:T(8,128)(2,1)S(1)} %get-tuple-element.130), channel_id=1, source_target_pairs={{0,16},{8,24},{16,0},{24,8},{1,17},{9,25},{17,1},{25,9},{2,18},{10... | collective-permute-start | bytes 442376 | tf_op jit(solution)/shard_map/ppermute | solution.py:534
  71.6 3.2 %collective-permute-done.19.far_same = bf16[48,768]{1,0:T(8,128)(2,1)S(1)} collective-permute-done((bf16[48,768]{1,0:T(8,128)(2,1)S(1)}, bf16[48,768]{1,0:T(8,128)(2,1)S(1)}, u32[]{:S(2)}, u32[]{:S(2)}) %collective-permute-start.19) | collective-permute-done | bytes 73760 | tf_op jit(solution)/shard_map/ppermute | solution.py:560
  74.9 0.7 collective-permute-done.21.far_cross
  75.6 0.3 collective-permute-done.26.refs_3_
  76.0 0.6 last_parts_value_out.1
  76.6 0.1 collective-permute-start.28
  76.7 0.9 %collective-permute-start.27 = (bf16[24,1536]{1,0:T(8,128)(2,1)S(1)}, bf16[24,1536]{1,0:T(8,128)(2,1)S(1)}, u32[]{:S(2)}, u32[]{:S(2)}) collective-permute-start(bf16[24,1536]{1,0:T(8,128)(2,1)S(1)} %get-tuple-element.133), channel_id=1, source_target_pairs={{0,4},{2,6},{4,0},{6,2},{1,5},{3,7},{5,1},{7,3},{8,12},{10,14},{12... | collective-permute-start | bytes 221192 | tf_op jit(solution)/shard_map/ppermute | solution.py:560
  77.6 1.8 %collective-permute-start.29 = (bf16[24,1536]{1,0:T(8,128)(2,1)S(1)}, bf16[24,1536]{1,0:T(8,128)(2,1)S(1)}, u32[]{:S(2)}, u32[]{:S(2)}) collective-permute-start(bf16[24,1536]{1,0:T(8,128)(2,1)S(1)} %get-tuple-element.135), channel_id=1, source_target_pairs={{0,5},{1,4},{2,7},{3,6},{4,1},{5,0},{6,3},{7,2},{8,13},{9,12},{10,... | collective-permute-start | bytes 221192 | tf_op jit(solution)/shard_map/ppermute | solution.py:561
  79.4 1.3 %place_query_key.1 = (f32[48,768]{1,0:T(8,128)}, f32[48,768]{1,0:T(8,128)}) custom-call(s32[5]{0:T(128)S(1)} %stack.23.scalars, f32[48,768]{1,0:T(8,128)S(1)} %get-tuple-element.116.same, f32[48,768]{1,0:T(8,128)S(1)} %get-tuple-element.117.cross), custom_call_target="tpu_custom_call" | custom-call | flops 1 | bytes 1 | tf_op jit(solution)/shard_map/place_query_key/pallas_call | solution.py:476
  80.7 4.5 %collective-permute-done.27.far_same = bf16[24,1536]{1,0:T(8,128)(2,1)S(1)} collective-permute-done((bf16[24,1536]{1,0:T(8,128)(2,1)S(1)}, bf16[24,1536]{1,0:T(8,128)(2,1)S(1)}, u32[]{:S(2)}, u32[]{:S(2)}) %collective-permute-start.27) | collective-permute-done | bytes 73760 | tf_op jit(solution)/shard_map/ppermute | solution.py:560
  85.2 1.5 %collective-permute-done.29.far_cross = bf16[24,1536]{1,0:T(8,128)(2,1)S(1)} collective-permute-done((bf16[24,1536]{1,0:T(8,128)(2,1)S(1)}, bf16[24,1536]{1,0:T(8,128)(2,1)S(1)}, u32[]{:S(2)}, u32[]{:S(2)}) %collective-permute-start.29) | collective-permute-done | bytes 73760 | tf_op jit(solution)/shard_map/ppermute | solution.py:561
  86.7 1.3 %last_sum_value_out.1 = (f32[48,768]{1,0:T(8,128)}, f32[24,1536]{1,0:T(8,128)}) custom-call(s32[5]{0:T(128)S(1)} %stack.23.scalars, f32[24,1536]{1,0:T(8,128)S(1)} %get-tuple-element.132.mine, bf16[24,1536]{1,0:T(8,128)(2,1)S(1)} %collective-permute-done.27.far_same, f32[24,1536]{1,0:T(8,128)S(1)} %collective-permute-done.28.near_cross, ...), custom_call_target="tpu_custom_call" | custom-call | flops 1 | bytes 1 | tf_op jit(solution)/shard_map/last_sum_value_out/pallas_call | solution.py:476
  (31 shorter events, 0.1 us)
Async XLA Ops:
  1.4 7.5 %collective-permute-start.2 = (s32[1,4,3]{2,1,0:T(4,128)S(1)}, s32[1,4,3]{2,1,0:T(4,128)S(1)}, u32[]{:S(2)}, u32[]{:S(2)}) collective-permute-start(s32[1,4,3]{2,1,0:T(4,128)S(1)} %copy.13.partners), channel_id=1, source_target_pairs={{0,2},{2,0},{4,6},{6,4},{1,3},{3,1},{5,7},{7,5},{8,10},{10,8},{12,... | collective-permute-start | bytes 152 | tf_op jit(solution)/shard_map/ppermute | solution.py:433
  4.4 4.5 %collective-permute-start.1 = (s32[1,4,3]{2,1,0:T(4,128)S(1)}, s32[1,4,3]{2,1,0:T(4,128)S(1)}, u32[]{:S(2)}, u32[]{:S(2)}) collective-permute-start(s32[1,4,3]{2,1,0:T(4,128)S(1)} %copy.13.partners), channel_id=1, source_target_pairs={{0,4},{2,6},{4,0},{6,2},{1,5},{3,7},{5,1},{7,3},{8,12},{10,14},{12... | collective-permute-start | bytes 152 | tf_op jit(solution)/shard_map/ppermute | solution.py:433
  7.0 5.4 %collective-permute-start = (s32[1,4,3]{2,1,0:T(4,128)S(1)}, s32[1,4,3]{2,1,0:T(4,128)S(1)}, u32[]{:S(2)}, u32[]{:S(2)}) collective-permute-start(s32[1,4,3]{2,1,0:T(4,128)S(1)} %copy.13.partners), channel_id=1, source_target_pairs={{0,6},{2,4},{4,2},{6,0},{1,7},{3,5},{5,3},{7,1},{8,14},{10,12},{12... | collective-permute-start | bytes 152 | tf_op jit(solution)/shard_map/ppermute | solution.py:433
  7.0 10.6 %collective-permute-start.6 = (bf16[4,32,1536]{2,1,0:T(8,128)(2,1)}, bf16[4,32,1536]{2,1,0:T(8,128)(2,1)S(1)}, u32[]{:S(2)}, u32[]{:S(2)}) collective-permute-start(bf16[4,32,1536]{2,1,0:T(8,128)(2,1)} %bitcast.7), channel_id=1, source_target_pairs={{0,1},{1,0},{2,3},{3,2},{4,5},{5,4},{6,7},{7,6},{8,9},{9,8},{10,11... | collective-permute-start | bytes 1179656 | tf_op jit(solution)/shard_map/ppermute | solution.py:438
  7.0 10.6 %collective-permute-start.7 = (bf16[4,32,1536]{2,1,0:T(8,128)(2,1)}, bf16[4,32,1536]{2,1,0:T(8,128)(2,1)S(1)}, u32[]{:S(2)}, u32[]{:S(2)}) collective-permute-start(bf16[4,32,1536]{2,1,0:T(8,128)(2,1)} %bitcast.10), channel_id=1, source_target_pairs={{0,1},{1,0},{2,3},{3,2},{4,5},{5,4},{6,7},{7,6},{8,9},{9,8},{10,11... | collective-permute-start | bytes 1179656 | tf_op jit(solution)/shard_map/ppermute | solution.py:439
  7.5 4.9 %copy-start.4 = (bf16[1,4,1,32,1536]{4,3,2,1,0:T(8,128)(2,1)S(1)}, bf16[1,4,1,32,1536]{4,3,2,1,0:T(8,128)(2,1)}, u32[]{:S(2)}) copy-start(bf16[1,4,1,32,1536]{4,3,2,1,0:T(8,128)(2,1)} %param.10) | copy-start | bytes 1179652
  8.8 8.8 %copy-start = (bf16[1536,768]{1,0:T(8,128)(2,1)S(1)}, bf16[1536,768]{1,0:T(8,128)(2,1)}, u32[]{:S(2)}) copy-start(bf16[1536,768]{1,0:T(8,128)(2,1)} %refs_11_.1) | copy-start | bytes 7077892
  8.9 8.8 %copy-start.1 = (bf16[1536,768]{1,0:T(8,128)(2,1)S(1)}, bf16[1536,768]{1,0:T(8,128)(2,1)}, u32[]{:S(2)}) copy-start(bf16[1536,768]{1,0:T(8,128)(2,1)} %refs_12_.1) | copy-start | bytes 7077892
  8.9 8.8 %copy-start.2 = (bf16[1536,768]{1,0:T(8,128)(2,1)S(1)}, bf16[1536,768]{1,0:T(8,128)(2,1)}, u32[]{:S(2)}) copy-start(bf16[1536,768]{1,0:T(8,128)(2,1)} %w_query.1) | copy-start | bytes 7077892
  8.9 8.8 %copy-start.3 = (bf16[768,1536]{1,0:T(8,128)(2,1)S(1)}, bf16[768,1536]{1,0:T(8,128)(2,1)}, u32[]{:S(2)}) copy-start(bf16[768,1536]{1,0:T(8,128)(2,1)} %w_out.1) | copy-start | bytes 7077892
  8.9 8.8 %copy-start.5 = (bf16[1,4,1,32,1536]{4,3,2,1,0:T(8,128)(2,1)S(1)}, bf16[1,4,1,32,1536]{4,3,2,1,0:T(8,128)(2,1)}, u32[]{:S(2)}) copy-start(bf16[1,4,1,32,1536]{4,3,2,1,0:T(8,128)(2,1)} %param.18) | copy-start | bytes 1179652
  8.9 8.8 %copy-start.6 = (bf16[9,1536]{1,0:T(8,128)(2,1)S(1)}, bf16[9,1536]{1,0:T(8,128)(2,1)}, u32[]{:S(2)}) copy-start(bf16[9,1536]{1,0:T(8,128)(2,1)} %taps.1) | copy-start | bytes 82948
  8.9 8.8 %copy-start.7 = (f32[1536]{0:T(1024)S(1)}, f32[1536]{0:T(1024)}, u32[]{:S(2)}) copy-start(f32[1536]{0:T(1024)} %refs_10_.1) | copy-start | bytes 18436
  13.2 8.7 %collective-permute-start.3 = (bf16[32,1536]{1,0:T(8,128)(2,1)S(1)}, bf16[32,1536]{1,0:T(8,128)(2,1)S(1)}, u32[]{:S(2)}, u32[]{:S(2)}) collective-permute-start(bf16[32,1536]{1,0:T(8,128)(2,1)S(1)} %get-tuple-element.74), channel_id=1, source_target_pairs={{0,6},{2,4},{4,2},{6,0},{1,7},{3,5},{5,3},{7,1},{8,14},{10,12},{12... | collective-permute-start | bytes 294920 | tf_op jit(solution)/shard_map/ppermute | solution.py:450
  13.6 8.7 %collective-permute-start.4 = (bf16[32,1536]{1,0:T(8,128)(2,1)S(1)}, bf16[32,1536]{1,0:T(8,128)(2,1)S(1)}, u32[]{:S(2)}, u32[]{:S(2)}) collective-permute-start(bf16[32,1536]{1,0:T(8,128)(2,1)S(1)} %get-tuple-element.75), channel_id=1, source_target_pairs={{0,4},{2,6},{4,0},{6,2},{1,5},{3,7},{5,1},{7,3},{8,12},{10,14},{12... | collective-permute-start | bytes 294920 | tf_op jit(solution)/shard_map/ppermute | solution.py:450
  13.6 8.7 %collective-permute-start.5 = (bf16[32,1536]{1,0:T(8,128)(2,1)S(1)}, bf16[32,1536]{1,0:T(8,128)(2,1)S(1)}, u32[]{:S(2)}, u32[]{:S(2)}) collective-permute-start(bf16[32,1536]{1,0:T(8,128)(2,1)S(1)} %get-tuple-element.76), channel_id=1, source_target_pairs={{0,2},{2,0},{4,6},{6,4},{1,3},{3,1},{5,7},{7,5},{8,10},{10,8},{12,... | collective-permute-start | bytes 294920 | tf_op jit(solution)/shard_map/ppermute | solution.py:450
  22.3 1.3 %collective-permute-start.8 = (bf16[32,1536]{1,0:T(8,128)(2,1)S(1)}, bf16[32,1536]{1,0:T(8,128)(2,1)S(1)}, u32[]{:S(2)}, u32[]{:S(2)}) collective-permute-start(bf16[32,1536]{1,0:T(8,128)(2,1)S(1)} %collective-permute-done.3.refs_0_), channel_id=1, source_target_pairs={{0,1},{1,0},{2,3},{3,2},{4,5},{5,4},{6,7},{7,6},{8,9},{9,8},{10,11... | collective-permute-start | bytes 294920 | tf_op jit(solution)/shard_map/ppermute | solution.py:473
  22.4 1.4 %collective-permute-start.9 = (bf16[32,1536]{1,0:T(8,128)(2,1)S(1)}, bf16[32,1536]{1,0:T(8,128)(2,1)S(1)}, u32[]{:S(2)}, u32[]{:S(2)}) collective-permute-start(bf16[32,1536]{1,0:T(8,128)(2,1)S(1)} %collective-permute-done.4.refs_1_), channel_id=1, source_target_pairs={{0,1},{1,0},{2,3},{3,2},{4,5},{5,4},{6,7},{7,6},{8,9},{9,8},{10,11... | collective-permute-start | bytes 294920 | tf_op jit(solution)/shard_map/ppermute | solution.py:473
  22.8 1.3 %collective-permute-start.10 = (bf16[32,1536]{1,0:T(8,128)(2,1)S(1)}, bf16[32,1536]{1,0:T(8,128)(2,1)S(1)}, u32[]{:S(2)}, u32[]{:S(2)}) collective-permute-start(bf16[32,1536]{1,0:T(8,128)(2,1)S(1)} %collective-permute-done.5.refs_2_), channel_id=1, source_target_pairs={{0,1},{1,0},{2,3},{3,2},{4,5},{5,4},{6,7},{7,6},{8,9},{9,8},{10,11... | collective-permute-start | bytes 294920 | tf_op jit(solution)/shard_map/ppermute | solution.py:473
  27.3 1.8 %collective-permute-start.11 = (bf16[384,256]{1,0:T(8,128)(2,1)S(1)}, bf16[384,256]{1,0:T(8,128)(2,1)S(1)}, u32[]{:S(2)}, u32[]{:S(2)}) collective-permute-start(bf16[384,256]{1,0:T(8,128)(2,1)S(1)} %get-tuple-element.98.mine), channel_id=1, source_target_pairs={{0,1},{1,0},{2,3},{3,2},{4,5},{5,4},{6,7},{7,6},{8,9},{9,8},{10,11... | collective-permute-start | bytes 589832 | tf_op jit(solution)/shard_map/ppermute | solution.py:508
  30.4 28.9 %collective-permute-start.22 = (bf16[2,2,2,48,1536]{4,3,2,1,0:T(8,128)(2,1)S(1)}, bf16[2,2,2,48,1536]{4,3,2,1,0:T(8,128)(2,1)S(1)}, u32[]{:S(2)}, u32[]{:S(2)}) collective-permute-start(bf16[2,2,2,48,1536]{4,3,2,1,0:T(8,128)(2,1)S(1)} %grad_value_out_sent.1), channel_id=1, source_target_pairs={{0,2},{2,0},{4,6},{6,4},{1,3},{3,1},{5,7},{7,5},{8,10},{10,8},{12,... | collective-permute-start | bytes 3538952 | tf_op jit(solution)/shard_map/ppermute | solution.py:578
  32.7 9.9 %collective-permute-start.13 = (bf16[384,384]{1,0:T(8,128)(2,1)S(1)}, bf16[384,384]{1,0:T(8,128)(2,1)S(1)}, u32[]{:S(2)}, u32[]{:S(2)}) collective-permute-start(bf16[384,384]{1,0:T(8,128)(2,1)S(1)} %get-tuple-element.104), channel_id=1, source_target_pairs={{0,8},{8,0},{16,24},{24,16},{1,9},{9,1},{17,25},{25,17},{2,10},{10... | collective-permute-start | bytes 884744 | tf_op jit(solution)/shard_map/ppermute | solution.py:526
  34.2 9.9 %collective-permute-start.14 = (bf16[384,384]{1,0:T(8,128)(2,1)S(1)}, bf16[384,384]{1,0:T(8,128)(2,1)S(1)}, u32[]{:S(2)}, u32[]{:S(2)}) collective-permute-start(bf16[384,384]{1,0:T(8,128)(2,1)S(1)} %get-tuple-element.106), channel_id=1, source_target_pairs={{0,16},{8,24},{16,0},{24,8},{1,17},{9,25},{17,1},{25,9},{2,18},{10... | collective-permute-start | bytes 884744 | tf_op jit(solution)/shard_map/ppermute | solution.py:526
  37.0 11.9 %collective-permute-start.12 = (bf16[384,384]{1,0:T(8,128)(2,1)S(1)}, bf16[384,384]{1,0:T(8,128)(2,1)S(1)}, u32[]{:S(2)}, u32[]{:S(2)}) collective-permute-start(bf16[384,384]{1,0:T(8,128)(2,1)S(1)} %get-tuple-element.102), channel_id=1, source_target_pairs={{0,8},{8,0},{16,24},{24,16},{1,9},{9,1},{17,25},{25,17},{2,10},{10... | collective-permute-start | bytes 884744 | tf_op jit(solution)/shard_map/ppermute | solution.py:526
  37.6 12.8 %collective-permute-start.16 = (bf16[384,384]{1,0:T(8,128)(2,1)S(1)}, bf16[384,384]{1,0:T(8,128)(2,1)S(1)}, u32[]{:S(2)}, u32[]{:S(2)}) collective-permute-start(bf16[384,384]{1,0:T(8,128)(2,1)S(1)} %get-tuple-element.108), channel_id=1, source_target_pairs={{0,16},{8,24},{16,0},{24,8},{1,17},{9,25},{17,1},{25,9},{2,18},{10... | collective-permute-start | bytes 884744 | tf_op jit(solution)/shard_map/ppermute | solution.py:526
  44.3 11.3 %collective-permute-start.15 = (bf16[384,384]{1,0:T(8,128)(2,1)S(1)}, bf16[384,384]{1,0:T(8,128)(2,1)S(1)}, u32[]{:S(2)}, u32[]{:S(2)}) collective-permute-start(bf16[384,384]{1,0:T(8,128)(2,1)S(1)} %get-tuple-element.107), channel_id=1, source_target_pairs={{0,16},{8,24},{16,0},{24,8},{1,17},{9,25},{17,1},{25,9},{2,18},{10... | collective-permute-start | bytes 884744 | tf_op jit(solution)/shard_map/ppermute | solution.py:534
  45.8 9.7 %collective-permute-start.17 = (bf16[384,384]{1,0:T(8,128)(2,1)S(1)}, bf16[384,384]{1,0:T(8,128)(2,1)S(1)}, u32[]{:S(2)}, u32[]{:S(2)}) collective-permute-start(bf16[384,384]{1,0:T(8,128)(2,1)S(1)} %get-tuple-element.109), channel_id=1, source_target_pairs={{0,8},{8,0},{16,24},{24,16},{1,9},{9,1},{17,25},{25,17},{2,10},{10... | collective-permute-start | bytes 884744 | tf_op jit(solution)/shard_map/ppermute | solution.py:534
  56.4 8.6 %collective-permute-start.18 = (bf16[2,96,768]{2,1,0:T(8,128)(2,1)S(1)}, bf16[2,96,768]{2,1,0:T(8,128)(2,1)S(1)}, u32[]{:S(2)}, u32[]{:S(2)}) collective-permute-start(bf16[2,96,768]{2,1,0:T(8,128)(2,1)S(1)} %get-tuple-element.111), channel_id=1, source_target_pairs={{0,2},{2,0},{4,6},{6,4},{1,3},{3,1},{5,7},{7,5},{8,10},{10,8},{12,... | collective-permute-start | bytes 884744 | tf_op jit(solution)/shard_map/ppermute | solution.py:602
  59.4 9.1 %collective-permute-start.23 = (bf16[2,2,48,768]{3,2,1,0:T(8,128)(2,1)S(1)}, bf16[2,2,48,768]{3,2,1,0:T(8,128)(2,1)S(1)}, u32[]{:S(2)}, u32[]{:S(2)}) collective-permute-start(bf16[2,2,48,768]{3,2,1,0:T(8,128)(2,1)S(1)} %get-tuple-element.123), channel_id=1, source_target_pairs={{0,8},{8,0},{16,24},{24,16},{1,9},{9,1},{17,25},{25,17},{2,10},{10... | collective-permute-start | bytes 884744 | tf_op jit(solution)/shard_map/ppermute | solution.py:526
  61.0 7.6 %collective-permute-start.24 = (bf16[2,2,48,768]{3,2,1,0:T(8,128)(2,1)S(1)}, bf16[2,2,48,768]{3,2,1,0:T(8,128)(2,1)S(1)}, u32[]{:S(2)}, u32[]{:S(2)}) collective-permute-start(bf16[2,2,48,768]{3,2,1,0:T(8,128)(2,1)S(1)} %get-tuple-element.125), channel_id=1, source_target_pairs={{0,16},{8,24},{16,0},{24,8},{1,17},{9,25},{17,1},{25,9},{2,18},{10... | collective-permute-start | bytes 884744 | tf_op jit(solution)/shard_map/ppermute | solution.py:526
  65.6 10.0 %collective-permute-start.20 = (f32[48,768]{1,0:T(8,128)S(1)}, f32[48,768]{1,0:T(8,128)S(1)}, u32[]{:S(2)}, u32[]{:S(2)}) collective-permute-start(f32[48,768]{1,0:T(8,128)S(1)} %get-tuple-element.114), channel_id=1, source_target_pairs={{0,1},{1,0},{2,3},{3,2},{4,5},{5,4},{6,7},{7,6},{8,9},{9,8},{10,11... | collective-permute-start | bytes 442376 | tf_op jit(solution)/shard_map/ppermute | solution.py:562
  65.7 9.2 %collective-permute-start.19 = (bf16[48,768]{1,0:T(8,128)(2,1)S(1)}, bf16[48,768]{1,0:T(8,128)(2,1)S(1)}, u32[]{:S(2)}, u32[]{:S(2)}) collective-permute-start(bf16[48,768]{1,0:T(8,128)(2,1)S(1)} %get-tuple-element.113), channel_id=1, source_target_pairs={{0,4},{2,6},{4,0},{6,2},{1,5},{3,7},{5,1},{7,3},{8,12},{10,14},{12... | collective-permute-start | bytes 221192 | tf_op jit(solution)/shard_map/ppermute | solution.py:560
  67.4 8.2 %collective-permute-start.21 = (bf16[48,768]{1,0:T(8,128)(2,1)S(1)}, bf16[48,768]{1,0:T(8,128)(2,1)S(1)}, u32[]{:S(2)}, u32[]{:S(2)}) collective-permute-start(bf16[48,768]{1,0:T(8,128)(2,1)S(1)} %get-tuple-element.115), channel_id=1, source_target_pairs={{0,5},{1,4},{2,7},{3,6},{4,1},{5,0},{6,3},{7,2},{8,13},{9,12},{10,... | collective-permute-start | bytes 221192 | tf_op jit(solution)/shard_map/ppermute | solution.py:561
  68.7 6.9 %collective-permute-start.25 = (bf16[2,48,768]{2,1,0:T(8,128)(2,1)S(1)}, bf16[2,48,768]{2,1,0:T(8,128)(2,1)S(1)}, u32[]{:S(2)}, u32[]{:S(2)}) collective-permute-start(bf16[2,48,768]{2,1,0:T(8,128)(2,1)S(1)} %get-tuple-element.128), channel_id=1, source_target_pairs={{0,8},{8,0},{16,24},{24,16},{1,9},{9,1},{17,25},{25,17},{2,10},{10... | collective-permute-start | bytes 442376 | tf_op jit(solution)/shard_map/ppermute | solution.py:534
  70.1 5.8 %collective-permute-start.26 = (bf16[2,48,768]{2,1,0:T(8,128)(2,1)S(1)}, bf16[2,48,768]{2,1,0:T(8,128)(2,1)S(1)}, u32[]{:S(2)}, u32[]{:S(2)}) collective-permute-start(bf16[2,48,768]{2,1,0:T(8,128)(2,1)S(1)} %get-tuple-element.130), channel_id=1, source_target_pairs={{0,16},{8,24},{16,0},{24,8},{1,17},{9,25},{17,1},{25,9},{2,18},{10... | collective-permute-start | bytes 442376 | tf_op jit(solution)/shard_map/ppermute | solution.py:534
  76.6 10.1 %collective-permute-start.28 = (f32[24,1536]{1,0:T(8,128)S(1)}, f32[24,1536]{1,0:T(8,128)S(1)}, u32[]{:S(2)}, u32[]{:S(2)}) collective-permute-start(f32[24,1536]{1,0:T(8,128)S(1)} %get-tuple-element.134), channel_id=1, source_target_pairs={{0,1},{1,0},{2,3},{3,2},{4,5},{5,4},{6,7},{7,6},{8,9},{9,8},{10,11... | collective-permute-start | bytes 442376 | tf_op jit(solution)/shard_map/ppermute | solution.py:562
  76.7 8.5 %collective-permute-start.27 = (bf16[24,1536]{1,0:T(8,128)(2,1)S(1)}, bf16[24,1536]{1,0:T(8,128)(2,1)S(1)}, u32[]{:S(2)}, u32[]{:S(2)}) collective-permute-start(bf16[24,1536]{1,0:T(8,128)(2,1)S(1)} %get-tuple-element.133), channel_id=1, source_target_pairs={{0,4},{2,6},{4,0},{6,2},{1,5},{3,7},{5,1},{7,3},{8,12},{10,14},{12... | collective-permute-start | bytes 221192 | tf_op jit(solution)/shard_map/ppermute | solution.py:560
  77.6 9.1 %collective-permute-start.29 = (bf16[24,1536]{1,0:T(8,128)(2,1)S(1)}, bf16[24,1536]{1,0:T(8,128)(2,1)S(1)}, u32[]{:S(2)}, u32[]{:S(2)}) collective-permute-start(bf16[24,1536]{1,0:T(8,128)(2,1)S(1)} %get-tuple-element.135), channel_id=1, source_target_pairs={{0,5},{1,4},{2,7},{3,6},{4,1},{5,0},{6,3},{7,2},{8,13},{9,12},{10,... | collective-permute-start | bytes 221192 | tf_op jit(solution)/shard_map/ppermute | solution.py:561

commit v21 on v20

--- a/solution.py
+++ b/solution.py
@@ -257,10 +257,11 @@
         later[...] = (keep[1] + got[...].astype(jnp.float32)).astype(jnp.bfloat16)
 
 
-def value_out_kernel(sent, scalars, normed_t, normed_far_t, dvalue, mine, theirs, upstream, target):
+def value_out_kernel(sent, scalars, normed_t, normed_far_t, dvalue, mine, theirs, upstream, *targets):
     row, x, y = scalars[0], scalars[3], scalars[4]
     take_second = lax.rem(scalars[1], jnp.int32(2)) == (0 if sent else 1)
-    _, _, pairs, size, _ = target.shape
+    stay, go_on = targets if sent else (targets[0].at[0], targets[0].at[1])
+    _, pairs, size, _ = stay.shape
     half, quarter = upstream.shape[1] // 2, normed_t.shape[0] // 4
     value_right = dvalue[...]
     lanes = value_right.shape[1]
@@ -282,25 +283,22 @@
                     rows[i].append(jnp.where(take_second, second, first))
     right = upstream[:, core_half(scalars, half)]
     own, far, out = [jnp.concatenate(parts, axis=0) for parts in rows]
-    grad_v = times((own, far), value_right).astype(target.dtype)
-    grad_o = dot_nn(out, right).astype(target.dtype)
-    for i, place in enumerate(places):
-        target[(*place, slice(None), slice(0, half))] = grad_o[i * size : (i + 1) * size]
+    grad_v = times((own, far), value_right).astype(stay.dtype)
+    grad_o = dot_nn(out, right).astype(stay.dtype)
+    for i, (dy, dx, pair) in enumerate(places):
+        (stay, go_on)[dy][dx, pair, :, :half] = grad_o[i * size : (i + 1) * size]
         for core in range(2):
             columns = slice(half + core * lanes, half + (core + 1) * lanes)
             part = grad_v[(2 * i + core) * size : (2 * i + core + 1) * size]
-            target[(*place, slice(None), columns)] = part
-
-
-def view_sum_kernel(keep, got, x_send, y_send, x_keep, y_keep):
-    half = y_send.shape[3]
-    for second in range(2):
-        for target, first in ((x_send, 1), (x_keep, 0)):
-            total = keep[second, first, :, :, half:] + got[second, first, :, :, half:].astype(jnp.float32)
-            target[second] = total.astype(target.dtype)
-        for target, first in ((y_send, 1), (y_keep, 0)):
-            total = keep[first, second, :, :, :half] + got[first, second, :, :, :half].astype(jnp.float32)
-            target[second] = total.astype(target.dtype)
+            (stay, go_on)[dx][dy, pair, :, columns] = part
+
+
+def view_sum_kernel(block, keep, got, x_part, y_part):
+    half = y_part.shape[3]
+    for i in range(2):
+        total = keep[block, i] + got[i].astype(jnp.float32)
+        x_part[i] = total[:, :, half:].astype(x_part.dtype)
+        y_part[i] = total[:, :, :half].astype(y_part.dtype)
 
 
 def first_sum_kernel(x_keep, x_got, y_keep, y_got, x_later, y_later, x_now, y_now):
@@ -564,18 +562,15 @@
 
     tile = (2 * o_rows, width // 2 + 2 * part)
     operands = (scalars, normed_t, normed_far_t, after(dvalue, dkey), mixed_t, mixed_other, upstream)
-    send, keep = (
-        call(
-            functools.partial(value_out_kernel, sent),
-            [shape((2, 2, pairs, *tile), kind)],
-            operands,
-            name,
-            SMEM,
-            24,
-        )[0]
-        for sent, kind, name in ((True, bf16, "grad_value_out_sent"), (False, f32, "grad_value_out_kept"))
+    tiles = (2, pairs, *tile)
+    stay, send = call(
+        functools.partial(value_out_kernel, True), [shape(tiles, bf16)] * 2, operands, "grad_value_out_sent", SMEM, 24
     )
     got = lax.ppermute(send, "view", neighbours)
+    got_stay = lax.ppermute(after(stay, got), "view", neighbours)
+    keep = call(
+        functools.partial(value_out_kernel, False), [shape((2, *tiles), f32)], operands, "grad_value_out_kept", SMEM, 24
+    )[0]
     q_later, k_later, q_now, k_now, q_keep, k_keep = call(
         query_key_kernel,
         [shape(block, bf16) for block in (q_block, q_block, q_block, q_block)]
@@ -591,6 +586,14 @@
         go_on_kernel, [shape(q_block, bf16), shape(q_block, bf16)], (after(q_keep, keep), q_got, k_keep, k_got), "first_sum_query_key"
     )
     q_second, k_second = second_exchange(later)
+    vo_shapes = ((2, pairs, 2 * o_rows, 2 * part), (2, pairs, 2 * o_rows, width // 2))
+
+    def view_sum(block, arrived, kind, name):
+        results = [shape(dims, kind) for dims in vo_shapes]
+        return call(functools.partial(view_sum_kernel, block), results, (keep, arrived), name)
+
+    vo_parts = view_sum(1, after(got, q_first, k_first), bf16, "view_sum_sent")
+    vo_got = first_exchange(vo_parts)
     qk_tile = (2 * q_rows, 2 * part)
     qk_send, qk_keep = call(
         query_key_tiles_kernel,
@@ -600,23 +603,15 @@
         SMEM,
     )
     qk_addends = (qk_keep, lax.ppermute(qk_send, "view", neighbours))
-    x_shape, y_shape = (2, pairs, 2 * o_rows, 2 * part), (2, pairs, 2 * o_rows, width // 2)
-    vo_parts = call(
-        view_sum_kernel,
-        [shape(x_shape, bf16), shape(y_shape, bf16), shape(x_shape, f32), shape(y_shape, f32)],
-        (keep, after(got, qk_send)),
-        "view_sum_value_out",
-    )
-    vo_got = first_exchange(vo_parts)
-    qk_last = last_parts(qk_addends, query_key_cores, "query_key")
-    vo_parts[2] = after(vo_parts[2], qk_last[0])
+    vo_parts = vo_parts + view_sum(0, after(got_stay, qk_send), f32, "view_sum_kept")
     vo_sums = first_sum(vo_parts, vo_got, "first_sum_value_out")
     v_got, o_got = second_exchange(vo_sums)
     addends = (vo_sums[3], o_got, vo_sums[2], v_got)
+    qk_last = last_parts((after(qk_addends[0], vo_sums[0]), qk_addends[1]), query_key_cores, "query_key")
     qk_total = call(
-        add_kernel, [shape((q_rows, 2 * part), f32)] * 2, qk_last, "last_sum_query_key", cost=MUCH
-    )
-    vo_last = last_parts((after(addends[0], qk_total[0]), *addends[1:]), value_out_cores, "value_out")
+        add_kernel, [shape((q_rows, 2 * part), f32)] * 2, qk_last, "last_sum_query_key"
+    )
+    vo_last = last_parts((after(addends[0], qk_last[0]), *addends[1:]), value_out_cores, "value_out")
     grad_query, grad_key = call(
         place_query_key_kernel,
         [shape((q_rows, inner), f32)] * 2,

time: 88.1 us -> 85.7 us (0.973)
  waiting for transfers between devices: 34.3 us -> 32.9 us
  starting transfers between devices: 31.5 us -> 30.4 us
    ppermute x1, waiting for transfers between devices: 1.03 us -> 9.24 us  [shards(): got = lax.ppermute(send, 'view', neighbours)]
    ppermute x3, waiting for transfers between devices: 7.03 us -> 1.14 us  [first_exchange(): lax.ppermute(sends[0], 'scene', along_x)]
    ppermute x3, waiting for transfers between devices: 3.21 us -> 0.01 us  [first_exchange(): lax.ppermute(sends[1], 'scene', along_y)]
    ppermute x2, waiting for transfers between devices: 0.01 us -> 1.51 us  [second_exchange(): lax.ppermute(sums[1], 'scene', along_x)]
    ppermute x2, waiting for transfers between devices: 7.72 us -> 6.6 us  [last_parts(): lax.ppermute(far_same, 'view', [(i, i ^ 2) for i in range(groups)])]
    ppermute x2, starting transfers between devices: 1.95 us -> 3.06 us  [second_exchange(): lax.ppermute(sums[1], 'scene', along_x)]
    ppermute x1, waiting for transfers between devices: 2.5 us -> 1.41 us  [shards(): qk_addends = (qk_keep, lax.ppermute(qk_send, 'view', neighbours))]
    ppermute x2, starting transfers between devices: 3.1 us -> 2.06 us  [second_exchange(): lax.ppermute(sums[0], 'scene', along_y)]
  transfers between devices with their start and end apart: 30 -> 31, of which waited for: 18 -> 16; matrix products, arithmetic and copies ran while one was open for 0% -> 0% of each run, Pallas kernels for 16% -> 17%
where the time goes in v21:
time: 85.7 us; the launch traced here: 85.6 us
  waiting for transfers between devices  32.9 us (38%)
  starting transfers between devices  30.4 us (35%)
  Pallas kernels  20.5 us (24%)
  between operations  0.91 us (1%)
  local copies, waits for them, and re-layouts  0.89 us (1%)
    pallas_call x14, Pallas kernels, call(): pl.pallas_call(kernel_body, in_specs=[first] + [VMEM] * (len(operands) -...  11.1 us
    ppermute x1, waiting for transfers between devices, shards(): got = lax.ppermute(send, 'view', neighbours)  9.24 us
    ppermute x2, waiting for transfers between devices, last_parts(): lax.ppermute(far_same, 'view', [(i, i ^ 2) for i in range(groups)])  6.6 us
    ppermute x2, waiting for transfers between devices, second_exchange(): lax.ppermute(sums[0], 'scene', along_y)  6.12 us
    ppermute x3, starting transfers between devices, shards(): granted = [lax.ppermute(partners, 'view', pairs) for pairs in between]  5.62 us
    ppermute x3, starting transfers between devices, shards(): lax.ppermute(part_out, 'view', pairs)  4.45 us
    pallas_call x1, Pallas kernels, shards(): pl.pallas_call(project_kernel, in_specs=[SMEM] + [VMEM] * 10, out_specs=[...  4.13 us
    ppermute x3, waiting for transfers between devices, shards(): granted = [lax.ppermute(partners, 'view', pairs) for pairs in between]  3.48 us
  transfers between devices with their start and end apart: 31, of which 16 were waited for; matrix products, arithmetic and copies ran while one was open for 0% of the time, Pallas kernels for 17%

profile of v21, /device:TPU:0, one launch (start us, length us, event | category | flops | bytes accessed | tf_op | source)
XLA Modules:
  0.0 85.6 jit_solution(14895905794555381271)
XLA Ops:
  0.6 0.8 copy.13.partners
  1.4 3.0 %collective-permute-start.2 = (s32[1,4,3]{2,1,0:T(4,128)S(1)}, s32[1,4,3]{2,1,0:T(4,128)S(1)}, u32[]{:S(2)}, u32[]{:S(2)}) collective-permute-start(s32[1,4,3]{2,1,0:T(4,128)S(1)} %copy.13.partners), channel_id=1, source_target_pairs={{0,2},{2,0},{4,6},{6,4},{1,3},{3,1},{5,7},{7,5},{8,10},{10,8},{12,... | collective-permute-start | bytes 152 | tf_op jit(solution)/shard_map/ppermute | solution.py:431
  4.4 2.6 %collective-permute-start.1 = (s32[1,4,3]{2,1,0:T(4,128)S(1)}, s32[1,4,3]{2,1,0:T(4,128)S(1)}, u32[]{:S(2)}, u32[]{:S(2)}) collective-permute-start(s32[1,4,3]{2,1,0:T(4,128)S(1)} %copy.13.partners), channel_id=1, source_target_pairs={{0,4},{2,6},{4,0},{6,2},{1,5},{3,7},{5,1},{7,3},{8,12},{10,14},{12... | collective-permute-start | bytes 152 | tf_op jit(solution)/shard_map/ppermute | solution.py:431
  7.0 0.5 collective-permute-start.7
  7.5 1.2 %alive.1 = s32[16]{0:T(128)S(1)} custom-call(s32[1,4,3]{2,1,0:T(4,128)S(1)} %copy.13.partners), custom_call_target="tpu_custom_call" | custom-call | flops 40000000000 | bytes 1 | tf_op jit(solution)/shard_map/alive/pallas_call | solution.py:421
  8.8 0.1 stack.23.scalars
  8.9 0.0 copy-start.5
  8.9 3.5 %collective-permute-done.refs_0_ = s32[1,4,3]{2,1,0:T(4,128)S(1)} collective-permute-done((s32[1,4,3]{2,1,0:T(4,128)S(1)}, s32[1,4,3]{2,1,0:T(4,128)S(1)}, u32[]{:S(2)}, u32[]{:S(2)}) %collective-permute-start) | collective-permute-done | bytes 80 | tf_op jit(solution)/shard_map/ppermute | solution.py:431
  12.4 0.8 pick.1
  13.2 0.4 collective-permute-start.3
  13.6 4.0 %collective-permute-start.5 = (bf16[32,1536]{1,0:T(8,128)(2,1)S(1)}, bf16[32,1536]{1,0:T(8,128)(2,1)S(1)}, u32[]{:S(2)}, u32[]{:S(2)}) collective-permute-start(bf16[32,1536]{1,0:T(8,128)(2,1)S(1)} %get-tuple-element.80), channel_id=1, source_target_pairs={{0,2},{2,0},{4,6},{6,4},{1,3},{3,1},{5,7},{7,5},{8,10},{10,8},{12,... | collective-permute-start | bytes 294920 | tf_op jit(solution)/shard_map/ppermute | solution.py:448
  17.7 4.1 %project.1 = (bf16[1536,256]{1,0:T(8,128)(2,1)S(1)}, bf16[256,384]{1,0:T(8,128)(2,1)S(1)}, bf16[256,384]{1,0:T(8,128)(2,1)S(1)}, bf16[256,1536]{1,0:T(8,128)(2,1...) custom-call(s32[5]{0:T(128)S(1)} %stack.23.scalars, ...), custom_call_target="tpu_custom_call" | custom-call | flops 1 | bytes 1 | tf_op jit(solution)/shard_map/project/pallas_call | solution.py:450
  21.9 0.4 collective-permute-done.4.refs_1_
  22.3 0.1 collective-permute-start.8
  22.4 0.4 collective-permute-start.9
  22.8 0.1 collective-permute-start.10
  22.9 0.7 collective-permute-done.8.refs_3_
  23.6 0.2 collective-permute-done.9.refs_4_
  23.7 0.4 collective-permute-done.10.refs_5_
  24.1 3.2 %attention_forward.1 = (bf16[1536,192]{1,0:T(8,128)(2,1)S(1)}, bf16[192,384]{1,0:T(8,128)(2,1)S(1)}, bf16[192,384]{1,0:T(8,128)(2,1)S(1)}, f32[3,64,512]{2,1,0:T...) custom-call(s32[5]{0:T(128)S(1)} %stack.23.scalars, ...), custom_call_target="tpu_custom_call" | custom-call | flops 1 | bytes 1 | tf_op jit(solution)/shard_map/attention_forward/pallas_call | solution.py:486
  27.3 0.2 collective-permute-start.11
  27.5 1.6 %attention_backward.1 = (bf16[256,384]{1,0:T(8,128)(2,1)S(1)}, bf16[448,384]{1,0:T(8,128)(2,1)S(1)}) custom-call(bf16[3,512,128]{2,1,0:T(8,128)(2,1)S(1)} %get-tuple-element.87.refs_6_.query_stack, bf16[3,512,128]{2,1,0:T(8,128)(2,1)S(1)} %get-tuple-element.88.refs_7_.grad_stack, f32[3,64,512]{2,1,0:T(8,128)S(1)} %get-tuple-element.92.dprob_own, ...), custom_call_target="tpu_custom_call" | custom-call | flops 1 | bytes 1 | tf_op jit(solution)/shard_map/attention_backward/pallas_call | solution.py:474
  29.1 1.3 %grad_value_out_sent.1 = (bf16[2,2,48,1536]{3,2,1,0:T(8,128)(2,1)S(1)}, bf16[2,2,48,1536]{3,2,1,0:T(8,128)(2,1)S(1)}) custom-call(s32[5]{0:T(128)S(1)} %stack.23.scalars, bf16[1536,256]{1,0:T(8,128)(2,1)S(1)} %get-tuple-element.82.normed_t, bf16[1536,192]{1,0:T(8,128)(2,1)S(1)} %get-tuple-element.91.normed_far_t, ...), custom_call_target="tpu_custom_call" | custom-call | flops 1 | bytes 1 | tf_op jit(solution)/shard_map/grad_value_out_sent/pallas_call | solution.py:474
  30.4 0.4 collective-permute-start.18
  30.7 1.9 %grad_query_key.1 = (bf16[384,384]{1,0:T(8,128)(2,1)S(1)}, bf16[384,384]{1,0:T(8,128)(2,1)S(1)}, bf16[384,384]{1,0:T(8,128)(2,1)S(1)}, bf16[384,384]{1,0:T(8,128...) custom-call(s32[5]{0:T(128)S(1)} %stack.23.scalars, ...), custom_call_target="tpu_custom_call" | custom-call | flops 1 | bytes 1 | tf_op jit(solution)/shard_map/grad_query_key/pallas_call | solution.py:474
  32.7 1.5 %collective-permute-start.13 = (bf16[384,384]{1,0:T(8,128)(2,1)S(1)}, bf16[384,384]{1,0:T(8,128)(2,1)S(1)}, u32[]{:S(2)}, u32[]{:S(2)}) collective-permute-start(bf16[384,384]{1,0:T(8,128)(2,1)S(1)} %get-tuple-element.109), channel_id=1, source_target_pairs={{0,8},{8,0},{16,24},{24,16},{1,9},{9,1},{17,25},{25,17},{2,10},{10... | collective-permute-start | bytes 884744 | tf_op jit(solution)/shard_map/ppermute | solution.py:524
  34.2 1.5 %collective-permute-start.14 = (bf16[384,384]{1,0:T(8,128)(2,1)S(1)}, bf16[384,384]{1,0:T(8,128)(2,1)S(1)}, u32[]{:S(2)}, u32[]{:S(2)}) collective-permute-start(bf16[384,384]{1,0:T(8,128)(2,1)S(1)} %get-tuple-element.111), channel_id=1, source_target_pairs={{0,16},{8,24},{16,0},{24,8},{1,17},{9,25},{17,1},{25,9},{2,18},{10... | collective-permute-start | bytes 884744 | tf_op jit(solution)/shard_map/ppermute | solution.py:524
  35.7 0.5 collective-permute-start.12
  36.3 0.5 collective-permute-start.16
  36.8 9.2 %collective-permute-done.18.got = bf16[2,2,48,1536]{3,2,1,0:T(8,128)(2,1)S(1)} collective-permute-done((bf16[2,2,48,1536]{3,2,1,0:T(8,128)(2,1)S(1)}, bf16[2,2,48,1536]{3,2,1,0:T(8,128)(2,1)S(1)}, u32[]{:S(2)}, u32[]{:S(2)}) %collective-permute-start.18) | collective-permute-done | bytes 589856 | tf_op jit(solution)/shard_map/ppermute | solution.py:569
  46.0 0.3 collective-permute-start.19
  46.3 1.3 %grad_value_out_kept.1.keep = f32[2,2,2,48,1536]{4,3,2,1,0:T(8,128)S(1)} custom-call(s32[5]{0:T(128)S(1)} %stack.23.scalars, bf16[1536,256]{1,0:T(8,128)(2,1)S(1)} %get-tuple-element.82.normed_t, bf16[1536,192]{1,0:T(8,128)(2,1)S(1)} %get-tuple-element.91.normed_far_t, bf16[448,384]{1,0:T(8,128)(2,1)S(1)} %get-tuple-element.101.dvalue, ...), custom_call_target="tpu_custom_call" | custom-call | flops 1 | bytes 1 | tf_op jit(solution)/shard_map/grad_value_out_kept/pallas_call | solution.py:474
  47.6 0.1 first_sum_query_key.1
  47.8 1.6 %collective-permute-start.15 = (bf16[384,384]{1,0:T(8,128)(2,1)S(1)}, bf16[384,384]{1,0:T(8,128)(2,1)S(1)}, u32[]{:S(2)}, u32[]{:S(2)}) collective-permute-start(bf16[384,384]{1,0:T(8,128)(2,1)S(1)} %get-tuple-element.112), channel_id=1, source_target_pairs={{0,16},{8,24},{16,0},{24,8},{1,17},{9,25},{17,1},{25,9},{2,18},{10... | collective-permute-start | bytes 884744 | tf_op jit(solution)/shard_map/ppermute | solution.py:532
  49.3 1.5 %collective-permute-start.17 = (bf16[384,384]{1,0:T(8,128)(2,1)S(1)}, bf16[384,384]{1,0:T(8,128)(2,1)S(1)}, u32[]{:S(2)}, u32[]{:S(2)}) collective-permute-start(bf16[384,384]{1,0:T(8,128)(2,1)S(1)} %get-tuple-element.114), channel_id=1, source_target_pairs={{0,8},{8,0},{16,24},{24,16},{1,9},{9,1},{17,25},{25,17},{2,10},{10... | collective-permute-start | bytes 884744 | tf_op jit(solution)/shard_map/ppermute | solution.py:532
  50.8 0.1 view_sum_sent.1
  50.9 0.6 collective-permute-start.20
  51.5 0.5 collective-permute-start.21
  52.1 5.7 %collective-permute-done.15.q_second = bf16[384,384]{1,0:T(8,128)(2,1)S(1)} collective-permute-done((bf16[384,384]{1,0:T(8,128)(2,1)S(1)}, bf16[384,384]{1,0:T(8,128)(2,1)S(1)}, u32[]{:S(2)}, u32[]{:S(2)}) %collective-permute-start.15) | collective-permute-done | bytes 294944 | tf_op jit(solution)/shard_map/ppermute | solution.py:532
  57.8 1.5 %collective-permute-done.17.k_second = bf16[384,384]{1,0:T(8,128)(2,1)S(1)} collective-permute-done((bf16[384,384]{1,0:T(8,128)(2,1)S(1)}, bf16[384,384]{1,0:T(8,128)(2,1)S(1)}, u32[]{:S(2)}, u32[]{:S(2)}) %collective-permute-start.17) | collective-permute-done | bytes 294944 | tf_op jit(solution)/shard_map/ppermute | solution.py:532
  59.3 0.8 second_sum_query_key.1
  60.1 1.8 %collective-permute-start.22 = (bf16[2,96,768]{2,1,0:T(8,128)(2,1)S(1)}, bf16[2,96,768]{2,1,0:T(8,128)(2,1)S(1)}, u32[]{:S(2)}, u32[]{:S(2)}) collective-permute-start(bf16[2,96,768]{2,1,0:T(8,128)(2,1)S(1)} %get-tuple-element.118), channel_id=1, source_target_pairs={{0,2},{2,0},{4,6},{6,4},{1,3},{3,1},{5,7},{7,5},{8,10},{10,8},{12,... | collective-permute-start | bytes 884744 | tf_op jit(solution)/shard_map/ppermute | solution.py:605
  61.9 0.4 collective-permute-done.19.got
  62.3 0.1 view_sum_kept.1
  62.4 1.1 %collective-permute-done.20.x_got = bf16[2,2,48,768]{3,2,1,0:T(8,128)(2,1)S(1)} collective-permute-done((bf16[2,2,48,768]{3,2,1,0:T(8,128)(2,1)S(1)}, bf16[2,2,48,768]{3,2,1,0:T(8,128)(2,1)S(1)}, u32[]{:S(2)}, u32[]{:S(2)}) %collective-permute-start.20) | collective-permute-done | bytes 294944 | tf_op jit(solution)/shard_map/ppermute | solution.py:524
  63.6 0.1 first_sum_value_out.1
  63.7 1.6 %collective-permute-start.26 = (bf16[2,48,768]{2,1,0:T(8,128)(2,1)S(1)}, bf16[2,48,768]{2,1,0:T(8,128)(2,1)S(1)}, u32[]{:S(2)}, u32[]{:S(2)}) collective-permute-start(bf16[2,48,768]{2,1,0:T(8,128)(2,1)S(1)} %get-tuple-element.137), channel_id=1, source_target_pairs={{0,8},{8,0},{16,24},{24,16},{1,9},{9,1},{17,25},{25,17},{2,10},{10... | collective-permute-start | bytes 442376 | tf_op jit(solution)/shard_map/ppermute | solution.py:532
  65.2 0.5 collective-permute-start.27
  65.7 1.4 %collective-permute-done.22.refs_1_ = bf16[2,96,768]{2,1,0:T(8,128)(2,1)S(1)} collective-permute-done((bf16[2,96,768]{2,1,0:T(8,128)(2,1)S(1)}, bf16[2,96,768]{2,1,0:T(8,128)(2,1)S(1)}, u32[]{:S(2)}, u32[]{:S(2)}) %collective-permute-start.22) | collective-permute-done | bytes 294944 | tf_op jit(solution)/shard_map/ppermute | solution.py:605
  67.1 0.6 last_parts_query_key.1
  67.8 0.1 collective-permute-start.24
  67.9 2.1 %collective-permute-start.23 = (bf16[48,768]{1,0:T(8,128)(2,1)S(1)}, bf16[48,768]{1,0:T(8,128)(2,1)S(1)}, u32[]{:S(2)}, u32[]{:S(2)}) collective-permute-start(bf16[48,768]{1,0:T(8,128)(2,1)S(1)} %get-tuple-element.128), channel_id=1, source_target_pairs={{0,4},{2,6},{4,0},{6,2},{1,5},{3,7},{5,1},{7,3},{8,12},{10,14},{12... | collective-permute-start | bytes 221192 | tf_op jit(solution)/shard_map/ppermute | solution.py:558
  70.0 0.4 collective-permute-done.27.refs_3_
  70.4 0.6 last_parts_value_out.1
  71.0 0.1 collective-permute-start.29
  71.1 2.4 %collective-permute-start.25 = (bf16[48,768]{1,0:T(8,128)(2,1)S(1)}, bf16[48,768]{1,0:T(8,128)(2,1)S(1)}, u32[]{:S(2)}, u32[]{:S(2)}) collective-permute-start(bf16[48,768]{1,0:T(8,128)(2,1)S(1)} %get-tuple-element.130), channel_id=1, source_target_pairs={{0,5},{1,4},{2,7},{3,6},{4,1},{5,0},{6,3},{7,2},{8,13},{9,12},{10,... | collective-permute-start | bytes 221192 | tf_op jit(solution)/shard_map/ppermute | solution.py:559
  73.5 0.6 collective-permute-start.28
  74.1 0.9 %collective-permute-done.23.far_same = bf16[48,768]{1,0:T(8,128)(2,1)S(1)} collective-permute-done((bf16[48,768]{1,0:T(8,128)(2,1)S(1)}, bf16[48,768]{1,0:T(8,128)(2,1)S(1)}, u32[]{:S(2)}, u32[]{:S(2)}) %collective-permute-start.23) | collective-permute-done | bytes 73760 | tf_op jit(solution)/shard_map/ppermute | solution.py:558
  75.0 0.8 collective-permute-start.30
  75.9 0.3 collective-permute-done.25.far_cross
  76.2 1.3 %place_query_key.1 = (f32[48,768]{1,0:T(8,128)}, f32[48,768]{1,0:T(8,128)}) custom-call(s32[5]{0:T(128)S(1)} %stack.23.scalars, f32[48,768]{1,0:T(8,128)S(1)} %get-tuple-element.131.same, f32[48,768]{1,0:T(8,128)S(1)} %get-tuple-element.132.cross), custom_call_target="tpu_custom_call" | custom-call | flops 1 | bytes 1 | tf_op jit(solution)/shard_map/place_query_key/pallas_call | solution.py:474
  77.5 5.7 %collective-permute-done.28.far_same = bf16[24,1536]{1,0:T(8,128)(2,1)S(1)} collective-permute-done((bf16[24,1536]{1,0:T(8,128)(2,1)S(1)}, bf16[24,1536]{1,0:T(8,128)(2,1)S(1)}, u32[]{:S(2)}, u32[]{:S(2)}) %collective-permute-start.28) | collective-permute-done | bytes 73760 | tf_op jit(solution)/shard_map/ppermute | solution.py:558
  83.2 1.0 %collective-permute-done.30.far_cross = bf16[24,1536]{1,0:T(8,128)(2,1)S(1)} collective-permute-done((bf16[24,1536]{1,0:T(8,128)(2,1)S(1)}, bf16[24,1536]{1,0:T(8,128)(2,1)S(1)}, u32[]{:S(2)}, u32[]{:S(2)}) %collective-permute-start.30) | collective-permute-done | bytes 73760 | tf_op jit(solution)/shard_map/ppermute | solution.py:559
  84.3 1.3 %last_sum_value_out.1 = (f32[48,768]{1,0:T(8,128)}, f32[24,1536]{1,0:T(8,128)}) custom-call(s32[5]{0:T(128)S(1)} %stack.23.scalars, f32[24,1536]{1,0:T(8,128)S(1)} %get-tuple-element.140.mine, bf16[24,1536]{1,0:T(8,128)(2,1)S(1)} %collective-permute-done.28.far_same, f32[24,1536]{1,0:T(8,128)S(1)} %collective-permute-done.29.near_cross, ...), custom_call_target="tpu_custom_call" | custom-call | flops 1 | bytes 1 | tf_op jit(solution)/shard_map/last_sum_value_out/pallas_call | solution.py:474
  (34 shorter events, 0.1 us)
Async XLA Ops:
  1.4 7.5 %collective-permute-start.2 = (s32[1,4,3]{2,1,0:T(4,128)S(1)}, s32[1,4,3]{2,1,0:T(4,128)S(1)}, u32[]{:S(2)}, u32[]{:S(2)}) collective-permute-start(s32[1,4,3]{2,1,0:T(4,128)S(1)} %copy.13.partners), channel_id=1, source_target_pairs={{0,2},{2,0},{4,6},{6,4},{1,3},{3,1},{5,7},{7,5},{8,10},{10,8},{12,... | collective-permute-start | bytes 152 | tf_op jit(solution)/shard_map/ppermute | solution.py:431
  4.4 4.5 %collective-permute-start.1 = (s32[1,4,3]{2,1,0:T(4,128)S(1)}, s32[1,4,3]{2,1,0:T(4,128)S(1)}, u32[]{:S(2)}, u32[]{:S(2)}) collective-permute-start(s32[1,4,3]{2,1,0:T(4,128)S(1)} %copy.13.partners), channel_id=1, source_target_pairs={{0,4},{2,6},{4,0},{6,2},{1,5},{3,7},{5,1},{7,3},{8,12},{10,14},{12... | collective-permute-start | bytes 152 | tf_op jit(solution)/shard_map/ppermute | solution.py:431
  7.0 5.4 %collective-permute-start = (s32[1,4,3]{2,1,0:T(4,128)S(1)}, s32[1,4,3]{2,1,0:T(4,128)S(1)}, u32[]{:S(2)}, u32[]{:S(2)}) collective-permute-start(s32[1,4,3]{2,1,0:T(4,128)S(1)} %copy.13.partners), channel_id=1, source_target_pairs={{0,6},{2,4},{4,2},{6,0},{1,7},{3,5},{5,3},{7,1},{8,14},{10,12},{12... | collective-permute-start | bytes 152 | tf_op jit(solution)/shard_map/ppermute | solution.py:431
  7.0 10.6 %collective-permute-start.6 = (bf16[4,32,1536]{2,1,0:T(8,128)(2,1)}, bf16[4,32,1536]{2,1,0:T(8,128)(2,1)S(1)}, u32[]{:S(2)}, u32[]{:S(2)}) collective-permute-start(bf16[4,32,1536]{2,1,0:T(8,128)(2,1)} %bitcast.7), channel_id=1, source_target_pairs={{0,1},{1,0},{2,3},{3,2},{4,5},{5,4},{6,7},{7,6},{8,9},{9,8},{10,11... | collective-permute-start | bytes 1179656 | tf_op jit(solution)/shard_map/ppermute | solution.py:436
  7.0 10.6 %collective-permute-start.7 = (bf16[4,32,1536]{2,1,0:T(8,128)(2,1)}, bf16[4,32,1536]{2,1,0:T(8,128)(2,1)S(1)}, u32[]{:S(2)}, u32[]{:S(2)}) collective-permute-start(bf16[4,32,1536]{2,1,0:T(8,128)(2,1)} %bitcast.10), channel_id=1, source_target_pairs={{0,1},{1,0},{2,3},{3,2},{4,5},{5,4},{6,7},{7,6},{8,9},{9,8},{10,11... | collective-permute-start | bytes 1179656 | tf_op jit(solution)/shard_map/ppermute | solution.py:437
  7.5 4.9 %copy-start.4 = (bf16[1,4,1,32,1536]{4,3,2,1,0:T(8,128)(2,1)S(1)}, bf16[1,4,1,32,1536]{4,3,2,1,0:T(8,128)(2,1)}, u32[]{:S(2)}) copy-start(bf16[1,4,1,32,1536]{4,3,2,1,0:T(8,128)(2,1)} %param.10) | copy-start | bytes 1179652
  8.8 8.8 %copy-start = (bf16[1536,768]{1,0:T(8,128)(2,1)S(1)}, bf16[1536,768]{1,0:T(8,128)(2,1)}, u32[]{:S(2)}) copy-start(bf16[1536,768]{1,0:T(8,128)(2,1)} %refs_11_.1) | copy-start | bytes 7077892
  8.9 8.8 %copy-start.1 = (bf16[1536,768]{1,0:T(8,128)(2,1)S(1)}, bf16[1536,768]{1,0:T(8,128)(2,1)}, u32[]{:S(2)}) copy-start(bf16[1536,768]{1,0:T(8,128)(2,1)} %refs_12_.1) | copy-start | bytes 7077892
  8.9 8.8 %copy-start.2 = (bf16[1536,768]{1,0:T(8,128)(2,1)S(1)}, bf16[1536,768]{1,0:T(8,128)(2,1)}, u32[]{:S(2)}) copy-start(bf16[1536,768]{1,0:T(8,128)(2,1)} %w_query.1) | copy-start | bytes 7077892
  8.9 8.8 %copy-start.3 = (bf16[768,1536]{1,0:T(8,128)(2,1)S(1)}, bf16[768,1536]{1,0:T(8,128)(2,1)}, u32[]{:S(2)}) copy-start(bf16[768,1536]{1,0:T(8,128)(2,1)} %w_out.1) | copy-start | bytes 7077892
  8.9 8.8 %copy-start.5 = (bf16[1,4,1,32,1536]{4,3,2,1,0:T(8,128)(2,1)S(1)}, bf16[1,4,1,32,1536]{4,3,2,1,0:T(8,128)(2,1)}, u32[]{:S(2)}) copy-start(bf16[1,4,1,32,1536]{4,3,2,1,0:T(8,128)(2,1)} %param.18) | copy-start | bytes 1179652
  8.9 8.8 %copy-start.6 = (bf16[9,1536]{1,0:T(8,128)(2,1)S(1)}, bf16[9,1536]{1,0:T(8,128)(2,1)}, u32[]{:S(2)}) copy-start(bf16[9,1536]{1,0:T(8,128)(2,1)} %taps.1) | copy-start | bytes 82948
  8.9 8.8 %copy-start.7 = (f32[1536]{0:T(1024)S(1)}, f32[1536]{0:T(1024)}, u32[]{:S(2)}) copy-start(f32[1536]{0:T(1024)} %refs_10_.1) | copy-start | bytes 18436
  13.2 8.7 %collective-permute-start.3 = (bf16[32,1536]{1,0:T(8,128)(2,1)S(1)}, bf16[32,1536]{1,0:T(8,128)(2,1)S(1)}, u32[]{:S(2)}, u32[]{:S(2)}) collective-permute-start(bf16[32,1536]{1,0:T(8,128)(2,1)S(1)} %get-tuple-element.78), channel_id=1, source_target_pairs={{0,6},{2,4},{4,2},{6,0},{1,7},{3,5},{5,3},{7,1},{8,14},{10,12},{12... | collective-permute-start | bytes 294920 | tf_op jit(solution)/shard_map/ppermute | solution.py:448
  13.6 8.7 %collective-permute-start.4 = (bf16[32,1536]{1,0:T(8,128)(2,1)S(1)}, bf16[32,1536]{1,0:T(8,128)(2,1)S(1)}, u32[]{:S(2)}, u32[]{:S(2)}) collective-permute-start(bf16[32,1536]{1,0:T(8,128)(2,1)S(1)} %get-tuple-element.79), channel_id=1, source_target_pairs={{0,4},{2,6},{4,0},{6,2},{1,5},{3,7},{5,1},{7,3},{8,12},{10,14},{12... | collective-permute-start | bytes 294920 | tf_op jit(solution)/shard_map/ppermute | solution.py:448
  13.6 8.7 %collective-permute-start.5 = (bf16[32,1536]{1,0:T(8,128)(2,1)S(1)}, bf16[32,1536]{1,0:T(8,128)(2,1)S(1)}, u32[]{:S(2)}, u32[]{:S(2)}) collective-permute-start(bf16[32,1536]{1,0:T(8,128)(2,1)S(1)} %get-tuple-element.80), channel_id=1, source_target_pairs={{0,2},{2,0},{4,6},{6,4},{1,3},{3,1},{5,7},{7,5},{8,10},{10,8},{12,... | collective-permute-start | bytes 294920 | tf_op jit(solution)/shard_map/ppermute | solution.py:448
  22.3 1.3 %collective-permute-start.8 = (bf16[32,1536]{1,0:T(8,128)(2,1)S(1)}, bf16[32,1536]{1,0:T(8,128)(2,1)S(1)}, u32[]{:S(2)}, u32[]{:S(2)}) collective-permute-start(bf16[32,1536]{1,0:T(8,128)(2,1)S(1)} %collective-permute-done.3.refs_0_), channel_id=1, source_target_pairs={{0,1},{1,0},{2,3},{3,2},{4,5},{5,4},{6,7},{7,6},{8,9},{9,8},{10,11... | collective-permute-start | bytes 294920 | tf_op jit(solution)/shard_map/ppermute | solution.py:471
  22.4 1.4 %collective-permute-start.9 = (bf16[32,1536]{1,0:T(8,128)(2,1)S(1)}, bf16[32,1536]{1,0:T(8,128)(2,1)S(1)}, u32[]{:S(2)}, u32[]{:S(2)}) collective-permute-start(bf16[32,1536]{1,0:T(8,128)(2,1)S(1)} %collective-permute-done.4.refs_1_), channel_id=1, source_target_pairs={{0,1},{1,0},{2,3},{3,2},{4,5},{5,4},{6,7},{7,6},{8,9},{9,8},{10,11... | collective-permute-start | bytes 294920 | tf_op jit(solution)/shard_map/ppermute | solution.py:471
  22.8 1.3 %collective-permute-start.10 = (bf16[32,1536]{1,0:T(8,128)(2,1)S(1)}, bf16[32,1536]{1,0:T(8,128)(2,1)S(1)}, u32[]{:S(2)}, u32[]{:S(2)}) collective-permute-start(bf16[32,1536]{1,0:T(8,128)(2,1)S(1)} %collective-permute-done.5.refs_2_), channel_id=1, source_target_pairs={{0,1},{1,0},{2,3},{3,2},{4,5},{5,4},{6,7},{7,6},{8,9},{9,8},{10,11... | collective-permute-start | bytes 294920 | tf_op jit(solution)/shard_map/ppermute | solution.py:471
  27.3 1.8 %collective-permute-start.11 = (bf16[384,256]{1,0:T(8,128)(2,1)S(1)}, bf16[384,256]{1,0:T(8,128)(2,1)S(1)}, u32[]{:S(2)}, u32[]{:S(2)}) collective-permute-start(bf16[384,256]{1,0:T(8,128)(2,1)S(1)} %get-tuple-element.102.mine), channel_id=1, source_target_pairs={{0,1},{1,0},{2,3},{3,2},{4,5},{5,4},{6,7},{7,6},{8,9},{9,8},{10,11... | collective-permute-start | bytes 589832 | tf_op jit(solution)/shard_map/ppermute | solution.py:506
  30.4 15.7 %collective-permute-start.18 = (bf16[2,2,48,1536]{3,2,1,0:T(8,128)(2,1)S(1)}, bf16[2,2,48,1536]{3,2,1,0:T(8,128)(2,1)S(1)}, u32[]{:S(2)}, u32[]{:S(2)}) collective-permute-start(bf16[2,2,48,1536]{3,2,1,0:T(8,128)(2,1)S(1)} %get-tuple-element.104), channel_id=1, source_target_pairs={{0,2},{2,0},{4,6},{6,4},{1,3},{3,1},{5,7},{7,5},{8,10},{10,8},{12,... | collective-permute-start | bytes 1769480 | tf_op jit(solution)/shard_map/ppermute | solution.py:569
  32.7 14.9 %collective-permute-start.13 = (bf16[384,384]{1,0:T(8,128)(2,1)S(1)}, bf16[384,384]{1,0:T(8,128)(2,1)S(1)}, u32[]{:S(2)}, u32[]{:S(2)}) collective-permute-start(bf16[384,384]{1,0:T(8,128)(2,1)S(1)} %get-tuple-element.109), channel_id=1, source_target_pairs={{0,8},{8,0},{16,24},{24,16},{1,9},{9,1},{17,25},{25,17},{2,10},{10... | collective-permute-start | bytes 884744 | tf_op jit(solution)/shard_map/ppermute | solution.py:524
  34.2 13.4 %collective-permute-start.14 = (bf16[384,384]{1,0:T(8,128)(2,1)S(1)}, bf16[384,384]{1,0:T(8,128)(2,1)S(1)}, u32[]{:S(2)}, u32[]{:S(2)}) collective-permute-start(bf16[384,384]{1,0:T(8,128)(2,1)S(1)} %get-tuple-element.111), channel_id=1, source_target_pairs={{0,16},{8,24},{16,0},{24,8},{1,17},{9,25},{17,1},{25,9},{2,18},{10... | collective-permute-start | bytes 884744 | tf_op jit(solution)/shard_map/ppermute | solution.py:524
  35.7 15.1 %collective-permute-start.12 = (bf16[384,384]{1,0:T(8,128)(2,1)S(1)}, bf16[384,384]{1,0:T(8,128)(2,1)S(1)}, u32[]{:S(2)}, u32[]{:S(2)}) collective-permute-start(bf16[384,384]{1,0:T(8,128)(2,1)S(1)} %get-tuple-element.107), channel_id=1, source_target_pairs={{0,8},{8,0},{16,24},{24,16},{1,9},{9,1},{17,25},{25,17},{2,10},{10... | collective-permute-start | bytes 884744 | tf_op jit(solution)/shard_map/ppermute | solution.py:524
  36.3 14.5 %collective-permute-start.16 = (bf16[384,384]{1,0:T(8,128)(2,1)S(1)}, bf16[384,384]{1,0:T(8,128)(2,1)S(1)}, u32[]{:S(2)}, u32[]{:S(2)}) collective-permute-start(bf16[384,384]{1,0:T(8,128)(2,1)S(1)} %get-tuple-element.113), channel_id=1, source_target_pairs={{0,16},{8,24},{16,0},{24,8},{1,17},{9,25},{17,1},{25,9},{2,18},{10... | collective-permute-start | bytes 884744 | tf_op jit(solution)/shard_map/ppermute | solution.py:524
  46.0 16.3 %collective-permute-start.19 = (bf16[2,2,48,1536]{3,2,1,0:T(8,128)(2,1)S(1)}, bf16[2,2,48,1536]{3,2,1,0:T(8,128)(2,1)S(1)}, u32[]{:S(2)}, u32[]{:S(2)}) collective-permute-start(bf16[2,2,48,1536]{3,2,1,0:T(8,128)(2,1)S(1)} %get-tuple-element.117), channel_id=1, source_target_pairs={{0,2},{2,0},{4,6},{6,4},{1,3},{3,1},{5,7},{7,5},{8,10},{10,8},{12,... | collective-permute-start | bytes 1769480 | tf_op jit(solution)/shard_map/ppermute | solution.py:570
  47.8 10.0 %collective-permute-start.15 = (bf16[384,384]{1,0:T(8,128)(2,1)S(1)}, bf16[384,384]{1,0:T(8,128)(2,1)S(1)}, u32[]{:S(2)}, u32[]{:S(2)}) collective-permute-start(bf16[384,384]{1,0:T(8,128)(2,1)S(1)} %get-tuple-element.112), channel_id=1, source_target_pairs={{0,16},{8,24},{16,0},{24,8},{1,17},{9,25},{17,1},{25,9},{2,18},{10... | collective-permute-start | bytes 884744 | tf_op jit(solution)/shard_map/ppermute | solution.py:532
  49.3 9.9 %collective-permute-start.17 = (bf16[384,384]{1,0:T(8,128)(2,1)S(1)}, bf16[384,384]{1,0:T(8,128)(2,1)S(1)}, u32[]{:S(2)}, u32[]{:S(2)}) collective-permute-start(bf16[384,384]{1,0:T(8,128)(2,1)S(1)} %get-tuple-element.114), channel_id=1, source_target_pairs={{0,8},{8,0},{16,24},{24,16},{1,9},{9,1},{17,25},{25,17},{2,10},{10... | collective-permute-start | bytes 884744 | tf_op jit(solution)/shard_map/ppermute | solution.py:532
  50.9 12.6 %collective-permute-start.20 = (bf16[2,2,48,768]{3,2,1,0:T(8,128)(2,1)S(1)}, bf16[2,2,48,768]{3,2,1,0:T(8,128)(2,1)S(1)}, u32[]{:S(2)}, u32[]{:S(2)}) collective-permute-start(bf16[2,2,48,768]{3,2,1,0:T(8,128)(2,1)S(1)} %get-tuple-element.122), channel_id=1, source_target_pairs={{0,8},{8,0},{16,24},{24,16},{1,9},{9,1},{17,25},{25,17},{2,10},{10... | collective-permute-start | bytes 884744 | tf_op jit(solution)/shard_map/ppermute | solution.py:524
  51.5 12.0 %collective-permute-start.21 = (bf16[2,2,48,768]{3,2,1,0:T(8,128)(2,1)S(1)}, bf16[2,2,48,768]{3,2,1,0:T(8,128)(2,1)S(1)}, u32[]{:S(2)}, u32[]{:S(2)}) collective-permute-start(bf16[2,2,48,768]{3,2,1,0:T(8,128)(2,1)S(1)} %get-tuple-element.124), channel_id=1, source_target_pairs={{0,16},{8,24},{16,0},{24,8},{1,17},{9,25},{17,1},{25,9},{2,18},{10... | collective-permute-start | bytes 884744 | tf_op jit(solution)/shard_map/ppermute | solution.py:524
  60.1 7.1 %collective-permute-start.22 = (bf16[2,96,768]{2,1,0:T(8,128)(2,1)S(1)}, bf16[2,96,768]{2,1,0:T(8,128)(2,1)S(1)}, u32[]{:S(2)}, u32[]{:S(2)}) collective-permute-start(bf16[2,96,768]{2,1,0:T(8,128)(2,1)S(1)} %get-tuple-element.118), channel_id=1, source_target_pairs={{0,2},{2,0},{4,6},{6,4},{1,3},{3,1},{5,7},{7,5},{8,10},{10,8},{12,... | collective-permute-start | bytes 884744 | tf_op jit(solution)/shard_map/ppermute | solution.py:605
  63.7 6.3 %collective-permute-start.26 = (bf16[2,48,768]{2,1,0:T(8,128)(2,1)S(1)}, bf16[2,48,768]{2,1,0:T(8,128)(2,1)S(1)}, u32[]{:S(2)}, u32[]{:S(2)}) collective-permute-start(bf16[2,48,768]{2,1,0:T(8,128)(2,1)S(1)} %get-tuple-element.137), channel_id=1, source_target_pairs={{0,8},{8,0},{16,24},{24,16},{1,9},{9,1},{17,25},{25,17},{2,10},{10... | collective-permute-start | bytes 442376 | tf_op jit(solution)/shard_map/ppermute | solution.py:532
  65.2 5.1 %collective-permute-start.27 = (bf16[2,48,768]{2,1,0:T(8,128)(2,1)S(1)}, bf16[2,48,768]{2,1,0:T(8,128)(2,1)S(1)}, u32[]{:S(2)}, u32[]{:S(2)}) collective-permute-start(bf16[2,48,768]{2,1,0:T(8,128)(2,1)S(1)} %get-tuple-element.125), channel_id=1, source_target_pairs={{0,16},{8,24},{16,0},{24,8},{1,17},{9,25},{17,1},{25,9},{2,18},{10... | collective-permute-start | bytes 442376 | tf_op jit(solution)/shard_map/ppermute | solution.py:532
  67.8 8.4 %collective-permute-start.24 = (f32[48,768]{1,0:T(8,128)S(1)}, f32[48,768]{1,0:T(8,128)S(1)}, u32[]{:S(2)}, u32[]{:S(2)}) collective-permute-start(f32[48,768]{1,0:T(8,128)S(1)} %get-tuple-element.129), channel_id=1, source_target_pairs={{0,1},{1,0},{2,3},{3,2},{4,5},{5,4},{6,7},{7,6},{8,9},{9,8},{10,11... | collective-permute-start | bytes 442376 | tf_op jit(solution)/shard_map/ppermute | solution.py:560
  67.9 7.2 %collective-permute-start.23 = (bf16[48,768]{1,0:T(8,128)(2,1)S(1)}, bf16[48,768]{1,0:T(8,128)(2,1)S(1)}, u32[]{:S(2)}, u32[]{:S(2)}) collective-permute-start(bf16[48,768]{1,0:T(8,128)(2,1)S(1)} %get-tuple-element.128), channel_id=1, source_target_pairs={{0,4},{2,6},{4,0},{6,2},{1,5},{3,7},{5,1},{7,3},{8,12},{10,14},{12... | collective-permute-start | bytes 221192 | tf_op jit(solution)/shard_map/ppermute | solution.py:558
  71.0 13.2 %collective-permute-start.29 = (f32[24,1536]{1,0:T(8,128)S(1)}, f32[24,1536]{1,0:T(8,128)S(1)}, u32[]{:S(2)}, u32[]{:S(2)}) collective-permute-start(f32[24,1536]{1,0:T(8,128)S(1)} %get-tuple-element.142), channel_id=1, source_target_pairs={{0,1},{1,0},{2,3},{3,2},{4,5},{5,4},{6,7},{7,6},{8,9},{9,8},{10,11... | collective-permute-start | bytes 442376 | tf_op jit(solution)/shard_map/ppermute | solution.py:560
  71.1 5.1 %collective-permute-start.25 = (bf16[48,768]{1,0:T(8,128)(2,1)S(1)}, bf16[48,768]{1,0:T(8,128)(2,1)S(1)}, u32[]{:S(2)}, u32[]{:S(2)}) collective-permute-start(bf16[48,768]{1,0:T(8,128)(2,1)S(1)} %get-tuple-element.130), channel_id=1, source_target_pairs={{0,5},{1,4},{2,7},{3,6},{4,1},{5,0},{6,3},{7,2},{8,13},{9,12},{10,... | collective-permute-start | bytes 221192 | tf_op jit(solution)/shard_map/ppermute | solution.py:559
  73.5 9.7 %collective-permute-start.28 = (bf16[24,1536]{1,0:T(8,128)(2,1)S(1)}, bf16[24,1536]{1,0:T(8,128)(2,1)S(1)}, u32[]{:S(2)}, u32[]{:S(2)}) collective-permute-start(bf16[24,1536]{1,0:T(8,128)(2,1)S(1)} %get-tuple-element.141), channel_id=1, source_target_pairs={{0,4},{2,6},{4,0},{6,2},{1,5},{3,7},{5,1},{7,3},{8,12},{10,14},{12... | collective-permute-start | bytes 221192 | tf_op jit(solution)/shard_map/ppermute | solution.py:558
  75.0 9.2 %collective-permute-start.30 = (bf16[24,1536]{1,0:T(8,128)(2,1)S(1)}, bf16[24,1536]{1,0:T(8,128)(2,1)S(1)}, u32[]{:S(2)}, u32[]{:S(2)}) collective-permute-start(bf16[24,1536]{1,0:T(8,128)(2,1)S(1)} %get-tuple-element.143), channel_id=1, source_target_pairs={{0,5},{1,4},{2,7},{3,6},{4,1},{5,0},{6,3},{7,2},{8,13},{9,12},{10,... | collective-permute-start | bytes 221192 | tf_op jit(solution)/shard_map/ppermute | solution.py:559

commit v22 on v21

--- a/solution.py
+++ b/solution.py
@@ -567,7 +567,6 @@
         functools.partial(value_out_kernel, True), [shape(tiles, bf16)] * 2, operands, "grad_value_out_sent", SMEM, 24
     )
     got = lax.ppermute(send, "view", neighbours)
-    got_stay = lax.ppermute(after(stay, got), "view", neighbours)
     keep = call(
         functools.partial(value_out_kernel, False), [shape((2, *tiles), f32)], operands, "grad_value_out_kept", SMEM, 24
     )[0]
@@ -586,6 +585,7 @@
         go_on_kernel, [shape(q_block, bf16), shape(q_block, bf16)], (after(q_keep, keep), q_got, k_keep, k_got), "first_sum_query_key"
     )
     q_second, k_second = second_exchange(later)
+    got_stay = lax.ppermute(after(stay, got, later[0]), "view", neighbours)
     vo_shapes = ((2, pairs, 2 * o_rows, 2 * part), (2, pairs, 2 * o_rows, width // 2))
 
     def view_sum(block, arrived, kind, name):

time: 85.7 us -> 84.1 us (0.981)
  waiting for transfers between devices: 32.9 us -> 31.1 us
    ppermute x1, waiting for transfers between devices: 9.24 us -> 1.78 us  [shards(): got = lax.ppermute(send, 'view', neighbours)]
    ppermute x2, waiting for transfers between devices: 1.37 us -> 6.12 us  [last_parts(): lax.ppermute(far_cross, ('view', 'row'), [(i, i ^ 5) for i in range(targe...]
    ppermute x2, waiting for transfers between devices: 6.6 us -> 2.14 us  [last_parts(): lax.ppermute(far_same, 'view', [(i, i ^ 2) for i in range(groups)])]
    ppermute x2, waiting for transfers between devices: 6.12 us -> 1.71 us  [second_exchange(): lax.ppermute(sums[0], 'scene', along_y)]
    ppermute x3, waiting for transfers between devices: 1.14 us -> 4.48 us  [first_exchange(): lax.ppermute(sends[0], 'scene', along_x)]
    ppermute x2, waiting for transfers between devices: 1.51 us -> 4.77 us  [second_exchange(): lax.ppermute(sums[1], 'scene', along_x)]
    ppermute x2, starting transfers between devices: 3.28 us -> 1.68 us  [last_parts(): lax.ppermute(far_cross, ('view', 'row'), [(i, i ^ 5) for i in range(targe...]
    ppermute x1, waiting for transfers between devices: 0.39 us -> 1.91 us  [shards(): got_stay = lax.ppermute(after(stay, got, later[0]), 'view', neighbours)]
  transfers between devices with their start and end apart: 31 -> 31, of which waited for: 16 -> 17; matrix products, arithmetic and copies ran while one was open for 0% -> 0% of each run, Pallas kernels for 17% -> 18%
where the time goes in v22:
time: 84.1 us; the launch traced here: 83.9 us
  waiting for transfers between devices  31.1 us (37%)
  starting transfers between devices  30.5 us (36%)
  Pallas kernels  20.5 us (24%)
  between operations  0.91 us (1%)
  local copies, waits for them, and re-layouts  0.89 us (1%)
    pallas_call x14, Pallas kernels, call(): pl.pallas_call(kernel_body, in_specs=[first] + [VMEM] * (len(operands) -...  11.2 us
    ppermute x2, waiting for transfers between devices, last_parts(): lax.ppermute(far_cross, ('view', 'row'), [(i, i ^ 5) for i in range(targe...  6.12 us
    ppermute x3, starting transfers between devices, shards(): granted = [lax.ppermute(partners, 'view', pairs) for pairs in between]  5.62 us
    ppermute x2, waiting for transfers between devices, second_exchange(): lax.ppermute(sums[1], 'scene', along_x)  4.77 us
    ppermute x3, waiting for transfers between devices, first_exchange(): lax.ppermute(sends[0], 'scene', along_x)  4.48 us
    ppermute x3, starting transfers between devices, shards(): lax.ppermute(part_out, 'view', pairs)  4.45 us
    pallas_call x1, Pallas kernels, shards(): pl.pallas_call(project_kernel, in_specs=[SMEM] + [VMEM] * 10, out_specs=[...  4.13 us
    ppermute x3, waiting for transfers between devices, shards(): granted = [lax.ppermute(partners, 'view', pairs) for pairs in between]  3.48 us
  transfers between devices with their start and end apart: 31, of which 17 were waited for; matrix products, arithmetic and copies ran while one was open for 0% of the time, Pallas kernels for 18%

profile of v22, /device:TPU:0, one launch (start us, length us, event | category | flops | bytes accessed | tf_op | source)
XLA Modules:
  0.0 83.9 jit_solution(9112157339609180023)
XLA Ops:
  0.6 0.8 copy.13.partners
  1.4 3.0 %collective-permute-start.2 = (s32[1,4,3]{2,1,0:T(4,128)S(1)}, s32[1,4,3]{2,1,0:T(4,128)S(1)}, u32[]{:S(2)}, u32[]{:S(2)}) collective-permute-start(s32[1,4,3]{2,1,0:T(4,128)S(1)} %copy.13.partners), channel_id=1, source_target_pairs={{0,2},{2,0},{4,6},{6,4},{1,3},{3,1},{5,7},{7,5},{8,10},{10,8},{12,... | collective-permute-start | bytes 152 | tf_op jit(solution)/shard_map/ppermute | solution.py:431
  4.4 2.6 %collective-permute-start.1 = (s32[1,4,3]{2,1,0:T(4,128)S(1)}, s32[1,4,3]{2,1,0:T(4,128)S(1)}, u32[]{:S(2)}, u32[]{:S(2)}) collective-permute-start(s32[1,4,3]{2,1,0:T(4,128)S(1)} %copy.13.partners), channel_id=1, source_target_pairs={{0,4},{2,6},{4,0},{6,2},{1,5},{3,7},{5,1},{7,3},{8,12},{10,14},{12... | collective-permute-start | bytes 152 | tf_op jit(solution)/shard_map/ppermute | solution.py:431
  7.0 0.5 collective-permute-start.7
  7.5 1.2 %alive.1 = s32[16]{0:T(128)S(1)} custom-call(s32[1,4,3]{2,1,0:T(4,128)S(1)} %copy.13.partners), custom_call_target="tpu_custom_call" | custom-call | flops 40000000000 | bytes 1 | tf_op jit(solution)/shard_map/alive/pallas_call | solution.py:421
  8.8 0.1 stack.23.scalars
  8.9 0.0 copy-start.6
  8.9 3.5 %collective-permute-done.refs_0_ = s32[1,4,3]{2,1,0:T(4,128)S(1)} collective-permute-done((s32[1,4,3]{2,1,0:T(4,128)S(1)}, s32[1,4,3]{2,1,0:T(4,128)S(1)}, u32[]{:S(2)}, u32[]{:S(2)}) %collective-permute-start) | collective-permute-done | bytes 80 | tf_op jit(solution)/shard_map/ppermute | solution.py:431
  12.4 0.8 pick.1
  13.2 0.4 collective-permute-start.3
  13.6 4.0 %collective-permute-start.5 = (bf16[32,1536]{1,0:T(8,128)(2,1)S(1)}, bf16[32,1536]{1,0:T(8,128)(2,1)S(1)}, u32[]{:S(2)}, u32[]{:S(2)}) collective-permute-start(bf16[32,1536]{1,0:T(8,128)(2,1)S(1)} %get-tuple-element.80), channel_id=1, source_target_pairs={{0,2},{2,0},{4,6},{6,4},{1,3},{3,1},{5,7},{7,5},{8,10},{10,8},{12,... | collective-permute-start | bytes 294920 | tf_op jit(solution)/shard_map/ppermute | solution.py:448
  17.7 4.1 %project.1 = (bf16[1536,256]{1,0:T(8,128)(2,1)S(1)}, bf16[256,384]{1,0:T(8,128)(2,1)S(1)}, bf16[256,384]{1,0:T(8,128)(2,1)S(1)}, bf16[256,1536]{1,0:T(8,128)(2,1...) custom-call(s32[5]{0:T(128)S(1)} %stack.23.scalars, ...), custom_call_target="tpu_custom_call" | custom-call | flops 1 | bytes 1 | tf_op jit(solution)/shard_map/project/pallas_call | solution.py:450
  21.9 0.4 collective-permute-done.4.refs_1_
  22.3 0.1 collective-permute-start.8
  22.4 0.4 collective-permute-start.9
  22.8 0.1 collective-permute-start.10
  22.9 0.7 collective-permute-done.8.refs_3_
  23.6 0.2 collective-permute-done.9.refs_4_
  23.7 0.4 collective-permute-done.10.refs_5_
  24.1 3.2 %attention_forward.1 = (bf16[1536,192]{1,0:T(8,128)(2,1)S(1)}, bf16[192,384]{1,0:T(8,128)(2,1)S(1)}, bf16[192,384]{1,0:T(8,128)(2,1)S(1)}, f32[3,64,512]{2,1,0:T...) custom-call(s32[5]{0:T(128)S(1)} %stack.23.scalars, ...), custom_call_target="tpu_custom_call" | custom-call | flops 1 | bytes 1 | tf_op jit(solution)/shard_map/attention_forward/pallas_call | solution.py:486
  27.3 0.2 collective-permute-start.11
  27.5 1.6 %attention_backward.1 = (bf16[256,384]{1,0:T(8,128)(2,1)S(1)}, bf16[448,384]{1,0:T(8,128)(2,1)S(1)}) custom-call(bf16[3,512,128]{2,1,0:T(8,128)(2,1)S(1)} %get-tuple-element.87.refs_6_.query_stack, bf16[3,512,128]{2,1,0:T(8,128)(2,1)S(1)} %get-tuple-element.88.refs_7_.grad_stack, f32[3,64,512]{2,1,0:T(8,128)S(1)} %get-tuple-element.92.dprob_own, ...), custom_call_target="tpu_custom_call" | custom-call | flops 1 | bytes 1 | tf_op jit(solution)/shard_map/attention_backward/pallas_call | solution.py:474
  29.1 1.3 %grad_value_out_sent.1 = (bf16[2,2,48,1536]{3,2,1,0:T(8,128)(2,1)S(1)}, bf16[2,2,48,1536]{3,2,1,0:T(8,128)(2,1)S(1)}) custom-call(s32[5]{0:T(128)S(1)} %stack.23.scalars, bf16[1536,256]{1,0:T(8,128)(2,1)S(1)} %get-tuple-element.82.normed_t, bf16[1536,192]{1,0:T(8,128)(2,1)S(1)} %get-tuple-element.91.normed_far_t, ...), custom_call_target="tpu_custom_call" | custom-call | flops 1 | bytes 1 | tf_op jit(solution)/shard_map/grad_value_out_sent/pallas_call | solution.py:474
  30.4 0.4 collective-permute-start.18
  30.7 1.9 %grad_query_key.1 = (bf16[384,384]{1,0:T(8,128)(2,1)S(1)}, bf16[384,384]{1,0:T(8,128)(2,1)S(1)}, bf16[384,384]{1,0:T(8,128)(2,1)S(1)}, bf16[384,384]{1,0:T(8,128...) custom-call(s32[5]{0:T(128)S(1)} %stack.23.scalars, ...), custom_call_target="tpu_custom_call" | custom-call | flops 1 | bytes 1 | tf_op jit(solution)/shard_map/grad_query_key/pallas_call | solution.py:474
  32.7 1.5 %collective-permute-start.13 = (bf16[384,384]{1,0:T(8,128)(2,1)S(1)}, bf16[384,384]{1,0:T(8,128)(2,1)S(1)}, u32[]{:S(2)}, u32[]{:S(2)}) collective-permute-start(bf16[384,384]{1,0:T(8,128)(2,1)S(1)} %get-tuple-element.109), channel_id=1, source_target_pairs={{0,8},{8,0},{16,24},{24,16},{1,9},{9,1},{17,25},{25,17},{2,10},{10... | collective-permute-start | bytes 884744 | tf_op jit(solution)/shard_map/ppermute | solution.py:524
  34.2 1.5 %collective-permute-start.14 = (bf16[384,384]{1,0:T(8,128)(2,1)S(1)}, bf16[384,384]{1,0:T(8,128)(2,1)S(1)}, u32[]{:S(2)}, u32[]{:S(2)}) collective-permute-start(bf16[384,384]{1,0:T(8,128)(2,1)S(1)} %get-tuple-element.111), channel_id=1, source_target_pairs={{0,16},{8,24},{16,0},{24,8},{1,17},{9,25},{17,1},{25,9},{2,18},{10... | collective-permute-start | bytes 884744 | tf_op jit(solution)/shard_map/ppermute | solution.py:524
  35.7 1.3 %grad_value_out_kept.1.keep = f32[2,2,2,48,1536]{4,3,2,1,0:T(8,128)S(1)} custom-call(s32[5]{0:T(128)S(1)} %stack.23.scalars, bf16[1536,256]{1,0:T(8,128)(2,1)S(1)} %get-tuple-element.82.normed_t, bf16[1536,192]{1,0:T(8,128)(2,1)S(1)} %get-tuple-element.91.normed_far_t, bf16[448,384]{1,0:T(8,128)(2,1)S(1)} %get-tuple-element.101.dvalue, ...), custom_call_target="tpu_custom_call" | custom-call | flops 1 | bytes 1 | tf_op jit(solution)/shard_map/grad_value_out_kept/pallas_call | solution.py:474
  37.0 0.6 collective-permute-start.12
  37.6 0.5 collective-permute-start.16
  38.1 4.5 %collective-permute-done.13.q_got = bf16[384,384]{1,0:T(8,128)(2,1)S(1)} collective-permute-done((bf16[384,384]{1,0:T(8,128)(2,1)S(1)}, bf16[384,384]{1,0:T(8,128)(2,1)S(1)}, u32[]{:S(2)}, u32[]{:S(2)}) %collective-permute-start.13) | collective-permute-done | bytes 294944 | tf_op jit(solution)/shard_map/ppermute | solution.py:524
  42.6 1.5 %collective-permute-done.14.k_got = bf16[384,384]{1,0:T(8,128)(2,1)S(1)} collective-permute-done((bf16[384,384]{1,0:T(8,128)(2,1)S(1)}, bf16[384,384]{1,0:T(8,128)(2,1)S(1)}, u32[]{:S(2)}, u32[]{:S(2)}) %collective-permute-start.14) | collective-permute-done | bytes 294944 | tf_op jit(solution)/shard_map/ppermute | solution.py:524
  44.1 0.1 first_sum_query_key.1
  44.2 1.8 %collective-permute-done.18.got = bf16[2,2,48,1536]{3,2,1,0:T(8,128)(2,1)S(1)} collective-permute-done((bf16[2,2,48,1536]{3,2,1,0:T(8,128)(2,1)S(1)}, bf16[2,2,48,1536]{3,2,1,0:T(8,128)(2,1)S(1)}, u32[]{:S(2)}, u32[]{:S(2)}) %collective-permute-start.18) | collective-permute-done | bytes 589856 | tf_op jit(solution)/shard_map/ppermute | solution.py:569
  46.0 0.3 collective-permute-start.19
  46.3 1.5 %collective-permute-start.17 = (bf16[384,384]{1,0:T(8,128)(2,1)S(1)}, bf16[384,384]{1,0:T(8,128)(2,1)S(1)}, u32[]{:S(2)}, u32[]{:S(2)}) collective-permute-start(bf16[384,384]{1,0:T(8,128)(2,1)S(1)} %get-tuple-element.114), channel_id=1, source_target_pairs={{0,8},{8,0},{16,24},{24,16},{1,9},{9,1},{17,25},{25,17},{2,10},{10... | collective-permute-start | bytes 884744 | tf_op jit(solution)/shard_map/ppermute | solution.py:532
  47.8 1.5 %collective-permute-start.15 = (bf16[384,384]{1,0:T(8,128)(2,1)S(1)}, bf16[384,384]{1,0:T(8,128)(2,1)S(1)}, u32[]{:S(2)}, u32[]{:S(2)}) collective-permute-start(bf16[384,384]{1,0:T(8,128)(2,1)S(1)} %get-tuple-element.112), channel_id=1, source_target_pairs={{0,16},{8,24},{16,0},{24,8},{1,17},{9,25},{17,1},{25,9},{2,18},{10... | collective-permute-start | bytes 884744 | tf_op jit(solution)/shard_map/ppermute | solution.py:532
  49.4 0.1 view_sum_sent.1
  49.5 0.6 collective-permute-start.20
  50.1 1.4 %collective-permute-start.21 = (bf16[2,2,48,768]{3,2,1,0:T(8,128)(2,1)S(1)}, bf16[2,2,48,768]{3,2,1,0:T(8,128)(2,1)S(1)}, u32[]{:S(2)}, u32[]{:S(2)}) collective-permute-start(bf16[2,2,48,768]{3,2,1,0:T(8,128)(2,1)S(1)} %get-tuple-element.124), channel_id=1, source_target_pairs={{0,16},{8,24},{16,0},{24,8},{1,17},{9,25},{17,1},{25,9},{2,18},{10... | collective-permute-start | bytes 884744 | tf_op jit(solution)/shard_map/ppermute | solution.py:524
  51.5 4.8 %collective-permute-done.17.k_second = bf16[384,384]{1,0:T(8,128)(2,1)S(1)} collective-permute-done((bf16[384,384]{1,0:T(8,128)(2,1)S(1)}, bf16[384,384]{1,0:T(8,128)(2,1)S(1)}, u32[]{:S(2)}, u32[]{:S(2)}) %collective-permute-start.17) | collective-permute-done | bytes 294944 | tf_op jit(solution)/shard_map/ppermute | solution.py:532
  56.3 1.5 %collective-permute-done.15.q_second = bf16[384,384]{1,0:T(8,128)(2,1)S(1)} collective-permute-done((bf16[384,384]{1,0:T(8,128)(2,1)S(1)}, bf16[384,384]{1,0:T(8,128)(2,1)S(1)}, u32[]{:S(2)}, u32[]{:S(2)}) %collective-permute-start.15) | collective-permute-done | bytes 294944 | tf_op jit(solution)/shard_map/ppermute | solution.py:532
  57.8 0.8 second_sum_query_key.1
  58.6 1.8 %collective-permute-start.22 = (bf16[2,96,768]{2,1,0:T(8,128)(2,1)S(1)}, bf16[2,96,768]{2,1,0:T(8,128)(2,1)S(1)}, u32[]{:S(2)}, u32[]{:S(2)}) collective-permute-start(bf16[2,96,768]{2,1,0:T(8,128)(2,1)S(1)} %get-tuple-element.118), channel_id=1, source_target_pairs={{0,2},{2,0},{4,6},{6,4},{1,3},{3,1},{5,7},{7,5},{8,10},{10,8},{12,... | collective-permute-start | bytes 884744 | tf_op jit(solution)/shard_map/ppermute | solution.py:605
  60.4 1.9 %collective-permute-done.19.got = bf16[2,2,48,1536]{3,2,1,0:T(8,128)(2,1)S(1)} collective-permute-done((bf16[2,2,48,1536]{3,2,1,0:T(8,128)(2,1)S(1)}, bf16[2,2,48,1536]{3,2,1,0:T(8,128)(2,1)S(1)}, u32[]{:S(2)}, u32[]{:S(2)}) %collective-permute-start.19) | collective-permute-done | bytes 589856 | tf_op jit(solution)/shard_map/ppermute | solution.py:588
  62.3 0.1 view_sum_kept.1
  62.4 0.1 first_sum_value_out.1
  62.6 1.6 %collective-permute-start.26 = (bf16[2,48,768]{2,1,0:T(8,128)(2,1)S(1)}, bf16[2,48,768]{2,1,0:T(8,128)(2,1)S(1)}, u32[]{:S(2)}, u32[]{:S(2)}) collective-permute-start(bf16[2,48,768]{2,1,0:T(8,128)(2,1)S(1)} %get-tuple-element.137), channel_id=1, source_target_pairs={{0,8},{8,0},{16,24},{24,16},{1,9},{9,1},{17,25},{25,17},{2,10},{10... | collective-permute-start | bytes 442376 | tf_op jit(solution)/shard_map/ppermute | solution.py:532
  64.1 1.5 %collective-permute-start.27 = (bf16[2,48,768]{2,1,0:T(8,128)(2,1)S(1)}, bf16[2,48,768]{2,1,0:T(8,128)(2,1)S(1)}, u32[]{:S(2)}, u32[]{:S(2)}) collective-permute-start(bf16[2,48,768]{2,1,0:T(8,128)(2,1)S(1)} %get-tuple-element.125), channel_id=1, source_target_pairs={{0,16},{8,24},{16,0},{24,8},{1,17},{9,25},{17,1},{25,9},{2,18},{10... | collective-permute-start | bytes 442376 | tf_op jit(solution)/shard_map/ppermute | solution.py:532
  65.7 1.5 %collective-permute-done.22.refs_1_ = bf16[2,96,768]{2,1,0:T(8,128)(2,1)S(1)} collective-permute-done((bf16[2,96,768]{2,1,0:T(8,128)(2,1)S(1)}, bf16[2,96,768]{2,1,0:T(8,128)(2,1)S(1)}, u32[]{:S(2)}, u32[]{:S(2)}) %collective-permute-start.22) | collective-permute-done | bytes 294944 | tf_op jit(solution)/shard_map/ppermute | solution.py:605
  67.1 0.6 last_parts_query_key.1
  67.8 0.1 collective-permute-start.24
  67.9 1.2 %collective-permute-start.23 = (bf16[48,768]{1,0:T(8,128)(2,1)S(1)}, bf16[48,768]{1,0:T(8,128)(2,1)S(1)}, u32[]{:S(2)}, u32[]{:S(2)}) collective-permute-start(bf16[48,768]{1,0:T(8,128)(2,1)S(1)} %get-tuple-element.128), channel_id=1, source_target_pairs={{0,4},{2,6},{4,0},{6,2},{1,5},{3,7},{5,1},{7,3},{8,12},{10,14},{12... | collective-permute-start | bytes 221192 | tf_op jit(solution)/shard_map/ppermute | solution.py:558
  69.1 0.2 collective-permute-done.27.refs_3_
  69.3 0.6 last_parts_value_out.1
  69.9 0.1 collective-permute-start.29
  70.0 1.7 %collective-permute-start.25 = (bf16[48,768]{1,0:T(8,128)(2,1)S(1)}, bf16[48,768]{1,0:T(8,128)(2,1)S(1)}, u32[]{:S(2)}, u32[]{:S(2)}) collective-permute-start(bf16[48,768]{1,0:T(8,128)(2,1)S(1)} %get-tuple-element.130), channel_id=1, source_target_pairs={{0,5},{1,4},{2,7},{3,6},{4,1},{5,0},{6,3},{7,2},{8,13},{9,12},{10,... | collective-permute-start | bytes 221192 | tf_op jit(solution)/shard_map/ppermute | solution.py:559
  71.7 1.4 %collective-permute-start.28 = (bf16[24,1536]{1,0:T(8,128)(2,1)S(1)}, bf16[24,1536]{1,0:T(8,128)(2,1)S(1)}, u32[]{:S(2)}, u32[]{:S(2)}) collective-permute-start(bf16[24,1536]{1,0:T(8,128)(2,1)S(1)} %get-tuple-element.141), channel_id=1, source_target_pairs={{0,4},{2,6},{4,0},{6,2},{1,5},{3,7},{5,1},{7,3},{8,12},{10,14},{12... | collective-permute-start | bytes 221192 | tf_op jit(solution)/shard_map/ppermute | solution.py:558
  73.0 1.8 %collective-permute-done.23.far_same = bf16[48,768]{1,0:T(8,128)(2,1)S(1)} collective-permute-done((bf16[48,768]{1,0:T(8,128)(2,1)S(1)}, bf16[48,768]{1,0:T(8,128)(2,1)S(1)}, u32[]{:S(2)}, u32[]{:S(2)}) %collective-permute-start.23) | collective-permute-done | bytes 73760 | tf_op jit(solution)/shard_map/ppermute | solution.py:558
  74.8 4.6 %collective-permute-done.25.far_cross = bf16[48,768]{1,0:T(8,128)(2,1)S(1)} collective-permute-done((bf16[48,768]{1,0:T(8,128)(2,1)S(1)}, bf16[48,768]{1,0:T(8,128)(2,1)S(1)}, u32[]{:S(2)}, u32[]{:S(2)}) %collective-permute-start.25) | collective-permute-done | bytes 73760 | tf_op jit(solution)/shard_map/ppermute | solution.py:559
  79.5 1.3 %place_query_key.1 = (f32[48,768]{1,0:T(8,128)}, f32[48,768]{1,0:T(8,128)}) custom-call(s32[5]{0:T(128)S(1)} %stack.23.scalars, f32[48,768]{1,0:T(8,128)S(1)} %get-tuple-element.131.same, f32[48,768]{1,0:T(8,128)S(1)} %get-tuple-element.132.cross), custom_call_target="tpu_custom_call" | custom-call | flops 1 | bytes 1 | tf_op jit(solution)/shard_map/place_query_key/pallas_call | solution.py:474
  80.8 0.4 collective-permute-done.28.far_same
  81.1 1.5 %collective-permute-done.30.far_cross = bf16[24,1536]{1,0:T(8,128)(2,1)S(1)} collective-permute-done((bf16[24,1536]{1,0:T(8,128)(2,1)S(1)}, bf16[24,1536]{1,0:T(8,128)(2,1)S(1)}, u32[]{:S(2)}, u32[]{:S(2)}) %collective-permute-start.30) | collective-permute-done | bytes 73760 | tf_op jit(solution)/shard_map/ppermute | solution.py:559
  82.6 1.3 %last_sum_value_out.1 = (f32[48,768]{1,0:T(8,128)}, f32[24,1536]{1,0:T(8,128)}) custom-call(s32[5]{0:T(128)S(1)} %stack.23.scalars, f32[24,1536]{1,0:T(8,128)S(1)} %get-tuple-element.140.mine, bf16[24,1536]{1,0:T(8,128)(2,1)S(1)} %collective-permute-done.28.far_same, f32[24,1536]{1,0:T(8,128)S(1)} %collective-permute-done.29.near_cross, ...), custom_call_target="tpu_custom_call" | custom-call | flops 1 | bytes 1 | tf_op jit(solution)/shard_map/last_sum_value_out/pallas_call | solution.py:474
  (34 shorter events, 0.1 us)
Async XLA Ops:
  1.4 7.5 %collective-permute-start.2 = (s32[1,4,3]{2,1,0:T(4,128)S(1)}, s32[1,4,3]{2,1,0:T(4,128)S(1)}, u32[]{:S(2)}, u32[]{:S(2)}) collective-permute-start(s32[1,4,3]{2,1,0:T(4,128)S(1)} %copy.13.partners), channel_id=1, source_target_pairs={{0,2},{2,0},{4,6},{6,4},{1,3},{3,1},{5,7},{7,5},{8,10},{10,8},{12,... | collective-permute-start | bytes 152 | tf_op jit(solution)/shard_map/ppermute | solution.py:431
  4.4 4.5 %collective-permute-start.1 = (s32[1,4,3]{2,1,0:T(4,128)S(1)}, s32[1,4,3]{2,1,0:T(4,128)S(1)}, u32[]{:S(2)}, u32[]{:S(2)}) collective-permute-start(s32[1,4,3]{2,1,0:T(4,128)S(1)} %copy.13.partners), channel_id=1, source_target_pairs={{0,4},{2,6},{4,0},{6,2},{1,5},{3,7},{5,1},{7,3},{8,12},{10,14},{12... | collective-permute-start | bytes 152 | tf_op jit(solution)/shard_map/ppermute | solution.py:431
  7.0 5.4 %collective-permute-start = (s32[1,4,3]{2,1,0:T(4,128)S(1)}, s32[1,4,3]{2,1,0:T(4,128)S(1)}, u32[]{:S(2)}, u32[]{:S(2)}) collective-permute-start(s32[1,4,3]{2,1,0:T(4,128)S(1)} %copy.13.partners), channel_id=1, source_target_pairs={{0,6},{2,4},{4,2},{6,0},{1,7},{3,5},{5,3},{7,1},{8,14},{10,12},{12... | collective-permute-start | bytes 152 | tf_op jit(solution)/shard_map/ppermute | solution.py:431
  7.0 10.6 %collective-permute-start.6 = (bf16[4,32,1536]{2,1,0:T(8,128)(2,1)}, bf16[4,32,1536]{2,1,0:T(8,128)(2,1)S(1)}, u32[]{:S(2)}, u32[]{:S(2)}) collective-permute-start(bf16[4,32,1536]{2,1,0:T(8,128)(2,1)} %bitcast.7), channel_id=1, source_target_pairs={{0,1},{1,0},{2,3},{3,2},{4,5},{5,4},{6,7},{7,6},{8,9},{9,8},{10,11... | collective-permute-start | bytes 1179656 | tf_op jit(solution)/shard_map/ppermute | solution.py:436
  7.0 10.6 %collective-permute-start.7 = (bf16[4,32,1536]{2,1,0:T(8,128)(2,1)}, bf16[4,32,1536]{2,1,0:T(8,128)(2,1)S(1)}, u32[]{:S(2)}, u32[]{:S(2)}) collective-permute-start(bf16[4,32,1536]{2,1,0:T(8,128)(2,1)} %bitcast.10), channel_id=1, source_target_pairs={{0,1},{1,0},{2,3},{3,2},{4,5},{5,4},{6,7},{7,6},{8,9},{9,8},{10,11... | collective-permute-start | bytes 1179656 | tf_op jit(solution)/shard_map/ppermute | solution.py:437
  7.5 4.9 %copy-start.4 = (bf16[1,4,1,32,1536]{4,3,2,1,0:T(8,128)(2,1)S(1)}, bf16[1,4,1,32,1536]{4,3,2,1,0:T(8,128)(2,1)}, u32[]{:S(2)}) copy-start(bf16[1,4,1,32,1536]{4,3,2,1,0:T(8,128)(2,1)} %param.10) | copy-start | bytes 1179652
  8.8 8.8 %copy-start = (bf16[1536,768]{1,0:T(8,128)(2,1)S(1)}, bf16[1536,768]{1,0:T(8,128)(2,1)}, u32[]{:S(2)}) copy-start(bf16[1536,768]{1,0:T(8,128)(2,1)} %refs_11_.1) | copy-start | bytes 7077892
  8.9 8.8 %copy-start.1 = (bf16[1536,768]{1,0:T(8,128)(2,1)S(1)}, bf16[1536,768]{1,0:T(8,128)(2,1)}, u32[]{:S(2)}) copy-start(bf16[1536,768]{1,0:T(8,128)(2,1)} %refs_12_.1) | copy-start | bytes 7077892
  8.9 8.8 %copy-start.2 = (bf16[1536,768]{1,0:T(8,128)(2,1)S(1)}, bf16[1536,768]{1,0:T(8,128)(2,1)}, u32[]{:S(2)}) copy-start(bf16[1536,768]{1,0:T(8,128)(2,1)} %w_query.1) | copy-start | bytes 7077892
  8.9 8.8 %copy-start.3 = (bf16[768,1536]{1,0:T(8,128)(2,1)S(1)}, bf16[768,1536]{1,0:T(8,128)(2,1)}, u32[]{:S(2)}) copy-start(bf16[768,1536]{1,0:T(8,128)(2,1)} %w_out.1) | copy-start | bytes 7077892
  8.9 8.8 %copy-start.5 = (bf16[1,4,1,32,1536]{4,3,2,1,0:T(8,128)(2,1)S(1)}, bf16[1,4,1,32,1536]{4,3,2,1,0:T(8,128)(2,1)}, u32[]{:S(2)}) copy-start(bf16[1,4,1,32,1536]{4,3,2,1,0:T(8,128)(2,1)} %param.18) | copy-start | bytes 1179652
  8.9 8.8 %copy-start.6 = (bf16[9,1536]{1,0:T(8,128)(2,1)S(1)}, bf16[9,1536]{1,0:T(8,128)(2,1)}, u32[]{:S(2)}) copy-start(bf16[9,1536]{1,0:T(8,128)(2,1)} %taps.1) | copy-start | bytes 82948
  8.9 8.8 %copy-start.7 = (f32[1536]{0:T(1024)S(1)}, f32[1536]{0:T(1024)}, u32[]{:S(2)}) copy-start(f32[1536]{0:T(1024)} %refs_10_.1) | copy-start | bytes 18436
  13.2 8.7 %collective-permute-start.3 = (bf16[32,1536]{1,0:T(8,128)(2,1)S(1)}, bf16[32,1536]{1,0:T(8,128)(2,1)S(1)}, u32[]{:S(2)}, u32[]{:S(2)}) collective-permute-start(bf16[32,1536]{1,0:T(8,128)(2,1)S(1)} %get-tuple-element.78), channel_id=1, source_target_pairs={{0,6},{2,4},{4,2},{6,0},{1,7},{3,5},{5,3},{7,1},{8,14},{10,12},{12... | collective-permute-start | bytes 294920 | tf_op jit(solution)/shard_map/ppermute | solution.py:448
  13.6 8.7 %collective-permute-start.4 = (bf16[32,1536]{1,0:T(8,128)(2,1)S(1)}, bf16[32,1536]{1,0:T(8,128)(2,1)S(1)}, u32[]{:S(2)}, u32[]{:S(2)}) collective-permute-start(bf16[32,1536]{1,0:T(8,128)(2,1)S(1)} %get-tuple-element.79), channel_id=1, source_target_pairs={{0,4},{2,6},{4,0},{6,2},{1,5},{3,7},{5,1},{7,3},{8,12},{10,14},{12... | collective-permute-start | bytes 294920 | tf_op jit(solution)/shard_map/ppermute | solution.py:448
  13.6 8.7 %collective-permute-start.5 = (bf16[32,1536]{1,0:T(8,128)(2,1)S(1)}, bf16[32,1536]{1,0:T(8,128)(2,1)S(1)}, u32[]{:S(2)}, u32[]{:S(2)}) collective-permute-start(bf16[32,1536]{1,0:T(8,128)(2,1)S(1)} %get-tuple-element.80), channel_id=1, source_target_pairs={{0,2},{2,0},{4,6},{6,4},{1,3},{3,1},{5,7},{7,5},{8,10},{10,8},{12,... | collective-permute-start | bytes 294920 | tf_op jit(solution)/shard_map/ppermute | solution.py:448
  22.3 1.3 %collective-permute-start.8 = (bf16[32,1536]{1,0:T(8,128)(2,1)S(1)}, bf16[32,1536]{1,0:T(8,128)(2,1)S(1)}, u32[]{:S(2)}, u32[]{:S(2)}) collective-permute-start(bf16[32,1536]{1,0:T(8,128)(2,1)S(1)} %collective-permute-done.3.refs_0_), channel_id=1, source_target_pairs={{0,1},{1,0},{2,3},{3,2},{4,5},{5,4},{6,7},{7,6},{8,9},{9,8},{10,11... | collective-permute-start | bytes 294920 | tf_op jit(solution)/shard_map/ppermute | solution.py:471
  22.4 1.4 %collective-permute-start.9 = (bf16[32,1536]{1,0:T(8,128)(2,1)S(1)}, bf16[32,1536]{1,0:T(8,128)(2,1)S(1)}, u32[]{:S(2)}, u32[]{:S(2)}) collective-permute-start(bf16[32,1536]{1,0:T(8,128)(2,1)S(1)} %collective-permute-done.4.refs_1_), channel_id=1, source_target_pairs={{0,1},{1,0},{2,3},{3,2},{4,5},{5,4},{6,7},{7,6},{8,9},{9,8},{10,11... | collective-permute-start | bytes 294920 | tf_op jit(solution)/shard_map/ppermute | solution.py:471
  22.8 1.3 %collective-permute-start.10 = (bf16[32,1536]{1,0:T(8,128)(2,1)S(1)}, bf16[32,1536]{1,0:T(8,128)(2,1)S(1)}, u32[]{:S(2)}, u32[]{:S(2)}) collective-permute-start(bf16[32,1536]{1,0:T(8,128)(2,1)S(1)} %collective-permute-done.5.refs_2_), channel_id=1, source_target_pairs={{0,1},{1,0},{2,3},{3,2},{4,5},{5,4},{6,7},{7,6},{8,9},{9,8},{10,11... | collective-permute-start | bytes 294920 | tf_op jit(solution)/shard_map/ppermute | solution.py:471
  27.3 1.8 %collective-permute-start.11 = (bf16[384,256]{1,0:T(8,128)(2,1)S(1)}, bf16[384,256]{1,0:T(8,128)(2,1)S(1)}, u32[]{:S(2)}, u32[]{:S(2)}) collective-permute-start(bf16[384,256]{1,0:T(8,128)(2,1)S(1)} %get-tuple-element.102.mine), channel_id=1, source_target_pairs={{0,1},{1,0},{2,3},{3,2},{4,5},{5,4},{6,7},{7,6},{8,9},{9,8},{10,11... | collective-permute-start | bytes 589832 | tf_op jit(solution)/shard_map/ppermute | solution.py:506
  30.4 15.7 %collective-permute-start.18 = (bf16[2,2,48,1536]{3,2,1,0:T(8,128)(2,1)S(1)}, bf16[2,2,48,1536]{3,2,1,0:T(8,128)(2,1)S(1)}, u32[]{:S(2)}, u32[]{:S(2)}) collective-permute-start(bf16[2,2,48,1536]{3,2,1,0:T(8,128)(2,1)S(1)} %get-tuple-element.104), channel_id=1, source_target_pairs={{0,2},{2,0},{4,6},{6,4},{1,3},{3,1},{5,7},{7,5},{8,10},{10,8},{12,... | collective-permute-start | bytes 1769480 | tf_op jit(solution)/shard_map/ppermute | solution.py:569
  32.7 9.9 %collective-permute-start.13 = (bf16[384,384]{1,0:T(8,128)(2,1)S(1)}, bf16[384,384]{1,0:T(8,128)(2,1)S(1)}, u32[]{:S(2)}, u32[]{:S(2)}) collective-permute-start(bf16[384,384]{1,0:T(8,128)(2,1)S(1)} %get-tuple-element.109), channel_id=1, source_target_pairs={{0,8},{8,0},{16,24},{24,16},{1,9},{9,1},{17,25},{25,17},{2,10},{10... | collective-permute-start | bytes 884744 | tf_op jit(solution)/shard_map/ppermute | solution.py:524
  34.2 9.9 %collective-permute-start.14 = (bf16[384,384]{1,0:T(8,128)(2,1)S(1)}, bf16[384,384]{1,0:T(8,128)(2,1)S(1)}, u32[]{:S(2)}, u32[]{:S(2)}) collective-permute-start(bf16[384,384]{1,0:T(8,128)(2,1)S(1)} %get-tuple-element.111), channel_id=1, source_target_pairs={{0,16},{8,24},{16,0},{24,8},{1,17},{9,25},{17,1},{25,9},{2,18},{10... | collective-permute-start | bytes 884744 | tf_op jit(solution)/shard_map/ppermute | solution.py:524
  37.0 12.3 %collective-permute-start.12 = (bf16[384,384]{1,0:T(8,128)(2,1)S(1)}, bf16[384,384]{1,0:T(8,128)(2,1)S(1)}, u32[]{:S(2)}, u32[]{:S(2)}) collective-permute-start(bf16[384,384]{1,0:T(8,128)(2,1)S(1)} %get-tuple-element.107), channel_id=1, source_target_pairs={{0,8},{8,0},{16,24},{24,16},{1,9},{9,1},{17,25},{25,17},{2,10},{10... | collective-permute-start | bytes 884744 | tf_op jit(solution)/shard_map/ppermute | solution.py:524
  37.6 11.7 %collective-permute-start.16 = (bf16[384,384]{1,0:T(8,128)(2,1)S(1)}, bf16[384,384]{1,0:T(8,128)(2,1)S(1)}, u32[]{:S(2)}, u32[]{:S(2)}) collective-permute-start(bf16[384,384]{1,0:T(8,128)(2,1)S(1)} %get-tuple-element.113), channel_id=1, source_target_pairs={{0,16},{8,24},{16,0},{24,8},{1,17},{9,25},{17,1},{25,9},{2,18},{10... | collective-permute-start | bytes 884744 | tf_op jit(solution)/shard_map/ppermute | solution.py:524
  46.0 16.3 %collective-permute-start.19 = (bf16[2,2,48,1536]{3,2,1,0:T(8,128)(2,1)S(1)}, bf16[2,2,48,1536]{3,2,1,0:T(8,128)(2,1)S(1)}, u32[]{:S(2)}, u32[]{:S(2)}) collective-permute-start(bf16[2,2,48,1536]{3,2,1,0:T(8,128)(2,1)S(1)} %get-tuple-element.117), channel_id=1, source_target_pairs={{0,2},{2,0},{4,6},{6,4},{1,3},{3,1},{5,7},{7,5},{8,10},{10,8},{12,... | collective-permute-start | bytes 1769480 | tf_op jit(solution)/shard_map/ppermute | solution.py:588
  46.3 9.9 %collective-permute-start.17 = (bf16[384,384]{1,0:T(8,128)(2,1)S(1)}, bf16[384,384]{1,0:T(8,128)(2,1)S(1)}, u32[]{:S(2)}, u32[]{:S(2)}) collective-permute-start(bf16[384,384]{1,0:T(8,128)(2,1)S(1)} %get-tuple-element.114), channel_id=1, source_target_pairs={{0,8},{8,0},{16,24},{24,16},{1,9},{9,1},{17,25},{25,17},{2,10},{10... | collective-permute-start | bytes 884744 | tf_op jit(solution)/shard_map/ppermute | solution.py:532
  47.8 9.9 %collective-permute-start.15 = (bf16[384,384]{1,0:T(8,128)(2,1)S(1)}, bf16[384,384]{1,0:T(8,128)(2,1)S(1)}, u32[]{:S(2)}, u32[]{:S(2)}) collective-permute-start(bf16[384,384]{1,0:T(8,128)(2,1)S(1)} %get-tuple-element.112), channel_id=1, source_target_pairs={{0,16},{8,24},{16,0},{24,8},{1,17},{9,25},{17,1},{25,9},{2,18},{10... | collective-permute-start | bytes 884744 | tf_op jit(solution)/shard_map/ppermute | solution.py:532
  49.5 12.9 %collective-permute-start.20 = (bf16[2,2,48,768]{3,2,1,0:T(8,128)(2,1)S(1)}, bf16[2,2,48,768]{3,2,1,0:T(8,128)(2,1)S(1)}, u32[]{:S(2)}, u32[]{:S(2)}) collective-permute-start(bf16[2,2,48,768]{3,2,1,0:T(8,128)(2,1)S(1)} %get-tuple-element.122), channel_id=1, source_target_pairs={{0,8},{8,0},{16,24},{24,16},{1,9},{9,1},{17,25},{25,17},{2,10},{10... | collective-permute-start | bytes 884744 | tf_op jit(solution)/shard_map/ppermute | solution.py:524
  50.1 12.3 %collective-permute-start.21 = (bf16[2,2,48,768]{3,2,1,0:T(8,128)(2,1)S(1)}, bf16[2,2,48,768]{3,2,1,0:T(8,128)(2,1)S(1)}, u32[]{:S(2)}, u32[]{:S(2)}) collective-permute-start(bf16[2,2,48,768]{3,2,1,0:T(8,128)(2,1)S(1)} %get-tuple-element.124), channel_id=1, source_target_pairs={{0,16},{8,24},{16,0},{24,8},{1,17},{9,25},{17,1},{25,9},{2,18},{10... | collective-permute-start | bytes 884744 | tf_op jit(solution)/shard_map/ppermute | solution.py:524
  58.6 8.6 %collective-permute-start.22 = (bf16[2,96,768]{2,1,0:T(8,128)(2,1)S(1)}, bf16[2,96,768]{2,1,0:T(8,128)(2,1)S(1)}, u32[]{:S(2)}, u32[]{:S(2)}) collective-permute-start(bf16[2,96,768]{2,1,0:T(8,128)(2,1)S(1)} %get-tuple-element.118), channel_id=1, source_target_pairs={{0,2},{2,0},{4,6},{6,4},{1,3},{3,1},{5,7},{7,5},{8,10},{10,8},{12,... | collective-permute-start | bytes 884744 | tf_op jit(solution)/shard_map/ppermute | solution.py:605
  62.6 6.5 %collective-permute-start.26 = (bf16[2,48,768]{2,1,0:T(8,128)(2,1)S(1)}, bf16[2,48,768]{2,1,0:T(8,128)(2,1)S(1)}, u32[]{:S(2)}, u32[]{:S(2)}) collective-permute-start(bf16[2,48,768]{2,1,0:T(8,128)(2,1)S(1)} %get-tuple-element.137), channel_id=1, source_target_pairs={{0,8},{8,0},{16,24},{24,16},{1,9},{9,1},{17,25},{25,17},{2,10},{10... | collective-permute-start | bytes 442376 | tf_op jit(solution)/shard_map/ppermute | solution.py:532
  64.1 5.1 %collective-permute-start.27 = (bf16[2,48,768]{2,1,0:T(8,128)(2,1)S(1)}, bf16[2,48,768]{2,1,0:T(8,128)(2,1)S(1)}, u32[]{:S(2)}, u32[]{:S(2)}) collective-permute-start(bf16[2,48,768]{2,1,0:T(8,128)(2,1)S(1)} %get-tuple-element.125), channel_id=1, source_target_pairs={{0,16},{8,24},{16,0},{24,8},{1,17},{9,25},{17,1},{25,9},{2,18},{10... | collective-permute-start | bytes 442376 | tf_op jit(solution)/shard_map/ppermute | solution.py:532
  67.8 11.7 %collective-permute-start.24 = (f32[48,768]{1,0:T(8,128)S(1)}, f32[48,768]{1,0:T(8,128)S(1)}, u32[]{:S(2)}, u32[]{:S(2)}) collective-permute-start(f32[48,768]{1,0:T(8,128)S(1)} %get-tuple-element.129), channel_id=1, source_target_pairs={{0,1},{1,0},{2,3},{3,2},{4,5},{5,4},{6,7},{7,6},{8,9},{9,8},{10,11... | collective-permute-start | bytes 442376 | tf_op jit(solution)/shard_map/ppermute | solution.py:560
  67.9 7.0 %collective-permute-start.23 = (bf16[48,768]{1,0:T(8,128)(2,1)S(1)}, bf16[48,768]{1,0:T(8,128)(2,1)S(1)}, u32[]{:S(2)}, u32[]{:S(2)}) collective-permute-start(bf16[48,768]{1,0:T(8,128)(2,1)S(1)} %get-tuple-element.128), channel_id=1, source_target_pairs={{0,4},{2,6},{4,0},{6,2},{1,5},{3,7},{5,1},{7,3},{8,12},{10,14},{12... | collective-permute-start | bytes 221192 | tf_op jit(solution)/shard_map/ppermute | solution.py:558
  69.9 12.7 %collective-permute-start.29 = (f32[24,1536]{1,0:T(8,128)S(1)}, f32[24,1536]{1,0:T(8,128)S(1)}, u32[]{:S(2)}, u32[]{:S(2)}) collective-permute-start(f32[24,1536]{1,0:T(8,128)S(1)} %get-tuple-element.142), channel_id=1, source_target_pairs={{0,1},{1,0},{2,3},{3,2},{4,5},{5,4},{6,7},{7,6},{8,9},{9,8},{10,11... | collective-permute-start | bytes 442376 | tf_op jit(solution)/shard_map/ppermute | solution.py:560
  70.0 9.5 %collective-permute-start.25 = (bf16[48,768]{1,0:T(8,128)(2,1)S(1)}, bf16[48,768]{1,0:T(8,128)(2,1)S(1)}, u32[]{:S(2)}, u32[]{:S(2)}) collective-permute-start(bf16[48,768]{1,0:T(8,128)(2,1)S(1)} %get-tuple-element.130), channel_id=1, source_target_pairs={{0,5},{1,4},{2,7},{3,6},{4,1},{5,0},{6,3},{7,2},{8,13},{9,12},{10,... | collective-permute-start | bytes 221192 | tf_op jit(solution)/shard_map/ppermute | solution.py:559
  71.7 9.5 %collective-permute-start.28 = (bf16[24,1536]{1,0:T(8,128)(2,1)S(1)}, bf16[24,1536]{1,0:T(8,128)(2,1)S(1)}, u32[]{:S(2)}, u32[]{:S(2)}) collective-permute-start(bf16[24,1536]{1,0:T(8,128)(2,1)S(1)} %get-tuple-element.141), channel_id=1, source_target_pairs={{0,4},{2,6},{4,0},{6,2},{1,5},{3,7},{5,1},{7,3},{8,12},{10,14},{12... | collective-permute-start | bytes 221192 | tf_op jit(solution)/shard_map/ppermute | solution.py:558
  74.8 7.8 %collective-permute-start.30 = (bf16[24,1536]{1,0:T(8,128)(2,1)S(1)}, bf16[24,1536]{1,0:T(8,128)(2,1)S(1)}, u32[]{:S(2)}, u32[]{:S(2)}) collective-permute-start(bf16[24,1536]{1,0:T(8,128)(2,1)S(1)} %get-tuple-element.143), channel_id=1, source_target_pairs={{0,5},{1,4},{2,7},{3,6},{4,1},{5,0},{6,3},{7,2},{8,13},{9,12},{10,... | collective-permute-start | bytes 221192 | tf_op jit(solution)/shard_map/ppermute | solution.py:559

commit v23 on v22

--- a/solution.py
+++ b/solution.py
@@ -611,7 +611,7 @@
     qk_total = call(
         add_kernel, [shape((q_rows, 2 * part), f32)] * 2, qk_last, "last_sum_query_key"
     )
-    vo_last = last_parts((after(addends[0], qk_last[0]), *addends[1:]), value_out_cores, "value_out")
+    vo_last = last_parts(addends, value_out_cores, "value_out")
     grad_query, grad_key = call(
         place_query_key_kernel,
         [shape((q_rows, inner), f32)] * 2,

time: 84.1 us -> 84.1 us (level)
  no operation moved by 1% of the time
where the time goes in v23:
time: 84.1 us; the launch traced here: 83.9 us
  waiting for transfers between devices  31.1 us (37%)
  starting transfers between devices  30.5 us (36%)
  Pallas kernels  20.5 us (24%)
  between operations  0.91 us (1%)
  local copies, waits for them, and re-layouts  0.89 us (1%)
    pallas_call x14, Pallas kernels, call(): pl.pallas_call(kernel_body, in_specs=[first] + [VMEM] * (len(operands) -...  11.2 us
    ppermute x2, waiting for transfers between devices, last_parts(): lax.ppermute(far_cross, ('view', 'row'), [(i, i ^ 5) for i in range(targe...  6.12 us
    ppermute x3, starting transfers between devices, shards(): granted = [lax.ppermute(partners, 'view', pairs) for pairs in between]  5.62 us
    ppermute x2, waiting for transfers between devices, second_exchange(): lax.ppermute(sums[1], 'scene', along_x)  4.77 us
    ppermute x3, waiting for transfers between devices, first_exchange(): lax.ppermute(sends[0], 'scene', along_x)  4.48 us
    ppermute x3, starting transfers between devices, shards(): lax.ppermute(part_out, 'view', pairs)  4.45 us
    pallas_call x1, Pallas kernels, shards(): pl.pallas_call(project_kernel, in_specs=[SMEM] + [VMEM] * 10, out_specs=[...  4.13 us
    ppermute x3, waiting for transfers between devices, shards(): granted = [lax.ppermute(partners, 'view', pairs) for pairs in between]  3.48 us
  transfers between devices with their start and end apart: 31, of which 17 were waited for; matrix products, arithmetic and copies ran while one was open for 0% of the time, Pallas kernels for 18%

profile of v23, /device:TPU:0, one launch (start us, length us, event | category | flops | bytes accessed | tf_op | source)
XLA Modules:
  0.0 83.9 jit_solution(9112157339609180023)
XLA Ops:
  0.6 0.8 copy.13.partners
  1.4 3.0 %collective-permute-start.2 = (s32[1,4,3]{2,1,0:T(4,128)S(1)}, s32[1,4,3]{2,1,0:T(4,128)S(1)}, u32[]{:S(2)}, u32[]{:S(2)}) collective-permute-start(s32[1,4,3]{2,1,0:T(4,128)S(1)} %copy.13.partners), channel_id=1, source_target_pairs={{0,2},{2,0},{4,6},{6,4},{1,3},{3,1},{5,7},{7,5},{8,10},{10,8},{12,... | collective-permute-start | bytes 152 | tf_op jit(solution)/shard_map/ppermute | solution.py:431
  4.4 2.6 %collective-permute-start.1 = (s32[1,4,3]{2,1,0:T(4,128)S(1)}, s32[1,4,3]{2,1,0:T(4,128)S(1)}, u32[]{:S(2)}, u32[]{:S(2)}) collective-permute-start(s32[1,4,3]{2,1,0:T(4,128)S(1)} %copy.13.partners), channel_id=1, source_target_pairs={{0,4},{2,6},{4,0},{6,2},{1,5},{3,7},{5,1},{7,3},{8,12},{10,14},{12... | collective-permute-start | bytes 152 | tf_op jit(solution)/shard_map/ppermute | solution.py:431
  7.0 0.5 collective-permute-start.7
  7.5 1.2 %alive.1 = s32[16]{0:T(128)S(1)} custom-call(s32[1,4,3]{2,1,0:T(4,128)S(1)} %copy.13.partners), custom_call_target="tpu_custom_call" | custom-call | flops 40000000000 | bytes 1 | tf_op jit(solution)/shard_map/alive/pallas_call | solution.py:421
  8.8 0.1 stack.23.scalars
  8.9 0.0 copy-start.6
  8.9 3.5 %collective-permute-done.refs_0_ = s32[1,4,3]{2,1,0:T(4,128)S(1)} collective-permute-done((s32[1,4,3]{2,1,0:T(4,128)S(1)}, s32[1,4,3]{2,1,0:T(4,128)S(1)}, u32[]{:S(2)}, u32[]{:S(2)}) %collective-permute-start) | collective-permute-done | bytes 80 | tf_op jit(solution)/shard_map/ppermute | solution.py:431
  12.4 0.8 pick.1
  13.2 0.4 collective-permute-start.3
  13.6 4.0 %collective-permute-start.5 = (bf16[32,1536]{1,0:T(8,128)(2,1)S(1)}, bf16[32,1536]{1,0:T(8,128)(2,1)S(1)}, u32[]{:S(2)}, u32[]{:S(2)}) collective-permute-start(bf16[32,1536]{1,0:T(8,128)(2,1)S(1)} %get-tuple-element.79), channel_id=1, source_target_pairs={{0,2},{2,0},{4,6},{6,4},{1,3},{3,1},{5,7},{7,5},{8,10},{10,8},{12,... | collective-permute-start | bytes 294920 | tf_op jit(solution)/shard_map/ppermute | solution.py:448
  17.7 4.1 %project.1 = (bf16[1536,256]{1,0:T(8,128)(2,1)S(1)}, bf16[256,384]{1,0:T(8,128)(2,1)S(1)}, bf16[256,384]{1,0:T(8,128)(2,1)S(1)}, bf16[256,1536]{1,0:T(8,128)(2,1...) custom-call(s32[5]{0:T(128)S(1)} %stack.23.scalars, ...), custom_call_target="tpu_custom_call" | custom-call | flops 1 | bytes 1 | tf_op jit(solution)/shard_map/project/pallas_call | solution.py:450
  21.9 0.4 collective-permute-done.4.refs_1_
  22.3 0.1 collective-permute-start.8
  22.4 0.4 collective-permute-start.9
  22.8 0.1 collective-permute-start.10
  22.9 0.7 collective-permute-done.8.refs_3_
  23.6 0.2 collective-permute-done.9.refs_4_
  23.7 0.4 collective-permute-done.10.refs_5_
  24.1 3.2 %attention_forward.1 = (bf16[1536,192]{1,0:T(8,128)(2,1)S(1)}, bf16[192,384]{1,0:T(8,128)(2,1)S(1)}, bf16[192,384]{1,0:T(8,128)(2,1)S(1)}, f32[3,64,512]{2,1,0:T...) custom-call(s32[5]{0:T(128)S(1)} %stack.23.scalars, ...), custom_call_target="tpu_custom_call" | custom-call | flops 1 | bytes 1 | tf_op jit(solution)/shard_map/attention_forward/pallas_call | solution.py:486
  27.3 0.2 collective-permute-start.11
  27.5 1.6 %attention_backward.1 = (bf16[256,384]{1,0:T(8,128)(2,1)S(1)}, bf16[448,384]{1,0:T(8,128)(2,1)S(1)}) custom-call(bf16[3,512,128]{2,1,0:T(8,128)(2,1)S(1)} %get-tuple-element.86.refs_6_.query_stack, bf16[3,512,128]{2,1,0:T(8,128)(2,1)S(1)} %get-tuple-element.87.refs_7_.grad_stack, f32[3,64,512]{2,1,0:T(8,128)S(1)} %get-tuple-element.91.dprob_own, ...), custom_call_target="tpu_custom_call" | custom-call | flops 1 | bytes 1 | tf_op jit(solution)/shard_map/attention_backward/pallas_call | solution.py:474
  29.1 1.3 %grad_value_out_sent.1 = (bf16[2,2,48,1536]{3,2,1,0:T(8,128)(2,1)S(1)}, bf16[2,2,48,1536]{3,2,1,0:T(8,128)(2,1)S(1)}) custom-call(s32[5]{0:T(128)S(1)} %stack.23.scalars, bf16[1536,256]{1,0:T(8,128)(2,1)S(1)} %get-tuple-element.81.normed_t, bf16[1536,192]{1,0:T(8,128)(2,1)S(1)} %get-tuple-element.90.normed_far_t, ...), custom_call_target="tpu_custom_call" | custom-call | flops 1 | bytes 1 | tf_op jit(solution)/shard_map/grad_value_out_sent/pallas_call | solution.py:474
  30.4 0.4 collective-permute-start.18
  30.7 1.9 %grad_query_key.1 = (bf16[384,384]{1,0:T(8,128)(2,1)S(1)}, bf16[384,384]{1,0:T(8,128)(2,1)S(1)}, bf16[384,384]{1,0:T(8,128)(2,1)S(1)}, bf16[384,384]{1,0:T(8,128...) custom-call(s32[5]{0:T(128)S(1)} %stack.23.scalars, ...), custom_call_target="tpu_custom_call" | custom-call | flops 1 | bytes 1 | tf_op jit(solution)/shard_map/grad_query_key/pallas_call | solution.py:474
  32.7 1.5 %collective-permute-start.13 = (bf16[384,384]{1,0:T(8,128)(2,1)S(1)}, bf16[384,384]{1,0:T(8,128)(2,1)S(1)}, u32[]{:S(2)}, u32[]{:S(2)}) collective-permute-start(bf16[384,384]{1,0:T(8,128)(2,1)S(1)} %get-tuple-element.108), channel_id=1, source_target_pairs={{0,8},{8,0},{16,24},{24,16},{1,9},{9,1},{17,25},{25,17},{2,10},{10... | collective-permute-start | bytes 884744 | tf_op jit(solution)/shard_map/ppermute | solution.py:524
  34.2 1.5 %collective-permute-start.14 = (bf16[384,384]{1,0:T(8,128)(2,1)S(1)}, bf16[384,384]{1,0:T(8,128)(2,1)S(1)}, u32[]{:S(2)}, u32[]{:S(2)}) collective-permute-start(bf16[384,384]{1,0:T(8,128)(2,1)S(1)} %get-tuple-element.110), channel_id=1, source_target_pairs={{0,16},{8,24},{16,0},{24,8},{1,17},{9,25},{17,1},{25,9},{2,18},{10... | collective-permute-start | bytes 884744 | tf_op jit(solution)/shard_map/ppermute | solution.py:524
  35.7 1.3 %grad_value_out_kept.1.keep = f32[2,2,2,48,1536]{4,3,2,1,0:T(8,128)S(1)} custom-call(s32[5]{0:T(128)S(1)} %stack.23.scalars, bf16[1536,256]{1,0:T(8,128)(2,1)S(1)} %get-tuple-element.81.normed_t, bf16[1536,192]{1,0:T(8,128)(2,1)S(1)} %get-tuple-element.90.normed_far_t, bf16[448,384]{1,0:T(8,128)(2,1)S(1)} %get-tuple-element.100.dvalue, ...), custom_call_target="tpu_custom_call" | custom-call | flops 1 | bytes 1 | tf_op jit(solution)/shard_map/grad_value_out_kept/pallas_call | solution.py:474
  37.0 0.6 collective-permute-start.12
  37.6 0.5 collective-permute-start.16
  38.1 4.5 %collective-permute-done.13.q_got = bf16[384,384]{1,0:T(8,128)(2,1)S(1)} collective-permute-done((bf16[384,384]{1,0:T(8,128)(2,1)S(1)}, bf16[384,384]{1,0:T(8,128)(2,1)S(1)}, u32[]{:S(2)}, u32[]{:S(2)}) %collective-permute-start.13) | collective-permute-done | bytes 294944 | tf_op jit(solution)/shard_map/ppermute | solution.py:524
  42.6 1.5 %collective-permute-done.14.k_got = bf16[384,384]{1,0:T(8,128)(2,1)S(1)} collective-permute-done((bf16[384,384]{1,0:T(8,128)(2,1)S(1)}, bf16[384,384]{1,0:T(8,128)(2,1)S(1)}, u32[]{:S(2)}, u32[]{:S(2)}) %collective-permute-start.14) | collective-permute-done | bytes 294944 | tf_op jit(solution)/shard_map/ppermute | solution.py:524
  44.1 0.1 first_sum_query_key.1
  44.2 1.8 %collective-permute-done.18.got = bf16[2,2,48,1536]{3,2,1,0:T(8,128)(2,1)S(1)} collective-permute-done((bf16[2,2,48,1536]{3,2,1,0:T(8,128)(2,1)S(1)}, bf16[2,2,48,1536]{3,2,1,0:T(8,128)(2,1)S(1)}, u32[]{:S(2)}, u32[]{:S(2)}) %collective-permute-start.18) | collective-permute-done | bytes 589856 | tf_op jit(solution)/shard_map/ppermute | solution.py:569
  46.0 0.3 collective-permute-start.19
  46.3 1.5 %collective-permute-start.17 = (bf16[384,384]{1,0:T(8,128)(2,1)S(1)}, bf16[384,384]{1,0:T(8,128)(2,1)S(1)}, u32[]{:S(2)}, u32[]{:S(2)}) collective-permute-start(bf16[384,384]{1,0:T(8,128)(2,1)S(1)} %get-tuple-element.113), channel_id=1, source_target_pairs={{0,8},{8,0},{16,24},{24,16},{1,9},{9,1},{17,25},{25,17},{2,10},{10... | collective-permute-start | bytes 884744 | tf_op jit(solution)/shard_map/ppermute | solution.py:532
  47.8 1.5 %collective-permute-start.15 = (bf16[384,384]{1,0:T(8,128)(2,1)S(1)}, bf16[384,384]{1,0:T(8,128)(2,1)S(1)}, u32[]{:S(2)}, u32[]{:S(2)}) collective-permute-start(bf16[384,384]{1,0:T(8,128)(2,1)S(1)} %get-tuple-element.111), channel_id=1, source_target_pairs={{0,16},{8,24},{16,0},{24,8},{1,17},{9,25},{17,1},{25,9},{2,18},{10... | collective-permute-start | bytes 884744 | tf_op jit(solution)/shard_map/ppermute | solution.py:532
  49.4 0.1 view_sum_sent.1
  49.5 0.6 collective-permute-start.20
  50.1 1.4 %collective-permute-start.21 = (bf16[2,2,48,768]{3,2,1,0:T(8,128)(2,1)S(1)}, bf16[2,2,48,768]{3,2,1,0:T(8,128)(2,1)S(1)}, u32[]{:S(2)}, u32[]{:S(2)}) collective-permute-start(bf16[2,2,48,768]{3,2,1,0:T(8,128)(2,1)S(1)} %get-tuple-element.123), channel_id=1, source_target_pairs={{0,16},{8,24},{16,0},{24,8},{1,17},{9,25},{17,1},{25,9},{2,18},{10... | collective-permute-start | bytes 884744 | tf_op jit(solution)/shard_map/ppermute | solution.py:524
  51.5 4.8 %collective-permute-done.17.k_second = bf16[384,384]{1,0:T(8,128)(2,1)S(1)} collective-permute-done((bf16[384,384]{1,0:T(8,128)(2,1)S(1)}, bf16[384,384]{1,0:T(8,128)(2,1)S(1)}, u32[]{:S(2)}, u32[]{:S(2)}) %collective-permute-start.17) | collective-permute-done | bytes 294944 | tf_op jit(solution)/shard_map/ppermute | solution.py:532
  56.3 1.5 %collective-permute-done.15.q_second = bf16[384,384]{1,0:T(8,128)(2,1)S(1)} collective-permute-done((bf16[384,384]{1,0:T(8,128)(2,1)S(1)}, bf16[384,384]{1,0:T(8,128)(2,1)S(1)}, u32[]{:S(2)}, u32[]{:S(2)}) %collective-permute-start.15) | collective-permute-done | bytes 294944 | tf_op jit(solution)/shard_map/ppermute | solution.py:532
  57.8 0.8 second_sum_query_key.1
  58.6 1.8 %collective-permute-start.22 = (bf16[2,96,768]{2,1,0:T(8,128)(2,1)S(1)}, bf16[2,96,768]{2,1,0:T(8,128)(2,1)S(1)}, u32[]{:S(2)}, u32[]{:S(2)}) collective-permute-start(bf16[2,96,768]{2,1,0:T(8,128)(2,1)S(1)} %get-tuple-element.117), channel_id=1, source_target_pairs={{0,2},{2,0},{4,6},{6,4},{1,3},{3,1},{5,7},{7,5},{8,10},{10,8},{12,... | collective-permute-start | bytes 884744 | tf_op jit(solution)/shard_map/ppermute | solution.py:605
  60.4 1.9 %collective-permute-done.19.got = bf16[2,2,48,1536]{3,2,1,0:T(8,128)(2,1)S(1)} collective-permute-done((bf16[2,2,48,1536]{3,2,1,0:T(8,128)(2,1)S(1)}, bf16[2,2,48,1536]{3,2,1,0:T(8,128)(2,1)S(1)}, u32[]{:S(2)}, u32[]{:S(2)}) %collective-permute-start.19) | collective-permute-done | bytes 589856 | tf_op jit(solution)/shard_map/ppermute | solution.py:588
  62.3 0.1 view_sum_kept.1
  62.4 0.1 first_sum_value_out.1
  62.6 1.6 %collective-permute-start.26 = (bf16[2,48,768]{2,1,0:T(8,128)(2,1)S(1)}, bf16[2,48,768]{2,1,0:T(8,128)(2,1)S(1)}, u32[]{:S(2)}, u32[]{:S(2)}) collective-permute-start(bf16[2,48,768]{2,1,0:T(8,128)(2,1)S(1)} %get-tuple-element.135), channel_id=1, source_target_pairs={{0,8},{8,0},{16,24},{24,16},{1,9},{9,1},{17,25},{25,17},{2,10},{10... | collective-permute-start | bytes 442376 | tf_op jit(solution)/shard_map/ppermute | solution.py:532
  64.1 1.5 %collective-permute-start.27 = (bf16[2,48,768]{2,1,0:T(8,128)(2,1)S(1)}, bf16[2,48,768]{2,1,0:T(8,128)(2,1)S(1)}, u32[]{:S(2)}, u32[]{:S(2)}) collective-permute-start(bf16[2,48,768]{2,1,0:T(8,128)(2,1)S(1)} %get-tuple-element.124), channel_id=1, source_target_pairs={{0,16},{8,24},{16,0},{24,8},{1,17},{9,25},{17,1},{25,9},{2,18},{10... | collective-permute-start | bytes 442376 | tf_op jit(solution)/shard_map/ppermute | solution.py:532
  65.7 1.5 %collective-permute-done.22.refs_1_ = bf16[2,96,768]{2,1,0:T(8,128)(2,1)S(1)} collective-permute-done((bf16[2,96,768]{2,1,0:T(8,128)(2,1)S(1)}, bf16[2,96,768]{2,1,0:T(8,128)(2,1)S(1)}, u32[]{:S(2)}, u32[]{:S(2)}) %collective-permute-start.22) | collective-permute-done | bytes 294944 | tf_op jit(solution)/shard_map/ppermute | solution.py:605
  67.1 0.6 last_parts_query_key.1
  67.8 0.1 collective-permute-start.24
  67.9 1.2 %collective-permute-start.23 = (bf16[48,768]{1,0:T(8,128)(2,1)S(1)}, bf16[48,768]{1,0:T(8,128)(2,1)S(1)}, u32[]{:S(2)}, u32[]{:S(2)}) collective-permute-start(bf16[48,768]{1,0:T(8,128)(2,1)S(1)} %get-tuple-element.127), channel_id=1, source_target_pairs={{0,4},{2,6},{4,0},{6,2},{1,5},{3,7},{5,1},{7,3},{8,12},{10,14},{12... | collective-permute-start | bytes 221192 | tf_op jit(solution)/shard_map/ppermute | solution.py:558
  69.1 0.2 collective-permute-done.27.refs_3_
  69.3 0.6 last_parts_value_out.1
  69.9 0.1 collective-permute-start.29
  70.0 1.7 %collective-permute-start.25 = (bf16[48,768]{1,0:T(8,128)(2,1)S(1)}, bf16[48,768]{1,0:T(8,128)(2,1)S(1)}, u32[]{:S(2)}, u32[]{:S(2)}) collective-permute-start(bf16[48,768]{1,0:T(8,128)(2,1)S(1)} %get-tuple-element.129), channel_id=1, source_target_pairs={{0,5},{1,4},{2,7},{3,6},{4,1},{5,0},{6,3},{7,2},{8,13},{9,12},{10,... | collective-permute-start | bytes 221192 | tf_op jit(solution)/shard_map/ppermute | solution.py:559
  71.7 1.4 %collective-permute-start.28 = (bf16[24,1536]{1,0:T(8,128)(2,1)S(1)}, bf16[24,1536]{1,0:T(8,128)(2,1)S(1)}, u32[]{:S(2)}, u32[]{:S(2)}) collective-permute-start(bf16[24,1536]{1,0:T(8,128)(2,1)S(1)} %get-tuple-element.139), channel_id=1, source_target_pairs={{0,4},{2,6},{4,0},{6,2},{1,5},{3,7},{5,1},{7,3},{8,12},{10,14},{12... | collective-permute-start | bytes 221192 | tf_op jit(solution)/shard_map/ppermute | solution.py:558
  73.0 1.8 %collective-permute-done.23.far_same = bf16[48,768]{1,0:T(8,128)(2,1)S(1)} collective-permute-done((bf16[48,768]{1,0:T(8,128)(2,1)S(1)}, bf16[48,768]{1,0:T(8,128)(2,1)S(1)}, u32[]{:S(2)}, u32[]{:S(2)}) %collective-permute-start.23) | collective-permute-done | bytes 73760 | tf_op jit(solution)/shard_map/ppermute | solution.py:558
  74.8 4.6 %collective-permute-done.25.far_cross = bf16[48,768]{1,0:T(8,128)(2,1)S(1)} collective-permute-done((bf16[48,768]{1,0:T(8,128)(2,1)S(1)}, bf16[48,768]{1,0:T(8,128)(2,1)S(1)}, u32[]{:S(2)}, u32[]{:S(2)}) %collective-permute-start.25) | collective-permute-done | bytes 73760 | tf_op jit(solution)/shard_map/ppermute | solution.py:559
  79.5 1.3 %place_query_key.1 = (f32[48,768]{1,0:T(8,128)}, f32[48,768]{1,0:T(8,128)}) custom-call(s32[5]{0:T(128)S(1)} %stack.23.scalars, f32[48,768]{1,0:T(8,128)S(1)} %get-tuple-element.130.same, f32[48,768]{1,0:T(8,128)S(1)} %get-tuple-element.131.cross), custom_call_target="tpu_custom_call" | custom-call | flops 1 | bytes 1 | tf_op jit(solution)/shard_map/place_query_key/pallas_call | solution.py:474
  80.8 0.4 collective-permute-done.28.far_same
  81.1 1.5 %collective-permute-done.30.far_cross = bf16[24,1536]{1,0:T(8,128)(2,1)S(1)} collective-permute-done((bf16[24,1536]{1,0:T(8,128)(2,1)S(1)}, bf16[24,1536]{1,0:T(8,128)(2,1)S(1)}, u32[]{:S(2)}, u32[]{:S(2)}) %collective-permute-start.30) | collective-permute-done | bytes 73760 | tf_op jit(solution)/shard_map/ppermute | solution.py:559
  82.6 1.3 %last_sum_value_out.1 = (f32[48,768]{1,0:T(8,128)}, f32[24,1536]{1,0:T(8,128)}) custom-call(s32[5]{0:T(128)S(1)} %stack.23.scalars, f32[24,1536]{1,0:T(8,128)S(1)} %get-tuple-element.138.mine, bf16[24,1536]{1,0:T(8,128)(2,1)S(1)} %collective-permute-done.28.far_same, f32[24,1536]{1,0:T(8,128)S(1)} %collective-permute-done.29.near_cross, ...), custom_call_target="tpu_custom_call" | custom-call | flops 1 | bytes 1 | tf_op jit(solution)/shard_map/last_sum_value_out/pallas_call | solution.py:474
  (34 shorter events, 0.1 us)
Async XLA Ops:
  1.4 7.5 %collective-permute-start.2 = (s32[1,4,3]{2,1,0:T(4,128)S(1)}, s32[1,4,3]{2,1,0:T(4,128)S(1)}, u32[]{:S(2)}, u32[]{:S(2)}) collective-permute-start(s32[1,4,3]{2,1,0:T(4,128)S(1)} %copy.13.partners), channel_id=1, source_target_pairs={{0,2},{2,0},{4,6},{6,4},{1,3},{3,1},{5,7},{7,5},{8,10},{10,8},{12,... | collective-permute-start | bytes 152 | tf_op jit(solution)/shard_map/ppermute | solution.py:431
  4.4 4.5 %collective-permute-start.1 = (s32[1,4,3]{2,1,0:T(4,128)S(1)}, s32[1,4,3]{2,1,0:T(4,128)S(1)}, u32[]{:S(2)}, u32[]{:S(2)}) collective-permute-start(s32[1,4,3]{2,1,0:T(4,128)S(1)} %copy.13.partners), channel_id=1, source_target_pairs={{0,4},{2,6},{4,0},{6,2},{1,5},{3,7},{5,1},{7,3},{8,12},{10,14},{12... | collective-permute-start | bytes 152 | tf_op jit(solution)/shard_map/ppermute | solution.py:431
  7.0 5.4 %collective-permute-start = (s32[1,4,3]{2,1,0:T(4,128)S(1)}, s32[1,4,3]{2,1,0:T(4,128)S(1)}, u32[]{:S(2)}, u32[]{:S(2)}) collective-permute-start(s32[1,4,3]{2,1,0:T(4,128)S(1)} %copy.13.partners), channel_id=1, source_target_pairs={{0,6},{2,4},{4,2},{6,0},{1,7},{3,5},{5,3},{7,1},{8,14},{10,12},{12... | collective-permute-start | bytes 152 | tf_op jit(solution)/shard_map/ppermute | solution.py:431
  7.0 10.6 %collective-permute-start.6 = (bf16[4,32,1536]{2,1,0:T(8,128)(2,1)}, bf16[4,32,1536]{2,1,0:T(8,128)(2,1)S(1)}, u32[]{:S(2)}, u32[]{:S(2)}) collective-permute-start(bf16[4,32,1536]{2,1,0:T(8,128)(2,1)} %bitcast.7), channel_id=1, source_target_pairs={{0,1},{1,0},{2,3},{3,2},{4,5},{5,4},{6,7},{7,6},{8,9},{9,8},{10,11... | collective-permute-start | bytes 1179656 | tf_op jit(solution)/shard_map/ppermute | solution.py:436
  7.0 10.6 %collective-permute-start.7 = (bf16[4,32,1536]{2,1,0:T(8,128)(2,1)}, bf16[4,32,1536]{2,1,0:T(8,128)(2,1)S(1)}, u32[]{:S(2)}, u32[]{:S(2)}) collective-permute-start(bf16[4,32,1536]{2,1,0:T(8,128)(2,1)} %bitcast.10), channel_id=1, source_target_pairs={{0,1},{1,0},{2,3},{3,2},{4,5},{5,4},{6,7},{7,6},{8,9},{9,8},{10,11... | collective-permute-start | bytes 1179656 | tf_op jit(solution)/shard_map/ppermute | solution.py:437
  7.5 4.9 %copy-start.4 = (bf16[1,4,1,32,1536]{4,3,2,1,0:T(8,128)(2,1)S(1)}, bf16[1,4,1,32,1536]{4,3,2,1,0:T(8,128)(2,1)}, u32[]{:S(2)}) copy-start(bf16[1,4,1,32,1536]{4,3,2,1,0:T(8,128)(2,1)} %param.10) | copy-start | bytes 1179652
  8.8 8.8 %copy-start = (bf16[1536,768]{1,0:T(8,128)(2,1)S(1)}, bf16[1536,768]{1,0:T(8,128)(2,1)}, u32[]{:S(2)}) copy-start(bf16[1536,768]{1,0:T(8,128)(2,1)} %refs_11_.1) | copy-start | bytes 7077892
  8.9 8.8 %copy-start.1 = (bf16[1536,768]{1,0:T(8,128)(2,1)S(1)}, bf16[1536,768]{1,0:T(8,128)(2,1)}, u32[]{:S(2)}) copy-start(bf16[1536,768]{1,0:T(8,128)(2,1)} %refs_12_.1) | copy-start | bytes 7077892
  8.9 8.8 %copy-start.2 = (bf16[1536,768]{1,0:T(8,128)(2,1)S(1)}, bf16[1536,768]{1,0:T(8,128)(2,1)}, u32[]{:S(2)}) copy-start(bf16[1536,768]{1,0:T(8,128)(2,1)} %w_query.1) | copy-start | bytes 7077892
  8.9 8.8 %copy-start.3 = (bf16[768,1536]{1,0:T(8,128)(2,1)S(1)}, bf16[768,1536]{1,0:T(8,128)(2,1)}, u32[]{:S(2)}) copy-start(bf16[768,1536]{1,0:T(8,128)(2,1)} %w_out.1) | copy-start | bytes 7077892
  8.9 8.8 %copy-start.5 = (bf16[1,4,1,32,1536]{4,3,2,1,0:T(8,128)(2,1)S(1)}, bf16[1,4,1,32,1536]{4,3,2,1,0:T(8,128)(2,1)}, u32[]{:S(2)}) copy-start(bf16[1,4,1,32,1536]{4,3,2,1,0:T(8,128)(2,1)} %param.18) | copy-start | bytes 1179652
  8.9 8.8 %copy-start.6 = (bf16[9,1536]{1,0:T(8,128)(2,1)S(1)}, bf16[9,1536]{1,0:T(8,128)(2,1)}, u32[]{:S(2)}) copy-start(bf16[9,1536]{1,0:T(8,128)(2,1)} %taps.1) | copy-start | bytes 82948
  8.9 8.8 %copy-start.7 = (f32[1536]{0:T(1024)S(1)}, f32[1536]{0:T(1024)}, u32[]{:S(2)}) copy-start(f32[1536]{0:T(1024)} %refs_10_.1) | copy-start | bytes 18436
  13.2 8.7 %collective-permute-start.3 = (bf16[32,1536]{1,0:T(8,128)(2,1)S(1)}, bf16[32,1536]{1,0:T(8,128)(2,1)S(1)}, u32[]{:S(2)}, u32[]{:S(2)}) collective-permute-start(bf16[32,1536]{1,0:T(8,128)(2,1)S(1)} %get-tuple-element.77), channel_id=1, source_target_pairs={{0,6},{2,4},{4,2},{6,0},{1,7},{3,5},{5,3},{7,1},{8,14},{10,12},{12... | collective-permute-start | bytes 294920 | tf_op jit(solution)/shard_map/ppermute | solution.py:448
  13.6 8.7 %collective-permute-start.4 = (bf16[32,1536]{1,0:T(8,128)(2,1)S(1)}, bf16[32,1536]{1,0:T(8,128)(2,1)S(1)}, u32[]{:S(2)}, u32[]{:S(2)}) collective-permute-start(bf16[32,1536]{1,0:T(8,128)(2,1)S(1)} %get-tuple-element.78), channel_id=1, source_target_pairs={{0,4},{2,6},{4,0},{6,2},{1,5},{3,7},{5,1},{7,3},{8,12},{10,14},{12... | collective-permute-start | bytes 294920 | tf_op jit(solution)/shard_map/ppermute | solution.py:448
  13.6 8.7 %collective-permute-start.5 = (bf16[32,1536]{1,0:T(8,128)(2,1)S(1)}, bf16[32,1536]{1,0:T(8,128)(2,1)S(1)}, u32[]{:S(2)}, u32[]{:S(2)}) collective-permute-start(bf16[32,1536]{1,0:T(8,128)(2,1)S(1)} %get-tuple-element.79), channel_id=1, source_target_pairs={{0,2},{2,0},{4,6},{6,4},{1,3},{3,1},{5,7},{7,5},{8,10},{10,8},{12,... | collective-permute-start | bytes 294920 | tf_op jit(solution)/shard_map/ppermute | solution.py:448
  22.3 1.3 %collective-permute-start.8 = (bf16[32,1536]{1,0:T(8,128)(2,1)S(1)}, bf16[32,1536]{1,0:T(8,128)(2,1)S(1)}, u32[]{:S(2)}, u32[]{:S(2)}) collective-permute-start(bf16[32,1536]{1,0:T(8,128)(2,1)S(1)} %collective-permute-done.3.refs_0_), channel_id=1, source_target_pairs={{0,1},{1,0},{2,3},{3,2},{4,5},{5,4},{6,7},{7,6},{8,9},{9,8},{10,11... | collective-permute-start | bytes 294920 | tf_op jit(solution)/shard_map/ppermute | solution.py:471
  22.4 1.4 %collective-permute-start.9 = (bf16[32,1536]{1,0:T(8,128)(2,1)S(1)}, bf16[32,1536]{1,0:T(8,128)(2,1)S(1)}, u32[]{:S(2)}, u32[]{:S(2)}) collective-permute-start(bf16[32,1536]{1,0:T(8,128)(2,1)S(1)} %collective-permute-done.4.refs_1_), channel_id=1, source_target_pairs={{0,1},{1,0},{2,3},{3,2},{4,5},{5,4},{6,7},{7,6},{8,9},{9,8},{10,11... | collective-permute-start | bytes 294920 | tf_op jit(solution)/shard_map/ppermute | solution.py:471
  22.8 1.3 %collective-permute-start.10 = (bf16[32,1536]{1,0:T(8,128)(2,1)S(1)}, bf16[32,1536]{1,0:T(8,128)(2,1)S(1)}, u32[]{:S(2)}, u32[]{:S(2)}) collective-permute-start(bf16[32,1536]{1,0:T(8,128)(2,1)S(1)} %collective-permute-done.5.refs_2_), channel_id=1, source_target_pairs={{0,1},{1,0},{2,3},{3,2},{4,5},{5,4},{6,7},{7,6},{8,9},{9,8},{10,11... | collective-permute-start | bytes 294920 | tf_op jit(solution)/shard_map/ppermute | solution.py:471
  27.3 1.8 %collective-permute-start.11 = (bf16[384,256]{1,0:T(8,128)(2,1)S(1)}, bf16[384,256]{1,0:T(8,128)(2,1)S(1)}, u32[]{:S(2)}, u32[]{:S(2)}) collective-permute-start(bf16[384,256]{1,0:T(8,128)(2,1)S(1)} %get-tuple-element.101.mine), channel_id=1, source_target_pairs={{0,1},{1,0},{2,3},{3,2},{4,5},{5,4},{6,7},{7,6},{8,9},{9,8},{10,11... | collective-permute-start | bytes 589832 | tf_op jit(solution)/shard_map/ppermute | solution.py:506
  30.4 15.7 %collective-permute-start.18 = (bf16[2,2,48,1536]{3,2,1,0:T(8,128)(2,1)S(1)}, bf16[2,2,48,1536]{3,2,1,0:T(8,128)(2,1)S(1)}, u32[]{:S(2)}, u32[]{:S(2)}) collective-permute-start(bf16[2,2,48,1536]{3,2,1,0:T(8,128)(2,1)S(1)} %get-tuple-element.103), channel_id=1, source_target_pairs={{0,2},{2,0},{4,6},{6,4},{1,3},{3,1},{5,7},{7,5},{8,10},{10,8},{12,... | collective-permute-start | bytes 1769480 | tf_op jit(solution)/shard_map/ppermute | solution.py:569
  32.7 9.9 %collective-permute-start.13 = (bf16[384,384]{1,0:T(8,128)(2,1)S(1)}, bf16[384,384]{1,0:T(8,128)(2,1)S(1)}, u32[]{:S(2)}, u32[]{:S(2)}) collective-permute-start(bf16[384,384]{1,0:T(8,128)(2,1)S(1)} %get-tuple-element.108), channel_id=1, source_target_pairs={{0,8},{8,0},{16,24},{24,16},{1,9},{9,1},{17,25},{25,17},{2,10},{10... | collective-permute-start | bytes 884744 | tf_op jit(solution)/shard_map/ppermute | solution.py:524
  34.2 9.9 %collective-permute-start.14 = (bf16[384,384]{1,0:T(8,128)(2,1)S(1)}, bf16[384,384]{1,0:T(8,128)(2,1)S(1)}, u32[]{:S(2)}, u32[]{:S(2)}) collective-permute-start(bf16[384,384]{1,0:T(8,128)(2,1)S(1)} %get-tuple-element.110), channel_id=1, source_target_pairs={{0,16},{8,24},{16,0},{24,8},{1,17},{9,25},{17,1},{25,9},{2,18},{10... | collective-permute-start | bytes 884744 | tf_op jit(solution)/shard_map/ppermute | solution.py:524
  37.0 12.3 %collective-permute-start.12 = (bf16[384,384]{1,0:T(8,128)(2,1)S(1)}, bf16[384,384]{1,0:T(8,128)(2,1)S(1)}, u32[]{:S(2)}, u32[]{:S(2)}) collective-permute-start(bf16[384,384]{1,0:T(8,128)(2,1)S(1)} %get-tuple-element.106), channel_id=1, source_target_pairs={{0,8},{8,0},{16,24},{24,16},{1,9},{9,1},{17,25},{25,17},{2,10},{10... | collective-permute-start | bytes 884744 | tf_op jit(solution)/shard_map/ppermute | solution.py:524
  37.6 11.7 %collective-permute-start.16 = (bf16[384,384]{1,0:T(8,128)(2,1)S(1)}, bf16[384,384]{1,0:T(8,128)(2,1)S(1)}, u32[]{:S(2)}, u32[]{:S(2)}) collective-permute-start(bf16[384,384]{1,0:T(8,128)(2,1)S(1)} %get-tuple-element.112), channel_id=1, source_target_pairs={{0,16},{8,24},{16,0},{24,8},{1,17},{9,25},{17,1},{25,9},{2,18},{10... | collective-permute-start | bytes 884744 | tf_op jit(solution)/shard_map/ppermute | solution.py:524
  46.0 16.3 %collective-permute-start.19 = (bf16[2,2,48,1536]{3,2,1,0:T(8,128)(2,1)S(1)}, bf16[2,2,48,1536]{3,2,1,0:T(8,128)(2,1)S(1)}, u32[]{:S(2)}, u32[]{:S(2)}) collective-permute-start(bf16[2,2,48,1536]{3,2,1,0:T(8,128)(2,1)S(1)} %get-tuple-element.116), channel_id=1, source_target_pairs={{0,2},{2,0},{4,6},{6,4},{1,3},{3,1},{5,7},{7,5},{8,10},{10,8},{12,... | collective-permute-start | bytes 1769480 | tf_op jit(solution)/shard_map/ppermute | solution.py:588
  46.3 9.9 %collective-permute-start.17 = (bf16[384,384]{1,0:T(8,128)(2,1)S(1)}, bf16[384,384]{1,0:T(8,128)(2,1)S(1)}, u32[]{:S(2)}, u32[]{:S(2)}) collective-permute-start(bf16[384,384]{1,0:T(8,128)(2,1)S(1)} %get-tuple-element.113), channel_id=1, source_target_pairs={{0,8},{8,0},{16,24},{24,16},{1,9},{9,1},{17,25},{25,17},{2,10},{10... | collective-permute-start | bytes 884744 | tf_op jit(solution)/shard_map/ppermute | solution.py:532
  47.8 9.9 %collective-permute-start.15 = (bf16[384,384]{1,0:T(8,128)(2,1)S(1)}, bf16[384,384]{1,0:T(8,128)(2,1)S(1)}, u32[]{:S(2)}, u32[]{:S(2)}) collective-permute-start(bf16[384,384]{1,0:T(8,128)(2,1)S(1)} %get-tuple-element.111), channel_id=1, source_target_pairs={{0,16},{8,24},{16,0},{24,8},{1,17},{9,25},{17,1},{25,9},{2,18},{10... | collective-permute-start | bytes 884744 | tf_op jit(solution)/shard_map/ppermute | solution.py:532
  49.5 12.9 %collective-permute-start.20 = (bf16[2,2,48,768]{3,2,1,0:T(8,128)(2,1)S(1)}, bf16[2,2,48,768]{3,2,1,0:T(8,128)(2,1)S(1)}, u32[]{:S(2)}, u32[]{:S(2)}) collective-permute-start(bf16[2,2,48,768]{3,2,1,0:T(8,128)(2,1)S(1)} %get-tuple-element.121), channel_id=1, source_target_pairs={{0,8},{8,0},{16,24},{24,16},{1,9},{9,1},{17,25},{25,17},{2,10},{10... | collective-permute-start | bytes 884744 | tf_op jit(solution)/shard_map/ppermute | solution.py:524
  50.1 12.3 %collective-permute-start.21 = (bf16[2,2,48,768]{3,2,1,0:T(8,128)(2,1)S(1)}, bf16[2,2,48,768]{3,2,1,0:T(8,128)(2,1)S(1)}, u32[]{:S(2)}, u32[]{:S(2)}) collective-permute-start(bf16[2,2,48,768]{3,2,1,0:T(8,128)(2,1)S(1)} %get-tuple-element.123), channel_id=1, source_target_pairs={{0,16},{8,24},{16,0},{24,8},{1,17},{9,25},{17,1},{25,9},{2,18},{10... | collective-permute-start | bytes 884744 | tf_op jit(solution)/shard_map/ppermute | solution.py:524
  58.6 8.6 %collective-permute-start.22 = (bf16[2,96,768]{2,1,0:T(8,128)(2,1)S(1)}, bf16[2,96,768]{2,1,0:T(8,128)(2,1)S(1)}, u32[]{:S(2)}, u32[]{:S(2)}) collective-permute-start(bf16[2,96,768]{2,1,0:T(8,128)(2,1)S(1)} %get-tuple-element.117), channel_id=1, source_target_pairs={{0,2},{2,0},{4,6},{6,4},{1,3},{3,1},{5,7},{7,5},{8,10},{10,8},{12,... | collective-permute-start | bytes 884744 | tf_op jit(solution)/shard_map/ppermute | solution.py:605
  62.6 6.5 %collective-permute-start.26 = (bf16[2,48,768]{2,1,0:T(8,128)(2,1)S(1)}, bf16[2,48,768]{2,1,0:T(8,128)(2,1)S(1)}, u32[]{:S(2)}, u32[]{:S(2)}) collective-permute-start(bf16[2,48,768]{2,1,0:T(8,128)(2,1)S(1)} %get-tuple-element.135), channel_id=1, source_target_pairs={{0,8},{8,0},{16,24},{24,16},{1,9},{9,1},{17,25},{25,17},{2,10},{10... | collective-permute-start | bytes 442376 | tf_op jit(solution)/shard_map/ppermute | solution.py:532
  64.1 5.1 %collective-permute-start.27 = (bf16[2,48,768]{2,1,0:T(8,128)(2,1)S(1)}, bf16[2,48,768]{2,1,0:T(8,128)(2,1)S(1)}, u32[]{:S(2)}, u32[]{:S(2)}) collective-permute-start(bf16[2,48,768]{2,1,0:T(8,128)(2,1)S(1)} %get-tuple-element.124), channel_id=1, source_target_pairs={{0,16},{8,24},{16,0},{24,8},{1,17},{9,25},{17,1},{25,9},{2,18},{10... | collective-permute-start | bytes 442376 | tf_op jit(solution)/shard_map/ppermute | solution.py:532
  67.8 11.7 %collective-permute-start.24 = (f32[48,768]{1,0:T(8,128)S(1)}, f32[48,768]{1,0:T(8,128)S(1)}, u32[]{:S(2)}, u32[]{:S(2)}) collective-permute-start(f32[48,768]{1,0:T(8,128)S(1)} %get-tuple-element.128), channel_id=1, source_target_pairs={{0,1},{1,0},{2,3},{3,2},{4,5},{5,4},{6,7},{7,6},{8,9},{9,8},{10,11... | collective-permute-start | bytes 442376 | tf_op jit(solution)/shard_map/ppermute | solution.py:560
  67.9 7.0 %collective-permute-start.23 = (bf16[48,768]{1,0:T(8,128)(2,1)S(1)}, bf16[48,768]{1,0:T(8,128)(2,1)S(1)}, u32[]{:S(2)}, u32[]{:S(2)}) collective-permute-start(bf16[48,768]{1,0:T(8,128)(2,1)S(1)} %get-tuple-element.127), channel_id=1, source_target_pairs={{0,4},{2,6},{4,0},{6,2},{1,5},{3,7},{5,1},{7,3},{8,12},{10,14},{12... | collective-permute-start | bytes 221192 | tf_op jit(solution)/shard_map/ppermute | solution.py:558
  69.9 12.7 %collective-permute-start.29 = (f32[24,1536]{1,0:T(8,128)S(1)}, f32[24,1536]{1,0:T(8,128)S(1)}, u32[]{:S(2)}, u32[]{:S(2)}) collective-permute-start(f32[24,1536]{1,0:T(8,128)S(1)} %get-tuple-element.140), channel_id=1, source_target_pairs={{0,1},{1,0},{2,3},{3,2},{4,5},{5,4},{6,7},{7,6},{8,9},{9,8},{10,11... | collective-permute-start | bytes 442376 | tf_op jit(solution)/shard_map/ppermute | solution.py:560
  70.0 9.5 %collective-permute-start.25 = (bf16[48,768]{1,0:T(8,128)(2,1)S(1)}, bf16[48,768]{1,0:T(8,128)(2,1)S(1)}, u32[]{:S(2)}, u32[]{:S(2)}) collective-permute-start(bf16[48,768]{1,0:T(8,128)(2,1)S(1)} %get-tuple-element.129), channel_id=1, source_target_pairs={{0,5},{1,4},{2,7},{3,6},{4,1},{5,0},{6,3},{7,2},{8,13},{9,12},{10,... | collective-permute-start | bytes 221192 | tf_op jit(solution)/shard_map/ppermute | solution.py:559
  71.7 9.5 %collective-permute-start.28 = (bf16[24,1536]{1,0:T(8,128)(2,1)S(1)}, bf16[24,1536]{1,0:T(8,128)(2,1)S(1)}, u32[]{:S(2)}, u32[]{:S(2)}) collective-permute-start(bf16[24,1536]{1,0:T(8,128)(2,1)S(1)} %get-tuple-element.139), channel_id=1, source_target_pairs={{0,4},{2,6},{4,0},{6,2},{1,5},{3,7},{5,1},{7,3},{8,12},{10,14},{12... | collective-permute-start | bytes 221192 | tf_op jit(solution)/shard_map/ppermute | solution.py:558
  74.8 7.8 %collective-permute-start.30 = (bf16[24,1536]{1,0:T(8,128)(2,1)S(1)}, bf16[24,1536]{1,0:T(8,128)(2,1)S(1)}, u32[]{:S(2)}, u32[]{:S(2)}) collective-permute-start(bf16[24,1536]{1,0:T(8,128)(2,1)S(1)} %get-tuple-element.141), channel_id=1, source_target_pairs={{0,5},{1,4},{2,7},{3,6},{4,1},{5,0},{6,3},{7,2},{8,13},{9,12},{10,... | collective-permute-start | bytes 221192 | tf_op jit(solution)/shard_map/ppermute | solution.py:559
